TPU v7x, 32 devices: a whole 2x2x4 slice. The times are simulated.
32 devices in a mesh: runs: 2 (over y), chain: 4 (over z), basin: 2 (over x), feat: 2 (over core).
Axes of the slice: x: 2, y: 2, z: 4, core: 2. Of those that a mesh axis runs over, the one named last changes fastest.
Arguments:
- features: bfloat16 [12288, 256], P(('runs', 'chain', 'basin')), parts along dimension 0, may hold values from -6 to 6
- cotangent: float32 [12288, 256], P(('runs', 'chain', 'basin')), parts along dimension 0, may hold values from -6 to 6
- w_in: bfloat16 [3, 256, 1024], P(None, None, 'feat'), may hold values from -0.375 to 0.375
- w_out: bfloat16 [3, 1024, 256], P(None, 'feat'), may hold values from -0.1875 to 0.1875
- block_index: int32 [48, 4], P(('chain', 'basin')), may hold values from 0 to 8, as said below
- block_values: bfloat16 [48, 4, 128, 128], P(('chain', 'basin')), may hold values from -0.25 to 0.25
- send_rows: int32 [8, 2, 128], P(('chain', 'basin')), may hold values from 0 to 767
- send_count: int32 [8, 2], P(('chain', 'basin')), may hold values from 42 to 128, as said below
Outputs:
- grad_features: float32 [12288, 256], P(('runs', 'chain', 'basin')), parts along dimension 0
- grad_w_in: float32 [6, 256, 1024], P('runs', None, 'feat'), parts along dimension 0
- grad_w_out: float32 [6, 1024, 256], P('runs', 'feat'), parts along dimension 0
There are 2 independent parts, one for each index of `runs`. A program takes and returns all parts, laid end to end along the dimension named above; an argument that names none is the same for every part. Nothing has to cross between parts.
Inputs may be any that keep to these rules, and one draw needn't show every extreme that they name: `block_index`: in every shard, block row k lists block k first among its 4 entries, and every block from 6 to 8 appears in some block row. `send_count`: at most 128 live slots from one shard to one group; in every draw some group receives 128 live slots from every shard.
All inputs are finite; a program needn't handle non-finite values.
Results may differ from a plain program's by a relative error of at most 0.018.
Values may be sent and summed in bfloat16 or wider, within the bound.
No kernel may reach another device: no remote copies, remote signals or barrier semaphores. Data moves between devices by JAX's collectives and lax.ppermute only.
A program may use at most 64 MiB of HBM per device.

v0:
```python
import jax
import jax.numpy as jnp
from jax import lax
from jax.sharding import PartitionSpec as P

BLOCK = 128
DIVERT_CAP = 128


eps = 1e-06
highest = lax.Precision.HIGHEST


def passed_along(block, axis, distance):
    devices = range(lax.axis_size(axis))
    route = [(i - distance, i) for i in devices if i - distance in devices]
    return lax.ppermute(block, axis, route)


def silu_grad(pre_act):
    sigm = jax.nn.sigmoid(pre_act)
    return sigm * (1.0 + pre_act * (1.0 - sigm))


def mix_rows(source_table, index_rows, value_rows):
    latent = source_table.shape[-1]
    blocks = source_table.reshape(-1, BLOCK, latent)
    picked = blocks[index_rows]
    mixed = jnp.einsum("ktij,ktjh->kih", value_rows, picked, preferred_element_type=jnp.float32)
    return mixed.reshape(-1, latent)


def spread_rows(grad_rows, index_rows, value_rows, sources):
    latent = grad_rows.shape[-1]
    grad_blocks = grad_rows.reshape(-1, BLOCK, latent)
    products = jnp.einsum(
        "ktij,kih->ktjh", value_rows, grad_blocks, preferred_element_type=jnp.float32
    )
    onehot = (index_rows[:, :, None] == jnp.arange(sources, dtype=jnp.int32)[None, None, :]).astype(
        jnp.float32
    )
    return jnp.einsum("kts,ktjh->sjh", onehot, products, precision=highest).reshape(-1, latent)


def route(outgoing, backward):
    if backward:
        return lax.all_to_all(
            outgoing.astype(jnp.bfloat16), "basin", split_axis=0, concat_axis=0, tiled=True
        ).astype(outgoing.dtype)
    return lax.all_to_all(outgoing, "basin", split_axis=0, concat_axis=0, tiled=True)


def build_table(message, row_picks, live_slots):
    reaches = message.shape[0]
    upstream = passed_along(message[reaches - BLOCK :], "chain", 1)
    outgoing = jnp.where(live_slots[:, :, None], message[row_picks], jnp.zeros((), jnp.bfloat16))
    incoming = route(outgoing, False).reshape(-1, message.shape[1])
    return jnp.concatenate([message, upstream, incoming], axis=0)


def collect_grads(dtable, reaches, row_picks, live_slots):
    latent = dtable.shape[1]
    dlocal = dtable[:reaches]
    grad_up = dtable[reaches : reaches + BLOCK]
    grad_inc = dtable[reaches + BLOCK :].reshape(-1, DIVERT_CAP, latent)
    downhill = passed_along(grad_up.astype(jnp.bfloat16), "chain", -1).astype(grad_up.dtype)
    dlocal = dlocal.at[reaches - BLOCK :].add(downhill)
    returned = jnp.where(live_slots[:, :, None], route(grad_inc, True), 0.0)
    return dlocal.at[row_picks.reshape(-1)].add(returned.reshape(-1, latent))


def norm_forward(state_now, mixed):
    residual = state_now + mixed
    row_scale = lax.rsqrt(jnp.mean(residual * residual, axis=-1, keepdims=True) + eps)
    return (residual, row_scale)


def norm_backward(grad_state, residual, row_scale):
    normed = residual * row_scale
    return row_scale * (grad_state - normed * jnp.mean(grad_state * normed, axis=-1, keepdims=True))


def shards(features, cotangent, w_in, w_out, block_index, block_values, send_rows, send_count):
    reaches = features.shape[0]
    groups = lax.axis_size("basin")
    sources = reaches // BLOCK + 1 + groups
    row_picks = send_rows[0]
    live_slots = jnp.arange(DIVERT_CAP, dtype=jnp.int32)[None, :] < send_count[0][:, None]
    grad_scale = float(reaches * lax.axis_size("chain") * groups) ** (-0.5)
    layers = w_in.shape[0]
    grads_in = []
    grads_out = []
    saved = []
    state_now = features.astype(jnp.float32)
    for layer_id in range(layers):
        inputs = state_now.astype(jnp.bfloat16)
        pre_act = jnp.dot(inputs, w_in[layer_id], preferred_element_type=jnp.float32)
        active = jax.nn.silu(pre_act).astype(jnp.bfloat16)
        partial_msg = jnp.dot(active, w_out[layer_id], preferred_element_type=jnp.float32)
        message = lax.psum(partial_msg.astype(jnp.bfloat16), "feat")
        source_table = build_table(message, row_picks, live_slots)
        residual, row_scale = norm_forward(
            state_now, mix_rows(source_table, block_index, block_values)
        )
        saved.append((inputs, pre_act, active, residual, row_scale))
        state_now = residual * row_scale
    grad_state = cotangent
    for layer_id in reversed(range(layers)):
        inputs, pre_act, active, residual, row_scale = saved[layer_id]
        dtotal = norm_backward(grad_state, residual, row_scale)
        dtable = spread_rows(dtotal.astype(jnp.bfloat16), block_index, block_values, sources)
        grad_msg = collect_grads(dtable, reaches, row_picks, live_slots).astype(jnp.bfloat16)
        grad_act = jnp.dot(grad_msg, w_out[layer_id].T, preferred_element_type=jnp.float32)
        grad_pre = (grad_act * silu_grad(pre_act)).astype(jnp.bfloat16)
        partial_in = jnp.dot(grad_pre, w_in[layer_id].T, preferred_element_type=jnp.float32)
        grad_state = dtotal + lax.psum(partial_in.astype(jnp.bfloat16), "feat").astype(jnp.float32)
        grads_out.append(
            jnp.dot(active.T, grad_msg, preferred_element_type=jnp.float32) * grad_scale
        )
        grads_in.append(
            jnp.dot(inputs.T, grad_pre, preferred_element_type=jnp.float32) * grad_scale
        )
    summed_in, summed_out = lax.psum(
        (jnp.stack(grads_in[::-1]), jnp.stack(grads_out[::-1])), ("chain", "basin")
    )
    return (grad_state, summed_in, summed_out)


def solution(mesh):
    placed = (
        P(("runs", "chain", "basin"), None),
        P(("runs", "chain", "basin"), None),
        P(None, None, "feat"),
        P(None, "feat", None),
        P(("chain", "basin"), None),
        P(("chain", "basin"), None, None, None),
        P(("chain", "basin"), None, None),
        P(("chain", "basin"), None),
    )
    return jax.shard_map(
        shards,
        mesh=mesh,
        in_specs=placed,
        out_specs=(
            P(("runs", "chain", "basin"), None),
            P("runs", None, "feat"),
            P("runs", "feat", None),
        ),
        check_vma=False,
    )
```

profile of v0, /device:TPU:0, one launch (start us, length us, event | category | flops | bytes accessed | tf_op | source)
XLA Modules:
  0.0 466.9 jit_solution(3491309719418798308)
XLA Ops:
  7.2 2.8 multiply_convert_fusion.5
  12.7 21.0 %all-reduce.9.cloned.1.call-done = bf16[768,256]{1,0:T(8,128)(2,1)} async-done(((bf16[768,256]{1,0:T(8,128)(2,1)}), bf16[768,256]{1,0:T(8,128)(2,1)}) %all-reduce.9.cloned.1.call-update) | async-done | bytes 393232 | tf_op jit(solution)/shard_map/psum | solution.py:100
  34.7 3.6 collective-permute-start
  41.1 3.4 all-to-all-start
  44.6 4.4 all-to-all-done
  56.5 17.7 %all-reduce.11.cloned.1.call-done = bf16[768,256]{1,0:T(8,128)(2,1)} async-done(((bf16[768,256]{1,0:T(8,128)(2,1)}), bf16[768,256]{1,0:T(8,128)(2,1)}) %all-reduce.11.cloned.1.call-update) | async-done | bytes 393232 | tf_op jit(solution)/shard_map/psum | solution.py:100
  75.2 3.6 collective-permute-start.1
  81.6 3.4 all-to-all-start.1
  85.0 4.4 all-to-all-done.1
  93.5 2.7 multiply_convert_fusion.3
  99.2 17.7 %all-reduce.13.cloned.1.call-done = bf16[768,256]{1,0:T(8,128)(2,1)} async-done(((bf16[768,256]{1,0:T(8,128)(2,1)}), bf16[768,256]{1,0:T(8,128)(2,1)}) %all-reduce.13.cloned.1.call-update) | async-done | bytes 393232 | tf_op jit(solution)/shard_map/psum | solution.py:100
  117.9 3.6 collective-permute-start.2
  124.3 3.4 all-to-all-start.2
  127.7 4.4 all-to-all-done.2
  141.6 5.1 %copy.39 = f32[6,4,128,256]{3,0,1,2:T(8,128)} copy(f32[6,4,128,256]{2,3,1,0:T(8,128)} %convolution_bitcast_fusion.2) | data formatting | bytes 6291456 | tf_op jit(solution)/shard_map/ktij,kih->ktjh/dot_general | solution.py:36
  146.7 5.7 %fusion.53 = (bf16[9,128,256]{2,0,1:T(8,128)(2,1)S(1)}, f32[9,128,256]{2,0,1:T(8,128)}) fusion(f32[6,4,128,256]{3,0,1,2:T(8,128)} %copy.39, s32[6,4]{0,1:T(4,128)S(1)} %copy-done.28), kind=kOutput, calls=%fused_computation.133 | convolution fusion | flops 85229784 | bytes 4915296 | tf_op jit(solution)/shard_map/kts,ktjh->sjh/dot_general | solution.py:42
  153.3 3.4 all-to-all-start.3
  163.8 4.6 collective-permute-done.3
  177.1 19.1 %all-reduce.15.cloned.1.call-done = bf16[768,256]{1,0:T(8,128)(2,1)} async-done(((bf16[768,256]{1,0:T(8,128)(2,1)}), bf16[768,256]{1,0:T(8,128)(2,1)}) %all-reduce.15.cloned.1.call-update) | async-done | bytes 393232 | tf_op jit(solution)/shard_map/psum | solution.py:116
  201.3 5.1 %copy.43 = f32[6,4,128,256]{3,0,1,2:T(8,128)} copy(f32[6,4,128,256]{2,3,1,0:T(8,128)} %convolution_bitcast_fusion.1) | data formatting | bytes 6291456 | tf_op jit(solution)/shard_map/ktij,kih->ktjh/dot_general | solution.py:36
  206.5 5.7 %fusion.54 = (bf16[9,128,256]{2,0,1:T(8,128)(2,1)S(1)}, f32[9,128,256]{2,0,1:T(8,128)}) fusion(f32[6,4,128,256]{3,0,1,2:T(8,128)} %copy.43, s32[6,4]{0,1:T(4,128)S(1)} %copy-done.28), kind=kOutput, calls=%fused_computation.134 | convolution fusion | flops 85229784 | bytes 4915296 | tf_op jit(solution)/shard_map/kts,ktjh->sjh/dot_general | solution.py:42
  214.0 3.4 all-to-all-start.4
  225.0 4.0 collective-permute-done.4
  230.6 3.9 scatter_fusion.1
  245.3 14.1 %all-reduce.17.cloned.1.call-done = bf16[768,256]{1,0:T(8,128)(2,1)} async-done(((bf16[768,256]{1,0:T(8,128)(2,1)}), bf16[768,256]{1,0:T(8,128)(2,1)}) %all-reduce.17.cloned.1.call-update) | async-done | bytes 393232 | tf_op jit(solution)/shard_map/psum | solution.py:116
  263.3 5.1 %copy.47 = f32[6,4,128,256]{3,0,1,2:T(8,128)} copy(f32[6,4,128,256]{2,3,1,0:T(8,128)} %convolution_bitcast_fusion) | data formatting | bytes 6291456 | tf_op jit(solution)/shard_map/ktij,kih->ktjh/dot_general | solution.py:36
  268.4 5.8 %fusion.55 = (bf16[9,128,256]{2,0,1:T(8,128)(2,1)S(1)}, f32[9,128,256]{2,0,1:T(8,128)}) fusion(f32[6,4,128,256]{3,0,1,2:T(8,128)} %copy.47, s32[6,4]{0,1:T(4,128)S(1)} %copy-done.28), kind=kOutput, calls=%fused_computation.135 | convolution fusion | flops 85229784 | bytes 4915296 | tf_op jit(solution)/shard_map/kts,ktjh->sjh/dot_general | solution.py:42
  276.0 4.0 all-to-all-start.5
  287.5 3.2 collective-permute-done.5
  306.6 14.3 %all-reduce.19.cloned.1.call-done = bf16[768,256]{1,0:T(8,128)(2,1)} async-done(((bf16[768,256]{1,0:T(8,128)(2,1)}), bf16[768,256]{1,0:T(8,128)(2,1)}) %all-reduce.19.cloned.1.call-update) | async-done | bytes 393232 | tf_op jit(solution)/shard_map/psum | solution.py:116
  323.0 132.7 %all-reduce.21.cloned.1.call-done = (f32[3,256,512]{1,2,0:T(8,128)}, f32[3,512,256]{2,1,0:T(8,128)}) async-done(((f32[3,256,512]{1,2,0:T(8,128)}, f32[3,512,256]{2,1,0:T(8,128)}), (f32[3,256,512]{1,2,0:T(8,128)}, f32[3,512,256]{2,1,0:T(8,128)})) %all-reduce.21.cloned.1.call-update) | async-done | bytes 3145744 | tf_op jit(solution)/shard_map/psum | solution.py:123
  455.7 3.1 copy.52
  (186 shorter events, 113.4 us)
Async XLA Ops:
  7.2 42.5 %copy-start = (bf16[6,4,128,128]{3,2,1,0:T(8,128)(2,1)S(1)}, bf16[6,4,128,128]{3,2,1,0:T(8,128)(2,1)}, u32[]{:S(2)}) copy-start(bf16[6,4,128,128]{3,2,1,0:T(8,128)(2,1)} %param.19) | copy-start | bytes 2359300
  7.2 26.6 %all-reduce.9.cloned.1.call-start = ((), (), s32[]{:S(2)}) async-start(), calls=%async_computation.6 | async-start | bytes 786432 | tf_op jit(solution)/shard_map/psum | solution.py:100
  10.0 30.4 %copy-start.17 = (bf16[768,512]{1,0:T(8,128)(2,1)}, bf16[768,512]{1,0:T(8,128)(2,1)S(1)}, u32[]{:S(2)}) copy-start(bf16[768,512]{1,0:T(8,128)(2,1)S(1)} %get-tuple-element.60) | copy-start | bytes 2359300
  10.0 2.6 copy-start.31
  33.8 15.2 %copy-start.4 = (bf16[768,256]{1,0:T(8,128)(2,1)S(1)}, bf16[768,256]{1,0:T(8,128)(2,1)}, u32[]{:S(2)}) copy-start(bf16[768,256]{1,0:T(8,128)(2,1)} %all-reduce.9.cloned.1.call-done) | copy-start | bytes 1179652
  34.7 9.9 %collective-permute-start = (bf16[128,256]{1,0:T(8,128)(2,1)S(1)}, bf16[128,256]{1,0:T(8,128)(2,1)S(1)}, u32[]{:S(2)}, u32[]{:S(2)}) collective-permute-start(bf16[128,256]{1,0:T(8,128)(2,1)S(1)} %slice.180), channel_id=1, source_target_pairs={{0,4},{4,8},{8,12},{1,5},{5,9},{9,13},{2,6},{6,10},{10,14},{3,7},{... | collective-permute-start | bytes 196616 | tf_op jit(solution)/shard_map/ppermute | solution.py:17
  41.1 7.8 %all-to-all-start = ((bf16[2,128,256]{2,1,0:T(8,128)(2,1)}), bf16[2,128,256]{2,1,0:T(8,128)(2,1)S(1)}, u32[]{:S(2)}, u32[]{:S(2)}) async-start(bf16[2,128,256]{2,1,0:T(8,128)(2,1)} %broadcast_select_fusion.2), calls=%async_computation | async-start | bytes 262144 | tf_op jit(solution)/shard_map/all_to_all | solution.py:50
  44.5 29.7 %all-reduce.11.cloned.1.call-start = ((), (), s32[]{:S(2)}) async-start(), calls=%async_computation.7 | async-start | bytes 786432 | tf_op jit(solution)/shard_map/psum | solution.py:100
  74.2 15.2 %copy-start.5 = (bf16[768,256]{1,0:T(8,128)(2,1)S(1)}, bf16[768,256]{1,0:T(8,128)(2,1)}, u32[]{:S(2)}) copy-start(bf16[768,256]{1,0:T(8,128)(2,1)} %all-reduce.11.cloned.1.call-done) | copy-start | bytes 1179652
  75.2 9.9 %collective-permute-start.1 = (bf16[128,256]{1,0:T(8,128)(2,1)S(1)}, bf16[128,256]{1,0:T(8,128)(2,1)S(1)}, u32[]{:S(2)}, u32[]{:S(2)}) collective-permute-start(bf16[128,256]{1,0:T(8,128)(2,1)S(1)} %slice.181), channel_id=1, source_target_pairs={{0,4},{4,8},{8,12},{1,5},{5,9},{9,13},{2,6},{6,10},{10,14},{3,7},{... | collective-permute-start | bytes 196616 | tf_op jit(solution)/shard_map/ppermute | solution.py:17
  81.6 7.8 %all-to-all-start.1 = ((bf16[2,128,256]{2,1,0:T(8,128)(2,1)}), bf16[2,128,256]{2,1,0:T(8,128)(2,1)S(1)}, u32[]{:S(2)}, u32[]{:S(2)}) async-start(bf16[2,128,256]{2,1,0:T(8,128)(2,1)} %broadcast_select_fusion.1), calls=%async_computation.1 | async-start | bytes 262144 | tf_op jit(solution)/shard_map/all_to_all | solution.py:50
  85.0 32.0 %all-reduce.13.cloned.1.call-start = ((), (), s32[]{:S(2)}) async-start(), calls=%async_computation.8 | async-start | bytes 786432 | tf_op jit(solution)/shard_map/psum | solution.py:100
  116.9 15.2 %copy-start.6 = (bf16[768,256]{1,0:T(8,128)(2,1)S(1)}, bf16[768,256]{1,0:T(8,128)(2,1)}, u32[]{:S(2)}) copy-start(bf16[768,256]{1,0:T(8,128)(2,1)} %all-reduce.13.cloned.1.call-done) | copy-start | bytes 1179652
  117.9 9.8 %collective-permute-start.2 = (bf16[128,256]{1,0:T(8,128)(2,1)S(1)}, bf16[128,256]{1,0:T(8,128)(2,1)S(1)}, u32[]{:S(2)}, u32[]{:S(2)}) collective-permute-start(bf16[128,256]{1,0:T(8,128)(2,1)S(1)} %slice.182), channel_id=1, source_target_pairs={{0,4},{4,8},{8,12},{1,5},{5,9},{9,13},{2,6},{6,10},{10,14},{3,7},{... | collective-permute-start | bytes 196616 | tf_op jit(solution)/shard_map/ppermute | solution.py:17
  124.3 7.8 %all-to-all-start.2 = ((bf16[2,128,256]{2,1,0:T(8,128)(2,1)}), bf16[2,128,256]{2,1,0:T(8,128)(2,1)S(1)}, u32[]{:S(2)}, u32[]{:S(2)}) async-start(bf16[2,128,256]{2,1,0:T(8,128)(2,1)} %broadcast_select_fusion), calls=%async_computation.2 | async-start | bytes 262144 | tf_op jit(solution)/shard_map/all_to_all | solution.py:50
  127.7 4.4 copy-start.27
  153.3 10.4 %all-to-all-start.3 = ((bf16[2,128,256]{2,1,0:T(8,128)(2,1)}), bf16[2,128,256]{2,1,0:T(8,128)(2,1)S(1)}, u32[]{:S(2)}, u32[]{:S(2)}) async-start(bf16[2,128,256]{2,1,0:T(8,128)(2,1)} %copy.41), calls=%async_computation.3 | async-start | bytes 262144 | tf_op jit(solution)/shard_map/all_to_all | solution.py:47
  156.7 39.6 %all-reduce.15.cloned.1.call-start = ((), (), s32[]{:S(2)}) async-start(), calls=%async_computation.9 | async-start | bytes 786432 | tf_op jit(solution)/shard_map/psum | solution.py:116
  162.0 6.5 %collective-permute-start.3 = (bf16[128,256]{1,0:T(8,128)(2,1)}, bf16[128,256]{1,0:T(8,128)(2,1)}, u32[]{:S(2)}, u32[]{:S(2)}) collective-permute-start(bf16[128,256]{1,0:T(8,128)(2,1)} %bitcast.189), channel_id=1, source_target_pairs={{4,0},{8,4},{12,8},{5,1},{9,5},{13,9},{6,2},{10,6},{14,10},{7,3},{... | collective-permute-start | bytes 196616 | tf_op jit(solution)/shard_map/ppermute | solution.py:17
  214.0 10.9 %all-to-all-start.4 = ((bf16[2,128,256]{2,1,0:T(8,128)(2,1)}), bf16[2,128,256]{2,1,0:T(8,128)(2,1)S(1)}, u32[]{:S(2)}, u32[]{:S(2)}) async-start(bf16[2,128,256]{2,1,0:T(8,128)(2,1)} %copy.45), calls=%async_computation.4 | async-start | bytes 262144 | tf_op jit(solution)/shard_map/all_to_all | solution.py:47
  217.4 42.0 %all-reduce.17.cloned.1.call-start = ((), (), s32[]{:S(2)}) async-start(), calls=%async_computation.10 | async-start | bytes 786432 | tf_op jit(solution)/shard_map/psum | solution.py:116
  222.5 6.5 %collective-permute-start.4 = (bf16[128,256]{1,0:T(8,128)(2,1)}, bf16[128,256]{1,0:T(8,128)(2,1)}, u32[]{:S(2)}, u32[]{:S(2)}) collective-permute-start(bf16[128,256]{1,0:T(8,128)(2,1)} %bitcast.188), channel_id=1, source_target_pairs={{4,0},{8,4},{12,8},{5,1},{9,5},{13,9},{6,2},{10,6},{14,10},{7,3},{... | collective-permute-start | bytes 196616 | tf_op jit(solution)/shard_map/ppermute | solution.py:17
  240.0 2.6 copy-start.21
  244.0 15.3 %copy-start.2 = (f32[768,256]{1,0:T(8,128)S(1)}, f32[768,256]{1,0:T(8,128)}, u32[]{:S(2)}) copy-start(f32[768,256]{1,0:T(8,128)} %get-tuple-element.51) | copy-start | bytes 2359300
  268.4 11.7 %copy-start.24 = (bf16[768,512]{1,0:T(8,128)(2,1)S(1)}, bf16[768,512]{1,0:T(8,128)(2,1)}, u32[]{:S(2)}) copy-start(bf16[768,512]{1,0:T(8,128)(2,1)} %copy-done.23) | copy-start | bytes 2359300
  276.0 9.7 %all-to-all-start.5 = ((bf16[2,128,256]{2,1,0:T(8,128)(2,1)}), bf16[2,128,256]{2,1,0:T(8,128)(2,1)}, u32[]{:S(2)}, u32[]{:S(2)}) async-start(bf16[2,128,256]{2,1,0:T(8,128)(2,1)} %copy.49), calls=%async_computation.5 | async-start | bytes 262144 | tf_op jit(solution)/shard_map/all_to_all | solution.py:47
  280.0 40.8 %all-reduce.19.cloned.1.call-start = ((), (), s32[]{:S(2)}) async-start(), calls=%async_computation.11 | async-start | bytes 786432 | tf_op jit(solution)/shard_map/psum | solution.py:116
  283.6 8.1 %copy-start.29 = (s32[256,1]{0,1:T(1,128)S(1)}, s32[256,1]{0,1:T(1,128)}, u32[]{:S(2)}) copy-start(s32[256,1]{0,1:T(1,128)} %compare_select_fusion) | copy-start | bytes 3076
  284.2 6.5 %collective-permute-start.5 = (bf16[128,256]{1,0:T(8,128)(2,1)}, bf16[128,256]{1,0:T(8,128)(2,1)}, u32[]{:S(2)}, u32[]{:S(2)}) collective-permute-start(bf16[128,256]{1,0:T(8,128)(2,1)} %bitcast.187), channel_id=1, source_target_pairs={{4,0},{8,4},{12,8},{5,1},{9,5},{13,9},{6,2},{10,6},{14,10},{7,3},{... | collective-permute-start | bytes 196616 | tf_op jit(solution)/shard_map/ppermute | solution.py:17
  301.5 154.2 %all-reduce.21.cloned.1.call-start = ((), (), s32[]{:S(2)}) async-start(), calls=%async_computation.12 | async-start | bytes 6291456 | tf_op jit(solution)/shard_map/psum | solution.py:123
  301.6 2.6 copy-start.26
  455.7 3.1 copy-start.15
  (22 other events, 33.0 us)
Sparse Core Ops, SparseCore 0:
  12.5 21.1 all-reduce.8
  56.6 17.5 all-reduce.10
  99.3 17.5 all-reduce.12
  177.2 18.9 all-reduce.14
  240.1 19.1 all-reduce.16
  301.6 19.1 all-reduce.18
  325.1 130.6 all-reduce.20
where the time goes:
time: 469 us; the launch traced here: 467 us
  waiting for transfers between devices  262 us (56%)
  matrix products  64.6 us (14%)
  local copies, waits for them, and re-layouts  58.1 us (12%)
  starting transfers between devices  36.1 us (8%)
  other arithmetic  31.5 us (7%)
  between operations  14.8 us (3%)
    psum x1, waiting for transfers between devices, shards(): lax.psum((jnp.stack(grads_in[::-1]), jnp.stack(grads_out[::-1])), ('chain...  133 us
    psum x3, waiting for transfers between devices, shards(): message = lax.psum(partial_msg.astype(jnp.bfloat16), 'feat')  56.5 us
    psum x3, waiting for transfers between devices, shards(): lax.psum(partial_in.astype(jnp.bfloat16), 'feat').astype(jnp.float32)  47.5 us
    dot_general x3, matrix products, spread_rows(): jnp.einsum('kts,ktjh->sjh', onehot, products, precision=highest)  17.2 us
    dot_general x3, local copies, waits for them, and re-layouts, spread_rows(): jnp.einsum('ktij,kih->ktjh', value_rows, grad_blocks, preferred_element_t...  15.4 us
    unnamed x75, local copies, waits for them, and re-layouts  15.2 us
    ppermute x6, starting transfers between devices, passed_along(): return lax.ppermute(block, axis, route)  15 us
    all_to_all x3, waiting for transfers between devices, route(): lax.all_to_all(outgoing, 'basin', split_axis=0, concat_axis=0, tiled=True)  13.2 us
  transfers between devices with their start and end apart: 19, of which 13 were waited for; matrix products, arithmetic and copies ran while one was open for 8% of the time, Pallas kernels for 0%

commit v1 on v0

v1 whole, which is shorter than its diff:
```python
import functools

import jax
import jax.numpy as jnp
from jax import lax
from jax.experimental import pallas as pl
from jax.experimental.pallas import tpu as pltpu
from jax.sharding import PartitionSpec as P

BLOCK = 128
EPS = 1e-06
F32 = jnp.float32
BF16 = jnp.bfloat16
VMEM = pl.BlockSpec(memory_space=pltpu.VMEM)
SMEM = pl.BlockSpec(memory_space=pltpu.SMEM)
NN = (((1,), (0,)), ((), ()))
NT = (((1,), (1,)), ((), ()))
TN = (((0,), (0,)), ((), ()))


def mm(a, b, dims=NN):
    return lax.dot_general(a, b, dims, preferred_element_type=F32)


def call(body, outs, ins, flops, scratch=(), name=None):
    return pl.pallas_call(
        body,
        out_shape=[jax.ShapeDtypeStruct(s, d) for s, d in outs],
        in_specs=[SMEM if x.dtype == jnp.int32 and x.size < 100 else VMEM for x in ins],
        out_specs=[VMEM] * len(outs),
        scratch_shapes=list(scratch),
        compiler_params=pltpu.CompilerParams(vmem_limit_bytes=32 * 1024 * 1024),
        cost_estimate=pl.CostEstimate(flops=flops, bytes_accessed=4_000_000, transcendentals=0),
        name=name,
    )(*ins)


def sigmoid(v):
    return 1.0 / (1.0 + jnp.exp(-v))


def message_of(x, halves):
    total = None
    for w_in, w_out in halves:
        pre = mm(x, w_in)
        part = mm((pre * sigmoid(pre)).astype(BF16), w_out)
        total = part if total is None else total + part
    return total.astype(BF16)


def message_grad(x, dmsg, halves):
    total = None
    kept = None
    for w_in, w_out in halves:
        pre = mm(x, w_in)
        sig = sigmoid(pre)
        dact = mm(dmsg, w_out, NT)
        dpre = (dact * (sig * (1.0 + pre * (1.0 - sig)))).astype(BF16)
        if kept is None:
            kept = ((pre * sig).astype(BF16), dpre)
        part = mm(dpre, w_in, NT)
        total = part if total is None else total + part
    return total, kept


def normed_of(total):
    scale = lax.rsqrt(jnp.mean(total * total, axis=-1, keepdims=True) + EPS)
    return scale, scale * total


def norm_grad(grad, total):
    scale, normed = normed_of(total)
    return scale * (grad - normed * jnp.mean(grad * normed, axis=-1, keepdims=True))


def setup_kernel(groups, rows, send_rows, send_count, features, *outs):
    pick, spread, pick_self, up = outs[:4]
    sends = outs[4:]
    b = lax.axis_index("basin")
    lane = lax.broadcasted_iota(jnp.int32, (1, BLOCK), 1)
    for s in range(groups):
        target = lax.rem(b + s, groups)
        chosen = send_rows[0, pl.ds(target, 1), :]
        chosen = jnp.where(lane < send_count[0, target], chosen, -1)
        across = jnp.broadcast_to(chosen, (BLOCK, BLOCK))
        down = across.T
        for r in range(rows // BLOCK):
            at = lax.broadcasted_iota(jnp.int32, (BLOCK, BLOCK), 1) + r * BLOCK
            hot = (down == at).astype(F32).astype(BF16)
            if s == 0:
                pick_self[:, r * BLOCK : (r + 1) * BLOCK] = hot
            else:
                pick[(s - 1) * BLOCK : s * BLOCK, r * BLOCK : (r + 1) * BLOCK] = hot
                at = lax.broadcasted_iota(jnp.int32, (BLOCK, BLOCK), 0) + r * BLOCK
                spread[r * BLOCK : (r + 1) * BLOCK, (s - 1) * BLOCK : s * BLOCK] = (
                    (across == at).astype(F32).astype(BF16)
                )
    up[...] = features[rows - BLOCK :, :]
    for s, send in enumerate(sends):
        send[...] = mm(pick[s * BLOCK : (s + 1) * BLOCK, :], features[...]).astype(BF16)


def adjacency_kernel(groups, rows, index, values, pick_self, local, local_t, remote, remote_t, acc):
    own = rows // BLOCK
    b = lax.axis_index("basin")
    acc[...] = jnp.zeros_like(acc)
    for k in range(own):
        for t in range(index.shape[1]):
            v = index[k, t]
            sender = lax.rem(b + groups - (v - own - 1), groups)
            far = jnp.where(v == own, own + 1, jnp.where(sender == 0, own, own + 1 + sender))
            at = jnp.where(v < own, v, far)
            here = (pl.ds(k * BLOCK, BLOCK), pl.ds(pl.multiple_of(at * BLOCK, BLOCK), BLOCK))
            acc[here] += values[k, t].astype(F32)
    mine = acc[:, rows : rows + BLOCK].astype(BF16)
    full = acc[:, :rows] + mm(mine, pick_self[...])
    local[...] = full.astype(BF16)
    local_t[...] = full.T.astype(BF16)
    far = acc[:, rows + BLOCK :]
    remote[...] = far.astype(BF16)
    remote_t[...] = far.T.astype(BF16)


def shadow_fwd_kernel(layer, inputs, local, wi0, wi1, wo0, wo1, mixed, msg):
    halves = [(wi0[layer], wo0[layer]), (wi1[layer], wo1[layer])]
    rows = inputs.shape[0]
    for r in range(0, rows, 256):
        msg[r : r + 256, :] = message_of(inputs[r : r + 256, :], halves)
    mixed[...] = mm(local[...], msg[...])


def mixed_total(layer, state, mixed, received, remote, weights):
    wi0, wi1, wo0, wo1 = weights
    halves = [(wi0[layer], wo0[layer]), (wi1[layer], wo1[layer])]
    far = jnp.concatenate([x[...] for x in received], axis=0)
    return state + mixed[...] + mm(remote[...], message_of(far, halves))


def post_fwd_kernel(layer, groups, *refs):
    prev, mixed, remote, pick = refs[:4]
    weights = refs[4:8]
    received = refs[8 : 8 + groups]
    total, inputs, up = refs[8 + groups : 11 + groups]
    sends = refs[11 + groups :]
    state = prev[...].astype(F32) if layer == 0 else normed_of(prev[...])[1]
    total[...] = mixed_total(layer, state, mixed, received, remote, weights)
    new = normed_of(total[...])[1].astype(BF16)
    inputs[...] = new
    up[...] = new[new.shape[0] - BLOCK :, :]
    for s, send in enumerate(sends):
        send[...] = mm(pick[s * BLOCK : (s + 1) * BLOCK, :], new).astype(BF16)


def start_bwd(layer, dtotal_now, weights, received, remote_t, outs):
    dtotal, dround, far_x, far_dmsg, far_act, far_dpre = outs[:6]
    backs = outs[6:]
    wi0, wi1, wo0, wo1 = weights
    halves = [(wi0[layer], wo0[layer]), (wi1[layer], wo1[layer])]
    dtotal[...] = dtotal_now
    dround[...] = dtotal_now.astype(BF16)
    far = jnp.concatenate([x[...] for x in received], axis=0)
    dmsg = mm(remote_t[...], dround[...]).astype(BF16)
    back, (act, dpre) = message_grad(far, dmsg, halves)
    far_x[...] = far
    far_dmsg[...] = dmsg
    far_act[...] = act
    far_dpre[...] = dpre
    for s, out in enumerate(backs):
        out[...] = back[s * BLOCK : (s + 1) * BLOCK, :].astype(BF16)


def turn_kernel(layer, groups, *refs):
    prev, mixed, remote, remote_t, cot = refs[:5]
    weights = refs[5:9]
    received = refs[9 : 9 + groups]
    outs = refs[9 + groups :]
    state = normed_of(prev[...])[1]
    total = mixed_total(layer, state, mixed, received, remote, weights)
    start_bwd(layer, norm_grad(cot[...], total), weights, received, remote_t, outs)


def shadow_bwd_kernel(layer, grad_scale, *refs):
    dround, inputs, local_t = refs[:3]
    wi0, wi1, wo0, wo1 = refs[3:7]
    far_x, far_dmsg, far_act, far_dpre = refs[7:11]
    back, g_in, g_out, dmsg, act, dpre = refs[11:]
    halves = [(wi0[layer], wo0[layer]), (wi1[layer], wo1[layer])]
    dmsg[...] = mm(local_t[...], dround[...]).astype(BF16)
    rows = inputs.shape[0]
    for r in range(0, rows, 256):
        here = slice(r, r + 256)
        grad, (a, d) = message_grad(inputs[here, :], dmsg[here, :], halves)
        back[here, :] = grad
        act[here, :] = a
        dpre[here, :] = d
    g_in[...] = (
        (mm(inputs[...], dpre[...], TN) + mm(far_x[...], far_dpre[...], TN)) * grad_scale
    ).astype(BF16)
    g_out[...] = (
        (mm(act[...], dmsg[...], TN) + mm(far_act[...], far_dmsg[...], TN)) * grad_scale
    ).astype(BF16)


def gathered_grad(dtotal, back, returned, spread):
    grad = dtotal[...] + back[...]
    if len(returned) > 1:
        far = jnp.concatenate([x[...] for x in returned[1:]], axis=0)
        grad = grad + mm(spread[...], far)
    rows = grad.shape[0]
    low = grad[rows - BLOCK :, :] + returned[0][...].astype(F32)
    return jnp.concatenate([grad[: rows - BLOCK, :], low], axis=0)


def post_bwd_kernel(layer, groups, *refs):
    dtotal, back, spread, remote_t, total = refs[:5]
    weights = refs[5:9]
    returned = refs[9 : 9 + groups]
    received = refs[9 + groups : 9 + 2 * groups]
    outs = refs[9 + 2 * groups :]
    grad = gathered_grad(dtotal, back, returned, spread)
    start_bwd(layer, norm_grad(grad, total[...]), weights, received, remote_t, outs)


def last_kernel(groups, *refs):
    dtotal, back, spread = refs[:3]
    refs[3 + groups][...] = gathered_grad(dtotal, back, refs[3 : 3 + groups], spread)


def along(x, axis, distance):
    n = lax.axis_size(axis)
    return lax.ppermute(x, axis, [(i, i + distance) for i in range(n) if 0 <= i + distance < n])


def around(x, axis, distance):
    n = lax.axis_size(axis)
    return lax.ppermute(x, axis, [(i, (i + distance) % n) for i in range(n)])


def exchange(up, sends, sign):
    return [along(up, "chain", sign)] + [
        around(x, "basin", sign * (s + 1)) for s, x in enumerate(sends)
    ]


def shards(features, cotangent, w_in, w_out, block_index, block_values, send_rows, send_count):
    rows, latent = features.shape
    groups = lax.axis_size("basin")
    layers, _, half = w_in.shape
    far_rows = groups * BLOCK
    sent_rows = max(groups - 1, 1) * BLOCK
    own = rows // BLOCK
    grad_scale = float(rows * lax.axis_size("chain") * groups) ** (-0.5)

    def act16(n, m=latent):
        return ((n, m), BF16)

    wi1 = around(w_in, "feat", 1)
    wo1 = around(w_out, "feat", 1)
    weights = (w_in, wi1, w_out, wo1)
    ffn = 4 * latent * 2 * half

    pick, spread, pick_self, up, *sends = call(
        functools.partial(setup_kernel, groups, rows),
        [act16(sent_rows, rows), act16(rows, sent_rows), act16(BLOCK, rows), act16(BLOCK)]
        + [act16(BLOCK)] * (groups - 1),
        [send_rows, send_count, features],
        2 * rows * sent_rows * latent,
        name="setup",
    )
    received = [exchange(up, sends, 1)]
    local, local_t, remote, remote_t = call(
        functools.partial(adjacency_kernel, groups, rows),
        [act16(rows, rows), act16(rows, rows), act16(rows, far_rows), act16(far_rows, rows)],
        [block_index, block_values, pick_self],
        2 * rows * rows * BLOCK,
        scratch=[pltpu.VMEM((rows, (own + groups + 1) * BLOCK), F32)],
        name="adjacency",
    )
    inputs = [features]
    totals = []
    for layer in range(layers):
        mixed, _ = call(
            functools.partial(shadow_fwd_kernel, layer),
            [((rows, latent), F32), act16(rows)],
            [inputs[layer], local, *weights],
            rows * ffn + 2 * rows * rows * latent,
            name=f"local{layer}",
        )
        prev = features if layer == 0 else totals[-1]
        if layer + 1 < layers:
            total, new, up, *sends = call(
                functools.partial(post_fwd_kernel, layer, groups),
                [((rows, latent), F32), act16(rows)] + [act16(BLOCK)] * groups,
                [prev, mixed, remote, pick, *weights, *received[layer]],
                far_rows * ffn + 2 * rows * far_rows * latent,
                name=f"mix{layer}",
            )
            totals.append(total)
            inputs.append(new)
            received.append(exchange(up, sends, 1))
    bwd_outs = (
        [((rows, latent), F32), act16(rows), act16(far_rows), act16(far_rows)]
        + [act16(far_rows, half)] * 2
        + [act16(BLOCK)] * groups
    )
    last = layers - 1
    outs = call(
        functools.partial(turn_kernel, last, groups),
        bwd_outs,
        [totals[-1], mixed, remote, remote_t, cotangent, *weights, *received[last]],
        2 * far_rows * ffn,
        name="turn",
    )
    summed = []
    for layer in reversed(range(layers)):
        dtotal, dround = outs[:2]
        far_saved = outs[2:6]
        returned = exchange(outs[6], outs[7:], -1)
        back, g_in, g_out, *_ = call(
            functools.partial(shadow_bwd_kernel, layer, grad_scale),
            [((rows, latent), F32), act16(latent, half), act16(half), act16(rows)]
            + [act16(rows, half)] * 2,
            [dround, inputs[layer], local_t, *weights, *far_saved],
            3 * rows * ffn + 2 * rows * rows * latent,
            name=f"back{layer}",
        )
        summed.append(lax.psum((g_in, g_out), ("chain", "basin")))
        if layer:
            outs = call(
                functools.partial(post_bwd_kernel, layer - 1, groups),
                bwd_outs,
                [dtotal, back, spread, remote_t, totals[layer - 1]]
                + [*weights, *returned, *received[layer - 1]],
                2 * far_rows * ffn,
                name=f"join{layer}",
            )
    (grad,) = call(
        functools.partial(last_kernel, groups),
        [((rows, latent), F32)],
        [dtotal, back, spread, *returned],
        2 * rows * sent_rows * latent,
        name="join0",
    )
    summed_in = jnp.stack([x for x, _ in summed[::-1]]).astype(F32)
    summed_out = jnp.stack([x for _, x in summed[::-1]]).astype(F32)
    return (grad, summed_in, summed_out)


def solution(mesh):
    placed = (
        P(("runs", "chain", "basin"), None),
        P(("runs", "chain", "basin"), None),
        P(None, None, "feat"),
        P(None, "feat", None),
        P(("chain", "basin"), None),
        P(("chain", "basin"), None, None, None),
        P(("chain", "basin"), None, None),
        P(("chain", "basin"), None),
    )
    return jax.shard_map(
        shards,
        mesh=mesh,
        in_specs=placed,
        out_specs=(
            P(("runs", "chain", "basin"), None),
            P("runs", None, "feat"),
            P("runs", "feat", None),
        ),
        check_vma=False,
    )
```

time: 469 us -> 171 us (0.36)
  waiting for transfers between devices: 262 us -> 92.3 us
  matrix products: 64.6 us -> 0 us
  local copies, waits for them, and re-layouts: 58.1 us -> 7.14 us
  Pallas kernels: 0 us -> 29.9 us
  other arithmetic: 31.5 us -> 3.71 us
  starting transfers between devices: 36.1 us -> 23 us
    psum x7 -> x1, waiting for transfers between devices: 237 us -> 84.2 us  [shards(): summed.append(lax.psum((g_in, g_out), ('chain', 'basin')))]
    dot_general x27 -> x0, matrix products: 64.6 us -> none  [the longest x3 17.2 us: spread_rows(): jnp.einsum('kts,ktjh->sjh', onehot, products, precision=highest)]
    pallas_call x0 -> x14, Pallas kernels: none -> 29.9 us  [call(): pl.pallas_call(body, out_shape=[jax.ShapeDtypeStruct(s, d) for s, d in ou...]
    all_to_all x6 -> x0, starting transfers between devices: 20.9 us -> none  [the longest x3 10.8 us: route(): lax.all_to_all(outgoing.astype(jnp.bfloat16), 'basin', split_axis=0, conc...]
    dot_general x3 -> x0, local copies, waits for them, and re-layouts: 15.4 us -> none  [spread_rows(): jnp.einsum('ktij,kih->ktjh', value_rows, grad_blocks, preferred_element_t...]
    all_to_all x6 -> x0, waiting for transfers between devices: 13.2 us -> none  [the longest x3 13.2 us: route(): lax.all_to_all(outgoing, 'basin', split_axis=0, concat_axis=0, tiled=True)]
    scatter-add x6 -> x0, other arithmetic: 12.4 us -> none  [the longest x3 9 us: collect_grads(): return dlocal.at[row_picks.reshape(-1)].add(returned.reshape(-1, latent))]
    slice x18 -> x0, local copies, waits for them, and re-layouts: 12.1 us -> none  [the longest x6 4.32 us: collect_grads(): dlocal = dtable[:reaches]]
  transfers between devices with their start and end apart: 19 -> 15, of which waited for: 13 -> 5; matrix products, arithmetic and copies ran while one was open for 8% -> 0% of each run, Pallas kernels for 0% -> 11%
where the time goes in v1:
time: 171 us; the launch traced here: 170 us
  waiting for transfers between devices  92.3 us (54%)
  Pallas kernels  29.9 us (17%)
  starting transfers between devices  23 us (13%)
  between operations  14.2 us (8%)
  local copies, waits for them, and re-layouts  7.14 us (4%)
  other arithmetic  3.71 us (2%)
    psum x1, waiting for transfers between devices, shards(): summed.append(lax.psum((g_in, g_out), ('chain', 'basin')))  84.2 us
    pallas_call x14, Pallas kernels, call(): pl.pallas_call(body, out_shape=[jax.ShapeDtypeStruct(s, d) for s, d in ou...  29.9 us
    ppermute x6, starting transfers between devices, along(): lax.ppermute(x, axis, [(i, i + distance) for i in range(n) if 0 <= i + di...  16.1 us
    unnamed x33, local copies, waits for them, and re-layouts  7.14 us
    ppermute x8, starting transfers between devices, around(): return lax.ppermute(x, axis, [(i, (i + distance) % n) for i in range(n)])  6.9 us
    ppermute x6, waiting for transfers between devices, along(): lax.ppermute(x, axis, [(i, i + distance) for i in range(n) if 0 <= i + di...  4.73 us
  transfers between devices with their start and end apart: 15, of which 5 were waited for; matrix products, arithmetic and copies ran while one was open for 0% of the time, Pallas kernels for 11%

profile of v1, /device:TPU:0, one launch (start us, length us, event | category | flops | bytes accessed | tf_op | source)
XLA Modules:
  0.0 170.2 jit_solution(16532923193205533621)
XLA Ops:
  7.8 1.0 copy-done.3
  10.2 1.3 setup.1
  11.5 4.9 %collective-permute-start.2 = (bf16[128,256]{1,0:T(8,128)(2,1)}, bf16[128,256]{1,0:T(8,128)(2,1)S(1)}, u32[]{:S(2)}, u32[]{:S(2)}) collective-permute-start(bf16[128,256]{1,0:T(8,128)(2,1)} %get-tuple-element.61), channel_id=1, source_target_pairs={{0,4},{4,8},{8,12},{1,5},{5,9},{9,13},{2,6},{6,10},{10,14},{3,7},{... | collective-permute-start | bytes 196616 | tf_op jit(solution)/shard_map/ppermute | solution.py:231
  16.4 1.6 collective-permute-start.3
  18.7 1.1 copy-done.6
  19.8 1.6 adjacency.1
  21.5 1.1 copy-done.1
  22.6 2.1 %local0.1 = (f32[768,256]{1,0:T(8,128)S(1)}, bf16[768,256]{1,0:T(8,128)(2,1)}) custom-call(bf16[768,256]{1,0:T(8,128)(2,1)S(1)} %copy-done.4, bf16[768,768]{1,0:T(8,128)(2,1)S(1)} %get-tuple-element.57.local, bf16[3,256,512]{2,1,0:T(8,128)(2,1)S(1)} %copy-done, bf16[3,256,512]{2,1,0:T(8,128)(2,1)S(1)} %collective-permute-done.wi1.refs_5_.refs_6_.refs_4_, ...), custom_call_target="tpu_custom_call" | custom-call | flops 1107296256 | bytes 4000000 | tf_op jit(solution)/shard_map/local0/pallas_call | solution.py:26
  24.7 1.3 mix0.1
  26.0 3.5 %collective-permute-start.4 = (bf16[128,256]{1,0:T(8,128)(2,1)S(1)}, bf16[128,256]{1,0:T(8,128)(2,1)S(1)}, u32[]{:S(2)}, u32[]{:S(2)}) collective-permute-start(bf16[128,256]{1,0:T(8,128)(2,1)S(1)} %get-tuple-element.66), channel_id=1, source_target_pairs={{0,4},{4,8},{8,12},{1,5},{5,9},{9,13},{2,6},{6,10},{10,14},{3,7},{... | collective-permute-start | bytes 196616 | tf_op jit(solution)/shard_map/ppermute | solution.py:231
  30.1 2.1 %local1.1 = (f32[768,256]{1,0:T(8,128)S(1)}, bf16[768,256]{1,0:T(8,128)(2,1)}) custom-call(bf16[768,256]{1,0:T(8,128)(2,1)S(1)} %get-tuple-element.64.inputs.refs_1_, bf16[768,768]{1,0:T(8,128)(2,1)S(1)} %get-tuple-element.57.local, bf16[3,256,512]{2,1,0:T(8,128)(2,1)S(1)} %copy-done, ...), custom_call_target="tpu_custom_call" | custom-call | flops 1107296256 | bytes 4000000 | tf_op jit(solution)/shard_map/local1/pallas_call | solution.py:26
  32.2 1.7 collective-permute-done.5.refs_9_.refs_12_
  33.8 1.3 mix1.1
  35.1 3.5 %collective-permute-start.6 = (bf16[128,256]{1,0:T(8,128)(2,1)S(1)}, bf16[128,256]{1,0:T(8,128)(2,1)S(1)}, u32[]{:S(2)}, u32[]{:S(2)}) collective-permute-start(bf16[128,256]{1,0:T(8,128)(2,1)S(1)} %get-tuple-element.72), channel_id=1, source_target_pairs={{0,4},{4,8},{8,12},{1,5},{5,9},{9,13},{2,6},{6,10},{10,14},{3,7},{... | collective-permute-start | bytes 196616 | tf_op jit(solution)/shard_map/ppermute | solution.py:231
  39.2 2.1 %local2.1 = (f32[768,256]{1,0:T(8,128)S(1)}, bf16[768,256]{1,0:T(8,128)(2,1)}) custom-call(bf16[768,256]{1,0:T(8,128)(2,1)S(1)} %get-tuple-element.69.inputs.refs_1_, bf16[768,768]{1,0:T(8,128)(2,1)S(1)} %get-tuple-element.57.local, bf16[3,256,512]{2,1,0:T(8,128)(2,1)S(1)} %copy-done, ...), custom_call_target="tpu_custom_call" | custom-call | flops 1107296256 | bytes 4000000 | tf_op jit(solution)/shard_map/local2/pallas_call | solution.py:26
  41.3 1.7 collective-permute-done.7.refs_10_
  42.9 2.2 %turn.1 = (f32[768,256]{1,0:T(8,128)S(1)}, bf16[768,256]{1,0:T(8,128)(2,1)S(1)}, bf16[256,256]{1,0:T(8,128)(2,1)S(1)}, bf16[256,256]{1,0:T(8,128)(2,1)S(1)}, bf1...) custom-call(f32[768,256]{1,0:T(8,128)S(1)} %get-tuple-element.68.ref, ...), custom_call_target="tpu_custom_call" | custom-call | flops 536870912 | bytes 4000000 | tf_op jit(solution)/shard_map/turn/pallas_call | solution.py:26
  45.1 1.5 collective-permute-start.8
  47.2 4.0 %back2.1 = (f32[768,256]{1,0:T(8,128)S(1)}, bf16[256,512]{1,0:T(8,128)(2,1)}, bf16[512,256]{1,0:T(8,128)(2,1)}, bf16[768,256]{1,0:T(8,128)(2,1)}, bf16[768,512]{1,0:T(8,128)(2,1)}, /*index=5*/bf16[768,512]{1,0:T(8,128)(2,1)}) custom-call(bf16[768,256]{1,0:T(8,128)(2,1)S(1)} %get-tuple-element.75.refs_0_, ...), custom_call_target="tpu_custom_call" | custom-call | flops 2717908992 | bytes 4000000 | tf_op jit(solution)/shard_map/back2/pallas_call | solution.py:26
  51.3 1.4 join2.1
  52.7 1.3 collective-permute-start.10
  54.0 1.5 collective-permute-start.11
  55.5 4.0 %back1.1 = (f32[768,256]{1,0:T(8,128)S(1)}, bf16[256,512]{1,0:T(8,128)(2,1)}, bf16[512,256]{1,0:T(8,128)(2,1)}, bf16[768,256]{1,0:T(8,128)(2,1)}, bf16[768,512]{1,0:T(8,128)(2,1)}, /*index=5*/bf16[768,512]{1,0:T(8,128)(2,1)}) custom-call(bf16[768,256]{1,0:T(8,128)(2,1)S(1)} %get-tuple-element.86.refs_0_, ...), custom_call_target="tpu_custom_call" | custom-call | flops 2717908992 | bytes 4000000 | tf_op jit(solution)/shard_map/back1/pallas_call | solution.py:26
  59.5 1.5 join1.1
  61.9 4.0 %back0.1 = (f32[768,256]{1,0:T(8,128)S(1)}, bf16[256,512]{1,0:T(8,128)(2,1)}, bf16[512,256]{1,0:T(8,128)(2,1)}, bf16[768,256]{1,0:T(8,128)(2,1)}, bf16[768,512]{1,0:T(8,128)(2,1)}, /*index=5*/bf16[768,512]{1,0:T(8,128)(2,1)}) custom-call(bf16[768,256]{1,0:T(8,128)(2,1)S(1)} %get-tuple-element.95.refs_0_, bf16[768,256]{1,0:T(8,128)(2,1)S(1)} %copy-done.4, ...), custom_call_target="tpu_custom_call" | custom-call | flops 2717908992 | bytes 4000000 | tf_op jit(solution)/shard_map/back0/pallas_call | solution.py:26
  66.7 1.4 collective-permute-start.12
  68.2 1.5 collective-permute-start.13
  69.7 4.6 %collective-permute-done.12.refs_3_ = bf16[128,256]{1,0:T(8,128)(2,1)S(1)} collective-permute-done((bf16[128,256]{1,0:T(8,128)(2,1)S(1)}, bf16[128,256]{1,0:T(8,128)(2,1)S(1)}, u32[]{:S(2)}, u32[]{:S(2)}) %collective-permute-start.12) | collective-permute-done | bytes 65568 | tf_op jit(solution)/shard_map/ppermute | solution.py:231
  74.3 1.1 join0.1
  75.4 84.2 %all-reduce.3.cloned.1.call-done = (bf16[1,256,512]{2,1,0:T(8,128)(2,1)}, bf16[1,256,512]{2,1,0:T(8,128)(2,1)}, bf16[1,256,512]{2,1,0:T(8,128)(2,1)}, bf16[1,512...) async-done(((bf16[1,256,512]{2,1,0:T(8,128)(2,1)}, bf16[1,256,512]{2,1,0:T(8,128)(2,1)}, bf16[1,256,512]{2,1,0:T(8,128)(2,1)}, ...) | async-done | bytes 1572880 | tf_op jit(solution)/shard_map/psum | solution.py:327
  159.6 2.4 %maximum_convert_fusion = f32[3,256,512]{2,1,0:T(8,128)} fusion(bf16[1,256,512]{2,1,0:T(8,128)(2,1)} %get-tuple-element.109, bf16[1,256,512]{2,1,0:T(8,128)(2,1)} %get-tuple-element.110, bf16[1,256,512]{2,1,0:T(8,128)(2,1)} %get-tuple-element.111), kind=kLoop, calls=%fused_computation | loop fusion | flops 1179648 | bytes 2359296 | tf_op jit(solution)/shard_map/convert_element_type | solution.py:344
  162.1 1.3 maximum_convert_fusion.1
  (48 shorter events, 6.5 us)
Async XLA Ops:
  7.2 14.3 %copy-start = (bf16[3,256,512]{2,1,0:T(8,128)(2,1)S(1)}, bf16[3,256,512]{2,1,0:T(8,128)(2,1)}, u32[]{:S(2)}) copy-start(bf16[3,256,512]{2,1,0:T(8,128)(2,1)} %refs_3_.5) | copy-start | bytes 2359300
  7.2 152.5 %all-reduce.3.cloned.1.call-start = ((), (), s32[]{:S(2)}) async-start(), calls=%async_computation | async-start | bytes 3145728 | tf_op jit(solution)/shard_map/psum | solution.py:327
  7.2 14.2 %collective-permute-start = (bf16[3,256,512]{2,1,0:T(8,128)(2,1)}, bf16[3,256,512]{2,1,0:T(8,128)(2,1)S(1)}, u32[]{:S(2)}, u32[]{:S(2)}) collective-permute-start(bf16[3,256,512]{2,1,0:T(8,128)(2,1)} %refs_3_.5), channel_id=1, source_target_pairs={{0,1},{1,0},{2,3},{3,2},{4,5},{5,4},{6,7},{7,6},{8,9},{9,8},{10,11... | collective-permute-start | bytes 2359304 | tf_op jit(solution)/shard_map/ppermute | solution.py:236
  7.7 13.7 %collective-permute-start.1 = (bf16[3,512,256]{2,1,0:T(8,128)(2,1)}, bf16[3,512,256]{2,1,0:T(8,128)(2,1)S(1)}, u32[]{:S(2)}, u32[]{:S(2)}) collective-permute-start(bf16[3,512,256]{2,1,0:T(8,128)(2,1)} %refs_5_.11), channel_id=1, source_target_pairs={{0,1},{1,0},{2,3},{3,2},{4,5},{5,4},{6,7},{7,6},{8,9},{9,8},{10,11... | collective-permute-start | bytes 2359304 | tf_op jit(solution)/shard_map/ppermute | solution.py:236
  7.8 1.0 copy-start.3
  8.8 0.7 copy-start.11
  9.5 0.7 copy-start.12
  10.1 11.3 %copy-start.4 = (bf16[768,256]{1,0:T(8,128)(2,1)S(1)}, bf16[768,256]{1,0:T(8,128)(2,1)}, u32[]{:S(2)}) copy-start(bf16[768,256]{1,0:T(8,128)(2,1)} %refs_1_.1) | copy-start | bytes 1179652
  11.5 13.2 %collective-permute-start.2 = (bf16[128,256]{1,0:T(8,128)(2,1)}, bf16[128,256]{1,0:T(8,128)(2,1)S(1)}, u32[]{:S(2)}, u32[]{:S(2)}) collective-permute-start(bf16[128,256]{1,0:T(8,128)(2,1)} %get-tuple-element.61), channel_id=1, source_target_pairs={{0,4},{4,8},{8,12},{1,5},{5,9},{9,13},{2,6},{6,10},{10,14},{3,7},{... | collective-permute-start | bytes 196616 | tf_op jit(solution)/shard_map/ppermute | solution.py:231
  16.4 8.3 %collective-permute-start.3 = (bf16[128,256]{1,0:T(8,128)(2,1)S(1)}, bf16[128,256]{1,0:T(8,128)(2,1)S(1)}, u32[]{:S(2)}, u32[]{:S(2)}) collective-permute-start(bf16[128,256]{1,0:T(8,128)(2,1)S(1)} %get-tuple-element.62), channel_id=1, source_target_pairs={{0,2},{2,0},{1,3},{3,1},{4,6},{6,4},{5,7},{7,5},{8,10},{10,8},{9,1... | collective-permute-start | bytes 196616 | tf_op jit(solution)/shard_map/ppermute | solution.py:236
  18.7 1.1 copy-start.6
  21.5 1.1 copy-start.1
  22.6 2.1 %copy-start.2 = (bf16[3,512,256]{2,1,0:T(8,128)(2,1)S(1)}, bf16[3,512,256]{2,1,0:T(8,128)(2,1)}, u32[]{:S(2)}) copy-start(bf16[3,512,256]{2,1,0:T(8,128)(2,1)} %refs_5_.11) | copy-start | bytes 2359300
  26.0 6.2 %collective-permute-start.4 = (bf16[128,256]{1,0:T(8,128)(2,1)S(1)}, bf16[128,256]{1,0:T(8,128)(2,1)S(1)}, u32[]{:S(2)}, u32[]{:S(2)}) collective-permute-start(bf16[128,256]{1,0:T(8,128)(2,1)S(1)} %get-tuple-element.66), channel_id=1, source_target_pairs={{0,4},{4,8},{8,12},{1,5},{5,9},{9,13},{2,6},{6,10},{10,14},{3,7},{... | collective-permute-start | bytes 196616 | tf_op jit(solution)/shard_map/ppermute | solution.py:231
  29.5 4.3 %collective-permute-start.5 = (bf16[128,256]{1,0:T(8,128)(2,1)S(1)}, bf16[128,256]{1,0:T(8,128)(2,1)S(1)}, u32[]{:S(2)}, u32[]{:S(2)}) collective-permute-start(bf16[128,256]{1,0:T(8,128)(2,1)S(1)} %get-tuple-element.67), channel_id=1, source_target_pairs={{0,2},{2,0},{1,3},{3,1},{4,6},{6,4},{5,7},{7,5},{8,10},{10,8},{9,1... | collective-permute-start | bytes 196616 | tf_op jit(solution)/shard_map/ppermute | solution.py:236
  35.1 6.2 %collective-permute-start.6 = (bf16[128,256]{1,0:T(8,128)(2,1)S(1)}, bf16[128,256]{1,0:T(8,128)(2,1)S(1)}, u32[]{:S(2)}, u32[]{:S(2)}) collective-permute-start(bf16[128,256]{1,0:T(8,128)(2,1)S(1)} %get-tuple-element.72), channel_id=1, source_target_pairs={{0,4},{4,8},{8,12},{1,5},{5,9},{9,13},{2,6},{6,10},{10,14},{3,7},{... | collective-permute-start | bytes 196616 | tf_op jit(solution)/shard_map/ppermute | solution.py:231
  38.6 4.3 %collective-permute-start.7 = (bf16[128,256]{1,0:T(8,128)(2,1)S(1)}, bf16[128,256]{1,0:T(8,128)(2,1)S(1)}, u32[]{:S(2)}, u32[]{:S(2)}) collective-permute-start(bf16[128,256]{1,0:T(8,128)(2,1)S(1)} %get-tuple-element.73), channel_id=1, source_target_pairs={{0,2},{2,0},{1,3},{3,1},{4,6},{6,4},{5,7},{7,5},{8,10},{10,8},{9,1... | collective-permute-start | bytes 196616 | tf_op jit(solution)/shard_map/ppermute | solution.py:236
  39.2 3.7 %copy-start.5 = (f32[768,256]{1,0:T(8,128)S(1)}, f32[768,256]{1,0:T(8,128)}, u32[]{:S(2)}) copy-start(f32[768,256]{1,0:T(8,128)} %refs_4_.5) | copy-start | bytes 2359300
  45.1 6.2 %collective-permute-start.8 = (bf16[128,256]{1,0:T(8,128)(2,1)S(1)}, bf16[128,256]{1,0:T(8,128)(2,1)S(1)}, u32[]{:S(2)}, u32[]{:S(2)}) collective-permute-start(bf16[128,256]{1,0:T(8,128)(2,1)S(1)} %get-tuple-element.83), channel_id=1, source_target_pairs={{4,0},{8,4},{12,8},{5,1},{9,5},{13,9},{6,2},{10,6},{14,10},{7,3},{... | collective-permute-start | bytes 196616 | tf_op jit(solution)/shard_map/ppermute | solution.py:231
  46.6 4.7 %collective-permute-start.9 = (bf16[128,256]{1,0:T(8,128)(2,1)S(1)}, bf16[128,256]{1,0:T(8,128)(2,1)S(1)}, u32[]{:S(2)}, u32[]{:S(2)}) collective-permute-start(bf16[128,256]{1,0:T(8,128)(2,1)S(1)} %get-tuple-element.84), channel_id=1, source_target_pairs={{0,2},{2,0},{1,3},{3,1},{4,6},{6,4},{5,7},{7,5},{8,10},{10,8},{9,1... | collective-permute-start | bytes 196616 | tf_op jit(solution)/shard_map/ppermute | solution.py:236
  52.7 6.8 %collective-permute-start.10 = (bf16[128,256]{1,0:T(8,128)(2,1)S(1)}, bf16[128,256]{1,0:T(8,128)(2,1)S(1)}, u32[]{:S(2)}, u32[]{:S(2)}) collective-permute-start(bf16[128,256]{1,0:T(8,128)(2,1)S(1)} %get-tuple-element.92), channel_id=1, source_target_pairs={{4,0},{8,4},{12,8},{5,1},{9,5},{13,9},{6,2},{10,6},{14,10},{7,3},{... | collective-permute-start | bytes 196616 | tf_op jit(solution)/shard_map/ppermute | solution.py:231
  54.0 5.5 %collective-permute-start.11 = (bf16[128,256]{1,0:T(8,128)(2,1)S(1)}, bf16[128,256]{1,0:T(8,128)(2,1)S(1)}, u32[]{:S(2)}, u32[]{:S(2)}) collective-permute-start(bf16[128,256]{1,0:T(8,128)(2,1)S(1)} %get-tuple-element.93), channel_id=1, source_target_pairs={{0,2},{2,0},{1,3},{3,1},{4,6},{6,4},{5,7},{7,5},{8,10},{10,8},{9,1... | collective-permute-start | bytes 196616 | tf_op jit(solution)/shard_map/ppermute | solution.py:236
  61.0 0.9 copy-start.7
  65.8 0.9 copy-start.9
  66.7 7.6 %copy-start.8 = (f32[768,256]{1,0:T(8,128)S(1)}, f32[768,256]{1,0:T(8,128)}, u32[]{:S(2)}) copy-start(f32[768,256]{1,0:T(8,128)} %copy-done.7) | copy-start | bytes 2359300
  66.7 7.6 %copy-start.10 = (f32[768,256]{1,0:T(8,128)S(1)}, f32[768,256]{1,0:T(8,128)}, u32[]{:S(2)}) copy-start(f32[768,256]{1,0:T(8,128)} %copy-done.9) | copy-start | bytes 2359300
  66.7 7.5 %collective-permute-start.12 = (bf16[128,256]{1,0:T(8,128)(2,1)S(1)}, bf16[128,256]{1,0:T(8,128)(2,1)S(1)}, u32[]{:S(2)}, u32[]{:S(2)}) collective-permute-start(bf16[128,256]{1,0:T(8,128)(2,1)S(1)} %get-tuple-element.101), channel_id=1, source_target_pairs={{4,0},{8,4},{12,8},{5,1},{9,5},{13,9},{6,2},{10,6},{14,10},{7,3},{... | collective-permute-start | bytes 196616 | tf_op jit(solution)/shard_map/ppermute | solution.py:231
  68.2 6.1 %collective-permute-start.13 = (bf16[128,256]{1,0:T(8,128)(2,1)S(1)}, bf16[128,256]{1,0:T(8,128)(2,1)S(1)}, u32[]{:S(2)}, u32[]{:S(2)}) collective-permute-start(bf16[128,256]{1,0:T(8,128)(2,1)S(1)} %get-tuple-element.102), channel_id=1, source_target_pairs={{0,2},{2,0},{1,3},{3,1},{4,6},{6,4},{5,7},{7,5},{8,10},{10,8},{9,1... | collective-permute-start | bytes 196616 | tf_op jit(solution)/shard_map/ppermute | solution.py:236
  159.6 2.5 %copy-start.13 = (bf16[1,512,256]{2,1,0:T(8,128)(2,1)S(1)}, bf16[1,512,256]{2,1,0:T(8,128)(2,1)}, u32[]{:S(2)}) copy-start(bf16[1,512,256]{2,1,0:T(8,128)(2,1)} %get-tuple-element.112) | copy-start | bytes 786436
  159.6 2.5 %copy-start.14 = (bf16[1,512,256]{2,1,0:T(8,128)(2,1)S(1)}, bf16[1,512,256]{2,1,0:T(8,128)(2,1)}, u32[]{:S(2)}) copy-start(bf16[1,512,256]{2,1,0:T(8,128)(2,1)} %get-tuple-element.113) | copy-start | bytes 786436
  159.6 2.5 %copy-start.15 = (bf16[1,512,256]{2,1,0:T(8,128)(2,1)S(1)}, bf16[1,512,256]{2,1,0:T(8,128)(2,1)}, u32[]{:S(2)}) copy-start(bf16[1,512,256]{2,1,0:T(8,128)(2,1)} %get-tuple-element.114) | copy-start | bytes 786436
Sparse Core Ops, SparseCore 0:
  66.9 92.7 all-reduce.2

commit v2 on v1

--- a/solution.py
+++ b/solution.py
@@ -8,10 +8,12 @@
 from jax.sharding import PartitionSpec as P
 
 BLOCK = 128
+LANES = 128
 EPS = 1e-06
 F32 = jnp.float32
 BF16 = jnp.bfloat16
 VMEM = pl.BlockSpec(memory_space=pltpu.VMEM)
+ANY = pl.BlockSpec(memory_space=pl.ANY)
 SMEM = pl.BlockSpec(memory_space=pltpu.SMEM)
 NN = (((1,), (0,)), ((), ()))
 NT = (((1,), (1,)), ((), ()))
@@ -179,26 +181,121 @@
     start_bwd(layer, norm_grad(cot[...], total), weights, received, remote_t, outs)
 
 
-def shadow_bwd_kernel(layer, grad_scale, *refs):
+def shadow_bwd_kernel(layer, grad_scale, pieces, *refs):
     dround, inputs, local_t = refs[:3]
     wi0, wi1, wo0, wo1 = refs[3:7]
     far_x, far_dmsg, far_act, far_dpre = refs[7:11]
-    back, g_in, g_out, dmsg, act, dpre = refs[11:]
+    back = refs[11]
+    grads, dmsg, act, dpre = refs[-4:]
     halves = [(wi0[layer], wo0[layer]), (wi1[layer], wo1[layer])]
     dmsg[...] = mm(local_t[...], dround[...]).astype(BF16)
-    rows = inputs.shape[0]
+    rows, latent = inputs.shape
+    hidden = act.shape[1]
     for r in range(0, rows, 256):
         here = slice(r, r + 256)
         grad, (a, d) = message_grad(inputs[here, :], dmsg[here, :], halves)
         back[here, :] = grad
         act[here, :] = a
         dpre[here, :] = d
-    g_in[...] = (
-        (mm(inputs[...], dpre[...], TN) + mm(far_x[...], far_dpre[...], TN)) * grad_scale
-    ).astype(BF16)
-    g_out[...] = (
-        (mm(act[...], dmsg[...], TN) + mm(far_act[...], far_dmsg[...], TN)) * grad_scale
-    ).astype(BF16)
+    g_in = (mm(inputs[...], dpre[...], TN) + mm(far_x[...], far_dpre[...], TN)) * grad_scale
+    for j in range(hidden // LANES):
+        grads[j * latent : (j + 1) * latent, :] = g_in[:, j * LANES : (j + 1) * LANES]
+    g_out = (mm(act[...], dmsg[...], TN) + mm(far_act[...], far_dmsg[...], TN)) * grad_scale
+    for j in range(latent // LANES):
+        at = hidden // LANES * latent + j * hidden
+        grads[at : at + hidden, :] = g_out[:, j * LANES : (j + 1) * LANES]
+    outs = refs[12:-4]
+    for lo, hi, axes in pieces:
+        n = lax.axis_size(axes[0])
+        scatter_parts(grads.at[lo:hi], axes[0], outs[:n])
+        outs = outs[n:]
+
+
+def scatter_parts(block, axis, outs):
+    n = lax.axis_size(axis)
+    m = block.shape[0] // n
+    me = lax.axis_index(axis)
+    for s, out in enumerate(outs):
+        part = block[pl.ds(pl.multiple_of(lax.rem(me + s, n) * m, m), m), :]
+        out[...] = part.astype(out.dtype)
+
+
+def add_scatter_kernel(axis, parts, *refs):
+    acc = refs[-1]
+    acc[...] = refs[0][...]
+    for part in refs[1:parts]:
+        acc[...] += part[...].astype(F32)
+    scatter_parts(acc, axis, refs[parts:-1])
+
+
+def add_kernel(*refs):
+    total = refs[0][...]
+    for part in refs[1:-1]:
+        total = total + part[...].astype(F32)
+    refs[-1][...] = total.astype(BF16)
+
+
+def place(axis, parts, out):
+    n = lax.axis_size(axis)
+    m = parts[0].shape[0]
+    me = lax.axis_index(axis)
+    for s, part in enumerate(parts):
+        at = pl.ds(pl.multiple_of(lax.rem(me + n - s, n) * m, m), m)
+        out[at, :] = part[...].astype(out.dtype)
+
+
+def place_kernel(axis, *refs):
+    place(axis, refs[:-1], refs[-1])
+
+
+def write_kernel(layer, pieces, kept, *refs):
+    out_in, out_out, grads, slab_in, slab_out, sem = refs[-6:]
+    parts = refs[kept : kept + sum(lax.axis_size(axes[0]) for _, _, axes in pieces)]
+    for lo, hi, axes in pieces:
+        n = lax.axis_size(axes[0])
+        place(axes[0], parts[:n], grads.at[lo:hi])
+        parts = parts[n:]
+    latent, hidden = slab_in.shape
+    for j in range(hidden // LANES):
+        slab_in[:, j * LANES : (j + 1) * LANES] = grads[j * latent : (j + 1) * latent, :]
+    first = pltpu.make_async_copy(slab_in, out_in.at[layer], sem.at[0])
+    first.start()
+    for j in range(latent // LANES):
+        at = hidden // LANES * latent + j * hidden
+        slab_out[:, j * LANES : (j + 1) * LANES] = grads[at : at + hidden, :]
+    second = pltpu.make_async_copy(slab_out, out_out.at[layer], sem.at[1])
+    second.start()
+    first.wait()
+    second.wait()
+
+
+def shifted(parts, axis):
+    return [around(x, axis, s + 1) for s, x in enumerate(parts)]
+
+
+def summed_piece(parts, axes, name):
+    n0, n1 = lax.axis_size(axes[0]), lax.axis_size(axes[1])
+    m = parts[0].shape[0]
+    got = shifted(parts[1:], axes[0])
+    parts = call(
+        functools.partial(add_scatter_kernel, axes[1], n0),
+        [((m // n1, LANES), F32)] + [((m // n1, LANES), BF16)] * (n1 - 1),
+        [parts[0], *got],
+        1_000_000,
+        scratch=[pltpu.VMEM((m, LANES), F32)],
+        name=f"add_{name}",
+    )
+    got = shifted(parts[1:], axes[1])
+    (own,) = call(add_kernel, [((m // n1, LANES), BF16)], [parts[0], *got], 1_000_000, name=f"end_{name}")
+    got = shifted([own] * (n1 - 1), axes[1])
+    (own,) = call(
+        functools.partial(place_kernel, axes[1]),
+        [((m, LANES), BF16)],
+        [own, *got],
+        1_000_000,
+        name=f"place_{name}",
+    )
+    return [own, *shifted([own] * (n0 - 1), axes[0])]
 
 
 def gathered_grad(dtotal, back, returned, spread):
@@ -311,20 +408,55 @@
         2 * far_rows * ffn,
         name="turn",
     )
-    summed = []
+    grad_rows = 2 * latent * half // LANES
+    pieces = [(0, grad_rows, ("basin", "chain"))]
+    part_shapes = []
+    for lo, hi, axes in pieces:
+        n = lax.axis_size(axes[0])
+        m = (hi - lo) // n
+        part_shapes += [((m, LANES), F32)] + [((m, LANES), BF16)] * (n - 1)
+    written = []
     for layer in reversed(range(layers)):
         dtotal, dround = outs[:2]
         far_saved = outs[2:6]
         returned = exchange(outs[6], outs[7:], -1)
-        back, g_in, g_out, *_ = call(
-            functools.partial(shadow_bwd_kernel, layer, grad_scale),
-            [((rows, latent), F32), act16(latent, half), act16(half), act16(rows)]
-            + [act16(rows, half)] * 2,
+        back, *parts = call(
+            functools.partial(shadow_bwd_kernel, layer, grad_scale, pieces),
+            [((rows, latent), F32)] + part_shapes,
             [dround, inputs[layer], local_t, *weights, *far_saved],
             3 * rows * ffn + 2 * rows * rows * latent,
+            scratch=[
+                pltpu.VMEM((grad_rows, LANES), F32),
+                pltpu.VMEM((rows, latent), BF16),
+                pltpu.VMEM((rows, half), BF16),
+                pltpu.VMEM((rows, half), BF16),
+            ],
             name=f"back{layer}",
         )
-        summed.append(lax.psum((g_in, g_out), ("chain", "basin")))
+        ready = []
+        for i, (_, _, axes) in enumerate(pieces):
+            n = lax.axis_size(axes[0])
+            ready += summed_piece(parts[:n], axes, f"{layer}_{i}")
+            parts = parts[n:]
+        written = pl.pallas_call(
+            functools.partial(write_kernel, layer, pieces, len(written)),
+            out_shape=[
+                jax.ShapeDtypeStruct((layers, latent, half), F32),
+                jax.ShapeDtypeStruct((layers, half, latent), F32),
+            ],
+            in_specs=[ANY] * len(written) + [VMEM] * len(ready),
+            out_specs=[ANY] * 2,
+            scratch_shapes=[
+                pltpu.VMEM((grad_rows, LANES), F32),
+                pltpu.VMEM((latent, half), F32),
+                pltpu.VMEM((half, latent), F32),
+                pltpu.SemaphoreType.DMA((2,)),
+            ],
+            input_output_aliases={i: i for i in range(len(written))},
+            compiler_params=pltpu.CompilerParams(vmem_limit_bytes=32 * 1024 * 1024),
+            cost_estimate=pl.CostEstimate(flops=0, bytes_accessed=4_000_000, transcendentals=0),
+            name=f"write{layer}",
+        )(*written, *ready)
         if layer:
             outs = call(
                 functools.partial(post_bwd_kernel, layer - 1, groups),
@@ -341,9 +473,7 @@
         2 * rows * sent_rows * latent,
         name="join0",
     )
-    summed_in = jnp.stack([x for x, _ in summed[::-1]]).astype(F32)
-    summed_out = jnp.stack([x for _, x in summed[::-1]]).astype(F32)
-    return (grad, summed_in, summed_out)
+    return (grad, *written)
 
 
 def solution(mesh):

time: 171 us -> 114 us (0.67)
  waiting for transfers between devices: 92.3 us -> 17.5 us
  starting transfers between devices: 23 us -> 58.5 us
  between operations: 14.2 us -> 1.12 us
  other arithmetic: 3.71 us -> 0 us
  local copies, waits for them, and re-layouts: 7.14 us -> 5.37 us
    psum x1 -> x0, waiting for transfers between devices: 84.2 us -> none  [shards(): summed.append(lax.psum((g_in, g_out), ('chain', 'basin')))]
    ppermute x8 -> x32, starting transfers between devices: 6.9 us -> 42.6 us  [around(): return lax.ppermute(x, axis, [(i, (i + distance) % n) for i in range(n)])]
    ppermute x8 -> x32, waiting for transfers between devices: 3.33 us -> 13.1 us  [around(): return lax.ppermute(x, axis, [(i, (i + distance) % n) for i in range(n)])]
    convert_element_type x2 -> x0, other arithmetic: 3.71 us -> none  [the longest x1 2.45 us: shards(): summed_in = jnp.stack([x for x, _ in summed[::-1]]).astype(F32)]
    pallas_call x0 -> x3, Pallas kernels: none -> 3.41 us  [shards(): pl.pallas_call(functools.partial(write_kernel, layer, pieces, len(written...]
    pallas_call x14 -> x23, Pallas kernels: 29.9 us -> 27.9 us  [call(): pl.pallas_call(body, out_shape=[jax.ShapeDtypeStruct(s, d) for s, d in ou...]
    unnamed x33 -> x19, local copies, waits for them, and re-layouts: 7.14 us -> 5.37 us
  transfers between devices with their start and end apart: 15 -> 38, of which waited for: 5 -> 9; matrix products, arithmetic and copies ran while one was open for 0% -> 1% of each run, Pallas kernels for 11% -> 22%
where the time goes in v2:
time: 114 us
  starting transfers between devices  58.5 us (51%)
  Pallas kernels  31.3 us (27%)
  waiting for transfers between devices  17.5 us (15%)
  local copies, waits for them, and re-layouts  5.37 us (5%)
    ppermute x32, starting transfers between devices, around(): return lax.ppermute(x, axis, [(i, (i + distance) % n) for i in range(n)])  42.6 us
    pallas_call x23, Pallas kernels, call(): pl.pallas_call(body, out_shape=[jax.ShapeDtypeStruct(s, d) for s, d in ou...  27.9 us
    ppermute x6, starting transfers between devices, along(): lax.ppermute(x, axis, [(i, i + distance) for i in range(n) if 0 <= i + di...  15.9 us
    ppermute x32, waiting for transfers between devices, around(): return lax.ppermute(x, axis, [(i, (i + distance) % n) for i in range(n)])  13.1 us
    unnamed x19, local copies, waits for them, and re-layouts  5.37 us
    ppermute x6, waiting for transfers between devices, along(): lax.ppermute(x, axis, [(i, i + distance) for i in range(n) if 0 <= i + di...  4.44 us
    pallas_call x3, Pallas kernels, shards(): pl.pallas_call(functools.partial(write_kernel, layer, pieces, len(written...  3.41 us
  transfers between devices with their start and end apart: 38, of which 9 were waited for; matrix products, arithmetic and copies ran while one was open for 1% of the time, Pallas kernels for 22%

profile of v2, /device:TPU:0, one launch (start us, length us, event | category | flops | bytes accessed | tf_op | source)
XLA Modules:
  0.0 113.8 jit_solution(13552325395126148626)
XLA Ops:
  4.9 4.9 %collective-permute-start.2 = (bf16[128,256]{1,0:T(8,128)(2,1)}, bf16[128,256]{1,0:T(8,128)(2,1)S(1)}, u32[]{:S(2)}, u32[]{:S(2)}) collective-permute-start(bf16[128,256]{1,0:T(8,128)(2,1)} %get-tuple-element.79), channel_id=1, source_target_pairs={{0,4},{4,8},{8,12},{1,5},{5,9},{9,13},{2,6},{6,10},{10,14},{3,7},{... | collective-permute-start | bytes 196616 | tf_op jit(solution)/shard_map/ppermute | solution.py:328
  9.8 1.6 %collective-permute-start.3 = (bf16[128,256]{1,0:T(8,128)(2,1)S(1)}, bf16[128,256]{1,0:T(8,128)(2,1)S(1)}, u32[]{:S(2)}, u32[]{:S(2)}) collective-permute-start(bf16[128,256]{1,0:T(8,128)(2,1)S(1)} %get-tuple-element.80), channel_id=1, source_target_pairs={{0,2},{2,0},{1,3},{3,1},{4,6},{6,4},{5,7},{7,5},{8,10},{10,8},{9,1... | collective-permute-start | bytes 196616 | tf_op jit(solution)/shard_map/ppermute | solution.py:333
  13.3 1.6 %adjacency.1 = (bf16[768,768]{1,0:T(8,128)(2,1)S(1)}, bf16[768,768]{1,0:T(8,128)(2,1)S(1)}, bf16[768,256]{1,0:T(8,128)(2,1)S(1)}, bf16[256,768]{1,0:T(8,128)(2,1)S(1)}) custom-call(s32[6,4]{1,0:T(8,128)S(1)} %copy.15.index, bf16[6,4,128,128]{3,2,1,0:T(8,128)(2,1)S(1)} %copy-done.6, bf16[128,768]{1,0:T(8,128)(2,1)S(1)} %get-tuple-element.74.pick_self), custom_call_target="tpu_custom_call" | custom-call | flops 150994944 | bytes 4000000 | tf_op jit(solution)/shard_map/adjacency/pallas_call | solution.py:28
  16.1 2.1 %local0.1 = (f32[768,256]{1,0:T(8,128)S(1)}, bf16[768,256]{1,0:T(8,128)(2,1)}) custom-call(bf16[768,256]{1,0:T(8,128)(2,1)S(1)} %copy-done.4, bf16[768,768]{1,0:T(8,128)(2,1)S(1)} %get-tuple-element.75.local, bf16[3,256,512]{2,1,0:T(8,128)(2,1)S(1)} %copy-done, bf16[3,256,512]{2,1,0:T(8,128)(2,1)S(1)} %collective-permute-done.wi1.refs_5_.refs_6_.refs_4_, ...), custom_call_target="tpu_custom_call" | custom-call | flops 1107296256 | bytes 4000000 | tf_op jit(solution)/shard_map/local0/pallas_call | solution.py:28
  19.4 3.5 %collective-permute-start.4 = (bf16[128,256]{1,0:T(8,128)(2,1)S(1)}, bf16[128,256]{1,0:T(8,128)(2,1)S(1)}, u32[]{:S(2)}, u32[]{:S(2)}) collective-permute-start(bf16[128,256]{1,0:T(8,128)(2,1)S(1)} %get-tuple-element.84), channel_id=1, source_target_pairs={{0,4},{4,8},{8,12},{1,5},{5,9},{9,13},{2,6},{6,10},{10,14},{3,7},{... | collective-permute-start | bytes 196616 | tf_op jit(solution)/shard_map/ppermute | solution.py:328
  23.5 2.1 %local1.1 = (f32[768,256]{1,0:T(8,128)S(1)}, bf16[768,256]{1,0:T(8,128)(2,1)}) custom-call(bf16[768,256]{1,0:T(8,128)(2,1)S(1)} %get-tuple-element.82.inputs.refs_1_, bf16[768,768]{1,0:T(8,128)(2,1)S(1)} %get-tuple-element.75.local, bf16[3,256,512]{2,1,0:T(8,128)(2,1)S(1)} %copy-done, ...), custom_call_target="tpu_custom_call" | custom-call | flops 1107296256 | bytes 4000000 | tf_op jit(solution)/shard_map/local1/pallas_call | solution.py:28
  25.6 1.7 %collective-permute-done.5.refs_9_.refs_12_ = bf16[128,256]{1,0:T(8,128)(2,1)S(1)} collective-permute-done((bf16[128,256]{1,0:T(8,128)(2,1)S(1)}, bf16[128,256]{1,0:T(8,128)(2,1)S(1)}, u32[]{:S(2)}, u32[]{:S(2)}) %collective-permute-start.5) | collective-permute-done | bytes 65568 | tf_op jit(solution)/shard_map/ppermute | solution.py:333
  28.5 3.5 %collective-permute-start.6 = (bf16[128,256]{1,0:T(8,128)(2,1)S(1)}, bf16[128,256]{1,0:T(8,128)(2,1)S(1)}, u32[]{:S(2)}, u32[]{:S(2)}) collective-permute-start(bf16[128,256]{1,0:T(8,128)(2,1)S(1)} %get-tuple-element.90), channel_id=1, source_target_pairs={{0,4},{4,8},{8,12},{1,5},{5,9},{9,13},{2,6},{6,10},{10,14},{3,7},{... | collective-permute-start | bytes 196616 | tf_op jit(solution)/shard_map/ppermute | solution.py:328
  32.6 2.1 %local2.1 = (f32[768,256]{1,0:T(8,128)S(1)}, bf16[768,256]{1,0:T(8,128)(2,1)}) custom-call(bf16[768,256]{1,0:T(8,128)(2,1)S(1)} %get-tuple-element.87.inputs.refs_1_, bf16[768,768]{1,0:T(8,128)(2,1)S(1)} %get-tuple-element.75.local, bf16[3,256,512]{2,1,0:T(8,128)(2,1)S(1)} %copy-done, ...), custom_call_target="tpu_custom_call" | custom-call | flops 1107296256 | bytes 4000000 | tf_op jit(solution)/shard_map/local2/pallas_call | solution.py:28
  34.7 1.6 %collective-permute-done.7.refs_10_ = bf16[128,256]{1,0:T(8,128)(2,1)S(1)} collective-permute-done((bf16[128,256]{1,0:T(8,128)(2,1)S(1)}, bf16[128,256]{1,0:T(8,128)(2,1)S(1)}, u32[]{:S(2)}, u32[]{:S(2)}) %collective-permute-start.7) | collective-permute-done | bytes 65568 | tf_op jit(solution)/shard_map/ppermute | solution.py:333
  36.4 2.2 %turn.1 = (f32[768,256]{1,0:T(8,128)S(1)}, bf16[768,256]{1,0:T(8,128)(2,1)S(1)}, bf16[256,256]{1,0:T(8,128)(2,1)S(1)}, bf16[256,256]{1,0:T(8,128)(2,1)S(1)}, bf1...) custom-call(f32[768,256]{1,0:T(8,128)S(1)} %get-tuple-element.86.ref, ...), custom_call_target="tpu_custom_call" | custom-call | flops 536870912 | bytes 4000000 | tf_op jit(solution)/shard_map/turn/pallas_call | solution.py:28
  38.5 1.5 %collective-permute-start.8 = (bf16[128,256]{1,0:T(8,128)(2,1)S(1)}, bf16[128,256]{1,0:T(8,128)(2,1)S(1)}, u32[]{:S(2)}, u32[]{:S(2)}) collective-permute-start(bf16[128,256]{1,0:T(8,128)(2,1)S(1)} %get-tuple-element.101), channel_id=1, source_target_pairs={{4,0},{8,4},{12,8},{5,1},{9,5},{13,9},{6,2},{10,6},{14,10},{7,3},{... | collective-permute-start | bytes 196616 | tf_op jit(solution)/shard_map/ppermute | solution.py:328
  40.6 3.2 %back2.1 = (f32[768,256]{1,0:T(8,128)S(1)}, f32[1024,128]{1,0:T(8,128)S(1)}, bf16[1024,128]{1,0:T(8,128)(2,1)S(1)}) custom-call(bf16[768,256]{1,0:T(8,128)(2,1)S(1)} %get-tuple-element.93.refs_0_, bf16[768,256]{1,0:T(8,128)(2,1)S(1)} %get-tuple-element.87.inputs.refs_1_, bf16[768,768]{1,0:T(8,128)(2,1)S(1)} %get-tuple-element.94.refs_2_, ...), custom_call_target="tpu_custom_call" | custom-call | flops 2717908992 | bytes 4000000 | tf_op jit(solution)/shard_map/back2/pallas_call | solution.py:28
  43.8 1.6 %collective-permute-start.14 = (bf16[1024,128]{1,0:T(8,128)(2,1)S(1)}, bf16[1024,128]{1,0:T(8,128)(2,1)S(1)}, u32[]{:S(2)}, u32[]{:S(2)}) collective-permute-start(bf16[1024,128]{1,0:T(8,128)(2,1)S(1)} %get-tuple-element.122), channel_id=1, source_target_pairs={{0,2},{2,0},{1,3},{3,1},{4,6},{6,4},{5,7},{7,5},{8,10},{10,8},{9,1... | collective-permute-start | bytes 786440 | tf_op jit(solution)/shard_map/ppermute | solution.py:333
  45.4 1.4 %join2.1 = (f32[768,256]{1,0:T(8,128)S(1)}, bf16[768,256]{1,0:T(8,128)(2,1)S(1)}, bf16[256,256]{1,0:T(8,128)(2,1)S(1)}, bf16[256,256]{1,0:T(8,128)(2,1)S(1)}, bf...) custom-call(f32[768,256]{1,0:T(8,128)S(1)} %get-tuple-element.92.ref, ...), custom_call_target="tpu_custom_call" | custom-call | flops 536870912 | bytes 4000000 | tf_op jit(solution)/shard_map/join2/pallas_call | solution.py:28
  48.7 3.2 %back1.1 = (f32[768,256]{1,0:T(8,128)S(1)}, f32[1024,128]{1,0:T(8,128)S(1)}, bf16[1024,128]{1,0:T(8,128)(2,1)S(1)}) custom-call(bf16[768,256]{1,0:T(8,128)(2,1)S(1)} %get-tuple-element.104.refs_0_, bf16[768,256]{1,0:T(8,128)(2,1)S(1)} %get-tuple-element.82.inputs.refs_1_, bf16[768,768]{1,0:T(8,128)(2,1)S(1)} %get-tuple-element.94.refs_2_, ...), custom_call_target="tpu_custom_call" | custom-call | flops 2717908992 | bytes 4000000 | tf_op jit(solution)/shard_map/back1/pallas_call | solution.py:28
  51.9 1.6 %collective-permute-start.22 = (bf16[1024,128]{1,0:T(8,128)(2,1)S(1)}, bf16[1024,128]{1,0:T(8,128)(2,1)S(1)}, u32[]{:S(2)}, u32[]{:S(2)}) collective-permute-start(bf16[1024,128]{1,0:T(8,128)(2,1)S(1)} %get-tuple-element.130), channel_id=1, source_target_pairs={{0,2},{2,0},{1,3},{3,1},{4,6},{6,4},{5,7},{7,5},{8,10},{10,8},{9,1... | collective-permute-start | bytes 786440 | tf_op jit(solution)/shard_map/ppermute | solution.py:333
  55.1 3.2 %back0.1 = (f32[768,256]{1,0:T(8,128)S(1)}, f32[1024,128]{1,0:T(8,128)S(1)}, bf16[1024,128]{1,0:T(8,128)(2,1)S(1)}) custom-call(bf16[768,256]{1,0:T(8,128)(2,1)S(1)} %get-tuple-element.113.refs_0_, bf16[768,256]{1,0:T(8,128)(2,1)S(1)} %copy-done.4, bf16[768,768]{1,0:T(8,128)(2,1)S(1)} %get-tuple-element.94.refs_2_, bf16[3,256,512]{2,1,0:T(8,128)(2,1)S(1)} %copy-done, ...), custom_call_target="tpu_custom_call" | custom-call | flops 2717908992 | bytes 4000000 | tf_op jit(solution)/shard_map/back0/pallas_call | solution.py:28
  59.0 3.2 %collective-permute-start.15 = (bf16[256,128]{1,0:T(8,128)(2,1)S(1)}, bf16[256,128]{1,0:T(8,128)(2,1)S(1)}, u32[]{:S(2)}, u32[]{:S(2)}) collective-permute-start(bf16[256,128]{1,0:T(8,128)(2,1)S(1)} %get-tuple-element.124), channel_id=1, source_target_pairs={{0,4},{4,8},{8,12},{12,0},{1,5},{5,9},{9,13},{13,1},{2,6},{6,10},{... | collective-permute-start | bytes 196616 | tf_op jit(solution)/shard_map/ppermute | solution.py:333
  62.1 1.5 %collective-permute-start.16 = (bf16[256,128]{1,0:T(8,128)(2,1)S(1)}, bf16[256,128]{1,0:T(8,128)(2,1)S(1)}, u32[]{:S(2)}, u32[]{:S(2)}) collective-permute-start(bf16[256,128]{1,0:T(8,128)(2,1)S(1)} %get-tuple-element.125), channel_id=1, source_target_pairs={{0,8},{4,12},{8,0},{12,4},{1,9},{5,13},{9,1},{13,5},{2,10},{6,14},... | collective-permute-start | bytes 196616 | tf_op jit(solution)/shard_map/ppermute | solution.py:333
  63.6 2.8 %collective-permute-start.17 = (bf16[256,128]{1,0:T(8,128)(2,1)S(1)}, bf16[256,128]{1,0:T(8,128)(2,1)S(1)}, u32[]{:S(2)}, u32[]{:S(2)}) collective-permute-start(bf16[256,128]{1,0:T(8,128)(2,1)S(1)} %get-tuple-element.126), channel_id=1, source_target_pairs={{0,12},{4,0},{8,4},{12,8},{1,13},{5,1},{9,5},{13,9},{2,14},{6,2},{... | collective-permute-start | bytes 196616 | tf_op jit(solution)/shard_map/ppermute | solution.py:333
  66.7 3.3 %collective-permute-start.24 = (bf16[256,128]{1,0:T(8,128)(2,1)S(1)}, bf16[256,128]{1,0:T(8,128)(2,1)S(1)}, u32[]{:S(2)}, u32[]{:S(2)}) collective-permute-start(bf16[256,128]{1,0:T(8,128)(2,1)S(1)} %get-tuple-element.133), channel_id=1, source_target_pairs={{0,8},{4,12},{8,0},{12,4},{1,9},{5,13},{9,1},{13,5},{2,10},{6,14},... | collective-permute-start | bytes 196616 | tf_op jit(solution)/shard_map/ppermute | solution.py:333
  70.6 1.7 %collective-permute-start.31 = (bf16[256,128]{1,0:T(8,128)(2,1)S(1)}, bf16[256,128]{1,0:T(8,128)(2,1)S(1)}, u32[]{:S(2)}, u32[]{:S(2)}) collective-permute-start(bf16[256,128]{1,0:T(8,128)(2,1)S(1)} %get-tuple-element.140), channel_id=1, source_target_pairs={{0,4},{4,8},{8,12},{12,0},{1,5},{5,9},{9,13},{13,1},{2,6},{6,10},{... | collective-permute-start | bytes 196616 | tf_op jit(solution)/shard_map/ppermute | solution.py:333
  72.3 2.1 %collective-permute-start.32 = (bf16[256,128]{1,0:T(8,128)(2,1)S(1)}, bf16[256,128]{1,0:T(8,128)(2,1)S(1)}, u32[]{:S(2)}, u32[]{:S(2)}) collective-permute-start(bf16[256,128]{1,0:T(8,128)(2,1)S(1)} %get-tuple-element.141), channel_id=1, source_target_pairs={{0,8},{4,12},{8,0},{12,4},{1,9},{5,13},{9,1},{13,5},{2,10},{6,14},... | collective-permute-start | bytes 196616 | tf_op jit(solution)/shard_map/ppermute | solution.py:333
  75.9 4.8 %collective-permute-start.20 = (bf16[256,128]{1,0:T(8,128)(2,1)S(1)}, bf16[256,128]{1,0:T(8,128)(2,1)S(1)}, u32[]{:S(2)}, u32[]{:S(2)}) collective-permute-start(bf16[256,128]{1,0:T(8,128)(2,1)S(1)} %end_2_0.1.refs_0_), channel_id=1, source_target_pairs={{0,12},{4,0},{8,4},{12,8},{1,13},{5,1},{9,5},{13,9},{2,14},{6,2},{... | collective-permute-start | bytes 196616 | tf_op jit(solution)/shard_map/ppermute | solution.py:333
  81.3 4.3 %collective-permute-start.28 = (bf16[256,128]{1,0:T(8,128)(2,1)S(1)}, bf16[256,128]{1,0:T(8,128)(2,1)S(1)}, u32[]{:S(2)}, u32[]{:S(2)}) collective-permute-start(bf16[256,128]{1,0:T(8,128)(2,1)S(1)} %end_1_0.1.refs_0_), channel_id=1, source_target_pairs={{0,12},{4,0},{8,4},{12,8},{1,13},{5,1},{9,5},{13,9},{2,14},{6,2},{... | collective-permute-start | bytes 196616 | tf_op jit(solution)/shard_map/ppermute | solution.py:333
  86.4 2.4 %collective-permute-done.19.refs_2_ = bf16[256,128]{1,0:T(8,128)(2,1)S(1)} collective-permute-done((bf16[256,128]{1,0:T(8,128)(2,1)S(1)}, bf16[256,128]{1,0:T(8,128)(2,1)S(1)}, u32[]{:S(2)}, u32[]{:S(2)}) %collective-permute-start.19) | collective-permute-done | bytes 65568 | tf_op jit(solution)/shard_map/ppermute | solution.py:333
  89.8 1.9 %collective-permute-start.35 = (bf16[256,128]{1,0:T(8,128)(2,1)S(1)}, bf16[256,128]{1,0:T(8,128)(2,1)S(1)}, u32[]{:S(2)}, u32[]{:S(2)}) collective-permute-start(bf16[256,128]{1,0:T(8,128)(2,1)S(1)} %end_0_0.1.refs_0_), channel_id=1, source_target_pairs={{0,8},{4,12},{8,0},{12,4},{1,9},{5,13},{9,1},{13,5},{2,10},{6,14},... | collective-permute-start | bytes 196616 | tf_op jit(solution)/shard_map/ppermute | solution.py:333
  95.7 2.2 %collective-permute-done.34.refs_1_ = bf16[256,128]{1,0:T(8,128)(2,1)S(1)} collective-permute-done((bf16[256,128]{1,0:T(8,128)(2,1)S(1)}, bf16[256,128]{1,0:T(8,128)(2,1)S(1)}, u32[]{:S(2)}, u32[]{:S(2)}) %collective-permute-start.34) | collective-permute-done | bytes 65568 | tf_op jit(solution)/shard_map/ppermute | solution.py:333
  98.0 1.6 %collective-permute-start.37 = (bf16[1024,128]{1,0:T(8,128)(2,1)S(1)}, bf16[1024,128]{1,0:T(8,128)(2,1)S(1)}, u32[]{:S(2)}, u32[]{:S(2)}) collective-permute-start(bf16[1024,128]{1,0:T(8,128)(2,1)S(1)} %place_0_0.1.refs_2_), channel_id=1, source_target_pairs={{0,2},{2,0},{1,3},{3,1},{4,6},{6,4},{5,7},{7,5},{8,10},{10,8},{9,1... | collective-permute-start | bytes 786440 | tf_op jit(solution)/shard_map/ppermute | solution.py:333
  101.4 4.3 %collective-permute-done.12.refs_3_ = bf16[128,256]{1,0:T(8,128)(2,1)S(1)} collective-permute-done((bf16[128,256]{1,0:T(8,128)(2,1)S(1)}, bf16[128,256]{1,0:T(8,128)(2,1)S(1)}, u32[]{:S(2)}, u32[]{:S(2)}) %collective-permute-start.12) | collective-permute-done | bytes 65568 | tf_op jit(solution)/shard_map/ppermute | solution.py:328
  105.7 3.4 %collective-permute-done.13.refs_4_ = bf16[128,256]{1,0:T(8,128)(2,1)S(1)} collective-permute-done((bf16[128,256]{1,0:T(8,128)(2,1)S(1)}, bf16[128,256]{1,0:T(8,128)(2,1)S(1)}, u32[]{:S(2)}, u32[]{:S(2)}) %collective-permute-start.13) | collective-permute-done | bytes 65568 | tf_op jit(solution)/shard_map/ppermute | solution.py:333
  (89 shorter events, 30.9 us)
Async XLA Ops:
  0.6 14.2 %collective-permute-start = (bf16[3,256,512]{2,1,0:T(8,128)(2,1)}, bf16[3,256,512]{2,1,0:T(8,128)(2,1)S(1)}, u32[]{:S(2)}, u32[]{:S(2)}) collective-permute-start(bf16[3,256,512]{2,1,0:T(8,128)(2,1)} %refs_3_.5), channel_id=1, source_target_pairs={{0,1},{1,0},{2,3},{3,2},{4,5},{5,4},{6,7},{7,6},{8,9},{9,8},{10,11... | collective-permute-start | bytes 2359304 | tf_op jit(solution)/shard_map/ppermute | solution.py:333
  1.2 13.7 %collective-permute-start.1 = (bf16[3,512,256]{2,1,0:T(8,128)(2,1)}, bf16[3,512,256]{2,1,0:T(8,128)(2,1)S(1)}, u32[]{:S(2)}, u32[]{:S(2)}) collective-permute-start(bf16[3,512,256]{2,1,0:T(8,128)(2,1)} %refs_5_.11), channel_id=1, source_target_pairs={{0,1},{1,0},{2,3},{3,2},{4,5},{5,4},{6,7},{7,6},{8,9},{9,8},{10,11... | collective-permute-start | bytes 2359304 | tf_op jit(solution)/shard_map/ppermute | solution.py:333
  4.9 13.2 %collective-permute-start.2 = (bf16[128,256]{1,0:T(8,128)(2,1)}, bf16[128,256]{1,0:T(8,128)(2,1)S(1)}, u32[]{:S(2)}, u32[]{:S(2)}) collective-permute-start(bf16[128,256]{1,0:T(8,128)(2,1)} %get-tuple-element.79), channel_id=1, source_target_pairs={{0,4},{4,8},{8,12},{1,5},{5,9},{9,13},{2,6},{6,10},{10,14},{3,7},{... | collective-permute-start | bytes 196616 | tf_op jit(solution)/shard_map/ppermute | solution.py:328
  9.8 8.3 %collective-permute-start.3 = (bf16[128,256]{1,0:T(8,128)(2,1)S(1)}, bf16[128,256]{1,0:T(8,128)(2,1)S(1)}, u32[]{:S(2)}, u32[]{:S(2)}) collective-permute-start(bf16[128,256]{1,0:T(8,128)(2,1)S(1)} %get-tuple-element.80), channel_id=1, source_target_pairs={{0,2},{2,0},{1,3},{3,1},{4,6},{6,4},{5,7},{7,5},{8,10},{10,8},{9,1... | collective-permute-start | bytes 196616 | tf_op jit(solution)/shard_map/ppermute | solution.py:333
  19.4 6.2 %collective-permute-start.4 = (bf16[128,256]{1,0:T(8,128)(2,1)S(1)}, bf16[128,256]{1,0:T(8,128)(2,1)S(1)}, u32[]{:S(2)}, u32[]{:S(2)}) collective-permute-start(bf16[128,256]{1,0:T(8,128)(2,1)S(1)} %get-tuple-element.84), channel_id=1, source_target_pairs={{0,4},{4,8},{8,12},{1,5},{5,9},{9,13},{2,6},{6,10},{10,14},{3,7},{... | collective-permute-start | bytes 196616 | tf_op jit(solution)/shard_map/ppermute | solution.py:328
  28.5 6.2 %collective-permute-start.6 = (bf16[128,256]{1,0:T(8,128)(2,1)S(1)}, bf16[128,256]{1,0:T(8,128)(2,1)S(1)}, u32[]{:S(2)}, u32[]{:S(2)}) collective-permute-start(bf16[128,256]{1,0:T(8,128)(2,1)S(1)} %get-tuple-element.90), channel_id=1, source_target_pairs={{0,4},{4,8},{8,12},{1,5},{5,9},{9,13},{2,6},{6,10},{10,14},{3,7},{... | collective-permute-start | bytes 196616 | tf_op jit(solution)/shard_map/ppermute | solution.py:328
  38.5 6.8 %collective-permute-start.8 = (bf16[128,256]{1,0:T(8,128)(2,1)S(1)}, bf16[128,256]{1,0:T(8,128)(2,1)S(1)}, u32[]{:S(2)}, u32[]{:S(2)}) collective-permute-start(bf16[128,256]{1,0:T(8,128)(2,1)S(1)} %get-tuple-element.101), channel_id=1, source_target_pairs={{4,0},{8,4},{12,8},{5,1},{9,5},{13,9},{6,2},{10,6},{14,10},{7,3},{... | collective-permute-start | bytes 196616 | tf_op jit(solution)/shard_map/ppermute | solution.py:328
  43.8 15.1 %collective-permute-start.14 = (bf16[1024,128]{1,0:T(8,128)(2,1)S(1)}, bf16[1024,128]{1,0:T(8,128)(2,1)S(1)}, u32[]{:S(2)}, u32[]{:S(2)}) collective-permute-start(bf16[1024,128]{1,0:T(8,128)(2,1)S(1)} %get-tuple-element.122), channel_id=1, source_target_pairs={{0,2},{2,0},{1,3},{3,1},{4,6},{6,4},{5,7},{7,5},{8,10},{10,8},{9,1... | collective-permute-start | bytes 786440 | tf_op jit(solution)/shard_map/ppermute | solution.py:333
  46.8 6.8 %collective-permute-start.10 = (bf16[128,256]{1,0:T(8,128)(2,1)S(1)}, bf16[128,256]{1,0:T(8,128)(2,1)S(1)}, u32[]{:S(2)}, u32[]{:S(2)}) collective-permute-start(bf16[128,256]{1,0:T(8,128)(2,1)S(1)} %get-tuple-element.110), channel_id=1, source_target_pairs={{4,0},{8,4},{12,8},{5,1},{9,5},{13,9},{6,2},{10,6},{14,10},{7,3},{... | collective-permute-start | bytes 196616 | tf_op jit(solution)/shard_map/ppermute | solution.py:328
  51.9 14.6 %collective-permute-start.22 = (bf16[1024,128]{1,0:T(8,128)(2,1)S(1)}, bf16[1024,128]{1,0:T(8,128)(2,1)S(1)}, u32[]{:S(2)}, u32[]{:S(2)}) collective-permute-start(bf16[1024,128]{1,0:T(8,128)(2,1)S(1)} %get-tuple-element.130), channel_id=1, source_target_pairs={{0,2},{2,0},{1,3},{3,1},{4,6},{6,4},{5,7},{7,5},{8,10},{10,8},{9,1... | collective-permute-start | bytes 786440 | tf_op jit(solution)/shard_map/ppermute | solution.py:333
  58.3 11.7 %collective-permute-start.30 = (bf16[1024,128]{1,0:T(8,128)(2,1)S(1)}, bf16[1024,128]{1,0:T(8,128)(2,1)S(1)}, u32[]{:S(2)}, u32[]{:S(2)}) collective-permute-start(bf16[1024,128]{1,0:T(8,128)(2,1)S(1)} %get-tuple-element.138), channel_id=1, source_target_pairs={{0,2},{2,0},{1,3},{3,1},{4,6},{6,4},{5,7},{7,5},{8,10},{10,8},{9,1... | collective-permute-start | bytes 786440 | tf_op jit(solution)/shard_map/ppermute | solution.py:333
  59.0 7.7 %collective-permute-start.15 = (bf16[256,128]{1,0:T(8,128)(2,1)S(1)}, bf16[256,128]{1,0:T(8,128)(2,1)S(1)}, u32[]{:S(2)}, u32[]{:S(2)}) collective-permute-start(bf16[256,128]{1,0:T(8,128)(2,1)S(1)} %get-tuple-element.124), channel_id=1, source_target_pairs={{0,4},{4,8},{8,12},{12,0},{1,5},{5,9},{9,13},{13,1},{2,6},{6,10},{... | collective-permute-start | bytes 196616 | tf_op jit(solution)/shard_map/ppermute | solution.py:333
  62.1 8.5 %collective-permute-start.16 = (bf16[256,128]{1,0:T(8,128)(2,1)S(1)}, bf16[256,128]{1,0:T(8,128)(2,1)S(1)}, u32[]{:S(2)}, u32[]{:S(2)}) collective-permute-start(bf16[256,128]{1,0:T(8,128)(2,1)S(1)} %get-tuple-element.125), channel_id=1, source_target_pairs={{0,8},{4,12},{8,0},{12,4},{1,9},{5,13},{9,1},{13,5},{2,10},{6,14},... | collective-permute-start | bytes 196616 | tf_op jit(solution)/shard_map/ppermute | solution.py:333
  63.6 8.7 %collective-permute-start.17 = (bf16[256,128]{1,0:T(8,128)(2,1)S(1)}, bf16[256,128]{1,0:T(8,128)(2,1)S(1)}, u32[]{:S(2)}, u32[]{:S(2)}) collective-permute-start(bf16[256,128]{1,0:T(8,128)(2,1)S(1)} %get-tuple-element.126), channel_id=1, source_target_pairs={{0,12},{4,0},{8,4},{12,8},{1,13},{5,1},{9,5},{13,9},{2,14},{6,2},{... | collective-permute-start | bytes 196616 | tf_op jit(solution)/shard_map/ppermute | solution.py:333
  66.6 7.9 %collective-permute-start.23 = (bf16[256,128]{1,0:T(8,128)(2,1)S(1)}, bf16[256,128]{1,0:T(8,128)(2,1)S(1)}, u32[]{:S(2)}, u32[]{:S(2)}) collective-permute-start(bf16[256,128]{1,0:T(8,128)(2,1)S(1)} %get-tuple-element.132), channel_id=1, source_target_pairs={{0,4},{4,8},{8,12},{12,0},{1,5},{5,9},{9,13},{13,1},{2,6},{6,10},{... | collective-permute-start | bytes 196616 | tf_op jit(solution)/shard_map/ppermute | solution.py:333
  66.7 9.2 %collective-permute-start.24 = (bf16[256,128]{1,0:T(8,128)(2,1)S(1)}, bf16[256,128]{1,0:T(8,128)(2,1)S(1)}, u32[]{:S(2)}, u32[]{:S(2)}) collective-permute-start(bf16[256,128]{1,0:T(8,128)(2,1)S(1)} %get-tuple-element.133), channel_id=1, source_target_pairs={{0,8},{4,12},{8,0},{12,4},{1,9},{5,13},{9,1},{13,5},{2,10},{6,14},... | collective-permute-start | bytes 196616 | tf_op jit(solution)/shard_map/ppermute | solution.py:333
  69.9 10.7 %collective-permute-start.25 = (bf16[256,128]{1,0:T(8,128)(2,1)S(1)}, bf16[256,128]{1,0:T(8,128)(2,1)S(1)}, u32[]{:S(2)}, u32[]{:S(2)}) collective-permute-start(bf16[256,128]{1,0:T(8,128)(2,1)S(1)} %get-tuple-element.134), channel_id=1, source_target_pairs={{0,12},{4,0},{8,4},{12,8},{1,13},{5,1},{9,5},{13,9},{2,14},{6,2},{... | collective-permute-start | bytes 196616 | tf_op jit(solution)/shard_map/ppermute | solution.py:333
  70.6 10.1 %collective-permute-start.31 = (bf16[256,128]{1,0:T(8,128)(2,1)S(1)}, bf16[256,128]{1,0:T(8,128)(2,1)S(1)}, u32[]{:S(2)}, u32[]{:S(2)}) collective-permute-start(bf16[256,128]{1,0:T(8,128)(2,1)S(1)} %get-tuple-element.140), channel_id=1, source_target_pairs={{0,4},{4,8},{8,12},{12,0},{1,5},{5,9},{9,13},{13,1},{2,6},{6,10},{... | collective-permute-start | bytes 196616 | tf_op jit(solution)/shard_map/ppermute | solution.py:333
  72.3 9.0 %collective-permute-start.32 = (bf16[256,128]{1,0:T(8,128)(2,1)S(1)}, bf16[256,128]{1,0:T(8,128)(2,1)S(1)}, u32[]{:S(2)}, u32[]{:S(2)}) collective-permute-start(bf16[256,128]{1,0:T(8,128)(2,1)S(1)} %get-tuple-element.141), channel_id=1, source_target_pairs={{0,8},{4,12},{8,0},{12,4},{1,9},{5,13},{9,1},{13,5},{2,10},{6,14},... | collective-permute-start | bytes 196616 | tf_op jit(solution)/shard_map/ppermute | solution.py:333
  74.5 11.2 %collective-permute-start.33 = (bf16[256,128]{1,0:T(8,128)(2,1)S(1)}, bf16[256,128]{1,0:T(8,128)(2,1)S(1)}, u32[]{:S(2)}, u32[]{:S(2)}) collective-permute-start(bf16[256,128]{1,0:T(8,128)(2,1)S(1)} %get-tuple-element.142), channel_id=1, source_target_pairs={{0,12},{4,0},{8,4},{12,8},{1,13},{5,1},{9,5},{13,9},{2,14},{6,2},{... | collective-permute-start | bytes 196616 | tf_op jit(solution)/shard_map/ppermute | solution.py:333
  75.9 9.9 %collective-permute-start.20 = (bf16[256,128]{1,0:T(8,128)(2,1)S(1)}, bf16[256,128]{1,0:T(8,128)(2,1)S(1)}, u32[]{:S(2)}, u32[]{:S(2)}) collective-permute-start(bf16[256,128]{1,0:T(8,128)(2,1)S(1)} %end_2_0.1.refs_0_), channel_id=1, source_target_pairs={{0,12},{4,0},{8,4},{12,8},{1,13},{5,1},{9,5},{13,9},{2,14},{6,2},{... | collective-permute-start | bytes 196616 | tf_op jit(solution)/shard_map/ppermute | solution.py:333
  80.7 8.0 %collective-permute-start.19 = (bf16[256,128]{1,0:T(8,128)(2,1)S(1)}, bf16[256,128]{1,0:T(8,128)(2,1)S(1)}, u32[]{:S(2)}, u32[]{:S(2)}) collective-permute-start(bf16[256,128]{1,0:T(8,128)(2,1)S(1)} %end_2_0.1.refs_0_), channel_id=1, source_target_pairs={{0,8},{4,12},{8,0},{12,4},{1,9},{5,13},{9,1},{13,5},{2,10},{6,14},... | collective-permute-start | bytes 196616 | tf_op jit(solution)/shard_map/ppermute | solution.py:333
  80.7 9.1 %collective-permute-start.18 = (bf16[256,128]{1,0:T(8,128)(2,1)S(1)}, bf16[256,128]{1,0:T(8,128)(2,1)S(1)}, u32[]{:S(2)}, u32[]{:S(2)}) collective-permute-start(bf16[256,128]{1,0:T(8,128)(2,1)S(1)} %end_2_0.1.refs_0_), channel_id=1, source_target_pairs={{0,4},{4,8},{8,12},{12,0},{1,5},{5,9},{9,13},{13,1},{2,6},{6,10},{... | collective-permute-start | bytes 196616 | tf_op jit(solution)/shard_map/ppermute | solution.py:333
  81.3 10.4 %collective-permute-start.28 = (bf16[256,128]{1,0:T(8,128)(2,1)S(1)}, bf16[256,128]{1,0:T(8,128)(2,1)S(1)}, u32[]{:S(2)}, u32[]{:S(2)}) collective-permute-start(bf16[256,128]{1,0:T(8,128)(2,1)S(1)} %end_1_0.1.refs_0_), channel_id=1, source_target_pairs={{0,12},{4,0},{8,4},{12,8},{1,13},{5,1},{9,5},{13,9},{2,14},{6,2},{... | collective-permute-start | bytes 196616 | tf_op jit(solution)/shard_map/ppermute | solution.py:333
  85.7 7.1 %collective-permute-start.27 = (bf16[256,128]{1,0:T(8,128)(2,1)S(1)}, bf16[256,128]{1,0:T(8,128)(2,1)S(1)}, u32[]{:S(2)}, u32[]{:S(2)}) collective-permute-start(bf16[256,128]{1,0:T(8,128)(2,1)S(1)} %end_1_0.1.refs_0_), channel_id=1, source_target_pairs={{0,8},{4,12},{8,0},{12,4},{1,9},{5,13},{9,1},{13,5},{2,10},{6,14},... | collective-permute-start | bytes 196616 | tf_op jit(solution)/shard_map/ppermute | solution.py:333
  85.8 8.2 %collective-permute-start.26 = (bf16[256,128]{1,0:T(8,128)(2,1)S(1)}, bf16[256,128]{1,0:T(8,128)(2,1)S(1)}, u32[]{:S(2)}, u32[]{:S(2)}) collective-permute-start(bf16[256,128]{1,0:T(8,128)(2,1)S(1)} %end_1_0.1.refs_0_), channel_id=1, source_target_pairs={{0,4},{4,8},{8,12},{12,0},{1,5},{5,9},{9,13},{13,1},{2,6},{6,10},{... | collective-permute-start | bytes 196616 | tf_op jit(solution)/shard_map/ppermute | solution.py:333
  88.7 6.2 %collective-permute-start.36 = (bf16[256,128]{1,0:T(8,128)(2,1)S(1)}, bf16[256,128]{1,0:T(8,128)(2,1)S(1)}, u32[]{:S(2)}, u32[]{:S(2)}) collective-permute-start(bf16[256,128]{1,0:T(8,128)(2,1)S(1)} %end_0_0.1.refs_0_), channel_id=1, source_target_pairs={{0,12},{4,0},{8,4},{12,8},{1,13},{5,1},{9,5},{13,9},{2,14},{6,2},{... | collective-permute-start | bytes 196616 | tf_op jit(solution)/shard_map/ppermute | solution.py:333
  91.8 6.2 %collective-permute-start.34 = (bf16[256,128]{1,0:T(8,128)(2,1)S(1)}, bf16[256,128]{1,0:T(8,128)(2,1)S(1)}, u32[]{:S(2)}, u32[]{:S(2)}) collective-permute-start(bf16[256,128]{1,0:T(8,128)(2,1)S(1)} %end_0_0.1.refs_0_), channel_id=1, source_target_pairs={{0,4},{4,8},{8,12},{12,0},{1,5},{5,9},{9,13},{13,1},{2,6},{6,10},{... | collective-permute-start | bytes 196616 | tf_op jit(solution)/shard_map/ppermute | solution.py:333
  92.7 17.4 %collective-permute-start.21 = (bf16[1024,128]{1,0:T(8,128)(2,1)S(1)}, bf16[1024,128]{1,0:T(8,128)(2,1)S(1)}, u32[]{:S(2)}, u32[]{:S(2)}) collective-permute-start(bf16[1024,128]{1,0:T(8,128)(2,1)S(1)} %place_2_0.1.refs_0_), channel_id=1, source_target_pairs={{0,2},{2,0},{1,3},{3,1},{4,6},{6,4},{5,7},{7,5},{8,10},{10,8},{9,1... | collective-permute-start | bytes 786440 | tf_op jit(solution)/shard_map/ppermute | solution.py:333
  94.1 17.3 %collective-permute-start.29 = (bf16[1024,128]{1,0:T(8,128)(2,1)S(1)}, bf16[1024,128]{1,0:T(8,128)(2,1)S(1)}, u32[]{:S(2)}, u32[]{:S(2)}) collective-permute-start(bf16[1024,128]{1,0:T(8,128)(2,1)S(1)} %place_1_0.1.refs_2_), channel_id=1, source_target_pairs={{0,2},{2,0},{1,3},{3,1},{4,6},{6,4},{5,7},{7,5},{8,10},{10,8},{9,1... | collective-permute-start | bytes 786440 | tf_op jit(solution)/shard_map/ppermute | solution.py:333
  98.0 14.5 %collective-permute-start.37 = (bf16[1024,128]{1,0:T(8,128)(2,1)S(1)}, bf16[1024,128]{1,0:T(8,128)(2,1)S(1)}, u32[]{:S(2)}, u32[]{:S(2)}) collective-permute-start(bf16[1024,128]{1,0:T(8,128)(2,1)S(1)} %place_0_0.1.refs_2_), channel_id=1, source_target_pairs={{0,2},{2,0},{1,3},{3,1},{4,6},{6,4},{5,7},{7,5},{8,10},{10,8},{9,1... | collective-permute-start | bytes 786440 | tf_op jit(solution)/shard_map/ppermute | solution.py:333
  100.8 8.2 %collective-permute-start.13 = (bf16[128,256]{1,0:T(8,128)(2,1)S(1)}, bf16[128,256]{1,0:T(8,128)(2,1)S(1)}, u32[]{:S(2)}, u32[]{:S(2)}) collective-permute-start(bf16[128,256]{1,0:T(8,128)(2,1)S(1)} %get-tuple-element.120), channel_id=1, source_target_pairs={{0,2},{2,0},{1,3},{3,1},{4,6},{6,4},{5,7},{7,5},{8,10},{10,8},{9,1... | collective-permute-start | bytes 196616 | tf_op jit(solution)/shard_map/ppermute | solution.py:333
  (15 other events, 67.6 us)

commit v3 on v2

--- a/solution.py
+++ b/solution.py
@@ -24,17 +24,19 @@
     return lax.dot_general(a, b, dims, preferred_element_type=F32)
 
 
-def call(body, outs, ins, flops, scratch=(), name=None):
+def call(body, outs, ins, flops, scratch=(), name=None, after=()):
+    skipped = len(after)
     return pl.pallas_call(
-        body,
+        lambda *refs: body(*refs[skipped:]),
         out_shape=[jax.ShapeDtypeStruct(s, d) for s, d in outs],
-        in_specs=[SMEM if x.dtype == jnp.int32 and x.size < 100 else VMEM for x in ins],
+        in_specs=[ANY] * skipped
+        + [SMEM if x.dtype == jnp.int32 and x.size < 100 else VMEM for x in ins],
         out_specs=[VMEM] * len(outs),
         scratch_shapes=list(scratch),
         compiler_params=pltpu.CompilerParams(vmem_limit_bytes=32 * 1024 * 1024),
         cost_estimate=pl.CostEstimate(flops=flops, bytes_accessed=4_000_000, transcendentals=0),
         name=name,
-    )(*ins)
+    )(*after, *ins)
 
 
 def sigmoid(v):
@@ -273,29 +275,52 @@
     return [around(x, axis, s + 1) for s, x in enumerate(parts)]
 
 
-def summed_piece(parts, axes, name):
-    n0, n1 = lax.axis_size(axes[0]), lax.axis_size(axes[1])
-    m = parts[0].shape[0]
-    got = shifted(parts[1:], axes[0])
-    parts = call(
-        functools.partial(add_scatter_kernel, axes[1], n0),
-        [((m // n1, LANES), F32)] + [((m // n1, LANES), BF16)] * (n1 - 1),
-        [parts[0], *got],
-        1_000_000,
-        scratch=[pltpu.VMEM((m, LANES), F32)],
-        name=f"add_{name}",
-    )
-    got = shifted(parts[1:], axes[1])
-    (own,) = call(add_kernel, [((m // n1, LANES), BF16)], [parts[0], *got], 1_000_000, name=f"end_{name}")
-    got = shifted([own] * (n1 - 1), axes[1])
-    (own,) = call(
-        functools.partial(place_kernel, axes[1]),
-        [((m, LANES), BF16)],
-        [own, *got],
-        1_000_000,
-        name=f"place_{name}",
-    )
-    return [own, *shifted([own] * (n0 - 1), axes[0])]
+class Sum:
+    def __init__(self, parts, axes, name):
+        self.axes, self.name = axes, name
+        self.parts = [parts[0], *shifted(parts[1:], axes[0])]
+
+    def add(self, after):
+        n = lax.axis_size(self.axes[1])
+        m = self.parts[0].shape[0]
+        own, *sent = call(
+            functools.partial(add_scatter_kernel, self.axes[1], len(self.parts)),
+            [((m // n, LANES), F32)] + [((m // n, LANES), BF16)] * (n - 1),
+            self.parts,
+            1_000_000,
+            scratch=[pltpu.VMEM((m, LANES), F32)],
+            name=f"add_{self.name}",
+            after=after,
+        )
+        self.parts = [own, *shifted(sent, self.axes[1])]
+        return [own]
+
+    def end(self, after):
+        n = lax.axis_size(self.axes[1])
+        (own,) = call(
+            add_kernel,
+            [(self.parts[0].shape, BF16)],
+            self.parts,
+            1_000_000,
+            name=f"end_{self.name}",
+            after=after,
+        )
+        self.parts = [own, *shifted([own] * (n - 1), self.axes[1])]
+        return [own]
+
+    def place(self, after):
+        n = lax.axis_size(self.axes[0])
+        m = self.parts[0].shape[0]
+        (own,) = call(
+            functools.partial(place_kernel, self.axes[1]),
+            [((m * len(self.parts), LANES), BF16)],
+            self.parts,
+            1_000_000,
+            name=f"place_{self.name}",
+            after=after,
+        )
+        self.parts = [own, *shifted([own] * (n - 1), self.axes[0])]
+        return [own]
 
 
 def gathered_grad(dtotal, back, returned, spread):
@@ -415,15 +440,15 @@
         n = lax.axis_size(axes[0])
         m = (hi - lo) // n
         part_shapes += [((m, LANES), F32)] + [((m, LANES), BF16)] * (n - 1)
-    written = []
-    for layer in reversed(range(layers)):
-        dtotal, dround = outs[:2]
-        far_saved = outs[2:6]
-        returned = exchange(outs[6], outs[7:], -1)
-        back, *parts = call(
+    returned = {}
+    sums = {}
+
+    def back(layer, outs, after=()):
+        returned[layer] = exchange(outs[6], outs[7:], -1)
+        grad, *parts = call(
             functools.partial(shadow_bwd_kernel, layer, grad_scale, pieces),
             [((rows, latent), F32)] + part_shapes,
-            [dround, inputs[layer], local_t, *weights, *far_saved],
+            [outs[1], inputs[layer], local_t, *weights, *outs[2:6]],
             3 * rows * ffn + 2 * rows * rows * latent,
             scratch=[
                 pltpu.VMEM((grad_rows, LANES), F32),
@@ -432,19 +457,45 @@
                 pltpu.VMEM((rows, half), BF16),
             ],
             name=f"back{layer}",
+            after=after,
         )
-        ready = []
+        sums[layer] = []
         for i, (_, _, axes) in enumerate(pieces):
             n = lax.axis_size(axes[0])
-            ready += summed_piece(parts[:n], axes, f"{layer}_{i}")
+            sums[layer].append(Sum(parts[:n], axes, f"{layer}_{i}"))
             parts = parts[n:]
-        written = pl.pallas_call(
-            functools.partial(write_kernel, layer, pieces, len(written)),
+        return [outs[0], grad]
+
+    def join(layer, state, after=()):
+        if layer:
+            return call(
+                functools.partial(post_bwd_kernel, layer - 1, groups),
+                bwd_outs,
+                [*state, spread, remote_t, totals[layer - 1]]
+                + [*weights, *returned[layer], *received[layer - 1]],
+                2 * far_rows * ffn,
+                name=f"join{layer}",
+                after=after,
+            )
+        return call(
+            functools.partial(last_kernel, groups),
+            [((rows, latent), F32)],
+            [*state, spread, *returned[layer]],
+            2 * rows * sent_rows * latent,
+            name="join0",
+            after=after,
+        )
+
+    def write(layer, written, after):
+        ready = [x for piece in sums[layer] for x in piece.parts]
+        kept = [*written, *after]
+        return pl.pallas_call(
+            functools.partial(write_kernel, layer, pieces, len(kept)),
             out_shape=[
                 jax.ShapeDtypeStruct((layers, latent, half), F32),
                 jax.ShapeDtypeStruct((layers, half, latent), F32),
             ],
-            in_specs=[ANY] * len(written) + [VMEM] * len(ready),
+            in_specs=[ANY] * len(kept) + [VMEM] * len(ready),
             out_specs=[ANY] * 2,
             scratch_shapes=[
                 pltpu.VMEM((grad_rows, LANES), F32),
@@ -456,23 +507,38 @@
             compiler_params=pltpu.CompilerParams(vmem_limit_bytes=32 * 1024 * 1024),
             cost_estimate=pl.CostEstimate(flops=0, bytes_accessed=4_000_000, transcendentals=0),
             name=f"write{layer}",
-        )(*written, *ready)
+        )(*written, *after, *ready)
+
+    def stage(which, layer, after):
+        for piece in sums[layer]:
+            after = getattr(piece, which)(after)
+        return after
+
+    at = []
+    for layer in reversed(range(layers)):
+        state = back(layer, outs, at)
+        at = state[1:]
+        if layer + 2 < layers:
+            at = stage("end", layer + 2, at)
+        if layer + 1 < layers:
+            at = stage("add", layer + 1, at)
         if layer:
-            outs = call(
-                functools.partial(post_bwd_kernel, layer - 1, groups),
-                bwd_outs,
-                [dtotal, back, spread, remote_t, totals[layer - 1]]
-                + [*weights, *returned, *received[layer - 1]],
-                2 * far_rows * ffn,
-                name=f"join{layer}",
-            )
-    (grad,) = call(
-        functools.partial(last_kernel, groups),
-        [((rows, latent), F32)],
-        [dtotal, back, spread, *returned],
-        2 * rows * sent_rows * latent,
-        name="join0",
-    )
+            outs = join(layer, state, at)
+            at = outs[1:2]
+    (grad,) = join(0, state, at)
+    at = [grad]
+    for layer in reversed(range(2, layers)):
+        at = stage("place", layer, at)
+    at = stage("add", 0, at)
+    at = stage("end", 1, at)
+    written = []
+    for layer in reversed(range(2, layers)):
+        written = write(layer, written, at)
+    at = stage("end", 0, written[:1] or at)
+    at = stage("place", 1, at)
+    at = stage("place", 0, at)
+    written = write(1, written, at)
+    written = write(0, written, [])
     return (grad, *written)
 
 

time: 114 us -> 115 us (level)
  local copies, waits for them, and re-layouts: 5.37 us -> 7.91 us
  starting transfers between devices: 58.5 us -> 56.4 us
    ppermute x32, waiting for transfers between devices: 13.1 us -> 17.6 us  [around(): return lax.ppermute(x, axis, [(i, (i + distance) % n) for i in range(n)])]
    ppermute x6, waiting for transfers between devices: 4.44 us -> 0.02 us  [along(): lax.ppermute(x, axis, [(i, i + distance) for i in range(n) if 0 <= i + di...]
    unnamed x19 -> x23, local copies, waits for them, and re-layouts: 5.37 us -> 7.91 us
    ppermute x32, starting transfers between devices: 42.6 us -> 40.4 us  [around(): return lax.ppermute(x, axis, [(i, (i + distance) % n) for i in range(n)])]
where the time goes in v3:
time: 115 us; the launch traced here: 114 us
  starting transfers between devices  56.4 us (49%)
  Pallas kernels  31.4 us (27%)
  waiting for transfers between devices  17.6 us (15%)
  local copies, waits for them, and re-layouts  7.91 us (7%)
    ppermute x32, starting transfers between devices, around(): return lax.ppermute(x, axis, [(i, (i + distance) % n) for i in range(n)])  40.4 us
    pallas_call x23, Pallas kernels, call(): pl.pallas_call(lambda *refs: body(*refs[skipped:]), out_shape=[jax.ShapeD...  28 us
    ppermute x32, waiting for transfers between devices, around(): return lax.ppermute(x, axis, [(i, (i + distance) % n) for i in range(n)])  17.6 us
    ppermute x6, starting transfers between devices, along(): lax.ppermute(x, axis, [(i, i + distance) for i in range(n) if 0 <= i + di...  15.9 us
    unnamed x23, local copies, waits for them, and re-layouts  7.91 us
    pallas_call x3, Pallas kernels, write(): pl.pallas_call(functools.partial(write_kernel, layer, pieces, len(kept)),...  3.39 us
  transfers between devices with their start and end apart: 38, of which 9 were waited for; matrix products, arithmetic and copies ran while one was open for 1% of the time, Pallas kernels for 22%

profile of v3, /device:TPU:0, one launch (start us, length us, event | category | flops | bytes accessed | tf_op | source)
XLA Modules:
  0.0 114.3 jit_solution(14067736299223373993)
XLA Ops:
  4.9 4.9 %collective-permute-start.2 = (bf16[128,256]{1,0:T(8,128)(2,1)}, bf16[128,256]{1,0:T(8,128)(2,1)S(1)}, u32[]{:S(2)}, u32[]{:S(2)}) collective-permute-start(bf16[128,256]{1,0:T(8,128)(2,1)} %get-tuple-element.79), channel_id=1, source_target_pairs={{0,4},{4,8},{8,12},{1,5},{5,9},{9,13},{2,6},{6,10},{10,14},{3,7},{... | collective-permute-start | bytes 196616 | tf_op jit(solution)/shard_map/ppermute | solution.py:353
  9.8 1.6 %collective-permute-start.3 = (bf16[128,256]{1,0:T(8,128)(2,1)S(1)}, bf16[128,256]{1,0:T(8,128)(2,1)S(1)}, u32[]{:S(2)}, u32[]{:S(2)}) collective-permute-start(bf16[128,256]{1,0:T(8,128)(2,1)S(1)} %get-tuple-element.80), channel_id=1, source_target_pairs={{0,2},{2,0},{1,3},{3,1},{4,6},{6,4},{5,7},{7,5},{8,10},{10,8},{9,1... | collective-permute-start | bytes 196616 | tf_op jit(solution)/shard_map/ppermute | solution.py:358
  13.3 1.6 %adjacency.1 = (bf16[768,768]{1,0:T(8,128)(2,1)S(1)}, bf16[768,768]{1,0:T(8,128)(2,1)S(1)}, bf16[768,256]{1,0:T(8,128)(2,1)S(1)}, bf16[256,768]{1,0:T(8,128)(2,1)S(1)}) custom-call(s32[6,4]{1,0:T(8,128)S(1)} %copy.15.refs_0_, bf16[6,4,128,128]{3,2,1,0:T(8,128)(2,1)S(1)} %copy-done.8, bf16[128,768]{1,0:T(8,128)(2,1)S(1)} %get-tuple-element.74.refs_2_), custom_call_target="tpu_custom_call" | custom-call | flops 150994944 | bytes 4000000 | tf_op jit(solution)/shard_map/adjacency/pallas_call | solution.py:29
  16.1 2.1 %local0.1 = (f32[768,256]{1,0:T(8,128)S(1)}, bf16[768,256]{1,0:T(8,128)(2,1)}) custom-call(bf16[768,256]{1,0:T(8,128)(2,1)S(1)} %copy-done.5, bf16[768,768]{1,0:T(8,128)(2,1)S(1)} %get-tuple-element.75.refs_1_, bf16[3,256,512]{2,1,0:T(8,128)(2,1)S(1)} %copy-done, bf16[3,256,512]{2,1,0:T(8,128)(2,1)S(1)} %collective-permute-done.refs_3_.refs_5_.refs_6_.refs_4_.refs_7_, ...), custom_call_target="tpu_custom_call" | custom-call | flops 1107296256 | bytes 4000000 | tf_op jit(solution)/shard_map/local0/pallas_call | solution.py:29
  19.4 3.5 %collective-permute-start.4 = (bf16[128,256]{1,0:T(8,128)(2,1)S(1)}, bf16[128,256]{1,0:T(8,128)(2,1)S(1)}, u32[]{:S(2)}, u32[]{:S(2)}) collective-permute-start(bf16[128,256]{1,0:T(8,128)(2,1)S(1)} %get-tuple-element.84), channel_id=1, source_target_pairs={{0,4},{4,8},{8,12},{1,5},{5,9},{9,13},{2,6},{6,10},{10,14},{3,7},{... | collective-permute-start | bytes 196616 | tf_op jit(solution)/shard_map/ppermute | solution.py:353
  23.5 2.1 %local1.1 = (f32[768,256]{1,0:T(8,128)S(1)}, bf16[768,256]{1,0:T(8,128)(2,1)}) custom-call(bf16[768,256]{1,0:T(8,128)(2,1)S(1)} %get-tuple-element.82.refs_0_.refs_2_, bf16[768,768]{1,0:T(8,128)(2,1)S(1)} %get-tuple-element.75.refs_1_, bf16[3,256,512]{2,1,0:T(8,128)(2,1)S(1)} %copy-done, ...), custom_call_target="tpu_custom_call" | custom-call | flops 1107296256 | bytes 4000000 | tf_op jit(solution)/shard_map/local1/pallas_call | solution.py:29
  25.6 1.6 %collective-permute-done.5.refs_9_.refs_13_ = bf16[128,256]{1,0:T(8,128)(2,1)S(1)} collective-permute-done((bf16[128,256]{1,0:T(8,128)(2,1)S(1)}, bf16[128,256]{1,0:T(8,128)(2,1)S(1)}, u32[]{:S(2)}, u32[]{:S(2)}) %collective-permute-start.5) | collective-permute-done | bytes 65568 | tf_op jit(solution)/shard_map/ppermute | solution.py:358
  28.5 3.5 %collective-permute-start.6 = (bf16[128,256]{1,0:T(8,128)(2,1)S(1)}, bf16[128,256]{1,0:T(8,128)(2,1)S(1)}, u32[]{:S(2)}, u32[]{:S(2)}) collective-permute-start(bf16[128,256]{1,0:T(8,128)(2,1)S(1)} %get-tuple-element.90), channel_id=1, source_target_pairs={{0,4},{4,8},{8,12},{1,5},{5,9},{9,13},{2,6},{6,10},{10,14},{3,7},{... | collective-permute-start | bytes 196616 | tf_op jit(solution)/shard_map/ppermute | solution.py:353
  32.6 2.1 %local2.1 = (f32[768,256]{1,0:T(8,128)S(1)}, bf16[768,256]{1,0:T(8,128)(2,1)}) custom-call(bf16[768,256]{1,0:T(8,128)(2,1)S(1)} %get-tuple-element.87.refs_0_.refs_1_, bf16[768,768]{1,0:T(8,128)(2,1)S(1)} %get-tuple-element.75.refs_1_, bf16[3,256,512]{2,1,0:T(8,128)(2,1)S(1)} %copy-done, ...), custom_call_target="tpu_custom_call" | custom-call | flops 1107296256 | bytes 4000000 | tf_op jit(solution)/shard_map/local2/pallas_call | solution.py:29
  34.7 1.6 %collective-permute-done.7.refs_10_ = bf16[128,256]{1,0:T(8,128)(2,1)S(1)} collective-permute-done((bf16[128,256]{1,0:T(8,128)(2,1)S(1)}, bf16[128,256]{1,0:T(8,128)(2,1)S(1)}, u32[]{:S(2)}, u32[]{:S(2)}) %collective-permute-start.7) | collective-permute-done | bytes 65568 | tf_op jit(solution)/shard_map/ppermute | solution.py:358
  36.4 2.2 %turn.1 = (f32[768,256]{1,0:T(8,128)S(1)}, bf16[768,256]{1,0:T(8,128)(2,1)S(1)}, bf16[256,256]{1,0:T(8,128)(2,1)S(1)}, bf16[256,256]{1,0:T(8,128)(2,1)S(1)}, bf1...) custom-call(f32[768,256]{1,0:T(8,128)S(1)} %get-tuple-element.86.ref, ...), custom_call_target="tpu_custom_call" | custom-call | flops 536870912 | bytes 4000000 | tf_op jit(solution)/shard_map/turn/pallas_call | solution.py:29
  40.7 3.2 %back2.1 = (f32[768,256]{1,0:T(8,128)S(1)}, f32[1024,128]{1,0:T(8,128)S(1)}, bf16[1024,128]{1,0:T(8,128)(2,1)S(1)}) custom-call(bf16[768,256]{1,0:T(8,128)(2,1)S(1)} %get-tuple-element.92.refs_0_, bf16[768,256]{1,0:T(8,128)(2,1)S(1)} %get-tuple-element.87.refs_0_.refs_1_, bf16[768,768]{1,0:T(8,128)(2,1)S(1)} %get-tuple-element.93.refs_2_.refs_3_, ...), custom_call_target="tpu_custom_call" | custom-call | flops 2717908992 | bytes 4000000 | tf_op jit(solution)/shard_map/back2/pallas_call | solution.py:29
  43.8 1.6 %collective-permute-start.10 = (bf16[1024,128]{1,0:T(8,128)(2,1)S(1)}, bf16[1024,128]{1,0:T(8,128)(2,1)S(1)}, u32[]{:S(2)}, u32[]{:S(2)}) collective-permute-start(bf16[1024,128]{1,0:T(8,128)(2,1)S(1)} %get-tuple-element.110), channel_id=1, source_target_pairs={{0,2},{2,0},{1,3},{3,1},{4,6},{6,4},{5,7},{7,5},{8,10},{10,8},{9,1... | collective-permute-start | bytes 786440 | tf_op jit(solution)/shard_map/ppermute | solution.py:358
  48.8 3.2 %back1.1 = (f32[768,256]{1,0:T(8,128)S(1)}, f32[1024,128]{1,0:T(8,128)S(1)}, bf16[1024,128]{1,0:T(8,128)(2,1)S(1)}) custom-call(bf16[768,256]{1,0:T(8,128)(2,1)S(1)} %get-tuple-element.103.refs_0_.refs_1_, bf16[768,256]{1,0:T(8,128)(2,1)S(1)} %get-tuple-element.103.refs_0_.refs_1_, bf16[768,256]{1,0:T(8,128)(2,1)S(1)} %get-tuple-element.82.refs_0_.refs_2_, ...), custom_call_target="tpu_custom_call" | custom-call | flops 2717908992 | bytes 4000000 | tf_op jit(solution)/shard_map/back1/pallas_call | solution.py:29
  52.1 3.3 %collective-permute-start.13 = (bf16[256,128]{1,0:T(8,128)(2,1)S(1)}, bf16[256,128]{1,0:T(8,128)(2,1)S(1)}, u32[]{:S(2)}, u32[]{:S(2)}) collective-permute-start(bf16[256,128]{1,0:T(8,128)(2,1)S(1)} %get-tuple-element.121), channel_id=1, source_target_pairs={{0,4},{4,8},{8,12},{12,0},{1,5},{5,9},{9,13},{13,1},{2,6},{6,10},{... | collective-permute-start | bytes 196616 | tf_op jit(solution)/shard_map/ppermute | solution.py:358
  56.9 1.5 %collective-permute-start.14 = (bf16[256,128]{1,0:T(8,128)(2,1)S(1)}, bf16[256,128]{1,0:T(8,128)(2,1)S(1)}, u32[]{:S(2)}, u32[]{:S(2)}) collective-permute-start(bf16[256,128]{1,0:T(8,128)(2,1)S(1)} %get-tuple-element.122), channel_id=1, source_target_pairs={{0,8},{4,12},{8,0},{12,4},{1,9},{5,13},{9,1},{13,5},{2,10},{6,14},... | collective-permute-start | bytes 196616 | tf_op jit(solution)/shard_map/ppermute | solution.py:358
  58.5 2.8 %collective-permute-start.15 = (bf16[256,128]{1,0:T(8,128)(2,1)S(1)}, bf16[256,128]{1,0:T(8,128)(2,1)S(1)}, u32[]{:S(2)}, u32[]{:S(2)}) collective-permute-start(bf16[256,128]{1,0:T(8,128)(2,1)S(1)} %get-tuple-element.123), channel_id=1, source_target_pairs={{0,12},{4,0},{8,4},{12,8},{1,13},{5,1},{9,5},{13,9},{2,14},{6,2},{... | collective-permute-start | bytes 196616 | tf_op jit(solution)/shard_map/ppermute | solution.py:358
  64.6 3.2 %back0.1 = (f32[768,256]{1,0:T(8,128)S(1)}, f32[1024,128]{1,0:T(8,128)S(1)}, bf16[1024,128]{1,0:T(8,128)(2,1)S(1)}) custom-call(bf16[768,256]{1,0:T(8,128)(2,1)S(1)} %get-tuple-element.115.refs_0_.refs_1_, bf16[768,256]{1,0:T(8,128)(2,1)S(1)} %get-tuple-element.115.refs_0_.refs_1_, bf16[768,256]{1,0:T(8,128)(2,1)S(1)} %copy-done.5, ...), custom_call_target="tpu_custom_call" | custom-call | flops 2717908992 | bytes 4000000 | tf_op jit(solution)/shard_map/back0/pallas_call | solution.py:29
  67.8 1.6 %collective-permute-start.22 = (bf16[1024,128]{1,0:T(8,128)(2,1)S(1)}, bf16[1024,128]{1,0:T(8,128)(2,1)S(1)}, u32[]{:S(2)}, u32[]{:S(2)}) collective-permute-start(bf16[1024,128]{1,0:T(8,128)(2,1)S(1)} %get-tuple-element.131), channel_id=1, source_target_pairs={{0,2},{2,0},{1,3},{3,1},{4,6},{6,4},{5,7},{7,5},{8,10},{10,8},{9,1... | collective-permute-start | bytes 786440 | tf_op jit(solution)/shard_map/ppermute | solution.py:358
  70.7 2.9 %collective-permute-start.20 = (bf16[256,128]{1,0:T(8,128)(2,1)S(1)}, bf16[256,128]{1,0:T(8,128)(2,1)S(1)}, u32[]{:S(2)}, u32[]{:S(2)}) collective-permute-start(bf16[256,128]{1,0:T(8,128)(2,1)S(1)} %end_2_0.1.refs_0_.refs_1_), channel_id=1, source_target_pairs={{0,8},{4,12},{8,0},{12,4},{1,9},{5,13},{9,1},{13,5},{2,10},{6,14},... | collective-permute-start | bytes 196616 | tf_op jit(solution)/shard_map/ppermute | solution.py:358
  74.9 2.6 %collective-permute-done.20.refs_3_ = bf16[256,128]{1,0:T(8,128)(2,1)S(1)} collective-permute-done((bf16[256,128]{1,0:T(8,128)(2,1)S(1)}, bf16[256,128]{1,0:T(8,128)(2,1)S(1)}, u32[]{:S(2)}, u32[]{:S(2)}) %collective-permute-start.20) | collective-permute-done | bytes 65568 | tf_op jit(solution)/shard_map/ppermute | solution.py:358
  77.5 2.9 %collective-permute-done.19.refs_2_ = bf16[256,128]{1,0:T(8,128)(2,1)S(1)} collective-permute-done((bf16[256,128]{1,0:T(8,128)(2,1)S(1)}, bf16[256,128]{1,0:T(8,128)(2,1)S(1)}, u32[]{:S(2)}, u32[]{:S(2)}) %collective-permute-start.19) | collective-permute-done | bytes 65568 | tf_op jit(solution)/shard_map/ppermute | solution.py:358
  82.2 3.8 %collective-permute-start.25 = (bf16[256,128]{1,0:T(8,128)(2,1)S(1)}, bf16[256,128]{1,0:T(8,128)(2,1)S(1)}, u32[]{:S(2)}, u32[]{:S(2)}) collective-permute-start(bf16[256,128]{1,0:T(8,128)(2,1)S(1)} %get-tuple-element.135), channel_id=1, source_target_pairs={{0,12},{4,0},{8,4},{12,8},{1,13},{5,1},{9,5},{13,9},{2,14},{6,2},{... | collective-permute-start | bytes 196616 | tf_op jit(solution)/shard_map/ppermute | solution.py:358
  86.6 1.6 %collective-permute-done.23.refs_2_ = bf16[256,128]{1,0:T(8,128)(2,1)S(1)} collective-permute-done((bf16[256,128]{1,0:T(8,128)(2,1)S(1)}, bf16[256,128]{1,0:T(8,128)(2,1)S(1)}, u32[]{:S(2)}, u32[]{:S(2)}) %collective-permute-start.23) | collective-permute-done | bytes 65568 | tf_op jit(solution)/shard_map/ppermute | solution.py:358
  88.3 2.8 %collective-permute-start.29 = (bf16[256,128]{1,0:T(8,128)(2,1)S(1)}, bf16[256,128]{1,0:T(8,128)(2,1)S(1)}, u32[]{:S(2)}, u32[]{:S(2)}) collective-permute-start(bf16[256,128]{1,0:T(8,128)(2,1)S(1)} %get-tuple-element.140), channel_id=1, source_target_pairs={{0,12},{4,0},{8,4},{12,8},{1,13},{5,1},{9,5},{13,9},{2,14},{6,2},{... | collective-permute-start | bytes 196616 | tf_op jit(solution)/shard_map/ppermute | solution.py:358
  91.1 1.6 %collective-permute-start.32 = (bf16[256,128]{1,0:T(8,128)(2,1)S(1)}, bf16[256,128]{1,0:T(8,128)(2,1)S(1)}, u32[]{:S(2)}, u32[]{:S(2)}) collective-permute-start(bf16[256,128]{1,0:T(8,128)(2,1)S(1)} %end_1_0.1.refs_0_.refs_1_), channel_id=1, source_target_pairs={{0,12},{4,0},{8,4},{12,8},{1,13},{5,1},{9,5},{13,9},{2,14},{6,2},{... | collective-permute-start | bytes 196616 | tf_op jit(solution)/shard_map/ppermute | solution.py:358
  96.8 2.9 %collective-permute-start.35 = (bf16[256,128]{1,0:T(8,128)(2,1)S(1)}, bf16[256,128]{1,0:T(8,128)(2,1)S(1)}, u32[]{:S(2)}, u32[]{:S(2)}) collective-permute-start(bf16[256,128]{1,0:T(8,128)(2,1)S(1)} %end_0_0.1.refs_0_.refs_1_), channel_id=1, source_target_pairs={{0,12},{4,0},{8,4},{12,8},{1,13},{5,1},{9,5},{13,9},{2,14},{6,2},{... | collective-permute-start | bytes 196616 | tf_op jit(solution)/shard_map/ppermute | solution.py:358
  100.9 1.8 %collective-permute-start.36 = (bf16[1024,128]{1,0:T(8,128)(2,1)S(1)}, bf16[1024,128]{1,0:T(8,128)(2,1)S(1)}, u32[]{:S(2)}, u32[]{:S(2)}) collective-permute-start(bf16[1024,128]{1,0:T(8,128)(2,1)S(1)} %place_1_0.1.refs_0_.refs_3_), channel_id=1, source_target_pairs={{0,2},{2,0},{1,3},{3,1},{4,6},{6,4},{5,7},{7,5},{8,10},{10,8},{9,1... | collective-permute-start | bytes 786440 | tf_op jit(solution)/shard_map/ppermute | solution.py:358
  102.7 2.1 %collective-permute-done.34.refs_3_ = bf16[256,128]{1,0:T(8,128)(2,1)S(1)} collective-permute-done((bf16[256,128]{1,0:T(8,128)(2,1)S(1)}, bf16[256,128]{1,0:T(8,128)(2,1)S(1)}, u32[]{:S(2)}, u32[]{:S(2)}) %collective-permute-start.34) | collective-permute-done | bytes 65568 | tf_op jit(solution)/shard_map/ppermute | solution.py:358
  104.9 1.6 %collective-permute-done.33.refs_2_ = bf16[256,128]{1,0:T(8,128)(2,1)S(1)} collective-permute-done((bf16[256,128]{1,0:T(8,128)(2,1)S(1)}, bf16[256,128]{1,0:T(8,128)(2,1)S(1)}, u32[]{:S(2)}, u32[]{:S(2)}) %collective-permute-start.33) | collective-permute-done | bytes 65568 | tf_op jit(solution)/shard_map/ppermute | solution.py:358
  106.5 2.1 %collective-permute-start.37 = (bf16[1024,128]{1,0:T(8,128)(2,1)S(1)}, bf16[1024,128]{1,0:T(8,128)(2,1)S(1)}, u32[]{:S(2)}, u32[]{:S(2)}) collective-permute-start(bf16[1024,128]{1,0:T(8,128)(2,1)S(1)} %place_0_0.1.refs_2_), channel_id=1, source_target_pairs={{0,2},{2,0},{1,3},{3,1},{4,6},{6,4},{5,7},{7,5},{8,10},{10,8},{9,1... | collective-permute-start | bytes 786440 | tf_op jit(solution)/shard_map/ppermute | solution.py:358
  109.8 3.2 %collective-permute-done.37.refs_3_ = bf16[1024,128]{1,0:T(8,128)(2,1)S(1)} collective-permute-done((bf16[1024,128]{1,0:T(8,128)(2,1)S(1)}, bf16[1024,128]{1,0:T(8,128)(2,1)S(1)}, u32[]{:S(2)}, u32[]{:S(2)}) %collective-permute-start.37) | collective-permute-done | bytes 262176 | tf_op jit(solution)/shard_map/ppermute | solution.py:358
  (93 shorter events, 33.9 us)
Async XLA Ops:
  0.6 14.2 %collective-permute-start = (bf16[3,256,512]{2,1,0:T(8,128)(2,1)}, bf16[3,256,512]{2,1,0:T(8,128)(2,1)S(1)}, u32[]{:S(2)}, u32[]{:S(2)}) collective-permute-start(bf16[3,256,512]{2,1,0:T(8,128)(2,1)} %refs_4_.15), channel_id=1, source_target_pairs={{0,1},{1,0},{2,3},{3,2},{4,5},{5,4},{6,7},{7,6},{8,9},{9,8},{10,11... | collective-permute-start | bytes 2359304 | tf_op jit(solution)/shard_map/ppermute | solution.py:358
  1.2 13.7 %collective-permute-start.1 = (bf16[3,512,256]{2,1,0:T(8,128)(2,1)}, bf16[3,512,256]{2,1,0:T(8,128)(2,1)S(1)}, u32[]{:S(2)}, u32[]{:S(2)}) collective-permute-start(bf16[3,512,256]{2,1,0:T(8,128)(2,1)} %refs_6_.11), channel_id=1, source_target_pairs={{0,1},{1,0},{2,3},{3,2},{4,5},{5,4},{6,7},{7,6},{8,9},{9,8},{10,11... | collective-permute-start | bytes 2359304 | tf_op jit(solution)/shard_map/ppermute | solution.py:358
  4.9 13.2 %collective-permute-start.2 = (bf16[128,256]{1,0:T(8,128)(2,1)}, bf16[128,256]{1,0:T(8,128)(2,1)S(1)}, u32[]{:S(2)}, u32[]{:S(2)}) collective-permute-start(bf16[128,256]{1,0:T(8,128)(2,1)} %get-tuple-element.79), channel_id=1, source_target_pairs={{0,4},{4,8},{8,12},{1,5},{5,9},{9,13},{2,6},{6,10},{10,14},{3,7},{... | collective-permute-start | bytes 196616 | tf_op jit(solution)/shard_map/ppermute | solution.py:353
  9.8 8.3 %collective-permute-start.3 = (bf16[128,256]{1,0:T(8,128)(2,1)S(1)}, bf16[128,256]{1,0:T(8,128)(2,1)S(1)}, u32[]{:S(2)}, u32[]{:S(2)}) collective-permute-start(bf16[128,256]{1,0:T(8,128)(2,1)S(1)} %get-tuple-element.80), channel_id=1, source_target_pairs={{0,2},{2,0},{1,3},{3,1},{4,6},{6,4},{5,7},{7,5},{8,10},{10,8},{9,1... | collective-permute-start | bytes 196616 | tf_op jit(solution)/shard_map/ppermute | solution.py:358
  19.4 6.2 %collective-permute-start.4 = (bf16[128,256]{1,0:T(8,128)(2,1)S(1)}, bf16[128,256]{1,0:T(8,128)(2,1)S(1)}, u32[]{:S(2)}, u32[]{:S(2)}) collective-permute-start(bf16[128,256]{1,0:T(8,128)(2,1)S(1)} %get-tuple-element.84), channel_id=1, source_target_pairs={{0,4},{4,8},{8,12},{1,5},{5,9},{9,13},{2,6},{6,10},{10,14},{3,7},{... | collective-permute-start | bytes 196616 | tf_op jit(solution)/shard_map/ppermute | solution.py:353
  28.5 6.2 %collective-permute-start.6 = (bf16[128,256]{1,0:T(8,128)(2,1)S(1)}, bf16[128,256]{1,0:T(8,128)(2,1)S(1)}, u32[]{:S(2)}, u32[]{:S(2)}) collective-permute-start(bf16[128,256]{1,0:T(8,128)(2,1)S(1)} %get-tuple-element.90), channel_id=1, source_target_pairs={{0,4},{4,8},{8,12},{1,5},{5,9},{9,13},{2,6},{6,10},{10,14},{3,7},{... | collective-permute-start | bytes 196616 | tf_op jit(solution)/shard_map/ppermute | solution.py:353
  38.6 6.8 %collective-permute-start.8 = (bf16[128,256]{1,0:T(8,128)(2,1)S(1)}, bf16[128,256]{1,0:T(8,128)(2,1)S(1)}, u32[]{:S(2)}, u32[]{:S(2)}) collective-permute-start(bf16[128,256]{1,0:T(8,128)(2,1)S(1)} %get-tuple-element.101), channel_id=1, source_target_pairs={{4,0},{8,4},{12,8},{5,1},{9,5},{13,9},{6,2},{10,6},{14,10},{7,3},{... | collective-permute-start | bytes 196616 | tf_op jit(solution)/shard_map/ppermute | solution.py:353
  43.8 8.1 %collective-permute-start.10 = (bf16[1024,128]{1,0:T(8,128)(2,1)S(1)}, bf16[1024,128]{1,0:T(8,128)(2,1)S(1)}, u32[]{:S(2)}, u32[]{:S(2)}) collective-permute-start(bf16[1024,128]{1,0:T(8,128)(2,1)S(1)} %get-tuple-element.110), channel_id=1, source_target_pairs={{0,2},{2,0},{1,3},{3,1},{4,6},{6,4},{5,7},{7,5},{8,10},{10,8},{9,1... | collective-permute-start | bytes 786440 | tf_op jit(solution)/shard_map/ppermute | solution.py:358
  46.9 11.6 %collective-permute-start.11 = (bf16[128,256]{1,0:T(8,128)(2,1)S(1)}, bf16[128,256]{1,0:T(8,128)(2,1)S(1)}, u32[]{:S(2)}, u32[]{:S(2)}) collective-permute-start(bf16[128,256]{1,0:T(8,128)(2,1)S(1)} %get-tuple-element.113), channel_id=1, source_target_pairs={{4,0},{8,4},{12,8},{5,1},{9,5},{13,9},{6,2},{10,6},{14,10},{7,3},{... | collective-permute-start | bytes 196616 | tf_op jit(solution)/shard_map/ppermute | solution.py:353
  48.2 13.1 %collective-permute-start.12 = (bf16[128,256]{1,0:T(8,128)(2,1)S(1)}, bf16[128,256]{1,0:T(8,128)(2,1)S(1)}, u32[]{:S(2)}, u32[]{:S(2)}) collective-permute-start(bf16[128,256]{1,0:T(8,128)(2,1)S(1)} %get-tuple-element.114), channel_id=1, source_target_pairs={{0,2},{2,0},{1,3},{3,1},{4,6},{6,4},{5,7},{7,5},{8,10},{10,8},{9,1... | collective-permute-start | bytes 196616 | tf_op jit(solution)/shard_map/ppermute | solution.py:358
  52.1 12.0 %collective-permute-start.13 = (bf16[256,128]{1,0:T(8,128)(2,1)S(1)}, bf16[256,128]{1,0:T(8,128)(2,1)S(1)}, u32[]{:S(2)}, u32[]{:S(2)}) collective-permute-start(bf16[256,128]{1,0:T(8,128)(2,1)S(1)} %get-tuple-element.121), channel_id=1, source_target_pairs={{0,4},{4,8},{8,12},{12,0},{1,5},{5,9},{9,13},{13,1},{2,6},{6,10},{... | collective-permute-start | bytes 196616 | tf_op jit(solution)/shard_map/ppermute | solution.py:358
  55.4 15.3 %collective-permute-start.16 = (bf16[1024,128]{1,0:T(8,128)(2,1)S(1)}, bf16[1024,128]{1,0:T(8,128)(2,1)S(1)}, u32[]{:S(2)}, u32[]{:S(2)}) collective-permute-start(bf16[1024,128]{1,0:T(8,128)(2,1)S(1)} %get-tuple-element.125), channel_id=1, source_target_pairs={{0,2},{2,0},{1,3},{3,1},{4,6},{6,4},{5,7},{7,5},{8,10},{10,8},{9,1... | collective-permute-start | bytes 786440 | tf_op jit(solution)/shard_map/ppermute | solution.py:358
  56.9 10.9 %collective-permute-start.14 = (bf16[256,128]{1,0:T(8,128)(2,1)S(1)}, bf16[256,128]{1,0:T(8,128)(2,1)S(1)}, u32[]{:S(2)}, u32[]{:S(2)}) collective-permute-start(bf16[256,128]{1,0:T(8,128)(2,1)S(1)} %get-tuple-element.122), channel_id=1, source_target_pairs={{0,8},{4,12},{8,0},{12,4},{1,9},{5,13},{9,1},{13,5},{2,10},{6,14},... | collective-permute-start | bytes 196616 | tf_op jit(solution)/shard_map/ppermute | solution.py:358
  58.5 11.0 %collective-permute-start.15 = (bf16[256,128]{1,0:T(8,128)(2,1)S(1)}, bf16[256,128]{1,0:T(8,128)(2,1)S(1)}, u32[]{:S(2)}, u32[]{:S(2)}) collective-permute-start(bf16[256,128]{1,0:T(8,128)(2,1)S(1)} %get-tuple-element.123), channel_id=1, source_target_pairs={{0,12},{4,0},{8,4},{12,8},{1,13},{5,1},{9,5},{13,9},{2,14},{6,2},{... | collective-permute-start | bytes 196616 | tf_op jit(solution)/shard_map/ppermute | solution.py:358
  62.8 10.9 %collective-permute-start.17 = (bf16[128,256]{1,0:T(8,128)(2,1)S(1)}, bf16[128,256]{1,0:T(8,128)(2,1)S(1)}, u32[]{:S(2)}, u32[]{:S(2)}) collective-permute-start(bf16[128,256]{1,0:T(8,128)(2,1)S(1)} %get-tuple-element.128), channel_id=1, source_target_pairs={{4,0},{8,4},{12,8},{5,1},{9,5},{13,9},{6,2},{10,6},{14,10},{7,3},{... | collective-permute-start | bytes 196616 | tf_op jit(solution)/shard_map/ppermute | solution.py:353
  64.1 9.7 %collective-permute-start.18 = (bf16[128,256]{1,0:T(8,128)(2,1)S(1)}, bf16[128,256]{1,0:T(8,128)(2,1)S(1)}, u32[]{:S(2)}, u32[]{:S(2)}) collective-permute-start(bf16[128,256]{1,0:T(8,128)(2,1)S(1)} %get-tuple-element.129), channel_id=1, source_target_pairs={{0,2},{2,0},{1,3},{3,1},{4,6},{6,4},{5,7},{7,5},{8,10},{10,8},{9,1... | collective-permute-start | bytes 196616 | tf_op jit(solution)/shard_map/ppermute | solution.py:358
  67.8 18.1 %collective-permute-start.22 = (bf16[1024,128]{1,0:T(8,128)(2,1)S(1)}, bf16[1024,128]{1,0:T(8,128)(2,1)S(1)}, u32[]{:S(2)}, u32[]{:S(2)}) collective-permute-start(bf16[1024,128]{1,0:T(8,128)(2,1)S(1)} %get-tuple-element.131), channel_id=1, source_target_pairs={{0,2},{2,0},{1,3},{3,1},{4,6},{6,4},{5,7},{7,5},{8,10},{10,8},{9,1... | collective-permute-start | bytes 786440 | tf_op jit(solution)/shard_map/ppermute | solution.py:358
  70.7 6.8 %collective-permute-start.20 = (bf16[256,128]{1,0:T(8,128)(2,1)S(1)}, bf16[256,128]{1,0:T(8,128)(2,1)S(1)}, u32[]{:S(2)}, u32[]{:S(2)}) collective-permute-start(bf16[256,128]{1,0:T(8,128)(2,1)S(1)} %end_2_0.1.refs_0_.refs_1_), channel_id=1, source_target_pairs={{0,8},{4,12},{8,0},{12,4},{1,9},{5,13},{9,1},{13,5},{2,10},{6,14},... | collective-permute-start | bytes 196616 | tf_op jit(solution)/shard_map/ppermute | solution.py:358
  73.6 6.8 %collective-permute-start.19 = (bf16[256,128]{1,0:T(8,128)(2,1)S(1)}, bf16[256,128]{1,0:T(8,128)(2,1)S(1)}, u32[]{:S(2)}, u32[]{:S(2)}) collective-permute-start(bf16[256,128]{1,0:T(8,128)(2,1)S(1)} %end_2_0.1.refs_0_.refs_1_), channel_id=1, source_target_pairs={{0,4},{4,8},{8,12},{12,0},{1,5},{5,9},{9,13},{13,1},{2,6},{6,10},{... | collective-permute-start | bytes 196616 | tf_op jit(solution)/shard_map/ppermute | solution.py:358
  81.6 11.1 %collective-permute-start.26 = (bf16[1024,128]{1,0:T(8,128)(2,1)S(1)}, bf16[1024,128]{1,0:T(8,128)(2,1)S(1)}, u32[]{:S(2)}, u32[]{:S(2)}) collective-permute-start(bf16[1024,128]{1,0:T(8,128)(2,1)S(1)} %place_2_0.1.refs_0_.refs_1_), channel_id=1, source_target_pairs={{0,2},{2,0},{1,3},{3,1},{4,6},{6,4},{5,7},{7,5},{8,10},{10,8},{9,1... | collective-permute-start | bytes 786440 | tf_op jit(solution)/shard_map/ppermute | solution.py:358
  82.1 6.2 %collective-permute-start.23 = (bf16[256,128]{1,0:T(8,128)(2,1)S(1)}, bf16[256,128]{1,0:T(8,128)(2,1)S(1)}, u32[]{:S(2)}, u32[]{:S(2)}) collective-permute-start(bf16[256,128]{1,0:T(8,128)(2,1)S(1)} %get-tuple-element.133), channel_id=1, source_target_pairs={{0,4},{4,8},{8,12},{12,0},{1,5},{5,9},{9,13},{13,1},{2,6},{6,10},{... | collective-permute-start | bytes 196616 | tf_op jit(solution)/shard_map/ppermute | solution.py:358
  82.1 6.2 %collective-permute-start.24 = (bf16[256,128]{1,0:T(8,128)(2,1)S(1)}, bf16[256,128]{1,0:T(8,128)(2,1)S(1)}, u32[]{:S(2)}, u32[]{:S(2)}) collective-permute-start(bf16[256,128]{1,0:T(8,128)(2,1)S(1)} %get-tuple-element.134), channel_id=1, source_target_pairs={{0,8},{4,12},{8,0},{12,4},{1,9},{5,13},{9,1},{13,5},{2,10},{6,14},... | collective-permute-start | bytes 196616 | tf_op jit(solution)/shard_map/ppermute | solution.py:358
  82.2 8.9 %collective-permute-start.25 = (bf16[256,128]{1,0:T(8,128)(2,1)S(1)}, bf16[256,128]{1,0:T(8,128)(2,1)S(1)}, u32[]{:S(2)}, u32[]{:S(2)}) collective-permute-start(bf16[256,128]{1,0:T(8,128)(2,1)S(1)} %get-tuple-element.135), channel_id=1, source_target_pairs={{0,12},{4,0},{8,4},{12,8},{1,13},{5,1},{9,5},{13,9},{2,14},{6,2},{... | collective-permute-start | bytes 196616 | tf_op jit(solution)/shard_map/ppermute | solution.py:358
  86.0 8.3 %collective-permute-start.27 = (bf16[256,128]{1,0:T(8,128)(2,1)S(1)}, bf16[256,128]{1,0:T(8,128)(2,1)S(1)}, u32[]{:S(2)}, u32[]{:S(2)}) collective-permute-start(bf16[256,128]{1,0:T(8,128)(2,1)S(1)} %get-tuple-element.138), channel_id=1, source_target_pairs={{0,4},{4,8},{8,12},{12,0},{1,5},{5,9},{9,13},{13,1},{2,6},{6,10},{... | collective-permute-start | bytes 196616 | tf_op jit(solution)/shard_map/ppermute | solution.py:358
  88.3 7.1 %collective-permute-start.28 = (bf16[256,128]{1,0:T(8,128)(2,1)S(1)}, bf16[256,128]{1,0:T(8,128)(2,1)S(1)}, u32[]{:S(2)}, u32[]{:S(2)}) collective-permute-start(bf16[256,128]{1,0:T(8,128)(2,1)S(1)} %get-tuple-element.139), channel_id=1, source_target_pairs={{0,8},{4,12},{8,0},{12,4},{1,9},{5,13},{9,1},{13,5},{2,10},{6,14},... | collective-permute-start | bytes 196616 | tf_op jit(solution)/shard_map/ppermute | solution.py:358
  88.3 7.1 %collective-permute-start.29 = (bf16[256,128]{1,0:T(8,128)(2,1)S(1)}, bf16[256,128]{1,0:T(8,128)(2,1)S(1)}, u32[]{:S(2)}, u32[]{:S(2)}) collective-permute-start(bf16[256,128]{1,0:T(8,128)(2,1)S(1)} %get-tuple-element.140), channel_id=1, source_target_pairs={{0,12},{4,0},{8,4},{12,8},{1,13},{5,1},{9,5},{13,9},{2,14},{6,2},{... | collective-permute-start | bytes 196616 | tf_op jit(solution)/shard_map/ppermute | solution.py:358
  91.1 9.3 %collective-permute-start.32 = (bf16[256,128]{1,0:T(8,128)(2,1)S(1)}, bf16[256,128]{1,0:T(8,128)(2,1)S(1)}, u32[]{:S(2)}, u32[]{:S(2)}) collective-permute-start(bf16[256,128]{1,0:T(8,128)(2,1)S(1)} %end_1_0.1.refs_0_.refs_1_), channel_id=1, source_target_pairs={{0,12},{4,0},{8,4},{12,8},{1,13},{5,1},{9,5},{13,9},{2,14},{6,2},{... | collective-permute-start | bytes 196616 | tf_op jit(solution)/shard_map/ppermute | solution.py:358
  92.8 8.1 %collective-permute-start.31 = (bf16[256,128]{1,0:T(8,128)(2,1)S(1)}, bf16[256,128]{1,0:T(8,128)(2,1)S(1)}, u32[]{:S(2)}, u32[]{:S(2)}) collective-permute-start(bf16[256,128]{1,0:T(8,128)(2,1)S(1)} %end_1_0.1.refs_0_.refs_1_), channel_id=1, source_target_pairs={{0,8},{4,12},{8,0},{12,4},{1,9},{5,13},{9,1},{13,5},{2,10},{6,14},... | collective-permute-start | bytes 196616 | tf_op jit(solution)/shard_map/ppermute | solution.py:358
  94.3 6.6 %collective-permute-start.30 = (bf16[256,128]{1,0:T(8,128)(2,1)S(1)}, bf16[256,128]{1,0:T(8,128)(2,1)S(1)}, u32[]{:S(2)}, u32[]{:S(2)}) collective-permute-start(bf16[256,128]{1,0:T(8,128)(2,1)S(1)} %end_1_0.1.refs_0_.refs_1_), channel_id=1, source_target_pairs={{0,4},{4,8},{8,12},{12,0},{1,5},{5,9},{9,13},{13,1},{2,6},{6,10},{... | collective-permute-start | bytes 196616 | tf_op jit(solution)/shard_map/ppermute | solution.py:358
  100.4 6.1 %collective-permute-start.33 = (bf16[256,128]{1,0:T(8,128)(2,1)S(1)}, bf16[256,128]{1,0:T(8,128)(2,1)S(1)}, u32[]{:S(2)}, u32[]{:S(2)}) collective-permute-start(bf16[256,128]{1,0:T(8,128)(2,1)S(1)} %end_0_0.1.refs_0_.refs_1_), channel_id=1, source_target_pairs={{0,4},{4,8},{8,12},{12,0},{1,5},{5,9},{9,13},{13,1},{2,6},{6,10},{... | collective-permute-start | bytes 196616 | tf_op jit(solution)/shard_map/ppermute | solution.py:358
  100.9 7.8 %collective-permute-start.36 = (bf16[1024,128]{1,0:T(8,128)(2,1)S(1)}, bf16[1024,128]{1,0:T(8,128)(2,1)S(1)}, u32[]{:S(2)}, u32[]{:S(2)}) collective-permute-start(bf16[1024,128]{1,0:T(8,128)(2,1)S(1)} %place_1_0.1.refs_0_.refs_3_), channel_id=1, source_target_pairs={{0,2},{2,0},{1,3},{3,1},{4,6},{6,4},{5,7},{7,5},{8,10},{10,8},{9,1... | collective-permute-start | bytes 786440 | tf_op jit(solution)/shard_map/ppermute | solution.py:358
  106.5 6.5 %collective-permute-start.37 = (bf16[1024,128]{1,0:T(8,128)(2,1)S(1)}, bf16[1024,128]{1,0:T(8,128)(2,1)S(1)}, u32[]{:S(2)}, u32[]{:S(2)}) collective-permute-start(bf16[1024,128]{1,0:T(8,128)(2,1)S(1)} %place_0_0.1.refs_2_), channel_id=1, source_target_pairs={{0,2},{2,0},{1,3},{3,1},{4,6},{6,4},{5,7},{7,5},{8,10},{10,8},{9,1... | collective-permute-start | bytes 786440 | tf_op jit(solution)/shard_map/ppermute | solution.py:358
  (17 other events, 69.1 us)

commit v4 on v1

v4 whole, which is shorter than its diff:
```python
import functools

import jax
import jax.numpy as jnp
from jax import lax
from jax.experimental import pallas as pl
from jax.experimental.pallas import tpu as pltpu
from jax.sharding import PartitionSpec as P

BLOCK = 128
LANES = 128
EPS = 1e-06
F32 = jnp.float32
BF16 = jnp.bfloat16
VMEM = pl.BlockSpec(memory_space=pltpu.VMEM)
SMEM = pl.BlockSpec(memory_space=pltpu.SMEM)
ANY = pl.BlockSpec(memory_space=pl.ANY)
NN = (((1,), (0,)), ((), ()))
NT = (((1,), (1,)), ((), ()))
TN = (((0,), (0,)), ((), ()))


def mm(a, b, dims=NN):
    return lax.dot_general(a, b, dims, preferred_element_type=F32)


LIMIT = 24 * 1024 * 1024


def call(body, outs, ins, flops, scratch=(), name=None, after=()):
    skipped = len(after)
    return pl.pallas_call(
        lambda *refs: body(*refs[skipped:]),
        out_shape=[jax.ShapeDtypeStruct(s, d) for s, d in outs],
        in_specs=[ANY] * skipped + [SMEM if x.ndim == 2 and x.shape[1] == 4 else VMEM for x in ins],
        out_specs=[VMEM] * len(outs),
        scratch_shapes=list(scratch),
        compiler_params=pltpu.CompilerParams(vmem_limit_bytes=LIMIT),
        cost_estimate=pl.CostEstimate(flops=flops, bytes_accessed=4_000_000, transcendentals=0),
        name=name,
    )(*after, *ins)


def sigmoid(v):
    return 1.0 / (1.0 + jnp.exp(-v))


def message_of(x, halves):
    total = None
    for w_in, w_out in halves:
        pre = mm(x, w_in)
        part = mm((pre * sigmoid(pre)).astype(BF16), w_out)
        total = part if total is None else total + part
    return total.astype(BF16)


def message_grad(x, dmsg, halves):
    total = None
    kept = None
    for w_in, w_out in halves:
        pre = mm(x, w_in)
        sig = sigmoid(pre)
        dact = mm(dmsg, w_out, NT)
        dpre = (dact * (sig * (1.0 + pre * (1.0 - sig)))).astype(BF16)
        if kept is None:
            kept = ((pre * sig).astype(BF16), dpre)
        part = mm(dpre, w_in, NT)
        total = part if total is None else total + part
    return total, kept


def normed_of(total):
    scale = lax.rsqrt(jnp.mean(total * total, axis=-1, keepdims=True) + EPS)
    return scale, scale * total


def norm_grad(grad, total):
    scale, normed = normed_of(total)
    return scale * (grad - normed * jnp.mean(grad * normed, axis=-1, keepdims=True))


def route_place(route, feat, pairs):
    return route // 2 + jnp.where(route % 2 == feat, 0, pairs)


def setup_kernel(groups, pairs, features, sent, *refs):
    pick, spread, pick_self = refs[:3]
    sends = refs[3:]
    rows = features.shape[0]
    b, feat = lax.axis_index("basin"), lax.axis_index("feat")
    for route in range(-1, 2 * pairs):
        if route == 0:
            chosen = lax.broadcasted_iota(jnp.int32, (1, BLOCK), 1) + (rows - BLOCK)
        elif route >= groups:
            chosen = jnp.full((1, BLOCK), -1, jnp.int32)
        else:
            chosen = sent[pl.ds(lax.rem(b + max(route, 0), groups), 1), :]
        across = jnp.broadcast_to(chosen, (BLOCK, BLOCK))
        down = across.T
        for r in range(0, rows, BLOCK):
            at = lax.broadcasted_iota(jnp.int32, (BLOCK, BLOCK), 1) + r
            hot = (down == at).astype(F32).astype(BF16)
            if route < 0:
                pick_self[:, r : r + BLOCK] = hot
                continue

            @pl.when(route % 2 == feat)
            def _():
                pick[route // 2 * BLOCK : (route // 2 + 1) * BLOCK, r : r + BLOCK] = hot

            at = lax.broadcasted_iota(jnp.int32, (BLOCK, BLOCK), 0) + r
            place = pl.multiple_of(route_place(route, feat, pairs) * BLOCK, BLOCK)
            spread[r : r + BLOCK, pl.ds(place, BLOCK)] = (across == at).astype(F32).astype(BF16)
    for i, send in enumerate(sends):
        send[...] = mm(pick[i * BLOCK : (i + 1) * BLOCK, :], features[...]).astype(BF16)


def build_adjacency(groups, pairs, rows, index, values, pick_self, outs, acc):
    local, local_t, remote, remote_t = outs
    own = rows // BLOCK
    b, feat = lax.axis_index("basin"), lax.axis_index("feat")
    acc[...] = jnp.zeros_like(acc)
    for k in range(own):
        for t in range(index.shape[1]):
            v = index[k, t]
            route = jnp.where(v == own, 0, lax.rem(b + groups - (v - own - 1), groups))
            far = own + 1 + route_place(route, feat, pairs)
            far = jnp.where((v > own) & (route == 0), own, far)
            at = jnp.where(v < own, v, far)
            here = (pl.ds(k * BLOCK, BLOCK), pl.ds(pl.multiple_of(at * BLOCK, BLOCK), BLOCK))
            acc[here] += values[k, t].astype(F32)
    mine = acc[:, rows : rows + BLOCK].astype(BF16)
    full = acc[:, :rows] + mm(mine, pick_self[...])
    local[...] = full.astype(BF16)
    local_t[...] = full.T.astype(BF16)
    far = acc[:, rows + BLOCK :]
    remote[...] = far.astype(BF16)
    remote_t[...] = far.T.astype(BF16)


def own_messages(layer, inputs, weights, msg):
    wi0, wi1, wo0, wo1 = weights
    halves = [(wi0[layer], wo0[layer]), (wi1[layer], wo1[layer])]
    for r in range(0, inputs.shape[0], 256):
        msg[r : r + 256, :] = message_of(inputs[r : r + 256, :], halves)


def first_kernel(groups, pairs, *refs):
    inputs, pick_self, index, values = refs[:4]
    weights, msg, outs = refs[4:8], refs[8], refs[9:13]
    own_messages(0, inputs, weights, msg)
    build_adjacency(groups, pairs, inputs.shape[0], index, values, pick_self, outs, refs[13])


def local_kernel(layer, *refs):
    own_messages(layer, refs[0], refs[1:5], refs[5])


def remote_mixed(layer, received, remote, weights):
    wi0, wi1, wo0, wo1 = weights
    halves = [(wi0[layer], wo0[layer]), (wi1[layer], wo1[layer])]
    far = jnp.concatenate([x[...] for x in received], axis=0)
    return mm(remote, message_of(far, halves))


def part_kernel(layer, pairs, *refs):
    local, msg, remote = refs[:3]
    weights, received, mixed = refs[3:7], refs[7 : 7 + pairs], refs[-1]
    mixed[...] = mm(local[...], msg[...]) + remote_mixed(
        layer, received, remote[:, : pairs * BLOCK], weights
    )


def mixed_total(layer, state, mixed, received, remote, weights):
    return state + mixed[...] + remote_mixed(
        layer, received, remote[:, len(received) * BLOCK :], weights
    )


def mix_kernel(layer, pairs, *refs):
    prev, mixed, remote, pick = refs[:4]
    weights = refs[4:8]
    received = refs[8 : 8 + pairs]
    total, inputs = refs[8 + pairs : 10 + pairs]
    sends = refs[10 + pairs :]
    state = prev[...].astype(F32) if layer == 0 else normed_of(prev[...])[1]
    total[...] = mixed_total(layer, state, mixed, received, remote, weights)
    new = normed_of(total[...])[1].astype(BF16)
    inputs[...] = new
    for i, send in enumerate(sends):
        send[...] = mm(pick[i * BLOCK : (i + 1) * BLOCK, :], new).astype(BF16)


def start_bwd(layer, dtotal_now, weights, received, remote_t, outs):
    dtotal, dround, far_dmsg, far_act, far_dpre = outs[:5]
    backs = outs[5:]
    wi0, wi1, wo0, wo1 = weights
    halves = [(wi0[layer], wo0[layer]), (wi1[layer], wo1[layer])]
    dtotal[...] = dtotal_now
    dround[...] = dtotal_now.astype(BF16)
    far = jnp.concatenate([x[...] for x in received], axis=0)
    dmsg = mm(remote_t[: far.shape[0], :], dround[...]).astype(BF16)
    back, (act, dpre) = message_grad(far, dmsg, halves)
    far_dmsg[...] = dmsg
    far_act[...] = act
    far_dpre[...] = dpre
    for i, out in enumerate(backs):
        out[...] = back[i * BLOCK : (i + 1) * BLOCK, :].astype(BF16)


def turn_kernel(layer, pairs, *refs):
    prev, mixed, remote, remote_t, cot = refs[:5]
    weights = refs[5:9]
    mine, others = refs[9 : 9 + pairs], refs[9 + pairs : 9 + 2 * pairs]
    outs = refs[9 + 2 * pairs :]
    state = normed_of(prev[...])[1]
    total = mixed_total(layer, state, mixed, others, remote, weights)
    start_bwd(layer, norm_grad(cot[...], total), weights, mine, remote_t, outs)


def back_kernel(layer, *refs):
    dround, inputs, local_t = refs[:3]
    wi0, wi1, wo0, wo1 = refs[3:7]
    back, dmsg, act, dpre = refs[7:]
    halves = [(wi0[layer], wo0[layer]), (wi1[layer], wo1[layer])]
    dmsg[...] = mm(local_t[...], dround[...]).astype(BF16)
    for r in range(0, inputs.shape[0], 256):
        here = slice(r, r + 256)
        back[here, :], (act[here, :], dpre[here, :]) = message_grad(
            inputs[here, :], dmsg[here, :], halves
        )


def weights_kernel(layer, grad_scale, pairs, pieces, *refs):
    dround, remote_t, w_in, w_out, inputs, dmsg, act, dpre = refs[:8]
    far_dmsg, far_act, far_dpre = refs[8:11]
    mine, others = refs[11 : 11 + pairs], refs[11 + pairs : 11 + 2 * pairs]
    outs = refs[11 + 2 * pairs : -1]
    grads = refs[-1]
    near = jnp.concatenate([x[...] for x in mine], axis=0)
    far = jnp.concatenate([x[...] for x in others], axis=0)
    dmsg2 = mm(remote_t[near.shape[0] :, :], dround[...]).astype(BF16)
    pre = mm(far, w_in[layer])
    sig = sigmoid(pre)
    dpre2 = (mm(dmsg2, w_out[layer], NT) * (sig * (1.0 + pre * (1.0 - sig)))).astype(BF16)
    act2 = (pre * sig).astype(BF16)
    latent, hidden = inputs.shape[1], act.shape[1]
    g_in = mm(inputs[...], dpre[...], TN) + mm(near, far_dpre[...], TN) + mm(far, dpre2, TN)
    g_in = g_in * grad_scale
    for j in range(hidden // LANES):
        grads[j * latent : (j + 1) * latent, :] = g_in[:, j * LANES : (j + 1) * LANES]
    g_out = mm(act[...], dmsg[...], TN) + mm(far_act[...], far_dmsg[...], TN) + mm(act2, dmsg2, TN)
    g_out = g_out * grad_scale
    for j in range(latent // LANES):
        at = hidden // LANES * latent + j * hidden
        grads[at : at + hidden, :] = g_out[:, j * LANES : (j + 1) * LANES]
    for lo, hi, stages in pieces:
        if stages:
            split(grads.at[lo:hi], stages[0], outs[:2])
            outs = outs[2:]
        else:
            outs[0][...] = grads[lo:hi, :].astype(BF16)
            outs = outs[1:]


def upper(stage):
    axis, d = stage
    return lax.rem(lax.axis_index(axis) // d, 2)


def split(block, stage, outs):
    m = block.shape[0] // 2
    bit = upper(stage)
    keep, send = outs
    keep[...] = block[pl.ds(pl.multiple_of(bit * m, m), m), :]
    send[...] = block[pl.ds(pl.multiple_of((1 - bit) * m, m), m), :].astype(BF16)


def add_split_kernel(stage, keep, got, *refs):
    acc = refs[-1]
    acc[...] = keep[...] + got[...].astype(F32)
    split(acc, stage, refs[:-1])


def add_kernel(keep, got, out):
    out[...] = (keep[...] + got[...].astype(F32)).astype(BF16)


def place(stage, own, got, out):
    m = own.shape[0]
    bit = upper(stage)
    out[pl.ds(pl.multiple_of(bit * m, m), m), :] = own[...].astype(out.dtype)
    out[pl.ds(pl.multiple_of((1 - bit) * m, m), m), :] = got[...].astype(out.dtype)


def place_kernel(stage, own, got, out):
    place(stage, own, got, out)


def write_kernel(layer, pieces, kept, *refs):
    out_in, out_out, token, grads, slab_in, slab_out, sem = refs[-7:]
    parts = refs[kept:-7]
    token[...] = jnp.zeros_like(token)
    for lo, hi, stages in pieces:
        if stages:
            place(stages[0], parts[0], parts[1], grads.at[lo:hi])
            parts = parts[2:]
        else:
            grads[lo:hi, :] = parts[0][...].astype(F32)
            parts = parts[1:]
    latent, hidden = slab_in.shape
    for j in range(hidden // LANES):
        slab_in[:, j * LANES : (j + 1) * LANES] = grads[j * latent : (j + 1) * latent, :]
    first = pltpu.make_async_copy(slab_in, out_in.at[layer], sem.at[0])
    first.start()
    for j in range(latent // LANES):
        at = hidden // LANES * latent + j * hidden
        slab_out[:, j * LANES : (j + 1) * LANES] = grads[at : at + hidden, :]
    second = pltpu.make_async_copy(slab_out, out_out.at[layer], sem.at[1])
    second.start()
    first.wait()
    second.wait()


class Sum:
    def __init__(self, parts, stages, name):
        self.stages, self.name = stages, name
        self.done = 0
        if stages:
            self.keep, send = parts
            self.got = swapped(send, stages[0])
        else:
            self.parts = [lax.psum(parts[0], ("chain", "basin"))]

    def step(self, after):
        n = len(self.stages)
        i = self.done
        self.done += 1
        name = f"sum_{self.name}_{i}"
        if i < n - 1:
            half = (self.keep.shape[0] // 2, LANES)
            self.keep, send = call(
                functools.partial(add_split_kernel, self.stages[i + 1]),
                [(half, F32), (half, BF16)],
                [self.keep, self.got],
                1_000_000,
                scratch=[pltpu.VMEM(self.keep.shape, F32)],
                name=name,
                after=after,
            )
            self.got = swapped(send, self.stages[i + 1])
        else:
            if i == n - 1:
                body, shape = add_kernel, self.keep.shape
            else:
                body = functools.partial(place_kernel, self.stages[2 * n - 1 - i])
                shape = (self.keep.shape[0] * 2, LANES)
            (self.keep,) = call(
                body, [(shape, BF16)], [self.keep, self.got], 1_000_000, name=name, after=after
            )
            self.got = swapped(self.keep, self.stages[2 * n - 2 - i])
        self.parts = [self.keep, self.got]
        return [self.keep]


def gathered_grad(dtotal, back, returned, spread):
    far = jnp.concatenate([x[...] for x in returned], axis=0)
    return dtotal[...] + back[...] + mm(spread[...], far)


def join_kernel(layer, pairs, *refs):
    dtotal, back, spread, remote_t, total = refs[:5]
    weights = refs[5:9]
    returned = refs[9 : 9 + 2 * pairs]
    mine = refs[9 + 2 * pairs : 9 + 3 * pairs]
    outs = refs[9 + 3 * pairs :]
    grad = gathered_grad(dtotal, back, returned, spread)
    start_bwd(layer, norm_grad(grad, total[...]), weights, mine, remote_t, outs)


def last_kernel(*refs):
    dtotal, back, spread = refs[:3]
    refs[-2][...] = gathered_grad(dtotal, back, refs[3:-2], spread)
    refs[-1][...] = jnp.zeros_like(refs[-1])


def around(x, axis, distance):
    n = lax.axis_size(axis)
    return lax.ppermute(x, axis, [(i, (i + distance) % n) for i in range(n)])


def swapped(x, stage):
    axis, d = stage
    return lax.ppermute(x, axis, [(i, i ^ d) for i in range(lax.axis_size(axis))])


def routed(sends, sign):
    chain, groups = lax.axis_size("chain"), lax.axis_size("basin")
    got = []
    for i, x in enumerate(sends):
        perm = []
        for c in range(chain):
            for b in range(groups):
                for feat in range(2):
                    route = 2 * i + feat
                    to_c = c + sign if route == 0 else c
                    to_b = (b + sign * route) % groups
                    if 0 <= to_c < chain and route < groups:
                        start, end = (c * groups + b) * 2 + feat, (to_c * groups + to_b) * 2 + feat
                        perm.append((start, end))
        got.append(lax.ppermute(x, ("chain", "basin", "feat"), perm))
    return got


def other_core(got):
    return [around(x, "feat", 1) for x in got]


def shards(features, cotangent, w_in, w_out, block_index, block_values, send_rows, send_count):
    rows, latent = features.shape
    groups = lax.axis_size("basin")
    pairs = (groups + 1) // 2
    layers, _, half = w_in.shape
    far_rows = 2 * pairs * BLOCK
    own = rows // BLOCK
    grad_scale = float(rows * lax.axis_size("chain") * groups) ** (-0.5)
    last = layers - 1

    def act16(n, m=latent):
        return ((n, m), BF16)

    wi1 = around(w_in, "feat", 1)
    wo1 = around(w_out, "feat", 1)
    ffn = 4 * latent * 2 * half

    live = jnp.arange(BLOCK, dtype=jnp.int32)[None, :] < send_count[0][:, None]
    pick, spread, pick_self, *sends = call(
        functools.partial(setup_kernel, groups, pairs),
        [act16(pairs * BLOCK, rows), act16(rows, far_rows), act16(BLOCK, rows)]
        + [act16(BLOCK)] * pairs,
        [features, jnp.where(live, send_rows[0], -1)],
        2 * rows * far_rows * latent,
        name="setup",
    )
    weights = (w_in, wi1, w_out, wo1)
    msg, local, local_t, remote, remote_t = [None] * 5
    inputs = [features]
    totals = []
    mine = []
    others = []
    for layer in range(layers):
        mine.append(routed(sends, 1))
        if layer == 0:
            msg, local, local_t, remote, remote_t = call(
                functools.partial(first_kernel, groups, pairs),
                [act16(rows), act16(rows, rows), act16(rows, rows)]
                + [act16(rows, far_rows), act16(far_rows, rows)],
                [features, pick_self, block_index, block_values, *weights],
                rows * ffn + 2 * rows * rows * BLOCK,
                scratch=[pltpu.VMEM((rows, rows + BLOCK + far_rows), F32)],
                name="first",
            )
        else:
            (msg,) = call(
                functools.partial(local_kernel, layer),
                [act16(rows)],
                [inputs[layer], *weights],
                rows * ffn,
                name=f"local{layer}",
            )
        mine[layer], msg = lax.optimization_barrier((mine[layer], msg))
        others.append(other_core(mine[layer]))
        (mixed,) = call(
            functools.partial(part_kernel, layer, pairs),
            [((rows, latent), F32)],
            [local, msg, remote, *weights, *mine[layer]],
            2 * rows * rows * latent,
            name=f"part{layer}",
        )
        prev = totals[-1] if layer else features
        if layer < last:
            total, new, *sends = call(
                functools.partial(mix_kernel, layer, pairs),
                [((rows, latent), F32), act16(rows)] + [act16(BLOCK)] * pairs,
                [prev, mixed, remote, pick, *weights, *others[layer]],
                far_rows * ffn + 2 * rows * far_rows * latent,
                name=f"mix{layer}",
            )
            totals.append(total)
            inputs.append(new)
    near_rows = pairs * BLOCK
    bwd_outs = (
        [((rows, latent), F32), act16(rows), act16(near_rows)]
        + [act16(near_rows, half)] * 2
        + [act16(BLOCK)] * pairs
    )
    outs = call(
        functools.partial(turn_kernel, last, pairs),
        bwd_outs,
        [totals[-1], mixed, remote, remote_t, cotangent, *weights, *mine[last], *others[last]],
        2 * far_rows * ffn,
        name="turn",
    )
    grad_rows = 2 * latent * half // LANES

    def pair_stages(axis):
        return [(axis, 1 << i) for i in range(lax.axis_size(axis).bit_length() - 1)]

    pieces = [[(0, grad_rows, pair_stages("basin") + pair_stages("chain"))]] * layers
    returned = {}
    sums = {}

    def back(layer, outs, after):
        near = routed(outs[5:], -1)
        grad, dmsg, act, dpre = call(
            functools.partial(back_kernel, layer),
            [((rows, latent), F32), act16(rows), act16(rows, half), act16(rows, half)],
            [outs[1], inputs[layer], local_t, *weights],
            2 * rows * ffn + 2 * rows * rows * latent,
            name=f"back{layer}",
            after=after,
        )
        if layer:
            near, grad = lax.optimization_barrier((near, grad))
            returned[layer] = near + other_core(near)
        else:
            returned[layer] = near
        shapes = []
        for lo, hi, stages in pieces[layer]:
            m = (hi - lo) // 2 if stages else hi - lo
            shapes += [((m, LANES), F32)] * bool(stages) + [((m, LANES), BF16)]
        parts = call(
            functools.partial(weights_kernel, layer, grad_scale, pairs, pieces[layer]),
            shapes,
            [outs[1], remote_t, w_in, w_out, inputs[layer], dmsg, act, dpre]
            + [*outs[2:5], *mine[layer], *others[layer]],
            rows * ffn,
            scratch=[pltpu.VMEM((grad_rows, LANES), F32)],
            name=f"weights{layer}",
        )
        parts_made = parts[:1]
        sums[layer] = []
        for i, (_, _, stages) in enumerate(pieces[layer]):
            n = 2 if stages else 1
            sums[layer].append(Sum(parts[:n], stages, f"{layer}_{i}"))
            parts = parts[n:]
        return [outs[0], grad], parts_made

    def join(layer, state, after):
        if layer:
            return call(
                functools.partial(join_kernel, layer - 1, pairs),
                bwd_outs,
                [*state, spread, remote_t, totals[layer - 1]]
                + [*weights, *returned[layer], *mine[layer - 1]],
                2 * far_rows * ffn,
                name=f"join{layer}",
                after=after,
            )
        return call(
            last_kernel,
            [((rows, latent), F32), ((8, LANES), F32)],
            [*state, spread, *returned[layer]],
            2 * rows * far_rows * latent,
            name="join0",
            after=after,
        )

    def write(layer, written, after):
        ready = [x for piece in sums.pop(layer) for x in piece.parts]
        kept = [*written, *after]
        return pl.pallas_call(
            functools.partial(write_kernel, layer, pieces[layer], len(kept)),
            out_shape=[
                jax.ShapeDtypeStruct((layers, latent, half), F32),
                jax.ShapeDtypeStruct((layers, half, latent), F32),
                jax.ShapeDtypeStruct((8, LANES), F32),
            ],
            in_specs=[ANY] * len(kept) + [VMEM] * len(ready),
            out_specs=[ANY] * 2 + [VMEM],
            scratch_shapes=[
                pltpu.VMEM((grad_rows, LANES), F32),
                pltpu.VMEM((latent, half), F32),
                pltpu.VMEM((half, latent), F32),
                pltpu.SemaphoreType.DMA((2,)),
            ],
            input_output_aliases={i: i for i in range(len(written))},
            compiler_params=pltpu.CompilerParams(vmem_limit_bytes=LIMIT),
            cost_estimate=pl.CostEstimate(flops=0, bytes_accessed=4_000_000, transcendentals=0),
            name=f"write{layer}",
        )(*written, *after, *ready)

    def step(layer, after):
        for piece in sums[layer]:
            after = piece.step(after)
        return after

    count = 2 * max(len(stages) for _, _, stages in pieces[0]) - 1
    at = []
    for layer in reversed(range(layers)):
        state, at = back(layer, outs, at)
        for above in reversed(range(layer + 1, layers)):
            at = step(above, at)
            if layer == 0 and above == last:
                near, at = lax.optimization_barrier((returned[0], at))
                returned[0] = near + other_core(near)
        if layer:
            outs = join(layer, state, at)
            at = outs[1:2]
    grad, token = join(0, state, at)
    at = [token]
    written = []
    for turn in range(layers - 1, layers - 1 + count):
        for layer in reversed(range(layers)):
            if layer in sums and sums[layer][0].done <= turn - (last - layer) < count:
                at = step(layer, at)
            elif layer and turn - (last - layer) == count:
                *written, token = write(layer, written, at)
                at = [token]
    for layer in reversed(range(layers)):
        if layer in sums:
            *written, _ = write(layer, written, [])
    return (grad, *written)


def solution(mesh):
    placed = (
        P(("runs", "chain", "basin"), None),
        P(("runs", "chain", "basin"), None),
        P(None, None, "feat"),
        P(None, "feat", None),
        P(("chain", "basin"), None),
        P(("chain", "basin"), None, None, None),
        P(("chain", "basin"), None, None),
        P(("chain", "basin"), None),
    )
    return jax.shard_map(
        shards,
        mesh=mesh,
        in_specs=placed,
        out_specs=(
            P(("runs", "chain", "basin"), None),
            P("runs", None, "feat"),
            P("runs", "feat", None),
        ),
        check_vma=False,
    )
```

time: 171 us -> 125 us (0.73)
  waiting for transfers between devices: 92.3 us -> 38.3 us
  starting transfers between devices: 23 us -> 45.3 us
  between operations: 14.2 us -> 1.19 us
  other arithmetic: 3.71 us -> 0.75 us
  Pallas kernels: 29.9 us -> 32.6 us
    psum x1 -> x0, waiting for transfers between devices: 84.2 us -> none  [shards(): summed.append(lax.psum((g_in, g_out), ('chain', 'basin')))]
    ppermute x6 -> x24, waiting for transfers between devices: 4.73 us -> 37.6 us  [the longest x18 26.9 us: swapped(): lax.ppermute(x, axis, [(i, i ^ d) for i in range(lax.axis_size(axis))])]
    ppermute x6 -> x24, starting transfers between devices: 16.1 us -> 43.5 us  [the longest x18 26.8 us: swapped(): lax.ppermute(x, axis, [(i, i ^ d) for i in range(lax.axis_size(axis))])]
    ppermute x8, starting transfers between devices: 6.9 us -> 1.79 us  [around(): return lax.ppermute(x, axis, [(i, (i + distance) % n) for i in range(n)])]
    convert_element_type x2 -> x0, other arithmetic: 3.71 us -> none  [the longest x1 2.45 us: shards(): summed_in = jnp.stack([x for x, _ in summed[::-1]]).astype(F32)]
    pallas_call x14 -> x37, Pallas kernels: 29.9 us -> 32.6 us  [the longest x34 28.6 us: call(): pl.pallas_call(lambda *refs: body(*refs[skipped:]), out_shape=[jax.ShapeD...]
    ppermute x8, waiting for transfers between devices: 3.33 us -> 0.78 us  [around(): return lax.ppermute(x, axis, [(i, (i + distance) % n) for i in range(n)])]
    unnamed x33 -> x19, local copies, waits for them, and re-layouts: 7.14 us -> 6.18 us
  transfers between devices with their start and end apart: 15 -> 32, of which waited for: 5 -> 16; matrix products, arithmetic and copies ran while one was open for 0% -> 1% of each run, Pallas kernels for 11% -> 22%
where the time goes in v4:
time: 125 us; the launch traced here: 124 us
  starting transfers between devices  45.3 us (36%)
  waiting for transfers between devices  38.3 us (31%)
  Pallas kernels  32.6 us (26%)
  local copies, waits for them, and re-layouts  6.18 us (5%)
    pallas_call x34, Pallas kernels, call(): pl.pallas_call(lambda *refs: body(*refs[skipped:]), out_shape=[jax.ShapeD...  28.6 us
    ppermute x18, waiting for transfers between devices, swapped(): lax.ppermute(x, axis, [(i, i ^ d) for i in range(lax.axis_size(axis))])  26.9 us
    ppermute x18, starting transfers between devices, swapped(): lax.ppermute(x, axis, [(i, i ^ d) for i in range(lax.axis_size(axis))])  26.8 us
    ppermute x6, starting transfers between devices, routed(): got.append(lax.ppermute(x, ('chain', 'basin', 'feat'), perm))  16.7 us
    ppermute x6, waiting for transfers between devices, routed(): got.append(lax.ppermute(x, ('chain', 'basin', 'feat'), perm))  10.6 us
    unnamed x19, local copies, waits for them, and re-layouts  6.18 us
    pallas_call x3, Pallas kernels, write(): pl.pallas_call(functools.partial(write_kernel, layer, pieces[layer], len(...  3.99 us
  transfers between devices with their start and end apart: 32, of which 16 were waited for; matrix products, arithmetic and copies ran while one was open for 1% of the time, Pallas kernels for 22%

profile of v4, /device:TPU:0, one launch (start us, length us, event | category | flops | bytes accessed | tf_op | source)
XLA Modules:
  0.0 124.3 jit_solution(3684995240557300247)
XLA Ops:
  3.6 4.9 %collective-permute-start.2 = (bf16[128,256]{1,0:T(8,128)(2,1)S(1)}, bf16[128,256]{1,0:T(8,128)(2,1)S(1)}, u32[]{:S(2)}, u32[]{:S(2)}) collective-permute-start(bf16[128,256]{1,0:T(8,128)(2,1)S(1)} %get-tuple-element.90), channel_id=1, source_target_pairs={{0,4},{1,3},{2,6},{3,1},{4,8},{5,7},{6,10},{7,5},{8,12},{9,11},{10... | collective-permute-start | bytes 196616 | tf_op jit(solution)/shard_map/ppermute | solution.py:411
  13.7 2.8 %first.1 = (bf16[768,256]{1,0:T(8,128)(2,1)S(1)}, bf16[768,768]{1,0:T(8,128)(2,1)S(1)}, bf16[768,768]{1,0:T(8,128)(2,1)S(1)}, bf16[768,256]{1,0:T(8,128)(2,1)S(1)}, bf16[256,768]{1,0:T(8,128)(2,1)S(1)}) custom-call(bf16[768,256]{1,0:T(8,128)(2,1)S(1)} %copy-done.5, bf16[128,768]{1,0:T(8,128)(2,1)S(1)} %get-tuple-element.88.refs_1_, ...), custom_call_target="tpu_custom_call" | custom-call | flops 956301312 | bytes 4000000 | tf_op jit(solution)/shard_map/first/pallas_call | solution.py:32
  18.8 3.5 %collective-permute-start.4 = (bf16[128,256]{1,0:T(8,128)(2,1)S(1)}, bf16[128,256]{1,0:T(8,128)(2,1)S(1)}, u32[]{:S(2)}, u32[]{:S(2)}) collective-permute-start(bf16[128,256]{1,0:T(8,128)(2,1)S(1)} %get-tuple-element.97), channel_id=1, source_target_pairs={{0,4},{1,3},{2,6},{3,1},{4,8},{5,7},{6,10},{7,5},{8,12},{9,11},{10... | collective-permute-start | bytes 196616 | tf_op jit(solution)/shard_map/ppermute | solution.py:411
  26.5 4.3 %collective-permute-start.6 = (bf16[128,256]{1,0:T(8,128)(2,1)S(1)}, bf16[128,256]{1,0:T(8,128)(2,1)S(1)}, u32[]{:S(2)}, u32[]{:S(2)}) collective-permute-start(bf16[128,256]{1,0:T(8,128)(2,1)S(1)} %get-tuple-element.102), channel_id=1, source_target_pairs={{0,4},{1,3},{2,6},{3,1},{4,8},{5,7},{6,10},{7,5},{8,12},{9,11},{10... | collective-permute-start | bytes 196616 | tf_op jit(solution)/shard_map/ppermute | solution.py:411
  34.0 1.8 %turn.1 = (f32[768,256]{1,0:T(8,128)S(1)}, bf16[768,256]{1,0:T(8,128)(2,1)S(1)}, bf16[128,256]{1,0:T(8,128)(2,1)S(1)}, bf16[128,512]{1,0:T(8,128)(2,1)S(1)}, bf1...) custom-call(f32[768,256]{1,0:T(8,128)S(1)} %get-tuple-element.101.refs_0_.refs_5_, f32[768,256]{1,0:T(8,128)S(1)} %part2.1.refs_1_, ...), custom_call_target="tpu_custom_call" | custom-call | flops 536870912 | bytes 4000000 | tf_op jit(solution)/shard_map/turn/pallas_call | solution.py:32
  35.8 1.5 %collective-permute-start.8 = (bf16[128,256]{1,0:T(8,128)(2,1)S(1)}, bf16[128,256]{1,0:T(8,128)(2,1)S(1)}, u32[]{:S(2)}, u32[]{:S(2)}) collective-permute-start(bf16[128,256]{1,0:T(8,128)(2,1)S(1)} %get-tuple-element.117), channel_id=1, source_target_pairs={{1,3},{3,1},{4,0},{5,7},{6,2},{7,5},{8,4},{9,11},{10,6},{11,9},{12... | collective-permute-start | bytes 196616 | tf_op jit(solution)/shard_map/ppermute | solution.py:411
  37.2 2.6 %back2.1 = (f32[768,256]{1,0:T(8,128)S(1)}, bf16[768,256]{1,0:T(8,128)(2,1)S(1)}, bf16[768,512]{1,0:T(8,128)(2,1)S(1)}, bf16[768,512]{1,0:T(8,128)(2,1)S(1)}) custom-call(bf16[768,256]{1,0:T(8,128)(2,1)S(1)} %get-tuple-element.107.refs_0_, bf16[768,256]{1,0:T(8,128)(2,1)S(1)} %get-tuple-element.103.refs_0_.refs_1_.refs_4_, ...), custom_call_target="tpu_custom_call" | custom-call | flops 1912602624 | bytes 4000000 | tf_op jit(solution)/shard_map/back2/pallas_call | solution.py:32
  39.9 2.4 %collective-permute-done.8.refs_10_ = bf16[128,256]{1,0:T(8,128)(2,1)S(1)} collective-permute-done((bf16[128,256]{1,0:T(8,128)(2,1)S(1)}, bf16[128,256]{1,0:T(8,128)(2,1)S(1)}, u32[]{:S(2)}, u32[]{:S(2)}) %collective-permute-start.8) | collective-permute-done | bytes 65568 | tf_op jit(solution)/shard_map/ppermute | solution.py:411
  43.5 1.6 %collective-permute-start.10 = (bf16[1024,128]{1,0:T(8,128)(2,1)S(1)}, bf16[1024,128]{1,0:T(8,128)(2,1)S(1)}, u32[]{:S(2)}, u32[]{:S(2)}) collective-permute-start(bf16[1024,128]{1,0:T(8,128)(2,1)S(1)} %get-tuple-element.130), channel_id=1, source_target_pairs={{0,2},{2,0},{1,3},{3,1},{4,6},{6,4},{5,7},{7,5},{8,10},{10,8},{9,1... | collective-permute-start | bytes 786440 | tf_op jit(solution)/shard_map/ppermute | solution.py:394
  47.6 2.6 %back1.1 = (f32[768,256]{1,0:T(8,128)S(1)}, bf16[768,256]{1,0:T(8,128)(2,1)S(1)}, bf16[768,512]{1,0:T(8,128)(2,1)S(1)}, bf16[768,512]{1,0:T(8,128)(2,1)S(1)}) custom-call(bf16[768,256]{1,0:T(8,128)(2,1)S(1)} %get-tuple-element.122.refs_0_.refs_1_, bf16[768,256]{1,0:T(8,128)(2,1)S(1)} %get-tuple-element.122.refs_0_.refs_1_, ...), custom_call_target="tpu_custom_call" | custom-call | flops 1912602624 | bytes 4000000 | tf_op jit(solution)/shard_map/back1/pallas_call | solution.py:32
  50.3 2.2 %collective-permute-done.11.refs_10_ = bf16[128,256]{1,0:T(8,128)(2,1)S(1)} collective-permute-done((bf16[128,256]{1,0:T(8,128)(2,1)S(1)}, bf16[128,256]{1,0:T(8,128)(2,1)S(1)}, u32[]{:S(2)}, u32[]{:S(2)}) %collective-permute-start.11) | collective-permute-done | bytes 65568 | tf_op jit(solution)/shard_map/ppermute | solution.py:411
  54.1 1.6 %collective-permute-start.15 = (bf16[1024,128]{1,0:T(8,128)(2,1)S(1)}, bf16[1024,128]{1,0:T(8,128)(2,1)S(1)}, u32[]{:S(2)}, u32[]{:S(2)}) collective-permute-start(bf16[1024,128]{1,0:T(8,128)(2,1)S(1)} %get-tuple-element.149), channel_id=1, source_target_pairs={{0,2},{2,0},{1,3},{3,1},{4,6},{6,4},{5,7},{7,5},{8,10},{10,8},{9,1... | collective-permute-start | bytes 786440 | tf_op jit(solution)/shard_map/ppermute | solution.py:394
  55.8 2.1 %collective-permute-start.14 = (bf16[512,128]{1,0:T(8,128)(2,1)S(1)}, bf16[512,128]{1,0:T(8,128)(2,1)S(1)}, u32[]{:S(2)}, u32[]{:S(2)}) collective-permute-start(bf16[512,128]{1,0:T(8,128)(2,1)S(1)} %get-tuple-element.146), channel_id=1, source_target_pairs={{0,4},{4,0},{8,12},{12,8},{1,5},{5,1},{9,13},{13,9},{2,6},{6,2},{1... | collective-permute-start | bytes 393224 | tf_op jit(solution)/shard_map/ppermute | solution.py:394
  59.1 2.6 %back0.1 = (f32[768,256]{1,0:T(8,128)S(1)}, bf16[768,256]{1,0:T(8,128)(2,1)S(1)}, bf16[768,512]{1,0:T(8,128)(2,1)S(1)}, bf16[768,512]{1,0:T(8,128)(2,1)S(1)}) custom-call(bf16[768,256]{1,0:T(8,128)(2,1)S(1)} %get-tuple-element.138.refs_0_.refs_1_, bf16[768,256]{1,0:T(8,128)(2,1)S(1)} %get-tuple-element.138.refs_0_.refs_1_, bf16[768,256]{1,0:T(8,128)(2,1)S(1)} %copy-done.6, ...), custom_call_target="tpu_custom_call" | custom-call | flops 1912602624 | bytes 4000000 | tf_op jit(solution)/shard_map/back0/pallas_call | solution.py:32
  65.1 4.8 %collective-permute-done.13.refs_4_ = bf16[128,256]{1,0:T(8,128)(2,1)S(1)} collective-permute-done((bf16[128,256]{1,0:T(8,128)(2,1)S(1)}, bf16[128,256]{1,0:T(8,128)(2,1)S(1)}, u32[]{:S(2)}, u32[]{:S(2)}) %collective-permute-start.13) | collective-permute-done | bytes 65568 | tf_op jit(solution)/shard_map/ppermute | solution.py:411
  71.5 2.4 %collective-permute-start.17 = (bf16[256,128]{1,0:T(8,128)(2,1)S(1)}, bf16[256,128]{1,0:T(8,128)(2,1)S(1)}, u32[]{:S(2)}, u32[]{:S(2)}) collective-permute-start(bf16[256,128]{1,0:T(8,128)(2,1)S(1)} %get-tuple-element.156), channel_id=1, source_target_pairs={{0,8},{4,12},{8,0},{12,4},{1,9},{5,13},{9,1},{13,5},{2,10},{6,14},... | collective-permute-start | bytes 196616 | tf_op jit(solution)/shard_map/ppermute | solution.py:394
  75.0 1.8 %collective-permute-done.17.refs_2_ = bf16[256,128]{1,0:T(8,128)(2,1)S(1)} collective-permute-done((bf16[256,128]{1,0:T(8,128)(2,1)S(1)}, bf16[256,128]{1,0:T(8,128)(2,1)S(1)}, u32[]{:S(2)}, u32[]{:S(2)}) %collective-permute-start.17) | collective-permute-done | bytes 65568 | tf_op jit(solution)/shard_map/ppermute | solution.py:394
  76.9 2.5 %collective-permute-start.20 = (bf16[256,128]{1,0:T(8,128)(2,1)S(1)}, bf16[256,128]{1,0:T(8,128)(2,1)S(1)}, u32[]{:S(2)}, u32[]{:S(2)}) collective-permute-start(bf16[256,128]{1,0:T(8,128)(2,1)S(1)} %sum_2_0_2.1.refs_0_.refs_1_), channel_id=1, source_target_pairs={{0,8},{4,12},{8,0},{12,4},{1,9},{5,13},{9,1},{13,5},{2,10},{6,14},... | collective-permute-start | bytes 196616 | tf_op jit(solution)/shard_map/ppermute | solution.py:394
  79.5 1.7 %collective-permute-start.22 = (bf16[512,128]{1,0:T(8,128)(2,1)S(1)}, bf16[512,128]{1,0:T(8,128)(2,1)S(1)}, u32[]{:S(2)}, u32[]{:S(2)}) collective-permute-start(bf16[512,128]{1,0:T(8,128)(2,1)S(1)} %get-tuple-element.162), channel_id=1, source_target_pairs={{0,4},{4,0},{8,12},{12,8},{1,5},{5,1},{9,13},{13,9},{2,6},{6,2},{1... | collective-permute-start | bytes 393224 | tf_op jit(solution)/shard_map/ppermute | solution.py:394
  81.2 1.5 %collective-permute-done.20.refs_2_ = bf16[256,128]{1,0:T(8,128)(2,1)S(1)} collective-permute-done((bf16[256,128]{1,0:T(8,128)(2,1)S(1)}, bf16[256,128]{1,0:T(8,128)(2,1)S(1)}, u32[]{:S(2)}, u32[]{:S(2)}) %collective-permute-start.20) | collective-permute-done | bytes 65568 | tf_op jit(solution)/shard_map/ppermute | solution.py:394
  82.8 1.9 %collective-permute-start.23 = (bf16[512,128]{1,0:T(8,128)(2,1)S(1)}, bf16[512,128]{1,0:T(8,128)(2,1)S(1)}, u32[]{:S(2)}, u32[]{:S(2)}) collective-permute-start(bf16[512,128]{1,0:T(8,128)(2,1)S(1)} %sum_2_0_3.1.refs_0_.refs_1_), channel_id=1, source_target_pairs={{0,4},{4,0},{8,12},{12,8},{1,5},{5,1},{9,13},{13,9},{2,6},{6,2},{1... | collective-permute-start | bytes 393224 | tf_op jit(solution)/shard_map/ppermute | solution.py:394
  84.7 2.2 %collective-permute-start.21 = (bf16[256,128]{1,0:T(8,128)(2,1)S(1)}, bf16[256,128]{1,0:T(8,128)(2,1)S(1)}, u32[]{:S(2)}, u32[]{:S(2)}) collective-permute-start(bf16[256,128]{1,0:T(8,128)(2,1)S(1)} %get-tuple-element.161), channel_id=1, source_target_pairs={{0,8},{4,12},{8,0},{12,4},{1,9},{5,13},{9,1},{13,5},{2,10},{6,14},... | collective-permute-start | bytes 196616 | tf_op jit(solution)/shard_map/ppermute | solution.py:394
  86.9 3.6 %collective-permute-done.21.refs_2_ = bf16[256,128]{1,0:T(8,128)(2,1)S(1)} collective-permute-done((bf16[256,128]{1,0:T(8,128)(2,1)S(1)}, bf16[256,128]{1,0:T(8,128)(2,1)S(1)}, u32[]{:S(2)}, u32[]{:S(2)}) %collective-permute-start.21) | collective-permute-done | bytes 65568 | tf_op jit(solution)/shard_map/ppermute | solution.py:394
  90.7 1.8 %collective-permute-start.26 = (bf16[1024,128]{1,0:T(8,128)(2,1)S(1)}, bf16[1024,128]{1,0:T(8,128)(2,1)S(1)}, u32[]{:S(2)}, u32[]{:S(2)}) collective-permute-start(bf16[1024,128]{1,0:T(8,128)(2,1)S(1)} %sum_2_0_4.1.refs_0_.refs_1_), channel_id=1, source_target_pairs={{0,2},{2,0},{1,3},{3,1},{4,6},{6,4},{5,7},{7,5},{8,10},{10,8},{9,1... | collective-permute-start | bytes 786440 | tf_op jit(solution)/shard_map/ppermute | solution.py:394
  93.3 5.2 %collective-permute-done.24.refs_2_ = bf16[256,128]{1,0:T(8,128)(2,1)S(1)} collective-permute-done((bf16[256,128]{1,0:T(8,128)(2,1)S(1)}, bf16[256,128]{1,0:T(8,128)(2,1)S(1)}, u32[]{:S(2)}, u32[]{:S(2)}) %collective-permute-start.24) | collective-permute-done | bytes 65568 | tf_op jit(solution)/shard_map/ppermute | solution.py:394
  99.2 4.7 %collective-permute-done.25.refs_2_ = bf16[256,128]{1,0:T(8,128)(2,1)S(1)} collective-permute-done((bf16[256,128]{1,0:T(8,128)(2,1)S(1)}, bf16[256,128]{1,0:T(8,128)(2,1)S(1)}, u32[]{:S(2)}, u32[]{:S(2)}) %collective-permute-start.25) | collective-permute-done | bytes 65568 | tf_op jit(solution)/shard_map/ppermute | solution.py:394
  107.1 3.8 %collective-permute-done.28.refs_2_ = bf16[256,128]{1,0:T(8,128)(2,1)S(1)} collective-permute-done((bf16[256,128]{1,0:T(8,128)(2,1)S(1)}, bf16[256,128]{1,0:T(8,128)(2,1)S(1)}, u32[]{:S(2)}, u32[]{:S(2)}) %collective-permute-start.28) | collective-permute-done | bytes 65568 | tf_op jit(solution)/shard_map/ppermute | solution.py:394
  110.9 2.1 %collective-permute-start.30 = (bf16[512,128]{1,0:T(8,128)(2,1)S(1)}, bf16[512,128]{1,0:T(8,128)(2,1)S(1)}, u32[]{:S(2)}, u32[]{:S(2)}) collective-permute-start(bf16[512,128]{1,0:T(8,128)(2,1)S(1)} %sum_0_0_3.1.refs_2_.refs_1_), channel_id=1, source_target_pairs={{0,4},{4,0},{8,12},{12,8},{1,5},{5,1},{9,13},{13,9},{2,6},{6,2},{1... | collective-permute-start | bytes 393224 | tf_op jit(solution)/shard_map/ppermute | solution.py:394
  114.1 1.8 %collective-permute-done.30.refs_2_ = bf16[512,128]{1,0:T(8,128)(2,1)S(1)} collective-permute-done((bf16[512,128]{1,0:T(8,128)(2,1)S(1)}, bf16[512,128]{1,0:T(8,128)(2,1)S(1)}, u32[]{:S(2)}, u32[]{:S(2)}) %collective-permute-start.30) | collective-permute-done | bytes 131104 | tf_op jit(solution)/shard_map/ppermute | solution.py:394
  116.0 2.0 %collective-permute-start.31 = (bf16[1024,128]{1,0:T(8,128)(2,1)S(1)}, bf16[1024,128]{1,0:T(8,128)(2,1)S(1)}, u32[]{:S(2)}, u32[]{:S(2)}) collective-permute-start(bf16[1024,128]{1,0:T(8,128)(2,1)S(1)} %sum_0_0_4.1.refs_2_), channel_id=1, source_target_pairs={{0,2},{2,0},{1,3},{3,1},{4,6},{6,4},{5,7},{7,5},{8,10},{10,8},{9,1... | collective-permute-start | bytes 786440 | tf_op jit(solution)/shard_map/ppermute | solution.py:394
  118.0 4.4 %collective-permute-done.31.refs_3_ = bf16[1024,128]{1,0:T(8,128)(2,1)S(1)} collective-permute-done((bf16[1024,128]{1,0:T(8,128)(2,1)S(1)}, bf16[1024,128]{1,0:T(8,128)(2,1)S(1)}, u32[]{:S(2)}, u32[]{:S(2)}) %collective-permute-start.31) | collective-permute-done | bytes 262176 | tf_op jit(solution)/shard_map/ppermute | solution.py:394
  122.4 1.7 %write0.1 = (f32[3,256,512]{2,1,0:T(8,128)}, f32[3,512,256]{2,1,0:T(8,128)}, f32[8,128]{1,0:T(8,128)}) custom-call(f32[3,256,512]{2,1,0:T(8,128)} %get-tuple-element.168.refs_0_, f32[3,512,256]{2,1,0:T(8,128)} %get-tuple-element.169.refs_1_, bf16[1024,128]{1,0:T(8,128)(2,1)S(1)} %sum_0_0_4.1.refs_2_, ...), custom_call_target="tpu_custom_call", output_to_operand_aliasing={{0}: (0, {}), {1}: (1, {})} | custom-call | bytes 4000000 | tf_op jit(solution)/shard_map/write0/pallas_call | solution.py:572
  (89 shorter events, 36.6 us)
Async XLA Ops:
  0.6 8.6 %collective-permute-start = (bf16[3,256,512]{2,1,0:T(8,128)(2,1)}, bf16[3,256,512]{2,1,0:T(8,128)(2,1)S(1)}, u32[]{:S(2)}, u32[]{:S(2)}) collective-permute-start(bf16[3,256,512]{2,1,0:T(8,128)(2,1)} %refs_2_.8), channel_id=1, source_target_pairs={{0,1},{1,0},{2,3},{3,2},{4,5},{5,4},{6,7},{7,6},{8,9},{9,8},{10,11... | collective-permute-start | bytes 2359304 | tf_op jit(solution)/shard_map/ppermute | solution.py:389
  1.1 8.1 %collective-permute-start.1 = (bf16[3,512,256]{2,1,0:T(8,128)(2,1)}, bf16[3,512,256]{2,1,0:T(8,128)(2,1)S(1)}, u32[]{:S(2)}, u32[]{:S(2)}) collective-permute-start(bf16[3,512,256]{2,1,0:T(8,128)(2,1)} %refs_3_.19), channel_id=1, source_target_pairs={{0,1},{1,0},{2,3},{3,2},{4,5},{5,4},{6,7},{7,6},{8,9},{9,8},{10,11... | collective-permute-start | bytes 2359304 | tf_op jit(solution)/shard_map/ppermute | solution.py:389
  3.6 12.9 %collective-permute-start.2 = (bf16[128,256]{1,0:T(8,128)(2,1)S(1)}, bf16[128,256]{1,0:T(8,128)(2,1)S(1)}, u32[]{:S(2)}, u32[]{:S(2)}) collective-permute-start(bf16[128,256]{1,0:T(8,128)(2,1)S(1)} %get-tuple-element.90), channel_id=1, source_target_pairs={{0,4},{1,3},{2,6},{3,1},{4,8},{5,7},{6,10},{7,5},{8,12},{9,11},{10... | collective-permute-start | bytes 196616 | tf_op jit(solution)/shard_map/ppermute | solution.py:411
  16.4 1.3 %collective-permute-start.3 = (bf16[128,256]{1,0:T(8,128)(2,1)S(1)}, bf16[128,256]{1,0:T(8,128)(2,1)S(1)}, u32[]{:S(2)}, u32[]{:S(2)}) collective-permute-start(bf16[128,256]{1,0:T(8,128)(2,1)S(1)} %collective-permute-done.2.refs_7_.refs_12_.refs_11_), channel_id=1, source_target_pairs={{0,1},{1,0},{2,3},{3,2},{4,5},{5,4},{6,7},{7,6},{8,9},{9,8},{10,11... | collective-permute-start | bytes 196616 | tf_op jit(solution)/shard_map/ppermute | solution.py:389
  18.8 5.4 %collective-permute-start.4 = (bf16[128,256]{1,0:T(8,128)(2,1)S(1)}, bf16[128,256]{1,0:T(8,128)(2,1)S(1)}, u32[]{:S(2)}, u32[]{:S(2)}) collective-permute-start(bf16[128,256]{1,0:T(8,128)(2,1)S(1)} %get-tuple-element.97), channel_id=1, source_target_pairs={{0,4},{1,3},{2,6},{3,1},{4,8},{5,7},{6,10},{7,5},{8,12},{9,11},{10... | collective-permute-start | bytes 196616 | tf_op jit(solution)/shard_map/ppermute | solution.py:411
  24.2 1.3 %collective-permute-start.5 = (bf16[128,256]{1,0:T(8,128)(2,1)S(1)}, bf16[128,256]{1,0:T(8,128)(2,1)S(1)}, u32[]{:S(2)}, u32[]{:S(2)}) collective-permute-start(bf16[128,256]{1,0:T(8,128)(2,1)S(1)} %collective-permute-done.4.refs_7_.refs_12_.refs_11_), channel_id=1, source_target_pairs={{0,1},{1,0},{2,3},{3,2},{4,5},{5,4},{6,7},{7,6},{8,9},{9,8},{10,11... | collective-permute-start | bytes 196616 | tf_op jit(solution)/shard_map/ppermute | solution.py:389
  26.5 6.2 %collective-permute-start.6 = (bf16[128,256]{1,0:T(8,128)(2,1)S(1)}, bf16[128,256]{1,0:T(8,128)(2,1)S(1)}, u32[]{:S(2)}, u32[]{:S(2)}) collective-permute-start(bf16[128,256]{1,0:T(8,128)(2,1)S(1)} %get-tuple-element.102), channel_id=1, source_target_pairs={{0,4},{1,3},{2,6},{3,1},{4,8},{5,7},{6,10},{7,5},{8,12},{9,11},{10... | collective-permute-start | bytes 196616 | tf_op jit(solution)/shard_map/ppermute | solution.py:411
  32.7 1.3 %collective-permute-start.7 = (bf16[128,256]{1,0:T(8,128)(2,1)S(1)}, bf16[128,256]{1,0:T(8,128)(2,1)S(1)}, u32[]{:S(2)}, u32[]{:S(2)}) collective-permute-start(bf16[128,256]{1,0:T(8,128)(2,1)S(1)} %collective-permute-done.6.refs_7_.refs_9_.refs_11_), channel_id=1, source_target_pairs={{0,1},{1,0},{2,3},{3,2},{4,5},{5,4},{6,7},{7,6},{8,9},{9,8},{10,11... | collective-permute-start | bytes 196616 | tf_op jit(solution)/shard_map/ppermute | solution.py:389
  35.8 6.5 %collective-permute-start.8 = (bf16[128,256]{1,0:T(8,128)(2,1)S(1)}, bf16[128,256]{1,0:T(8,128)(2,1)S(1)}, u32[]{:S(2)}, u32[]{:S(2)}) collective-permute-start(bf16[128,256]{1,0:T(8,128)(2,1)S(1)} %get-tuple-element.117), channel_id=1, source_target_pairs={{1,3},{3,1},{4,0},{5,7},{6,2},{7,5},{8,4},{9,11},{10,6},{11,9},{12... | collective-permute-start | bytes 196616 | tf_op jit(solution)/shard_map/ppermute | solution.py:411
  42.3 2.8 %collective-permute-start.9 = (bf16[128,256]{1,0:T(8,128)(2,1)S(1)}, bf16[128,256]{1,0:T(8,128)(2,1)S(1)}, u32[]{:S(2)}, u32[]{:S(2)}) collective-permute-start(bf16[128,256]{1,0:T(8,128)(2,1)S(1)} %collective-permute-done.8.refs_10_), channel_id=1, source_target_pairs={{0,1},{1,0},{2,3},{3,2},{4,5},{5,4},{6,7},{7,6},{8,9},{9,8},{10,11... | collective-permute-start | bytes 196616 | tf_op jit(solution)/shard_map/ppermute | solution.py:389
  43.5 12.2 %collective-permute-start.10 = (bf16[1024,128]{1,0:T(8,128)(2,1)S(1)}, bf16[1024,128]{1,0:T(8,128)(2,1)S(1)}, u32[]{:S(2)}, u32[]{:S(2)}) collective-permute-start(bf16[1024,128]{1,0:T(8,128)(2,1)S(1)} %get-tuple-element.130), channel_id=1, source_target_pairs={{0,2},{2,0},{1,3},{3,1},{4,6},{6,4},{5,7},{7,5},{8,10},{10,8},{9,1... | collective-permute-start | bytes 786440 | tf_op jit(solution)/shard_map/ppermute | solution.py:394
  46.3 6.2 %collective-permute-start.11 = (bf16[128,256]{1,0:T(8,128)(2,1)S(1)}, bf16[128,256]{1,0:T(8,128)(2,1)S(1)}, u32[]{:S(2)}, u32[]{:S(2)}) collective-permute-start(bf16[128,256]{1,0:T(8,128)(2,1)S(1)} %get-tuple-element.133), channel_id=1, source_target_pairs={{1,3},{3,1},{4,0},{5,7},{6,2},{7,5},{8,4},{9,11},{10,6},{11,9},{12... | collective-permute-start | bytes 196616 | tf_op jit(solution)/shard_map/ppermute | solution.py:411
  52.5 5.4 %collective-permute-start.12 = (bf16[128,256]{1,0:T(8,128)(2,1)S(1)}, bf16[128,256]{1,0:T(8,128)(2,1)S(1)}, u32[]{:S(2)}, u32[]{:S(2)}) collective-permute-start(bf16[128,256]{1,0:T(8,128)(2,1)S(1)} %collective-permute-done.11.refs_10_), channel_id=1, source_target_pairs={{0,1},{1,0},{2,3},{3,2},{4,5},{5,4},{6,7},{7,6},{8,9},{9,8},{10,11... | collective-permute-start | bytes 196616 | tf_op jit(solution)/shard_map/ppermute | solution.py:389
  54.1 16.6 %collective-permute-start.15 = (bf16[1024,128]{1,0:T(8,128)(2,1)S(1)}, bf16[1024,128]{1,0:T(8,128)(2,1)S(1)}, u32[]{:S(2)}, u32[]{:S(2)}) collective-permute-start(bf16[1024,128]{1,0:T(8,128)(2,1)S(1)} %get-tuple-element.149), channel_id=1, source_target_pairs={{0,2},{2,0},{1,3},{3,1},{4,6},{6,4},{5,7},{7,5},{8,10},{10,8},{9,1... | collective-permute-start | bytes 786440 | tf_op jit(solution)/shard_map/ppermute | solution.py:394
  55.8 9.2 %collective-permute-start.14 = (bf16[512,128]{1,0:T(8,128)(2,1)S(1)}, bf16[512,128]{1,0:T(8,128)(2,1)S(1)}, u32[]{:S(2)}, u32[]{:S(2)}) collective-permute-start(bf16[512,128]{1,0:T(8,128)(2,1)S(1)} %get-tuple-element.146), channel_id=1, source_target_pairs={{0,4},{4,0},{8,12},{12,8},{1,5},{5,1},{9,13},{13,9},{2,6},{6,2},{1... | collective-permute-start | bytes 393224 | tf_op jit(solution)/shard_map/ppermute | solution.py:394
  63.0 16.4 %collective-permute-start.19 = (bf16[1024,128]{1,0:T(8,128)(2,1)S(1)}, bf16[1024,128]{1,0:T(8,128)(2,1)S(1)}, u32[]{:S(2)}, u32[]{:S(2)}) collective-permute-start(bf16[1024,128]{1,0:T(8,128)(2,1)S(1)} %get-tuple-element.159), channel_id=1, source_target_pairs={{0,2},{2,0},{1,3},{3,1},{4,6},{6,4},{5,7},{7,5},{8,10},{10,8},{9,1... | collective-permute-start | bytes 786440 | tf_op jit(solution)/shard_map/ppermute | solution.py:394
  63.8 6.1 %collective-permute-start.13 = (bf16[128,256]{1,0:T(8,128)(2,1)S(1)}, bf16[128,256]{1,0:T(8,128)(2,1)S(1)}, u32[]{:S(2)}, u32[]{:S(2)}) collective-permute-start(bf16[128,256]{1,0:T(8,128)(2,1)S(1)} %get-tuple-element.137), channel_id=1, source_target_pairs={{1,3},{3,1},{4,0},{5,7},{6,2},{7,5},{8,4},{9,11},{10,6},{11,9},{12... | collective-permute-start | bytes 196616 | tf_op jit(solution)/shard_map/ppermute | solution.py:411
  69.9 4.0 %collective-permute-start.16 = (bf16[128,256]{1,0:T(8,128)(2,1)S(1)}, bf16[128,256]{1,0:T(8,128)(2,1)S(1)}, u32[]{:S(2)}, u32[]{:S(2)}) collective-permute-start(bf16[128,256]{1,0:T(8,128)(2,1)S(1)} %collective-permute-done.13.refs_4_), channel_id=1, source_target_pairs={{0,1},{1,0},{2,3},{3,2},{4,5},{5,4},{6,7},{7,6},{8,9},{9,8},{10,11... | collective-permute-start | bytes 196616 | tf_op jit(solution)/shard_map/ppermute | solution.py:389
  70.8 8.6 %collective-permute-start.18 = (bf16[512,128]{1,0:T(8,128)(2,1)S(1)}, bf16[512,128]{1,0:T(8,128)(2,1)S(1)}, u32[]{:S(2)}, u32[]{:S(2)}) collective-permute-start(bf16[512,128]{1,0:T(8,128)(2,1)S(1)} %get-tuple-element.157), channel_id=1, source_target_pairs={{0,4},{4,0},{8,12},{12,8},{1,5},{5,1},{9,13},{13,9},{2,6},{6,2},{1... | collective-permute-start | bytes 393224 | tf_op jit(solution)/shard_map/ppermute | solution.py:394
  71.5 5.4 %collective-permute-start.17 = (bf16[256,128]{1,0:T(8,128)(2,1)S(1)}, bf16[256,128]{1,0:T(8,128)(2,1)S(1)}, u32[]{:S(2)}, u32[]{:S(2)}) collective-permute-start(bf16[256,128]{1,0:T(8,128)(2,1)S(1)} %get-tuple-element.156), channel_id=1, source_target_pairs={{0,8},{4,12},{8,0},{12,4},{1,9},{5,13},{9,1},{13,5},{2,10},{6,14},... | collective-permute-start | bytes 196616 | tf_op jit(solution)/shard_map/ppermute | solution.py:394
  76.9 5.9 %collective-permute-start.20 = (bf16[256,128]{1,0:T(8,128)(2,1)S(1)}, bf16[256,128]{1,0:T(8,128)(2,1)S(1)}, u32[]{:S(2)}, u32[]{:S(2)}) collective-permute-start(bf16[256,128]{1,0:T(8,128)(2,1)S(1)} %sum_2_0_2.1.refs_0_.refs_1_), channel_id=1, source_target_pairs={{0,8},{4,12},{8,0},{12,4},{1,9},{5,13},{9,1},{13,5},{2,10},{6,14},... | collective-permute-start | bytes 196616 | tf_op jit(solution)/shard_map/ppermute | solution.py:394
  79.5 11.0 %collective-permute-start.22 = (bf16[512,128]{1,0:T(8,128)(2,1)S(1)}, bf16[512,128]{1,0:T(8,128)(2,1)S(1)}, u32[]{:S(2)}, u32[]{:S(2)}) collective-permute-start(bf16[512,128]{1,0:T(8,128)(2,1)S(1)} %get-tuple-element.162), channel_id=1, source_target_pairs={{0,4},{4,0},{8,12},{12,8},{1,5},{5,1},{9,13},{13,9},{2,6},{6,2},{1... | collective-permute-start | bytes 393224 | tf_op jit(solution)/shard_map/ppermute | solution.py:394
  82.8 7.9 %collective-permute-start.23 = (bf16[512,128]{1,0:T(8,128)(2,1)S(1)}, bf16[512,128]{1,0:T(8,128)(2,1)S(1)}, u32[]{:S(2)}, u32[]{:S(2)}) collective-permute-start(bf16[512,128]{1,0:T(8,128)(2,1)S(1)} %sum_2_0_3.1.refs_0_.refs_1_), channel_id=1, source_target_pairs={{0,4},{4,0},{8,12},{12,8},{1,5},{5,1},{9,13},{13,9},{2,6},{6,2},{1... | collective-permute-start | bytes 393224 | tf_op jit(solution)/shard_map/ppermute | solution.py:394
  84.7 5.9 %collective-permute-start.21 = (bf16[256,128]{1,0:T(8,128)(2,1)S(1)}, bf16[256,128]{1,0:T(8,128)(2,1)S(1)}, u32[]{:S(2)}, u32[]{:S(2)}) collective-permute-start(bf16[256,128]{1,0:T(8,128)(2,1)S(1)} %get-tuple-element.161), channel_id=1, source_target_pairs={{0,8},{4,12},{8,0},{12,4},{1,9},{5,13},{9,1},{13,5},{2,10},{6,14},... | collective-permute-start | bytes 196616 | tf_op jit(solution)/shard_map/ppermute | solution.py:394
  90.7 13.3 %collective-permute-start.26 = (bf16[1024,128]{1,0:T(8,128)(2,1)S(1)}, bf16[1024,128]{1,0:T(8,128)(2,1)S(1)}, u32[]{:S(2)}, u32[]{:S(2)}) collective-permute-start(bf16[1024,128]{1,0:T(8,128)(2,1)S(1)} %sum_2_0_4.1.refs_0_.refs_1_), channel_id=1, source_target_pairs={{0,2},{2,0},{1,3},{3,1},{4,6},{6,4},{5,7},{7,5},{8,10},{10,8},{9,1... | collective-permute-start | bytes 786440 | tf_op jit(solution)/shard_map/ppermute | solution.py:394
  92.5 6.0 %collective-permute-start.24 = (bf16[256,128]{1,0:T(8,128)(2,1)S(1)}, bf16[256,128]{1,0:T(8,128)(2,1)S(1)}, u32[]{:S(2)}, u32[]{:S(2)}) collective-permute-start(bf16[256,128]{1,0:T(8,128)(2,1)S(1)} %sum_1_0_2.1.refs_0_.refs_1_), channel_id=1, source_target_pairs={{0,8},{4,12},{8,0},{12,4},{1,9},{5,13},{9,1},{13,5},{2,10},{6,14},... | collective-permute-start | bytes 196616 | tf_op jit(solution)/shard_map/ppermute | solution.py:394
  98.5 6.6 %collective-permute-start.27 = (bf16[512,128]{1,0:T(8,128)(2,1)S(1)}, bf16[512,128]{1,0:T(8,128)(2,1)S(1)}, u32[]{:S(2)}, u32[]{:S(2)}) collective-permute-start(bf16[512,128]{1,0:T(8,128)(2,1)S(1)} %sum_1_0_3.1.refs_0_.refs_1_), channel_id=1, source_target_pairs={{0,4},{4,0},{8,12},{12,8},{1,5},{5,1},{9,13},{13,9},{2,6},{6,2},{1... | collective-permute-start | bytes 393224 | tf_op jit(solution)/shard_map/ppermute | solution.py:394
  98.6 5.3 %collective-permute-start.25 = (bf16[256,128]{1,0:T(8,128)(2,1)S(1)}, bf16[256,128]{1,0:T(8,128)(2,1)S(1)}, u32[]{:S(2)}, u32[]{:S(2)}) collective-permute-start(bf16[256,128]{1,0:T(8,128)(2,1)S(1)} %get-tuple-element.164), channel_id=1, source_target_pairs={{0,8},{4,12},{8,0},{12,4},{1,9},{5,13},{9,1},{13,5},{2,10},{6,14},... | collective-permute-start | bytes 196616 | tf_op jit(solution)/shard_map/ppermute | solution.py:394
  105.2 7.8 %collective-permute-start.29 = (bf16[1024,128]{1,0:T(8,128)(2,1)S(1)}, bf16[1024,128]{1,0:T(8,128)(2,1)S(1)}, u32[]{:S(2)}, u32[]{:S(2)}) collective-permute-start(bf16[1024,128]{1,0:T(8,128)(2,1)S(1)} %sum_1_0_4.1.refs_0_.refs_3_), channel_id=1, source_target_pairs={{0,2},{2,0},{1,3},{3,1},{4,6},{6,4},{5,7},{7,5},{8,10},{10,8},{9,1... | collective-permute-start | bytes 786440 | tf_op jit(solution)/shard_map/ppermute | solution.py:394
  105.7 5.2 %collective-permute-start.28 = (bf16[256,128]{1,0:T(8,128)(2,1)S(1)}, bf16[256,128]{1,0:T(8,128)(2,1)S(1)}, u32[]{:S(2)}, u32[]{:S(2)}) collective-permute-start(bf16[256,128]{1,0:T(8,128)(2,1)S(1)} %sum_0_0_2.1.refs_0_.refs_1_), channel_id=1, source_target_pairs={{0,8},{4,12},{8,0},{12,4},{1,9},{5,13},{9,1},{13,5},{2,10},{6,14},... | collective-permute-start | bytes 196616 | tf_op jit(solution)/shard_map/ppermute | solution.py:394
  110.9 5.0 %collective-permute-start.30 = (bf16[512,128]{1,0:T(8,128)(2,1)S(1)}, bf16[512,128]{1,0:T(8,128)(2,1)S(1)}, u32[]{:S(2)}, u32[]{:S(2)}) collective-permute-start(bf16[512,128]{1,0:T(8,128)(2,1)S(1)} %sum_0_0_3.1.refs_2_.refs_1_), channel_id=1, source_target_pairs={{0,4},{4,0},{8,12},{12,8},{1,5},{5,1},{9,13},{13,9},{2,6},{6,2},{1... | collective-permute-start | bytes 393224 | tf_op jit(solution)/shard_map/ppermute | solution.py:394
  116.0 6.4 %collective-permute-start.31 = (bf16[1024,128]{1,0:T(8,128)(2,1)S(1)}, bf16[1024,128]{1,0:T(8,128)(2,1)S(1)}, u32[]{:S(2)}, u32[]{:S(2)}) collective-permute-start(bf16[1024,128]{1,0:T(8,128)(2,1)S(1)} %sum_0_0_4.1.refs_2_), channel_id=1, source_target_pairs={{0,2},{2,0},{1,3},{3,1},{4,6},{6,4},{5,7},{7,5},{8,10},{10,8},{9,1... | collective-permute-start | bytes 786440 | tf_op jit(solution)/shard_map/ppermute | solution.py:394
  (9 other events, 14.2 us)

commit v5 on v4

--- a/solution.py
+++ b/solution.py
@@ -77,10 +77,6 @@
 def norm_grad(grad, total):
     scale, normed = normed_of(total)
     return scale * (grad - normed * jnp.mean(grad * normed, axis=-1, keepdims=True))
-
-
-def route_place(route, feat, pairs):
-    return route // 2 + jnp.where(route % 2 == feat, 0, pairs)
 
 
 def setup_kernel(groups, pairs, features, sent, *refs):
@@ -109,23 +105,24 @@
                 pick[route // 2 * BLOCK : (route // 2 + 1) * BLOCK, r : r + BLOCK] = hot
 
             at = lax.broadcasted_iota(jnp.int32, (BLOCK, BLOCK), 0) + r
-            place = pl.multiple_of(route_place(route, feat, pairs) * BLOCK, BLOCK)
-            spread[r : r + BLOCK, pl.ds(place, BLOCK)] = (across == at).astype(F32).astype(BF16)
+            if route < groups:
+                spread[r : r + BLOCK, route * BLOCK : (route + 1) * BLOCK] = (
+                    (across == at).astype(F32).astype(BF16)
+                )
     for i, send in enumerate(sends):
         send[...] = mm(pick[i * BLOCK : (i + 1) * BLOCK, :], features[...]).astype(BF16)
 
 
-def build_adjacency(groups, pairs, rows, index, values, pick_self, outs, acc):
+def build_adjacency(groups, rows, index, values, pick_self, outs, acc):
     local, local_t, remote, remote_t = outs
     own = rows // BLOCK
-    b, feat = lax.axis_index("basin"), lax.axis_index("feat")
+    b = lax.axis_index("basin")
     acc[...] = jnp.zeros_like(acc)
     for k in range(own):
         for t in range(index.shape[1]):
             v = index[k, t]
             route = jnp.where(v == own, 0, lax.rem(b + groups - (v - own - 1), groups))
-            far = own + 1 + route_place(route, feat, pairs)
-            far = jnp.where((v > own) & (route == 0), own, far)
+            far = jnp.where((v > own) & (route == 0), own, own + 1 + route)
             at = jnp.where(v < own, v, far)
             here = (pl.ds(k * BLOCK, BLOCK), pl.ds(pl.multiple_of(at * BLOCK, BLOCK), BLOCK))
             acc[here] += values[k, t].astype(F32)
@@ -145,35 +142,40 @@
         msg[r : r + 256, :] = message_of(inputs[r : r + 256, :], halves)
 
 
-def first_kernel(groups, pairs, *refs):
+def first_kernel(groups, *refs):
     inputs, pick_self, index, values = refs[:4]
     weights, msg, outs = refs[4:8], refs[8], refs[9:13]
     own_messages(0, inputs, weights, msg)
-    build_adjacency(groups, pairs, inputs.shape[0], index, values, pick_self, outs, refs[13])
+    build_adjacency(groups, inputs.shape[0], index, values, pick_self, outs, refs[13])
 
 
 def local_kernel(layer, *refs):
     own_messages(layer, refs[0], refs[1:5], refs[5])
 
 
-def remote_mixed(layer, received, remote, weights):
+def remote_mixed(layer, received, remote, feat, weights):
     wi0, wi1, wo0, wo1 = weights
     halves = [(wi0[layer], wo0[layer]), (wi1[layer], wo1[layer])]
-    far = jnp.concatenate([x[...] for x in received], axis=0)
-    return mm(remote, message_of(far, halves))
+    total = None
+    for i, block in enumerate(received):
+        route = jnp.minimum(2 * i + feat, remote.shape[1] // BLOCK - 1)
+        columns = remote[:, pl.ds(pl.multiple_of(route * BLOCK, BLOCK), BLOCK)]
+        part = mm(columns, message_of(block[...], halves))
+        total = part if total is None else total + part
+    return total
 
 
 def part_kernel(layer, pairs, *refs):
     local, msg, remote = refs[:3]
     weights, received, mixed = refs[3:7], refs[7 : 7 + pairs], refs[-1]
     mixed[...] = mm(local[...], msg[...]) + remote_mixed(
-        layer, received, remote[:, : pairs * BLOCK], weights
+        layer, received, remote, lax.axis_index("feat"), weights
     )
 
 
 def mixed_total(layer, state, mixed, received, remote, weights):
     return state + mixed[...] + remote_mixed(
-        layer, received, remote[:, len(received) * BLOCK :], weights
+        layer, received, remote, 1 - lax.axis_index("feat"), weights
     )
 
 
@@ -191,16 +193,23 @@
         send[...] = mm(pick[i * BLOCK : (i + 1) * BLOCK, :], new).astype(BF16)
 
 
-def start_bwd(layer, dtotal_now, weights, received, remote_t, outs):
-    dtotal, dround, far_dmsg, far_act, far_dpre = outs[:5]
-    backs = outs[5:]
+def start_bwd(layer, groups, dtotal_now, weights, mine, others, remote_t, outs):
+    dtotal, dround, far_x, far_dmsg, far_act, far_dpre = outs[:6]
+    backs = outs[6:]
     wi0, wi1, wo0, wo1 = weights
     halves = [(wi0[layer], wo0[layer]), (wi1[layer], wo1[layer])]
     dtotal[...] = dtotal_now
     dround[...] = dtotal_now.astype(BF16)
-    far = jnp.concatenate([x[...] for x in received], axis=0)
-    dmsg = mm(remote_t[: far.shape[0], :], dround[...]).astype(BF16)
-    back, (act, dpre) = message_grad(far, dmsg, halves)
+    for first in range(2):
+
+        @pl.when(lax.axis_index("feat") == first)
+        def _():
+            for route in range(groups):
+                block = (mine, others)[(route + first) % 2][route // 2]
+                far_x[route * BLOCK : (route + 1) * BLOCK, :] = block[...]
+
+    dmsg = mm(remote_t[...], dround[...]).astype(BF16)
+    back, (act, dpre) = message_grad(far_x[...], dmsg, halves)
     far_dmsg[...] = dmsg
     far_act[...] = act
     far_dpre[...] = dpre
@@ -208,20 +217,23 @@
         out[...] = back[i * BLOCK : (i + 1) * BLOCK, :].astype(BF16)
 
 
-def turn_kernel(layer, pairs, *refs):
+def turn_kernel(layer, groups, pairs, *refs):
     prev, mixed, remote, remote_t, cot = refs[:5]
     weights = refs[5:9]
     mine, others = refs[9 : 9 + pairs], refs[9 + pairs : 9 + 2 * pairs]
     outs = refs[9 + 2 * pairs :]
     state = normed_of(prev[...])[1]
     total = mixed_total(layer, state, mixed, others, remote, weights)
-    start_bwd(layer, norm_grad(cot[...], total), weights, mine, remote_t, outs)
-
-
-def back_kernel(layer, *refs):
+    dtotal = norm_grad(cot[...], total)
+    start_bwd(layer, groups, dtotal, weights, mine, others, remote_t, outs)
+
+
+def back_kernel(layer, grad_scale, stage, *refs):
     dround, inputs, local_t = refs[:3]
     wi0, wi1, wo0, wo1 = refs[3:7]
-    back, dmsg, act, dpre = refs[7:]
+    far_x, far_dmsg, far_act, far_dpre = refs[7:11]
+    back, keep, send = refs[11:14]
+    grads, dmsg, act, dpre = refs[14:]
     halves = [(wi0[layer], wo0[layer]), (wi1[layer], wo1[layer])]
     dmsg[...] = mm(local_t[...], dround[...]).astype(BF16)
     for r in range(0, inputs.shape[0], 256):
@@ -229,43 +241,22 @@
         back[here, :], (act[here, :], dpre[here, :]) = message_grad(
             inputs[here, :], dmsg[here, :], halves
         )
-
-
-def weights_kernel(layer, grad_scale, pairs, pieces, *refs):
-    dround, remote_t, w_in, w_out, inputs, dmsg, act, dpre = refs[:8]
-    far_dmsg, far_act, far_dpre = refs[8:11]
-    mine, others = refs[11 : 11 + pairs], refs[11 + pairs : 11 + 2 * pairs]
-    outs = refs[11 + 2 * pairs : -1]
-    grads = refs[-1]
-    near = jnp.concatenate([x[...] for x in mine], axis=0)
-    far = jnp.concatenate([x[...] for x in others], axis=0)
-    dmsg2 = mm(remote_t[near.shape[0] :, :], dround[...]).astype(BF16)
-    pre = mm(far, w_in[layer])
-    sig = sigmoid(pre)
-    dpre2 = (mm(dmsg2, w_out[layer], NT) * (sig * (1.0 + pre * (1.0 - sig)))).astype(BF16)
-    act2 = (pre * sig).astype(BF16)
     latent, hidden = inputs.shape[1], act.shape[1]
-    g_in = mm(inputs[...], dpre[...], TN) + mm(near, far_dpre[...], TN) + mm(far, dpre2, TN)
-    g_in = g_in * grad_scale
+    g_in = (mm(inputs[...], dpre[...], TN) + mm(far_x[...], far_dpre[...], TN)) * grad_scale
     for j in range(hidden // LANES):
         grads[j * latent : (j + 1) * latent, :] = g_in[:, j * LANES : (j + 1) * LANES]
-    g_out = mm(act[...], dmsg[...], TN) + mm(far_act[...], far_dmsg[...], TN) + mm(act2, dmsg2, TN)
-    g_out = g_out * grad_scale
+    g_out = (mm(act[...], dmsg[...], TN) + mm(far_act[...], far_dmsg[...], TN)) * grad_scale
     for j in range(latent // LANES):
         at = hidden // LANES * latent + j * hidden
         grads[at : at + hidden, :] = g_out[:, j * LANES : (j + 1) * LANES]
-    for lo, hi, stages in pieces:
-        if stages:
-            split(grads.at[lo:hi], stages[0], outs[:2])
-            outs = outs[2:]
-        else:
-            outs[0][...] = grads[lo:hi, :].astype(BF16)
-            outs = outs[1:]
+    split(grads, stage, (keep, send))
 
 
 def upper(stage):
-    axis, d = stage
-    return lax.rem(lax.axis_index(axis) // d, 2)
+    (axis0, d0), (axis1, d1) = stage
+    bit0 = lax.rem(lax.axis_index(axis0) // d0, 2)
+    bit1 = lax.rem(lax.axis_index(axis1) // d1, 2)
+    return jnp.where(lax.axis_index("feat") == 0, bit0, bit1)
 
 
 def split(block, stage, outs):
@@ -297,17 +288,11 @@
     place(stage, own, got, out)
 
 
-def write_kernel(layer, pieces, kept, *refs):
-    out_in, out_out, token, grads, slab_in, slab_out, sem = refs[-7:]
-    parts = refs[kept:-7]
+def write_kernel(layer, stage, kept, *refs):
+    own, got = refs[kept : kept + 2]
+    out_in, out_out, token, grads, slab_in, slab_out, sem = refs[kept + 2 :]
     token[...] = jnp.zeros_like(token)
-    for lo, hi, stages in pieces:
-        if stages:
-            place(stages[0], parts[0], parts[1], grads.at[lo:hi])
-            parts = parts[2:]
-        else:
-            grads[lo:hi, :] = parts[0][...].astype(F32)
-            parts = parts[1:]
+    place(stage, own, got, grads)
     latent, hidden = slab_in.shape
     for j in range(hidden // LANES):
         slab_in[:, j * LANES : (j + 1) * LANES] = grads[j * latent : (j + 1) * latent, :]
@@ -326,11 +311,8 @@
     def __init__(self, parts, stages, name):
         self.stages, self.name = stages, name
         self.done = 0
-        if stages:
-            self.keep, send = parts
-            self.got = swapped(send, stages[0])
-        else:
-            self.parts = [lax.psum(parts[0], ("chain", "basin"))]
+        self.keep, send = parts
+        self.got = swapped(send, stages[0])
 
     def step(self, after):
         n = len(self.stages)
@@ -359,7 +341,6 @@
                 body, [(shape, BF16)], [self.keep, self.got], 1_000_000, name=name, after=after
             )
             self.got = swapped(self.keep, self.stages[2 * n - 2 - i])
-        self.parts = [self.keep, self.got]
         return [self.keep]
 
 
@@ -368,14 +349,14 @@
     return dtotal[...] + back[...] + mm(spread[...], far)
 
 
-def join_kernel(layer, pairs, *refs):
+def join_kernel(layer, groups, pairs, *refs):
     dtotal, back, spread, remote_t, total = refs[:5]
-    weights = refs[5:9]
-    returned = refs[9 : 9 + 2 * pairs]
-    mine = refs[9 + 2 * pairs : 9 + 3 * pairs]
-    outs = refs[9 + 3 * pairs :]
+    weights, refs = refs[5:9], refs[9:]
+    returned, refs = refs[:groups], refs[groups:]
+    mine, others, outs = refs[:pairs], refs[pairs : 2 * pairs], refs[2 * pairs :]
     grad = gathered_grad(dtotal, back, returned, spread)
-    start_bwd(layer, norm_grad(grad, total[...]), weights, mine, remote_t, outs)
+    dtotal = norm_grad(grad, total[...])
+    start_bwd(layer, groups, dtotal, weights, mine, others, remote_t, outs)
 
 
 def last_kernel(*refs):
@@ -389,27 +370,42 @@
     return lax.ppermute(x, axis, [(i, (i + distance) % n) for i in range(n)])
 
 
+def over_mesh(x, target):
+    chain, groups, cores = (lax.axis_size(axis) for axis in ("chain", "basin", "feat"))
+    perm = []
+    for c in range(chain):
+        for b in range(groups):
+            for feat in range(cores):
+                to = target(c, b, feat)
+                if to is not None:
+                    start, end = (c * groups + b) * cores + feat, (to[0] * groups + to[1]) * cores
+                    perm.append((start, end + feat))
+    return lax.ppermute(x, ("chain", "basin", "feat"), perm)
+
+
 def swapped(x, stage):
-    axis, d = stage
-    return lax.ppermute(x, axis, [(i, i ^ d) for i in range(lax.axis_size(axis))])
-
-
-def routed(sends, sign):
-    chain, groups = lax.axis_size("chain"), lax.axis_size("basin")
-    got = []
-    for i, x in enumerate(sends):
-        perm = []
-        for c in range(chain):
-            for b in range(groups):
-                for feat in range(2):
-                    route = 2 * i + feat
-                    to_c = c + sign if route == 0 else c
-                    to_b = (b + sign * route) % groups
-                    if 0 <= to_c < chain and route < groups:
-                        start, end = (c * groups + b) * 2 + feat, (to_c * groups + to_b) * 2 + feat
-                        perm.append((start, end))
-        got.append(lax.ppermute(x, ("chain", "basin", "feat"), perm))
-    return got
+    def partner(c, b, feat):
+        axis, d = stage[feat]
+        return (c ^ d, b) if axis == "chain" else (c, b ^ d)
+
+    return over_mesh(x, partner)
+
+
+def forward(sends):
+    def target(i, c, b, feat):
+        route = 2 * i + feat
+        if route == 0:
+            return (c + 1, b) if c + 1 < lax.axis_size("chain") else None
+        groups = lax.axis_size("basin")
+        return (c, (b + route) % groups) if route < groups else None
+
+    return [over_mesh(x, functools.partial(target, i)) for i, x in enumerate(sends)]
+
+
+def backward(grads):
+    chain = lax.axis_size("chain")
+    up = lax.ppermute(grads[0], "chain", [(c, c - 1) for c in range(1, chain)])
+    return [up] + [around(x, "basin", -s) for s, x in enumerate(grads) if s]
 
 
 def other_core(got):
@@ -421,7 +417,7 @@
     groups = lax.axis_size("basin")
     pairs = (groups + 1) // 2
     layers, _, half = w_in.shape
-    far_rows = 2 * pairs * BLOCK
+    far_rows = groups * BLOCK
     own = rows // BLOCK
     grad_scale = float(rows * lax.axis_size("chain") * groups) ** (-0.5)
     last = layers - 1
@@ -449,10 +445,10 @@
     mine = []
     others = []
     for layer in range(layers):
-        mine.append(routed(sends, 1))
+        mine.append(forward(sends))
         if layer == 0:
             msg, local, local_t, remote, remote_t = call(
-                functools.partial(first_kernel, groups, pairs),
+                functools.partial(first_kernel, groups),
                 [act16(rows), act16(rows, rows), act16(rows, rows)]
                 + [act16(rows, far_rows), act16(far_rows, rows)],
                 [features, pick_self, block_index, block_values, *weights],
@@ -488,14 +484,13 @@
             )
             totals.append(total)
             inputs.append(new)
-    near_rows = pairs * BLOCK
     bwd_outs = (
-        [((rows, latent), F32), act16(rows), act16(near_rows)]
-        + [act16(near_rows, half)] * 2
-        + [act16(BLOCK)] * pairs
+        [((rows, latent), F32), act16(rows), act16(far_rows), act16(far_rows)]
+        + [act16(far_rows, half)] * 2
+        + [act16(BLOCK)] * groups
     )
     outs = call(
-        functools.partial(turn_kernel, last, pairs),
+        functools.partial(turn_kernel, last, groups, pairs),
         bwd_outs,
         [totals[-1], mixed, remote, remote_t, cotangent, *weights, *mine[last], *others[last]],
         2 * far_rows * ffn,
@@ -503,56 +498,44 @@
     )
     grad_rows = 2 * latent * half // LANES
 
-    def pair_stages(axis):
+    def distances(axis):
         return [(axis, 1 << i) for i in range(lax.axis_size(axis).bit_length() - 1)]
 
-    pieces = [[(0, grad_rows, pair_stages("basin") + pair_stages("chain"))]] * layers
+    over_basin, over_chain = distances("basin"), distances("chain")
+    n = len(over_basin)
+    stages = list(
+        zip(over_basin + over_chain, over_chain[:n] + over_basin + over_chain[n:], strict=True)
+    )
     returned = {}
     sums = {}
 
     def back(layer, outs, after):
-        near = routed(outs[5:], -1)
-        grad, dmsg, act, dpre = call(
-            functools.partial(back_kernel, layer),
-            [((rows, latent), F32), act16(rows), act16(rows, half), act16(rows, half)],
-            [outs[1], inputs[layer], local_t, *weights],
-            2 * rows * ffn + 2 * rows * rows * latent,
+        returned[layer] = backward(outs[6:])
+        grad, *parts = call(
+            functools.partial(back_kernel, layer, grad_scale, stages[0]),
+            [((rows, latent), F32), ((grad_rows // 2, LANES), F32)]
+            + [((grad_rows // 2, LANES), BF16)],
+            [outs[1], inputs[layer], local_t, *weights, *outs[2:6]],
+            3 * rows * ffn + 2 * rows * rows * latent,
+            scratch=[
+                pltpu.VMEM((grad_rows, LANES), F32),
+                pltpu.VMEM((rows, latent), BF16),
+                pltpu.VMEM((rows, half), BF16),
+                pltpu.VMEM((rows, half), BF16),
+            ],
             name=f"back{layer}",
             after=after,
         )
-        if layer:
-            near, grad = lax.optimization_barrier((near, grad))
-            returned[layer] = near + other_core(near)
-        else:
-            returned[layer] = near
-        shapes = []
-        for lo, hi, stages in pieces[layer]:
-            m = (hi - lo) // 2 if stages else hi - lo
-            shapes += [((m, LANES), F32)] * bool(stages) + [((m, LANES), BF16)]
-        parts = call(
-            functools.partial(weights_kernel, layer, grad_scale, pairs, pieces[layer]),
-            shapes,
-            [outs[1], remote_t, w_in, w_out, inputs[layer], dmsg, act, dpre]
-            + [*outs[2:5], *mine[layer], *others[layer]],
-            rows * ffn,
-            scratch=[pltpu.VMEM((grad_rows, LANES), F32)],
-            name=f"weights{layer}",
-        )
-        parts_made = parts[:1]
-        sums[layer] = []
-        for i, (_, _, stages) in enumerate(pieces[layer]):
-            n = 2 if stages else 1
-            sums[layer].append(Sum(parts[:n], stages, f"{layer}_{i}"))
-            parts = parts[n:]
-        return [outs[0], grad], parts_made
+        sums[layer] = Sum(parts, stages, f"{layer}")
+        return [outs[0], grad], [parts[0]]
 
     def join(layer, state, after):
         if layer:
             return call(
-                functools.partial(join_kernel, layer - 1, pairs),
+                functools.partial(join_kernel, layer - 1, groups, pairs),
                 bwd_outs,
                 [*state, spread, remote_t, totals[layer - 1]]
-                + [*weights, *returned[layer], *mine[layer - 1]],
+                + [*weights, *returned[layer], *mine[layer - 1], *others[layer - 1]],
                 2 * far_rows * ffn,
                 name=f"join{layer}",
                 after=after,
@@ -567,10 +550,10 @@
         )
 
     def write(layer, written, after):
-        ready = [x for piece in sums.pop(layer) for x in piece.parts]
+        ready = [sums[layer].keep, sums[layer].got]
         kept = [*written, *after]
         return pl.pallas_call(
-            functools.partial(write_kernel, layer, pieces[layer], len(kept)),
+            functools.partial(write_kernel, layer, stages[0], len(kept)),
             out_shape=[
                 jax.ShapeDtypeStruct((layers, latent, half), F32),
                 jax.ShapeDtypeStruct((layers, half, latent), F32),
@@ -590,36 +573,28 @@
             name=f"write{layer}",
         )(*written, *after, *ready)
 
-    def step(layer, after):
-        for piece in sums[layer]:
-            after = piece.step(after)
-        return after
-
-    count = 2 * max(len(stages) for _, _, stages in pieces[0]) - 1
+    count = 2 * len(stages) - 1
     at = []
     for layer in reversed(range(layers)):
         state, at = back(layer, outs, at)
-        for above in reversed(range(layer + 1, layers)):
-            at = step(above, at)
-            if layer == 0 and above == last:
-                near, at = lax.optimization_barrier((returned[0], at))
-                returned[0] = near + other_core(near)
         if layer:
+            for above in reversed(range(layer + 1, layers)):
+                at = sums[above].step(at)
             outs = join(layer, state, at)
             at = outs[1:2]
-    grad, token = join(0, state, at)
-    at = [token]
     written = []
-    for turn in range(layers - 1, layers - 1 + count):
-        for layer in reversed(range(layers)):
-            if layer in sums and sums[layer][0].done <= turn - (last - layer) < count:
-                at = step(layer, at)
-            elif layer and turn - (last - layer) == count:
+    waiting = list(reversed(range(layers)))
+    while waiting:
+        for layer in list(waiting):
+            if sums[layer].done < count:
+                at = sums[layer].step(at)
+            else:
                 *written, token = write(layer, written, at)
                 at = [token]
-    for layer in reversed(range(layers)):
-        if layer in sums:
-            *written, _ = write(layer, written, [])
+                waiting.remove(layer)
+            if layer == 1 and sums[layer].done == 1:
+                grad, token = join(0, state, at)
+                at = [token]
     return (grad, *written)
 
 

time: 125 us -> 119 us (0.952)
  waiting for transfers between devices: 38.3 us -> 27.8 us
  starting transfers between devices: 45.3 us -> 50.8 us
    ppermute x24, waiting for transfers between devices: 37.6 us -> 27.1 us  [the longest x21 25.3 us: over_mesh(): return lax.ppermute(x, ('chain', 'basin', 'feat'), perm)]
    ppermute x24, starting transfers between devices: 43.5 us -> 46.4 us  [the longest x21 42.1 us: over_mesh(): return lax.ppermute(x, ('chain', 'basin', 'feat'), perm)]
    ppermute x8, starting transfers between devices: 1.79 us -> 4.39 us  [around(): return lax.ppermute(x, axis, [(i, (i + distance) % n) for i in range(n)])]
    pallas_call x34 -> x31, Pallas kernels: 28.6 us -> 27.4 us  [call(): pl.pallas_call(lambda *refs: body(*refs[skipped:]), out_shape=[jax.ShapeD...]
  transfers between devices with their start and end apart: 32 -> 32, of which waited for: 16 -> 18; matrix products, arithmetic and copies ran while one was open for 1% -> 1% of each run, Pallas kernels for 22% -> 22%
where the time goes in v5:
time: 119 us; the launch traced here: 118 us
  starting transfers between devices  50.8 us (43%)
  Pallas kernels  31.4 us (26%)
  waiting for transfers between devices  27.8 us (23%)
  local copies, waits for them, and re-layouts  6.18 us (5%)
    ppermute x21, starting transfers between devices, over_mesh(): return lax.ppermute(x, ('chain', 'basin', 'feat'), perm)  42.1 us
    pallas_call x31, Pallas kernels, call(): pl.pallas_call(lambda *refs: body(*refs[skipped:]), out_shape=[jax.ShapeD...  27.4 us
    ppermute x21, waiting for transfers between devices, over_mesh(): return lax.ppermute(x, ('chain', 'basin', 'feat'), perm)  25.3 us
    unnamed x19, local copies, waits for them, and re-layouts  6.18 us
    ppermute x8, starting transfers between devices, around(): return lax.ppermute(x, axis, [(i, (i + distance) % n) for i in range(n)])  4.39 us
    ppermute x3, starting transfers between devices, backward(): up = lax.ppermute(grads[0], 'chain', [(c, c - 1) for c in range(1, chain)])  4.27 us
    pallas_call x3, Pallas kernels, write(): pl.pallas_call(functools.partial(write_kernel, layer, stages[0], len(kept...  3.99 us
  transfers between devices with their start and end apart: 32, of which 18 were waited for; matrix products, arithmetic and copies ran while one was open for 1% of the time, Pallas kernels for 22%

profile of v5, /device:TPU:0, one launch (start us, length us, event | category | flops | bytes accessed | tf_op | source)
XLA Modules:
  0.0 118.1 jit_solution(18331780844556337065)
XLA Ops:
  3.6 4.9 %collective-permute-start.2 = (bf16[128,256]{1,0:T(8,128)(2,1)S(1)}, bf16[128,256]{1,0:T(8,128)(2,1)S(1)}, u32[]{:S(2)}, u32[]{:S(2)}) collective-permute-start(bf16[128,256]{1,0:T(8,128)(2,1)S(1)} %get-tuple-element.81), channel_id=1, source_target_pairs={{0,4},{1,3},{2,6},{3,1},{4,8},{5,7},{6,10},{7,5},{8,12},{9,11},{10... | collective-permute-start | bytes 196616 | tf_op jit(solution)/shard_map/ppermute | solution.py:383
  13.7 2.7 %first.1 = (bf16[768,256]{1,0:T(8,128)(2,1)S(1)}, bf16[768,768]{1,0:T(8,128)(2,1)S(1)}, bf16[768,768]{1,0:T(8,128)(2,1)S(1)}, bf16[768,256]{1,0:T(8,128)(2,1)S(1)}, bf16[256,768]{1,0:T(8,128)(2,1)S(1)}) custom-call(bf16[768,256]{1,0:T(8,128)(2,1)S(1)} %copy-done.5, bf16[128,768]{1,0:T(8,128)(2,1)S(1)} %get-tuple-element.79.refs_1_, ...), custom_call_target="tpu_custom_call" | custom-call | flops 956301312 | bytes 4000000 | tf_op jit(solution)/shard_map/first/pallas_call | solution.py:32
  18.8 3.5 %collective-permute-start.4 = (bf16[128,256]{1,0:T(8,128)(2,1)S(1)}, bf16[128,256]{1,0:T(8,128)(2,1)S(1)}, u32[]{:S(2)}, u32[]{:S(2)}) collective-permute-start(bf16[128,256]{1,0:T(8,128)(2,1)S(1)} %get-tuple-element.88), channel_id=1, source_target_pairs={{0,4},{1,3},{2,6},{3,1},{4,8},{5,7},{6,10},{7,5},{8,12},{9,11},{10... | collective-permute-start | bytes 196616 | tf_op jit(solution)/shard_map/ppermute | solution.py:383
  26.5 4.3 %collective-permute-start.6 = (bf16[128,256]{1,0:T(8,128)(2,1)S(1)}, bf16[128,256]{1,0:T(8,128)(2,1)S(1)}, u32[]{:S(2)}, u32[]{:S(2)}) collective-permute-start(bf16[128,256]{1,0:T(8,128)(2,1)S(1)} %get-tuple-element.93), channel_id=1, source_target_pairs={{0,4},{1,3},{2,6},{3,1},{4,8},{5,7},{6,10},{7,5},{8,12},{9,11},{10... | collective-permute-start | bytes 196616 | tf_op jit(solution)/shard_map/ppermute | solution.py:383
  33.9 2.1 %turn.1 = (f32[768,256]{1,0:T(8,128)S(1)}, bf16[768,256]{1,0:T(8,128)(2,1)S(1)}, bf16[256,256]{1,0:T(8,128)(2,1)S(1)}, bf16[256,256]{1,0:T(8,128)(2,1)S(1)}, bf1...) custom-call(f32[768,256]{1,0:T(8,128)S(1)} %get-tuple-element.92.ref, ...), custom_call_target="tpu_custom_call" | custom-call | flops 536870912 | bytes 4000000 | tf_op jit(solution)/shard_map/turn/pallas_call | solution.py:32
  37.5 1.6 %collective-permute-start.9 = (bf16[128,256]{1,0:T(8,128)(2,1)S(1)}, bf16[128,256]{1,0:T(8,128)(2,1)S(1)}, u32[]{:S(2)}, u32[]{:S(2)}) collective-permute-start(bf16[128,256]{1,0:T(8,128)(2,1)S(1)} %get-tuple-element.109), channel_id=1, source_target_pairs={{0,2},{2,0},{1,3},{3,1},{4,6},{6,4},{5,7},{7,5},{8,10},{10,8},{9,1... | collective-permute-start | bytes 196616 | tf_op jit(solution)/shard_map/ppermute | solution.py:370
  39.0 3.2 %back2.1 = (f32[768,256]{1,0:T(8,128)S(1)}, f32[1024,128]{1,0:T(8,128)S(1)}, bf16[1024,128]{1,0:T(8,128)(2,1)S(1)}) custom-call(bf16[768,256]{1,0:T(8,128)(2,1)S(1)} %get-tuple-element.98.refs_0_, bf16[768,256]{1,0:T(8,128)(2,1)S(1)} %get-tuple-element.94.refs_0_.refs_1_, bf16[768,768]{1,0:T(8,128)(2,1)S(1)} %get-tuple-element.99.refs_2_.refs_3_, ...), custom_call_target="tpu_custom_call" | custom-call | flops 2717908992 | bytes 4000000 | tf_op jit(solution)/shard_map/back2/pallas_call | solution.py:32
  42.8 1.6 %join2.1 = (f32[768,256]{1,0:T(8,128)S(1)}, bf16[768,256]{1,0:T(8,128)(2,1)S(1)}, bf16[256,256]{1,0:T(8,128)(2,1)S(1)}, bf16[256,256]{1,0:T(8,128)(2,1)S(1)}, bf...) custom-call(f32[1024,128]{1,0:T(8,128)S(1)} %get-tuple-element.104.r, ...), custom_call_target="tpu_custom_call" | custom-call | flops 536870912 | bytes 4000000 | tf_op jit(solution)/shard_map/join2/pallas_call | solution.py:32
  45.7 1.5 %collective-permute-start.12 = (bf16[128,256]{1,0:T(8,128)(2,1)S(1)}, bf16[128,256]{1,0:T(8,128)(2,1)S(1)}, u32[]{:S(2)}, u32[]{:S(2)}) collective-permute-start(bf16[128,256]{1,0:T(8,128)(2,1)S(1)} %get-tuple-element.121), channel_id=1, source_target_pairs={{0,2},{2,0},{1,3},{3,1},{4,6},{6,4},{5,7},{7,5},{8,10},{10,8},{9,1... | collective-permute-start | bytes 196616 | tf_op jit(solution)/shard_map/ppermute | solution.py:370
  47.2 3.2 %back1.1 = (f32[768,256]{1,0:T(8,128)S(1)}, f32[1024,128]{1,0:T(8,128)S(1)}, bf16[1024,128]{1,0:T(8,128)(2,1)S(1)}) custom-call(bf16[768,256]{1,0:T(8,128)(2,1)S(1)} %get-tuple-element.110.refs_0_.refs_1_, bf16[768,256]{1,0:T(8,128)(2,1)S(1)} %get-tuple-element.110.refs_0_.refs_1_, bf16[768,256]{1,0:T(8,128)(2,1)S(1)} %get-tuple-element.89.refs_0_.refs_2_, ...), custom_call_target="tpu_custom_call" | custom-call | flops 2717908992 | bytes 4000000 | tf_op jit(solution)/shard_map/back1/pallas_call | solution.py:32
  52.0 1.6 %join1.1 = (f32[768,256]{1,0:T(8,128)S(1)}, bf16[768,256]{1,0:T(8,128)(2,1)S(1)}, bf16[256,256]{1,0:T(8,128)(2,1)S(1)}, bf16[256,256]{1,0:T(8,128)(2,1)S(1)}, bf...) custom-call(f32[512,128]{1,0:T(8,128)S(1)} %get-tuple-element.117.re, ...), custom_call_target="tpu_custom_call" | custom-call | flops 536870912 | bytes 4000000 | tf_op jit(solution)/shard_map/join1/pallas_call | solution.py:32
  53.6 3.2 %back0.1 = (f32[768,256]{1,0:T(8,128)S(1)}, f32[1024,128]{1,0:T(8,128)S(1)}, bf16[1024,128]{1,0:T(8,128)(2,1)S(1)}) custom-call(bf16[768,256]{1,0:T(8,128)(2,1)S(1)} %get-tuple-element.122.refs_0_.refs_1_, bf16[768,256]{1,0:T(8,128)(2,1)S(1)} %get-tuple-element.122.refs_0_.refs_1_, bf16[768,256]{1,0:T(8,128)(2,1)S(1)} %copy-done.6, ...), custom_call_target="tpu_custom_call" | custom-call | flops 2717908992 | bytes 4000000 | tf_op jit(solution)/shard_map/back0/pallas_call | solution.py:32
  57.8 3.3 %collective-permute-start.13 = (bf16[512,128]{1,0:T(8,128)(2,1)S(1)}, bf16[512,128]{1,0:T(8,128)(2,1)S(1)}, u32[]{:S(2)}, u32[]{:S(2)}) collective-permute-start(bf16[512,128]{1,0:T(8,128)(2,1)S(1)} %get-tuple-element.128), channel_id=1, source_target_pairs={{0,4},{1,3},{2,6},{3,1},{4,0},{5,7},{6,2},{7,5},{8,12},{9,11},{10,... | collective-permute-start | bytes 393224 | tf_op jit(solution)/shard_map/ppermute | solution.py:383
  61.1 1.5 %collective-permute-start.15 = (bf16[128,256]{1,0:T(8,128)(2,1)S(1)}, bf16[128,256]{1,0:T(8,128)(2,1)S(1)}, u32[]{:S(2)}, u32[]{:S(2)}) collective-permute-start(bf16[128,256]{1,0:T(8,128)(2,1)S(1)} %get-tuple-element.134), channel_id=1, source_target_pairs={{4,0},{8,4},{12,8},{5,1},{9,5},{13,9},{6,2},{10,6},{14,10},{7,3},{... | collective-permute-start | bytes 196616 | tf_op jit(solution)/shard_map/ppermute | solution.py:407
  63.2 2.3 %collective-permute-done.13.refs_2_ = bf16[512,128]{1,0:T(8,128)(2,1)S(1)} collective-permute-done((bf16[512,128]{1,0:T(8,128)(2,1)S(1)}, bf16[512,128]{1,0:T(8,128)(2,1)S(1)}, u32[]{:S(2)}, u32[]{:S(2)}) %collective-permute-start.13) | collective-permute-done | bytes 131104 | tf_op jit(solution)/shard_map/ppermute | solution.py:383
  68.5 3.1 %collective-permute-start.20 = (bf16[512,128]{1,0:T(8,128)(2,1)S(1)}, bf16[512,128]{1,0:T(8,128)(2,1)S(1)}, u32[]{:S(2)}, u32[]{:S(2)}) collective-permute-start(bf16[512,128]{1,0:T(8,128)(2,1)S(1)} %get-tuple-element.143), channel_id=1, source_target_pairs={{0,4},{1,3},{2,6},{3,1},{4,0},{5,7},{6,2},{7,5},{8,12},{9,11},{10,... | collective-permute-start | bytes 393224 | tf_op jit(solution)/shard_map/ppermute | solution.py:383
  71.6 2.8 %collective-permute-start.18 = (bf16[256,128]{1,0:T(8,128)(2,1)S(1)}, bf16[256,128]{1,0:T(8,128)(2,1)S(1)}, u32[]{:S(2)}, u32[]{:S(2)}) collective-permute-start(bf16[256,128]{1,0:T(8,128)(2,1)S(1)} %get-tuple-element.140), channel_id=1, source_target_pairs={{0,8},{1,9},{2,10},{3,11},{4,12},{5,13},{6,14},{7,15},{8,0},{9,1},... | collective-permute-start | bytes 196616 | tf_op jit(solution)/shard_map/ppermute | solution.py:383
  74.4 2.4 %collective-permute-done.18.refs_2_ = bf16[256,128]{1,0:T(8,128)(2,1)S(1)} collective-permute-done((bf16[256,128]{1,0:T(8,128)(2,1)S(1)}, bf16[256,128]{1,0:T(8,128)(2,1)S(1)}, u32[]{:S(2)}, u32[]{:S(2)}) %collective-permute-start.18) | collective-permute-done | bytes 65568 | tf_op jit(solution)/shard_map/ppermute | solution.py:383
  76.8 3.4 %collective-permute-start.21 = (bf16[256,128]{1,0:T(8,128)(2,1)S(1)}, bf16[256,128]{1,0:T(8,128)(2,1)S(1)}, u32[]{:S(2)}, u32[]{:S(2)}) collective-permute-start(bf16[256,128]{1,0:T(8,128)(2,1)S(1)} %sum_2_2.1.refs_0_.refs_1_), channel_id=1, source_target_pairs={{0,8},{1,9},{2,10},{3,11},{4,12},{5,13},{6,14},{7,15},{8,0},{9,1},... | collective-permute-start | bytes 196616 | tf_op jit(solution)/shard_map/ppermute | solution.py:383
  80.3 3.5 %collective-permute-done.21.refs_2_ = bf16[256,128]{1,0:T(8,128)(2,1)S(1)} collective-permute-done((bf16[256,128]{1,0:T(8,128)(2,1)S(1)}, bf16[256,128]{1,0:T(8,128)(2,1)S(1)}, u32[]{:S(2)}, u32[]{:S(2)}) %collective-permute-start.21) | collective-permute-done | bytes 65568 | tf_op jit(solution)/shard_map/ppermute | solution.py:383
  84.0 1.8 %collective-permute-start.22 = (bf16[256,128]{1,0:T(8,128)(2,1)S(1)}, bf16[256,128]{1,0:T(8,128)(2,1)S(1)}, u32[]{:S(2)}, u32[]{:S(2)}) collective-permute-start(bf16[256,128]{1,0:T(8,128)(2,1)S(1)} %get-tuple-element.145), channel_id=1, source_target_pairs={{0,8},{1,9},{2,10},{3,11},{4,12},{5,13},{6,14},{7,15},{8,0},{9,1},... | collective-permute-start | bytes 196616 | tf_op jit(solution)/shard_map/ppermute | solution.py:383
  87.0 2.3 %collective-permute-done.22.refs_2_ = bf16[256,128]{1,0:T(8,128)(2,1)S(1)} collective-permute-done((bf16[256,128]{1,0:T(8,128)(2,1)S(1)}, bf16[256,128]{1,0:T(8,128)(2,1)S(1)}, u32[]{:S(2)}, u32[]{:S(2)}) %collective-permute-start.22) | collective-permute-done | bytes 65568 | tf_op jit(solution)/shard_map/ppermute | solution.py:383
  89.3 2.4 %collective-permute-done.23.refs_2_ = bf16[256,128]{1,0:T(8,128)(2,1)S(1)} collective-permute-done((bf16[256,128]{1,0:T(8,128)(2,1)S(1)}, bf16[256,128]{1,0:T(8,128)(2,1)S(1)}, u32[]{:S(2)}, u32[]{:S(2)}) %collective-permute-start.23) | collective-permute-done | bytes 65568 | tf_op jit(solution)/shard_map/ppermute | solution.py:383
  92.3 2.9 %collective-permute-start.27 = (bf16[1024,128]{1,0:T(8,128)(2,1)S(1)}, bf16[1024,128]{1,0:T(8,128)(2,1)S(1)}, u32[]{:S(2)}, u32[]{:S(2)}) collective-permute-start(bf16[1024,128]{1,0:T(8,128)(2,1)S(1)} %sum_2_4.1.refs_0_.refs_1_), channel_id=1, source_target_pairs={{0,2},{1,5},{2,0},{3,7},{4,6},{5,1},{6,4},{7,3},{8,10},{9,13},{10,... | collective-permute-start | bytes 786440 | tf_op jit(solution)/shard_map/ppermute | solution.py:383
  95.9 2.2 %collective-permute-start.26 = (bf16[256,128]{1,0:T(8,128)(2,1)S(1)}, bf16[256,128]{1,0:T(8,128)(2,1)S(1)}, u32[]{:S(2)}, u32[]{:S(2)}) collective-permute-start(bf16[256,128]{1,0:T(8,128)(2,1)S(1)} %sum_0_2.1.refs_0_.refs_1_), channel_id=1, source_target_pairs={{0,8},{1,9},{2,10},{3,11},{4,12},{5,13},{6,14},{7,15},{8,0},{9,1},... | collective-permute-start | bytes 196616 | tf_op jit(solution)/shard_map/ppermute | solution.py:383
  98.1 2.2 %collective-permute-done.25.refs_2_ = bf16[256,128]{1,0:T(8,128)(2,1)S(1)} collective-permute-done((bf16[256,128]{1,0:T(8,128)(2,1)S(1)}, bf16[256,128]{1,0:T(8,128)(2,1)S(1)}, u32[]{:S(2)}, u32[]{:S(2)}) %collective-permute-start.25) | collective-permute-done | bytes 65568 | tf_op jit(solution)/shard_map/ppermute | solution.py:383
  100.4 1.7 %collective-permute-start.28 = (bf16[512,128]{1,0:T(8,128)(2,1)S(1)}, bf16[512,128]{1,0:T(8,128)(2,1)S(1)}, u32[]{:S(2)}, u32[]{:S(2)}) collective-permute-start(bf16[512,128]{1,0:T(8,128)(2,1)S(1)} %sum_1_3.1.refs_0_.refs_1_), channel_id=1, source_target_pairs={{0,4},{1,3},{2,6},{3,1},{4,0},{5,7},{6,2},{7,5},{8,12},{9,11},{10,... | collective-permute-start | bytes 393224 | tf_op jit(solution)/shard_map/ppermute | solution.py:383
  102.1 3.2 %collective-permute-start.29 = (bf16[512,128]{1,0:T(8,128)(2,1)S(1)}, bf16[512,128]{1,0:T(8,128)(2,1)S(1)}, u32[]{:S(2)}, u32[]{:S(2)}) collective-permute-start(bf16[512,128]{1,0:T(8,128)(2,1)S(1)} %sum_0_3.1.refs_0_.refs_1_), channel_id=1, source_target_pairs={{0,4},{1,3},{2,6},{3,1},{4,0},{5,7},{6,2},{7,5},{8,12},{9,11},{10,... | collective-permute-start | bytes 393224 | tf_op jit(solution)/shard_map/ppermute | solution.py:383
  107.0 2.7 %collective-permute-done.29.refs_2_ = bf16[512,128]{1,0:T(8,128)(2,1)S(1)} collective-permute-done((bf16[512,128]{1,0:T(8,128)(2,1)S(1)}, bf16[512,128]{1,0:T(8,128)(2,1)S(1)}, u32[]{:S(2)}, u32[]{:S(2)}) %collective-permute-start.29) | collective-permute-done | bytes 131104 | tf_op jit(solution)/shard_map/ppermute | solution.py:383
  109.8 3.5 %collective-permute-done.30.refs_4_ = bf16[1024,128]{1,0:T(8,128)(2,1)S(1)} collective-permute-done((bf16[1024,128]{1,0:T(8,128)(2,1)S(1)}, bf16[1024,128]{1,0:T(8,128)(2,1)S(1)}, u32[]{:S(2)}, u32[]{:S(2)}) %collective-permute-start.30) | collective-permute-done | bytes 262176 | tf_op jit(solution)/shard_map/ppermute | solution.py:383
  114.5 1.7 %collective-permute-done.31.refs_4_ = bf16[1024,128]{1,0:T(8,128)(2,1)S(1)} collective-permute-done((bf16[1024,128]{1,0:T(8,128)(2,1)S(1)}, bf16[1024,128]{1,0:T(8,128)(2,1)S(1)}, u32[]{:S(2)}, u32[]{:S(2)}) %collective-permute-start.31) | collective-permute-done | bytes 262176 | tf_op jit(solution)/shard_map/ppermute | solution.py:383
  116.2 1.7 %write0.1 = (f32[3,256,512]{2,1,0:T(8,128)}, f32[3,512,256]{2,1,0:T(8,128)}, f32[8,128]{1,0:T(8,128)}) custom-call(f32[3,256,512]{2,1,0:T(8,128)} %get-tuple-element.150.refs_0_, f32[3,512,256]{2,1,0:T(8,128)} %get-tuple-element.151.refs_1_, f32[8,128]{1,0:T(8,128)S(1)} %get-tuple-element.152.refs_2_, ...), custom_call_target="tpu_custom_call", output_to_operand_aliasing={{0}: (0, {}), {1}: (1, {})} | custom-call | bytes 4000000 | tf_op jit(solution)/shard_map/write0/pallas_call | solution.py:555
  (86 shorter events, 32.9 us)
Async XLA Ops:
  0.6 8.6 %collective-permute-start = (bf16[3,256,512]{2,1,0:T(8,128)(2,1)}, bf16[3,256,512]{2,1,0:T(8,128)(2,1)S(1)}, u32[]{:S(2)}, u32[]{:S(2)}) collective-permute-start(bf16[3,256,512]{2,1,0:T(8,128)(2,1)} %refs_4_.11), channel_id=1, source_target_pairs={{0,1},{1,0},{2,3},{3,2},{4,5},{5,4},{6,7},{7,6},{8,9},{9,8},{10,11... | collective-permute-start | bytes 2359304 | tf_op jit(solution)/shard_map/ppermute | solution.py:370
  1.1 8.1 %collective-permute-start.1 = (bf16[3,512,256]{2,1,0:T(8,128)(2,1)}, bf16[3,512,256]{2,1,0:T(8,128)(2,1)S(1)}, u32[]{:S(2)}, u32[]{:S(2)}) collective-permute-start(bf16[3,512,256]{2,1,0:T(8,128)(2,1)} %refs_6_.13), channel_id=1, source_target_pairs={{0,1},{1,0},{2,3},{3,2},{4,5},{5,4},{6,7},{7,6},{8,9},{9,8},{10,11... | collective-permute-start | bytes 2359304 | tf_op jit(solution)/shard_map/ppermute | solution.py:370
  3.6 12.8 %collective-permute-start.2 = (bf16[128,256]{1,0:T(8,128)(2,1)S(1)}, bf16[128,256]{1,0:T(8,128)(2,1)S(1)}, u32[]{:S(2)}, u32[]{:S(2)}) collective-permute-start(bf16[128,256]{1,0:T(8,128)(2,1)S(1)} %get-tuple-element.81), channel_id=1, source_target_pairs={{0,4},{1,3},{2,6},{3,1},{4,8},{5,7},{6,10},{7,5},{8,12},{9,11},{10... | collective-permute-start | bytes 196616 | tf_op jit(solution)/shard_map/ppermute | solution.py:383
  16.4 1.3 %collective-permute-start.3 = (bf16[128,256]{1,0:T(8,128)(2,1)S(1)}, bf16[128,256]{1,0:T(8,128)(2,1)S(1)}, u32[]{:S(2)}, u32[]{:S(2)}) collective-permute-start(bf16[128,256]{1,0:T(8,128)(2,1)S(1)} %collective-permute-done.2.refs_7_.refs_12_), channel_id=1, source_target_pairs={{0,1},{1,0},{2,3},{3,2},{4,5},{5,4},{6,7},{7,6},{8,9},{9,8},{10,11... | collective-permute-start | bytes 196616 | tf_op jit(solution)/shard_map/ppermute | solution.py:370
  18.8 5.4 %collective-permute-start.4 = (bf16[128,256]{1,0:T(8,128)(2,1)S(1)}, bf16[128,256]{1,0:T(8,128)(2,1)S(1)}, u32[]{:S(2)}, u32[]{:S(2)}) collective-permute-start(bf16[128,256]{1,0:T(8,128)(2,1)S(1)} %get-tuple-element.88), channel_id=1, source_target_pairs={{0,4},{1,3},{2,6},{3,1},{4,8},{5,7},{6,10},{7,5},{8,12},{9,11},{10... | collective-permute-start | bytes 196616 | tf_op jit(solution)/shard_map/ppermute | solution.py:383
  24.2 1.3 %collective-permute-start.5 = (bf16[128,256]{1,0:T(8,128)(2,1)S(1)}, bf16[128,256]{1,0:T(8,128)(2,1)S(1)}, u32[]{:S(2)}, u32[]{:S(2)}) collective-permute-start(bf16[128,256]{1,0:T(8,128)(2,1)S(1)} %collective-permute-done.4.refs_7_.refs_12_), channel_id=1, source_target_pairs={{0,1},{1,0},{2,3},{3,2},{4,5},{5,4},{6,7},{7,6},{8,9},{9,8},{10,11... | collective-permute-start | bytes 196616 | tf_op jit(solution)/shard_map/ppermute | solution.py:370
  26.5 6.2 %collective-permute-start.6 = (bf16[128,256]{1,0:T(8,128)(2,1)S(1)}, bf16[128,256]{1,0:T(8,128)(2,1)S(1)}, u32[]{:S(2)}, u32[]{:S(2)}) collective-permute-start(bf16[128,256]{1,0:T(8,128)(2,1)S(1)} %get-tuple-element.93), channel_id=1, source_target_pairs={{0,4},{1,3},{2,6},{3,1},{4,8},{5,7},{6,10},{7,5},{8,12},{9,11},{10... | collective-permute-start | bytes 196616 | tf_op jit(solution)/shard_map/ppermute | solution.py:383
  32.7 1.3 %collective-permute-start.7 = (bf16[128,256]{1,0:T(8,128)(2,1)S(1)}, bf16[128,256]{1,0:T(8,128)(2,1)S(1)}, u32[]{:S(2)}, u32[]{:S(2)}) collective-permute-start(bf16[128,256]{1,0:T(8,128)(2,1)S(1)} %collective-permute-done.6.refs_7_.refs_9_), channel_id=1, source_target_pairs={{0,1},{1,0},{2,3},{3,2},{4,5},{5,4},{6,7},{7,6},{8,9},{9,8},{10,11... | collective-permute-start | bytes 196616 | tf_op jit(solution)/shard_map/ppermute | solution.py:370
  36.0 6.8 %collective-permute-start.8 = (bf16[128,256]{1,0:T(8,128)(2,1)S(1)}, bf16[128,256]{1,0:T(8,128)(2,1)S(1)}, u32[]{:S(2)}, u32[]{:S(2)}) collective-permute-start(bf16[128,256]{1,0:T(8,128)(2,1)S(1)} %get-tuple-element.108), channel_id=1, source_target_pairs={{4,0},{8,4},{12,8},{5,1},{9,5},{13,9},{6,2},{10,6},{14,10},{7,3},{... | collective-permute-start | bytes 196616 | tf_op jit(solution)/shard_map/ppermute | solution.py:407
  37.5 5.4 %collective-permute-start.9 = (bf16[128,256]{1,0:T(8,128)(2,1)S(1)}, bf16[128,256]{1,0:T(8,128)(2,1)S(1)}, u32[]{:S(2)}, u32[]{:S(2)}) collective-permute-start(bf16[128,256]{1,0:T(8,128)(2,1)S(1)} %get-tuple-element.109), channel_id=1, source_target_pairs={{0,2},{2,0},{1,3},{3,1},{4,6},{6,4},{5,7},{7,5},{8,10},{10,8},{9,1... | collective-permute-start | bytes 196616 | tf_op jit(solution)/shard_map/ppermute | solution.py:370
  42.2 8.8 %collective-permute-start.10 = (bf16[1024,128]{1,0:T(8,128)(2,1)S(1)}, bf16[1024,128]{1,0:T(8,128)(2,1)S(1)}, u32[]{:S(2)}, u32[]{:S(2)}) collective-permute-start(bf16[1024,128]{1,0:T(8,128)(2,1)S(1)} %get-tuple-element.116), channel_id=1, source_target_pairs={{0,2},{1,5},{2,0},{3,7},{4,6},{5,1},{6,4},{7,3},{8,10},{9,13},{10,... | collective-permute-start | bytes 786440 | tf_op jit(solution)/shard_map/ppermute | solution.py:383
  44.4 7.6 %collective-permute-start.11 = (bf16[128,256]{1,0:T(8,128)(2,1)S(1)}, bf16[128,256]{1,0:T(8,128)(2,1)S(1)}, u32[]{:S(2)}, u32[]{:S(2)}) collective-permute-start(bf16[128,256]{1,0:T(8,128)(2,1)S(1)} %get-tuple-element.120), channel_id=1, source_target_pairs={{4,0},{8,4},{12,8},{5,1},{9,5},{13,9},{6,2},{10,6},{14,10},{7,3},{... | collective-permute-start | bytes 196616 | tf_op jit(solution)/shard_map/ppermute | solution.py:407
  45.7 6.3 %collective-permute-start.12 = (bf16[128,256]{1,0:T(8,128)(2,1)S(1)}, bf16[128,256]{1,0:T(8,128)(2,1)S(1)}, u32[]{:S(2)}, u32[]{:S(2)}) collective-permute-start(bf16[128,256]{1,0:T(8,128)(2,1)S(1)} %get-tuple-element.121), channel_id=1, source_target_pairs={{0,2},{2,0},{1,3},{3,1},{4,6},{6,4},{5,7},{7,5},{8,10},{10,8},{9,1... | collective-permute-start | bytes 196616 | tf_op jit(solution)/shard_map/ppermute | solution.py:370
  50.4 15.1 %collective-permute-start.14 = (bf16[1024,128]{1,0:T(8,128)(2,1)S(1)}, bf16[1024,128]{1,0:T(8,128)(2,1)S(1)}, u32[]{:S(2)}, u32[]{:S(2)}) collective-permute-start(bf16[1024,128]{1,0:T(8,128)(2,1)S(1)} %get-tuple-element.130), channel_id=1, source_target_pairs={{0,2},{1,5},{2,0},{3,7},{4,6},{5,1},{6,4},{7,3},{8,10},{9,13},{10,... | collective-permute-start | bytes 786440 | tf_op jit(solution)/shard_map/ppermute | solution.py:383
  56.8 11.6 %collective-permute-start.17 = (bf16[1024,128]{1,0:T(8,128)(2,1)S(1)}, bf16[1024,128]{1,0:T(8,128)(2,1)S(1)}, u32[]{:S(2)}, u32[]{:S(2)}) collective-permute-start(bf16[1024,128]{1,0:T(8,128)(2,1)S(1)} %get-tuple-element.138), channel_id=1, source_target_pairs={{0,2},{1,5},{2,0},{3,7},{4,6},{5,1},{6,4},{7,3},{8,10},{9,13},{10,... | collective-permute-start | bytes 786440 | tf_op jit(solution)/shard_map/ppermute | solution.py:383
  57.8 7.7 %collective-permute-start.13 = (bf16[512,128]{1,0:T(8,128)(2,1)S(1)}, bf16[512,128]{1,0:T(8,128)(2,1)S(1)}, u32[]{:S(2)}, u32[]{:S(2)}) collective-permute-start(bf16[512,128]{1,0:T(8,128)(2,1)S(1)} %get-tuple-element.128), channel_id=1, source_target_pairs={{0,4},{1,3},{2,6},{3,1},{4,0},{5,7},{6,2},{7,5},{8,12},{9,11},{10,... | collective-permute-start | bytes 393224 | tf_op jit(solution)/shard_map/ppermute | solution.py:383
  61.1 6.1 %collective-permute-start.15 = (bf16[128,256]{1,0:T(8,128)(2,1)S(1)}, bf16[128,256]{1,0:T(8,128)(2,1)S(1)}, u32[]{:S(2)}, u32[]{:S(2)}) collective-permute-start(bf16[128,256]{1,0:T(8,128)(2,1)S(1)} %get-tuple-element.134), channel_id=1, source_target_pairs={{4,0},{8,4},{12,8},{5,1},{9,5},{13,9},{6,2},{10,6},{14,10},{7,3},{... | collective-permute-start | bytes 196616 | tf_op jit(solution)/shard_map/ppermute | solution.py:407
  62.6 4.6 %collective-permute-start.16 = (bf16[128,256]{1,0:T(8,128)(2,1)S(1)}, bf16[128,256]{1,0:T(8,128)(2,1)S(1)}, u32[]{:S(2)}, u32[]{:S(2)}) collective-permute-start(bf16[128,256]{1,0:T(8,128)(2,1)S(1)} %get-tuple-element.135), channel_id=1, source_target_pairs={{0,2},{2,0},{1,3},{3,1},{4,6},{6,4},{5,7},{7,5},{8,10},{10,8},{9,1... | collective-permute-start | bytes 196616 | tf_op jit(solution)/shard_map/ppermute | solution.py:370
  65.7 14.5 %collective-permute-start.19 = (bf16[512,128]{1,0:T(8,128)(2,1)S(1)}, bf16[512,128]{1,0:T(8,128)(2,1)S(1)}, u32[]{:S(2)}, u32[]{:S(2)}) collective-permute-start(bf16[512,128]{1,0:T(8,128)(2,1)S(1)} %get-tuple-element.141), channel_id=1, source_target_pairs={{0,4},{1,3},{2,6},{3,1},{4,0},{5,7},{6,2},{7,5},{8,12},{9,11},{10,... | collective-permute-start | bytes 393224 | tf_op jit(solution)/shard_map/ppermute | solution.py:383
  68.5 11.7 %collective-permute-start.20 = (bf16[512,128]{1,0:T(8,128)(2,1)S(1)}, bf16[512,128]{1,0:T(8,128)(2,1)S(1)}, u32[]{:S(2)}, u32[]{:S(2)}) collective-permute-start(bf16[512,128]{1,0:T(8,128)(2,1)S(1)} %get-tuple-element.143), channel_id=1, source_target_pairs={{0,4},{1,3},{2,6},{3,1},{4,0},{5,7},{6,2},{7,5},{8,12},{9,11},{10,... | collective-permute-start | bytes 393224 | tf_op jit(solution)/shard_map/ppermute | solution.py:383
  71.6 5.2 %collective-permute-start.18 = (bf16[256,128]{1,0:T(8,128)(2,1)S(1)}, bf16[256,128]{1,0:T(8,128)(2,1)S(1)}, u32[]{:S(2)}, u32[]{:S(2)}) collective-permute-start(bf16[256,128]{1,0:T(8,128)(2,1)S(1)} %get-tuple-element.140), channel_id=1, source_target_pairs={{0,8},{1,9},{2,10},{3,11},{4,12},{5,13},{6,14},{7,15},{8,0},{9,1},... | collective-permute-start | bytes 196616 | tf_op jit(solution)/shard_map/ppermute | solution.py:383
  76.8 7.1 %collective-permute-start.21 = (bf16[256,128]{1,0:T(8,128)(2,1)S(1)}, bf16[256,128]{1,0:T(8,128)(2,1)S(1)}, u32[]{:S(2)}, u32[]{:S(2)}) collective-permute-start(bf16[256,128]{1,0:T(8,128)(2,1)S(1)} %sum_2_2.1.refs_0_.refs_1_), channel_id=1, source_target_pairs={{0,8},{1,9},{2,10},{3,11},{4,12},{5,13},{6,14},{7,15},{8,0},{9,1},... | collective-permute-start | bytes 196616 | tf_op jit(solution)/shard_map/ppermute | solution.py:383
  83.9 8.4 %collective-permute-start.24 = (bf16[512,128]{1,0:T(8,128)(2,1)S(1)}, bf16[512,128]{1,0:T(8,128)(2,1)S(1)}, u32[]{:S(2)}, u32[]{:S(2)}) collective-permute-start(bf16[512,128]{1,0:T(8,128)(2,1)S(1)} %sum_2_3.1.refs_0_.refs_1_), channel_id=1, source_target_pairs={{0,4},{1,3},{2,6},{3,1},{4,0},{5,7},{6,2},{7,5},{8,12},{9,11},{10,... | collective-permute-start | bytes 393224 | tf_op jit(solution)/shard_map/ppermute | solution.py:383
  84.0 5.3 %collective-permute-start.22 = (bf16[256,128]{1,0:T(8,128)(2,1)S(1)}, bf16[256,128]{1,0:T(8,128)(2,1)S(1)}, u32[]{:S(2)}, u32[]{:S(2)}) collective-permute-start(bf16[256,128]{1,0:T(8,128)(2,1)S(1)} %get-tuple-element.145), channel_id=1, source_target_pairs={{0,8},{1,9},{2,10},{3,11},{4,12},{5,13},{6,14},{7,15},{8,0},{9,1},... | collective-permute-start | bytes 196616 | tf_op jit(solution)/shard_map/ppermute | solution.py:383
  85.8 6.0 %collective-permute-start.23 = (bf16[256,128]{1,0:T(8,128)(2,1)S(1)}, bf16[256,128]{1,0:T(8,128)(2,1)S(1)}, u32[]{:S(2)}, u32[]{:S(2)}) collective-permute-start(bf16[256,128]{1,0:T(8,128)(2,1)S(1)} %get-tuple-element.146), channel_id=1, source_target_pairs={{0,8},{1,9},{2,10},{3,11},{4,12},{5,13},{6,14},{7,15},{8,0},{9,1},... | collective-permute-start | bytes 196616 | tf_op jit(solution)/shard_map/ppermute | solution.py:383
  92.3 13.1 %collective-permute-start.27 = (bf16[1024,128]{1,0:T(8,128)(2,1)S(1)}, bf16[1024,128]{1,0:T(8,128)(2,1)S(1)}, u32[]{:S(2)}, u32[]{:S(2)}) collective-permute-start(bf16[1024,128]{1,0:T(8,128)(2,1)S(1)} %sum_2_4.1.refs_0_.refs_1_), channel_id=1, source_target_pairs={{0,2},{1,5},{2,0},{3,7},{4,6},{5,1},{6,4},{7,3},{8,10},{9,13},{10,... | collective-permute-start | bytes 786440 | tf_op jit(solution)/shard_map/ppermute | solution.py:383
  95.2 5.2 %collective-permute-start.25 = (bf16[256,128]{1,0:T(8,128)(2,1)S(1)}, bf16[256,128]{1,0:T(8,128)(2,1)S(1)}, u32[]{:S(2)}, u32[]{:S(2)}) collective-permute-start(bf16[256,128]{1,0:T(8,128)(2,1)S(1)} %sum_1_2.1.refs_0_.refs_1_), channel_id=1, source_target_pairs={{0,8},{1,9},{2,10},{3,11},{4,12},{5,13},{6,14},{7,15},{8,0},{9,1},... | collective-permute-start | bytes 196616 | tf_op jit(solution)/shard_map/ppermute | solution.py:383
  95.9 6.1 %collective-permute-start.26 = (bf16[256,128]{1,0:T(8,128)(2,1)S(1)}, bf16[256,128]{1,0:T(8,128)(2,1)S(1)}, u32[]{:S(2)}, u32[]{:S(2)}) collective-permute-start(bf16[256,128]{1,0:T(8,128)(2,1)S(1)} %sum_0_2.1.refs_0_.refs_1_), channel_id=1, source_target_pairs={{0,8},{1,9},{2,10},{3,11},{4,12},{5,13},{6,14},{7,15},{8,0},{9,1},... | collective-permute-start | bytes 196616 | tf_op jit(solution)/shard_map/ppermute | solution.py:383
  100.4 6.5 %collective-permute-start.28 = (bf16[512,128]{1,0:T(8,128)(2,1)S(1)}, bf16[512,128]{1,0:T(8,128)(2,1)S(1)}, u32[]{:S(2)}, u32[]{:S(2)}) collective-permute-start(bf16[512,128]{1,0:T(8,128)(2,1)S(1)} %sum_1_3.1.refs_0_.refs_1_), channel_id=1, source_target_pairs={{0,4},{1,3},{2,6},{3,1},{4,0},{5,7},{6,2},{7,5},{8,12},{9,11},{10,... | collective-permute-start | bytes 393224 | tf_op jit(solution)/shard_map/ppermute | solution.py:383
  102.1 7.6 %collective-permute-start.29 = (bf16[512,128]{1,0:T(8,128)(2,1)S(1)}, bf16[512,128]{1,0:T(8,128)(2,1)S(1)}, u32[]{:S(2)}, u32[]{:S(2)}) collective-permute-start(bf16[512,128]{1,0:T(8,128)(2,1)S(1)} %sum_0_3.1.refs_0_.refs_1_), channel_id=1, source_target_pairs={{0,4},{1,3},{2,6},{3,1},{4,0},{5,7},{6,2},{7,5},{8,12},{9,11},{10,... | collective-permute-start | bytes 393224 | tf_op jit(solution)/shard_map/ppermute | solution.py:383
  106.9 6.4 %collective-permute-start.30 = (bf16[1024,128]{1,0:T(8,128)(2,1)S(1)}, bf16[1024,128]{1,0:T(8,128)(2,1)S(1)}, u32[]{:S(2)}, u32[]{:S(2)}) collective-permute-start(bf16[1024,128]{1,0:T(8,128)(2,1)S(1)} %sum_1_4.1.refs_0_.refs_3_), channel_id=1, source_target_pairs={{0,2},{1,5},{2,0},{3,7},{4,6},{5,1},{6,4},{7,3},{8,10},{9,13},{10,... | collective-permute-start | bytes 786440 | tf_op jit(solution)/shard_map/ppermute | solution.py:383
  109.7 6.4 %collective-permute-start.31 = (bf16[1024,128]{1,0:T(8,128)(2,1)S(1)}, bf16[1024,128]{1,0:T(8,128)(2,1)S(1)}, u32[]{:S(2)}, u32[]{:S(2)}) collective-permute-start(bf16[1024,128]{1,0:T(8,128)(2,1)S(1)} %sum_0_4.1.refs_2_.refs_3_), channel_id=1, source_target_pairs={{0,2},{1,5},{2,0},{3,7},{4,6},{5,1},{6,4},{7,3},{8,10},{9,13},{10,... | collective-permute-start | bytes 786440 | tf_op jit(solution)/shard_map/ppermute | solution.py:383
  (9 other events, 14.5 us)

commit v6 on v5

--- a/solution.py
+++ b/solution.py
@@ -27,7 +27,7 @@
 LIMIT = 24 * 1024 * 1024
 
 
-def call(body, outs, ins, flops, scratch=(), name=None, after=()):
+def call(body, outs, ins, flops, scratch=(), name=None, after=(), bytes_accessed=4_000_000):
     skipped = len(after)
     return pl.pallas_call(
         lambda *refs: body(*refs[skipped:]),
@@ -36,7 +36,9 @@
         out_specs=[VMEM] * len(outs),
         scratch_shapes=list(scratch),
         compiler_params=pltpu.CompilerParams(vmem_limit_bytes=LIMIT),
-        cost_estimate=pl.CostEstimate(flops=flops, bytes_accessed=4_000_000, transcendentals=0),
+        cost_estimate=pl.CostEstimate(
+            flops=flops, bytes_accessed=bytes_accessed, transcendentals=0
+        ),
         name=name,
     )(*after, *ins)
 
@@ -232,8 +234,8 @@
     dround, inputs, local_t = refs[:3]
     wi0, wi1, wo0, wo1 = refs[3:7]
     far_x, far_dmsg, far_act, far_dpre = refs[7:11]
-    back, keep, send = refs[11:14]
-    grads, dmsg, act, dpre = refs[14:]
+    back = refs[11]
+    grads, dmsg, act, dpre = refs[-4:]
     halves = [(wi0[layer], wo0[layer]), (wi1[layer], wo1[layer])]
     dmsg[...] = mm(local_t[...], dround[...]).astype(BF16)
     for r in range(0, inputs.shape[0], 256):
@@ -249,7 +251,7 @@
     for j in range(latent // LANES):
         at = hidden // LANES * latent + j * hidden
         grads[at : at + hidden, :] = g_out[:, j * LANES : (j + 1) * LANES]
-    split(grads, stage, (keep, send))
+    split(grads, stage, refs[12:14])
 
 
 def upper(stage):
@@ -273,6 +275,11 @@
     split(acc, stage, refs[:-1])
 
 
+def add_all_kernel(keep, got, own, send):
+    own[...] = keep[...] + got[...].astype(F32)
+    send[...] = own[...].astype(BF16)
+
+
 def add_kernel(keep, got, out):
     out[...] = (keep[...] + got[...].astype(F32)).astype(BF16)
 
@@ -289,10 +296,9 @@
 
 
 def write_kernel(layer, stage, kept, *refs):
-    own, got = refs[kept : kept + 2]
-    out_in, out_out, token, grads, slab_in, slab_out, sem = refs[kept + 2 :]
+    out_in, out_out, token, grads, slab_in, slab_out, sem = refs[-7:]
     token[...] = jnp.zeros_like(token)
-    place(stage, own, got, grads)
+    place(stage, refs[kept], refs[kept + 1], grads)
     latent, hidden = slab_in.shape
     for j in range(hidden // LANES):
         slab_in[:, j * LANES : (j + 1) * LANES] = grads[j * latent : (j + 1) * latent, :]
@@ -318,29 +324,31 @@
         n = len(self.stages)
         i = self.done
         self.done += 1
-        name = f"sum_{self.name}_{i}"
-        if i < n - 1:
-            half = (self.keep.shape[0] // 2, LANES)
-            self.keep, send = call(
-                functools.partial(add_split_kernel, self.stages[i + 1]),
-                [(half, F32), (half, BF16)],
-                [self.keep, self.got],
-                1_000_000,
-                scratch=[pltpu.VMEM(self.keep.shape, F32)],
-                name=name,
-                after=after,
-            )
-            self.got = swapped(send, self.stages[i + 1])
+        rows = self.keep.shape[0]
+        scratch = []
+        if i < n - 2:
+            body = functools.partial(add_split_kernel, self.stages[i + 1])
+            outs = [((rows // 2, LANES), F32), ((rows // 2, LANES), BF16)]
+            scratch = [pltpu.VMEM(self.keep.shape, F32)]
+        elif i == n - 2:
+            body, outs = add_all_kernel, [((rows, LANES), F32), ((rows, LANES), BF16)]
+        elif i == n - 1:
+            body, outs = add_kernel, [((rows, LANES), BF16)]
         else:
-            if i == n - 1:
-                body, shape = add_kernel, self.keep.shape
-            else:
-                body = functools.partial(place_kernel, self.stages[2 * n - 1 - i])
-                shape = (self.keep.shape[0] * 2, LANES)
-            (self.keep,) = call(
-                body, [(shape, BF16)], [self.keep, self.got], 1_000_000, name=name, after=after
-            )
-            self.got = swapped(self.keep, self.stages[2 * n - 2 - i])
+            body = functools.partial(place_kernel, self.stages[2 * n - 2 - i])
+            outs = [((rows * 2, LANES), BF16)]
+        self.keep, *send = call(
+            body,
+            outs,
+            [self.keep, self.got],
+            1,
+            scratch=scratch,
+            bytes_accessed=1,
+            name=f"sum_{self.name}_{i}",
+            after=after,
+        )
+        to = i + 1 if i < n - 1 else 2 * n - 3 - i
+        self.got = swapped(send[0] if send else self.keep, self.stages[to])
         return [self.keep]
 
 
@@ -511,10 +519,10 @@
 
     def back(layer, outs, after):
         returned[layer] = backward(outs[6:])
+        parts = [((grad_rows // 2, LANES), F32), ((grad_rows // 2, LANES), BF16)]
         grad, *parts = call(
             functools.partial(back_kernel, layer, grad_scale, stages[0]),
-            [((rows, latent), F32), ((grad_rows // 2, LANES), F32)]
-            + [((grad_rows // 2, LANES), BF16)],
+            [((rows, latent), F32), *parts],
             [outs[1], inputs[layer], local_t, *weights, *outs[2:6]],
             3 * rows * ffn + 2 * rows * rows * latent,
             scratch=[
@@ -569,11 +577,11 @@
             ],
             input_output_aliases={i: i for i in range(len(written))},
             compiler_params=pltpu.CompilerParams(vmem_limit_bytes=LIMIT),
-            cost_estimate=pl.CostEstimate(flops=0, bytes_accessed=4_000_000, transcendentals=0),
+            cost_estimate=pl.CostEstimate(flops=1, bytes_accessed=1, transcendentals=0),
             name=f"write{layer}",
         )(*written, *after, *ready)
 
-    count = 2 * len(stages) - 1
+    count = 2 * len(stages) - 2
     at = []
     for layer in reversed(range(layers)):
         state, at = back(layer, outs, at)
@@ -582,6 +590,10 @@
                 at = sums[above].step(at)
             outs = join(layer, state, at)
             at = outs[1:2]
+    for layer in reversed(range(1, last)):
+        at = sums[layer].step(at)
+    grad, token = join(0, state, at)
+    at = sums[0].step([token])
     written = []
     waiting = list(reversed(range(layers)))
     while waiting:
@@ -592,9 +604,6 @@
                 *written, token = write(layer, written, at)
                 at = [token]
                 waiting.remove(layer)
-            if layer == 1 and sums[layer].done == 1:
-                grad, token = join(0, state, at)
-                at = [token]
     return (grad, *written)
 
 

time: 119 us -> 105 us (0.88)
  waiting for transfers between devices: 27.8 us -> 19.7 us
  starting transfers between devices: 50.8 us -> 45.6 us
    ppermute x21 -> x18, waiting for transfers between devices: 25.3 us -> 16.6 us  [over_mesh(): return lax.ppermute(x, ('chain', 'basin', 'feat'), perm)]
    ppermute x21 -> x18, starting transfers between devices: 42.1 us -> 36.8 us  [over_mesh(): return lax.ppermute(x, ('chain', 'basin', 'feat'), perm)]
    pallas_call x31 -> x28, Pallas kernels: 27.4 us -> 27.3 us  [call(): pl.pallas_call(lambda *refs: body(*refs[skipped:]), out_shape=[jax.ShapeD...]
  transfers between devices with their start and end apart: 32 -> 29, of which waited for: 18 -> 15; matrix products, arithmetic and copies ran while one was open for 1% -> 1% of each run, Pallas kernels for 22% -> 24%
where the time goes in v6:
time: 105 us
  starting transfers between devices  45.6 us (43%)
  Pallas kernels  31.3 us (30%)
  waiting for transfers between devices  19.7 us (19%)
  local copies, waits for them, and re-layouts  6.18 us (6%)
  between operations  1.11 us (1%)
    ppermute x18, starting transfers between devices, over_mesh(): return lax.ppermute(x, ('chain', 'basin', 'feat'), perm)  36.8 us
    pallas_call x28, Pallas kernels, call(): pl.pallas_call(lambda *refs: body(*refs[skipped:]), out_shape=[jax.ShapeD...  27.3 us
    ppermute x18, waiting for transfers between devices, over_mesh(): return lax.ppermute(x, ('chain', 'basin', 'feat'), perm)  16.6 us
    unnamed x19, local copies, waits for them, and re-layouts  6.18 us
    ppermute x8, starting transfers between devices, around(): return lax.ppermute(x, axis, [(i, (i + distance) % n) for i in range(n)])  4.83 us
    ppermute x3, starting transfers between devices, backward(): up = lax.ppermute(grads[0], 'chain', [(c, c - 1) for c in range(1, chain)])  4.04 us
    pallas_call x3, Pallas kernels, write(): pl.pallas_call(functools.partial(write_kernel, layer, stages[0], len(kept...  4 us
    ppermute x3, waiting for transfers between devices, backward(): up = lax.ppermute(grads[0], 'chain', [(c, c - 1) for c in range(1, chain)])  2.31 us
  transfers between devices with their start and end apart: 29, of which 15 were waited for; matrix products, arithmetic and copies ran while one was open for 1% of the time, Pallas kernels for 24%

profile of v6, /device:TPU:0, one launch (start us, length us, event | category | flops | bytes accessed | tf_op | source)
XLA Modules:
  0.0 104.7 jit_solution(9368275111155600889)
XLA Ops:
  3.6 4.9 %collective-permute-start.2 = (bf16[128,256]{1,0:T(8,128)(2,1)S(1)}, bf16[128,256]{1,0:T(8,128)(2,1)S(1)}, u32[]{:S(2)}, u32[]{:S(2)}) collective-permute-start(bf16[128,256]{1,0:T(8,128)(2,1)S(1)} %get-tuple-element.81), channel_id=1, source_target_pairs={{0,4},{1,3},{2,6},{3,1},{4,8},{5,7},{6,10},{7,5},{8,12},{9,11},{10... | collective-permute-start | bytes 196616 | tf_op jit(solution)/shard_map/ppermute | solution.py:391
  13.7 2.7 %first.1 = (bf16[768,256]{1,0:T(8,128)(2,1)S(1)}, bf16[768,768]{1,0:T(8,128)(2,1)S(1)}, bf16[768,768]{1,0:T(8,128)(2,1)S(1)}, bf16[768,256]{1,0:T(8,128)(2,1)S(1)}, bf16[256,768]{1,0:T(8,128)(2,1)S(1)}) custom-call(bf16[768,256]{1,0:T(8,128)(2,1)S(1)} %copy-done.5, bf16[128,768]{1,0:T(8,128)(2,1)S(1)} %get-tuple-element.79.refs_1_, ...), custom_call_target="tpu_custom_call" | custom-call | flops 956301312 | bytes 4000000 | tf_op jit(solution)/shard_map/first/pallas_call | solution.py:32
  18.8 3.5 %collective-permute-start.4 = (bf16[128,256]{1,0:T(8,128)(2,1)S(1)}, bf16[128,256]{1,0:T(8,128)(2,1)S(1)}, u32[]{:S(2)}, u32[]{:S(2)}) collective-permute-start(bf16[128,256]{1,0:T(8,128)(2,1)S(1)} %get-tuple-element.88), channel_id=1, source_target_pairs={{0,4},{1,3},{2,6},{3,1},{4,8},{5,7},{6,10},{7,5},{8,12},{9,11},{10... | collective-permute-start | bytes 196616 | tf_op jit(solution)/shard_map/ppermute | solution.py:391
  22.3 1.2 %local1.1.refs_1_ = bf16[768,256]{1,0:T(8,128)(2,1)S(1)} custom-call(bf16[768,256]{1,0:T(8,128)(2,1)S(1)} %get-tuple-element.89.refs_0_.refs_2_, bf16[3,256,512]{2,1,0:T(8,128)(2,1)S(1)} %copy-done.1, bf16[3,256,512]{2,1,0:T(8,128)(2,1)S(1)} %collective-permute-done.refs_5_.refs_4_.refs_2_.refs_6_.refs_7_, bf16[3,512,256]{2,1,0:T(8,128)(2,1)S(1)} %copy-done.3, ...), custom_call_target="tpu_custom_call" | custom-call | flops 805306368 | bytes 4000000 | tf_op jit(solution)/shard_map/local1/pallas_call | solution.py:32
  26.5 4.3 %collective-permute-start.6 = (bf16[128,256]{1,0:T(8,128)(2,1)S(1)}, bf16[128,256]{1,0:T(8,128)(2,1)S(1)}, u32[]{:S(2)}, u32[]{:S(2)}) collective-permute-start(bf16[128,256]{1,0:T(8,128)(2,1)S(1)} %get-tuple-element.93), channel_id=1, source_target_pairs={{0,4},{1,3},{2,6},{3,1},{4,8},{5,7},{6,10},{7,5},{8,12},{9,11},{10... | collective-permute-start | bytes 196616 | tf_op jit(solution)/shard_map/ppermute | solution.py:391
  30.8 1.2 %local2.1.refs_1_ = bf16[768,256]{1,0:T(8,128)(2,1)S(1)} custom-call(bf16[768,256]{1,0:T(8,128)(2,1)S(1)} %get-tuple-element.94.refs_0_.refs_1_, bf16[3,256,512]{2,1,0:T(8,128)(2,1)S(1)} %copy-done.1, bf16[3,256,512]{2,1,0:T(8,128)(2,1)S(1)} %collective-permute-done.refs_5_.refs_4_.refs_2_.refs_6_.refs_7_, bf16[3,512,256]{2,1,0:T(8,128)(2,1)S(1)} %copy-done.3, ...), custom_call_target="tpu_custom_call" | custom-call | flops 805306368 | bytes 4000000 | tf_op jit(solution)/shard_map/local2/pallas_call | solution.py:32
  33.9 2.1 %turn.1 = (f32[768,256]{1,0:T(8,128)S(1)}, bf16[768,256]{1,0:T(8,128)(2,1)S(1)}, bf16[256,256]{1,0:T(8,128)(2,1)S(1)}, bf16[256,256]{1,0:T(8,128)(2,1)S(1)}, bf1...) custom-call(f32[768,256]{1,0:T(8,128)S(1)} %get-tuple-element.92.ref, ...), custom_call_target="tpu_custom_call" | custom-call | flops 536870912 | bytes 4000000 | tf_op jit(solution)/shard_map/turn/pallas_call | solution.py:32
  36.0 1.5 %collective-permute-start.8 = (bf16[128,256]{1,0:T(8,128)(2,1)S(1)}, bf16[128,256]{1,0:T(8,128)(2,1)S(1)}, u32[]{:S(2)}, u32[]{:S(2)}) collective-permute-start(bf16[128,256]{1,0:T(8,128)(2,1)S(1)} %get-tuple-element.108), channel_id=1, source_target_pairs={{4,0},{8,4},{12,8},{5,1},{9,5},{13,9},{6,2},{10,6},{14,10},{7,3},{... | collective-permute-start | bytes 196616 | tf_op jit(solution)/shard_map/ppermute | solution.py:415
  37.5 1.5 %collective-permute-start.9 = (bf16[128,256]{1,0:T(8,128)(2,1)S(1)}, bf16[128,256]{1,0:T(8,128)(2,1)S(1)}, u32[]{:S(2)}, u32[]{:S(2)}) collective-permute-start(bf16[128,256]{1,0:T(8,128)(2,1)S(1)} %get-tuple-element.109), channel_id=1, source_target_pairs={{0,2},{2,0},{1,3},{3,1},{4,6},{6,4},{5,7},{7,5},{8,10},{10,8},{9,1... | collective-permute-start | bytes 196616 | tf_op jit(solution)/shard_map/ppermute | solution.py:378
  39.0 3.2 %back2.1 = (f32[768,256]{1,0:T(8,128)S(1)}, f32[1024,128]{1,0:T(8,128)S(1)}, bf16[1024,128]{1,0:T(8,128)(2,1)S(1)}) custom-call(bf16[768,256]{1,0:T(8,128)(2,1)S(1)} %get-tuple-element.98.refs_0_, bf16[768,256]{1,0:T(8,128)(2,1)S(1)} %get-tuple-element.94.refs_0_.refs_1_, bf16[768,768]{1,0:T(8,128)(2,1)S(1)} %get-tuple-element.99.refs_2_.refs_3_, ...), custom_call_target="tpu_custom_call" | custom-call | flops 2717908992 | bytes 4000000 | tf_op jit(solution)/shard_map/back2/pallas_call | solution.py:32
  42.8 1.6 %join2.1 = (f32[768,256]{1,0:T(8,128)S(1)}, bf16[768,256]{1,0:T(8,128)(2,1)S(1)}, bf16[256,256]{1,0:T(8,128)(2,1)S(1)}, bf16[256,256]{1,0:T(8,128)(2,1)S(1)}, bf...) custom-call(f32[1024,128]{1,0:T(8,128)S(1)} %get-tuple-element.104.r, ...), custom_call_target="tpu_custom_call" | custom-call | flops 536870912 | bytes 4000000 | tf_op jit(solution)/shard_map/join2/pallas_call | solution.py:32
  44.4 1.3 %collective-permute-start.11 = (bf16[128,256]{1,0:T(8,128)(2,1)S(1)}, bf16[128,256]{1,0:T(8,128)(2,1)S(1)}, u32[]{:S(2)}, u32[]{:S(2)}) collective-permute-start(bf16[128,256]{1,0:T(8,128)(2,1)S(1)} %get-tuple-element.120), channel_id=1, source_target_pairs={{4,0},{8,4},{12,8},{5,1},{9,5},{13,9},{6,2},{10,6},{14,10},{7,3},{... | collective-permute-start | bytes 196616 | tf_op jit(solution)/shard_map/ppermute | solution.py:415
  45.7 1.5 %collective-permute-start.12 = (bf16[128,256]{1,0:T(8,128)(2,1)S(1)}, bf16[128,256]{1,0:T(8,128)(2,1)S(1)}, u32[]{:S(2)}, u32[]{:S(2)}) collective-permute-start(bf16[128,256]{1,0:T(8,128)(2,1)S(1)} %get-tuple-element.121), channel_id=1, source_target_pairs={{0,2},{2,0},{1,3},{3,1},{4,6},{6,4},{5,7},{7,5},{8,10},{10,8},{9,1... | collective-permute-start | bytes 196616 | tf_op jit(solution)/shard_map/ppermute | solution.py:378
  47.2 3.2 %back1.1 = (f32[768,256]{1,0:T(8,128)S(1)}, f32[1024,128]{1,0:T(8,128)S(1)}, bf16[1024,128]{1,0:T(8,128)(2,1)S(1)}) custom-call(bf16[768,256]{1,0:T(8,128)(2,1)S(1)} %get-tuple-element.110.refs_0_.refs_1_, bf16[768,256]{1,0:T(8,128)(2,1)S(1)} %get-tuple-element.110.refs_0_.refs_1_, bf16[768,256]{1,0:T(8,128)(2,1)S(1)} %get-tuple-element.89.refs_0_.refs_2_, ...), custom_call_target="tpu_custom_call" | custom-call | flops 2717908992 | bytes 4000000 | tf_op jit(solution)/shard_map/back1/pallas_call | solution.py:32
  52.0 1.6 %join1.1 = (f32[768,256]{1,0:T(8,128)S(1)}, bf16[768,256]{1,0:T(8,128)(2,1)S(1)}, bf16[256,256]{1,0:T(8,128)(2,1)S(1)}, bf16[256,256]{1,0:T(8,128)(2,1)S(1)}, bf...) custom-call(f32[512,128]{1,0:T(8,128)S(1)} %get-tuple-element.117.re, ...), custom_call_target="tpu_custom_call" | custom-call | flops 536870912 | bytes 4000000 | tf_op jit(solution)/shard_map/join1/pallas_call | solution.py:32
  53.6 3.2 %back0.1 = (f32[768,256]{1,0:T(8,128)S(1)}, f32[1024,128]{1,0:T(8,128)S(1)}, bf16[1024,128]{1,0:T(8,128)(2,1)S(1)}) custom-call(bf16[768,256]{1,0:T(8,128)(2,1)S(1)} %get-tuple-element.122.refs_0_.refs_1_, bf16[768,256]{1,0:T(8,128)(2,1)S(1)} %get-tuple-element.122.refs_0_.refs_1_, bf16[768,256]{1,0:T(8,128)(2,1)S(1)} %copy-done.6, ...), custom_call_target="tpu_custom_call" | custom-call | flops 2717908992 | bytes 4000000 | tf_op jit(solution)/shard_map/back0/pallas_call | solution.py:32
  57.9 1.3 %collective-permute-start.14 = (bf16[128,256]{1,0:T(8,128)(2,1)S(1)}, bf16[128,256]{1,0:T(8,128)(2,1)S(1)}, u32[]{:S(2)}, u32[]{:S(2)}) collective-permute-start(bf16[128,256]{1,0:T(8,128)(2,1)S(1)} %get-tuple-element.132), channel_id=1, source_target_pairs={{4,0},{8,4},{12,8},{5,1},{9,5},{13,9},{6,2},{10,6},{14,10},{7,3},{... | collective-permute-start | bytes 196616 | tf_op jit(solution)/shard_map/ppermute | solution.py:415
  60.2 3.4 %collective-permute-start.17 = (bf16[512,128]{1,0:T(8,128)(2,1)S(1)}, bf16[512,128]{1,0:T(8,128)(2,1)S(1)}, u32[]{:S(2)}, u32[]{:S(2)}) collective-permute-start(bf16[512,128]{1,0:T(8,128)(2,1)S(1)} %get-tuple-element.138), channel_id=1, source_target_pairs={{0,4},{1,3},{2,6},{3,1},{4,0},{5,7},{6,2},{7,5},{8,12},{9,11},{10,... | collective-permute-start | bytes 393224 | tf_op jit(solution)/shard_map/ppermute | solution.py:391
  63.8 1.5 %collective-permute-done.14.refs_4_ = bf16[128,256]{1,0:T(8,128)(2,1)S(1)} collective-permute-done((bf16[128,256]{1,0:T(8,128)(2,1)S(1)}, bf16[128,256]{1,0:T(8,128)(2,1)S(1)}, u32[]{:S(2)}, u32[]{:S(2)}) %collective-permute-start.14) | collective-permute-done | bytes 65568 | tf_op jit(solution)/shard_map/ppermute | solution.py:415
  65.3 1.1 %join0.1 = (f32[768,256]{1,0:T(8,128)}, f32[8,128]{1,0:T(8,128)S(1)}) custom-call(f32[512,128]{1,0:T(8,128)S(1)} %get-tuple-element.129.refs_0_.refs_1_, f32[768,256]{1,0:T(8,128)S(1)} %get-tuple-element.130.refs_1_, f32[768,256]{1,0:T(8,128)S(1)} %get-tuple-element.131.refs_2_, bf16[768,256]{1,0:T(8,128)(2,1)S(1)} %get-tuple-element.107.refs_3_, ...), custom_call_target="tpu_custom_call" | custom-call | flops 100663296 | bytes 4000000 | tf_op jit(solution)/shard_map/join0/pallas_call | solution.py:32
  66.6 2.9 %collective-permute-start.19 = (bf16[512,128]{1,0:T(8,128)(2,1)S(1)}, bf16[512,128]{1,0:T(8,128)(2,1)S(1)}, u32[]{:S(2)}, u32[]{:S(2)}) collective-permute-start(bf16[512,128]{1,0:T(8,128)(2,1)S(1)} %get-tuple-element.142), channel_id=1, source_target_pairs={{0,4},{1,3},{2,6},{3,1},{4,0},{5,7},{6,2},{7,5},{8,12},{9,11},{10,... | collective-permute-start | bytes 393224 | tf_op jit(solution)/shard_map/ppermute | solution.py:391
  69.5 4.7 %collective-permute-start.20 = (bf16[512,128]{1,0:T(8,128)(2,1)S(1)}, bf16[512,128]{1,0:T(8,128)(2,1)S(1)}, u32[]{:S(2)}, u32[]{:S(2)}) collective-permute-start(bf16[512,128]{1,0:T(8,128)(2,1)S(1)} %get-tuple-element.144), channel_id=1, source_target_pairs={{0,8},{1,9},{2,10},{3,11},{4,12},{5,13},{6,14},{7,15},{8,0},{9,1},... | collective-permute-start | bytes 393224 | tf_op jit(solution)/shard_map/ppermute | solution.py:391
  74.4 4.2 %collective-permute-start.22 = (bf16[512,128]{1,0:T(8,128)(2,1)S(1)}, bf16[512,128]{1,0:T(8,128)(2,1)S(1)}, u32[]{:S(2)}, u32[]{:S(2)}) collective-permute-start(bf16[512,128]{1,0:T(8,128)(2,1)S(1)} %get-tuple-element.146), channel_id=1, source_target_pairs={{0,8},{1,9},{2,10},{3,11},{4,12},{5,13},{6,14},{7,15},{8,0},{9,1},... | collective-permute-start | bytes 393224 | tf_op jit(solution)/shard_map/ppermute | solution.py:391
  78.5 6.5 %collective-permute-done.20.refs_2_ = bf16[512,128]{1,0:T(8,128)(2,1)S(1)} collective-permute-done((bf16[512,128]{1,0:T(8,128)(2,1)S(1)}, bf16[512,128]{1,0:T(8,128)(2,1)S(1)}, u32[]{:S(2)}, u32[]{:S(2)}) %collective-permute-start.20) | collective-permute-done | bytes 131104 | tf_op jit(solution)/shard_map/ppermute | solution.py:391
  85.1 1.9 %collective-permute-done.21.refs_2_ = bf16[512,128]{1,0:T(8,128)(2,1)S(1)} collective-permute-done((bf16[512,128]{1,0:T(8,128)(2,1)S(1)}, bf16[512,128]{1,0:T(8,128)(2,1)S(1)}, u32[]{:S(2)}, u32[]{:S(2)}) %collective-permute-start.21) | collective-permute-done | bytes 131104 | tf_op jit(solution)/shard_map/ppermute | solution.py:391
  90.3 2.0 %collective-permute-start.26 = (bf16[1024,128]{1,0:T(8,128)(2,1)S(1)}, bf16[1024,128]{1,0:T(8,128)(2,1)S(1)}, u32[]{:S(2)}, u32[]{:S(2)}) collective-permute-start(bf16[1024,128]{1,0:T(8,128)(2,1)S(1)} %sum_2_3.1.refs_0_.refs_1_), channel_id=1, source_target_pairs={{0,2},{1,5},{2,0},{3,7},{4,6},{5,1},{6,4},{7,3},{8,10},{9,13},{10,... | collective-permute-start | bytes 786440 | tf_op jit(solution)/shard_map/ppermute | solution.py:391
  92.3 1.2 %collective-permute-done.24.refs_2_ = bf16[512,128]{1,0:T(8,128)(2,1)S(1)} collective-permute-done((bf16[512,128]{1,0:T(8,128)(2,1)S(1)}, bf16[512,128]{1,0:T(8,128)(2,1)S(1)}, u32[]{:S(2)}, u32[]{:S(2)}) %collective-permute-start.24) | collective-permute-done | bytes 131104 | tf_op jit(solution)/shard_map/ppermute | solution.py:391
  93.5 1.5 %collective-permute-start.27 = (bf16[1024,128]{1,0:T(8,128)(2,1)S(1)}, bf16[1024,128]{1,0:T(8,128)(2,1)S(1)}, u32[]{:S(2)}, u32[]{:S(2)}) collective-permute-start(bf16[1024,128]{1,0:T(8,128)(2,1)S(1)} %sum_1_3.1.refs_0_.refs_3_), channel_id=1, source_target_pairs={{0,2},{1,5},{2,0},{3,7},{4,6},{5,1},{6,4},{7,3},{8,10},{9,13},{10,... | collective-permute-start | bytes 786440 | tf_op jit(solution)/shard_map/ppermute | solution.py:391
  95.1 1.2 %collective-permute-done.25.refs_2_ = bf16[512,128]{1,0:T(8,128)(2,1)S(1)} collective-permute-done((bf16[512,128]{1,0:T(8,128)(2,1)S(1)}, bf16[512,128]{1,0:T(8,128)(2,1)S(1)}, u32[]{:S(2)}, u32[]{:S(2)}) %collective-permute-start.25) | collective-permute-done | bytes 131104 | tf_op jit(solution)/shard_map/ppermute | solution.py:391
  96.4 1.5 %collective-permute-start.28 = (bf16[1024,128]{1,0:T(8,128)(2,1)S(1)}, bf16[1024,128]{1,0:T(8,128)(2,1)S(1)}, u32[]{:S(2)}, u32[]{:S(2)}) collective-permute-start(bf16[1024,128]{1,0:T(8,128)(2,1)S(1)} %sum_0_3.1.refs_0_.refs_3_), channel_id=1, source_target_pairs={{0,2},{1,5},{2,0},{3,7},{4,6},{5,1},{6,4},{7,3},{8,10},{9,13},{10,... | collective-permute-start | bytes 786440 | tf_op jit(solution)/shard_map/ppermute | solution.py:391
  101.1 1.7 %collective-permute-done.28.refs_4_ = bf16[1024,128]{1,0:T(8,128)(2,1)S(1)} collective-permute-done((bf16[1024,128]{1,0:T(8,128)(2,1)S(1)}, bf16[1024,128]{1,0:T(8,128)(2,1)S(1)}, u32[]{:S(2)}, u32[]{:S(2)}) %collective-permute-start.28) | collective-permute-done | bytes 262176 | tf_op jit(solution)/shard_map/ppermute | solution.py:391
  102.8 1.7 %write0.1 = (f32[3,256,512]{2,1,0:T(8,128)}, f32[3,512,256]{2,1,0:T(8,128)}, f32[8,128]{1,0:T(8,128)}) custom-call(f32[3,256,512]{2,1,0:T(8,128)} %get-tuple-element.150.refs_0_, f32[3,512,256]{2,1,0:T(8,128)} %get-tuple-element.151.refs_1_, f32[8,128]{1,0:T(8,128)S(1)} %get-tuple-element.152.refs_2_, ...), custom_call_target="tpu_custom_call", output_to_operand_aliasing={{0}: (0, {}), {1}: (1, {})} | custom-call | flops 1 | bytes 1 | tf_op jit(solution)/shard_map/write0/pallas_call | solution.py:563
  (77 shorter events, 26.7 us)
Async XLA Ops:
  0.6 8.6 %collective-permute-start = (bf16[3,256,512]{2,1,0:T(8,128)(2,1)}, bf16[3,256,512]{2,1,0:T(8,128)(2,1)S(1)}, u32[]{:S(2)}, u32[]{:S(2)}) collective-permute-start(bf16[3,256,512]{2,1,0:T(8,128)(2,1)} %refs_4_.11), channel_id=1, source_target_pairs={{0,1},{1,0},{2,3},{3,2},{4,5},{5,4},{6,7},{7,6},{8,9},{9,8},{10,11... | collective-permute-start | bytes 2359304 | tf_op jit(solution)/shard_map/ppermute | solution.py:378
  1.1 8.1 %collective-permute-start.1 = (bf16[3,512,256]{2,1,0:T(8,128)(2,1)}, bf16[3,512,256]{2,1,0:T(8,128)(2,1)S(1)}, u32[]{:S(2)}, u32[]{:S(2)}) collective-permute-start(bf16[3,512,256]{2,1,0:T(8,128)(2,1)} %refs_6_.13), channel_id=1, source_target_pairs={{0,1},{1,0},{2,3},{3,2},{4,5},{5,4},{6,7},{7,6},{8,9},{9,8},{10,11... | collective-permute-start | bytes 2359304 | tf_op jit(solution)/shard_map/ppermute | solution.py:378
  3.6 12.8 %collective-permute-start.2 = (bf16[128,256]{1,0:T(8,128)(2,1)S(1)}, bf16[128,256]{1,0:T(8,128)(2,1)S(1)}, u32[]{:S(2)}, u32[]{:S(2)}) collective-permute-start(bf16[128,256]{1,0:T(8,128)(2,1)S(1)} %get-tuple-element.81), channel_id=1, source_target_pairs={{0,4},{1,3},{2,6},{3,1},{4,8},{5,7},{6,10},{7,5},{8,12},{9,11},{10... | collective-permute-start | bytes 196616 | tf_op jit(solution)/shard_map/ppermute | solution.py:391
  13.7 2.8 %copy-start.1 = (bf16[3,256,512]{2,1,0:T(8,128)(2,1)S(1)}, bf16[3,256,512]{2,1,0:T(8,128)(2,1)}, u32[]{:S(2)}) copy-start(bf16[3,256,512]{2,1,0:T(8,128)(2,1)} %refs_4_.11) | copy-start | bytes 2359300
  13.7 2.8 %copy-start.3 = (bf16[3,512,256]{2,1,0:T(8,128)(2,1)S(1)}, bf16[3,512,256]{2,1,0:T(8,128)(2,1)}, u32[]{:S(2)}) copy-start(bf16[3,512,256]{2,1,0:T(8,128)(2,1)} %refs_6_.13) | copy-start | bytes 2359300
  16.4 1.3 %collective-permute-start.3 = (bf16[128,256]{1,0:T(8,128)(2,1)S(1)}, bf16[128,256]{1,0:T(8,128)(2,1)S(1)}, u32[]{:S(2)}, u32[]{:S(2)}) collective-permute-start(bf16[128,256]{1,0:T(8,128)(2,1)S(1)} %collective-permute-done.2.refs_7_.refs_12_), channel_id=1, source_target_pairs={{0,1},{1,0},{2,3},{3,2},{4,5},{5,4},{6,7},{7,6},{8,9},{9,8},{10,11... | collective-permute-start | bytes 196616 | tf_op jit(solution)/shard_map/ppermute | solution.py:378
  18.8 5.4 %collective-permute-start.4 = (bf16[128,256]{1,0:T(8,128)(2,1)S(1)}, bf16[128,256]{1,0:T(8,128)(2,1)S(1)}, u32[]{:S(2)}, u32[]{:S(2)}) collective-permute-start(bf16[128,256]{1,0:T(8,128)(2,1)S(1)} %get-tuple-element.88), channel_id=1, source_target_pairs={{0,4},{1,3},{2,6},{3,1},{4,8},{5,7},{6,10},{7,5},{8,12},{9,11},{10... | collective-permute-start | bytes 196616 | tf_op jit(solution)/shard_map/ppermute | solution.py:391
  24.2 1.3 %collective-permute-start.5 = (bf16[128,256]{1,0:T(8,128)(2,1)S(1)}, bf16[128,256]{1,0:T(8,128)(2,1)S(1)}, u32[]{:S(2)}, u32[]{:S(2)}) collective-permute-start(bf16[128,256]{1,0:T(8,128)(2,1)S(1)} %collective-permute-done.4.refs_7_.refs_12_), channel_id=1, source_target_pairs={{0,1},{1,0},{2,3},{3,2},{4,5},{5,4},{6,7},{7,6},{8,9},{9,8},{10,11... | collective-permute-start | bytes 196616 | tf_op jit(solution)/shard_map/ppermute | solution.py:378
  26.5 6.2 %collective-permute-start.6 = (bf16[128,256]{1,0:T(8,128)(2,1)S(1)}, bf16[128,256]{1,0:T(8,128)(2,1)S(1)}, u32[]{:S(2)}, u32[]{:S(2)}) collective-permute-start(bf16[128,256]{1,0:T(8,128)(2,1)S(1)} %get-tuple-element.93), channel_id=1, source_target_pairs={{0,4},{1,3},{2,6},{3,1},{4,8},{5,7},{6,10},{7,5},{8,12},{9,11},{10... | collective-permute-start | bytes 196616 | tf_op jit(solution)/shard_map/ppermute | solution.py:391
  32.0 1.9 %copy-start.8 = (f32[768,256]{1,0:T(8,128)S(1)}, f32[768,256]{1,0:T(8,128)}, u32[]{:S(2)}) copy-start(f32[768,256]{1,0:T(8,128)} %refs_4_.9) | copy-start | bytes 2359300
  32.7 1.3 %collective-permute-start.7 = (bf16[128,256]{1,0:T(8,128)(2,1)S(1)}, bf16[128,256]{1,0:T(8,128)(2,1)S(1)}, u32[]{:S(2)}, u32[]{:S(2)}) collective-permute-start(bf16[128,256]{1,0:T(8,128)(2,1)S(1)} %collective-permute-done.6.refs_7_.refs_9_), channel_id=1, source_target_pairs={{0,1},{1,0},{2,3},{3,2},{4,5},{5,4},{6,7},{7,6},{8,9},{9,8},{10,11... | collective-permute-start | bytes 196616 | tf_op jit(solution)/shard_map/ppermute | solution.py:378
  36.0 6.8 %collective-permute-start.8 = (bf16[128,256]{1,0:T(8,128)(2,1)S(1)}, bf16[128,256]{1,0:T(8,128)(2,1)S(1)}, u32[]{:S(2)}, u32[]{:S(2)}) collective-permute-start(bf16[128,256]{1,0:T(8,128)(2,1)S(1)} %get-tuple-element.108), channel_id=1, source_target_pairs={{4,0},{8,4},{12,8},{5,1},{9,5},{13,9},{6,2},{10,6},{14,10},{7,3},{... | collective-permute-start | bytes 196616 | tf_op jit(solution)/shard_map/ppermute | solution.py:415
  37.5 5.4 %collective-permute-start.9 = (bf16[128,256]{1,0:T(8,128)(2,1)S(1)}, bf16[128,256]{1,0:T(8,128)(2,1)S(1)}, u32[]{:S(2)}, u32[]{:S(2)}) collective-permute-start(bf16[128,256]{1,0:T(8,128)(2,1)S(1)} %get-tuple-element.109), channel_id=1, source_target_pairs={{0,2},{2,0},{1,3},{3,1},{4,6},{6,4},{5,7},{7,5},{8,10},{10,8},{9,1... | collective-permute-start | bytes 196616 | tf_op jit(solution)/shard_map/ppermute | solution.py:378
  42.2 8.8 %collective-permute-start.10 = (bf16[1024,128]{1,0:T(8,128)(2,1)S(1)}, bf16[1024,128]{1,0:T(8,128)(2,1)S(1)}, u32[]{:S(2)}, u32[]{:S(2)}) collective-permute-start(bf16[1024,128]{1,0:T(8,128)(2,1)S(1)} %get-tuple-element.116), channel_id=1, source_target_pairs={{0,2},{1,5},{2,0},{3,7},{4,6},{5,1},{6,4},{7,3},{8,10},{9,13},{10,... | collective-permute-start | bytes 786440 | tf_op jit(solution)/shard_map/ppermute | solution.py:391
  44.4 7.6 %collective-permute-start.11 = (bf16[128,256]{1,0:T(8,128)(2,1)S(1)}, bf16[128,256]{1,0:T(8,128)(2,1)S(1)}, u32[]{:S(2)}, u32[]{:S(2)}) collective-permute-start(bf16[128,256]{1,0:T(8,128)(2,1)S(1)} %get-tuple-element.120), channel_id=1, source_target_pairs={{4,0},{8,4},{12,8},{5,1},{9,5},{13,9},{6,2},{10,6},{14,10},{7,3},{... | collective-permute-start | bytes 196616 | tf_op jit(solution)/shard_map/ppermute | solution.py:415
  45.7 6.3 %collective-permute-start.12 = (bf16[128,256]{1,0:T(8,128)(2,1)S(1)}, bf16[128,256]{1,0:T(8,128)(2,1)S(1)}, u32[]{:S(2)}, u32[]{:S(2)}) collective-permute-start(bf16[128,256]{1,0:T(8,128)(2,1)S(1)} %get-tuple-element.121), channel_id=1, source_target_pairs={{0,2},{2,0},{1,3},{3,1},{4,6},{6,4},{5,7},{7,5},{8,10},{10,8},{9,1... | collective-permute-start | bytes 196616 | tf_op jit(solution)/shard_map/ppermute | solution.py:378
  50.4 13.2 %collective-permute-start.13 = (bf16[1024,128]{1,0:T(8,128)(2,1)S(1)}, bf16[1024,128]{1,0:T(8,128)(2,1)S(1)}, u32[]{:S(2)}, u32[]{:S(2)}) collective-permute-start(bf16[1024,128]{1,0:T(8,128)(2,1)S(1)} %get-tuple-element.128), channel_id=1, source_target_pairs={{0,2},{1,5},{2,0},{3,7},{4,6},{5,1},{6,4},{7,3},{8,10},{9,13},{10,... | collective-permute-start | bytes 786440 | tf_op jit(solution)/shard_map/ppermute | solution.py:391
  56.8 9.7 %collective-permute-start.16 = (bf16[1024,128]{1,0:T(8,128)(2,1)S(1)}, bf16[1024,128]{1,0:T(8,128)(2,1)S(1)}, u32[]{:S(2)}, u32[]{:S(2)}) collective-permute-start(bf16[1024,128]{1,0:T(8,128)(2,1)S(1)} %get-tuple-element.136), channel_id=1, source_target_pairs={{0,2},{1,5},{2,0},{3,7},{4,6},{5,1},{6,4},{7,3},{8,10},{9,13},{10,... | collective-permute-start | bytes 786440 | tf_op jit(solution)/shard_map/ppermute | solution.py:391
  57.9 7.4 %collective-permute-start.14 = (bf16[128,256]{1,0:T(8,128)(2,1)S(1)}, bf16[128,256]{1,0:T(8,128)(2,1)S(1)}, u32[]{:S(2)}, u32[]{:S(2)}) collective-permute-start(bf16[128,256]{1,0:T(8,128)(2,1)S(1)} %get-tuple-element.132), channel_id=1, source_target_pairs={{4,0},{8,4},{12,8},{5,1},{9,5},{13,9},{6,2},{10,6},{14,10},{7,3},{... | collective-permute-start | bytes 196616 | tf_op jit(solution)/shard_map/ppermute | solution.py:415
  59.1 6.2 %collective-permute-start.15 = (bf16[128,256]{1,0:T(8,128)(2,1)S(1)}, bf16[128,256]{1,0:T(8,128)(2,1)S(1)}, u32[]{:S(2)}, u32[]{:S(2)}) collective-permute-start(bf16[128,256]{1,0:T(8,128)(2,1)S(1)} %get-tuple-element.133), channel_id=1, source_target_pairs={{0,2},{2,0},{1,3},{3,1},{4,6},{6,4},{5,7},{7,5},{8,10},{10,8},{9,1... | collective-permute-start | bytes 196616 | tf_op jit(solution)/shard_map/ppermute | solution.py:378
  60.2 9.3 %collective-permute-start.17 = (bf16[512,128]{1,0:T(8,128)(2,1)S(1)}, bf16[512,128]{1,0:T(8,128)(2,1)S(1)}, u32[]{:S(2)}, u32[]{:S(2)}) collective-permute-start(bf16[512,128]{1,0:T(8,128)(2,1)S(1)} %get-tuple-element.138), channel_id=1, source_target_pairs={{0,4},{1,3},{2,6},{3,1},{4,0},{5,7},{6,2},{7,5},{8,12},{9,11},{10,... | collective-permute-start | bytes 393224 | tf_op jit(solution)/shard_map/ppermute | solution.py:391
  63.8 10.4 %collective-permute-start.18 = (bf16[512,128]{1,0:T(8,128)(2,1)S(1)}, bf16[512,128]{1,0:T(8,128)(2,1)S(1)}, u32[]{:S(2)}, u32[]{:S(2)}) collective-permute-start(bf16[512,128]{1,0:T(8,128)(2,1)S(1)} %get-tuple-element.140), channel_id=1, source_target_pairs={{0,4},{1,3},{2,6},{3,1},{4,0},{5,7},{6,2},{7,5},{8,12},{9,11},{10,... | collective-permute-start | bytes 393224 | tf_op jit(solution)/shard_map/ppermute | solution.py:391
  66.6 7.8 %collective-permute-start.19 = (bf16[512,128]{1,0:T(8,128)(2,1)S(1)}, bf16[512,128]{1,0:T(8,128)(2,1)S(1)}, u32[]{:S(2)}, u32[]{:S(2)}) collective-permute-start(bf16[512,128]{1,0:T(8,128)(2,1)S(1)} %get-tuple-element.142), channel_id=1, source_target_pairs={{0,4},{1,3},{2,6},{3,1},{4,0},{5,7},{6,2},{7,5},{8,12},{9,11},{10,... | collective-permute-start | bytes 393224 | tf_op jit(solution)/shard_map/ppermute | solution.py:391
  69.5 15.5 %collective-permute-start.20 = (bf16[512,128]{1,0:T(8,128)(2,1)S(1)}, bf16[512,128]{1,0:T(8,128)(2,1)S(1)}, u32[]{:S(2)}, u32[]{:S(2)}) collective-permute-start(bf16[512,128]{1,0:T(8,128)(2,1)S(1)} %get-tuple-element.144), channel_id=1, source_target_pairs={{0,8},{1,9},{2,10},{3,11},{4,12},{5,13},{6,14},{7,15},{8,0},{9,1},... | collective-permute-start | bytes 393224 | tf_op jit(solution)/shard_map/ppermute | solution.py:391
  74.2 12.8 %collective-permute-start.21 = (bf16[512,128]{1,0:T(8,128)(2,1)S(1)}, bf16[512,128]{1,0:T(8,128)(2,1)S(1)}, u32[]{:S(2)}, u32[]{:S(2)}) collective-permute-start(bf16[512,128]{1,0:T(8,128)(2,1)S(1)} %get-tuple-element.145), channel_id=1, source_target_pairs={{0,8},{1,9},{2,10},{3,11},{4,12},{5,13},{6,14},{7,15},{8,0},{9,1},... | collective-permute-start | bytes 393224 | tf_op jit(solution)/shard_map/ppermute | solution.py:391
  74.4 14.1 %collective-permute-start.22 = (bf16[512,128]{1,0:T(8,128)(2,1)S(1)}, bf16[512,128]{1,0:T(8,128)(2,1)S(1)}, u32[]{:S(2)}, u32[]{:S(2)}) collective-permute-start(bf16[512,128]{1,0:T(8,128)(2,1)S(1)} %get-tuple-element.146), channel_id=1, source_target_pairs={{0,8},{1,9},{2,10},{3,11},{4,12},{5,13},{6,14},{7,15},{8,0},{9,1},... | collective-permute-start | bytes 393224 | tf_op jit(solution)/shard_map/ppermute | solution.py:391
  85.0 5.2 %collective-permute-start.23 = (bf16[512,128]{1,0:T(8,128)(2,1)S(1)}, bf16[512,128]{1,0:T(8,128)(2,1)S(1)}, u32[]{:S(2)}, u32[]{:S(2)}) collective-permute-start(bf16[512,128]{1,0:T(8,128)(2,1)S(1)} %sum_2_2.1.refs_0_.refs_1_), channel_id=1, source_target_pairs={{0,4},{1,3},{2,6},{3,1},{4,0},{5,7},{6,2},{7,5},{8,12},{9,11},{10,... | collective-permute-start | bytes 393224 | tf_op jit(solution)/shard_map/ppermute | solution.py:391
  87.1 6.4 %collective-permute-start.24 = (bf16[512,128]{1,0:T(8,128)(2,1)S(1)}, bf16[512,128]{1,0:T(8,128)(2,1)S(1)}, u32[]{:S(2)}, u32[]{:S(2)}) collective-permute-start(bf16[512,128]{1,0:T(8,128)(2,1)S(1)} %sum_1_2.1.refs_0_.refs_1_), channel_id=1, source_target_pairs={{0,4},{1,3},{2,6},{3,1},{4,0},{5,7},{6,2},{7,5},{8,12},{9,11},{10,... | collective-permute-start | bytes 393224 | tf_op jit(solution)/shard_map/ppermute | solution.py:391
  88.5 7.8 %collective-permute-start.25 = (bf16[512,128]{1,0:T(8,128)(2,1)S(1)}, bf16[512,128]{1,0:T(8,128)(2,1)S(1)}, u32[]{:S(2)}, u32[]{:S(2)}) collective-permute-start(bf16[512,128]{1,0:T(8,128)(2,1)S(1)} %sum_0_2.1.refs_0_.refs_1_), channel_id=1, source_target_pairs={{0,4},{1,3},{2,6},{3,1},{4,0},{5,7},{6,2},{7,5},{8,12},{9,11},{10,... | collective-permute-start | bytes 393224 | tf_op jit(solution)/shard_map/ppermute | solution.py:391
  90.3 7.6 %collective-permute-start.26 = (bf16[1024,128]{1,0:T(8,128)(2,1)S(1)}, bf16[1024,128]{1,0:T(8,128)(2,1)S(1)}, u32[]{:S(2)}, u32[]{:S(2)}) collective-permute-start(bf16[1024,128]{1,0:T(8,128)(2,1)S(1)} %sum_2_3.1.refs_0_.refs_1_), channel_id=1, source_target_pairs={{0,2},{1,5},{2,0},{3,7},{4,6},{5,1},{6,4},{7,3},{8,10},{9,13},{10,... | collective-permute-start | bytes 786440 | tf_op jit(solution)/shard_map/ppermute | solution.py:391
  93.5 6.4 %collective-permute-start.27 = (bf16[1024,128]{1,0:T(8,128)(2,1)S(1)}, bf16[1024,128]{1,0:T(8,128)(2,1)S(1)}, u32[]{:S(2)}, u32[]{:S(2)}) collective-permute-start(bf16[1024,128]{1,0:T(8,128)(2,1)S(1)} %sum_1_3.1.refs_0_.refs_3_), channel_id=1, source_target_pairs={{0,2},{1,5},{2,0},{3,7},{4,6},{5,1},{6,4},{7,3},{8,10},{9,13},{10,... | collective-permute-start | bytes 786440 | tf_op jit(solution)/shard_map/ppermute | solution.py:391
  96.4 6.4 %collective-permute-start.28 = (bf16[1024,128]{1,0:T(8,128)(2,1)S(1)}, bf16[1024,128]{1,0:T(8,128)(2,1)S(1)}, u32[]{:S(2)}, u32[]{:S(2)}) collective-permute-start(bf16[1024,128]{1,0:T(8,128)(2,1)S(1)} %sum_0_3.1.refs_0_.refs_3_), channel_id=1, source_target_pairs={{0,2},{1,5},{2,0},{3,7},{4,6},{5,1},{6,4},{7,3},{8,10},{9,13},{10,... | collective-permute-start | bytes 786440 | tf_op jit(solution)/shard_map/ppermute | solution.py:391
  (6 other events, 7.0 us)

commit v7 on v6

--- a/solution.py
+++ b/solution.py
@@ -230,12 +230,11 @@
     start_bwd(layer, groups, dtotal, weights, mine, others, remote_t, outs)
 
 
-def back_kernel(layer, grad_scale, stage, *refs):
+def back_kernel(layer, grad_scale, *refs):
     dround, inputs, local_t = refs[:3]
     wi0, wi1, wo0, wo1 = refs[3:7]
     far_x, far_dmsg, far_act, far_dpre = refs[7:11]
-    back = refs[11]
-    grads, dmsg, act, dpre = refs[-4:]
+    back, grads, dmsg, act, dpre = refs[11:]
     halves = [(wi0[layer], wo0[layer]), (wi1[layer], wo1[layer])]
     dmsg[...] = mm(local_t[...], dround[...]).astype(BF16)
     for r in range(0, inputs.shape[0], 256):
@@ -251,7 +250,6 @@
     for j in range(latent // LANES):
         at = hidden // LANES * latent + j * hidden
         grads[at : at + hidden, :] = g_out[:, j * LANES : (j + 1) * LANES]
-    split(grads, stage, refs[12:14])
 
 
 def upper(stage):
@@ -261,29 +259,6 @@
     return jnp.where(lax.axis_index("feat") == 0, bit0, bit1)
 
 
-def split(block, stage, outs):
-    m = block.shape[0] // 2
-    bit = upper(stage)
-    keep, send = outs
-    keep[...] = block[pl.ds(pl.multiple_of(bit * m, m), m), :]
-    send[...] = block[pl.ds(pl.multiple_of((1 - bit) * m, m), m), :].astype(BF16)
-
-
-def add_split_kernel(stage, keep, got, *refs):
-    acc = refs[-1]
-    acc[...] = keep[...] + got[...].astype(F32)
-    split(acc, stage, refs[:-1])
-
-
-def add_all_kernel(keep, got, own, send):
-    own[...] = keep[...] + got[...].astype(F32)
-    send[...] = own[...].astype(BF16)
-
-
-def add_kernel(keep, got, out):
-    out[...] = (keep[...] + got[...].astype(F32)).astype(BF16)
-
-
 def place(stage, own, got, out):
     m = own.shape[0]
     bit = upper(stage)
@@ -291,14 +266,39 @@
     out[pl.ds(pl.multiple_of((1 - bit) * m, m), m), :] = got[...].astype(out.dtype)
 
 
-def place_kernel(stage, own, got, out):
-    place(stage, own, got, out)
-
-
-def write_kernel(layer, stage, kept, *refs):
+def sum_kernel(steps, *refs):
+    n_in = sum(1 + (kind != "split") for kind, *_ in steps)
+    n_out = len(steps) + 1 + max(group for *_, group, _ in steps)
+    ins, outs, accs = refs[:n_in], refs[n_in : n_in + n_out], refs[n_in + n_out :]
+    sends = outs[len(steps) :]
+    for (kind, stage, back, at, group, to), out in zip(steps, outs):
+        own, ins = ins[0], ins[1:]
+        m = own.shape[0]
+        send = sends[group].at[to : to + out.shape[0]]
+        if kind != "split":
+            got, ins = ins[0].at[at : at + m], ins[1:]
+        if kind in ("split", "add_split"):
+            if kind == "add_split":
+                acc, accs = accs[0], accs[1:]
+                acc[...] = own[...] + got[...].astype(F32)
+                own = acc
+            m = m // 2
+            bit = upper(stage)
+            out[...] = own[pl.ds(pl.multiple_of(bit * m, m), m), :]
+            send[...] = own[pl.ds(pl.multiple_of((1 - bit) * m, m), m), :].astype(BF16)
+        else:
+            if kind == "place":
+                place(back, own, got, out)
+            else:
+                out[...] = (own[...] + got[...].astype(F32)).astype(out.dtype)
+            send[...] = out[...].astype(BF16)
+
+
+def write_kernel(layer, stage, kept, at, *refs):
     out_in, out_out, token, grads, slab_in, slab_out, sem = refs[-7:]
     token[...] = jnp.zeros_like(token)
-    place(stage, refs[kept], refs[kept + 1], grads)
+    own = refs[kept]
+    place(stage, own, refs[kept + 1].at[at : at + own.shape[0]], grads)
     latent, hidden = slab_in.shape
     for j in range(hidden // LANES):
         slab_in[:, j * LANES : (j + 1) * LANES] = grads[j * latent : (j + 1) * latent, :]
@@ -314,42 +314,47 @@
 
 
 class Sum:
-    def __init__(self, parts, stages, name):
-        self.stages, self.name = stages, name
-        self.done = 0
-        self.keep, send = parts
-        self.got = swapped(send, stages[0])
-
-    def step(self, after):
-        n = len(self.stages)
-        i = self.done
-        self.done += 1
-        rows = self.keep.shape[0]
-        scratch = []
-        if i < n - 2:
-            body = functools.partial(add_split_kernel, self.stages[i + 1])
-            outs = [((rows // 2, LANES), F32), ((rows // 2, LANES), BF16)]
-            scratch = [pltpu.VMEM(self.keep.shape, F32)]
-        elif i == n - 2:
-            body, outs = add_all_kernel, [((rows, LANES), F32), ((rows, LANES), BF16)]
-        elif i == n - 1:
-            body, outs = add_kernel, [((rows, LANES), BF16)]
-        else:
-            body = functools.partial(place_kernel, self.stages[2 * n - 2 - i])
-            outs = [((rows * 2, LANES), BF16)]
-        self.keep, *send = call(
-            body,
-            outs,
-            [self.keep, self.got],
-            1,
-            scratch=scratch,
-            bytes_accessed=1,
-            name=f"sum_{self.name}_{i}",
-            after=after,
-        )
-        to = i + 1 if i < n - 1 else 2 * n - 3 - i
-        self.got = swapped(send[0] if send else self.keep, self.stages[to])
-        return [self.keep]
+    def __init__(self, whole, stages):
+        self.own, self.got, self.stages, self.done = whole, None, stages, 0
+
+    def next(self):
+        n, i, rows = len(self.stages), self.done, self.own.shape[0]
+        if i < n - 1:
+            return "add_split" if i else "split", self.stages[i], None, rows // 2, F32
+        if i == n - 1:
+            return "add", self.stages[i], None, rows, F32
+        stage = self.stages[2 * n - 2 - i]
+        if i == n:
+            return "add", stage, None, rows, BF16
+        return "place", stage, self.stages[2 * n - 1 - i], rows * 2, BF16
+
+
+def sum_step(sums, after):
+    steps, ins, outs, scratch, groups = [], [], [], [], {}
+    for one in sums:
+        kind, stage, back, rows, dtype = one.next()
+        group = groups.setdefault(stage, [len(groups), 0])
+        steps.append((kind, stage, back, one.got and one.got[1], *group))
+        group[1] += rows
+        ins += [one.own, one.got[0]] if one.got else [one.own]
+        outs.append(((rows, LANES), dtype))
+        if kind == "add_split":
+            scratch.append(pltpu.VMEM(one.own.shape, F32))
+    made = call(
+        functools.partial(sum_kernel, steps),
+        outs + [((rows, LANES), BF16) for _, rows in groups.values()],
+        ins,
+        1,
+        bytes_accessed=1,
+        scratch=scratch,
+        name="sum",
+        after=after,
+    )
+    arrived = [swapped(x, stage) for x, stage in zip(made[len(sums) :], groups)]
+    for one, own, (*_, group, at) in zip(sums, made, steps):
+        one.own, one.got = own, (arrived[group], at)
+        one.done += 1
+    return [made[0]]
 
 
 def gathered_grad(dtotal, back, returned, spread):
@@ -511,22 +516,19 @@
 
     over_basin, over_chain = distances("basin"), distances("chain")
     n = len(over_basin)
-    stages = list(
-        zip(over_basin + over_chain, over_chain[:n] + over_basin + over_chain[n:], strict=True)
-    )
+    orders = over_basin + over_chain, over_chain[:n] + over_basin + over_chain[n:]
+    stages = list(zip(*orders, strict=True)), list(zip(*orders[::-1], strict=True))
     returned = {}
     sums = {}
 
     def back(layer, outs, after):
         returned[layer] = backward(outs[6:])
-        parts = [((grad_rows // 2, LANES), F32), ((grad_rows // 2, LANES), BF16)]
-        grad, *parts = call(
-            functools.partial(back_kernel, layer, grad_scale, stages[0]),
-            [((rows, latent), F32), *parts],
+        grad, whole = call(
+            functools.partial(back_kernel, layer, grad_scale),
+            [((rows, latent), F32), ((grad_rows, LANES), F32)],
             [outs[1], inputs[layer], local_t, *weights, *outs[2:6]],
             3 * rows * ffn + 2 * rows * rows * latent,
             scratch=[
-                pltpu.VMEM((grad_rows, LANES), F32),
                 pltpu.VMEM((rows, latent), BF16),
                 pltpu.VMEM((rows, half), BF16),
                 pltpu.VMEM((rows, half), BF16),
@@ -534,8 +536,8 @@
             name=f"back{layer}",
             after=after,
         )
-        sums[layer] = Sum(parts, stages, f"{layer}")
-        return [outs[0], grad], [parts[0]]
+        sums[layer] = Sum(whole, stages[layer % 2])
+        return [outs[0], grad], [grad]
 
     def join(layer, state, after):
         if layer:
@@ -558,10 +560,12 @@
         )
 
     def write(layer, written, after):
-        ready = [sums[layer].keep, sums[layer].got]
+        ready = [sums[layer].own, sums[layer].got[0]]
         kept = [*written, *after]
         return pl.pallas_call(
-            functools.partial(write_kernel, layer, stages[0], len(kept)),
+            functools.partial(
+                write_kernel, layer, stages[layer % 2][0], len(kept), sums[layer].got[1]
+            ),
             out_shape=[
                 jax.ShapeDtypeStruct((layers, latent, half), F32),
                 jax.ShapeDtypeStruct((layers, half, latent), F32),
@@ -581,29 +585,33 @@
             name=f"write{layer}",
         )(*written, *after, *ready)
 
-    count = 2 * len(stages) - 2
+    count = 2 * len(stages[0]) - 1
     at = []
     for layer in reversed(range(layers)):
         state, at = back(layer, outs, at)
         if layer:
-            for above in reversed(range(layer + 1, layers)):
-                at = sums[above].step(at)
+            at = [*at, *returned[layer]]
+            at = sum_step([sums[above] for above in range(layer, layers)], at)
             outs = join(layer, state, at)
             at = outs[1:2]
-    for layer in reversed(range(1, last)):
-        at = sums[layer].step(at)
-    grad, token = join(0, state, at)
-    at = sums[0].step([token])
+    grad = None
+    while sums[0].done < count:
+        ready = [sums[0]]
+        if layers > 1 and sums[1].done < count and sums[1].next()[1] == sums[0].next()[1]:
+            ready.append(sums[1])
+        at = sum_step(ready, at)
+        if grad is None and sums[0].done == 3:
+            grad, token = join(0, state, at)
+            at = [token]
+        for layer in range(1, layers):
+            if sums[layer] not in ready and sums[layer].done < count:
+                if layer > 1 and sums[0].done == len(stages[0]):
+                    at = [*at, sums[0].got[0]]
+                at = sum_step([sums[layer]], at)
     written = []
-    waiting = list(reversed(range(layers)))
-    while waiting:
-        for layer in list(waiting):
-            if sums[layer].done < count:
-                at = sums[layer].step(at)
-            else:
-                *written, token = write(layer, written, at)
-                at = [token]
-                waiting.remove(layer)
+    for layer in reversed(range(layers)):
+        *written, token = write(layer, written, at)
+        at = [token]
     return (grad, *written)
 
 

time: 105 us -> 107 us (1.019)
  waiting for transfers between devices: 19.7 us -> 26.6 us
  starting transfers between devices: 45.6 us -> 40.9 us
    ppermute x18 -> x15, waiting for transfers between devices: 16.6 us -> 22.3 us  [over_mesh(): return lax.ppermute(x, ('chain', 'basin', 'feat'), perm)]
    ppermute x18 -> x15, starting transfers between devices: 36.8 us -> 33.1 us  [over_mesh(): return lax.ppermute(x, ('chain', 'basin', 'feat'), perm)]
    ppermute x3, waiting for transfers between devices: 2.31 us -> 3.56 us  [backward(): up = lax.ppermute(grads[0], 'chain', [(c, c - 1) for c in range(1, chain)])]
    ppermute x8, starting transfers between devices: 4.83 us -> 3.73 us  [around(): return lax.ppermute(x, axis, [(i, (i + distance) % n) for i in range(n)])]
  transfers between devices with their start and end apart: 29 -> 26, of which waited for: 15 -> 14; matrix products, arithmetic and copies ran while one was open for 1% -> 1% of each run, Pallas kernels for 24% -> 23%
where the time goes in v7:
time: 107 us
  starting transfers between devices  40.9 us (38%)
  Pallas kernels  31.1 us (29%)
  waiting for transfers between devices  26.6 us (25%)
  local copies, waits for them, and re-layouts  6.18 us (6%)
  between operations  1.12 us (1%)
    ppermute x15, starting transfers between devices, over_mesh(): return lax.ppermute(x, ('chain', 'basin', 'feat'), perm)  33.1 us
    pallas_call x28, Pallas kernels, call(): pl.pallas_call(lambda *refs: body(*refs[skipped:]), out_shape=[jax.ShapeD...  27.1 us
    ppermute x15, waiting for transfers between devices, over_mesh(): return lax.ppermute(x, ('chain', 'basin', 'feat'), perm)  22.3 us
    unnamed x19, local copies, waits for them, and re-layouts  6.18 us
    ppermute x3, starting transfers between devices, backward(): up = lax.ppermute(grads[0], 'chain', [(c, c - 1) for c in range(1, chain)])  4.04 us
    pallas_call x3, Pallas kernels, write(): pl.pallas_call(functools.partial(write_kernel, layer, stages[layer % 2][0...  4 us
    ppermute x8, starting transfers between devices, around(): return lax.ppermute(x, axis, [(i, (i + distance) % n) for i in range(n)])  3.73 us
    ppermute x3, waiting for transfers between devices, backward(): up = lax.ppermute(grads[0], 'chain', [(c, c - 1) for c in range(1, chain)])  3.56 us
  transfers between devices with their start and end apart: 26, of which 14 were waited for; matrix products, arithmetic and copies ran while one was open for 1% of the time, Pallas kernels for 23%

profile of v7, /device:TPU:0, one launch (start us, length us, event | category | flops | bytes accessed | tf_op | source)
XLA Modules:
  0.0 106.7 jit_solution(987518763567029439)
XLA Ops:
  3.6 4.9 %collective-permute-start.2 = (bf16[128,256]{1,0:T(8,128)(2,1)S(1)}, bf16[128,256]{1,0:T(8,128)(2,1)S(1)}, u32[]{:S(2)}, u32[]{:S(2)}) collective-permute-start(bf16[128,256]{1,0:T(8,128)(2,1)S(1)} %get-tuple-element.93), channel_id=1, source_target_pairs={{0,4},{1,3},{2,6},{3,1},{4,8},{5,7},{6,10},{7,5},{8,12},{9,11},{10... | collective-permute-start | bytes 196616 | tf_op jit(solution)/shard_map/ppermute | solution.py:396
  13.7 2.7 %first.1 = (bf16[768,256]{1,0:T(8,128)(2,1)S(1)}, bf16[768,768]{1,0:T(8,128)(2,1)S(1)}, bf16[768,768]{1,0:T(8,128)(2,1)S(1)}, bf16[768,256]{1,0:T(8,128)(2,1)S(1)}, bf16[256,768]{1,0:T(8,128)(2,1)S(1)}) custom-call(bf16[768,256]{1,0:T(8,128)(2,1)S(1)} %copy-done.5, bf16[128,768]{1,0:T(8,128)(2,1)S(1)} %get-tuple-element.91.refs_1_, ...), custom_call_target="tpu_custom_call" | custom-call | flops 956301312 | bytes 4000000 | tf_op jit(solution)/shard_map/first/pallas_call | solution.py:32
  18.8 3.5 %collective-permute-start.4 = (bf16[128,256]{1,0:T(8,128)(2,1)S(1)}, bf16[128,256]{1,0:T(8,128)(2,1)S(1)}, u32[]{:S(2)}, u32[]{:S(2)}) collective-permute-start(bf16[128,256]{1,0:T(8,128)(2,1)S(1)} %get-tuple-element.100), channel_id=1, source_target_pairs={{0,4},{1,3},{2,6},{3,1},{4,8},{5,7},{6,10},{7,5},{8,12},{9,11},{10... | collective-permute-start | bytes 196616 | tf_op jit(solution)/shard_map/ppermute | solution.py:396
  22.3 1.2 %local1.1.refs_1_ = bf16[768,256]{1,0:T(8,128)(2,1)S(1)} custom-call(bf16[768,256]{1,0:T(8,128)(2,1)S(1)} %get-tuple-element.101.refs_0_.refs_2_, bf16[3,256,512]{2,1,0:T(8,128)(2,1)S(1)} %copy-done.1, bf16[3,256,512]{2,1,0:T(8,128)(2,1)S(1)} %collective-permute-done.refs_5_.refs_4_.refs_2_.refs_6_.refs_7_, bf16[3,512,256]{2,1,0:T(8,128)(2,1)S(1)} %copy-done.3, ...), custom_call_target="tpu_custom_call" | custom-call | flops 805306368 | bytes 4000000 | tf_op jit(solution)/shard_map/local1/pallas_call | solution.py:32
  26.5 4.3 %collective-permute-start.6 = (bf16[128,256]{1,0:T(8,128)(2,1)S(1)}, bf16[128,256]{1,0:T(8,128)(2,1)S(1)}, u32[]{:S(2)}, u32[]{:S(2)}) collective-permute-start(bf16[128,256]{1,0:T(8,128)(2,1)S(1)} %get-tuple-element.105), channel_id=1, source_target_pairs={{0,4},{1,3},{2,6},{3,1},{4,8},{5,7},{6,10},{7,5},{8,12},{9,11},{10... | collective-permute-start | bytes 196616 | tf_op jit(solution)/shard_map/ppermute | solution.py:396
  30.8 1.2 %local2.1.refs_1_ = bf16[768,256]{1,0:T(8,128)(2,1)S(1)} custom-call(bf16[768,256]{1,0:T(8,128)(2,1)S(1)} %get-tuple-element.106.refs_0_.refs_1_, bf16[3,256,512]{2,1,0:T(8,128)(2,1)S(1)} %copy-done.1, bf16[3,256,512]{2,1,0:T(8,128)(2,1)S(1)} %collective-permute-done.refs_5_.refs_4_.refs_2_.refs_6_.refs_7_, bf16[3,512,256]{2,1,0:T(8,128)(2,1)S(1)} %copy-done.3, ...), custom_call_target="tpu_custom_call" | custom-call | flops 805306368 | bytes 4000000 | tf_op jit(solution)/shard_map/local2/pallas_call | solution.py:32
  33.9 2.1 %turn.1 = (f32[768,256]{1,0:T(8,128)S(1)}, bf16[768,256]{1,0:T(8,128)(2,1)S(1)}, bf16[256,256]{1,0:T(8,128)(2,1)S(1)}, bf16[256,256]{1,0:T(8,128)(2,1)S(1)}, bf1...) custom-call(f32[768,256]{1,0:T(8,128)S(1)} %get-tuple-element.104.re, ...), custom_call_target="tpu_custom_call" | custom-call | flops 536870912 | bytes 4000000 | tf_op jit(solution)/shard_map/turn/pallas_call | solution.py:32
  36.0 1.5 %collective-permute-start.8 = (bf16[128,256]{1,0:T(8,128)(2,1)S(1)}, bf16[128,256]{1,0:T(8,128)(2,1)S(1)}, u32[]{:S(2)}, u32[]{:S(2)}) collective-permute-start(bf16[128,256]{1,0:T(8,128)(2,1)S(1)} %get-tuple-element.117), channel_id=1, source_target_pairs={{4,0},{8,4},{12,8},{5,1},{9,5},{13,9},{6,2},{10,6},{14,10},{7,3},{... | collective-permute-start | bytes 196616 | tf_op jit(solution)/shard_map/ppermute | solution.py:420
  37.5 1.6 %collective-permute-start.9 = (bf16[128,256]{1,0:T(8,128)(2,1)S(1)}, bf16[128,256]{1,0:T(8,128)(2,1)S(1)}, u32[]{:S(2)}, u32[]{:S(2)}) collective-permute-start(bf16[128,256]{1,0:T(8,128)(2,1)S(1)} %get-tuple-element.118), channel_id=1, source_target_pairs={{0,2},{2,0},{1,3},{3,1},{4,6},{6,4},{5,7},{7,5},{8,10},{10,8},{9,1... | collective-permute-start | bytes 196616 | tf_op jit(solution)/shard_map/ppermute | solution.py:383
  39.0 3.0 %back2.1 = (f32[768,256]{1,0:T(8,128)S(1)}, f32[2048,128]{1,0:T(8,128)S(1)}) custom-call(bf16[768,256]{1,0:T(8,128)(2,1)S(1)} %get-tuple-element.110.refs_0_, bf16[768,256]{1,0:T(8,128)(2,1)S(1)} %get-tuple-element.106.refs_0_.refs_1_, bf16[768,768]{1,0:T(8,128)(2,1)S(1)} %get-tuple-element.111.refs_2_.refs_3_, bf16[3,256,512]{2,1,0:T(8,128)(2,1)S(1)} %copy-done.1, ...), custom_call_target="tpu_custom_call" | custom-call | flops 2717908992 | bytes 4000000 | tf_op jit(solution)/shard_map/back2/pallas_call | solution.py:32
  42.8 1.6 %collective-permute-start.12 = (bf16[1024,128]{1,0:T(8,128)(2,1)S(1)}, bf16[1024,128]{1,0:T(8,128)(2,1)S(1)}, u32[]{:S(2)}, u32[]{:S(2)}) collective-permute-start(bf16[1024,128]{1,0:T(8,128)(2,1)S(1)} %get-tuple-element.132), channel_id=1, source_target_pairs={{0,2},{1,5},{2,0},{3,7},{4,6},{5,1},{6,4},{7,3},{8,10},{9,13},{10,... | collective-permute-start | bytes 786440 | tf_op jit(solution)/shard_map/ppermute | solution.py:396
  44.4 1.6 %join2.1 = (f32[768,256]{1,0:T(8,128)S(1)}, bf16[768,256]{1,0:T(8,128)(2,1)S(1)}, bf16[256,256]{1,0:T(8,128)(2,1)S(1)}, bf16[256,256]{1,0:T(8,128)(2,1)S(1)}, bf...) custom-call(f32[1024,128]{1,0:T(8,128)S(1)} %get-tuple-element.120.r, ...), custom_call_target="tpu_custom_call" | custom-call | flops 536870912 | bytes 4000000 | tf_op jit(solution)/shard_map/join2/pallas_call | solution.py:32
  46.0 1.3 %collective-permute-start.10 = (bf16[128,256]{1,0:T(8,128)(2,1)S(1)}, bf16[128,256]{1,0:T(8,128)(2,1)S(1)}, u32[]{:S(2)}, u32[]{:S(2)}) collective-permute-start(bf16[128,256]{1,0:T(8,128)(2,1)S(1)} %get-tuple-element.129), channel_id=1, source_target_pairs={{4,0},{8,4},{12,8},{5,1},{9,5},{13,9},{6,2},{10,6},{14,10},{7,3},{... | collective-permute-start | bytes 196616 | tf_op jit(solution)/shard_map/ppermute | solution.py:420
  47.9 3.0 %back1.1 = (f32[768,256]{1,0:T(8,128)S(1)}, f32[2048,128]{1,0:T(8,128)S(1)}) custom-call(bf16[768,256]{1,0:T(8,128)(2,1)S(1)} %get-tuple-element.123.refs_0_.refs_1_, bf16[768,256]{1,0:T(8,128)(2,1)S(1)} %get-tuple-element.123.refs_0_.refs_1_, bf16[768,256]{1,0:T(8,128)(2,1)S(1)} %get-tuple-element.101.refs_0_.refs_2_, ...), custom_call_target="tpu_custom_call" | custom-call | flops 2717908992 | bytes 4000000 | tf_op jit(solution)/shard_map/back1/pallas_call | solution.py:32
  50.9 1.5 %collective-permute-done.10.refs_1_.refs_10_ = bf16[128,256]{1,0:T(8,128)(2,1)S(1)} collective-permute-done((bf16[128,256]{1,0:T(8,128)(2,1)S(1)}, bf16[128,256]{1,0:T(8,128)(2,1)S(1)}, u32[]{:S(2)}, u32[]{:S(2)}) %collective-permute-start.10) | collective-permute-done | bytes 65568 | tf_op jit(solution)/shard_map/ppermute | solution.py:420
  52.5 1.9 %collective-permute-start.13 = (bf16[1536,128]{1,0:T(8,128)(2,1)S(1)}, bf16[1536,128]{1,0:T(8,128)(2,1)S(1)}, u32[]{:S(2)}, u32[]{:S(2)}) collective-permute-start(bf16[1536,128]{1,0:T(8,128)(2,1)S(1)} %get-tuple-element.142), channel_id=1, source_target_pairs={{0,4},{1,3},{2,6},{3,1},{4,0},{5,7},{6,2},{7,5},{8,12},{9,11},{10,... | collective-permute-start | bytes 1179656 | tf_op jit(solution)/shard_map/ppermute | solution.py:396
  54.5 1.6 %join1.1 = (f32[768,256]{1,0:T(8,128)S(1)}, bf16[768,256]{1,0:T(8,128)(2,1)S(1)}, bf16[256,256]{1,0:T(8,128)(2,1)S(1)}, bf16[256,256]{1,0:T(8,128)(2,1)S(1)}, bf...) custom-call(f32[1024,128]{1,0:T(8,128)S(1)} %get-tuple-element.133.r, ...), custom_call_target="tpu_custom_call" | custom-call | flops 536870912 | bytes 4000000 | tf_op jit(solution)/shard_map/join1/pallas_call | solution.py:32
  56.0 3.0 %back0.1 = (f32[768,256]{1,0:T(8,128)S(1)}, f32[2048,128]{1,0:T(8,128)S(1)}) custom-call(bf16[768,256]{1,0:T(8,128)(2,1)S(1)} %get-tuple-element.135.refs_0_.refs_1_, bf16[768,256]{1,0:T(8,128)(2,1)S(1)} %get-tuple-element.135.refs_0_.refs_1_, bf16[768,256]{1,0:T(8,128)(2,1)S(1)} %copy-done.6, bf16[768,768]{1,0:T(8,128)(2,1)S(1)} %get-tuple-element.111.refs_2_.refs_3_, ...), custom_call_target="tpu_custom_call" | custom-call | flops 2717908992 | bytes 4000000 | tf_op jit(solution)/shard_map/back0/pallas_call | solution.py:32
  59.1 1.3 %collective-permute-done.13.refs_3_.refs_2_ = bf16[1536,128]{1,0:T(8,128)(2,1)S(1)} collective-permute-done((bf16[1536,128]{1,0:T(8,128)(2,1)S(1)}, bf16[1536,128]{1,0:T(8,128)(2,1)S(1)}, u32[]{:S(2)}, u32[]{:S(2)}) %collective-permute-start.13) | collective-permute-done | bytes 393248 | tf_op jit(solution)/shard_map/ppermute | solution.py:396
  61.3 3.5 %collective-permute-start.15 = (bf16[512,128]{1,0:T(8,128)(2,1)S(1)}, bf16[512,128]{1,0:T(8,128)(2,1)S(1)}, u32[]{:S(2)}, u32[]{:S(2)}) collective-permute-start(bf16[512,128]{1,0:T(8,128)(2,1)S(1)} %get-tuple-element.150), channel_id=1, source_target_pairs={{0,8},{1,9},{2,10},{3,11},{4,12},{5,13},{6,14},{7,15},{8,0},{9,1},... | collective-permute-start | bytes 393224 | tf_op jit(solution)/shard_map/ppermute | solution.py:396
  64.9 3.5 %collective-permute-done.14.refs_2_ = bf16[1536,128]{1,0:T(8,128)(2,1)S(1)} collective-permute-done((bf16[1536,128]{1,0:T(8,128)(2,1)S(1)}, bf16[1536,128]{1,0:T(8,128)(2,1)S(1)}, u32[]{:S(2)}, u32[]{:S(2)}) %collective-permute-start.14) | collective-permute-done | bytes 393248 | tf_op jit(solution)/shard_map/ppermute | solution.py:396
  68.5 1.9 %collective-permute-start.16 = (bf16[512,128]{1,0:T(8,128)(2,1)S(1)}, bf16[512,128]{1,0:T(8,128)(2,1)S(1)}, u32[]{:S(2)}, u32[]{:S(2)}) collective-permute-start(bf16[512,128]{1,0:T(8,128)(2,1)S(1)} %get-tuple-element.152), channel_id=1, source_target_pairs={{0,4},{1,3},{2,6},{3,1},{4,0},{5,7},{6,2},{7,5},{8,12},{9,11},{10,... | collective-permute-start | bytes 393224 | tf_op jit(solution)/shard_map/ppermute | solution.py:396
  70.5 3.5 %collective-permute-start.19 = (bf16[512,128]{1,0:T(8,128)(2,1)S(1)}, bf16[512,128]{1,0:T(8,128)(2,1)S(1)}, u32[]{:S(2)}, u32[]{:S(2)}) collective-permute-start(bf16[512,128]{1,0:T(8,128)(2,1)S(1)} %get-tuple-element.159), channel_id=1, source_target_pairs={{0,8},{1,9},{2,10},{3,11},{4,12},{5,13},{6,14},{7,15},{8,0},{9,1},... | collective-permute-start | bytes 393224 | tf_op jit(solution)/shard_map/ppermute | solution.py:396
  74.0 1.3 %collective-permute-start.17 = (bf16[128,256]{1,0:T(8,128)(2,1)S(1)}, bf16[128,256]{1,0:T(8,128)(2,1)S(1)}, u32[]{:S(2)}, u32[]{:S(2)}) collective-permute-start(bf16[128,256]{1,0:T(8,128)(2,1)S(1)} %get-tuple-element.155), channel_id=1, source_target_pairs={{4,0},{8,4},{12,8},{5,1},{9,5},{13,9},{6,2},{10,6},{14,10},{7,3},{... | collective-permute-start | bytes 196616 | tf_op jit(solution)/shard_map/ppermute | solution.py:420
  76.2 2.7 %collective-permute-start.21 = (bf16[512,128]{1,0:T(8,128)(2,1)S(1)}, bf16[512,128]{1,0:T(8,128)(2,1)S(1)}, u32[]{:S(2)}, u32[]{:S(2)}) collective-permute-start(bf16[512,128]{1,0:T(8,128)(2,1)S(1)} %get-tuple-element.162), channel_id=1, source_target_pairs={{0,4},{1,3},{2,6},{3,1},{4,0},{5,7},{6,2},{7,5},{8,12},{9,11},{10,... | collective-permute-start | bytes 393224 | tf_op jit(solution)/shard_map/ppermute | solution.py:396
  79.1 1.3 %collective-permute-done.17.refs_4_ = bf16[128,256]{1,0:T(8,128)(2,1)S(1)} collective-permute-done((bf16[128,256]{1,0:T(8,128)(2,1)S(1)}, bf16[128,256]{1,0:T(8,128)(2,1)S(1)}, u32[]{:S(2)}, u32[]{:S(2)}) %collective-permute-start.17) | collective-permute-done | bytes 65568 | tf_op jit(solution)/shard_map/ppermute | solution.py:420
  80.4 1.1 %join0.1 = (f32[768,256]{1,0:T(8,128)}, f32[8,128]{1,0:T(8,128)S(1)}) custom-call(f32[512,128]{1,0:T(8,128)S(1)} %get-tuple-element.153.refs_0_.refs_1_, f32[768,256]{1,0:T(8,128)S(1)} %get-tuple-element.154.refs_1_, f32[768,256]{1,0:T(8,128)S(1)} %get-tuple-element.140.refs_0_.refs_2_, bf16[768,256]{1,0:T(8,128)(2,1)S(1)} %get-tuple-element.122.refs_3_, ...), custom_call_target="tpu_custom_call" | custom-call | flops 100663296 | bytes 4000000 | tf_op jit(solution)/shard_map/join0/pallas_call | solution.py:32
  82.4 3.9 %collective-permute-done.20.refs_1_.refs_2_ = bf16[512,128]{1,0:T(8,128)(2,1)S(1)} collective-permute-done((bf16[512,128]{1,0:T(8,128)(2,1)S(1)}, bf16[512,128]{1,0:T(8,128)(2,1)S(1)}, u32[]{:S(2)}, u32[]{:S(2)}) %collective-permute-start.20) | collective-permute-done | bytes 131104 | tf_op jit(solution)/shard_map/ppermute | solution.py:396
  86.7 3.2 %collective-permute-start.23 = (bf16[1536,128]{1,0:T(8,128)(2,1)S(1)}, bf16[1536,128]{1,0:T(8,128)(2,1)S(1)}, u32[]{:S(2)}, u32[]{:S(2)}) collective-permute-start(bf16[1536,128]{1,0:T(8,128)(2,1)S(1)} %get-tuple-element.166), channel_id=1, source_target_pairs={{0,4},{1,3},{2,6},{3,1},{4,0},{5,7},{6,2},{7,5},{8,12},{9,11},{10,... | collective-permute-start | bytes 1179656 | tf_op jit(solution)/shard_map/ppermute | solution.py:396
  90.4 7.9 %collective-permute-done.23.refs_2_.refs_4_ = bf16[1536,128]{1,0:T(8,128)(2,1)S(1)} collective-permute-done((bf16[1536,128]{1,0:T(8,128)(2,1)S(1)}, bf16[1536,128]{1,0:T(8,128)(2,1)S(1)}, u32[]{:S(2)}, u32[]{:S(2)}) %collective-permute-start.23) | collective-permute-done | bytes 393248 | tf_op jit(solution)/shard_map/ppermute | solution.py:396
  100.8 4.1 %collective-permute-done.25.refs_4_ = bf16[1024,128]{1,0:T(8,128)(2,1)S(1)} collective-permute-done((bf16[1024,128]{1,0:T(8,128)(2,1)S(1)}, bf16[1024,128]{1,0:T(8,128)(2,1)S(1)}, u32[]{:S(2)}, u32[]{:S(2)}) %collective-permute-start.25) | collective-permute-done | bytes 262176 | tf_op jit(solution)/shard_map/ppermute | solution.py:396
  104.8 1.7 %write0.1 = (f32[3,256,512]{2,1,0:T(8,128)}, f32[3,512,256]{2,1,0:T(8,128)}, f32[8,128]{1,0:T(8,128)}) custom-call(f32[3,256,512]{2,1,0:T(8,128)} %get-tuple-element.173.refs_0_, f32[3,512,256]{2,1,0:T(8,128)} %get-tuple-element.174.refs_1_, f32[8,128]{1,0:T(8,128)S(1)} %get-tuple-element.175.refs_2_, ...), custom_call_target="tpu_custom_call", output_to_operand_aliasing={{0}: (0, {}), {1}: (1, {})} | custom-call | flops 1 | bytes 1 | tf_op jit(solution)/shard_map/write0/pallas_call | solution.py:565
  (71 shorter events, 23.2 us)
Async XLA Ops:
  0.6 8.6 %collective-permute-start = (bf16[3,256,512]{2,1,0:T(8,128)(2,1)}, bf16[3,256,512]{2,1,0:T(8,128)(2,1)S(1)}, u32[]{:S(2)}, u32[]{:S(2)}) collective-permute-start(bf16[3,256,512]{2,1,0:T(8,128)(2,1)} %refs_4_.11), channel_id=1, source_target_pairs={{0,1},{1,0},{2,3},{3,2},{4,5},{5,4},{6,7},{7,6},{8,9},{9,8},{10,11... | collective-permute-start | bytes 2359304 | tf_op jit(solution)/shard_map/ppermute | solution.py:383
  1.1 8.1 %collective-permute-start.1 = (bf16[3,512,256]{2,1,0:T(8,128)(2,1)}, bf16[3,512,256]{2,1,0:T(8,128)(2,1)S(1)}, u32[]{:S(2)}, u32[]{:S(2)}) collective-permute-start(bf16[3,512,256]{2,1,0:T(8,128)(2,1)} %refs_6_.13), channel_id=1, source_target_pairs={{0,1},{1,0},{2,3},{3,2},{4,5},{5,4},{6,7},{7,6},{8,9},{9,8},{10,11... | collective-permute-start | bytes 2359304 | tf_op jit(solution)/shard_map/ppermute | solution.py:383
  3.6 12.8 %collective-permute-start.2 = (bf16[128,256]{1,0:T(8,128)(2,1)S(1)}, bf16[128,256]{1,0:T(8,128)(2,1)S(1)}, u32[]{:S(2)}, u32[]{:S(2)}) collective-permute-start(bf16[128,256]{1,0:T(8,128)(2,1)S(1)} %get-tuple-element.93), channel_id=1, source_target_pairs={{0,4},{1,3},{2,6},{3,1},{4,8},{5,7},{6,10},{7,5},{8,12},{9,11},{10... | collective-permute-start | bytes 196616 | tf_op jit(solution)/shard_map/ppermute | solution.py:396
  9.3 1.1 %copy-start = (bf16[3,256,512]{2,1,0:T(8,128)(2,1)S(1)}, bf16[3,256,512]{2,1,0:T(8,128)(2,1)}, u32[]{:S(2)}) copy-start(bf16[3,256,512]{2,1,0:T(8,128)(2,1)} %refs_4_.11) | copy-start | bytes 2359300
  10.4 1.1 %copy-start.2 = (bf16[3,512,256]{2,1,0:T(8,128)(2,1)S(1)}, bf16[3,512,256]{2,1,0:T(8,128)(2,1)}, u32[]{:S(2)}) copy-start(bf16[3,512,256]{2,1,0:T(8,128)(2,1)} %refs_6_.13) | copy-start | bytes 2359300
  13.7 2.8 %copy-start.1 = (bf16[3,256,512]{2,1,0:T(8,128)(2,1)S(1)}, bf16[3,256,512]{2,1,0:T(8,128)(2,1)}, u32[]{:S(2)}) copy-start(bf16[3,256,512]{2,1,0:T(8,128)(2,1)} %refs_4_.11) | copy-start | bytes 2359300
  13.7 2.8 %copy-start.3 = (bf16[3,512,256]{2,1,0:T(8,128)(2,1)S(1)}, bf16[3,512,256]{2,1,0:T(8,128)(2,1)}, u32[]{:S(2)}) copy-start(bf16[3,512,256]{2,1,0:T(8,128)(2,1)} %refs_6_.13) | copy-start | bytes 2359300
  16.4 1.3 %collective-permute-start.3 = (bf16[128,256]{1,0:T(8,128)(2,1)S(1)}, bf16[128,256]{1,0:T(8,128)(2,1)S(1)}, u32[]{:S(2)}, u32[]{:S(2)}) collective-permute-start(bf16[128,256]{1,0:T(8,128)(2,1)S(1)} %collective-permute-done.2.refs_7_.refs_12_), channel_id=1, source_target_pairs={{0,1},{1,0},{2,3},{3,2},{4,5},{5,4},{6,7},{7,6},{8,9},{9,8},{10,11... | collective-permute-start | bytes 196616 | tf_op jit(solution)/shard_map/ppermute | solution.py:383
  18.8 5.4 %collective-permute-start.4 = (bf16[128,256]{1,0:T(8,128)(2,1)S(1)}, bf16[128,256]{1,0:T(8,128)(2,1)S(1)}, u32[]{:S(2)}, u32[]{:S(2)}) collective-permute-start(bf16[128,256]{1,0:T(8,128)(2,1)S(1)} %get-tuple-element.100), channel_id=1, source_target_pairs={{0,4},{1,3},{2,6},{3,1},{4,8},{5,7},{6,10},{7,5},{8,12},{9,11},{10... | collective-permute-start | bytes 196616 | tf_op jit(solution)/shard_map/ppermute | solution.py:396
  24.2 1.3 %collective-permute-start.5 = (bf16[128,256]{1,0:T(8,128)(2,1)S(1)}, bf16[128,256]{1,0:T(8,128)(2,1)S(1)}, u32[]{:S(2)}, u32[]{:S(2)}) collective-permute-start(bf16[128,256]{1,0:T(8,128)(2,1)S(1)} %collective-permute-done.4.refs_7_.refs_12_), channel_id=1, source_target_pairs={{0,1},{1,0},{2,3},{3,2},{4,5},{5,4},{6,7},{7,6},{8,9},{9,8},{10,11... | collective-permute-start | bytes 196616 | tf_op jit(solution)/shard_map/ppermute | solution.py:383
  26.5 6.2 %collective-permute-start.6 = (bf16[128,256]{1,0:T(8,128)(2,1)S(1)}, bf16[128,256]{1,0:T(8,128)(2,1)S(1)}, u32[]{:S(2)}, u32[]{:S(2)}) collective-permute-start(bf16[128,256]{1,0:T(8,128)(2,1)S(1)} %get-tuple-element.105), channel_id=1, source_target_pairs={{0,4},{1,3},{2,6},{3,1},{4,8},{5,7},{6,10},{7,5},{8,12},{9,11},{10... | collective-permute-start | bytes 196616 | tf_op jit(solution)/shard_map/ppermute | solution.py:396
  32.0 1.9 %copy-start.8 = (f32[768,256]{1,0:T(8,128)S(1)}, f32[768,256]{1,0:T(8,128)}, u32[]{:S(2)}) copy-start(f32[768,256]{1,0:T(8,128)} %refs_4_.9) | copy-start | bytes 2359300
  32.7 1.3 %collective-permute-start.7 = (bf16[128,256]{1,0:T(8,128)(2,1)S(1)}, bf16[128,256]{1,0:T(8,128)(2,1)S(1)}, u32[]{:S(2)}, u32[]{:S(2)}) collective-permute-start(bf16[128,256]{1,0:T(8,128)(2,1)S(1)} %collective-permute-done.6.refs_7_.refs_9_), channel_id=1, source_target_pairs={{0,1},{1,0},{2,3},{3,2},{4,5},{5,4},{6,7},{7,6},{8,9},{9,8},{10,11... | collective-permute-start | bytes 196616 | tf_op jit(solution)/shard_map/ppermute | solution.py:383
  36.0 6.8 %collective-permute-start.8 = (bf16[128,256]{1,0:T(8,128)(2,1)S(1)}, bf16[128,256]{1,0:T(8,128)(2,1)S(1)}, u32[]{:S(2)}, u32[]{:S(2)}) collective-permute-start(bf16[128,256]{1,0:T(8,128)(2,1)S(1)} %get-tuple-element.117), channel_id=1, source_target_pairs={{4,0},{8,4},{12,8},{5,1},{9,5},{13,9},{6,2},{10,6},{14,10},{7,3},{... | collective-permute-start | bytes 196616 | tf_op jit(solution)/shard_map/ppermute | solution.py:420
  37.5 5.3 %collective-permute-start.9 = (bf16[128,256]{1,0:T(8,128)(2,1)S(1)}, bf16[128,256]{1,0:T(8,128)(2,1)S(1)}, u32[]{:S(2)}, u32[]{:S(2)}) collective-permute-start(bf16[128,256]{1,0:T(8,128)(2,1)S(1)} %get-tuple-element.118), channel_id=1, source_target_pairs={{0,2},{2,0},{1,3},{3,1},{4,6},{6,4},{5,7},{7,5},{8,10},{10,8},{9,1... | collective-permute-start | bytes 196616 | tf_op jit(solution)/shard_map/ppermute | solution.py:383
  42.8 9.5 %collective-permute-start.12 = (bf16[1024,128]{1,0:T(8,128)(2,1)S(1)}, bf16[1024,128]{1,0:T(8,128)(2,1)S(1)}, u32[]{:S(2)}, u32[]{:S(2)}) collective-permute-start(bf16[1024,128]{1,0:T(8,128)(2,1)S(1)} %get-tuple-element.132), channel_id=1, source_target_pairs={{0,2},{1,5},{2,0},{3,7},{4,6},{5,1},{6,4},{7,3},{8,10},{9,13},{10,... | collective-permute-start | bytes 786440 | tf_op jit(solution)/shard_map/ppermute | solution.py:396
  46.0 6.4 %collective-permute-start.10 = (bf16[128,256]{1,0:T(8,128)(2,1)S(1)}, bf16[128,256]{1,0:T(8,128)(2,1)S(1)}, u32[]{:S(2)}, u32[]{:S(2)}) collective-permute-start(bf16[128,256]{1,0:T(8,128)(2,1)S(1)} %get-tuple-element.129), channel_id=1, source_target_pairs={{4,0},{8,4},{12,8},{5,1},{9,5},{13,9},{6,2},{10,6},{14,10},{7,3},{... | collective-permute-start | bytes 196616 | tf_op jit(solution)/shard_map/ppermute | solution.py:420
  47.3 5.1 %collective-permute-start.11 = (bf16[128,256]{1,0:T(8,128)(2,1)S(1)}, bf16[128,256]{1,0:T(8,128)(2,1)S(1)}, u32[]{:S(2)}, u32[]{:S(2)}) collective-permute-start(bf16[128,256]{1,0:T(8,128)(2,1)S(1)} %get-tuple-element.130), channel_id=1, source_target_pairs={{0,2},{2,0},{1,3},{3,1},{4,6},{6,4},{5,7},{7,5},{8,10},{10,8},{9,1... | collective-permute-start | bytes 196616 | tf_op jit(solution)/shard_map/ppermute | solution.py:383
  52.5 7.8 %collective-permute-start.13 = (bf16[1536,128]{1,0:T(8,128)(2,1)S(1)}, bf16[1536,128]{1,0:T(8,128)(2,1)S(1)}, u32[]{:S(2)}, u32[]{:S(2)}) collective-permute-start(bf16[1536,128]{1,0:T(8,128)(2,1)S(1)} %get-tuple-element.142), channel_id=1, source_target_pairs={{0,4},{1,3},{2,6},{3,1},{4,0},{5,7},{6,2},{7,5},{8,12},{9,11},{10,... | collective-permute-start | bytes 1179656 | tf_op jit(solution)/shard_map/ppermute | solution.py:396
  54.5 1.6 %copy-start.6 = (bf16[768,256]{1,0:T(8,128)(2,1)S(1)}, bf16[768,256]{1,0:T(8,128)(2,1)}, u32[]{:S(2)}) copy-start(bf16[768,256]{1,0:T(8,128)(2,1)} %refs_2_.2) | copy-start | bytes 1179652
  60.6 7.8 %collective-permute-start.14 = (bf16[1536,128]{1,0:T(8,128)(2,1)S(1)}, bf16[1536,128]{1,0:T(8,128)(2,1)S(1)}, u32[]{:S(2)}, u32[]{:S(2)}) collective-permute-start(bf16[1536,128]{1,0:T(8,128)(2,1)S(1)} %get-tuple-element.146), channel_id=1, source_target_pairs={{0,2},{1,5},{2,0},{3,7},{4,6},{5,1},{6,4},{7,3},{8,10},{9,13},{10,... | collective-permute-start | bytes 1179656 | tf_op jit(solution)/shard_map/ppermute | solution.py:396
  61.3 14.8 %collective-permute-start.15 = (bf16[512,128]{1,0:T(8,128)(2,1)S(1)}, bf16[512,128]{1,0:T(8,128)(2,1)S(1)}, u32[]{:S(2)}, u32[]{:S(2)}) collective-permute-start(bf16[512,128]{1,0:T(8,128)(2,1)S(1)} %get-tuple-element.150), channel_id=1, source_target_pairs={{0,8},{1,9},{2,10},{3,11},{4,12},{5,13},{6,14},{7,15},{8,0},{9,1},... | collective-permute-start | bytes 393224 | tf_op jit(solution)/shard_map/ppermute | solution.py:396
  68.5 10.4 %collective-permute-start.16 = (bf16[512,128]{1,0:T(8,128)(2,1)S(1)}, bf16[512,128]{1,0:T(8,128)(2,1)S(1)}, u32[]{:S(2)}, u32[]{:S(2)}) collective-permute-start(bf16[512,128]{1,0:T(8,128)(2,1)S(1)} %get-tuple-element.152), channel_id=1, source_target_pairs={{0,4},{1,3},{2,6},{3,1},{4,0},{5,7},{6,2},{7,5},{8,12},{9,11},{10,... | collective-permute-start | bytes 393224 | tf_op jit(solution)/shard_map/ppermute | solution.py:396
  70.5 11.1 %collective-permute-start.19 = (bf16[512,128]{1,0:T(8,128)(2,1)S(1)}, bf16[512,128]{1,0:T(8,128)(2,1)S(1)}, u32[]{:S(2)}, u32[]{:S(2)}) collective-permute-start(bf16[512,128]{1,0:T(8,128)(2,1)S(1)} %get-tuple-element.159), channel_id=1, source_target_pairs={{0,8},{1,9},{2,10},{3,11},{4,12},{5,13},{6,14},{7,15},{8,0},{9,1},... | collective-permute-start | bytes 393224 | tf_op jit(solution)/shard_map/ppermute | solution.py:396
  74.0 6.4 %collective-permute-start.17 = (bf16[128,256]{1,0:T(8,128)(2,1)S(1)}, bf16[128,256]{1,0:T(8,128)(2,1)S(1)}, u32[]{:S(2)}, u32[]{:S(2)}) collective-permute-start(bf16[128,256]{1,0:T(8,128)(2,1)S(1)} %get-tuple-element.155), channel_id=1, source_target_pairs={{4,0},{8,4},{12,8},{5,1},{9,5},{13,9},{6,2},{10,6},{14,10},{7,3},{... | collective-permute-start | bytes 196616 | tf_op jit(solution)/shard_map/ppermute | solution.py:420
  75.3 5.1 %collective-permute-start.18 = (bf16[128,256]{1,0:T(8,128)(2,1)S(1)}, bf16[128,256]{1,0:T(8,128)(2,1)S(1)}, u32[]{:S(2)}, u32[]{:S(2)}) collective-permute-start(bf16[128,256]{1,0:T(8,128)(2,1)S(1)} %get-tuple-element.156), channel_id=1, source_target_pairs={{0,2},{2,0},{1,3},{3,1},{4,6},{6,4},{5,7},{7,5},{8,10},{10,8},{9,1... | collective-permute-start | bytes 196616 | tf_op jit(solution)/shard_map/ppermute | solution.py:383
  76.2 6.1 %collective-permute-start.21 = (bf16[512,128]{1,0:T(8,128)(2,1)S(1)}, bf16[512,128]{1,0:T(8,128)(2,1)S(1)}, u32[]{:S(2)}, u32[]{:S(2)}) collective-permute-start(bf16[512,128]{1,0:T(8,128)(2,1)S(1)} %get-tuple-element.162), channel_id=1, source_target_pairs={{0,4},{1,3},{2,6},{3,1},{4,0},{5,7},{6,2},{7,5},{8,12},{9,11},{10,... | collective-permute-start | bytes 393224 | tf_op jit(solution)/shard_map/ppermute | solution.py:396
  79.0 7.3 %collective-permute-start.20 = (bf16[512,128]{1,0:T(8,128)(2,1)S(1)}, bf16[512,128]{1,0:T(8,128)(2,1)S(1)}, u32[]{:S(2)}, u32[]{:S(2)}) collective-permute-start(bf16[512,128]{1,0:T(8,128)(2,1)S(1)} %get-tuple-element.161), channel_id=1, source_target_pairs={{0,8},{1,9},{2,10},{3,11},{4,12},{5,13},{6,14},{7,15},{8,0},{9,1},... | collective-permute-start | bytes 393224 | tf_op jit(solution)/shard_map/ppermute | solution.py:396
  81.6 5.0 %collective-permute-start.22 = (bf16[512,128]{1,0:T(8,128)(2,1)S(1)}, bf16[512,128]{1,0:T(8,128)(2,1)S(1)}, u32[]{:S(2)}, u32[]{:S(2)}) collective-permute-start(bf16[512,128]{1,0:T(8,128)(2,1)S(1)} %get-tuple-element.164), channel_id=1, source_target_pairs={{0,2},{1,5},{2,0},{3,7},{4,6},{5,1},{6,4},{7,3},{8,10},{9,13},{10,... | collective-permute-start | bytes 393224 | tf_op jit(solution)/shard_map/ppermute | solution.py:396
  86.7 11.6 %collective-permute-start.23 = (bf16[1536,128]{1,0:T(8,128)(2,1)S(1)}, bf16[1536,128]{1,0:T(8,128)(2,1)S(1)}, u32[]{:S(2)}, u32[]{:S(2)}) collective-permute-start(bf16[1536,128]{1,0:T(8,128)(2,1)S(1)} %get-tuple-element.166), channel_id=1, source_target_pairs={{0,4},{1,3},{2,6},{3,1},{4,0},{5,7},{6,2},{7,5},{8,12},{9,11},{10,... | collective-permute-start | bytes 1179656 | tf_op jit(solution)/shard_map/ppermute | solution.py:396
  89.9 8.6 %collective-permute-start.24 = (bf16[1024,128]{1,0:T(8,128)(2,1)S(1)}, bf16[1024,128]{1,0:T(8,128)(2,1)S(1)}, u32[]{:S(2)}, u32[]{:S(2)}) collective-permute-start(bf16[1024,128]{1,0:T(8,128)(2,1)S(1)} %get-tuple-element.168), channel_id=1, source_target_pairs={{0,2},{1,5},{2,0},{3,7},{4,6},{5,1},{6,4},{7,3},{8,10},{9,13},{10,... | collective-permute-start | bytes 786440 | tf_op jit(solution)/shard_map/ppermute | solution.py:396
  98.4 6.4 %collective-permute-start.25 = (bf16[1024,128]{1,0:T(8,128)(2,1)S(1)}, bf16[1024,128]{1,0:T(8,128)(2,1)S(1)}, u32[]{:S(2)}, u32[]{:S(2)}) collective-permute-start(bf16[1024,128]{1,0:T(8,128)(2,1)S(1)} %get-tuple-element.176), channel_id=1, source_target_pairs={{0,2},{1,5},{2,0},{3,7},{4,6},{5,1},{6,4},{7,3},{8,10},{9,13},{10,... | collective-permute-start | bytes 786440 | tf_op jit(solution)/shard_map/ppermute | solution.py:396
  (3 other events, 3.1 us)

commit v8 on v7

--- a/solution.py
+++ b/solution.py
@@ -27,12 +27,12 @@
 LIMIT = 24 * 1024 * 1024
 
 
-def call(body, outs, ins, flops, scratch=(), name=None, after=(), bytes_accessed=4_000_000):
+def call(body, outs, ins, flops, scratch=(), name=None, after=(), bytes_accessed=4_000_000, scalars=None):
     skipped = len(after)
     return pl.pallas_call(
         lambda *refs: body(*refs[skipped:]),
         out_shape=[jax.ShapeDtypeStruct(s, d) for s, d in outs],
-        in_specs=[ANY] * skipped + [SMEM if x.ndim == 2 and x.shape[1] == 4 else VMEM for x in ins],
+        in_specs=[ANY] * skipped + [SMEM if x is scalars else VMEM for x in ins],
         out_specs=[VMEM] * len(outs),
         scratch_shapes=list(scratch),
         compiler_params=pltpu.CompilerParams(vmem_limit_bytes=LIMIT),
@@ -82,9 +82,10 @@
 
 
 def setup_kernel(groups, pairs, features, sent, *refs):
-    pick, spread, pick_self = refs[:3]
-    sends = refs[3:]
+    pick, spread, pick_self, held = refs[:4]
+    sends = refs[4:]
     rows = features.shape[0]
+    held[...] = features[...]
     b, feat = lax.axis_index("basin"), lax.axis_index("feat")
     for route in range(-1, 2 * pairs):
         if route == 0:
@@ -115,14 +116,15 @@
         send[...] = mm(pick[i * BLOCK : (i + 1) * BLOCK, :], features[...]).astype(BF16)
 
 
-def build_adjacency(groups, rows, index, values, pick_self, outs, acc):
-    local, local_t, remote, remote_t = outs
+def adjacency_kernel(groups, sources, values, pick_self, _, *refs):
+    local, local_t, remote, remote_t, acc = refs
+    rows = local.shape[0]
     own = rows // BLOCK
     b = lax.axis_index("basin")
     acc[...] = jnp.zeros_like(acc)
     for k in range(own):
-        for t in range(index.shape[1]):
-            v = index[k, t]
+        for t in range(values.shape[1]):
+            v = sources[t, k]
             route = jnp.where(v == own, 0, lax.rem(b + groups - (v - own - 1), groups))
             far = jnp.where((v > own) & (route == 0), own, own + 1 + route)
             at = jnp.where(v < own, v, far)
@@ -142,13 +144,6 @@
     halves = [(wi0[layer], wo0[layer]), (wi1[layer], wo1[layer])]
     for r in range(0, inputs.shape[0], 256):
         msg[r : r + 256, :] = message_of(inputs[r : r + 256, :], halves)
-
-
-def first_kernel(groups, *refs):
-    inputs, pick_self, index, values = refs[:4]
-    weights, msg, outs = refs[4:8], refs[8], refs[9:13]
-    own_messages(0, inputs, weights, msg)
-    build_adjacency(groups, inputs.shape[0], index, values, pick_self, outs, refs[13])
 
 
 def local_kernel(layer, *refs):
@@ -443,40 +438,41 @@
     ffn = 4 * latent * 2 * half
 
     live = jnp.arange(BLOCK, dtype=jnp.int32)[None, :] < send_count[0][:, None]
-    pick, spread, pick_self, *sends = call(
+    sent = jnp.where(live, send_rows[0], -1)
+    sources = block_index.T
+    pick, spread, pick_self, features, *sends = call(
         functools.partial(setup_kernel, groups, pairs),
-        [act16(pairs * BLOCK, rows), act16(rows, far_rows), act16(BLOCK, rows)]
+        [act16(pairs * BLOCK, rows), act16(rows, far_rows), act16(BLOCK, rows), act16(rows)]
         + [act16(BLOCK)] * pairs,
-        [features, jnp.where(live, send_rows[0], -1)],
+        [features, sent],
         2 * rows * far_rows * latent,
         name="setup",
     )
     weights = (w_in, wi1, w_out, wo1)
-    msg, local, local_t, remote, remote_t = [None] * 5
     inputs = [features]
     totals = []
     mine = []
     others = []
     for layer in range(layers):
         mine.append(forward(sends))
+        (msg,) = call(
+            functools.partial(local_kernel, layer),
+            [act16(rows)],
+            [inputs[layer], *weights],
+            rows * ffn,
+            name=f"local{layer}",
+        )
         if layer == 0:
-            msg, local, local_t, remote, remote_t = call(
-                functools.partial(first_kernel, groups),
-                [act16(rows), act16(rows, rows), act16(rows, rows)]
-                + [act16(rows, far_rows), act16(far_rows, rows)],
-                [features, pick_self, block_index, block_values, *weights],
-                rows * ffn + 2 * rows * rows * BLOCK,
+            local, local_t, remote, remote_t = call(
+                functools.partial(adjacency_kernel, groups),
+                [act16(rows, rows), act16(rows, rows), act16(rows, far_rows), act16(far_rows, rows)],
+                [sources, block_values, pick_self, msg],
+                2 * rows * rows * BLOCK,
                 scratch=[pltpu.VMEM((rows, rows + BLOCK + far_rows), F32)],
-                name="first",
+                name="adjacency",
+                scalars=sources,
             )
-        else:
-            (msg,) = call(
-                functools.partial(local_kernel, layer),
-                [act16(rows)],
-                [inputs[layer], *weights],
-                rows * ffn,
-                name=f"local{layer}",
-            )
+            mine[0], local = lax.optimization_barrier((mine[0], local))
         mine[layer], msg = lax.optimization_barrier((mine[layer], msg))
         others.append(other_core(mine[layer]))
         (mixed,) = call(
@@ -599,14 +595,14 @@
         ready = [sums[0]]
         if layers > 1 and sums[1].done < count and sums[1].next()[1] == sums[0].next()[1]:
             ready.append(sums[1])
+        if sums[0].done == len(stages[0]):
+            at = at + [sums[above].got[0] for above in range(2, layers)]
         at = sum_step(ready, at)
-        if grad is None and sums[0].done == 3:
+        if grad is None and sums[0].done == len(stages[0]) + 1:
             grad, token = join(0, state, at)
             at = [token]
-        for layer in range(1, layers):
+        for layer in range(1, layers)[:: 1 if sums[0].done < len(stages[0]) else -1]:
             if sums[layer] not in ready and sums[layer].done < count:
-                if layer > 1 and sums[0].done == len(stages[0]):
-                    at = [*at, sums[0].got[0]]
                 at = sum_step([sums[layer]], at)
     written = []
     for layer in reversed(range(layers)):

time: 107 us -> 109 us (1.019)
  starting transfers between devices: 40.9 us -> 45.8 us
  local copies, waits for them, and re-layouts: 6.18 us -> 3.28 us
    ppermute x15, waiting for transfers between devices: 22.3 us -> 17 us  [over_mesh(): return lax.ppermute(x, ('chain', 'basin', 'feat'), perm)]
    ppermute x3, waiting for transfers between devices: 3.56 us -> 8.78 us  [backward(): up = lax.ppermute(grads[0], 'chain', [(c, c - 1) for c in range(1, chain)])]
    ppermute x15, starting transfers between devices: 33.1 us -> 37.7 us  [over_mesh(): return lax.ppermute(x, ('chain', 'basin', 'feat'), perm)]
    unnamed x19 -> x16, local copies, waits for them, and re-layouts: 6.18 us -> 3.28 us
    pallas_call x28 -> x29, Pallas kernels: 27.1 us -> 27.5 us  [call(): pl.pallas_call(lambda *refs: body(*refs[skipped:]), out_shape=[jax.ShapeD...]
where the time goes in v8:
time: 109 us
  starting transfers between devices  45.8 us (42%)
  Pallas kernels  31.5 us (29%)
  waiting for transfers between devices  26.6 us (24%)
  local copies, waits for them, and re-layouts  3.28 us (3%)
  between operations  1.17 us (1%)
    ppermute x15, starting transfers between devices, over_mesh(): return lax.ppermute(x, ('chain', 'basin', 'feat'), perm)  37.7 us
    pallas_call x29, Pallas kernels, call(): pl.pallas_call(lambda *refs: body(*refs[skipped:]), out_shape=[jax.ShapeD...  27.5 us
    ppermute x15, waiting for transfers between devices, over_mesh(): return lax.ppermute(x, ('chain', 'basin', 'feat'), perm)  17 us
    ppermute x3, waiting for transfers between devices, backward(): up = lax.ppermute(grads[0], 'chain', [(c, c - 1) for c in range(1, chain)])  8.78 us
    ppermute x8, starting transfers between devices, around(): return lax.ppermute(x, axis, [(i, (i + distance) % n) for i in range(n)])  4.08 us
    ppermute x3, starting transfers between devices, backward(): up = lax.ppermute(grads[0], 'chain', [(c, c - 1) for c in range(1, chain)])  4.04 us
    pallas_call x3, Pallas kernels, write(): pl.pallas_call(functools.partial(write_kernel, layer, stages[layer % 2][0...  4 us
    unnamed x16, local copies, waits for them, and re-layouts  3.28 us
  transfers between devices with their start and end apart: 26, of which 14 were waited for; matrix products, arithmetic and copies ran while one was open for 1% of the time, Pallas kernels for 23%

profile of v8, /device:TPU:0, one launch (start us, length us, event | category | flops | bytes accessed | tf_op | source)
XLA Modules:
  0.0 109.1 jit_solution(13834643106772748587)
XLA Ops:
  3.6 4.9 %collective-permute-start = (bf16[128,256]{1,0:T(8,128)(2,1)S(1)}, bf16[128,256]{1,0:T(8,128)(2,1)S(1)}, u32[]{:S(2)}, u32[]{:S(2)}) collective-permute-start(bf16[128,256]{1,0:T(8,128)(2,1)S(1)} %get-tuple-element.94), channel_id=1, source_target_pairs={{0,4},{1,3},{2,6},{3,1},{4,8},{5,7},{6,10},{7,5},{8,12},{9,11},{10... | collective-permute-start | bytes 196616 | tf_op jit(solution)/shard_map/ppermute | solution.py:391
  12.1 1.6 %adjacency.1 = (bf16[768,768]{1,0:T(8,128)(2,1)S(1)}, bf16[768,768]{1,0:T(8,128)(2,1)S(1)}, bf16[768,256]{1,0:T(8,128)(2,1)S(1)}, bf16[256,768]{1,0:T(8,128)(2,1)S(1)}) custom-call(s32[4,6]{1,0:T(4,128)S(1)} %bitcast.4, bf16[6,4,128,128]{3,2,1,0:T(8,128)(2,1)S(1)} %copy-done.5, bf16[128,768]{1,0:T(8,128)(2,1)S(1)} %get-tuple-element.95.refs_2_, ...), custom_call_target="tpu_custom_call" | custom-call | flops 150994944 | bytes 4000000 | tf_op jit(solution)/shard_map/adjacency/pallas_call | solution.py:32
  16.1 3.5 %collective-permute-start.4 = (bf16[128,256]{1,0:T(8,128)(2,1)S(1)}, bf16[128,256]{1,0:T(8,128)(2,1)S(1)}, u32[]{:S(2)}, u32[]{:S(2)}) collective-permute-start(bf16[128,256]{1,0:T(8,128)(2,1)S(1)} %get-tuple-element.104), channel_id=1, source_target_pairs={{0,4},{1,3},{2,6},{3,1},{4,8},{5,7},{6,10},{7,5},{8,12},{9,11},{10... | collective-permute-start | bytes 196616 | tf_op jit(solution)/shard_map/ppermute | solution.py:391
  19.6 1.2 %local1.1.refs_1_ = bf16[768,256]{1,0:T(8,128)(2,1)S(1)} custom-call(bf16[768,256]{1,0:T(8,128)(2,1)S(1)} %get-tuple-element.105.refs_0_.refs_2_, bf16[3,256,512]{2,1,0:T(8,128)(2,1)S(1)} %copy-done.1, bf16[3,256,512]{2,1,0:T(8,128)(2,1)S(1)} %collective-permute-done.1.refs_2_.refs_4_.refs_5_.refs_6_.refs_7_, bf16[3,512,256]{2,1,0:T(8,128)(2,1)S(1)} %copy-done.3, ...), custom_call_target="tpu_custom_call" | custom-call | flops 805306368 | bytes 4000000 | tf_op jit(solution)/shard_map/local1/pallas_call | solution.py:32
  23.8 4.3 %collective-permute-start.6 = (bf16[128,256]{1,0:T(8,128)(2,1)S(1)}, bf16[128,256]{1,0:T(8,128)(2,1)S(1)}, u32[]{:S(2)}, u32[]{:S(2)}) collective-permute-start(bf16[128,256]{1,0:T(8,128)(2,1)S(1)} %get-tuple-element.109), channel_id=1, source_target_pairs={{0,4},{1,3},{2,6},{3,1},{4,8},{5,7},{6,10},{7,5},{8,12},{9,11},{10... | collective-permute-start | bytes 196616 | tf_op jit(solution)/shard_map/ppermute | solution.py:391
  31.2 2.1 %turn.1 = (f32[768,256]{1,0:T(8,128)S(1)}, bf16[768,256]{1,0:T(8,128)(2,1)S(1)}, bf16[256,256]{1,0:T(8,128)(2,1)S(1)}, bf16[256,256]{1,0:T(8,128)(2,1)S(1)}, bf1...) custom-call(f32[768,256]{1,0:T(8,128)S(1)} %get-tuple-element.108.re, ...), custom_call_target="tpu_custom_call" | custom-call | flops 536870912 | bytes 4000000 | tf_op jit(solution)/shard_map/turn/pallas_call | solution.py:32
  33.2 1.5 %collective-permute-start.8 = (bf16[128,256]{1,0:T(8,128)(2,1)S(1)}, bf16[128,256]{1,0:T(8,128)(2,1)S(1)}, u32[]{:S(2)}, u32[]{:S(2)}) collective-permute-start(bf16[128,256]{1,0:T(8,128)(2,1)S(1)} %get-tuple-element.121), channel_id=1, source_target_pairs={{4,0},{8,4},{12,8},{5,1},{9,5},{13,9},{6,2},{10,6},{14,10},{7,3},{... | collective-permute-start | bytes 196616 | tf_op jit(solution)/shard_map/ppermute | solution.py:415
  34.7 1.6 %collective-permute-start.9 = (bf16[128,256]{1,0:T(8,128)(2,1)S(1)}, bf16[128,256]{1,0:T(8,128)(2,1)S(1)}, u32[]{:S(2)}, u32[]{:S(2)}) collective-permute-start(bf16[128,256]{1,0:T(8,128)(2,1)S(1)} %get-tuple-element.122), channel_id=1, source_target_pairs={{0,2},{2,0},{1,3},{3,1},{4,6},{6,4},{5,7},{7,5},{8,10},{10,8},{9,1... | collective-permute-start | bytes 196616 | tf_op jit(solution)/shard_map/ppermute | solution.py:378
  36.3 3.0 %back2.1 = (f32[768,256]{1,0:T(8,128)S(1)}, f32[2048,128]{1,0:T(8,128)S(1)}) custom-call(bf16[768,256]{1,0:T(8,128)(2,1)S(1)} %get-tuple-element.114.refs_0_, bf16[768,256]{1,0:T(8,128)(2,1)S(1)} %get-tuple-element.110.refs_0_.refs_1_, bf16[768,768]{1,0:T(8,128)(2,1)S(1)} %get-tuple-element.115.refs_2_.refs_3_, bf16[3,256,512]{2,1,0:T(8,128)(2,1)S(1)} %copy-done.1, ...), custom_call_target="tpu_custom_call" | custom-call | flops 2717908992 | bytes 4000000 | tf_op jit(solution)/shard_map/back2/pallas_call | solution.py:32
  40.1 1.6 %collective-permute-start.12 = (bf16[1024,128]{1,0:T(8,128)(2,1)S(1)}, bf16[1024,128]{1,0:T(8,128)(2,1)S(1)}, u32[]{:S(2)}, u32[]{:S(2)}) collective-permute-start(bf16[1024,128]{1,0:T(8,128)(2,1)S(1)} %get-tuple-element.136), channel_id=1, source_target_pairs={{0,2},{1,5},{2,0},{3,7},{4,6},{5,1},{6,4},{7,3},{8,10},{9,13},{10,... | collective-permute-start | bytes 786440 | tf_op jit(solution)/shard_map/ppermute | solution.py:391
  41.7 1.6 %join2.1 = (f32[768,256]{1,0:T(8,128)S(1)}, bf16[768,256]{1,0:T(8,128)(2,1)S(1)}, bf16[256,256]{1,0:T(8,128)(2,1)S(1)}, bf16[256,256]{1,0:T(8,128)(2,1)S(1)}, bf...) custom-call(f32[1024,128]{1,0:T(8,128)S(1)} %get-tuple-element.124.r, ...), custom_call_target="tpu_custom_call" | custom-call | flops 536870912 | bytes 4000000 | tf_op jit(solution)/shard_map/join2/pallas_call | solution.py:32
  43.2 1.3 %collective-permute-start.10 = (bf16[128,256]{1,0:T(8,128)(2,1)S(1)}, bf16[128,256]{1,0:T(8,128)(2,1)S(1)}, u32[]{:S(2)}, u32[]{:S(2)}) collective-permute-start(bf16[128,256]{1,0:T(8,128)(2,1)S(1)} %get-tuple-element.133), channel_id=1, source_target_pairs={{4,0},{8,4},{12,8},{5,1},{9,5},{13,9},{6,2},{10,6},{14,10},{7,3},{... | collective-permute-start | bytes 196616 | tf_op jit(solution)/shard_map/ppermute | solution.py:415
  45.1 3.0 %back1.1 = (f32[768,256]{1,0:T(8,128)S(1)}, f32[2048,128]{1,0:T(8,128)S(1)}) custom-call(bf16[768,256]{1,0:T(8,128)(2,1)S(1)} %get-tuple-element.127.refs_0_.refs_1_, bf16[768,256]{1,0:T(8,128)(2,1)S(1)} %get-tuple-element.127.refs_0_.refs_1_, bf16[768,256]{1,0:T(8,128)(2,1)S(1)} %get-tuple-element.105.refs_0_.refs_2_, ...), custom_call_target="tpu_custom_call" | custom-call | flops 2717908992 | bytes 4000000 | tf_op jit(solution)/shard_map/back1/pallas_call | solution.py:32
  48.2 1.5 %collective-permute-done.10.refs_1_.refs_10_ = bf16[128,256]{1,0:T(8,128)(2,1)S(1)} collective-permute-done((bf16[128,256]{1,0:T(8,128)(2,1)S(1)}, bf16[128,256]{1,0:T(8,128)(2,1)S(1)}, u32[]{:S(2)}, u32[]{:S(2)}) %collective-permute-start.10) | collective-permute-done | bytes 65568 | tf_op jit(solution)/shard_map/ppermute | solution.py:415
  49.8 1.9 %collective-permute-start.13 = (bf16[1536,128]{1,0:T(8,128)(2,1)S(1)}, bf16[1536,128]{1,0:T(8,128)(2,1)S(1)}, u32[]{:S(2)}, u32[]{:S(2)}) collective-permute-start(bf16[1536,128]{1,0:T(8,128)(2,1)S(1)} %get-tuple-element.146), channel_id=1, source_target_pairs={{0,4},{1,3},{2,6},{3,1},{4,0},{5,7},{6,2},{7,5},{8,12},{9,11},{10,... | collective-permute-start | bytes 1179656 | tf_op jit(solution)/shard_map/ppermute | solution.py:391
  51.7 1.8 %join1.1 = (f32[768,256]{1,0:T(8,128)S(1)}, bf16[768,256]{1,0:T(8,128)(2,1)S(1)}, bf16[256,256]{1,0:T(8,128)(2,1)S(1)}, bf16[256,256]{1,0:T(8,128)(2,1)S(1)}, bf...) custom-call(f32[1024,128]{1,0:T(8,128)S(1)} %get-tuple-element.137.r, ...), custom_call_target="tpu_custom_call" | custom-call | flops 536870912 | bytes 4000000 | tf_op jit(solution)/shard_map/join1/pallas_call | solution.py:32
  53.5 3.0 %back0.1 = (f32[768,256]{1,0:T(8,128)S(1)}, f32[2048,128]{1,0:T(8,128)S(1)}) custom-call(bf16[768,256]{1,0:T(8,128)(2,1)S(1)} %get-tuple-element.139.refs_0_.refs_1_, bf16[768,256]{1,0:T(8,128)(2,1)S(1)} %get-tuple-element.139.refs_0_.refs_1_, bf16[768,256]{1,0:T(8,128)(2,1)S(1)} %get-tuple-element.93.refs_0_.refs_2_, ...), custom_call_target="tpu_custom_call" | custom-call | flops 2717908992 | bytes 4000000 | tf_op jit(solution)/shard_map/back0/pallas_call | solution.py:32
  58.6 3.5 %collective-permute-start.15 = (bf16[512,128]{1,0:T(8,128)(2,1)S(1)}, bf16[512,128]{1,0:T(8,128)(2,1)S(1)}, u32[]{:S(2)}, u32[]{:S(2)}) collective-permute-start(bf16[512,128]{1,0:T(8,128)(2,1)S(1)} %get-tuple-element.154), channel_id=1, source_target_pairs={{0,8},{1,9},{2,10},{3,11},{4,12},{5,13},{6,14},{7,15},{8,0},{9,1},... | collective-permute-start | bytes 393224 | tf_op jit(solution)/shard_map/ppermute | solution.py:391
  62.1 3.5 %collective-permute-done.14.refs_2_ = bf16[1536,128]{1,0:T(8,128)(2,1)S(1)} collective-permute-done((bf16[1536,128]{1,0:T(8,128)(2,1)S(1)}, bf16[1536,128]{1,0:T(8,128)(2,1)S(1)}, u32[]{:S(2)}, u32[]{:S(2)}) %collective-permute-start.14) | collective-permute-done | bytes 393248 | tf_op jit(solution)/shard_map/ppermute | solution.py:391
  65.8 1.9 %collective-permute-start.16 = (bf16[512,128]{1,0:T(8,128)(2,1)S(1)}, bf16[512,128]{1,0:T(8,128)(2,1)S(1)}, u32[]{:S(2)}, u32[]{:S(2)}) collective-permute-start(bf16[512,128]{1,0:T(8,128)(2,1)S(1)} %get-tuple-element.156), channel_id=1, source_target_pairs={{0,4},{1,3},{2,6},{3,1},{4,0},{5,7},{6,2},{7,5},{8,12},{9,11},{10,... | collective-permute-start | bytes 393224 | tf_op jit(solution)/shard_map/ppermute | solution.py:391
  68.7 3.2 %collective-permute-start.18 = (bf16[512,128]{1,0:T(8,128)(2,1)S(1)}, bf16[512,128]{1,0:T(8,128)(2,1)S(1)}, u32[]{:S(2)}, u32[]{:S(2)}) collective-permute-start(bf16[512,128]{1,0:T(8,128)(2,1)S(1)} %get-tuple-element.160), channel_id=1, source_target_pairs={{0,8},{1,9},{2,10},{3,11},{4,12},{5,13},{6,14},{7,15},{8,0},{9,1},... | collective-permute-start | bytes 393224 | tf_op jit(solution)/shard_map/ppermute | solution.py:391
  71.9 3.2 %collective-permute-done.17.refs_2_ = bf16[512,128]{1,0:T(8,128)(2,1)S(1)} collective-permute-done((bf16[512,128]{1,0:T(8,128)(2,1)S(1)}, bf16[512,128]{1,0:T(8,128)(2,1)S(1)}, u32[]{:S(2)}, u32[]{:S(2)}) %collective-permute-start.17) | collective-permute-done | bytes 131104 | tf_op jit(solution)/shard_map/ppermute | solution.py:391
  75.5 5.6 %collective-permute-start.20 = (bf16[512,128]{1,0:T(8,128)(2,1)S(1)}, bf16[512,128]{1,0:T(8,128)(2,1)S(1)}, u32[]{:S(2)}, u32[]{:S(2)}) collective-permute-start(bf16[512,128]{1,0:T(8,128)(2,1)S(1)} %get-tuple-element.163), channel_id=1, source_target_pairs={{0,8},{1,9},{2,10},{3,11},{4,12},{5,13},{6,14},{7,15},{8,0},{9,1},... | collective-permute-start | bytes 393224 | tf_op jit(solution)/shard_map/ppermute | solution.py:391
  82.4 1.6 %collective-permute-done.20.refs_3_ = bf16[512,128]{1,0:T(8,128)(2,1)S(1)} collective-permute-done((bf16[512,128]{1,0:T(8,128)(2,1)S(1)}, bf16[512,128]{1,0:T(8,128)(2,1)S(1)}, u32[]{:S(2)}, u32[]{:S(2)}) %collective-permute-start.20) | collective-permute-done | bytes 131104 | tf_op jit(solution)/shard_map/ppermute | solution.py:391
  84.0 3.5 %collective-permute-done.21.refs_5_ = bf16[512,128]{1,0:T(8,128)(2,1)S(1)} collective-permute-done((bf16[512,128]{1,0:T(8,128)(2,1)S(1)}, bf16[512,128]{1,0:T(8,128)(2,1)S(1)}, u32[]{:S(2)}, u32[]{:S(2)}) %collective-permute-start.21) | collective-permute-done | bytes 131104 | tf_op jit(solution)/shard_map/ppermute | solution.py:391
  87.6 2.8 %collective-permute-start.24 = (bf16[1536,128]{1,0:T(8,128)(2,1)S(1)}, bf16[1536,128]{1,0:T(8,128)(2,1)S(1)}, u32[]{:S(2)}, u32[]{:S(2)}) collective-permute-start(bf16[1536,128]{1,0:T(8,128)(2,1)S(1)} %get-tuple-element.171), channel_id=1, source_target_pairs={{0,4},{1,3},{2,6},{3,1},{4,0},{5,7},{6,2},{7,5},{8,12},{9,11},{10,... | collective-permute-start | bytes 1179656 | tf_op jit(solution)/shard_map/ppermute | solution.py:391
  90.4 1.3 %collective-permute-start.22 = (bf16[128,256]{1,0:T(8,128)(2,1)S(1)}, bf16[128,256]{1,0:T(8,128)(2,1)S(1)}, u32[]{:S(2)}, u32[]{:S(2)}) collective-permute-start(bf16[128,256]{1,0:T(8,128)(2,1)S(1)} %get-tuple-element.167), channel_id=1, source_target_pairs={{4,0},{8,4},{12,8},{5,1},{9,5},{13,9},{6,2},{10,6},{14,10},{7,3},{... | collective-permute-start | bytes 196616 | tf_op jit(solution)/shard_map/ppermute | solution.py:415
  91.7 1.2 %collective-permute-start.23 = (bf16[128,256]{1,0:T(8,128)(2,1)S(1)}, bf16[128,256]{1,0:T(8,128)(2,1)S(1)}, u32[]{:S(2)}, u32[]{:S(2)}) collective-permute-start(bf16[128,256]{1,0:T(8,128)(2,1)S(1)} %get-tuple-element.168), channel_id=1, source_target_pairs={{0,2},{2,0},{1,3},{3,1},{4,6},{6,4},{5,7},{7,5},{8,10},{10,8},{9,1... | collective-permute-start | bytes 196616 | tf_op jit(solution)/shard_map/ppermute | solution.py:378
  92.9 6.6 %collective-permute-done.22.refs_4_ = bf16[128,256]{1,0:T(8,128)(2,1)S(1)} collective-permute-done((bf16[128,256]{1,0:T(8,128)(2,1)S(1)}, bf16[128,256]{1,0:T(8,128)(2,1)S(1)}, u32[]{:S(2)}, u32[]{:S(2)}) %collective-permute-start.22) | collective-permute-done | bytes 65568 | tf_op jit(solution)/shard_map/ppermute | solution.py:415
  100.7 1.4 %collective-permute-start.25 = (bf16[1024,128]{1,0:T(8,128)(2,1)S(1)}, bf16[1024,128]{1,0:T(8,128)(2,1)S(1)}, u32[]{:S(2)}, u32[]{:S(2)}) collective-permute-start(bf16[1024,128]{1,0:T(8,128)(2,1)S(1)} %get-tuple-element.180), channel_id=1, source_target_pairs={{0,2},{1,5},{2,0},{3,7},{4,6},{5,1},{6,4},{7,3},{8,10},{9,13},{10,... | collective-permute-start | bytes 786440 | tf_op jit(solution)/shard_map/ppermute | solution.py:391
  104.4 2.7 %collective-permute-done.25.refs_4_ = bf16[1024,128]{1,0:T(8,128)(2,1)S(1)} collective-permute-done((bf16[1024,128]{1,0:T(8,128)(2,1)S(1)}, bf16[1024,128]{1,0:T(8,128)(2,1)S(1)}, u32[]{:S(2)}, u32[]{:S(2)}) %collective-permute-start.25) | collective-permute-done | bytes 262176 | tf_op jit(solution)/shard_map/ppermute | solution.py:391
  107.1 1.7 %write0.1 = (f32[3,256,512]{2,1,0:T(8,128)}, f32[3,512,256]{2,1,0:T(8,128)}, f32[8,128]{1,0:T(8,128)}) custom-call(f32[3,256,512]{2,1,0:T(8,128)} %get-tuple-element.177.refs_0_, f32[3,512,256]{2,1,0:T(8,128)} %get-tuple-element.178.refs_1_, f32[8,128]{1,0:T(8,128)S(1)} %get-tuple-element.179.refs_2_, ...), custom_call_target="tpu_custom_call", output_to_operand_aliasing={{0}: (0, {}), {1}: (1, {})} | custom-call | flops 1 | bytes 1 | tf_op jit(solution)/shard_map/write0/pallas_call | solution.py:561
  (69 shorter events, 24.8 us)
Async XLA Ops:
  0.6 7.9 %collective-permute-start.1 = (bf16[3,256,512]{2,1,0:T(8,128)(2,1)}, bf16[3,256,512]{2,1,0:T(8,128)(2,1)S(1)}, u32[]{:S(2)}, u32[]{:S(2)}) collective-permute-start(bf16[3,256,512]{2,1,0:T(8,128)(2,1)} %refs_4_.9), channel_id=1, source_target_pairs={{0,1},{1,0},{2,3},{3,2},{4,5},{5,4},{6,7},{7,6},{8,9},{9,8},{10,11... | collective-permute-start | bytes 2359304 | tf_op jit(solution)/shard_map/ppermute | solution.py:378
  1.1 7.4 %collective-permute-start.2 = (bf16[3,512,256]{2,1,0:T(8,128)(2,1)}, bf16[3,512,256]{2,1,0:T(8,128)(2,1)S(1)}, u32[]{:S(2)}, u32[]{:S(2)}) collective-permute-start(bf16[3,512,256]{2,1,0:T(8,128)(2,1)} %refs_6_.11), channel_id=1, source_target_pairs={{0,1},{1,0},{2,3},{3,2},{4,5},{5,4},{6,7},{7,6},{8,9},{9,8},{10,11... | collective-permute-start | bytes 2359304 | tf_op jit(solution)/shard_map/ppermute | solution.py:378
  3.6 10.1 %collective-permute-start = (bf16[128,256]{1,0:T(8,128)(2,1)S(1)}, bf16[128,256]{1,0:T(8,128)(2,1)S(1)}, u32[]{:S(2)}, u32[]{:S(2)}) collective-permute-start(bf16[128,256]{1,0:T(8,128)(2,1)S(1)} %get-tuple-element.94), channel_id=1, source_target_pairs={{0,4},{1,3},{2,6},{3,1},{4,8},{5,7},{6,10},{7,5},{8,12},{9,11},{10... | collective-permute-start | bytes 196616 | tf_op jit(solution)/shard_map/ppermute | solution.py:391
  8.5 1.1 %copy-start = (bf16[3,256,512]{2,1,0:T(8,128)(2,1)S(1)}, bf16[3,256,512]{2,1,0:T(8,128)(2,1)}, u32[]{:S(2)}) copy-start(bf16[3,256,512]{2,1,0:T(8,128)(2,1)} %refs_4_.9) | copy-start | bytes 2359300
  10.8 1.3 %copy-start.5 = (bf16[6,4,128,128]{3,2,1,0:T(8,128)(2,1)S(1)}, bf16[6,4,128,128]{3,2,1,0:T(8,128)(2,1)}, u32[]{:S(2)}) copy-start(bf16[6,4,128,128]{3,2,1,0:T(8,128)(2,1)} %refs_1_.5) | copy-start | bytes 2359300
  10.8 1.3 %copy-start.7 = (s32[6,4]{0,1:T(4,128)S(1)}, s32[6,4]{0,1:T(4,128)}, u32[]{:S(2)}) copy-start(s32[6,4]{0,1:T(4,128)} %param.12) | copy-start | bytes 292
  10.8 3.0 %copy-start.3 = (bf16[3,512,256]{2,1,0:T(8,128)(2,1)S(1)}, bf16[3,512,256]{2,1,0:T(8,128)(2,1)}, u32[]{:S(2)}) copy-start(bf16[3,512,256]{2,1,0:T(8,128)(2,1)} %refs_6_.11) | copy-start | bytes 2359300
  12.0 1.7 %copy-start.1 = (bf16[3,256,512]{2,1,0:T(8,128)(2,1)S(1)}, bf16[3,256,512]{2,1,0:T(8,128)(2,1)}, u32[]{:S(2)}) copy-start(bf16[3,256,512]{2,1,0:T(8,128)(2,1)} %refs_4_.9) | copy-start | bytes 2359300
  13.7 1.3 %collective-permute-start.3 = (bf16[128,256]{1,0:T(8,128)(2,1)S(1)}, bf16[128,256]{1,0:T(8,128)(2,1)S(1)}, u32[]{:S(2)}, u32[]{:S(2)}) collective-permute-start(bf16[128,256]{1,0:T(8,128)(2,1)S(1)} %collective-permute-done.refs_7_.refs_12_), channel_id=1, source_target_pairs={{0,1},{1,0},{2,3},{3,2},{4,5},{5,4},{6,7},{7,6},{8,9},{9,8},{10,11... | collective-permute-start | bytes 196616 | tf_op jit(solution)/shard_map/ppermute | solution.py:378
  16.1 5.4 %collective-permute-start.4 = (bf16[128,256]{1,0:T(8,128)(2,1)S(1)}, bf16[128,256]{1,0:T(8,128)(2,1)S(1)}, u32[]{:S(2)}, u32[]{:S(2)}) collective-permute-start(bf16[128,256]{1,0:T(8,128)(2,1)S(1)} %get-tuple-element.104), channel_id=1, source_target_pairs={{0,4},{1,3},{2,6},{3,1},{4,8},{5,7},{6,10},{7,5},{8,12},{9,11},{10... | collective-permute-start | bytes 196616 | tf_op jit(solution)/shard_map/ppermute | solution.py:391
  21.4 1.3 %collective-permute-start.5 = (bf16[128,256]{1,0:T(8,128)(2,1)S(1)}, bf16[128,256]{1,0:T(8,128)(2,1)S(1)}, u32[]{:S(2)}, u32[]{:S(2)}) collective-permute-start(bf16[128,256]{1,0:T(8,128)(2,1)S(1)} %collective-permute-done.4.refs_7_.refs_12_), channel_id=1, source_target_pairs={{0,1},{1,0},{2,3},{3,2},{4,5},{5,4},{6,7},{7,6},{8,9},{9,8},{10,11... | collective-permute-start | bytes 196616 | tf_op jit(solution)/shard_map/ppermute | solution.py:378
  23.8 6.2 %collective-permute-start.6 = (bf16[128,256]{1,0:T(8,128)(2,1)S(1)}, bf16[128,256]{1,0:T(8,128)(2,1)S(1)}, u32[]{:S(2)}, u32[]{:S(2)}) collective-permute-start(bf16[128,256]{1,0:T(8,128)(2,1)S(1)} %get-tuple-element.109), channel_id=1, source_target_pairs={{0,4},{1,3},{2,6},{3,1},{4,8},{5,7},{6,10},{7,5},{8,12},{9,11},{10... | collective-permute-start | bytes 196616 | tf_op jit(solution)/shard_map/ppermute | solution.py:391
  29.3 1.9 %copy-start.4 = (f32[768,256]{1,0:T(8,128)S(1)}, f32[768,256]{1,0:T(8,128)}, u32[]{:S(2)}) copy-start(f32[768,256]{1,0:T(8,128)} %refs_4_.7) | copy-start | bytes 2359300
  29.9 1.3 %collective-permute-start.7 = (bf16[128,256]{1,0:T(8,128)(2,1)S(1)}, bf16[128,256]{1,0:T(8,128)(2,1)S(1)}, u32[]{:S(2)}, u32[]{:S(2)}) collective-permute-start(bf16[128,256]{1,0:T(8,128)(2,1)S(1)} %collective-permute-done.6.refs_7_.refs_9_), channel_id=1, source_target_pairs={{0,1},{1,0},{2,3},{3,2},{4,5},{5,4},{6,7},{7,6},{8,9},{9,8},{10,11... | collective-permute-start | bytes 196616 | tf_op jit(solution)/shard_map/ppermute | solution.py:378
  33.2 6.8 %collective-permute-start.8 = (bf16[128,256]{1,0:T(8,128)(2,1)S(1)}, bf16[128,256]{1,0:T(8,128)(2,1)S(1)}, u32[]{:S(2)}, u32[]{:S(2)}) collective-permute-start(bf16[128,256]{1,0:T(8,128)(2,1)S(1)} %get-tuple-element.121), channel_id=1, source_target_pairs={{4,0},{8,4},{12,8},{5,1},{9,5},{13,9},{6,2},{10,6},{14,10},{7,3},{... | collective-permute-start | bytes 196616 | tf_op jit(solution)/shard_map/ppermute | solution.py:415
  34.7 5.3 %collective-permute-start.9 = (bf16[128,256]{1,0:T(8,128)(2,1)S(1)}, bf16[128,256]{1,0:T(8,128)(2,1)S(1)}, u32[]{:S(2)}, u32[]{:S(2)}) collective-permute-start(bf16[128,256]{1,0:T(8,128)(2,1)S(1)} %get-tuple-element.122), channel_id=1, source_target_pairs={{0,2},{2,0},{1,3},{3,1},{4,6},{6,4},{5,7},{7,5},{8,10},{10,8},{9,1... | collective-permute-start | bytes 196616 | tf_op jit(solution)/shard_map/ppermute | solution.py:378
  40.1 9.5 %collective-permute-start.12 = (bf16[1024,128]{1,0:T(8,128)(2,1)S(1)}, bf16[1024,128]{1,0:T(8,128)(2,1)S(1)}, u32[]{:S(2)}, u32[]{:S(2)}) collective-permute-start(bf16[1024,128]{1,0:T(8,128)(2,1)S(1)} %get-tuple-element.136), channel_id=1, source_target_pairs={{0,2},{1,5},{2,0},{3,7},{4,6},{5,1},{6,4},{7,3},{8,10},{9,13},{10,... | collective-permute-start | bytes 786440 | tf_op jit(solution)/shard_map/ppermute | solution.py:391
  43.2 6.4 %collective-permute-start.10 = (bf16[128,256]{1,0:T(8,128)(2,1)S(1)}, bf16[128,256]{1,0:T(8,128)(2,1)S(1)}, u32[]{:S(2)}, u32[]{:S(2)}) collective-permute-start(bf16[128,256]{1,0:T(8,128)(2,1)S(1)} %get-tuple-element.133), channel_id=1, source_target_pairs={{4,0},{8,4},{12,8},{5,1},{9,5},{13,9},{6,2},{10,6},{14,10},{7,3},{... | collective-permute-start | bytes 196616 | tf_op jit(solution)/shard_map/ppermute | solution.py:415
  44.5 5.1 %collective-permute-start.11 = (bf16[128,256]{1,0:T(8,128)(2,1)S(1)}, bf16[128,256]{1,0:T(8,128)(2,1)S(1)}, u32[]{:S(2)}, u32[]{:S(2)}) collective-permute-start(bf16[128,256]{1,0:T(8,128)(2,1)S(1)} %get-tuple-element.134), channel_id=1, source_target_pairs={{0,2},{2,0},{1,3},{3,1},{4,6},{6,4},{5,7},{7,5},{8,10},{10,8},{9,1... | collective-permute-start | bytes 196616 | tf_op jit(solution)/shard_map/ppermute | solution.py:378
  49.8 7.8 %collective-permute-start.13 = (bf16[1536,128]{1,0:T(8,128)(2,1)S(1)}, bf16[1536,128]{1,0:T(8,128)(2,1)S(1)}, u32[]{:S(2)}, u32[]{:S(2)}) collective-permute-start(bf16[1536,128]{1,0:T(8,128)(2,1)S(1)} %get-tuple-element.146), channel_id=1, source_target_pairs={{0,4},{1,3},{2,6},{3,1},{4,0},{5,7},{6,2},{7,5},{8,12},{9,11},{10,... | collective-permute-start | bytes 1179656 | tf_op jit(solution)/shard_map/ppermute | solution.py:391
  57.8 7.8 %collective-permute-start.14 = (bf16[1536,128]{1,0:T(8,128)(2,1)S(1)}, bf16[1536,128]{1,0:T(8,128)(2,1)S(1)}, u32[]{:S(2)}, u32[]{:S(2)}) collective-permute-start(bf16[1536,128]{1,0:T(8,128)(2,1)S(1)} %get-tuple-element.150), channel_id=1, source_target_pairs={{0,2},{1,5},{2,0},{3,7},{4,6},{5,1},{6,4},{7,3},{8,10},{9,13},{10,... | collective-permute-start | bytes 1179656 | tf_op jit(solution)/shard_map/ppermute | solution.py:391
  58.6 9.1 %collective-permute-start.15 = (bf16[512,128]{1,0:T(8,128)(2,1)S(1)}, bf16[512,128]{1,0:T(8,128)(2,1)S(1)}, u32[]{:S(2)}, u32[]{:S(2)}) collective-permute-start(bf16[512,128]{1,0:T(8,128)(2,1)S(1)} %get-tuple-element.154), channel_id=1, source_target_pairs={{0,8},{1,9},{2,10},{3,11},{4,12},{5,13},{6,14},{7,15},{8,0},{9,1},... | collective-permute-start | bytes 393224 | tf_op jit(solution)/shard_map/ppermute | solution.py:391
  65.8 6.1 %collective-permute-start.16 = (bf16[512,128]{1,0:T(8,128)(2,1)S(1)}, bf16[512,128]{1,0:T(8,128)(2,1)S(1)}, u32[]{:S(2)}, u32[]{:S(2)}) collective-permute-start(bf16[512,128]{1,0:T(8,128)(2,1)S(1)} %get-tuple-element.156), channel_id=1, source_target_pairs={{0,4},{1,3},{2,6},{3,1},{4,0},{5,7},{6,2},{7,5},{8,12},{9,11},{10,... | collective-permute-start | bytes 393224 | tf_op jit(solution)/shard_map/ppermute | solution.py:391
  67.8 7.3 %collective-permute-start.17 = (bf16[512,128]{1,0:T(8,128)(2,1)S(1)}, bf16[512,128]{1,0:T(8,128)(2,1)S(1)}, u32[]{:S(2)}, u32[]{:S(2)}) collective-permute-start(bf16[512,128]{1,0:T(8,128)(2,1)S(1)} %get-tuple-element.158), channel_id=1, source_target_pairs={{0,4},{1,3},{2,6},{3,1},{4,0},{5,7},{6,2},{7,5},{8,12},{9,11},{10,... | collective-permute-start | bytes 393224 | tf_op jit(solution)/shard_map/ppermute | solution.py:391
  68.7 12.4 %collective-permute-start.18 = (bf16[512,128]{1,0:T(8,128)(2,1)S(1)}, bf16[512,128]{1,0:T(8,128)(2,1)S(1)}, u32[]{:S(2)}, u32[]{:S(2)}) collective-permute-start(bf16[512,128]{1,0:T(8,128)(2,1)S(1)} %get-tuple-element.160), channel_id=1, source_target_pairs={{0,8},{1,9},{2,10},{3,11},{4,12},{5,13},{6,14},{7,15},{8,0},{9,1},... | collective-permute-start | bytes 393224 | tf_op jit(solution)/shard_map/ppermute | solution.py:391
  75.2 12.3 %collective-permute-start.19 = (bf16[1024,128]{1,0:T(8,128)(2,1)S(1)}, bf16[1024,128]{1,0:T(8,128)(2,1)S(1)}, u32[]{:S(2)}, u32[]{:S(2)}) collective-permute-start(bf16[1024,128]{1,0:T(8,128)(2,1)S(1)} %get-tuple-element.162), channel_id=1, source_target_pairs={{0,2},{1,5},{2,0},{3,7},{4,6},{5,1},{6,4},{7,3},{8,10},{9,13},{10,... | collective-permute-start | bytes 786440 | tf_op jit(solution)/shard_map/ppermute | solution.py:391
  75.5 8.5 %collective-permute-start.20 = (bf16[512,128]{1,0:T(8,128)(2,1)S(1)}, bf16[512,128]{1,0:T(8,128)(2,1)S(1)}, u32[]{:S(2)}, u32[]{:S(2)}) collective-permute-start(bf16[512,128]{1,0:T(8,128)(2,1)S(1)} %get-tuple-element.163), channel_id=1, source_target_pairs={{0,8},{1,9},{2,10},{3,11},{4,12},{5,13},{6,14},{7,15},{8,0},{9,1},... | collective-permute-start | bytes 393224 | tf_op jit(solution)/shard_map/ppermute | solution.py:391
  81.1 6.4 %collective-permute-start.21 = (bf16[512,128]{1,0:T(8,128)(2,1)S(1)}, bf16[512,128]{1,0:T(8,128)(2,1)S(1)}, u32[]{:S(2)}, u32[]{:S(2)}) collective-permute-start(bf16[512,128]{1,0:T(8,128)(2,1)S(1)} %get-tuple-element.164), channel_id=1, source_target_pairs={{0,2},{1,5},{2,0},{3,7},{4,6},{5,1},{6,4},{7,3},{8,10},{9,13},{10,... | collective-permute-start | bytes 393224 | tf_op jit(solution)/shard_map/ppermute | solution.py:391
  87.6 13.1 %collective-permute-start.24 = (bf16[1536,128]{1,0:T(8,128)(2,1)S(1)}, bf16[1536,128]{1,0:T(8,128)(2,1)S(1)}, u32[]{:S(2)}, u32[]{:S(2)}) collective-permute-start(bf16[1536,128]{1,0:T(8,128)(2,1)S(1)} %get-tuple-element.171), channel_id=1, source_target_pairs={{0,4},{1,3},{2,6},{3,1},{4,0},{5,7},{6,2},{7,5},{8,12},{9,11},{10,... | collective-permute-start | bytes 1179656 | tf_op jit(solution)/shard_map/ppermute | solution.py:391
  90.4 9.1 %collective-permute-start.22 = (bf16[128,256]{1,0:T(8,128)(2,1)S(1)}, bf16[128,256]{1,0:T(8,128)(2,1)S(1)}, u32[]{:S(2)}, u32[]{:S(2)}) collective-permute-start(bf16[128,256]{1,0:T(8,128)(2,1)S(1)} %get-tuple-element.167), channel_id=1, source_target_pairs={{4,0},{8,4},{12,8},{5,1},{9,5},{13,9},{6,2},{10,6},{14,10},{7,3},{... | collective-permute-start | bytes 196616 | tf_op jit(solution)/shard_map/ppermute | solution.py:415
  91.7 7.8 %collective-permute-start.23 = (bf16[128,256]{1,0:T(8,128)(2,1)S(1)}, bf16[128,256]{1,0:T(8,128)(2,1)S(1)}, u32[]{:S(2)}, u32[]{:S(2)}) collective-permute-start(bf16[128,256]{1,0:T(8,128)(2,1)S(1)} %get-tuple-element.168), channel_id=1, source_target_pairs={{0,2},{2,0},{1,3},{3,1},{4,6},{6,4},{5,7},{7,5},{8,10},{10,8},{9,1... | collective-permute-start | bytes 196616 | tf_op jit(solution)/shard_map/ppermute | solution.py:378
  100.7 6.4 %collective-permute-start.25 = (bf16[1024,128]{1,0:T(8,128)(2,1)S(1)}, bf16[1024,128]{1,0:T(8,128)(2,1)S(1)}, u32[]{:S(2)}, u32[]{:S(2)}) collective-permute-start(bf16[1024,128]{1,0:T(8,128)(2,1)S(1)} %get-tuple-element.180), channel_id=1, source_target_pairs={{0,2},{1,5},{2,0},{3,7},{4,6},{5,1},{6,4},{7,3},{8,10},{9,13},{10,... | collective-permute-start | bytes 786440 | tf_op jit(solution)/shard_map/ppermute | solution.py:391
  (2 other events, 2.1 us)

commit v9 on v8

--- a/solution.py
+++ b/solution.py
@@ -513,7 +513,7 @@
     over_basin, over_chain = distances("basin"), distances("chain")
     n = len(over_basin)
     orders = over_basin + over_chain, over_chain[:n] + over_basin + over_chain[n:]
-    stages = list(zip(*orders, strict=True)), list(zip(*orders[::-1], strict=True))
+    stages = list(zip(*orders, strict=True))
     returned = {}
     sums = {}
 
@@ -532,7 +532,7 @@
             name=f"back{layer}",
             after=after,
         )
-        sums[layer] = Sum(whole, stages[layer % 2])
+        sums[layer] = Sum(whole, stages)
         return [outs[0], grad], [grad]
 
     def join(layer, state, after):
@@ -560,7 +560,7 @@
         kept = [*written, *after]
         return pl.pallas_call(
             functools.partial(
-                write_kernel, layer, stages[layer % 2][0], len(kept), sums[layer].got[1]
+                write_kernel, layer, stages[0], len(kept), sums[layer].got[1]
             ),
             out_shape=[
                 jax.ShapeDtypeStruct((layers, latent, half), F32),
@@ -581,28 +581,26 @@
             name=f"write{layer}",
         )(*written, *after, *ready)
 
-    count = 2 * len(stages[0]) - 1
+    count = 2 * len(stages) - 1
     at = []
     for layer in reversed(range(layers)):
         state, at = back(layer, outs, at)
+        arrived = [sums[above].got[0] for above in range(layer + 2, layers)]
+        at = sum_step([sums[layer]], at + returned[layer] + arrived)
         if layer:
-            at = [*at, *returned[layer]]
-            at = sum_step([sums[above] for above in range(layer, layers)], at)
+            for above in range(layer + 1, layers):
+                at = sum_step([sums[above]], at)
             outs = join(layer, state, at)
             at = outs[1:2]
-    grad = None
+    for layer in reversed(range(1, layers)):
+        at = sum_step([sums[layer]], at)
+    grad, token = join(0, state, at)
+    at = sum_step([sums[0]], [token])
     while sums[0].done < count:
-        ready = [sums[0]]
-        if layers > 1 and sums[1].done < count and sums[1].next()[1] == sums[0].next()[1]:
-            ready.append(sums[1])
-        if sums[0].done == len(stages[0]):
-            at = at + [sums[above].got[0] for above in range(2, layers)]
-        at = sum_step(ready, at)
-        if grad is None and sums[0].done == len(stages[0]) + 1:
-            grad, token = join(0, state, at)
-            at = [token]
-        for layer in range(1, layers)[:: 1 if sums[0].done < len(stages[0]) else -1]:
-            if sums[layer] not in ready and sums[layer].done < count:
+        for layer in reversed(range(layers)):
+            if sums[layer].done < count:
+                if layer == 0 and sums[0].done == count - 1:
+                    at = at + [sums[above].got[0] for above in range(2, layers)]
                 at = sum_step([sums[layer]], at)
     written = []
     for layer in reversed(range(layers)):

time: 109 us -> 101 us (0.927)
  waiting for transfers between devices: 26.6 us -> 15.5 us
  starting transfers between devices: 45.8 us -> 48.2 us
    ppermute x3, waiting for transfers between devices: 8.78 us -> 2.21 us  [backward(): up = lax.ppermute(grads[0], 'chain', [(c, c - 1) for c in range(1, chain)])]
    ppermute x15 -> x18, waiting for transfers between devices: 17 us -> 12.5 us  [over_mesh(): return lax.ppermute(x, ('chain', 'basin', 'feat'), perm)]
    ppermute x15 -> x18, starting transfers between devices: 37.7 us -> 39.6 us  [over_mesh(): return lax.ppermute(x, ('chain', 'basin', 'feat'), perm)]
    pallas_call x29 -> x32, Pallas kernels: 27.5 us -> 27.3 us  [call(): pl.pallas_call(lambda *refs: body(*refs[skipped:]), out_shape=[jax.ShapeD...]
  transfers between devices with their start and end apart: 26 -> 29, of which waited for: 14 -> 14; matrix products, arithmetic and copies ran while one was open for 1% -> 1% of each run, Pallas kernels for 23% -> 25%
where the time goes in v9:
time: 101 us; the launch traced here: 100 us
  starting transfers between devices  48.2 us (48%)
  Pallas kernels  31.3 us (31%)
  waiting for transfers between devices  15.5 us (15%)
  local copies, waits for them, and re-layouts  3.28 us (3%)
  between operations  1.21 us (1%)
    ppermute x18, starting transfers between devices, over_mesh(): return lax.ppermute(x, ('chain', 'basin', 'feat'), perm)  39.6 us
    pallas_call x32, Pallas kernels, call(): pl.pallas_call(lambda *refs: body(*refs[skipped:]), out_shape=[jax.ShapeD...  27.3 us
    ppermute x18, waiting for transfers between devices, over_mesh(): return lax.ppermute(x, ('chain', 'basin', 'feat'), perm)  12.5 us
    ppermute x8, starting transfers between devices, around(): return lax.ppermute(x, axis, [(i, (i + distance) % n) for i in range(n)])  4.3 us
    ppermute x3, starting transfers between devices, backward(): up = lax.ppermute(grads[0], 'chain', [(c, c - 1) for c in range(1, chain)])  4.28 us
    pallas_call x3, Pallas kernels, write(): pl.pallas_call(functools.partial(write_kernel, layer, stages[0], len(kept...  4 us
    unnamed x16, local copies, waits for them, and re-layouts  3.28 us
    ppermute x3, waiting for transfers between devices, backward(): up = lax.ppermute(grads[0], 'chain', [(c, c - 1) for c in range(1, chain)])  2.21 us
  transfers between devices with their start and end apart: 29, of which 14 were waited for; matrix products, arithmetic and copies ran while one was open for 1% of the time, Pallas kernels for 25%

profile of v9, /device:TPU:0, one launch (start us, length us, event | category | flops | bytes accessed | tf_op | source)
XLA Modules:
  0.0 100.2 jit_solution(12254511917926941833)
XLA Ops:
  3.6 4.9 %collective-permute-start = (bf16[128,256]{1,0:T(8,128)(2,1)S(1)}, bf16[128,256]{1,0:T(8,128)(2,1)S(1)}, u32[]{:S(2)}, u32[]{:S(2)}) collective-permute-start(bf16[128,256]{1,0:T(8,128)(2,1)S(1)} %get-tuple-element.97), channel_id=1, source_target_pairs={{0,4},{1,3},{2,6},{3,1},{4,8},{5,7},{6,10},{7,5},{8,12},{9,11},{10... | collective-permute-start | bytes 196616 | tf_op jit(solution)/shard_map/ppermute | solution.py:391
  12.1 1.6 %adjacency.1 = (bf16[768,768]{1,0:T(8,128)(2,1)S(1)}, bf16[768,768]{1,0:T(8,128)(2,1)S(1)}, bf16[768,256]{1,0:T(8,128)(2,1)S(1)}, bf16[256,768]{1,0:T(8,128)(2,1)S(1)}) custom-call(s32[4,6]{1,0:T(4,128)S(1)} %bitcast.4, bf16[6,4,128,128]{3,2,1,0:T(8,128)(2,1)S(1)} %copy-done.5, bf16[128,768]{1,0:T(8,128)(2,1)S(1)} %get-tuple-element.98.refs_2_, ...), custom_call_target="tpu_custom_call" | custom-call | flops 150994944 | bytes 4000000 | tf_op jit(solution)/shard_map/adjacency/pallas_call | solution.py:32
  16.1 3.5 %collective-permute-start.4 = (bf16[128,256]{1,0:T(8,128)(2,1)S(1)}, bf16[128,256]{1,0:T(8,128)(2,1)S(1)}, u32[]{:S(2)}, u32[]{:S(2)}) collective-permute-start(bf16[128,256]{1,0:T(8,128)(2,1)S(1)} %get-tuple-element.107), channel_id=1, source_target_pairs={{0,4},{1,3},{2,6},{3,1},{4,8},{5,7},{6,10},{7,5},{8,12},{9,11},{10... | collective-permute-start | bytes 196616 | tf_op jit(solution)/shard_map/ppermute | solution.py:391
  23.8 4.3 %collective-permute-start.6 = (bf16[128,256]{1,0:T(8,128)(2,1)S(1)}, bf16[128,256]{1,0:T(8,128)(2,1)S(1)}, u32[]{:S(2)}, u32[]{:S(2)}) collective-permute-start(bf16[128,256]{1,0:T(8,128)(2,1)S(1)} %get-tuple-element.112), channel_id=1, source_target_pairs={{0,4},{1,3},{2,6},{3,1},{4,8},{5,7},{6,10},{7,5},{8,12},{9,11},{10... | collective-permute-start | bytes 196616 | tf_op jit(solution)/shard_map/ppermute | solution.py:391
  31.2 2.1 %turn.1 = (f32[768,256]{1,0:T(8,128)S(1)}, bf16[768,256]{1,0:T(8,128)(2,1)S(1)}, bf16[256,256]{1,0:T(8,128)(2,1)S(1)}, bf16[256,256]{1,0:T(8,128)(2,1)S(1)}, bf1...) custom-call(f32[768,256]{1,0:T(8,128)S(1)} %get-tuple-element.111.re, ...), custom_call_target="tpu_custom_call" | custom-call | flops 536870912 | bytes 4000000 | tf_op jit(solution)/shard_map/turn/pallas_call | solution.py:32
  33.3 1.5 %collective-permute-start.8 = (bf16[128,256]{1,0:T(8,128)(2,1)S(1)}, bf16[128,256]{1,0:T(8,128)(2,1)S(1)}, u32[]{:S(2)}, u32[]{:S(2)}) collective-permute-start(bf16[128,256]{1,0:T(8,128)(2,1)S(1)} %get-tuple-element.124), channel_id=1, source_target_pairs={{4,0},{8,4},{12,8},{5,1},{9,5},{13,9},{6,2},{10,6},{14,10},{7,3},{... | collective-permute-start | bytes 196616 | tf_op jit(solution)/shard_map/ppermute | solution.py:415
  34.7 1.6 %collective-permute-start.9 = (bf16[128,256]{1,0:T(8,128)(2,1)S(1)}, bf16[128,256]{1,0:T(8,128)(2,1)S(1)}, u32[]{:S(2)}, u32[]{:S(2)}) collective-permute-start(bf16[128,256]{1,0:T(8,128)(2,1)S(1)} %get-tuple-element.125), channel_id=1, source_target_pairs={{0,2},{2,0},{1,3},{3,1},{4,6},{6,4},{5,7},{7,5},{8,10},{10,8},{9,1... | collective-permute-start | bytes 196616 | tf_op jit(solution)/shard_map/ppermute | solution.py:378
  36.3 3.0 %back2.1 = (f32[768,256]{1,0:T(8,128)S(1)}, f32[2048,128]{1,0:T(8,128)S(1)}) custom-call(bf16[768,256]{1,0:T(8,128)(2,1)S(1)} %get-tuple-element.117.refs_0_, bf16[768,256]{1,0:T(8,128)(2,1)S(1)} %get-tuple-element.113.refs_0_.refs_1_, bf16[768,768]{1,0:T(8,128)(2,1)S(1)} %get-tuple-element.118.refs_2_.refs_3_, bf16[3,256,512]{2,1,0:T(8,128)(2,1)S(1)} %copy-done.1, ...), custom_call_target="tpu_custom_call" | custom-call | flops 2717908992 | bytes 4000000 | tf_op jit(solution)/shard_map/back2/pallas_call | solution.py:32
  40.1 1.6 %collective-permute-start.12 = (bf16[1024,128]{1,0:T(8,128)(2,1)S(1)}, bf16[1024,128]{1,0:T(8,128)(2,1)S(1)}, u32[]{:S(2)}, u32[]{:S(2)}) collective-permute-start(bf16[1024,128]{1,0:T(8,128)(2,1)S(1)} %get-tuple-element.140), channel_id=1, source_target_pairs={{0,2},{1,5},{2,0},{3,7},{4,6},{5,1},{6,4},{7,3},{8,10},{9,13},{10,... | collective-permute-start | bytes 786440 | tf_op jit(solution)/shard_map/ppermute | solution.py:391
  41.7 1.6 %join2.1 = (f32[768,256]{1,0:T(8,128)S(1)}, bf16[768,256]{1,0:T(8,128)(2,1)S(1)}, bf16[256,256]{1,0:T(8,128)(2,1)S(1)}, bf16[256,256]{1,0:T(8,128)(2,1)S(1)}, bf...) custom-call(f32[1024,128]{1,0:T(8,128)S(1)} %get-tuple-element.127.r, ...), custom_call_target="tpu_custom_call" | custom-call | flops 536870912 | bytes 4000000 | tf_op jit(solution)/shard_map/join2/pallas_call | solution.py:32
  43.2 1.3 %collective-permute-start.10 = (bf16[128,256]{1,0:T(8,128)(2,1)S(1)}, bf16[128,256]{1,0:T(8,128)(2,1)S(1)}, u32[]{:S(2)}, u32[]{:S(2)}) collective-permute-start(bf16[128,256]{1,0:T(8,128)(2,1)S(1)} %get-tuple-element.136), channel_id=1, source_target_pairs={{4,0},{8,4},{12,8},{5,1},{9,5},{13,9},{6,2},{10,6},{14,10},{7,3},{... | collective-permute-start | bytes 196616 | tf_op jit(solution)/shard_map/ppermute | solution.py:415
  45.1 3.0 %back1.1 = (f32[768,256]{1,0:T(8,128)S(1)}, f32[2048,128]{1,0:T(8,128)S(1)}) custom-call(bf16[768,256]{1,0:T(8,128)(2,1)S(1)} %get-tuple-element.130.refs_0_.refs_1_, bf16[768,256]{1,0:T(8,128)(2,1)S(1)} %get-tuple-element.130.refs_0_.refs_1_, bf16[768,256]{1,0:T(8,128)(2,1)S(1)} %get-tuple-element.108.refs_0_.refs_2_, ...), custom_call_target="tpu_custom_call" | custom-call | flops 2717908992 | bytes 4000000 | tf_op jit(solution)/shard_map/back1/pallas_call | solution.py:32
  48.2 1.5 %collective-permute-done.10.refs_1_.refs_10_ = bf16[128,256]{1,0:T(8,128)(2,1)S(1)} collective-permute-done((bf16[128,256]{1,0:T(8,128)(2,1)S(1)}, bf16[128,256]{1,0:T(8,128)(2,1)S(1)}, u32[]{:S(2)}, u32[]{:S(2)}) %collective-permute-start.10) | collective-permute-done | bytes 65568 | tf_op jit(solution)/shard_map/ppermute | solution.py:415
  50.5 1.6 %join1.1 = (f32[768,256]{1,0:T(8,128)S(1)}, bf16[768,256]{1,0:T(8,128)(2,1)S(1)}, bf16[256,256]{1,0:T(8,128)(2,1)S(1)}, bf16[256,256]{1,0:T(8,128)(2,1)S(1)}, bf...) custom-call(f32[512,128]{1,0:T(8,128)S(1)} %get-tuple-element.141.re, ...), custom_call_target="tpu_custom_call" | custom-call | flops 536870912 | bytes 4000000 | tf_op jit(solution)/shard_map/join1/pallas_call | solution.py:32
  52.1 1.5 %collective-permute-start.13 = (bf16[128,256]{1,0:T(8,128)(2,1)S(1)}, bf16[128,256]{1,0:T(8,128)(2,1)S(1)}, u32[]{:S(2)}, u32[]{:S(2)}) collective-permute-start(bf16[128,256]{1,0:T(8,128)(2,1)S(1)} %get-tuple-element.149), channel_id=1, source_target_pairs={{4,0},{8,4},{12,8},{5,1},{9,5},{13,9},{6,2},{10,6},{14,10},{7,3},{... | collective-permute-start | bytes 196616 | tf_op jit(solution)/shard_map/ppermute | solution.py:415
  53.6 1.5 %collective-permute-start.14 = (bf16[128,256]{1,0:T(8,128)(2,1)S(1)}, bf16[128,256]{1,0:T(8,128)(2,1)S(1)}, u32[]{:S(2)}, u32[]{:S(2)}) collective-permute-start(bf16[128,256]{1,0:T(8,128)(2,1)S(1)} %get-tuple-element.150), channel_id=1, source_target_pairs={{0,2},{2,0},{1,3},{3,1},{4,6},{6,4},{5,7},{7,5},{8,10},{10,8},{9,1... | collective-permute-start | bytes 196616 | tf_op jit(solution)/shard_map/ppermute | solution.py:378
  55.1 2.6 %collective-permute-start.15 = (bf16[512,128]{1,0:T(8,128)(2,1)S(1)}, bf16[512,128]{1,0:T(8,128)(2,1)S(1)}, u32[]{:S(2)}, u32[]{:S(2)}) collective-permute-start(bf16[512,128]{1,0:T(8,128)(2,1)S(1)} %get-tuple-element.151), channel_id=1, source_target_pairs={{0,4},{1,3},{2,6},{3,1},{4,0},{5,7},{6,2},{7,5},{8,12},{9,11},{10,... | collective-permute-start | bytes 393224 | tf_op jit(solution)/shard_map/ppermute | solution.py:391
  57.7 3.0 %back0.1 = (f32[768,256]{1,0:T(8,128)S(1)}, f32[2048,128]{1,0:T(8,128)S(1)}) custom-call(bf16[768,256]{1,0:T(8,128)(2,1)S(1)} %get-tuple-element.143.refs_0_.refs_1_, bf16[768,256]{1,0:T(8,128)(2,1)S(1)} %get-tuple-element.143.refs_0_.refs_1_, bf16[768,256]{1,0:T(8,128)(2,1)S(1)} %get-tuple-element.96.refs_0_.refs_2_, ...), custom_call_target="tpu_custom_call" | custom-call | flops 2717908992 | bytes 4000000 | tf_op jit(solution)/shard_map/back0/pallas_call | solution.py:32
  61.6 3.5 %collective-permute-start.18 = (bf16[512,128]{1,0:T(8,128)(2,1)S(1)}, bf16[512,128]{1,0:T(8,128)(2,1)S(1)}, u32[]{:S(2)}, u32[]{:S(2)}) collective-permute-start(bf16[512,128]{1,0:T(8,128)(2,1)S(1)} %get-tuple-element.162), channel_id=1, source_target_pairs={{0,8},{1,9},{2,10},{3,11},{4,12},{5,13},{6,14},{7,15},{8,0},{9,1},... | collective-permute-start | bytes 393224 | tf_op jit(solution)/shard_map/ppermute | solution.py:391
  65.3 1.9 %collective-permute-start.19 = (bf16[512,128]{1,0:T(8,128)(2,1)S(1)}, bf16[512,128]{1,0:T(8,128)(2,1)S(1)}, u32[]{:S(2)}, u32[]{:S(2)}) collective-permute-start(bf16[512,128]{1,0:T(8,128)(2,1)S(1)} %get-tuple-element.164), channel_id=1, source_target_pairs={{0,4},{1,3},{2,6},{3,1},{4,0},{5,7},{6,2},{7,5},{8,12},{9,11},{10,... | collective-permute-start | bytes 393224 | tf_op jit(solution)/shard_map/ppermute | solution.py:391
  68.5 2.2 %collective-permute-start.20 = (bf16[512,128]{1,0:T(8,128)(2,1)S(1)}, bf16[512,128]{1,0:T(8,128)(2,1)S(1)}, u32[]{:S(2)}, u32[]{:S(2)}) collective-permute-start(bf16[512,128]{1,0:T(8,128)(2,1)S(1)} %get-tuple-element.166), channel_id=1, source_target_pairs={{0,4},{1,3},{2,6},{3,1},{4,0},{5,7},{6,2},{7,5},{8,12},{9,11},{10,... | collective-permute-start | bytes 393224 | tf_op jit(solution)/shard_map/ppermute | solution.py:391
  71.7 3.1 %collective-permute-start.22 = (bf16[512,128]{1,0:T(8,128)(2,1)S(1)}, bf16[512,128]{1,0:T(8,128)(2,1)S(1)}, u32[]{:S(2)}, u32[]{:S(2)}) collective-permute-start(bf16[512,128]{1,0:T(8,128)(2,1)S(1)} %get-tuple-element.170), channel_id=1, source_target_pairs={{0,8},{1,9},{2,10},{3,11},{4,12},{5,13},{6,14},{7,15},{8,0},{9,1},... | collective-permute-start | bytes 393224 | tf_op jit(solution)/shard_map/ppermute | solution.py:391
  75.0 3.2 %collective-permute-start.23 = (bf16[512,128]{1,0:T(8,128)(2,1)S(1)}, bf16[512,128]{1,0:T(8,128)(2,1)S(1)}, u32[]{:S(2)}, u32[]{:S(2)}) collective-permute-start(bf16[512,128]{1,0:T(8,128)(2,1)S(1)} %get-tuple-element.172), channel_id=1, source_target_pairs={{0,8},{1,9},{2,10},{3,11},{4,12},{5,13},{6,14},{7,15},{8,0},{9,1},... | collective-permute-start | bytes 393224 | tf_op jit(solution)/shard_map/ppermute | solution.py:391
  79.0 3.4 %collective-permute-done.22.refs_2_ = bf16[512,128]{1,0:T(8,128)(2,1)S(1)} collective-permute-done((bf16[512,128]{1,0:T(8,128)(2,1)S(1)}, bf16[512,128]{1,0:T(8,128)(2,1)S(1)}, u32[]{:S(2)}, u32[]{:S(2)}) %collective-permute-start.22) | collective-permute-done | bytes 131104 | tf_op jit(solution)/shard_map/ppermute | solution.py:391
  82.5 1.3 %collective-permute-start.24 = (bf16[512,128]{1,0:T(8,128)(2,1)S(1)}, bf16[512,128]{1,0:T(8,128)(2,1)S(1)}, u32[]{:S(2)}, u32[]{:S(2)}) collective-permute-start(bf16[512,128]{1,0:T(8,128)(2,1)S(1)} %get-tuple-element.174), channel_id=1, source_target_pairs={{0,4},{1,3},{2,6},{3,1},{4,0},{5,7},{6,2},{7,5},{8,12},{9,11},{10,... | collective-permute-start | bytes 393224 | tf_op jit(solution)/shard_map/ppermute | solution.py:391
  83.8 1.4 %collective-permute-done.23.refs_2_ = bf16[512,128]{1,0:T(8,128)(2,1)S(1)} collective-permute-done((bf16[512,128]{1,0:T(8,128)(2,1)S(1)}, bf16[512,128]{1,0:T(8,128)(2,1)S(1)}, u32[]{:S(2)}, u32[]{:S(2)}) %collective-permute-start.23) | collective-permute-done | bytes 131104 | tf_op jit(solution)/shard_map/ppermute | solution.py:391
  85.3 1.3 %collective-permute-start.26 = (bf16[512,128]{1,0:T(8,128)(2,1)S(1)}, bf16[512,128]{1,0:T(8,128)(2,1)S(1)}, u32[]{:S(2)}, u32[]{:S(2)}) collective-permute-start(bf16[512,128]{1,0:T(8,128)(2,1)S(1)} %get-tuple-element.177), channel_id=1, source_target_pairs={{0,4},{1,3},{2,6},{3,1},{4,0},{5,7},{6,2},{7,5},{8,12},{9,11},{10,... | collective-permute-start | bytes 393224 | tf_op jit(solution)/shard_map/ppermute | solution.py:391
  88.0 2.2 %collective-permute-start.27 = (bf16[1024,128]{1,0:T(8,128)(2,1)S(1)}, bf16[1024,128]{1,0:T(8,128)(2,1)S(1)}, u32[]{:S(2)}, u32[]{:S(2)}) collective-permute-start(bf16[1024,128]{1,0:T(8,128)(2,1)S(1)} %get-tuple-element.182), channel_id=1, source_target_pairs={{0,2},{1,5},{2,0},{3,7},{4,6},{5,1},{6,4},{7,3},{8,10},{9,13},{10,... | collective-permute-start | bytes 786440 | tf_op jit(solution)/shard_map/ppermute | solution.py:391
  90.1 1.7 %collective-permute-done.26.refs_3_ = bf16[512,128]{1,0:T(8,128)(2,1)S(1)} collective-permute-done((bf16[512,128]{1,0:T(8,128)(2,1)S(1)}, bf16[512,128]{1,0:T(8,128)(2,1)S(1)}, u32[]{:S(2)}, u32[]{:S(2)}) %collective-permute-start.26) | collective-permute-done | bytes 131104 | tf_op jit(solution)/shard_map/ppermute | solution.py:391
  91.9 1.7 %collective-permute-start.28 = (bf16[1024,128]{1,0:T(8,128)(2,1)S(1)}, bf16[1024,128]{1,0:T(8,128)(2,1)S(1)}, u32[]{:S(2)}, u32[]{:S(2)}) collective-permute-start(bf16[1024,128]{1,0:T(8,128)(2,1)S(1)} %get-tuple-element.186), channel_id=1, source_target_pairs={{0,2},{1,5},{2,0},{3,7},{4,6},{5,1},{6,4},{7,3},{8,10},{9,13},{10,... | collective-permute-start | bytes 786440 | tf_op jit(solution)/shard_map/ppermute | solution.py:391
  95.8 2.5 %collective-permute-done.28.refs_4_ = bf16[1024,128]{1,0:T(8,128)(2,1)S(1)} collective-permute-done((bf16[1024,128]{1,0:T(8,128)(2,1)S(1)}, bf16[1024,128]{1,0:T(8,128)(2,1)S(1)}, u32[]{:S(2)}, u32[]{:S(2)}) %collective-permute-start.28) | collective-permute-done | bytes 262176 | tf_op jit(solution)/shard_map/ppermute | solution.py:391
  98.3 1.7 %write0.1 = (f32[3,256,512]{2,1,0:T(8,128)}, f32[3,512,256]{2,1,0:T(8,128)}, f32[8,128]{1,0:T(8,128)}) custom-call(f32[3,256,512]{2,1,0:T(8,128)} %get-tuple-element.183.refs_0_, f32[3,512,256]{2,1,0:T(8,128)} %get-tuple-element.184.refs_1_, f32[8,128]{1,0:T(8,128)S(1)} %get-tuple-element.185.refs_2_, ...), custom_call_target="tpu_custom_call", output_to_operand_aliasing={{0}: (0, {}), {1}: (1, {})} | custom-call | flops 1 | bytes 1 | tf_op jit(solution)/shard_map/write0/pallas_call | solution.py:561
  (78 shorter events, 26.4 us)
Async XLA Ops:
  0.6 7.9 %collective-permute-start.1 = (bf16[3,256,512]{2,1,0:T(8,128)(2,1)}, bf16[3,256,512]{2,1,0:T(8,128)(2,1)S(1)}, u32[]{:S(2)}, u32[]{:S(2)}) collective-permute-start(bf16[3,256,512]{2,1,0:T(8,128)(2,1)} %refs_4_.9), channel_id=1, source_target_pairs={{0,1},{1,0},{2,3},{3,2},{4,5},{5,4},{6,7},{7,6},{8,9},{9,8},{10,11... | collective-permute-start | bytes 2359304 | tf_op jit(solution)/shard_map/ppermute | solution.py:378
  1.1 7.4 %collective-permute-start.2 = (bf16[3,512,256]{2,1,0:T(8,128)(2,1)}, bf16[3,512,256]{2,1,0:T(8,128)(2,1)S(1)}, u32[]{:S(2)}, u32[]{:S(2)}) collective-permute-start(bf16[3,512,256]{2,1,0:T(8,128)(2,1)} %refs_6_.11), channel_id=1, source_target_pairs={{0,1},{1,0},{2,3},{3,2},{4,5},{5,4},{6,7},{7,6},{8,9},{9,8},{10,11... | collective-permute-start | bytes 2359304 | tf_op jit(solution)/shard_map/ppermute | solution.py:378
  3.6 10.1 %collective-permute-start = (bf16[128,256]{1,0:T(8,128)(2,1)S(1)}, bf16[128,256]{1,0:T(8,128)(2,1)S(1)}, u32[]{:S(2)}, u32[]{:S(2)}) collective-permute-start(bf16[128,256]{1,0:T(8,128)(2,1)S(1)} %get-tuple-element.97), channel_id=1, source_target_pairs={{0,4},{1,3},{2,6},{3,1},{4,8},{5,7},{6,10},{7,5},{8,12},{9,11},{10... | collective-permute-start | bytes 196616 | tf_op jit(solution)/shard_map/ppermute | solution.py:391
  10.8 3.0 %copy-start.3 = (bf16[3,512,256]{2,1,0:T(8,128)(2,1)S(1)}, bf16[3,512,256]{2,1,0:T(8,128)(2,1)}, u32[]{:S(2)}) copy-start(bf16[3,512,256]{2,1,0:T(8,128)(2,1)} %refs_6_.11) | copy-start | bytes 2359300
  12.0 1.7 %copy-start.1 = (bf16[3,256,512]{2,1,0:T(8,128)(2,1)S(1)}, bf16[3,256,512]{2,1,0:T(8,128)(2,1)}, u32[]{:S(2)}) copy-start(bf16[3,256,512]{2,1,0:T(8,128)(2,1)} %refs_4_.9) | copy-start | bytes 2359300
  13.7 1.3 %collective-permute-start.3 = (bf16[128,256]{1,0:T(8,128)(2,1)S(1)}, bf16[128,256]{1,0:T(8,128)(2,1)S(1)}, u32[]{:S(2)}, u32[]{:S(2)}) collective-permute-start(bf16[128,256]{1,0:T(8,128)(2,1)S(1)} %collective-permute-done.refs_7_.refs_12_), channel_id=1, source_target_pairs={{0,1},{1,0},{2,3},{3,2},{4,5},{5,4},{6,7},{7,6},{8,9},{9,8},{10,11... | collective-permute-start | bytes 196616 | tf_op jit(solution)/shard_map/ppermute | solution.py:378
  16.1 5.4 %collective-permute-start.4 = (bf16[128,256]{1,0:T(8,128)(2,1)S(1)}, bf16[128,256]{1,0:T(8,128)(2,1)S(1)}, u32[]{:S(2)}, u32[]{:S(2)}) collective-permute-start(bf16[128,256]{1,0:T(8,128)(2,1)S(1)} %get-tuple-element.107), channel_id=1, source_target_pairs={{0,4},{1,3},{2,6},{3,1},{4,8},{5,7},{6,10},{7,5},{8,12},{9,11},{10... | collective-permute-start | bytes 196616 | tf_op jit(solution)/shard_map/ppermute | solution.py:391
  21.4 1.3 %collective-permute-start.5 = (bf16[128,256]{1,0:T(8,128)(2,1)S(1)}, bf16[128,256]{1,0:T(8,128)(2,1)S(1)}, u32[]{:S(2)}, u32[]{:S(2)}) collective-permute-start(bf16[128,256]{1,0:T(8,128)(2,1)S(1)} %collective-permute-done.4.refs_7_.refs_12_), channel_id=1, source_target_pairs={{0,1},{1,0},{2,3},{3,2},{4,5},{5,4},{6,7},{7,6},{8,9},{9,8},{10,11... | collective-permute-start | bytes 196616 | tf_op jit(solution)/shard_map/ppermute | solution.py:378
  23.8 6.2 %collective-permute-start.6 = (bf16[128,256]{1,0:T(8,128)(2,1)S(1)}, bf16[128,256]{1,0:T(8,128)(2,1)S(1)}, u32[]{:S(2)}, u32[]{:S(2)}) collective-permute-start(bf16[128,256]{1,0:T(8,128)(2,1)S(1)} %get-tuple-element.112), channel_id=1, source_target_pairs={{0,4},{1,3},{2,6},{3,1},{4,8},{5,7},{6,10},{7,5},{8,12},{9,11},{10... | collective-permute-start | bytes 196616 | tf_op jit(solution)/shard_map/ppermute | solution.py:391
  29.3 1.9 %copy-start.4 = (f32[768,256]{1,0:T(8,128)S(1)}, f32[768,256]{1,0:T(8,128)}, u32[]{:S(2)}) copy-start(f32[768,256]{1,0:T(8,128)} %refs_4_.7) | copy-start | bytes 2359300
  29.9 1.3 %collective-permute-start.7 = (bf16[128,256]{1,0:T(8,128)(2,1)S(1)}, bf16[128,256]{1,0:T(8,128)(2,1)S(1)}, u32[]{:S(2)}, u32[]{:S(2)}) collective-permute-start(bf16[128,256]{1,0:T(8,128)(2,1)S(1)} %collective-permute-done.6.refs_7_.refs_9_), channel_id=1, source_target_pairs={{0,1},{1,0},{2,3},{3,2},{4,5},{5,4},{6,7},{7,6},{8,9},{9,8},{10,11... | collective-permute-start | bytes 196616 | tf_op jit(solution)/shard_map/ppermute | solution.py:378
  33.3 6.8 %collective-permute-start.8 = (bf16[128,256]{1,0:T(8,128)(2,1)S(1)}, bf16[128,256]{1,0:T(8,128)(2,1)S(1)}, u32[]{:S(2)}, u32[]{:S(2)}) collective-permute-start(bf16[128,256]{1,0:T(8,128)(2,1)S(1)} %get-tuple-element.124), channel_id=1, source_target_pairs={{4,0},{8,4},{12,8},{5,1},{9,5},{13,9},{6,2},{10,6},{14,10},{7,3},{... | collective-permute-start | bytes 196616 | tf_op jit(solution)/shard_map/ppermute | solution.py:415
  34.7 5.3 %collective-permute-start.9 = (bf16[128,256]{1,0:T(8,128)(2,1)S(1)}, bf16[128,256]{1,0:T(8,128)(2,1)S(1)}, u32[]{:S(2)}, u32[]{:S(2)}) collective-permute-start(bf16[128,256]{1,0:T(8,128)(2,1)S(1)} %get-tuple-element.125), channel_id=1, source_target_pairs={{0,2},{2,0},{1,3},{3,1},{4,6},{6,4},{5,7},{7,5},{8,10},{10,8},{9,1... | collective-permute-start | bytes 196616 | tf_op jit(solution)/shard_map/ppermute | solution.py:378
  40.1 10.3 %collective-permute-start.12 = (bf16[1024,128]{1,0:T(8,128)(2,1)S(1)}, bf16[1024,128]{1,0:T(8,128)(2,1)S(1)}, u32[]{:S(2)}, u32[]{:S(2)}) collective-permute-start(bf16[1024,128]{1,0:T(8,128)(2,1)S(1)} %get-tuple-element.140), channel_id=1, source_target_pairs={{0,2},{1,5},{2,0},{3,7},{4,6},{5,1},{6,4},{7,3},{8,10},{9,13},{10,... | collective-permute-start | bytes 786440 | tf_op jit(solution)/shard_map/ppermute | solution.py:391
  43.2 6.4 %collective-permute-start.10 = (bf16[128,256]{1,0:T(8,128)(2,1)S(1)}, bf16[128,256]{1,0:T(8,128)(2,1)S(1)}, u32[]{:S(2)}, u32[]{:S(2)}) collective-permute-start(bf16[128,256]{1,0:T(8,128)(2,1)S(1)} %get-tuple-element.136), channel_id=1, source_target_pairs={{4,0},{8,4},{12,8},{5,1},{9,5},{13,9},{6,2},{10,6},{14,10},{7,3},{... | collective-permute-start | bytes 196616 | tf_op jit(solution)/shard_map/ppermute | solution.py:415
  44.5 5.1 %collective-permute-start.11 = (bf16[128,256]{1,0:T(8,128)(2,1)S(1)}, bf16[128,256]{1,0:T(8,128)(2,1)S(1)}, u32[]{:S(2)}, u32[]{:S(2)}) collective-permute-start(bf16[128,256]{1,0:T(8,128)(2,1)S(1)} %get-tuple-element.137), channel_id=1, source_target_pairs={{0,2},{2,0},{1,3},{3,1},{4,6},{6,4},{5,7},{7,5},{8,10},{10,8},{9,1... | collective-permute-start | bytes 196616 | tf_op jit(solution)/shard_map/ppermute | solution.py:378
  49.7 15.5 %collective-permute-start.16 = (bf16[1024,128]{1,0:T(8,128)(2,1)S(1)}, bf16[1024,128]{1,0:T(8,128)(2,1)S(1)}, u32[]{:S(2)}, u32[]{:S(2)}) collective-permute-start(bf16[1024,128]{1,0:T(8,128)(2,1)S(1)} %get-tuple-element.155), channel_id=1, source_target_pairs={{0,2},{1,5},{2,0},{3,7},{4,6},{5,1},{6,4},{7,3},{8,10},{9,13},{10,... | collective-permute-start | bytes 786440 | tf_op jit(solution)/shard_map/ppermute | solution.py:391
  52.1 8.7 %collective-permute-start.13 = (bf16[128,256]{1,0:T(8,128)(2,1)S(1)}, bf16[128,256]{1,0:T(8,128)(2,1)S(1)}, u32[]{:S(2)}, u32[]{:S(2)}) collective-permute-start(bf16[128,256]{1,0:T(8,128)(2,1)S(1)} %get-tuple-element.149), channel_id=1, source_target_pairs={{4,0},{8,4},{12,8},{5,1},{9,5},{13,9},{6,2},{10,6},{14,10},{7,3},{... | collective-permute-start | bytes 196616 | tf_op jit(solution)/shard_map/ppermute | solution.py:415
  53.6 7.2 %collective-permute-start.14 = (bf16[128,256]{1,0:T(8,128)(2,1)S(1)}, bf16[128,256]{1,0:T(8,128)(2,1)S(1)}, u32[]{:S(2)}, u32[]{:S(2)}) collective-permute-start(bf16[128,256]{1,0:T(8,128)(2,1)S(1)} %get-tuple-element.150), channel_id=1, source_target_pairs={{0,2},{2,0},{1,3},{3,1},{4,6},{6,4},{5,7},{7,5},{8,10},{10,8},{9,1... | collective-permute-start | bytes 196616 | tf_op jit(solution)/shard_map/ppermute | solution.py:378
  55.1 5.7 %collective-permute-start.15 = (bf16[512,128]{1,0:T(8,128)(2,1)S(1)}, bf16[512,128]{1,0:T(8,128)(2,1)S(1)}, u32[]{:S(2)}, u32[]{:S(2)}) collective-permute-start(bf16[512,128]{1,0:T(8,128)(2,1)S(1)} %get-tuple-element.151), channel_id=1, source_target_pairs={{0,4},{1,3},{2,6},{3,1},{4,0},{5,7},{6,2},{7,5},{8,12},{9,11},{10,... | collective-permute-start | bytes 393224 | tf_op jit(solution)/shard_map/ppermute | solution.py:391
  60.9 7.5 %collective-permute-start.17 = (bf16[1024,128]{1,0:T(8,128)(2,1)S(1)}, bf16[1024,128]{1,0:T(8,128)(2,1)S(1)}, u32[]{:S(2)}, u32[]{:S(2)}) collective-permute-start(bf16[1024,128]{1,0:T(8,128)(2,1)S(1)} %get-tuple-element.160), channel_id=1, source_target_pairs={{0,2},{1,5},{2,0},{3,7},{4,6},{5,1},{6,4},{7,3},{8,10},{9,13},{10,... | collective-permute-start | bytes 786440 | tf_op jit(solution)/shard_map/ppermute | solution.py:391
  61.6 9.9 %collective-permute-start.18 = (bf16[512,128]{1,0:T(8,128)(2,1)S(1)}, bf16[512,128]{1,0:T(8,128)(2,1)S(1)}, u32[]{:S(2)}, u32[]{:S(2)}) collective-permute-start(bf16[512,128]{1,0:T(8,128)(2,1)S(1)} %get-tuple-element.162), channel_id=1, source_target_pairs={{0,8},{1,9},{2,10},{3,11},{4,12},{5,13},{6,14},{7,15},{8,0},{9,1},... | collective-permute-start | bytes 393224 | tf_op jit(solution)/shard_map/ppermute | solution.py:391
  65.3 6.4 %collective-permute-start.19 = (bf16[512,128]{1,0:T(8,128)(2,1)S(1)}, bf16[512,128]{1,0:T(8,128)(2,1)S(1)}, u32[]{:S(2)}, u32[]{:S(2)}) collective-permute-start(bf16[512,128]{1,0:T(8,128)(2,1)S(1)} %get-tuple-element.164), channel_id=1, source_target_pairs={{0,4},{1,3},{2,6},{3,1},{4,0},{5,7},{6,2},{7,5},{8,12},{9,11},{10,... | collective-permute-start | bytes 393224 | tf_op jit(solution)/shard_map/ppermute | solution.py:391
  68.5 6.5 %collective-permute-start.20 = (bf16[512,128]{1,0:T(8,128)(2,1)S(1)}, bf16[512,128]{1,0:T(8,128)(2,1)S(1)}, u32[]{:S(2)}, u32[]{:S(2)}) collective-permute-start(bf16[512,128]{1,0:T(8,128)(2,1)S(1)} %get-tuple-element.166), channel_id=1, source_target_pairs={{0,4},{1,3},{2,6},{3,1},{4,0},{5,7},{6,2},{7,5},{8,12},{9,11},{10,... | collective-permute-start | bytes 393224 | tf_op jit(solution)/shard_map/ppermute | solution.py:391
  71.6 6.7 %collective-permute-start.21 = (bf16[512,128]{1,0:T(8,128)(2,1)S(1)}, bf16[512,128]{1,0:T(8,128)(2,1)S(1)}, u32[]{:S(2)}, u32[]{:S(2)}) collective-permute-start(bf16[512,128]{1,0:T(8,128)(2,1)S(1)} %get-tuple-element.168), channel_id=1, source_target_pairs={{0,4},{1,3},{2,6},{3,1},{4,0},{5,7},{6,2},{7,5},{8,12},{9,11},{10,... | collective-permute-start | bytes 393224 | tf_op jit(solution)/shard_map/ppermute | solution.py:391
  71.7 10.7 %collective-permute-start.22 = (bf16[512,128]{1,0:T(8,128)(2,1)S(1)}, bf16[512,128]{1,0:T(8,128)(2,1)S(1)}, u32[]{:S(2)}, u32[]{:S(2)}) collective-permute-start(bf16[512,128]{1,0:T(8,128)(2,1)S(1)} %get-tuple-element.170), channel_id=1, source_target_pairs={{0,8},{1,9},{2,10},{3,11},{4,12},{5,13},{6,14},{7,15},{8,0},{9,1},... | collective-permute-start | bytes 393224 | tf_op jit(solution)/shard_map/ppermute | solution.py:391
  75.0 10.2 %collective-permute-start.23 = (bf16[512,128]{1,0:T(8,128)(2,1)S(1)}, bf16[512,128]{1,0:T(8,128)(2,1)S(1)}, u32[]{:S(2)}, u32[]{:S(2)}) collective-permute-start(bf16[512,128]{1,0:T(8,128)(2,1)S(1)} %get-tuple-element.172), channel_id=1, source_target_pairs={{0,8},{1,9},{2,10},{3,11},{4,12},{5,13},{6,14},{7,15},{8,0},{9,1},... | collective-permute-start | bytes 393224 | tf_op jit(solution)/shard_map/ppermute | solution.py:391
  78.3 11.9 %collective-permute-start.25 = (bf16[1024,128]{1,0:T(8,128)(2,1)S(1)}, bf16[1024,128]{1,0:T(8,128)(2,1)S(1)}, u32[]{:S(2)}, u32[]{:S(2)}) collective-permute-start(bf16[1024,128]{1,0:T(8,128)(2,1)S(1)} %get-tuple-element.176), channel_id=1, source_target_pairs={{0,2},{1,5},{2,0},{3,7},{4,6},{5,1},{6,4},{7,3},{8,10},{9,13},{10,... | collective-permute-start | bytes 786440 | tf_op jit(solution)/shard_map/ppermute | solution.py:391
  82.5 5.4 %collective-permute-start.24 = (bf16[512,128]{1,0:T(8,128)(2,1)S(1)}, bf16[512,128]{1,0:T(8,128)(2,1)S(1)}, u32[]{:S(2)}, u32[]{:S(2)}) collective-permute-start(bf16[512,128]{1,0:T(8,128)(2,1)S(1)} %get-tuple-element.174), channel_id=1, source_target_pairs={{0,4},{1,3},{2,6},{3,1},{4,0},{5,7},{6,2},{7,5},{8,12},{9,11},{10,... | collective-permute-start | bytes 393224 | tf_op jit(solution)/shard_map/ppermute | solution.py:391
  85.3 6.5 %collective-permute-start.26 = (bf16[512,128]{1,0:T(8,128)(2,1)S(1)}, bf16[512,128]{1,0:T(8,128)(2,1)S(1)}, u32[]{:S(2)}, u32[]{:S(2)}) collective-permute-start(bf16[512,128]{1,0:T(8,128)(2,1)S(1)} %get-tuple-element.177), channel_id=1, source_target_pairs={{0,4},{1,3},{2,6},{3,1},{4,0},{5,7},{6,2},{7,5},{8,12},{9,11},{10,... | collective-permute-start | bytes 393224 | tf_op jit(solution)/shard_map/ppermute | solution.py:391
  88.0 6.7 %collective-permute-start.27 = (bf16[1024,128]{1,0:T(8,128)(2,1)S(1)}, bf16[1024,128]{1,0:T(8,128)(2,1)S(1)}, u32[]{:S(2)}, u32[]{:S(2)}) collective-permute-start(bf16[1024,128]{1,0:T(8,128)(2,1)S(1)} %get-tuple-element.182), channel_id=1, source_target_pairs={{0,2},{1,5},{2,0},{3,7},{4,6},{5,1},{6,4},{7,3},{8,10},{9,13},{10,... | collective-permute-start | bytes 786440 | tf_op jit(solution)/shard_map/ppermute | solution.py:391
  91.9 6.4 %collective-permute-start.28 = (bf16[1024,128]{1,0:T(8,128)(2,1)S(1)}, bf16[1024,128]{1,0:T(8,128)(2,1)S(1)}, u32[]{:S(2)}, u32[]{:S(2)}) collective-permute-start(bf16[1024,128]{1,0:T(8,128)(2,1)S(1)} %get-tuple-element.186), channel_id=1, source_target_pairs={{0,2},{1,5},{2,0},{3,7},{4,6},{5,1},{6,4},{7,3},{8,10},{9,13},{10,... | collective-permute-start | bytes 786440 | tf_op jit(solution)/shard_map/ppermute | solution.py:391
  (5 other events, 5.8 us)

commit v10 on v9

--- a/solution.py
+++ b/solution.py
@@ -47,11 +47,15 @@
     return 1.0 / (1.0 + jnp.exp(-v))
 
 
+def half_message(x, w_in, w_out):
+    pre = mm(x, w_in)
+    return mm((pre * sigmoid(pre)).astype(BF16), w_out)
+
+
 def message_of(x, halves):
     total = None
     for w_in, w_out in halves:
-        pre = mm(x, w_in)
-        part = mm((pre * sigmoid(pre)).astype(BF16), w_out)
+        part = half_message(x, w_in, w_out)
         total = part if total is None else total + part
     return total.astype(BF16)
 
@@ -81,17 +85,15 @@
     return scale * (grad - normed * jnp.mean(grad * normed, axis=-1, keepdims=True))
 
 
-def setup_kernel(groups, pairs, features, sent, *refs):
+def setup_kernel(groups, features, sent, *refs):
     pick, spread, pick_self, held = refs[:4]
     sends = refs[4:]
     rows = features.shape[0]
     held[...] = features[...]
-    b, feat = lax.axis_index("basin"), lax.axis_index("feat")
-    for route in range(-1, 2 * pairs):
+    b = lax.axis_index("basin")
+    for route in range(-1, groups):
         if route == 0:
             chosen = lax.broadcasted_iota(jnp.int32, (1, BLOCK), 1) + (rows - BLOCK)
-        elif route >= groups:
-            chosen = jnp.full((1, BLOCK), -1, jnp.int32)
         else:
             chosen = sent[pl.ds(lax.rem(b + max(route, 0), groups), 1), :]
         across = jnp.broadcast_to(chosen, (BLOCK, BLOCK))
@@ -102,18 +104,19 @@
             if route < 0:
                 pick_self[:, r : r + BLOCK] = hot
                 continue
-
-            @pl.when(route % 2 == feat)
-            def _():
-                pick[route // 2 * BLOCK : (route // 2 + 1) * BLOCK, r : r + BLOCK] = hot
-
+            if route > 0:
+                pick[(route - 1) * BLOCK : route * BLOCK, r : r + BLOCK] = hot
             at = lax.broadcasted_iota(jnp.int32, (BLOCK, BLOCK), 0) + r
-            if route < groups:
-                spread[r : r + BLOCK, route * BLOCK : (route + 1) * BLOCK] = (
-                    (across == at).astype(F32).astype(BF16)
-                )
-    for i, send in enumerate(sends):
-        send[...] = mm(pick[i * BLOCK : (i + 1) * BLOCK, :], features[...]).astype(BF16)
+            spread[r : r + BLOCK, route * BLOCK : (route + 1) * BLOCK] = (
+                (across == at).astype(F32).astype(BF16)
+            )
+    pick_sends(features[...], pick, sends)
+
+
+def pick_sends(rows, pick, sends):
+    sends[0][...] = rows[rows.shape[0] - BLOCK :, :]
+    for s, send in enumerate(sends[1:]):
+        send[...] = mm(pick[s * BLOCK : (s + 1) * BLOCK, :], rows).astype(BF16)
 
 
 def adjacency_kernel(groups, sources, values, pick_self, _, *refs):
@@ -150,61 +153,63 @@
     own_messages(layer, refs[0], refs[1:5], refs[5])
 
 
-def remote_mixed(layer, received, remote, feat, weights):
+def half_kernel(x, w_in, w_out, part):
+    for r in range(0, x.shape[0], 256):
+        here = slice(r, r + 256)
+        part[here, :] = half_message(x[here, :], w_in[0], w_out[0])
+
+
+def other_half_kernel(x, w_in, w_out, part, msg):
+    for r in range(0, x.shape[0], 256):
+        here = slice(r, r + 256)
+        msg[here, :] = (part[here, :] + half_message(x[here, :], w_in[0], w_out[0])).astype(BF16)
+
+
+def remote_mixed(layer, received, columns, weights):
     wi0, wi1, wo0, wo1 = weights
     halves = [(wi0[layer], wo0[layer]), (wi1[layer], wo1[layer])]
-    total = None
-    for i, block in enumerate(received):
-        route = jnp.minimum(2 * i + feat, remote.shape[1] // BLOCK - 1)
-        columns = remote[:, pl.ds(pl.multiple_of(route * BLOCK, BLOCK), BLOCK)]
-        part = mm(columns, message_of(block[...], halves))
-        total = part if total is None else total + part
-    return total
-
-
-def part_kernel(layer, pairs, *refs):
+    far = jnp.concatenate([x[...] for x in received], axis=0)
+    return mm(columns, message_of(far, halves))
+
+
+def part_kernel(layer, *refs):
     local, msg, remote = refs[:3]
-    weights, received, mixed = refs[3:7], refs[7 : 7 + pairs], refs[-1]
-    mixed[...] = mm(local[...], msg[...]) + remote_mixed(
-        layer, received, remote, lax.axis_index("feat"), weights
-    )
-
-
-def mixed_total(layer, state, mixed, received, remote, weights):
-    return state + mixed[...] + remote_mixed(
-        layer, received, remote, 1 - lax.axis_index("feat"), weights
-    )
-
-
-def mix_kernel(layer, pairs, *refs):
+    weights, received, mixed = refs[3:7], refs[7:-1], refs[-1]
+    total = mm(local[...], msg[...])
+    if received:
+        total = total + remote_mixed(layer, received, remote[:, BLOCK:], weights)
+    mixed[...] = total
+
+
+def upstream_rows(got, swapped_got):
+    return got[...] + swapped_got[...]
+
+
+def mixed_total(layer, state, mixed, up, remote, weights):
+    return state + mixed[...] + remote_mixed(layer, [up], remote[:, :BLOCK], weights)
+
+
+def mix_kernel(layer, *refs):
     prev, mixed, remote, pick = refs[:4]
-    weights = refs[4:8]
-    received = refs[8 : 8 + pairs]
-    total, inputs = refs[8 + pairs : 10 + pairs]
-    sends = refs[10 + pairs :]
+    weights, up = refs[4:8], upstream_rows(*refs[8:10])
+    total, inputs = refs[10:12]
     state = prev[...].astype(F32) if layer == 0 else normed_of(prev[...])[1]
-    total[...] = mixed_total(layer, state, mixed, received, remote, weights)
+    total[...] = mixed_total(layer, state, mixed, up, remote, weights)
     new = normed_of(total[...])[1].astype(BF16)
     inputs[...] = new
-    for i, send in enumerate(sends):
-        send[...] = mm(pick[i * BLOCK : (i + 1) * BLOCK, :], new).astype(BF16)
-
-
-def start_bwd(layer, groups, dtotal_now, weights, mine, others, remote_t, outs):
+    pick_sends(new, pick, refs[12:])
+
+
+def start_bwd(layer, dtotal_now, weights, received, remote_t, outs):
     dtotal, dround, far_x, far_dmsg, far_act, far_dpre = outs[:6]
     backs = outs[6:]
     wi0, wi1, wo0, wo1 = weights
     halves = [(wi0[layer], wo0[layer]), (wi1[layer], wo1[layer])]
     dtotal[...] = dtotal_now
     dround[...] = dtotal_now.astype(BF16)
-    for first in range(2):
-
-        @pl.when(lax.axis_index("feat") == first)
-        def _():
-            for route in range(groups):
-                block = (mine, others)[(route + first) % 2][route // 2]
-                far_x[route * BLOCK : (route + 1) * BLOCK, :] = block[...]
-
+    far_x[:BLOCK, :] = upstream_rows(*received[:2])
+    for i, block in enumerate(received[2:]):
+        far_x[(i + 1) * BLOCK : (i + 2) * BLOCK, :] = block[...]
     dmsg = mm(remote_t[...], dround[...]).astype(BF16)
     back, (act, dpre) = message_grad(far_x[...], dmsg, halves)
     far_dmsg[...] = dmsg
@@ -214,15 +219,12 @@
         out[...] = back[i * BLOCK : (i + 1) * BLOCK, :].astype(BF16)
 
 
-def turn_kernel(layer, groups, pairs, *refs):
+def turn_kernel(layer, groups, *refs):
     prev, mixed, remote, remote_t, cot = refs[:5]
-    weights = refs[5:9]
-    mine, others = refs[9 : 9 + pairs], refs[9 + pairs : 9 + 2 * pairs]
-    outs = refs[9 + 2 * pairs :]
+    weights, received, outs = refs[5:9], refs[9 : 10 + groups], refs[10 + groups :]
     state = normed_of(prev[...])[1]
-    total = mixed_total(layer, state, mixed, others, remote, weights)
-    dtotal = norm_grad(cot[...], total)
-    start_bwd(layer, groups, dtotal, weights, mine, others, remote_t, outs)
+    total = mixed_total(layer, state, mixed, upstream_rows(*received[:2]), remote, weights)
+    start_bwd(layer, norm_grad(cot[...], total), weights, received, remote_t, outs)
 
 
 def back_kernel(layer, grad_scale, *refs):
@@ -357,14 +359,13 @@
     return dtotal[...] + back[...] + mm(spread[...], far)
 
 
-def join_kernel(layer, groups, pairs, *refs):
+def join_kernel(layer, groups, *refs):
     dtotal, back, spread, remote_t, total = refs[:5]
     weights, refs = refs[5:9], refs[9:]
     returned, refs = refs[:groups], refs[groups:]
-    mine, others, outs = refs[:pairs], refs[pairs : 2 * pairs], refs[2 * pairs :]
+    received, outs = refs[: groups + 1], refs[groups + 1 :]
     grad = gathered_grad(dtotal, back, returned, spread)
-    dtotal = norm_grad(grad, total[...])
-    start_bwd(layer, groups, dtotal, weights, mine, others, remote_t, outs)
+    start_bwd(layer, norm_grad(grad, total[...]), weights, received, remote_t, outs)
 
 
 def last_kernel(*refs):
@@ -400,14 +401,13 @@
 
 
 def forward(sends):
-    def target(i, c, b, feat):
-        route = 2 * i + feat
-        if route == 0:
-            return (c + 1, b) if c + 1 < lax.axis_size("chain") else None
-        groups = lax.axis_size("basin")
-        return (c, (b + route) % groups) if route < groups else None
-
-    return [over_mesh(x, functools.partial(target, i)) for i, x in enumerate(sends)]
+    chain = lax.axis_size("chain")
+
+    def downstream(c, b, feat):
+        return (c + 1, b) if c % 2 == feat and c + 1 < chain else None
+
+    up = over_mesh(sends[0], downstream)
+    return [up] + [around(x, "basin", s + 1) for s, x in enumerate(sends[1:])]
 
 
 def backward(grads):
@@ -416,14 +416,9 @@
     return [up] + [around(x, "basin", -s) for s, x in enumerate(grads) if s]
 
 
-def other_core(got):
-    return [around(x, "feat", 1) for x in got]
-
-
 def shards(features, cotangent, w_in, w_out, block_index, block_values, send_rows, send_count):
     rows, latent = features.shape
     groups = lax.axis_size("basin")
-    pairs = (groups + 1) // 2
     layers, _, half = w_in.shape
     far_rows = groups * BLOCK
     own = rows // BLOCK
@@ -441,9 +436,10 @@
     sent = jnp.where(live, send_rows[0], -1)
     sources = block_index.T
     pick, spread, pick_self, features, *sends = call(
-        functools.partial(setup_kernel, groups, pairs),
-        [act16(pairs * BLOCK, rows), act16(rows, far_rows), act16(BLOCK, rows), act16(rows)]
-        + [act16(BLOCK)] * pairs,
+        functools.partial(setup_kernel, groups),
+        [act16(max(groups - 1, 1) * BLOCK, rows), act16(rows, far_rows), act16(BLOCK, rows)]
+        + [act16(rows)]
+        + [act16(BLOCK)] * groups,
         [features, sent],
         2 * rows * far_rows * latent,
         name="setup",
@@ -451,18 +447,20 @@
     weights = (w_in, wi1, w_out, wo1)
     inputs = [features]
     totals = []
-    mine = []
-    others = []
+    received = []
     for layer in range(layers):
-        mine.append(forward(sends))
-        (msg,) = call(
-            functools.partial(local_kernel, layer),
-            [act16(rows)],
-            [inputs[layer], *weights],
-            rows * ffn,
-            name=f"local{layer}",
-        )
+        up, *others = forward(sends)
         if layer == 0:
+            (part,) = call(
+                half_kernel, [((rows, latent), F32)], [features, wi1, wo1], rows * ffn // 2, name="half"
+            )
+            (msg,) = call(
+                other_half_kernel,
+                [act16(rows)],
+                [features, w_in, w_out, part],
+                rows * ffn // 2,
+                name="local0",
+            )
             local, local_t, remote, remote_t = call(
                 functools.partial(adjacency_kernel, groups),
                 [act16(rows, rows), act16(rows, rows), act16(rows, far_rows), act16(far_rows, rows)],
@@ -472,22 +470,30 @@
                 name="adjacency",
                 scalars=sources,
             )
-            mine[0], local = lax.optimization_barrier((mine[0], local))
-        mine[layer], msg = lax.optimization_barrier((mine[layer], msg))
-        others.append(other_core(mine[layer]))
+            up, local = lax.optimization_barrier((up, local))
+        else:
+            (msg,) = call(
+                functools.partial(local_kernel, layer),
+                [act16(rows)],
+                [inputs[layer], *weights],
+                rows * ffn,
+                name=f"local{layer}",
+            )
+            up, msg = lax.optimization_barrier((up, msg))
+        received.append([up, around(up, "feat", 1), *others])
         (mixed,) = call(
-            functools.partial(part_kernel, layer, pairs),
+            functools.partial(part_kernel, layer),
             [((rows, latent), F32)],
-            [local, msg, remote, *weights, *mine[layer]],
+            [local, msg, remote, *weights, *others],
             2 * rows * rows * latent,
             name=f"part{layer}",
         )
         prev = totals[-1] if layer else features
         if layer < last:
             total, new, *sends = call(
-                functools.partial(mix_kernel, layer, pairs),
-                [((rows, latent), F32), act16(rows)] + [act16(BLOCK)] * pairs,
-                [prev, mixed, remote, pick, *weights, *others[layer]],
+                functools.partial(mix_kernel, layer),
+                [((rows, latent), F32), act16(rows)] + [act16(BLOCK)] * groups,
+                [prev, mixed, remote, pick, *weights, *received[layer][:2]],
                 far_rows * ffn + 2 * rows * far_rows * latent,
                 name=f"mix{layer}",
             )
@@ -499,9 +505,9 @@
         + [act16(BLOCK)] * groups
     )
     outs = call(
-        functools.partial(turn_kernel, last, groups, pairs),
+        functools.partial(turn_kernel, last, groups),
         bwd_outs,
-        [totals[-1], mixed, remote, remote_t, cotangent, *weights, *mine[last], *others[last]],
+        [totals[-1], mixed, remote, remote_t, cotangent, *weights, *received[last]],
         2 * far_rows * ffn,
         name="turn",
     )
@@ -538,10 +544,10 @@
     def join(layer, state, after):
         if layer:
             return call(
-                functools.partial(join_kernel, layer - 1, groups, pairs),
+                functools.partial(join_kernel, layer - 1, groups),
                 bwd_outs,
                 [*state, spread, remote_t, totals[layer - 1]]
-                + [*weights, *returned[layer], *mine[layer - 1], *others[layer - 1]],
+                + [*weights, *returned[layer], *received[layer - 1]],
                 2 * far_rows * ffn,
                 name=f"join{layer}",
                 after=after,
@@ -586,16 +592,14 @@
     for layer in reversed(range(layers)):
         state, at = back(layer, outs, at)
         arrived = [sums[above].got[0] for above in range(layer + 2, layers)]
-        at = sum_step([sums[layer]], at + returned[layer] + arrived)
+        if layer:
+            arrived += returned[layer]
+        at = sum_step([sums[layer]], at + arrived)
         if layer:
             for above in range(layer + 1, layers):
                 at = sum_step([sums[above]], at)
             outs = join(layer, state, at)
             at = outs[1:2]
-    for layer in reversed(range(1, layers)):
-        at = sum_step([sums[layer]], at)
-    grad, token = join(0, state, at)
-    at = sum_step([sums[0]], [token])
     while sums[0].done < count:
         for layer in reversed(range(layers)):
             if sums[layer].done < count:
@@ -604,6 +608,9 @@
                 at = sum_step([sums[layer]], at)
     written = []
     for layer in reversed(range(layers)):
+        if layer == 0:
+            grad, token = join(0, state, at)
+            at = [token]
         *written, token = write(layer, written, at)
         at = [token]
     return (grad, *written)

time: 101 us -> 97.5 us (0.965)
  local copies, waits for them, and re-layouts: 3.28 us -> 1.42 us
  starting transfers between devices: 48.2 us -> 46.7 us
    ppermute x18, waiting for transfers between devices: 12.5 us -> 8.01 us  [over_mesh(): return lax.ppermute(x, ('chain', 'basin', 'feat'), perm)]
    ppermute x8 -> x11, waiting for transfers between devices: 0.76 us -> 4.61 us  [around(): return lax.ppermute(x, axis, [(i, (i + distance) % n) for i in range(n)])]
    ppermute x18, starting transfers between devices: 39.6 us -> 36 us  [over_mesh(): return lax.ppermute(x, ('chain', 'basin', 'feat'), perm)]
    ppermute x8 -> x11, starting transfers between devices: 4.3 us -> 6.69 us  [around(): return lax.ppermute(x, axis, [(i, (i + distance) % n) for i in range(n)])]
    unnamed x16 -> x12, local copies, waits for them, and re-layouts: 3.28 us -> 1.42 us
    ppermute x3, waiting for transfers between devices: 2.21 us -> 3.58 us  [backward(): up = lax.ppermute(grads[0], 'chain', [(c, c - 1) for c in range(1, chain)])]
    pallas_call x32 -> x33, Pallas kernels: 27.3 us -> 26.9 us  [call(): pl.pallas_call(lambda *refs: body(*refs[skipped:]), out_shape=[jax.ShapeD...]
  transfers between devices with their start and end apart: 29 -> 32, of which waited for: 14 -> 12; matrix products, arithmetic and copies ran while one was open for 1% -> 1% of each run, Pallas kernels for 25% -> 26%
where the time goes in v10:
time: 97.5 us; the launch traced here: 97.2 us
  starting transfers between devices  46.7 us (48%)
  Pallas kernels  30.9 us (32%)
  waiting for transfers between devices  16.2 us (17%)
  local copies, waits for them, and re-layouts  1.42 us (1%)
  between operations  1.2 us (1%)
    ppermute x18, starting transfers between devices, over_mesh(): return lax.ppermute(x, ('chain', 'basin', 'feat'), perm)  36 us
    pallas_call x33, Pallas kernels, call(): pl.pallas_call(lambda *refs: body(*refs[skipped:]), out_shape=[jax.ShapeD...  26.9 us
    ppermute x18, waiting for transfers between devices, over_mesh(): return lax.ppermute(x, ('chain', 'basin', 'feat'), perm)  8.01 us
    ppermute x11, starting transfers between devices, around(): return lax.ppermute(x, axis, [(i, (i + distance) % n) for i in range(n)])  6.69 us
    ppermute x11, waiting for transfers between devices, around(): return lax.ppermute(x, axis, [(i, (i + distance) % n) for i in range(n)])  4.61 us
    ppermute x3, starting transfers between devices, backward(): up = lax.ppermute(grads[0], 'chain', [(c, c - 1) for c in range(1, chain)])  4.04 us
    pallas_call x3, Pallas kernels, write(): pl.pallas_call(functools.partial(write_kernel, layer, stages[0], len(kept...  4 us
    ppermute x3, waiting for transfers between devices, backward(): up = lax.ppermute(grads[0], 'chain', [(c, c - 1) for c in range(1, chain)])  3.58 us
  transfers between devices with their start and end apart: 32, of which 12 were waited for; matrix products, arithmetic and copies ran while one was open for 1% of the time, Pallas kernels for 26%

profile of v10, /device:TPU:0, one launch (start us, length us, event | category | flops | bytes accessed | tf_op | source)
XLA Modules:
  0.0 97.2 jit_solution(8580961597367923839)
XLA Ops:
  3.3 5.0 %collective-permute-start = (bf16[128,256]{1,0:T(8,128)(2,1)S(1)}, bf16[128,256]{1,0:T(8,128)(2,1)S(1)}, u32[]{:S(2)}, u32[]{:S(2)}) collective-permute-start(bf16[128,256]{1,0:T(8,128)(2,1)S(1)} %get-tuple-element.98), channel_id=1, source_target_pairs={{0,4},{2,6},{5,9},{7,11},{8,12},{10,14},{16,20},{18,22},{21,25},{2... | collective-permute-start | bytes 196616 | tf_op jit(solution)/shard_map/ppermute | solution.py:392
  8.3 1.6 %collective-permute-start.3 = (bf16[128,256]{1,0:T(8,128)(2,1)S(1)}, bf16[128,256]{1,0:T(8,128)(2,1)S(1)}, u32[]{:S(2)}, u32[]{:S(2)}) collective-permute-start(bf16[128,256]{1,0:T(8,128)(2,1)S(1)} %get-tuple-element.103), channel_id=1, source_target_pairs={{0,2},{2,0},{1,3},{3,1},{4,6},{6,4},{5,7},{7,5},{8,10},{10,8},{9,1... | collective-permute-start | bytes 196616 | tf_op jit(solution)/shard_map/ppermute | solution.py:379
  11.8 1.6 %adjacency.1 = (bf16[768,768]{1,0:T(8,128)(2,1)S(1)}, bf16[768,768]{1,0:T(8,128)(2,1)S(1)}, bf16[768,256]{1,0:T(8,128)(2,1)S(1)}, bf16[256,768]{1,0:T(8,128)(2,1)S(1)}) custom-call(s32[4,6]{1,0:T(4,128)S(1)} %bitcast.4, bf16[6,4,128,128]{3,2,1,0:T(8,128)(2,1)S(1)} %copy-done.3, bf16[128,768]{1,0:T(8,128)(2,1)S(1)} %get-tuple-element.99.refs_2_, ...), custom_call_target="tpu_custom_call" | custom-call | flops 150994944 | bytes 4000000 | tf_op jit(solution)/shard_map/adjacency/pallas_call | solution.py:32
  15.7 2.8 %collective-permute-start.5 = (bf16[128,256]{1,0:T(8,128)(2,1)S(1)}, bf16[128,256]{1,0:T(8,128)(2,1)S(1)}, u32[]{:S(2)}, u32[]{:S(2)}) collective-permute-start(bf16[128,256]{1,0:T(8,128)(2,1)S(1)} %get-tuple-element.107), channel_id=1, source_target_pairs={{0,4},{2,6},{5,9},{7,11},{8,12},{10,14},{16,20},{18,22},{21,25},{2... | collective-permute-start | bytes 196616 | tf_op jit(solution)/shard_map/ppermute | solution.py:392
  20.5 2.4 %collective-permute-done.6.refs_7_.refs_14_ = bf16[128,256]{1,0:T(8,128)(2,1)S(1)} collective-permute-done((bf16[128,256]{1,0:T(8,128)(2,1)S(1)}, bf16[128,256]{1,0:T(8,128)(2,1)S(1)}, u32[]{:S(2)}, u32[]{:S(2)}) %collective-permute-start.6) | collective-permute-done | bytes 65568 | tf_op jit(solution)/shard_map/ppermute | solution.py:379
  24.9 2.1 %collective-permute-start.8 = (bf16[128,256]{1,0:T(8,128)(2,1)S(1)}, bf16[128,256]{1,0:T(8,128)(2,1)S(1)}, u32[]{:S(2)}, u32[]{:S(2)}) collective-permute-start(bf16[128,256]{1,0:T(8,128)(2,1)S(1)} %get-tuple-element.113), channel_id=1, source_target_pairs={{0,4},{2,6},{5,9},{7,11},{8,12},{10,14},{16,20},{18,22},{21,25},{2... | collective-permute-start | bytes 196616 | tf_op jit(solution)/shard_map/ppermute | solution.py:392
  29.4 2.0 %collective-permute-done.9.refs_7_.refs_11_ = bf16[128,256]{1,0:T(8,128)(2,1)S(1)} collective-permute-done((bf16[128,256]{1,0:T(8,128)(2,1)S(1)}, bf16[128,256]{1,0:T(8,128)(2,1)S(1)}, u32[]{:S(2)}, u32[]{:S(2)}) %collective-permute-start.9) | collective-permute-done | bytes 65568 | tf_op jit(solution)/shard_map/ppermute | solution.py:379
  32.3 2.0 %turn.1 = (f32[768,256]{1,0:T(8,128)S(1)}, bf16[768,256]{1,0:T(8,128)(2,1)S(1)}, bf16[256,256]{1,0:T(8,128)(2,1)S(1)}, bf16[256,256]{1,0:T(8,128)(2,1)S(1)}, bf1...) custom-call(f32[768,256]{1,0:T(8,128)S(1)} %get-tuple-element.112.re, ...), custom_call_target="tpu_custom_call" | custom-call | flops 536870912 | bytes 4000000 | tf_op jit(solution)/shard_map/turn/pallas_call | solution.py:32
  34.3 1.5 %collective-permute-start.11 = (bf16[128,256]{1,0:T(8,128)(2,1)S(1)}, bf16[128,256]{1,0:T(8,128)(2,1)S(1)}, u32[]{:S(2)}, u32[]{:S(2)}) collective-permute-start(bf16[128,256]{1,0:T(8,128)(2,1)S(1)} %get-tuple-element.126), channel_id=1, source_target_pairs={{4,0},{8,4},{12,8},{5,1},{9,5},{13,9},{6,2},{10,6},{14,10},{7,3},{... | collective-permute-start | bytes 196616 | tf_op jit(solution)/shard_map/ppermute | solution.py:415
  36.8 3.0 %back2.1 = (f32[768,256]{1,0:T(8,128)S(1)}, f32[2048,128]{1,0:T(8,128)S(1)}) custom-call(bf16[768,256]{1,0:T(8,128)(2,1)S(1)} %get-tuple-element.119.refs_0_, bf16[768,256]{1,0:T(8,128)(2,1)S(1)} %get-tuple-element.114.refs_0_.refs_1_, bf16[768,768]{1,0:T(8,128)(2,1)S(1)} %get-tuple-element.120.refs_2_.refs_3_, bf16[3,256,512]{2,1,0:T(8,128)(2,1)S(1)} %copy-done, ...), custom_call_target="tpu_custom_call" | custom-call | flops 2717908992 | bytes 4000000 | tf_op jit(solution)/shard_map/back2/pallas_call | solution.py:32
  41.6 1.5 %join2.1 = (f32[768,256]{1,0:T(8,128)S(1)}, bf16[768,256]{1,0:T(8,128)(2,1)S(1)}, bf16[256,256]{1,0:T(8,128)(2,1)S(1)}, bf16[256,256]{1,0:T(8,128)(2,1)S(1)}, bf...) custom-call(f32[1024,128]{1,0:T(8,128)S(1)} %get-tuple-element.129.r, ...), custom_call_target="tpu_custom_call" | custom-call | flops 536870912 | bytes 4000000 | tf_op jit(solution)/shard_map/join2/pallas_call | solution.py:32
  43.0 1.3 %collective-permute-start.13 = (bf16[128,256]{1,0:T(8,128)(2,1)S(1)}, bf16[128,256]{1,0:T(8,128)(2,1)S(1)}, u32[]{:S(2)}, u32[]{:S(2)}) collective-permute-start(bf16[128,256]{1,0:T(8,128)(2,1)S(1)} %get-tuple-element.138), channel_id=1, source_target_pairs={{4,0},{8,4},{12,8},{5,1},{9,5},{13,9},{6,2},{10,6},{14,10},{7,3},{... | collective-permute-start | bytes 196616 | tf_op jit(solution)/shard_map/ppermute | solution.py:415
  45.5 3.0 %back1.1 = (f32[768,256]{1,0:T(8,128)S(1)}, f32[2048,128]{1,0:T(8,128)S(1)}) custom-call(bf16[768,256]{1,0:T(8,128)(2,1)S(1)} %get-tuple-element.132.refs_0_.refs_1_, bf16[768,256]{1,0:T(8,128)(2,1)S(1)} %get-tuple-element.132.refs_0_.refs_1_, bf16[768,256]{1,0:T(8,128)(2,1)S(1)} %get-tuple-element.108.refs_0_.refs_2_, ...), custom_call_target="tpu_custom_call" | custom-call | flops 2717908992 | bytes 4000000 | tf_op jit(solution)/shard_map/back1/pallas_call | solution.py:32
  50.8 2.2 %collective-permute-start.16 = (bf16[512,128]{1,0:T(8,128)(2,1)S(1)}, bf16[512,128]{1,0:T(8,128)(2,1)S(1)}, u32[]{:S(2)}, u32[]{:S(2)}) collective-permute-start(bf16[512,128]{1,0:T(8,128)(2,1)S(1)} %get-tuple-element.151), channel_id=1, source_target_pairs={{0,4},{1,3},{2,6},{3,1},{4,0},{5,7},{6,2},{7,5},{8,12},{9,11},{10,... | collective-permute-start | bytes 393224 | tf_op jit(solution)/shard_map/ppermute | solution.py:392
  53.0 1.5 %join1.1 = (f32[768,256]{1,0:T(8,128)S(1)}, bf16[768,256]{1,0:T(8,128)(2,1)S(1)}, bf16[256,256]{1,0:T(8,128)(2,1)S(1)}, bf16[256,256]{1,0:T(8,128)(2,1)S(1)}, bf...) custom-call(f32[512,128]{1,0:T(8,128)S(1)} %get-tuple-element.143.re, ...), custom_call_target="tpu_custom_call" | custom-call | flops 536870912 | bytes 4000000 | tf_op jit(solution)/shard_map/join1/pallas_call | solution.py:32
  54.5 3.0 %back0.1 = (f32[768,256]{1,0:T(8,128)S(1)}, f32[2048,128]{1,0:T(8,128)S(1)}) custom-call(bf16[768,256]{1,0:T(8,128)(2,1)S(1)} %get-tuple-element.145.refs_0_.refs_1_, bf16[768,256]{1,0:T(8,128)(2,1)S(1)} %get-tuple-element.145.refs_0_.refs_1_, bf16[768,256]{1,0:T(8,128)(2,1)S(1)} %get-tuple-element.97.refs_0_.refs_2_, ...), custom_call_target="tpu_custom_call" | custom-call | flops 2717908992 | bytes 4000000 | tf_op jit(solution)/shard_map/back0/pallas_call | solution.py:32
  58.6 2.0 %collective-permute-start.19 = (bf16[512,128]{1,0:T(8,128)(2,1)S(1)}, bf16[512,128]{1,0:T(8,128)(2,1)S(1)}, u32[]{:S(2)}, u32[]{:S(2)}) collective-permute-start(bf16[512,128]{1,0:T(8,128)(2,1)S(1)} %get-tuple-element.159), channel_id=1, source_target_pairs={{0,8},{1,9},{2,10},{3,11},{4,12},{5,13},{6,14},{7,15},{8,0},{9,1},... | collective-permute-start | bytes 393224 | tf_op jit(solution)/shard_map/ppermute | solution.py:392
  60.7 1.6 %collective-permute-start.20 = (bf16[512,128]{1,0:T(8,128)(2,1)S(1)}, bf16[512,128]{1,0:T(8,128)(2,1)S(1)}, u32[]{:S(2)}, u32[]{:S(2)}) collective-permute-start(bf16[512,128]{1,0:T(8,128)(2,1)S(1)} %get-tuple-element.161), channel_id=1, source_target_pairs={{0,4},{1,3},{2,6},{3,1},{4,0},{5,7},{6,2},{7,5},{8,12},{9,11},{10,... | collective-permute-start | bytes 393224 | tf_op jit(solution)/shard_map/ppermute | solution.py:392
  62.4 1.7 %collective-permute-done.18.refs_2_ = bf16[1024,128]{1,0:T(8,128)(2,1)S(1)} collective-permute-done((bf16[1024,128]{1,0:T(8,128)(2,1)S(1)}, bf16[1024,128]{1,0:T(8,128)(2,1)S(1)}, u32[]{:S(2)}, u32[]{:S(2)}) %collective-permute-start.18) | collective-permute-done | bytes 262176 | tf_op jit(solution)/shard_map/ppermute | solution.py:392
  64.1 2.2 %collective-permute-start.21 = (bf16[512,128]{1,0:T(8,128)(2,1)S(1)}, bf16[512,128]{1,0:T(8,128)(2,1)S(1)}, u32[]{:S(2)}, u32[]{:S(2)}) collective-permute-start(bf16[512,128]{1,0:T(8,128)(2,1)S(1)} %get-tuple-element.163), channel_id=1, source_target_pairs={{0,4},{1,3},{2,6},{3,1},{4,0},{5,7},{6,2},{7,5},{8,12},{9,11},{10,... | collective-permute-start | bytes 393224 | tf_op jit(solution)/shard_map/ppermute | solution.py:392
  67.1 2.8 %collective-permute-start.23 = (bf16[512,128]{1,0:T(8,128)(2,1)S(1)}, bf16[512,128]{1,0:T(8,128)(2,1)S(1)}, u32[]{:S(2)}, u32[]{:S(2)}) collective-permute-start(bf16[512,128]{1,0:T(8,128)(2,1)S(1)} %get-tuple-element.167), channel_id=1, source_target_pairs={{0,8},{1,9},{2,10},{3,11},{4,12},{5,13},{6,14},{7,15},{8,0},{9,1},... | collective-permute-start | bytes 393224 | tf_op jit(solution)/shard_map/ppermute | solution.py:392
  69.9 1.4 %collective-permute-done.21.refs_2_ = bf16[512,128]{1,0:T(8,128)(2,1)S(1)} collective-permute-done((bf16[512,128]{1,0:T(8,128)(2,1)S(1)}, bf16[512,128]{1,0:T(8,128)(2,1)S(1)}, u32[]{:S(2)}, u32[]{:S(2)}) %collective-permute-start.21) | collective-permute-done | bytes 131104 | tf_op jit(solution)/shard_map/ppermute | solution.py:392
  71.3 3.6 %collective-permute-start.24 = (bf16[512,128]{1,0:T(8,128)(2,1)S(1)}, bf16[512,128]{1,0:T(8,128)(2,1)S(1)}, u32[]{:S(2)}, u32[]{:S(2)}) collective-permute-start(bf16[512,128]{1,0:T(8,128)(2,1)S(1)} %get-tuple-element.169), channel_id=1, source_target_pairs={{0,8},{1,9},{2,10},{3,11},{4,12},{5,13},{6,14},{7,15},{8,0},{9,1},... | collective-permute-start | bytes 393224 | tf_op jit(solution)/shard_map/ppermute | solution.py:392
  74.9 1.5 %collective-permute-done.22.refs_2_ = bf16[512,128]{1,0:T(8,128)(2,1)S(1)} collective-permute-done((bf16[512,128]{1,0:T(8,128)(2,1)S(1)}, bf16[512,128]{1,0:T(8,128)(2,1)S(1)}, u32[]{:S(2)}, u32[]{:S(2)}) %collective-permute-start.22) | collective-permute-done | bytes 131104 | tf_op jit(solution)/shard_map/ppermute | solution.py:392
  77.0 2.2 %collective-permute-start.25 = (bf16[512,128]{1,0:T(8,128)(2,1)S(1)}, bf16[512,128]{1,0:T(8,128)(2,1)S(1)}, u32[]{:S(2)}, u32[]{:S(2)}) collective-permute-start(bf16[512,128]{1,0:T(8,128)(2,1)S(1)} %get-tuple-element.171), channel_id=1, source_target_pairs={{0,4},{1,3},{2,6},{3,1},{4,0},{5,7},{6,2},{7,5},{8,12},{9,11},{10,... | collective-permute-start | bytes 393224 | tf_op jit(solution)/shard_map/ppermute | solution.py:392
  79.3 2.7 %collective-permute-start.27 = (bf16[512,128]{1,0:T(8,128)(2,1)S(1)}, bf16[512,128]{1,0:T(8,128)(2,1)S(1)}, u32[]{:S(2)}, u32[]{:S(2)}) collective-permute-start(bf16[512,128]{1,0:T(8,128)(2,1)S(1)} %get-tuple-element.174), channel_id=1, source_target_pairs={{0,4},{1,3},{2,6},{3,1},{4,0},{5,7},{6,2},{7,5},{8,12},{9,11},{10,... | collective-permute-start | bytes 393224 | tf_op jit(solution)/shard_map/ppermute | solution.py:392
  82.0 1.6 %collective-permute-done.25.refs_2_ = bf16[512,128]{1,0:T(8,128)(2,1)S(1)} collective-permute-done((bf16[512,128]{1,0:T(8,128)(2,1)S(1)}, bf16[512,128]{1,0:T(8,128)(2,1)S(1)}, u32[]{:S(2)}, u32[]{:S(2)}) %collective-permute-start.25) | collective-permute-done | bytes 131104 | tf_op jit(solution)/shard_map/ppermute | solution.py:392
  83.6 1.6 %collective-permute-start.28 = (bf16[1024,128]{1,0:T(8,128)(2,1)S(1)}, bf16[1024,128]{1,0:T(8,128)(2,1)S(1)}, u32[]{:S(2)}, u32[]{:S(2)}) collective-permute-start(bf16[1024,128]{1,0:T(8,128)(2,1)S(1)} %get-tuple-element.179), channel_id=1, source_target_pairs={{0,2},{1,5},{2,0},{3,7},{4,6},{5,1},{6,4},{7,3},{8,10},{9,13},{10,... | collective-permute-start | bytes 786440 | tf_op jit(solution)/shard_map/ppermute | solution.py:392
  86.4 1.6 %collective-permute-start.31 = (bf16[1024,128]{1,0:T(8,128)(2,1)S(1)}, bf16[1024,128]{1,0:T(8,128)(2,1)S(1)}, u32[]{:S(2)}, u32[]{:S(2)}) collective-permute-start(bf16[1024,128]{1,0:T(8,128)(2,1)S(1)} %get-tuple-element.188), channel_id=1, source_target_pairs={{0,2},{1,5},{2,0},{3,7},{4,6},{5,1},{6,4},{7,3},{8,10},{9,13},{10,... | collective-permute-start | bytes 786440 | tf_op jit(solution)/shard_map/ppermute | solution.py:392
  88.0 1.3 %collective-permute-start.29 = (bf16[128,256]{1,0:T(8,128)(2,1)S(1)}, bf16[128,256]{1,0:T(8,128)(2,1)S(1)}, u32[]{:S(2)}, u32[]{:S(2)}) collective-permute-start(bf16[128,256]{1,0:T(8,128)(2,1)S(1)} %get-tuple-element.182), channel_id=1, source_target_pairs={{4,0},{8,4},{12,8},{5,1},{9,5},{13,9},{6,2},{10,6},{14,10},{7,3},{... | collective-permute-start | bytes 196616 | tf_op jit(solution)/shard_map/ppermute | solution.py:415
  92.2 2.0 %collective-permute-done.29.refs_4_ = bf16[128,256]{1,0:T(8,128)(2,1)S(1)} collective-permute-done((bf16[128,256]{1,0:T(8,128)(2,1)S(1)}, bf16[128,256]{1,0:T(8,128)(2,1)S(1)}, u32[]{:S(2)}, u32[]{:S(2)}) %collective-permute-start.29) | collective-permute-done | bytes 65568 | tf_op jit(solution)/shard_map/ppermute | solution.py:415
  95.3 1.7 %write0.1 = (f32[3,256,512]{2,1,0:T(8,128)}, f32[3,512,256]{2,1,0:T(8,128)}, f32[8,128]{1,0:T(8,128)}) custom-call(f32[3,256,512]{2,1,0:T(8,128)} %get-tuple-element.185.refs_0_, f32[3,512,256]{2,1,0:T(8,128)} %get-tuple-element.186.refs_1_, f32[8,128]{1,0:T(8,128)S(1)} %get-tuple-element.187.refs_2_, ...), custom_call_target="tpu_custom_call", output_to_operand_aliasing={{0}: (0, {}), {1}: (1, {})} | custom-call | flops 1 | bytes 1 | tf_op jit(solution)/shard_map/write0/pallas_call | solution.py:567
  (81 shorter events, 28.4 us)
Async XLA Ops:
  0.6 9.3 %collective-permute-start.1 = (bf16[3,256,512]{2,1,0:T(8,128)(2,1)}, bf16[3,256,512]{2,1,0:T(8,128)(2,1)S(1)}, u32[]{:S(2)}, u32[]{:S(2)}) collective-permute-start(bf16[3,256,512]{2,1,0:T(8,128)(2,1)} %refs_4_.9), channel_id=1, source_target_pairs={{0,1},{1,0},{2,3},{3,2},{4,5},{5,4},{6,7},{7,6},{8,9},{9,8},{10,11... | collective-permute-start | bytes 2359304 | tf_op jit(solution)/shard_map/ppermute | solution.py:379
  1.1 8.8 %collective-permute-start.2 = (bf16[3,512,256]{2,1,0:T(8,128)(2,1)}, bf16[3,512,256]{2,1,0:T(8,128)(2,1)S(1)}, u32[]{:S(2)}, u32[]{:S(2)}) collective-permute-start(bf16[3,512,256]{2,1,0:T(8,128)(2,1)} %refs_6_.11), channel_id=1, source_target_pairs={{0,1},{1,0},{2,3},{3,2},{4,5},{5,4},{6,7},{7,6},{8,9},{9,8},{10,11... | collective-permute-start | bytes 2359304 | tf_op jit(solution)/shard_map/ppermute | solution.py:379
  3.3 10.0 %collective-permute-start = (bf16[128,256]{1,0:T(8,128)(2,1)S(1)}, bf16[128,256]{1,0:T(8,128)(2,1)S(1)}, u32[]{:S(2)}, u32[]{:S(2)}) collective-permute-start(bf16[128,256]{1,0:T(8,128)(2,1)S(1)} %get-tuple-element.98), channel_id=1, source_target_pairs={{0,4},{2,6},{5,9},{7,11},{8,12},{10,14},{16,20},{18,22},{21,25},{2... | collective-permute-start | bytes 196616 | tf_op jit(solution)/shard_map/ppermute | solution.py:392
  8.3 5.1 %collective-permute-start.3 = (bf16[128,256]{1,0:T(8,128)(2,1)S(1)}, bf16[128,256]{1,0:T(8,128)(2,1)S(1)}, u32[]{:S(2)}, u32[]{:S(2)}) collective-permute-start(bf16[128,256]{1,0:T(8,128)(2,1)S(1)} %get-tuple-element.103), channel_id=1, source_target_pairs={{0,2},{2,0},{1,3},{3,1},{4,6},{6,4},{5,7},{7,5},{8,10},{10,8},{9,1... | collective-permute-start | bytes 196616 | tf_op jit(solution)/shard_map/ppermute | solution.py:379
  13.4 1.3 %collective-permute-start.4 = (bf16[128,256]{1,0:T(8,128)(2,1)S(1)}, bf16[128,256]{1,0:T(8,128)(2,1)S(1)}, u32[]{:S(2)}, u32[]{:S(2)}) collective-permute-start(bf16[128,256]{1,0:T(8,128)(2,1)S(1)} %collective-permute-done.refs_8_.refs_12_), channel_id=1, source_target_pairs={{0,1},{1,0},{2,3},{3,2},{4,5},{5,4},{6,7},{7,6},{8,9},{9,8},{10,11... | collective-permute-start | bytes 196616 | tf_op jit(solution)/shard_map/ppermute | solution.py:379
  15.7 4.7 %collective-permute-start.5 = (bf16[128,256]{1,0:T(8,128)(2,1)S(1)}, bf16[128,256]{1,0:T(8,128)(2,1)S(1)}, u32[]{:S(2)}, u32[]{:S(2)}) collective-permute-start(bf16[128,256]{1,0:T(8,128)(2,1)S(1)} %get-tuple-element.107), channel_id=1, source_target_pairs={{0,4},{2,6},{5,9},{7,11},{8,12},{10,14},{16,20},{18,22},{21,25},{2... | collective-permute-start | bytes 196616 | tf_op jit(solution)/shard_map/ppermute | solution.py:392
  18.5 4.3 %collective-permute-start.6 = (bf16[128,256]{1,0:T(8,128)(2,1)S(1)}, bf16[128,256]{1,0:T(8,128)(2,1)S(1)}, u32[]{:S(2)}, u32[]{:S(2)}) collective-permute-start(bf16[128,256]{1,0:T(8,128)(2,1)S(1)} %get-tuple-element.110), channel_id=1, source_target_pairs={{0,2},{2,0},{1,3},{3,1},{4,6},{6,4},{5,7},{7,5},{8,10},{10,8},{9,1... | collective-permute-start | bytes 196616 | tf_op jit(solution)/shard_map/ppermute | solution.py:379
  20.4 3.4 %collective-permute-start.7 = (bf16[128,256]{1,0:T(8,128)(2,1)S(1)}, bf16[128,256]{1,0:T(8,128)(2,1)S(1)}, u32[]{:S(2)}, u32[]{:S(2)}) collective-permute-start(bf16[128,256]{1,0:T(8,128)(2,1)S(1)} %collective-permute-done.5.refs_8_.refs_12_), channel_id=1, source_target_pairs={{0,1},{1,0},{2,3},{3,2},{4,5},{5,4},{6,7},{7,6},{8,9},{9,8},{10,11... | collective-permute-start | bytes 196616 | tf_op jit(solution)/shard_map/ppermute | solution.py:379
  24.9 4.3 %collective-permute-start.8 = (bf16[128,256]{1,0:T(8,128)(2,1)S(1)}, bf16[128,256]{1,0:T(8,128)(2,1)S(1)}, u32[]{:S(2)}, u32[]{:S(2)}) collective-permute-start(bf16[128,256]{1,0:T(8,128)(2,1)S(1)} %get-tuple-element.113), channel_id=1, source_target_pairs={{0,4},{2,6},{5,9},{7,11},{8,12},{10,14},{16,20},{18,22},{21,25},{2... | collective-permute-start | bytes 196616 | tf_op jit(solution)/shard_map/ppermute | solution.py:392
  27.0 4.3 %collective-permute-start.9 = (bf16[128,256]{1,0:T(8,128)(2,1)S(1)}, bf16[128,256]{1,0:T(8,128)(2,1)S(1)}, u32[]{:S(2)}, u32[]{:S(2)}) collective-permute-start(bf16[128,256]{1,0:T(8,128)(2,1)S(1)} %get-tuple-element.116), channel_id=1, source_target_pairs={{0,2},{2,0},{1,3},{3,1},{4,6},{6,4},{5,7},{7,5},{8,10},{10,8},{9,1... | collective-permute-start | bytes 196616 | tf_op jit(solution)/shard_map/ppermute | solution.py:379
  29.3 3.0 %collective-permute-start.10 = (bf16[128,256]{1,0:T(8,128)(2,1)S(1)}, bf16[128,256]{1,0:T(8,128)(2,1)S(1)}, u32[]{:S(2)}, u32[]{:S(2)}) collective-permute-start(bf16[128,256]{1,0:T(8,128)(2,1)S(1)} %collective-permute-done.8.refs_9_), channel_id=1, source_target_pairs={{0,1},{1,0},{2,3},{3,2},{4,5},{5,4},{6,7},{7,6},{8,9},{9,8},{10,11... | collective-permute-start | bytes 196616 | tf_op jit(solution)/shard_map/ppermute | solution.py:379
  34.3 6.2 %collective-permute-start.11 = (bf16[128,256]{1,0:T(8,128)(2,1)S(1)}, bf16[128,256]{1,0:T(8,128)(2,1)S(1)}, u32[]{:S(2)}, u32[]{:S(2)}) collective-permute-start(bf16[128,256]{1,0:T(8,128)(2,1)S(1)} %get-tuple-element.126), channel_id=1, source_target_pairs={{4,0},{8,4},{12,8},{5,1},{9,5},{13,9},{6,2},{10,6},{14,10},{7,3},{... | collective-permute-start | bytes 196616 | tf_op jit(solution)/shard_map/ppermute | solution.py:415
  35.8 4.7 %collective-permute-start.12 = (bf16[128,256]{1,0:T(8,128)(2,1)S(1)}, bf16[128,256]{1,0:T(8,128)(2,1)S(1)}, u32[]{:S(2)}, u32[]{:S(2)}) collective-permute-start(bf16[128,256]{1,0:T(8,128)(2,1)S(1)} %get-tuple-element.127), channel_id=1, source_target_pairs={{0,2},{2,0},{1,3},{3,1},{4,6},{6,4},{5,7},{7,5},{8,10},{10,8},{9,1... | collective-permute-start | bytes 196616 | tf_op jit(solution)/shard_map/ppermute | solution.py:379
  40.6 10.1 %collective-permute-start.15 = (bf16[1024,128]{1,0:T(8,128)(2,1)S(1)}, bf16[1024,128]{1,0:T(8,128)(2,1)S(1)}, u32[]{:S(2)}, u32[]{:S(2)}) collective-permute-start(bf16[1024,128]{1,0:T(8,128)(2,1)S(1)} %get-tuple-element.142), channel_id=1, source_target_pairs={{0,2},{1,5},{2,0},{3,7},{4,6},{5,1},{6,4},{7,3},{8,10},{9,13},{10,... | collective-permute-start | bytes 786440 | tf_op jit(solution)/shard_map/ppermute | solution.py:392
  43.0 6.4 %collective-permute-start.13 = (bf16[128,256]{1,0:T(8,128)(2,1)S(1)}, bf16[128,256]{1,0:T(8,128)(2,1)S(1)}, u32[]{:S(2)}, u32[]{:S(2)}) collective-permute-start(bf16[128,256]{1,0:T(8,128)(2,1)S(1)} %get-tuple-element.138), channel_id=1, source_target_pairs={{4,0},{8,4},{12,8},{5,1},{9,5},{13,9},{6,2},{10,6},{14,10},{7,3},{... | collective-permute-start | bytes 196616 | tf_op jit(solution)/shard_map/ppermute | solution.py:415
  44.3 5.1 %collective-permute-start.14 = (bf16[128,256]{1,0:T(8,128)(2,1)S(1)}, bf16[128,256]{1,0:T(8,128)(2,1)S(1)}, u32[]{:S(2)}, u32[]{:S(2)}) collective-permute-start(bf16[128,256]{1,0:T(8,128)(2,1)S(1)} %get-tuple-element.139), channel_id=1, source_target_pairs={{0,2},{2,0},{1,3},{3,1},{4,6},{6,4},{5,7},{7,5},{8,10},{10,8},{9,1... | collective-permute-start | bytes 196616 | tf_op jit(solution)/shard_map/ppermute | solution.py:379
  49.6 11.1 %collective-permute-start.17 = (bf16[1024,128]{1,0:T(8,128)(2,1)S(1)}, bf16[1024,128]{1,0:T(8,128)(2,1)S(1)}, u32[]{:S(2)}, u32[]{:S(2)}) collective-permute-start(bf16[1024,128]{1,0:T(8,128)(2,1)S(1)} %get-tuple-element.155), channel_id=1, source_target_pairs={{0,2},{1,5},{2,0},{3,7},{4,6},{5,1},{6,4},{7,3},{8,10},{9,13},{10,... | collective-permute-start | bytes 786440 | tf_op jit(solution)/shard_map/ppermute | solution.py:392
  50.8 6.7 %collective-permute-start.16 = (bf16[512,128]{1,0:T(8,128)(2,1)S(1)}, bf16[512,128]{1,0:T(8,128)(2,1)S(1)}, u32[]{:S(2)}, u32[]{:S(2)}) collective-permute-start(bf16[512,128]{1,0:T(8,128)(2,1)S(1)} %get-tuple-element.151), channel_id=1, source_target_pairs={{0,4},{1,3},{2,6},{3,1},{4,0},{5,7},{6,2},{7,5},{8,12},{9,11},{10,... | collective-permute-start | bytes 393224 | tf_op jit(solution)/shard_map/ppermute | solution.py:392
  57.6 6.4 %collective-permute-start.18 = (bf16[1024,128]{1,0:T(8,128)(2,1)S(1)}, bf16[1024,128]{1,0:T(8,128)(2,1)S(1)}, u32[]{:S(2)}, u32[]{:S(2)}) collective-permute-start(bf16[1024,128]{1,0:T(8,128)(2,1)S(1)} %get-tuple-element.157), channel_id=1, source_target_pairs={{0,2},{1,5},{2,0},{3,7},{4,6},{5,1},{6,4},{7,3},{8,10},{9,13},{10,... | collective-permute-start | bytes 786440 | tf_op jit(solution)/shard_map/ppermute | solution.py:392
  58.6 7.7 %collective-permute-start.19 = (bf16[512,128]{1,0:T(8,128)(2,1)S(1)}, bf16[512,128]{1,0:T(8,128)(2,1)S(1)}, u32[]{:S(2)}, u32[]{:S(2)}) collective-permute-start(bf16[512,128]{1,0:T(8,128)(2,1)S(1)} %get-tuple-element.159), channel_id=1, source_target_pairs={{0,8},{1,9},{2,10},{3,11},{4,12},{5,13},{6,14},{7,15},{8,0},{9,1},... | collective-permute-start | bytes 393224 | tf_op jit(solution)/shard_map/ppermute | solution.py:392
  60.7 6.3 %collective-permute-start.20 = (bf16[512,128]{1,0:T(8,128)(2,1)S(1)}, bf16[512,128]{1,0:T(8,128)(2,1)S(1)}, u32[]{:S(2)}, u32[]{:S(2)}) collective-permute-start(bf16[512,128]{1,0:T(8,128)(2,1)S(1)} %get-tuple-element.161), channel_id=1, source_target_pairs={{0,4},{1,3},{2,6},{3,1},{4,0},{5,7},{6,2},{7,5},{8,12},{9,11},{10,... | collective-permute-start | bytes 393224 | tf_op jit(solution)/shard_map/ppermute | solution.py:392
  64.1 7.1 %collective-permute-start.21 = (bf16[512,128]{1,0:T(8,128)(2,1)S(1)}, bf16[512,128]{1,0:T(8,128)(2,1)S(1)}, u32[]{:S(2)}, u32[]{:S(2)}) collective-permute-start(bf16[512,128]{1,0:T(8,128)(2,1)S(1)} %get-tuple-element.163), channel_id=1, source_target_pairs={{0,4},{1,3},{2,6},{3,1},{4,0},{5,7},{6,2},{7,5},{8,12},{9,11},{10,... | collective-permute-start | bytes 393224 | tf_op jit(solution)/shard_map/ppermute | solution.py:392
  66.4 10.0 %collective-permute-start.22 = (bf16[512,128]{1,0:T(8,128)(2,1)S(1)}, bf16[512,128]{1,0:T(8,128)(2,1)S(1)}, u32[]{:S(2)}, u32[]{:S(2)}) collective-permute-start(bf16[512,128]{1,0:T(8,128)(2,1)S(1)} %get-tuple-element.165), channel_id=1, source_target_pairs={{0,4},{1,3},{2,6},{3,1},{4,0},{5,7},{6,2},{7,5},{8,12},{9,11},{10,... | collective-permute-start | bytes 393224 | tf_op jit(solution)/shard_map/ppermute | solution.py:392
  67.1 9.8 %collective-permute-start.23 = (bf16[512,128]{1,0:T(8,128)(2,1)S(1)}, bf16[512,128]{1,0:T(8,128)(2,1)S(1)}, u32[]{:S(2)}, u32[]{:S(2)}) collective-permute-start(bf16[512,128]{1,0:T(8,128)(2,1)S(1)} %get-tuple-element.167), channel_id=1, source_target_pairs={{0,8},{1,9},{2,10},{3,11},{4,12},{5,13},{6,14},{7,15},{8,0},{9,1},... | collective-permute-start | bytes 393224 | tf_op jit(solution)/shard_map/ppermute | solution.py:392
  71.3 7.9 %collective-permute-start.24 = (bf16[512,128]{1,0:T(8,128)(2,1)S(1)}, bf16[512,128]{1,0:T(8,128)(2,1)S(1)}, u32[]{:S(2)}, u32[]{:S(2)}) collective-permute-start(bf16[512,128]{1,0:T(8,128)(2,1)S(1)} %get-tuple-element.169), channel_id=1, source_target_pairs={{0,8},{1,9},{2,10},{3,11},{4,12},{5,13},{6,14},{7,15},{8,0},{9,1},... | collective-permute-start | bytes 393224 | tf_op jit(solution)/shard_map/ppermute | solution.py:392
  76.4 8.8 %collective-permute-start.26 = (bf16[1024,128]{1,0:T(8,128)(2,1)S(1)}, bf16[1024,128]{1,0:T(8,128)(2,1)S(1)}, u32[]{:S(2)}, u32[]{:S(2)}) collective-permute-start(bf16[1024,128]{1,0:T(8,128)(2,1)S(1)} %get-tuple-element.173), channel_id=1, source_target_pairs={{0,2},{1,5},{2,0},{3,7},{4,6},{5,1},{6,4},{7,3},{8,10},{9,13},{10,... | collective-permute-start | bytes 786440 | tf_op jit(solution)/shard_map/ppermute | solution.py:392
  77.0 6.6 %collective-permute-start.25 = (bf16[512,128]{1,0:T(8,128)(2,1)S(1)}, bf16[512,128]{1,0:T(8,128)(2,1)S(1)}, u32[]{:S(2)}, u32[]{:S(2)}) collective-permute-start(bf16[512,128]{1,0:T(8,128)(2,1)S(1)} %get-tuple-element.171), channel_id=1, source_target_pairs={{0,4},{1,3},{2,6},{3,1},{4,0},{5,7},{6,2},{7,5},{8,12},{9,11},{10,... | collective-permute-start | bytes 393224 | tf_op jit(solution)/shard_map/ppermute | solution.py:392
  79.3 7.1 %collective-permute-start.27 = (bf16[512,128]{1,0:T(8,128)(2,1)S(1)}, bf16[512,128]{1,0:T(8,128)(2,1)S(1)}, u32[]{:S(2)}, u32[]{:S(2)}) collective-permute-start(bf16[512,128]{1,0:T(8,128)(2,1)S(1)} %get-tuple-element.174), channel_id=1, source_target_pairs={{0,4},{1,3},{2,6},{3,1},{4,0},{5,7},{6,2},{7,5},{8,12},{9,11},{10,... | collective-permute-start | bytes 393224 | tf_op jit(solution)/shard_map/ppermute | solution.py:392
  83.6 7.4 %collective-permute-start.28 = (bf16[1024,128]{1,0:T(8,128)(2,1)S(1)}, bf16[1024,128]{1,0:T(8,128)(2,1)S(1)}, u32[]{:S(2)}, u32[]{:S(2)}) collective-permute-start(bf16[1024,128]{1,0:T(8,128)(2,1)S(1)} %get-tuple-element.179), channel_id=1, source_target_pairs={{0,2},{1,5},{2,0},{3,7},{4,6},{5,1},{6,4},{7,3},{8,10},{9,13},{10,... | collective-permute-start | bytes 786440 | tf_op jit(solution)/shard_map/ppermute | solution.py:392
  86.4 8.9 %collective-permute-start.31 = (bf16[1024,128]{1,0:T(8,128)(2,1)S(1)}, bf16[1024,128]{1,0:T(8,128)(2,1)S(1)}, u32[]{:S(2)}, u32[]{:S(2)}) collective-permute-start(bf16[1024,128]{1,0:T(8,128)(2,1)S(1)} %get-tuple-element.188), channel_id=1, source_target_pairs={{0,2},{1,5},{2,0},{3,7},{4,6},{5,1},{6,4},{7,3},{8,10},{9,13},{10,... | collective-permute-start | bytes 786440 | tf_op jit(solution)/shard_map/ppermute | solution.py:392
  88.0 6.1 %collective-permute-start.29 = (bf16[128,256]{1,0:T(8,128)(2,1)S(1)}, bf16[128,256]{1,0:T(8,128)(2,1)S(1)}, u32[]{:S(2)}, u32[]{:S(2)}) collective-permute-start(bf16[128,256]{1,0:T(8,128)(2,1)S(1)} %get-tuple-element.182), channel_id=1, source_target_pairs={{4,0},{8,4},{12,8},{5,1},{9,5},{13,9},{6,2},{10,6},{14,10},{7,3},{... | collective-permute-start | bytes 196616 | tf_op jit(solution)/shard_map/ppermute | solution.py:415
  89.3 4.9 %collective-permute-start.30 = (bf16[128,256]{1,0:T(8,128)(2,1)S(1)}, bf16[128,256]{1,0:T(8,128)(2,1)S(1)}, u32[]{:S(2)}, u32[]{:S(2)}) collective-permute-start(bf16[128,256]{1,0:T(8,128)(2,1)S(1)} %get-tuple-element.183), channel_id=1, source_target_pairs={{0,2},{2,0},{1,3},{3,1},{4,6},{6,4},{5,7},{7,5},{8,10},{10,8},{9,1... | collective-permute-start | bytes 196616 | tf_op jit(solution)/shard_map/ppermute | solution.py:379
  (6 other events, 21.6 us)

commit v11 on v10

--- a/solution.py
+++ b/solution.py
@@ -142,27 +142,39 @@
     remote_t[...] = far.T.astype(BF16)
 
 
-def own_messages(layer, inputs, weights, msg):
-    wi0, wi1, wo0, wo1 = weights
-    halves = [(wi0[layer], wo0[layer]), (wi1[layer], wo1[layer])]
-    for r in range(0, inputs.shape[0], 256):
-        msg[r : r + 256, :] = message_of(inputs[r : r + 256, :], halves)
-
-
-def local_kernel(layer, *refs):
-    own_messages(layer, refs[0], refs[1:5], refs[5])
-
-
-def half_kernel(x, w_in, w_out, part):
+def message_half(x, w_in, w_out, slope, act_t=None):
+    pre = mm(x, w_in)
+    sig = sigmoid(pre)
+    act = (pre * sig).astype(BF16)
+    slope[...] = (sig * (1.0 + pre * (1.0 - sig))).astype(BF16)
+    if act_t is not None:
+        act_t[...] = act.T
+    return mm(act, w_out)
+
+
+def local_kernel(layer, x, wi0, wi1, wo0, wo1, msg, slope0, slope1, act_t, x_t):
     for r in range(0, x.shape[0], 256):
         here = slice(r, r + 256)
-        part[here, :] = half_message(x[here, :], w_in[0], w_out[0])
-
-
-def other_half_kernel(x, w_in, w_out, part, msg):
+        rows = x[here, :]
+        x_t[:, here] = rows.T
+        part = message_half(rows, wi0[layer], wo0[layer], slope0.at[here, :], act_t.at[:, here])
+        part = part + message_half(rows, wi1[layer], wo1[layer], slope1.at[here, :])
+        msg[here, :] = part.astype(BF16)
+
+
+def half_kernel(x, w_in, w_out, part, slope1):
     for r in range(0, x.shape[0], 256):
         here = slice(r, r + 256)
-        msg[here, :] = (part[here, :] + half_message(x[here, :], w_in[0], w_out[0])).astype(BF16)
+        part[here, :] = message_half(x[here, :], w_in[0], w_out[0], slope1.at[here, :])
+
+
+def other_half_kernel(x, w_in, w_out, part, msg, slope0, act_t, x_t):
+    for r in range(0, x.shape[0], 256):
+        here = slice(r, r + 256)
+        rows = x[here, :]
+        x_t[:, here] = rows.T
+        own = message_half(rows, w_in[0], w_out[0], slope0.at[here, :], act_t.at[:, here])
+        msg[here, :] = (part[here, :] + own).astype(BF16)
 
 
 def remote_mixed(layer, received, columns, weights):
@@ -228,22 +240,23 @@
 
 
 def back_kernel(layer, grad_scale, *refs):
-    dround, inputs, local_t = refs[:3]
-    wi0, wi1, wo0, wo1 = refs[3:7]
-    far_x, far_dmsg, far_act, far_dpre = refs[7:11]
-    back, grads, dmsg, act, dpre = refs[11:]
-    halves = [(wi0[layer], wo0[layer]), (wi1[layer], wo1[layer])]
+    dround, local_t, slope0, slope1, act_t, x_t = refs[:6]
+    wi0, wi1, wo0, wo1 = refs[6:10]
+    far_x, far_dmsg, far_act, far_dpre = refs[10:14]
+    back, grads, dmsg, dpre = refs[14:]
     dmsg[...] = mm(local_t[...], dround[...]).astype(BF16)
-    for r in range(0, inputs.shape[0], 256):
+    for r in range(0, dmsg.shape[0], 256):
         here = slice(r, r + 256)
-        back[here, :], (act[here, :], dpre[here, :]) = message_grad(
-            inputs[here, :], dmsg[here, :], halves
-        )
-    latent, hidden = inputs.shape[1], act.shape[1]
-    g_in = (mm(inputs[...], dpre[...], TN) + mm(far_x[...], far_dpre[...], TN)) * grad_scale
+        rows = dmsg[here, :]
+        dpre0 = (mm(rows, wo0[layer], NT) * slope0[here, :].astype(F32)).astype(BF16)
+        dpre1 = (mm(rows, wo1[layer], NT) * slope1[here, :].astype(F32)).astype(BF16)
+        dpre[here, :] = dpre0
+        back[here, :] = mm(dpre0, wi0[layer], NT) + mm(dpre1, wi1[layer], NT)
+    latent, hidden = x_t.shape[0], act_t.shape[0]
+    g_in = (mm(x_t[...], dpre[...]) + mm(far_x[...], far_dpre[...], TN)) * grad_scale
     for j in range(hidden // LANES):
         grads[j * latent : (j + 1) * latent, :] = g_in[:, j * LANES : (j + 1) * LANES]
-    g_out = (mm(act[...], dmsg[...], TN) + mm(far_act[...], far_dmsg[...], TN)) * grad_scale
+    g_out = (mm(act_t[...], dmsg[...]) + mm(far_act[...], far_dmsg[...], TN)) * grad_scale
     for j in range(latent // LANES):
         at = hidden // LANES * latent + j * hidden
         grads[at : at + hidden, :] = g_out[:, j * LANES : (j + 1) * LANES]
@@ -291,23 +304,41 @@
             send[...] = out[...].astype(BF16)
 
 
-def write_kernel(layer, stage, kept, at, *refs):
-    out_in, out_out, token, grads, slab_in, slab_out, sem = refs[-7:]
+def write_kernel(layer, stage, kept, halves, *refs):
+    parts, (out_in, out_out, token, slab_in, slab_out, sem) = refs[kept:-6], refs[-6:]
     token[...] = jnp.zeros_like(token)
-    own = refs[kept]
-    place(stage, own, refs[kept + 1].at[at : at + own.shape[0]], grads)
-    latent, hidden = slab_in.shape
-    for j in range(hidden // LANES):
-        slab_in[:, j * LANES : (j + 1) * LANES] = grads[j * latent : (j + 1) * latent, :]
-    first = pltpu.make_async_copy(slab_in, out_in.at[layer], sem.at[0])
-    first.start()
-    for j in range(latent // LANES):
-        at = hidden // LANES * latent + j * hidden
-        slab_out[:, j * LANES : (j + 1) * LANES] = grads[at : at + hidden, :]
-    second = pltpu.make_async_copy(slab_out, out_out.at[layer], sem.at[1])
-    second.start()
-    first.wait()
-    second.wait()
+    bit = upper(stage)
+    copies = []
+    for part, (at, other) in zip(parts, halves):
+        m = slab_in.size // LANES
+        rows = part.at[at : at + m]
+        upper_half = (1 - bit) if other else bit
+
+        @pl.when(upper_half == 0)
+        def _():
+            write_slab(rows, slab_in, out_in.at[layer], sem.at[0])
+
+        @pl.when(upper_half == 1)
+        def _():
+            write_slab(rows, slab_out, out_out.at[layer], sem.at[1])
+
+        copies.append(upper_half)
+    for upper_half in copies:
+
+        @pl.when(upper_half == 0)
+        def _():
+            pltpu.make_async_copy(slab_in, out_in.at[layer], sem.at[0]).wait()
+
+        @pl.when(upper_half == 1)
+        def _():
+            pltpu.make_async_copy(slab_out, out_out.at[layer], sem.at[1]).wait()
+
+
+def write_slab(rows, slab, out, sem):
+    n = slab.shape[0]
+    for j in range(slab.shape[1] // LANES):
+        slab[:, j * LANES : (j + 1) * LANES] = rows[j * n : (j + 1) * n, :].astype(F32)
+    pltpu.make_async_copy(slab, out, sem).start()
 
 
 class Sum:
@@ -446,17 +477,22 @@
     )
     weights = (w_in, wi1, w_out, wo1)
     inputs = [features]
+    saved = []
     totals = []
     received = []
     for layer in range(layers):
         up, *others = forward(sends)
         if layer == 0:
-            (part,) = call(
-                half_kernel, [((rows, latent), F32)], [features, wi1, wo1], rows * ffn // 2, name="half"
+            part, slope1 = call(
+                half_kernel,
+                [((rows, latent), F32), act16(rows, half)],
+                [features, wi1, wo1],
+                rows * ffn // 2,
+                name="half",
             )
-            (msg,) = call(
+            msg, slope0, act_t, x_t = call(
                 other_half_kernel,
-                [act16(rows)],
+                [act16(rows), act16(rows, half), act16(half, rows), act16(latent, rows)],
                 [features, w_in, w_out, part],
                 rows * ffn // 2,
                 name="local0",
@@ -472,14 +508,16 @@
             )
             up, local = lax.optimization_barrier((up, local))
         else:
-            (msg,) = call(
+            msg, slope0, slope1, act_t, x_t = call(
                 functools.partial(local_kernel, layer),
-                [act16(rows)],
+                [act16(rows), act16(rows, half), act16(rows, half)]
+                + [act16(half, rows), act16(latent, rows)],
                 [inputs[layer], *weights],
                 rows * ffn,
                 name=f"local{layer}",
             )
             up, msg = lax.optimization_barrier((up, msg))
+        saved.append([slope0, slope1, act_t, x_t])
         received.append([up, around(up, "feat", 1), *others])
         (mixed,) = call(
             functools.partial(part_kernel, layer),
@@ -528,11 +566,10 @@
         grad, whole = call(
             functools.partial(back_kernel, layer, grad_scale),
             [((rows, latent), F32), ((grad_rows, LANES), F32)],
-            [outs[1], inputs[layer], local_t, *weights, *outs[2:6]],
+            [outs[1], local_t, *saved[layer], *weights, *outs[2:6]],
             3 * rows * ffn + 2 * rows * rows * latent,
             scratch=[
                 pltpu.VMEM((rows, latent), BF16),
-                pltpu.VMEM((rows, half), BF16),
                 pltpu.VMEM((rows, half), BF16),
             ],
             name=f"back{layer}",
@@ -561,12 +598,17 @@
             after=after,
         )
 
-    def write(layer, written, after):
-        ready = [sums[layer].own, sums[layer].got[0]]
+    def write(layer, written, after, which=(0, 1)):
+        ready = [(sums[layer].own, 0), sums[layer].got]
+        ready = [ready[i] for i in which]
         kept = [*written, *after]
         return pl.pallas_call(
             functools.partial(
-                write_kernel, layer, stages[0], len(kept), sums[layer].got[1]
+                write_kernel,
+                layer,
+                stages[0],
+                len(kept),
+                [(at, i) for (_, at), i in zip(ready, which)],
             ),
             out_shape=[
                 jax.ShapeDtypeStruct((layers, latent, half), F32),
@@ -576,7 +618,6 @@
             in_specs=[ANY] * len(kept) + [VMEM] * len(ready),
             out_specs=[ANY] * 2 + [VMEM],
             scratch_shapes=[
-                pltpu.VMEM((grad_rows, LANES), F32),
                 pltpu.VMEM((latent, half), F32),
                 pltpu.VMEM((half, latent), F32),
                 pltpu.SemaphoreType.DMA((2,)),
@@ -585,7 +626,7 @@
             compiler_params=pltpu.CompilerParams(vmem_limit_bytes=LIMIT),
             cost_estimate=pl.CostEstimate(flops=1, bytes_accessed=1, transcendentals=0),
             name=f"write{layer}",
-        )(*written, *after, *ready)
+        )(*written, *after, *[x for x, _ in ready])
 
     count = 2 * len(stages) - 1
     at = []
@@ -607,12 +648,12 @@
                     at = at + [sums[above].got[0] for above in range(2, layers)]
                 at = sum_step([sums[layer]], at)
     written = []
-    for layer in reversed(range(layers)):
-        if layer == 0:
-            grad, token = join(0, state, at)
-            at = [token]
+    for layer in reversed(range(1, layers)):
         *written, token = write(layer, written, at)
         at = [token]
+    *written, token = write(0, written, at, (0,))
+    grad, token = join(0, state, [token])
+    *written, token = write(0, written, [token], (1,))
     return (grad, *written)
 
 

time: 97.5 us -> 99.4 us (1.019)
  starting transfers between devices: 46.7 us -> 51 us
  waiting for transfers between devices: 16.2 us -> 14.4 us
    ppermute x18, starting transfers between devices: 36 us -> 40.2 us  [over_mesh(): return lax.ppermute(x, ('chain', 'basin', 'feat'), perm)]
    ppermute x18, waiting for transfers between devices: 8.01 us -> 6.57 us  [over_mesh(): return lax.ppermute(x, ('chain', 'basin', 'feat'), perm)]
    ppermute x11, waiting for transfers between devices: 4.61 us -> 3.53 us  [around(): return lax.ppermute(x, axis, [(i, (i + distance) % n) for i in range(n)])]
    pallas_call x3 -> x4, Pallas kernels: 4 us -> 4.44 us  [write(): pl.pallas_call(functools.partial(write_kernel, layer, stages[0], len(kept...]
  transfers between devices with their start and end apart: 32 -> 32, of which waited for: 12 -> 12; matrix products, arithmetic and copies ran while one was open for 1% -> 1% of each run, Pallas kernels for 26% -> 25%
where the time goes in v11:
time: 99.4 us; the launch traced here: 99.1 us
  starting transfers between devices  51 us (51%)
  Pallas kernels  30.6 us (31%)
  waiting for transfers between devices  14.4 us (14%)
  between operations  1.26 us (1%)
  local copies, waits for them, and re-layouts  1.2 us (1%)
    ppermute x18, starting transfers between devices, over_mesh(): return lax.ppermute(x, ('chain', 'basin', 'feat'), perm)  40.2 us
    pallas_call x33, Pallas kernels, call(): pl.pallas_call(lambda *refs: body(*refs[skipped:]), out_shape=[jax.ShapeD...  26.2 us
    ppermute x11, starting transfers between devices, around(): return lax.ppermute(x, axis, [(i, (i + distance) % n) for i in range(n)])  6.63 us
    ppermute x18, waiting for transfers between devices, over_mesh(): return lax.ppermute(x, ('chain', 'basin', 'feat'), perm)  6.57 us
    pallas_call x4, Pallas kernels, write(): pl.pallas_call(functools.partial(write_kernel, layer, stages[0], len(kept...  4.44 us
    ppermute x3, waiting for transfers between devices, backward(): up = lax.ppermute(grads[0], 'chain', [(c, c - 1) for c in range(1, chain)])  4.27 us
    ppermute x3, starting transfers between devices, backward(): up = lax.ppermute(grads[0], 'chain', [(c, c - 1) for c in range(1, chain)])  4.08 us
    ppermute x11, waiting for transfers between devices, around(): return lax.ppermute(x, axis, [(i, (i + distance) % n) for i in range(n)])  3.53 us
  transfers between devices with their start and end apart: 32, of which 12 were waited for; matrix products, arithmetic and copies ran while one was open for 1% of the time, Pallas kernels for 25%

profile of v11, /device:TPU:0, one launch (start us, length us, event | category | flops | bytes accessed | tf_op | source)
XLA Modules:
  0.0 99.1 jit_solution(17498297924043789093)
XLA Ops:
  3.3 4.9 %collective-permute-start = (bf16[128,256]{1,0:T(8,128)(2,1)S(1)}, bf16[128,256]{1,0:T(8,128)(2,1)S(1)}, u32[]{:S(2)}, u32[]{:S(2)}) collective-permute-start(bf16[128,256]{1,0:T(8,128)(2,1)S(1)} %get-tuple-element.117), channel_id=1, source_target_pairs={{0,4},{2,6},{5,9},{7,11},{8,12},{10,14},{16,20},{18,22},{21,25},{2... | collective-permute-start | bytes 196616 | tf_op jit(solution)/shard_map/ppermute | solution.py:423
  8.2 1.6 %collective-permute-start.3 = (bf16[128,256]{1,0:T(8,128)(2,1)S(1)}, bf16[128,256]{1,0:T(8,128)(2,1)S(1)}, u32[]{:S(2)}, u32[]{:S(2)}) collective-permute-start(bf16[128,256]{1,0:T(8,128)(2,1)S(1)} %get-tuple-element.124), channel_id=1, source_target_pairs={{0,2},{2,0},{1,3},{3,1},{4,6},{6,4},{5,7},{7,5},{8,10},{10,8},{9,1... | collective-permute-start | bytes 196616 | tf_op jit(solution)/shard_map/ppermute | solution.py:410
  11.8 1.6 %adjacency.1 = (bf16[768,768]{1,0:T(8,128)(2,1)S(1)}, bf16[768,768]{1,0:T(8,128)(2,1)S(1)}, bf16[768,256]{1,0:T(8,128)(2,1)S(1)}, bf16[256,768]{1,0:T(8,128)(2,1)S(1)}) custom-call(s32[4,6]{1,0:T(4,128)S(1)} %bitcast.4, bf16[6,4,128,128]{3,2,1,0:T(8,128)(2,1)S(1)} %copy-done.3, bf16[128,768]{1,0:T(8,128)(2,1)S(1)} %get-tuple-element.118.refs_2_, ...), custom_call_target="tpu_custom_call" | custom-call | flops 150994944 | bytes 4000000 | tf_op jit(solution)/shard_map/adjacency/pallas_call | solution.py:32
  15.8 2.8 %collective-permute-start.5 = (bf16[128,256]{1,0:T(8,128)(2,1)S(1)}, bf16[128,256]{1,0:T(8,128)(2,1)S(1)}, u32[]{:S(2)}, u32[]{:S(2)}) collective-permute-start(bf16[128,256]{1,0:T(8,128)(2,1)S(1)} %get-tuple-element.128), channel_id=1, source_target_pairs={{0,4},{2,6},{5,9},{7,11},{8,12},{10,14},{16,20},{18,22},{21,25},{2... | collective-permute-start | bytes 196616 | tf_op jit(solution)/shard_map/ppermute | solution.py:423
  19.1 1.6 %local1.1 = (bf16[768,256]{1,0:T(8,128)(2,1)S(1)}, bf16[768,512]{1,0:T(8,128)(2,1)S(1)}, bf16[768,512]{1,0:T(8,128)(2,1)S(1)}, bf16[512,768]{1,0:T(8,128)(2,1)S(1)}, bf16[256,768]{1,0:T(8,128)(2,1)S(1)}) custom-call(bf16[768,256]{1,0:T(8,128)(2,1)S(1)} %get-tuple-element.129.refs_0_, bf16[3,256,512]{2,1,0:T(8,128)(2,1)S(1)} %copy-done, ...), custom_call_target="tpu_custom_call" | custom-call | flops 805306368 | bytes 4000000 | tf_op jit(solution)/shard_map/local1/pallas_call | solution.py:32
  20.8 2.0 %collective-permute-done.6.refs_7_.refs_14_ = bf16[128,256]{1,0:T(8,128)(2,1)S(1)} collective-permute-done((bf16[128,256]{1,0:T(8,128)(2,1)S(1)}, bf16[128,256]{1,0:T(8,128)(2,1)S(1)}, u32[]{:S(2)}, u32[]{:S(2)}) %collective-permute-start.6) | collective-permute-done | bytes 65568 | tf_op jit(solution)/shard_map/ppermute | solution.py:410
  24.9 2.3 %collective-permute-start.8 = (bf16[128,256]{1,0:T(8,128)(2,1)S(1)}, bf16[128,256]{1,0:T(8,128)(2,1)S(1)}, u32[]{:S(2)}, u32[]{:S(2)}) collective-permute-start(bf16[128,256]{1,0:T(8,128)(2,1)S(1)} %get-tuple-element.135), channel_id=1, source_target_pairs={{0,4},{2,6},{5,9},{7,11},{8,12},{10,14},{16,20},{18,22},{21,25},{2... | collective-permute-start | bytes 196616 | tf_op jit(solution)/shard_map/ppermute | solution.py:423
  28.6 1.6 %local2.1 = (bf16[768,256]{1,0:T(8,128)(2,1)S(1)}, bf16[768,512]{1,0:T(8,128)(2,1)S(1)}, bf16[768,512]{1,0:T(8,128)(2,1)S(1)}, bf16[512,768]{1,0:T(8,128)(2,1)S(1)}, bf16[256,768]{1,0:T(8,128)(2,1)S(1)}) custom-call(bf16[768,256]{1,0:T(8,128)(2,1)S(1)} %get-tuple-element.136.refs_0_, bf16[3,256,512]{2,1,0:T(8,128)(2,1)S(1)} %copy-done, ...), custom_call_target="tpu_custom_call" | custom-call | flops 805306368 | bytes 4000000 | tf_op jit(solution)/shard_map/local2/pallas_call | solution.py:32
  32.5 2.0 %turn.1 = (f32[768,256]{1,0:T(8,128)S(1)}, bf16[768,256]{1,0:T(8,128)(2,1)S(1)}, bf16[256,256]{1,0:T(8,128)(2,1)S(1)}, bf16[256,256]{1,0:T(8,128)(2,1)S(1)}, bf1...) custom-call(f32[768,256]{1,0:T(8,128)S(1)} %get-tuple-element.134.re, ...), custom_call_target="tpu_custom_call" | custom-call | flops 536870912 | bytes 4000000 | tf_op jit(solution)/shard_map/turn/pallas_call | solution.py:32
  35.8 1.4 %collective-permute-start.12 = (bf16[128,256]{1,0:T(8,128)(2,1)S(1)}, bf16[128,256]{1,0:T(8,128)(2,1)S(1)}, u32[]{:S(2)}, u32[]{:S(2)}) collective-permute-start(bf16[128,256]{1,0:T(8,128)(2,1)S(1)} %get-tuple-element.154), channel_id=1, source_target_pairs={{0,2},{2,0},{1,3},{3,1},{4,6},{6,4},{5,7},{7,5},{8,10},{10,8},{9,1... | collective-permute-start | bytes 196616 | tf_op jit(solution)/shard_map/ppermute | solution.py:410
  37.2 2.4 %back2.1 = (f32[768,256]{1,0:T(8,128)S(1)}, f32[2048,128]{1,0:T(8,128)S(1)}) custom-call(bf16[768,256]{1,0:T(8,128)(2,1)S(1)} %get-tuple-element.142.refs_0_, bf16[768,768]{1,0:T(8,128)(2,1)S(1)} %get-tuple-element.143.refs_1_.refs_2_, bf16[768,512]{1,0:T(8,128)(2,1)S(1)} %get-tuple-element.144.refs_2_, bf16[768,512]{1,0:T(8,128)(2,1)S(1)} %get-tuple-element.145.refs_3_, ...), custom_call_target="tpu_custom_call" | custom-call | flops 2717908992 | bytes 4000000 | tf_op jit(solution)/shard_map/back2/pallas_call | solution.py:32
  42.1 1.5 %join2.1 = (f32[768,256]{1,0:T(8,128)S(1)}, bf16[768,256]{1,0:T(8,128)(2,1)S(1)}, bf16[256,256]{1,0:T(8,128)(2,1)S(1)}, bf16[256,256]{1,0:T(8,128)(2,1)S(1)}, bf...) custom-call(f32[1024,128]{1,0:T(8,128)S(1)} %get-tuple-element.156.r, ...), custom_call_target="tpu_custom_call" | custom-call | flops 536870912 | bytes 4000000 | tf_op jit(solution)/shard_map/join2/pallas_call | solution.py:32
  43.6 1.5 %collective-permute-start.13 = (bf16[128,256]{1,0:T(8,128)(2,1)S(1)}, bf16[128,256]{1,0:T(8,128)(2,1)S(1)}, u32[]{:S(2)}, u32[]{:S(2)}) collective-permute-start(bf16[128,256]{1,0:T(8,128)(2,1)S(1)} %get-tuple-element.169), channel_id=1, source_target_pairs={{4,0},{8,4},{12,8},{5,1},{9,5},{13,9},{6,2},{10,6},{14,10},{7,3},{... | collective-permute-start | bytes 196616 | tf_op jit(solution)/shard_map/ppermute | solution.py:446
  45.9 2.4 %back1.1 = (f32[768,256]{1,0:T(8,128)S(1)}, f32[2048,128]{1,0:T(8,128)S(1)}) custom-call(bf16[768,256]{1,0:T(8,128)(2,1)S(1)} %get-tuple-element.159.refs_0_.refs_1_, bf16[768,256]{1,0:T(8,128)(2,1)S(1)} %get-tuple-element.159.refs_0_.refs_1_, bf16[768,768]{1,0:T(8,128)(2,1)S(1)} %get-tuple-element.143.refs_1_.refs_2_, ...), custom_call_target="tpu_custom_call" | custom-call | flops 2717908992 | bytes 4000000 | tf_op jit(solution)/shard_map/back1/pallas_call | solution.py:32
  48.3 1.5 %collective-permute-done.13.refs_1_.refs_10_ = bf16[128,256]{1,0:T(8,128)(2,1)S(1)} collective-permute-done((bf16[128,256]{1,0:T(8,128)(2,1)S(1)}, bf16[128,256]{1,0:T(8,128)(2,1)S(1)}, u32[]{:S(2)}, u32[]{:S(2)}) %collective-permute-start.13) | collective-permute-done | bytes 65568 | tf_op jit(solution)/shard_map/ppermute | solution.py:446
  50.8 2.4 %collective-permute-start.16 = (bf16[512,128]{1,0:T(8,128)(2,1)S(1)}, bf16[512,128]{1,0:T(8,128)(2,1)S(1)}, u32[]{:S(2)}, u32[]{:S(2)}) collective-permute-start(bf16[512,128]{1,0:T(8,128)(2,1)S(1)} %get-tuple-element.186), channel_id=1, source_target_pairs={{0,4},{1,3},{2,6},{3,1},{4,0},{5,7},{6,2},{7,5},{8,12},{9,11},{10,... | collective-permute-start | bytes 393224 | tf_op jit(solution)/shard_map/ppermute | solution.py:423
  53.2 1.5 %join1.1 = (f32[768,256]{1,0:T(8,128)S(1)}, bf16[768,256]{1,0:T(8,128)(2,1)S(1)}, bf16[256,256]{1,0:T(8,128)(2,1)S(1)}, bf16[256,256]{1,0:T(8,128)(2,1)S(1)}, bf...) custom-call(f32[512,128]{1,0:T(8,128)S(1)} %get-tuple-element.174.re, ...), custom_call_target="tpu_custom_call" | custom-call | flops 536870912 | bytes 4000000 | tf_op jit(solution)/shard_map/join1/pallas_call | solution.py:32
  54.7 2.4 %back0.1 = (f32[768,256]{1,0:T(8,128)S(1)}, f32[2048,128]{1,0:T(8,128)S(1)}) custom-call(bf16[768,256]{1,0:T(8,128)(2,1)S(1)} %get-tuple-element.176.refs_0_.refs_1_, bf16[768,256]{1,0:T(8,128)(2,1)S(1)} %get-tuple-element.176.refs_0_.refs_1_, bf16[768,768]{1,0:T(8,128)(2,1)S(1)} %get-tuple-element.143.refs_1_.refs_2_, ...), custom_call_target="tpu_custom_call" | custom-call | flops 2717908992 | bytes 4000000 | tf_op jit(solution)/shard_map/back0/pallas_call | solution.py:32
  57.2 1.4 %collective-permute-start.18 = (bf16[1024,128]{1,0:T(8,128)(2,1)S(1)}, bf16[1024,128]{1,0:T(8,128)(2,1)S(1)}, u32[]{:S(2)}, u32[]{:S(2)}) collective-permute-start(bf16[1024,128]{1,0:T(8,128)(2,1)S(1)} %get-tuple-element.192), channel_id=1, source_target_pairs={{0,2},{1,5},{2,0},{3,7},{4,6},{5,1},{6,4},{7,3},{8,10},{9,13},{10,... | collective-permute-start | bytes 786440 | tf_op jit(solution)/shard_map/ppermute | solution.py:423
  58.6 3.9 %collective-permute-start.19 = (bf16[512,128]{1,0:T(8,128)(2,1)S(1)}, bf16[512,128]{1,0:T(8,128)(2,1)S(1)}, u32[]{:S(2)}, u32[]{:S(2)}) collective-permute-start(bf16[512,128]{1,0:T(8,128)(2,1)S(1)} %get-tuple-element.194), channel_id=1, source_target_pairs={{0,8},{1,9},{2,10},{3,11},{4,12},{5,13},{6,14},{7,15},{8,0},{9,1},... | collective-permute-start | bytes 393224 | tf_op jit(solution)/shard_map/ppermute | solution.py:423
  63.8 2.1 %collective-permute-start.21 = (bf16[512,128]{1,0:T(8,128)(2,1)S(1)}, bf16[512,128]{1,0:T(8,128)(2,1)S(1)}, u32[]{:S(2)}, u32[]{:S(2)}) collective-permute-start(bf16[512,128]{1,0:T(8,128)(2,1)S(1)} %get-tuple-element.198), channel_id=1, source_target_pairs={{0,4},{1,3},{2,6},{3,1},{4,0},{5,7},{6,2},{7,5},{8,12},{9,11},{10,... | collective-permute-start | bytes 393224 | tf_op jit(solution)/shard_map/ppermute | solution.py:423
  66.7 2.0 %collective-permute-done.20.refs_2_ = bf16[512,128]{1,0:T(8,128)(2,1)S(1)} collective-permute-done((bf16[512,128]{1,0:T(8,128)(2,1)S(1)}, bf16[512,128]{1,0:T(8,128)(2,1)S(1)}, u32[]{:S(2)}, u32[]{:S(2)}) %collective-permute-start.20) | collective-permute-done | bytes 131104 | tf_op jit(solution)/shard_map/ppermute | solution.py:423
  68.7 2.9 %collective-permute-start.23 = (bf16[512,128]{1,0:T(8,128)(2,1)S(1)}, bf16[512,128]{1,0:T(8,128)(2,1)S(1)}, u32[]{:S(2)}, u32[]{:S(2)}) collective-permute-start(bf16[512,128]{1,0:T(8,128)(2,1)S(1)} %get-tuple-element.202), channel_id=1, source_target_pairs={{0,8},{1,9},{2,10},{3,11},{4,12},{5,13},{6,14},{7,15},{8,0},{9,1},... | collective-permute-start | bytes 393224 | tf_op jit(solution)/shard_map/ppermute | solution.py:423
  71.7 4.1 %collective-permute-start.24 = (bf16[512,128]{1,0:T(8,128)(2,1)S(1)}, bf16[512,128]{1,0:T(8,128)(2,1)S(1)}, u32[]{:S(2)}, u32[]{:S(2)}) collective-permute-start(bf16[512,128]{1,0:T(8,128)(2,1)S(1)} %get-tuple-element.204), channel_id=1, source_target_pairs={{0,8},{1,9},{2,10},{3,11},{4,12},{5,13},{6,14},{7,15},{8,0},{9,1},... | collective-permute-start | bytes 393224 | tf_op jit(solution)/shard_map/ppermute | solution.py:423
  76.5 1.6 %collective-permute-start.26 = (bf16[1024,128]{1,0:T(8,128)(2,1)S(1)}, bf16[1024,128]{1,0:T(8,128)(2,1)S(1)}, u32[]{:S(2)}, u32[]{:S(2)}) collective-permute-start(bf16[1024,128]{1,0:T(8,128)(2,1)S(1)} %get-tuple-element.208), channel_id=1, source_target_pairs={{0,2},{1,5},{2,0},{3,7},{4,6},{5,1},{6,4},{7,3},{8,10},{9,13},{10,... | collective-permute-start | bytes 786440 | tf_op jit(solution)/shard_map/ppermute | solution.py:423
  78.1 2.8 %collective-permute-start.25 = (bf16[512,128]{1,0:T(8,128)(2,1)S(1)}, bf16[512,128]{1,0:T(8,128)(2,1)S(1)}, u32[]{:S(2)}, u32[]{:S(2)}) collective-permute-start(bf16[512,128]{1,0:T(8,128)(2,1)S(1)} %get-tuple-element.206), channel_id=1, source_target_pairs={{0,4},{1,3},{2,6},{3,1},{4,0},{5,7},{6,2},{7,5},{8,12},{9,11},{10,... | collective-permute-start | bytes 393224 | tf_op jit(solution)/shard_map/ppermute | solution.py:423
  81.0 2.8 %collective-permute-start.27 = (bf16[512,128]{1,0:T(8,128)(2,1)S(1)}, bf16[512,128]{1,0:T(8,128)(2,1)S(1)}, u32[]{:S(2)}, u32[]{:S(2)}) collective-permute-start(bf16[512,128]{1,0:T(8,128)(2,1)S(1)} %get-tuple-element.209), channel_id=1, source_target_pairs={{0,4},{1,3},{2,6},{3,1},{4,0},{5,7},{6,2},{7,5},{8,12},{9,11},{10,... | collective-permute-start | bytes 393224 | tf_op jit(solution)/shard_map/ppermute | solution.py:423
  83.7 1.6 %collective-permute-done.25.refs_2_ = bf16[512,128]{1,0:T(8,128)(2,1)S(1)} collective-permute-done((bf16[512,128]{1,0:T(8,128)(2,1)S(1)}, bf16[512,128]{1,0:T(8,128)(2,1)S(1)}, u32[]{:S(2)}, u32[]{:S(2)}) %collective-permute-start.25) | collective-permute-done | bytes 131104 | tf_op jit(solution)/shard_map/ppermute | solution.py:423
  85.4 2.1 %collective-permute-start.28 = (bf16[1024,128]{1,0:T(8,128)(2,1)S(1)}, bf16[1024,128]{1,0:T(8,128)(2,1)S(1)}, u32[]{:S(2)}, u32[]{:S(2)}) collective-permute-start(bf16[1024,128]{1,0:T(8,128)(2,1)S(1)} %get-tuple-element.214), channel_id=1, source_target_pairs={{0,2},{1,5},{2,0},{3,7},{4,6},{5,1},{6,4},{7,3},{8,10},{9,13},{10,... | collective-permute-start | bytes 786440 | tf_op jit(solution)/shard_map/ppermute | solution.py:423
  88.2 2.0 %collective-permute-start.31 = (bf16[1024,128]{1,0:T(8,128)(2,1)S(1)}, bf16[1024,128]{1,0:T(8,128)(2,1)S(1)}, u32[]{:S(2)}, u32[]{:S(2)}) collective-permute-start(bf16[1024,128]{1,0:T(8,128)(2,1)S(1)} %get-tuple-element.226), channel_id=1, source_target_pairs={{0,2},{1,5},{2,0},{3,7},{4,6},{5,1},{6,4},{7,3},{8,10},{9,13},{10,... | collective-permute-start | bytes 786440 | tf_op jit(solution)/shard_map/ppermute | solution.py:423
  94.7 1.7 %collective-permute-done.29.refs_4_ = bf16[128,256]{1,0:T(8,128)(2,1)S(1)} collective-permute-done((bf16[128,256]{1,0:T(8,128)(2,1)S(1)}, bf16[128,256]{1,0:T(8,128)(2,1)S(1)}, u32[]{:S(2)}, u32[]{:S(2)}) %collective-permute-start.29) | collective-permute-done | bytes 65568 | tf_op jit(solution)/shard_map/ppermute | solution.py:446
  97.5 1.4 %write0.3 = (f32[3,256,512]{2,1,0:T(8,128)}, f32[3,512,256]{2,1,0:T(8,128)}, f32[8,128]{1,0:T(8,128)}) custom-call(f32[3,256,512]{2,1,0:T(8,128)} %get-tuple-element.223.refs_0_, f32[3,512,256]{2,1,0:T(8,128)} %get-tuple-element.224.refs_1_, f32[8,128]{1,0:T(8,128)S(1)} %get-tuple-element.225.refs_2_, ...), custom_call_target="tpu_custom_call", output_to_operand_aliasing={{0}: (0, {}), {1}: (1, {})} | custom-call | flops 1 | bytes 1 | tf_op jit(solution)/shard_map/write0/pallas_call | solution.py:605
  (82 shorter events, 28.3 us)
Async XLA Ops:
  0.7 9.1 %collective-permute-start.1 = (bf16[3,256,512]{2,1,0:T(8,128)(2,1)}, bf16[3,256,512]{2,1,0:T(8,128)(2,1)S(1)}, u32[]{:S(2)}, u32[]{:S(2)}) collective-permute-start(bf16[3,256,512]{2,1,0:T(8,128)(2,1)} %refs_7_.5), channel_id=1, source_target_pairs={{0,1},{1,0},{2,3},{3,2},{4,5},{5,4},{6,7},{7,6},{8,9},{9,8},{10,11... | collective-permute-start | bytes 2359304 | tf_op jit(solution)/shard_map/ppermute | solution.py:410
  1.2 8.6 %collective-permute-start.2 = (bf16[3,512,256]{2,1,0:T(8,128)(2,1)}, bf16[3,512,256]{2,1,0:T(8,128)(2,1)S(1)}, u32[]{:S(2)}, u32[]{:S(2)}) collective-permute-start(bf16[3,512,256]{2,1,0:T(8,128)(2,1)} %refs_9_.3), channel_id=1, source_target_pairs={{0,1},{1,0},{2,3},{3,2},{4,5},{5,4},{6,7},{7,6},{8,9},{9,8},{10,11... | collective-permute-start | bytes 2359304 | tf_op jit(solution)/shard_map/ppermute | solution.py:410
  3.3 10.1 %collective-permute-start = (bf16[128,256]{1,0:T(8,128)(2,1)S(1)}, bf16[128,256]{1,0:T(8,128)(2,1)S(1)}, u32[]{:S(2)}, u32[]{:S(2)}) collective-permute-start(bf16[128,256]{1,0:T(8,128)(2,1)S(1)} %get-tuple-element.117), channel_id=1, source_target_pairs={{0,4},{2,6},{5,9},{7,11},{8,12},{10,14},{16,20},{18,22},{21,25},{2... | collective-permute-start | bytes 196616 | tf_op jit(solution)/shard_map/ppermute | solution.py:423
  8.2 5.2 %collective-permute-start.3 = (bf16[128,256]{1,0:T(8,128)(2,1)S(1)}, bf16[128,256]{1,0:T(8,128)(2,1)S(1)}, u32[]{:S(2)}, u32[]{:S(2)}) collective-permute-start(bf16[128,256]{1,0:T(8,128)(2,1)S(1)} %get-tuple-element.124), channel_id=1, source_target_pairs={{0,2},{2,0},{1,3},{3,1},{4,6},{6,4},{5,7},{7,5},{8,10},{10,8},{9,1... | collective-permute-start | bytes 196616 | tf_op jit(solution)/shard_map/ppermute | solution.py:410
  13.4 1.3 %collective-permute-start.4 = (bf16[128,256]{1,0:T(8,128)(2,1)S(1)}, bf16[128,256]{1,0:T(8,128)(2,1)S(1)}, u32[]{:S(2)}, u32[]{:S(2)}) collective-permute-start(bf16[128,256]{1,0:T(8,128)(2,1)S(1)} %collective-permute-done.refs_8_.refs_12_), channel_id=1, source_target_pairs={{0,1},{1,0},{2,3},{3,2},{4,5},{5,4},{6,7},{7,6},{8,9},{9,8},{10,11... | collective-permute-start | bytes 196616 | tf_op jit(solution)/shard_map/ppermute | solution.py:410
  15.8 5.0 %collective-permute-start.5 = (bf16[128,256]{1,0:T(8,128)(2,1)S(1)}, bf16[128,256]{1,0:T(8,128)(2,1)S(1)}, u32[]{:S(2)}, u32[]{:S(2)}) collective-permute-start(bf16[128,256]{1,0:T(8,128)(2,1)S(1)} %get-tuple-element.128), channel_id=1, source_target_pairs={{0,4},{2,6},{5,9},{7,11},{8,12},{10,14},{16,20},{18,22},{21,25},{2... | collective-permute-start | bytes 196616 | tf_op jit(solution)/shard_map/ppermute | solution.py:423
  18.5 4.3 %collective-permute-start.6 = (bf16[128,256]{1,0:T(8,128)(2,1)S(1)}, bf16[128,256]{1,0:T(8,128)(2,1)S(1)}, u32[]{:S(2)}, u32[]{:S(2)}) collective-permute-start(bf16[128,256]{1,0:T(8,128)(2,1)S(1)} %get-tuple-element.132), channel_id=1, source_target_pairs={{0,2},{2,0},{1,3},{3,1},{4,6},{6,4},{5,7},{7,5},{8,10},{10,8},{9,1... | collective-permute-start | bytes 196616 | tf_op jit(solution)/shard_map/ppermute | solution.py:410
  20.8 3.1 %collective-permute-start.7 = (bf16[128,256]{1,0:T(8,128)(2,1)S(1)}, bf16[128,256]{1,0:T(8,128)(2,1)S(1)}, u32[]{:S(2)}, u32[]{:S(2)}) collective-permute-start(bf16[128,256]{1,0:T(8,128)(2,1)S(1)} %collective-permute-done.5.refs_8_.refs_12_), channel_id=1, source_target_pairs={{0,1},{1,0},{2,3},{3,2},{4,5},{5,4},{6,7},{7,6},{8,9},{9,8},{10,11... | collective-permute-start | bytes 196616 | tf_op jit(solution)/shard_map/ppermute | solution.py:410
  24.9 5.2 %collective-permute-start.8 = (bf16[128,256]{1,0:T(8,128)(2,1)S(1)}, bf16[128,256]{1,0:T(8,128)(2,1)S(1)}, u32[]{:S(2)}, u32[]{:S(2)}) collective-permute-start(bf16[128,256]{1,0:T(8,128)(2,1)S(1)} %get-tuple-element.135), channel_id=1, source_target_pairs={{0,4},{2,6},{5,9},{7,11},{8,12},{10,14},{16,20},{18,22},{21,25},{2... | collective-permute-start | bytes 196616 | tf_op jit(solution)/shard_map/ppermute | solution.py:423
  27.2 4.3 %collective-permute-start.9 = (bf16[128,256]{1,0:T(8,128)(2,1)S(1)}, bf16[128,256]{1,0:T(8,128)(2,1)S(1)}, u32[]{:S(2)}, u32[]{:S(2)}) collective-permute-start(bf16[128,256]{1,0:T(8,128)(2,1)S(1)} %get-tuple-element.139), channel_id=1, source_target_pairs={{0,2},{2,0},{1,3},{3,1},{4,6},{6,4},{5,7},{7,5},{8,10},{10,8},{9,1... | collective-permute-start | bytes 196616 | tf_op jit(solution)/shard_map/ppermute | solution.py:410
  30.2 2.3 %collective-permute-start.10 = (bf16[128,256]{1,0:T(8,128)(2,1)S(1)}, bf16[128,256]{1,0:T(8,128)(2,1)S(1)}, u32[]{:S(2)}, u32[]{:S(2)}) collective-permute-start(bf16[128,256]{1,0:T(8,128)(2,1)S(1)} %collective-permute-done.8.refs_9_), channel_id=1, source_target_pairs={{0,1},{1,0},{2,3},{3,2},{4,5},{5,4},{6,7},{7,6},{8,9},{9,8},{10,11... | collective-permute-start | bytes 196616 | tf_op jit(solution)/shard_map/ppermute | solution.py:410
  34.5 6.2 %collective-permute-start.11 = (bf16[128,256]{1,0:T(8,128)(2,1)S(1)}, bf16[128,256]{1,0:T(8,128)(2,1)S(1)}, u32[]{:S(2)}, u32[]{:S(2)}) collective-permute-start(bf16[128,256]{1,0:T(8,128)(2,1)S(1)} %get-tuple-element.153), channel_id=1, source_target_pairs={{4,0},{8,4},{12,8},{5,1},{9,5},{13,9},{6,2},{10,6},{14,10},{7,3},{... | collective-permute-start | bytes 196616 | tf_op jit(solution)/shard_map/ppermute | solution.py:446
  35.8 4.9 %collective-permute-start.12 = (bf16[128,256]{1,0:T(8,128)(2,1)S(1)}, bf16[128,256]{1,0:T(8,128)(2,1)S(1)}, u32[]{:S(2)}, u32[]{:S(2)}) collective-permute-start(bf16[128,256]{1,0:T(8,128)(2,1)S(1)} %get-tuple-element.154), channel_id=1, source_target_pairs={{0,2},{2,0},{1,3},{3,1},{4,6},{6,4},{5,7},{7,5},{8,10},{10,8},{9,1... | collective-permute-start | bytes 196616 | tf_op jit(solution)/shard_map/ppermute | solution.py:410
  40.8 10.0 %collective-permute-start.15 = (bf16[1024,128]{1,0:T(8,128)(2,1)S(1)}, bf16[1024,128]{1,0:T(8,128)(2,1)S(1)}, u32[]{:S(2)}, u32[]{:S(2)}) collective-permute-start(bf16[1024,128]{1,0:T(8,128)(2,1)S(1)} %get-tuple-element.173), channel_id=1, source_target_pairs={{0,2},{1,5},{2,0},{3,7},{4,6},{5,1},{6,4},{7,3},{8,10},{9,13},{10,... | collective-permute-start | bytes 786440 | tf_op jit(solution)/shard_map/ppermute | solution.py:423
  43.6 6.3 %collective-permute-start.13 = (bf16[128,256]{1,0:T(8,128)(2,1)S(1)}, bf16[128,256]{1,0:T(8,128)(2,1)S(1)}, u32[]{:S(2)}, u32[]{:S(2)}) collective-permute-start(bf16[128,256]{1,0:T(8,128)(2,1)S(1)} %get-tuple-element.169), channel_id=1, source_target_pairs={{4,0},{8,4},{12,8},{5,1},{9,5},{13,9},{6,2},{10,6},{14,10},{7,3},{... | collective-permute-start | bytes 196616 | tf_op jit(solution)/shard_map/ppermute | solution.py:446
  45.1 4.7 %collective-permute-start.14 = (bf16[128,256]{1,0:T(8,128)(2,1)S(1)}, bf16[128,256]{1,0:T(8,128)(2,1)S(1)}, u32[]{:S(2)}, u32[]{:S(2)}) collective-permute-start(bf16[128,256]{1,0:T(8,128)(2,1)S(1)} %get-tuple-element.170), channel_id=1, source_target_pairs={{0,2},{2,0},{1,3},{3,1},{4,6},{6,4},{5,7},{7,5},{8,10},{10,8},{9,1... | collective-permute-start | bytes 196616 | tf_op jit(solution)/shard_map/ppermute | solution.py:410
  49.9 12.6 %collective-permute-start.17 = (bf16[1024,128]{1,0:T(8,128)(2,1)S(1)}, bf16[1024,128]{1,0:T(8,128)(2,1)S(1)}, u32[]{:S(2)}, u32[]{:S(2)}) collective-permute-start(bf16[1024,128]{1,0:T(8,128)(2,1)S(1)} %get-tuple-element.190), channel_id=1, source_target_pairs={{0,2},{1,5},{2,0},{3,7},{4,6},{5,1},{6,4},{7,3},{8,10},{9,13},{10,... | collective-permute-start | bytes 786440 | tf_op jit(solution)/shard_map/ppermute | solution.py:423
  50.8 6.3 %collective-permute-start.16 = (bf16[512,128]{1,0:T(8,128)(2,1)S(1)}, bf16[512,128]{1,0:T(8,128)(2,1)S(1)}, u32[]{:S(2)}, u32[]{:S(2)}) collective-permute-start(bf16[512,128]{1,0:T(8,128)(2,1)S(1)} %get-tuple-element.186), channel_id=1, source_target_pairs={{0,4},{1,3},{2,6},{3,1},{4,0},{5,7},{6,2},{7,5},{8,12},{9,11},{10,... | collective-permute-start | bytes 393224 | tf_op jit(solution)/shard_map/ppermute | solution.py:423
  57.2 6.4 %collective-permute-start.18 = (bf16[1024,128]{1,0:T(8,128)(2,1)S(1)}, bf16[1024,128]{1,0:T(8,128)(2,1)S(1)}, u32[]{:S(2)}, u32[]{:S(2)}) collective-permute-start(bf16[1024,128]{1,0:T(8,128)(2,1)S(1)} %get-tuple-element.192), channel_id=1, source_target_pairs={{0,2},{1,5},{2,0},{3,7},{4,6},{5,1},{6,4},{7,3},{8,10},{9,13},{10,... | collective-permute-start | bytes 786440 | tf_op jit(solution)/shard_map/ppermute | solution.py:423
  58.6 8.0 %collective-permute-start.19 = (bf16[512,128]{1,0:T(8,128)(2,1)S(1)}, bf16[512,128]{1,0:T(8,128)(2,1)S(1)}, u32[]{:S(2)}, u32[]{:S(2)}) collective-permute-start(bf16[512,128]{1,0:T(8,128)(2,1)S(1)} %get-tuple-element.194), channel_id=1, source_target_pairs={{0,8},{1,9},{2,10},{3,11},{4,12},{5,13},{6,14},{7,15},{8,0},{9,1},... | collective-permute-start | bytes 393224 | tf_op jit(solution)/shard_map/ppermute | solution.py:423
  62.6 6.1 %collective-permute-start.20 = (bf16[512,128]{1,0:T(8,128)(2,1)S(1)}, bf16[512,128]{1,0:T(8,128)(2,1)S(1)}, u32[]{:S(2)}, u32[]{:S(2)}) collective-permute-start(bf16[512,128]{1,0:T(8,128)(2,1)S(1)} %get-tuple-element.196), channel_id=1, source_target_pairs={{0,4},{1,3},{2,6},{3,1},{4,0},{5,7},{6,2},{7,5},{8,12},{9,11},{10,... | collective-permute-start | bytes 393224 | tf_op jit(solution)/shard_map/ppermute | solution.py:423
  63.8 7.9 %collective-permute-start.21 = (bf16[512,128]{1,0:T(8,128)(2,1)S(1)}, bf16[512,128]{1,0:T(8,128)(2,1)S(1)}, u32[]{:S(2)}, u32[]{:S(2)}) collective-permute-start(bf16[512,128]{1,0:T(8,128)(2,1)S(1)} %get-tuple-element.198), channel_id=1, source_target_pairs={{0,4},{1,3},{2,6},{3,1},{4,0},{5,7},{6,2},{7,5},{8,12},{9,11},{10,... | collective-permute-start | bytes 393224 | tf_op jit(solution)/shard_map/ppermute | solution.py:423
  66.7 9.8 %collective-permute-start.22 = (bf16[512,128]{1,0:T(8,128)(2,1)S(1)}, bf16[512,128]{1,0:T(8,128)(2,1)S(1)}, u32[]{:S(2)}, u32[]{:S(2)}) collective-permute-start(bf16[512,128]{1,0:T(8,128)(2,1)S(1)} %get-tuple-element.200), channel_id=1, source_target_pairs={{0,4},{1,3},{2,6},{3,1},{4,0},{5,7},{6,2},{7,5},{8,12},{9,11},{10,... | collective-permute-start | bytes 393224 | tf_op jit(solution)/shard_map/ppermute | solution.py:423
  68.7 9.3 %collective-permute-start.23 = (bf16[512,128]{1,0:T(8,128)(2,1)S(1)}, bf16[512,128]{1,0:T(8,128)(2,1)S(1)}, u32[]{:S(2)}, u32[]{:S(2)}) collective-permute-start(bf16[512,128]{1,0:T(8,128)(2,1)S(1)} %get-tuple-element.202), channel_id=1, source_target_pairs={{0,8},{1,9},{2,10},{3,11},{4,12},{5,13},{6,14},{7,15},{8,0},{9,1},... | collective-permute-start | bytes 393224 | tf_op jit(solution)/shard_map/ppermute | solution.py:423
  71.7 9.2 %collective-permute-start.24 = (bf16[512,128]{1,0:T(8,128)(2,1)S(1)}, bf16[512,128]{1,0:T(8,128)(2,1)S(1)}, u32[]{:S(2)}, u32[]{:S(2)}) collective-permute-start(bf16[512,128]{1,0:T(8,128)(2,1)S(1)} %get-tuple-element.204), channel_id=1, source_target_pairs={{0,8},{1,9},{2,10},{3,11},{4,12},{5,13},{6,14},{7,15},{8,0},{9,1},... | collective-permute-start | bytes 393224 | tf_op jit(solution)/shard_map/ppermute | solution.py:423
  76.5 11.0 %collective-permute-start.26 = (bf16[1024,128]{1,0:T(8,128)(2,1)S(1)}, bf16[1024,128]{1,0:T(8,128)(2,1)S(1)}, u32[]{:S(2)}, u32[]{:S(2)}) collective-permute-start(bf16[1024,128]{1,0:T(8,128)(2,1)S(1)} %get-tuple-element.208), channel_id=1, source_target_pairs={{0,2},{1,5},{2,0},{3,7},{4,6},{5,1},{6,4},{7,3},{8,10},{9,13},{10,... | collective-permute-start | bytes 786440 | tf_op jit(solution)/shard_map/ppermute | solution.py:423
  78.1 7.2 %collective-permute-start.25 = (bf16[512,128]{1,0:T(8,128)(2,1)S(1)}, bf16[512,128]{1,0:T(8,128)(2,1)S(1)}, u32[]{:S(2)}, u32[]{:S(2)}) collective-permute-start(bf16[512,128]{1,0:T(8,128)(2,1)S(1)} %get-tuple-element.206), channel_id=1, source_target_pairs={{0,4},{1,3},{2,6},{3,1},{4,0},{5,7},{6,2},{7,5},{8,12},{9,11},{10,... | collective-permute-start | bytes 393224 | tf_op jit(solution)/shard_map/ppermute | solution.py:423
  81.0 7.2 %collective-permute-start.27 = (bf16[512,128]{1,0:T(8,128)(2,1)S(1)}, bf16[512,128]{1,0:T(8,128)(2,1)S(1)}, u32[]{:S(2)}, u32[]{:S(2)}) collective-permute-start(bf16[512,128]{1,0:T(8,128)(2,1)S(1)} %get-tuple-element.209), channel_id=1, source_target_pairs={{0,4},{1,3},{2,6},{3,1},{4,0},{5,7},{6,2},{7,5},{8,12},{9,11},{10,... | collective-permute-start | bytes 393224 | tf_op jit(solution)/shard_map/ppermute | solution.py:423
  85.4 7.3 %collective-permute-start.28 = (bf16[1024,128]{1,0:T(8,128)(2,1)S(1)}, bf16[1024,128]{1,0:T(8,128)(2,1)S(1)}, u32[]{:S(2)}, u32[]{:S(2)}) collective-permute-start(bf16[1024,128]{1,0:T(8,128)(2,1)S(1)} %get-tuple-element.214), channel_id=1, source_target_pairs={{0,2},{1,5},{2,0},{3,7},{4,6},{5,1},{6,4},{7,3},{8,10},{9,13},{10,... | collective-permute-start | bytes 786440 | tf_op jit(solution)/shard_map/ppermute | solution.py:423
  88.2 9.3 %collective-permute-start.31 = (bf16[1024,128]{1,0:T(8,128)(2,1)S(1)}, bf16[1024,128]{1,0:T(8,128)(2,1)S(1)}, u32[]{:S(2)}, u32[]{:S(2)}) collective-permute-start(bf16[1024,128]{1,0:T(8,128)(2,1)S(1)} %get-tuple-element.226), channel_id=1, source_target_pairs={{0,2},{1,5},{2,0},{3,7},{4,6},{5,1},{6,4},{7,3},{8,10},{9,13},{10,... | collective-permute-start | bytes 786440 | tf_op jit(solution)/shard_map/ppermute | solution.py:423
  90.2 6.1 %collective-permute-start.29 = (bf16[128,256]{1,0:T(8,128)(2,1)S(1)}, bf16[128,256]{1,0:T(8,128)(2,1)S(1)}, u32[]{:S(2)}, u32[]{:S(2)}) collective-permute-start(bf16[128,256]{1,0:T(8,128)(2,1)S(1)} %get-tuple-element.220), channel_id=1, source_target_pairs={{4,0},{8,4},{12,8},{5,1},{9,5},{13,9},{6,2},{10,6},{14,10},{7,3},{... | collective-permute-start | bytes 196616 | tf_op jit(solution)/shard_map/ppermute | solution.py:446
  91.5 4.9 %collective-permute-start.30 = (bf16[128,256]{1,0:T(8,128)(2,1)S(1)}, bf16[128,256]{1,0:T(8,128)(2,1)S(1)}, u32[]{:S(2)}, u32[]{:S(2)}) collective-permute-start(bf16[128,256]{1,0:T(8,128)(2,1)S(1)} %get-tuple-element.221), channel_id=1, source_target_pairs={{0,2},{2,0},{1,3},{3,1},{4,6},{6,4},{5,7},{7,5},{8,10},{10,8},{9,1... | collective-permute-start | bytes 196616 | tf_op jit(solution)/shard_map/ppermute | solution.py:410
  (6 other events, 25.7 us)

commit v12 on v11

--- a/solution.py
+++ b/solution.py
@@ -557,7 +557,7 @@
     over_basin, over_chain = distances("basin"), distances("chain")
     n = len(over_basin)
     orders = over_basin + over_chain, over_chain[:n] + over_basin + over_chain[n:]
-    stages = list(zip(*orders, strict=True))
+    stages = list(zip(*orders[::-1], strict=True))
     returned = {}
     sums = {}
 

time: 99.4 us -> 100 us (level)
  waiting for transfers between devices: 14.4 us -> 28.7 us
  starting transfers between devices: 51 us -> 37.7 us
    ppermute x18, waiting for transfers between devices: 6.57 us -> 21.8 us  [over_mesh(): return lax.ppermute(x, ('chain', 'basin', 'feat'), perm)]
    ppermute x18, starting transfers between devices: 40.2 us -> 25.3 us  [over_mesh(): return lax.ppermute(x, ('chain', 'basin', 'feat'), perm)]
    ppermute x11, starting transfers between devices: 6.63 us -> 8.33 us  [around(): return lax.ppermute(x, axis, [(i, (i + distance) % n) for i in range(n)])]
  transfers between devices with their start and end apart: 32 -> 32, of which waited for: 12 -> 15; matrix products, arithmetic and copies ran while one was open for 1% -> 1% of each run, Pallas kernels for 25% -> 25%
where the time goes in v12:
time: 100 us
  starting transfers between devices  37.7 us (38%)
  Pallas kernels  30.6 us (31%)
  waiting for transfers between devices  28.7 us (29%)
  between operations  1.26 us (1%)
  local copies, waits for them, and re-layouts  1.2 us (1%)
    pallas_call x33, Pallas kernels, call(): pl.pallas_call(lambda *refs: body(*refs[skipped:]), out_shape=[jax.ShapeD...  26.1 us
    ppermute x18, starting transfers between devices, over_mesh(): return lax.ppermute(x, ('chain', 'basin', 'feat'), perm)  25.3 us
    ppermute x18, waiting for transfers between devices, over_mesh(): return lax.ppermute(x, ('chain', 'basin', 'feat'), perm)  21.8 us
    ppermute x11, starting transfers between devices, around(): return lax.ppermute(x, axis, [(i, (i + distance) % n) for i in range(n)])  8.33 us
    pallas_call x4, Pallas kernels, write(): pl.pallas_call(functools.partial(write_kernel, layer, stages[0], len(kept...  4.42 us
    ppermute x3, starting transfers between devices, backward(): up = lax.ppermute(grads[0], 'chain', [(c, c - 1) for c in range(1, chain)])  4.1 us
    ppermute x11, waiting for transfers between devices, around(): return lax.ppermute(x, axis, [(i, (i + distance) % n) for i in range(n)])  3.53 us
    ppermute x3, waiting for transfers between devices, backward(): up = lax.ppermute(grads[0], 'chain', [(c, c - 1) for c in range(1, chain)])  3.46 us
  transfers between devices with their start and end apart: 32, of which 15 were waited for; matrix products, arithmetic and copies ran while one was open for 1% of the time, Pallas kernels for 25%

profile of v12, /device:TPU:0, one launch (start us, length us, event | category | flops | bytes accessed | tf_op | source)
XLA Modules:
  0.0 100.2 jit_solution(5634188136482493376)
XLA Ops:
  3.3 4.9 %collective-permute-start = (bf16[128,256]{1,0:T(8,128)(2,1)S(1)}, bf16[128,256]{1,0:T(8,128)(2,1)S(1)}, u32[]{:S(2)}, u32[]{:S(2)}) collective-permute-start(bf16[128,256]{1,0:T(8,128)(2,1)S(1)} %get-tuple-element.117), channel_id=1, source_target_pairs={{0,4},{2,6},{5,9},{7,11},{8,12},{10,14},{16,20},{18,22},{21,25},{2... | collective-permute-start | bytes 196616 | tf_op jit(solution)/shard_map/ppermute | solution.py:423
  8.2 1.6 %collective-permute-start.3 = (bf16[128,256]{1,0:T(8,128)(2,1)S(1)}, bf16[128,256]{1,0:T(8,128)(2,1)S(1)}, u32[]{:S(2)}, u32[]{:S(2)}) collective-permute-start(bf16[128,256]{1,0:T(8,128)(2,1)S(1)} %get-tuple-element.124), channel_id=1, source_target_pairs={{0,2},{2,0},{1,3},{3,1},{4,6},{6,4},{5,7},{7,5},{8,10},{10,8},{9,1... | collective-permute-start | bytes 196616 | tf_op jit(solution)/shard_map/ppermute | solution.py:410
  11.8 1.6 %adjacency.1 = (bf16[768,768]{1,0:T(8,128)(2,1)S(1)}, bf16[768,768]{1,0:T(8,128)(2,1)S(1)}, bf16[768,256]{1,0:T(8,128)(2,1)S(1)}, bf16[256,768]{1,0:T(8,128)(2,1)S(1)}) custom-call(s32[4,6]{1,0:T(4,128)S(1)} %bitcast.4, bf16[6,4,128,128]{3,2,1,0:T(8,128)(2,1)S(1)} %copy-done.3, bf16[128,768]{1,0:T(8,128)(2,1)S(1)} %get-tuple-element.118.refs_2_, ...), custom_call_target="tpu_custom_call" | custom-call | flops 150994944 | bytes 4000000 | tf_op jit(solution)/shard_map/adjacency/pallas_call | solution.py:32
  15.8 2.8 %collective-permute-start.5 = (bf16[128,256]{1,0:T(8,128)(2,1)S(1)}, bf16[128,256]{1,0:T(8,128)(2,1)S(1)}, u32[]{:S(2)}, u32[]{:S(2)}) collective-permute-start(bf16[128,256]{1,0:T(8,128)(2,1)S(1)} %get-tuple-element.128), channel_id=1, source_target_pairs={{0,4},{2,6},{5,9},{7,11},{8,12},{10,14},{16,20},{18,22},{21,25},{2... | collective-permute-start | bytes 196616 | tf_op jit(solution)/shard_map/ppermute | solution.py:423
  19.1 1.6 %local1.1 = (bf16[768,256]{1,0:T(8,128)(2,1)S(1)}, bf16[768,512]{1,0:T(8,128)(2,1)S(1)}, bf16[768,512]{1,0:T(8,128)(2,1)S(1)}, bf16[512,768]{1,0:T(8,128)(2,1)S(1)}, bf16[256,768]{1,0:T(8,128)(2,1)S(1)}) custom-call(bf16[768,256]{1,0:T(8,128)(2,1)S(1)} %get-tuple-element.129.refs_0_, bf16[3,256,512]{2,1,0:T(8,128)(2,1)S(1)} %copy-done, ...), custom_call_target="tpu_custom_call" | custom-call | flops 805306368 | bytes 4000000 | tf_op jit(solution)/shard_map/local1/pallas_call | solution.py:32
  20.8 2.0 %collective-permute-done.6.refs_7_.refs_14_ = bf16[128,256]{1,0:T(8,128)(2,1)S(1)} collective-permute-done((bf16[128,256]{1,0:T(8,128)(2,1)S(1)}, bf16[128,256]{1,0:T(8,128)(2,1)S(1)}, u32[]{:S(2)}, u32[]{:S(2)}) %collective-permute-start.6) | collective-permute-done | bytes 65568 | tf_op jit(solution)/shard_map/ppermute | solution.py:410
  24.9 2.3 %collective-permute-start.8 = (bf16[128,256]{1,0:T(8,128)(2,1)S(1)}, bf16[128,256]{1,0:T(8,128)(2,1)S(1)}, u32[]{:S(2)}, u32[]{:S(2)}) collective-permute-start(bf16[128,256]{1,0:T(8,128)(2,1)S(1)} %get-tuple-element.135), channel_id=1, source_target_pairs={{0,4},{2,6},{5,9},{7,11},{8,12},{10,14},{16,20},{18,22},{21,25},{2... | collective-permute-start | bytes 196616 | tf_op jit(solution)/shard_map/ppermute | solution.py:423
  27.2 1.4 %collective-permute-start.9 = (bf16[128,256]{1,0:T(8,128)(2,1)S(1)}, bf16[128,256]{1,0:T(8,128)(2,1)S(1)}, u32[]{:S(2)}, u32[]{:S(2)}) collective-permute-start(bf16[128,256]{1,0:T(8,128)(2,1)S(1)} %get-tuple-element.139), channel_id=1, source_target_pairs={{0,2},{2,0},{1,3},{3,1},{4,6},{6,4},{5,7},{7,5},{8,10},{10,8},{9,1... | collective-permute-start | bytes 196616 | tf_op jit(solution)/shard_map/ppermute | solution.py:410
  28.6 1.6 %local2.1 = (bf16[768,256]{1,0:T(8,128)(2,1)S(1)}, bf16[768,512]{1,0:T(8,128)(2,1)S(1)}, bf16[768,512]{1,0:T(8,128)(2,1)S(1)}, bf16[512,768]{1,0:T(8,128)(2,1)S(1)}, bf16[256,768]{1,0:T(8,128)(2,1)S(1)}) custom-call(bf16[768,256]{1,0:T(8,128)(2,1)S(1)} %get-tuple-element.136.refs_0_, bf16[3,256,512]{2,1,0:T(8,128)(2,1)S(1)} %copy-done, ...), custom_call_target="tpu_custom_call" | custom-call | flops 805306368 | bytes 4000000 | tf_op jit(solution)/shard_map/local2/pallas_call | solution.py:32
  32.5 2.0 %turn.1 = (f32[768,256]{1,0:T(8,128)S(1)}, bf16[768,256]{1,0:T(8,128)(2,1)S(1)}, bf16[256,256]{1,0:T(8,128)(2,1)S(1)}, bf16[256,256]{1,0:T(8,128)(2,1)S(1)}, bf1...) custom-call(f32[768,256]{1,0:T(8,128)S(1)} %get-tuple-element.134.re, ...), custom_call_target="tpu_custom_call" | custom-call | flops 536870912 | bytes 4000000 | tf_op jit(solution)/shard_map/turn/pallas_call | solution.py:32
  35.8 1.4 %collective-permute-start.12 = (bf16[128,256]{1,0:T(8,128)(2,1)S(1)}, bf16[128,256]{1,0:T(8,128)(2,1)S(1)}, u32[]{:S(2)}, u32[]{:S(2)}) collective-permute-start(bf16[128,256]{1,0:T(8,128)(2,1)S(1)} %get-tuple-element.154), channel_id=1, source_target_pairs={{0,2},{2,0},{1,3},{3,1},{4,6},{6,4},{5,7},{7,5},{8,10},{10,8},{9,1... | collective-permute-start | bytes 196616 | tf_op jit(solution)/shard_map/ppermute | solution.py:410
  37.2 2.4 %back2.1 = (f32[768,256]{1,0:T(8,128)S(1)}, f32[2048,128]{1,0:T(8,128)S(1)}) custom-call(bf16[768,256]{1,0:T(8,128)(2,1)S(1)} %get-tuple-element.142.refs_0_, bf16[768,768]{1,0:T(8,128)(2,1)S(1)} %get-tuple-element.143.refs_1_.refs_2_, bf16[768,512]{1,0:T(8,128)(2,1)S(1)} %get-tuple-element.144.refs_2_, bf16[768,512]{1,0:T(8,128)(2,1)S(1)} %get-tuple-element.145.refs_3_, ...), custom_call_target="tpu_custom_call" | custom-call | flops 2717908992 | bytes 4000000 | tf_op jit(solution)/shard_map/back2/pallas_call | solution.py:32
  40.8 2.2 %collective-permute-start.15 = (bf16[1024,128]{1,0:T(8,128)(2,1)S(1)}, bf16[1024,128]{1,0:T(8,128)(2,1)S(1)}, u32[]{:S(2)}, u32[]{:S(2)}) collective-permute-start(bf16[1024,128]{1,0:T(8,128)(2,1)S(1)} %get-tuple-element.173), channel_id=1, source_target_pairs={{0,4},{1,3},{2,6},{3,1},{4,0},{5,7},{6,2},{7,5},{8,12},{9,11},{10,... | collective-permute-start | bytes 786440 | tf_op jit(solution)/shard_map/ppermute | solution.py:423
  42.9 1.5 %join2.1 = (f32[768,256]{1,0:T(8,128)S(1)}, bf16[768,256]{1,0:T(8,128)(2,1)S(1)}, bf16[256,256]{1,0:T(8,128)(2,1)S(1)}, bf16[256,256]{1,0:T(8,128)(2,1)S(1)}, bf...) custom-call(f32[1024,128]{1,0:T(8,128)S(1)} %get-tuple-element.156.r, ...), custom_call_target="tpu_custom_call" | custom-call | flops 536870912 | bytes 4000000 | tf_op jit(solution)/shard_map/join2/pallas_call | solution.py:32
  44.4 1.5 %collective-permute-start.13 = (bf16[128,256]{1,0:T(8,128)(2,1)S(1)}, bf16[128,256]{1,0:T(8,128)(2,1)S(1)}, u32[]{:S(2)}, u32[]{:S(2)}) collective-permute-start(bf16[128,256]{1,0:T(8,128)(2,1)S(1)} %get-tuple-element.169), channel_id=1, source_target_pairs={{4,0},{8,4},{12,8},{5,1},{9,5},{13,9},{6,2},{10,6},{14,10},{7,3},{... | collective-permute-start | bytes 196616 | tf_op jit(solution)/shard_map/ppermute | solution.py:446
  45.9 1.4 %collective-permute-start.14 = (bf16[128,256]{1,0:T(8,128)(2,1)S(1)}, bf16[128,256]{1,0:T(8,128)(2,1)S(1)}, u32[]{:S(2)}, u32[]{:S(2)}) collective-permute-start(bf16[128,256]{1,0:T(8,128)(2,1)S(1)} %get-tuple-element.170), channel_id=1, source_target_pairs={{0,2},{2,0},{1,3},{3,1},{4,6},{6,4},{5,7},{7,5},{8,10},{10,8},{9,1... | collective-permute-start | bytes 196616 | tf_op jit(solution)/shard_map/ppermute | solution.py:410
  47.3 2.4 %back1.1 = (f32[768,256]{1,0:T(8,128)S(1)}, f32[2048,128]{1,0:T(8,128)S(1)}) custom-call(bf16[768,256]{1,0:T(8,128)(2,1)S(1)} %get-tuple-element.159.refs_0_.refs_1_, bf16[768,256]{1,0:T(8,128)(2,1)S(1)} %get-tuple-element.159.refs_0_.refs_1_, bf16[768,768]{1,0:T(8,128)(2,1)S(1)} %get-tuple-element.143.refs_1_.refs_2_, ...), custom_call_target="tpu_custom_call" | custom-call | flops 2717908992 | bytes 4000000 | tf_op jit(solution)/shard_map/back1/pallas_call | solution.py:32
  50.6 3.1 %collective-permute-start.17 = (bf16[1024,128]{1,0:T(8,128)(2,1)S(1)}, bf16[1024,128]{1,0:T(8,128)(2,1)S(1)}, u32[]{:S(2)}, u32[]{:S(2)}) collective-permute-start(bf16[1024,128]{1,0:T(8,128)(2,1)S(1)} %get-tuple-element.190), channel_id=1, source_target_pairs={{0,4},{1,3},{2,6},{3,1},{4,0},{5,7},{6,2},{7,5},{8,12},{9,11},{10,... | collective-permute-start | bytes 786440 | tf_op jit(solution)/shard_map/ppermute | solution.py:423
  53.8 1.4 %collective-permute-start.16 = (bf16[512,128]{1,0:T(8,128)(2,1)S(1)}, bf16[512,128]{1,0:T(8,128)(2,1)S(1)}, u32[]{:S(2)}, u32[]{:S(2)}) collective-permute-start(bf16[512,128]{1,0:T(8,128)(2,1)S(1)} %get-tuple-element.186), channel_id=1, source_target_pairs={{0,2},{1,5},{2,0},{3,7},{4,6},{5,1},{6,4},{7,3},{8,10},{9,13},{10,... | collective-permute-start | bytes 393224 | tf_op jit(solution)/shard_map/ppermute | solution.py:423
  55.2 1.5 %join1.1 = (f32[768,256]{1,0:T(8,128)S(1)}, bf16[768,256]{1,0:T(8,128)(2,1)S(1)}, bf16[256,256]{1,0:T(8,128)(2,1)S(1)}, bf16[256,256]{1,0:T(8,128)(2,1)S(1)}, bf...) custom-call(f32[512,128]{1,0:T(8,128)S(1)} %get-tuple-element.174.re, ...), custom_call_target="tpu_custom_call" | custom-call | flops 536870912 | bytes 4000000 | tf_op jit(solution)/shard_map/join1/pallas_call | solution.py:32
  56.7 2.4 %back0.1 = (f32[768,256]{1,0:T(8,128)S(1)}, f32[2048,128]{1,0:T(8,128)S(1)}) custom-call(bf16[768,256]{1,0:T(8,128)(2,1)S(1)} %get-tuple-element.176.refs_0_.refs_1_, bf16[768,256]{1,0:T(8,128)(2,1)S(1)} %get-tuple-element.176.refs_0_.refs_1_, bf16[768,768]{1,0:T(8,128)(2,1)S(1)} %get-tuple-element.143.refs_1_.refs_2_, ...), custom_call_target="tpu_custom_call" | custom-call | flops 2717908992 | bytes 4000000 | tf_op jit(solution)/shard_map/back0/pallas_call | solution.py:32
  61.1 1.4 %collective-permute-start.20 = (bf16[512,128]{1,0:T(8,128)(2,1)S(1)}, bf16[512,128]{1,0:T(8,128)(2,1)S(1)}, u32[]{:S(2)}, u32[]{:S(2)}) collective-permute-start(bf16[512,128]{1,0:T(8,128)(2,1)S(1)} %get-tuple-element.196), channel_id=1, source_target_pairs={{0,2},{1,5},{2,0},{3,7},{4,6},{5,1},{6,4},{7,3},{8,10},{9,13},{10,... | collective-permute-start | bytes 393224 | tf_op jit(solution)/shard_map/ppermute | solution.py:423
  62.6 9.0 %collective-permute-done.18.refs_2_ = bf16[1024,128]{1,0:T(8,128)(2,1)S(1)} collective-permute-done((bf16[1024,128]{1,0:T(8,128)(2,1)S(1)}, bf16[1024,128]{1,0:T(8,128)(2,1)S(1)}, u32[]{:S(2)}, u32[]{:S(2)}) %collective-permute-start.18) | collective-permute-done | bytes 262176 | tf_op jit(solution)/shard_map/ppermute | solution.py:423
  71.7 1.8 %collective-permute-start.21 = (bf16[512,128]{1,0:T(8,128)(2,1)S(1)}, bf16[512,128]{1,0:T(8,128)(2,1)S(1)}, u32[]{:S(2)}, u32[]{:S(2)}) collective-permute-start(bf16[512,128]{1,0:T(8,128)(2,1)S(1)} %get-tuple-element.198), channel_id=1, source_target_pairs={{0,2},{1,5},{2,0},{3,7},{4,6},{5,1},{6,4},{7,3},{8,10},{9,13},{10,... | collective-permute-start | bytes 393224 | tf_op jit(solution)/shard_map/ppermute | solution.py:423
  74.8 3.1 %collective-permute-done.21.refs_2_ = bf16[512,128]{1,0:T(8,128)(2,1)S(1)} collective-permute-done((bf16[512,128]{1,0:T(8,128)(2,1)S(1)}, bf16[512,128]{1,0:T(8,128)(2,1)S(1)}, u32[]{:S(2)}, u32[]{:S(2)}) %collective-permute-start.21) | collective-permute-done | bytes 131104 | tf_op jit(solution)/shard_map/ppermute | solution.py:423
  79.4 1.7 %collective-permute-done.23.refs_2_ = bf16[512,128]{1,0:T(8,128)(2,1)S(1)} collective-permute-done((bf16[512,128]{1,0:T(8,128)(2,1)S(1)}, bf16[512,128]{1,0:T(8,128)(2,1)S(1)}, u32[]{:S(2)}, u32[]{:S(2)}) %collective-permute-start.23) | collective-permute-done | bytes 131104 | tf_op jit(solution)/shard_map/ppermute | solution.py:423
  81.2 1.4 %collective-permute-start.25 = (bf16[512,128]{1,0:T(8,128)(2,1)S(1)}, bf16[512,128]{1,0:T(8,128)(2,1)S(1)}, u32[]{:S(2)}, u32[]{:S(2)}) collective-permute-start(bf16[512,128]{1,0:T(8,128)(2,1)S(1)} %get-tuple-element.206), channel_id=1, source_target_pairs={{0,2},{1,5},{2,0},{3,7},{4,6},{5,1},{6,4},{7,3},{8,10},{9,13},{10,... | collective-permute-start | bytes 393224 | tf_op jit(solution)/shard_map/ppermute | solution.py:423
  82.6 2.0 %collective-permute-done.24.refs_2_ = bf16[512,128]{1,0:T(8,128)(2,1)S(1)} collective-permute-done((bf16[512,128]{1,0:T(8,128)(2,1)S(1)}, bf16[512,128]{1,0:T(8,128)(2,1)S(1)}, u32[]{:S(2)}, u32[]{:S(2)}) %collective-permute-start.24) | collective-permute-done | bytes 131104 | tf_op jit(solution)/shard_map/ppermute | solution.py:423
  85.9 1.5 %collective-permute-done.25.refs_2_ = bf16[512,128]{1,0:T(8,128)(2,1)S(1)} collective-permute-done((bf16[512,128]{1,0:T(8,128)(2,1)S(1)}, bf16[512,128]{1,0:T(8,128)(2,1)S(1)}, u32[]{:S(2)}, u32[]{:S(2)}) %collective-permute-start.25) | collective-permute-done | bytes 131104 | tf_op jit(solution)/shard_map/ppermute | solution.py:423
  88.2 1.5 %collective-permute-done.27.refs_3_ = bf16[512,128]{1,0:T(8,128)(2,1)S(1)} collective-permute-done((bf16[512,128]{1,0:T(8,128)(2,1)S(1)}, bf16[512,128]{1,0:T(8,128)(2,1)S(1)}, u32[]{:S(2)}, u32[]{:S(2)}) %collective-permute-start.27) | collective-permute-done | bytes 131104 | tf_op jit(solution)/shard_map/ppermute | solution.py:423
  95.9 1.6 %collective-permute-done.29.refs_4_ = bf16[128,256]{1,0:T(8,128)(2,1)S(1)} collective-permute-done((bf16[128,256]{1,0:T(8,128)(2,1)S(1)}, bf16[128,256]{1,0:T(8,128)(2,1)S(1)}, u32[]{:S(2)}, u32[]{:S(2)}) %collective-permute-start.29) | collective-permute-done | bytes 65568 | tf_op jit(solution)/shard_map/ppermute | solution.py:446
  98.6 1.4 %write0.3 = (f32[3,256,512]{2,1,0:T(8,128)}, f32[3,512,256]{2,1,0:T(8,128)}, f32[8,128]{1,0:T(8,128)}) custom-call(f32[3,256,512]{2,1,0:T(8,128)} %get-tuple-element.223.refs_0_, f32[3,512,256]{2,1,0:T(8,128)} %get-tuple-element.224.refs_1_, f32[8,128]{1,0:T(8,128)S(1)} %get-tuple-element.225.refs_2_, ...), custom_call_target="tpu_custom_call", output_to_operand_aliasing={{0}: (0, {}), {1}: (1, {})} | custom-call | flops 1 | bytes 1 | tf_op jit(solution)/shard_map/write0/pallas_call | solution.py:605
  (82 shorter events, 29.8 us)
Async XLA Ops:
  0.7 9.1 %collective-permute-start.1 = (bf16[3,256,512]{2,1,0:T(8,128)(2,1)}, bf16[3,256,512]{2,1,0:T(8,128)(2,1)S(1)}, u32[]{:S(2)}, u32[]{:S(2)}) collective-permute-start(bf16[3,256,512]{2,1,0:T(8,128)(2,1)} %refs_7_.5), channel_id=1, source_target_pairs={{0,1},{1,0},{2,3},{3,2},{4,5},{5,4},{6,7},{7,6},{8,9},{9,8},{10,11... | collective-permute-start | bytes 2359304 | tf_op jit(solution)/shard_map/ppermute | solution.py:410
  1.2 8.6 %collective-permute-start.2 = (bf16[3,512,256]{2,1,0:T(8,128)(2,1)}, bf16[3,512,256]{2,1,0:T(8,128)(2,1)S(1)}, u32[]{:S(2)}, u32[]{:S(2)}) collective-permute-start(bf16[3,512,256]{2,1,0:T(8,128)(2,1)} %refs_9_.3), channel_id=1, source_target_pairs={{0,1},{1,0},{2,3},{3,2},{4,5},{5,4},{6,7},{7,6},{8,9},{9,8},{10,11... | collective-permute-start | bytes 2359304 | tf_op jit(solution)/shard_map/ppermute | solution.py:410
  3.3 10.1 %collective-permute-start = (bf16[128,256]{1,0:T(8,128)(2,1)S(1)}, bf16[128,256]{1,0:T(8,128)(2,1)S(1)}, u32[]{:S(2)}, u32[]{:S(2)}) collective-permute-start(bf16[128,256]{1,0:T(8,128)(2,1)S(1)} %get-tuple-element.117), channel_id=1, source_target_pairs={{0,4},{2,6},{5,9},{7,11},{8,12},{10,14},{16,20},{18,22},{21,25},{2... | collective-permute-start | bytes 196616 | tf_op jit(solution)/shard_map/ppermute | solution.py:423
  8.2 5.2 %collective-permute-start.3 = (bf16[128,256]{1,0:T(8,128)(2,1)S(1)}, bf16[128,256]{1,0:T(8,128)(2,1)S(1)}, u32[]{:S(2)}, u32[]{:S(2)}) collective-permute-start(bf16[128,256]{1,0:T(8,128)(2,1)S(1)} %get-tuple-element.124), channel_id=1, source_target_pairs={{0,2},{2,0},{1,3},{3,1},{4,6},{6,4},{5,7},{7,5},{8,10},{10,8},{9,1... | collective-permute-start | bytes 196616 | tf_op jit(solution)/shard_map/ppermute | solution.py:410
  13.4 1.3 %collective-permute-start.4 = (bf16[128,256]{1,0:T(8,128)(2,1)S(1)}, bf16[128,256]{1,0:T(8,128)(2,1)S(1)}, u32[]{:S(2)}, u32[]{:S(2)}) collective-permute-start(bf16[128,256]{1,0:T(8,128)(2,1)S(1)} %collective-permute-done.refs_8_.refs_12_), channel_id=1, source_target_pairs={{0,1},{1,0},{2,3},{3,2},{4,5},{5,4},{6,7},{7,6},{8,9},{9,8},{10,11... | collective-permute-start | bytes 196616 | tf_op jit(solution)/shard_map/ppermute | solution.py:410
  15.8 5.0 %collective-permute-start.5 = (bf16[128,256]{1,0:T(8,128)(2,1)S(1)}, bf16[128,256]{1,0:T(8,128)(2,1)S(1)}, u32[]{:S(2)}, u32[]{:S(2)}) collective-permute-start(bf16[128,256]{1,0:T(8,128)(2,1)S(1)} %get-tuple-element.128), channel_id=1, source_target_pairs={{0,4},{2,6},{5,9},{7,11},{8,12},{10,14},{16,20},{18,22},{21,25},{2... | collective-permute-start | bytes 196616 | tf_op jit(solution)/shard_map/ppermute | solution.py:423
  18.5 4.3 %collective-permute-start.6 = (bf16[128,256]{1,0:T(8,128)(2,1)S(1)}, bf16[128,256]{1,0:T(8,128)(2,1)S(1)}, u32[]{:S(2)}, u32[]{:S(2)}) collective-permute-start(bf16[128,256]{1,0:T(8,128)(2,1)S(1)} %get-tuple-element.132), channel_id=1, source_target_pairs={{0,2},{2,0},{1,3},{3,1},{4,6},{6,4},{5,7},{7,5},{8,10},{10,8},{9,1... | collective-permute-start | bytes 196616 | tf_op jit(solution)/shard_map/ppermute | solution.py:410
  20.8 3.1 %collective-permute-start.7 = (bf16[128,256]{1,0:T(8,128)(2,1)S(1)}, bf16[128,256]{1,0:T(8,128)(2,1)S(1)}, u32[]{:S(2)}, u32[]{:S(2)}) collective-permute-start(bf16[128,256]{1,0:T(8,128)(2,1)S(1)} %collective-permute-done.5.refs_8_.refs_12_), channel_id=1, source_target_pairs={{0,1},{1,0},{2,3},{3,2},{4,5},{5,4},{6,7},{7,6},{8,9},{9,8},{10,11... | collective-permute-start | bytes 196616 | tf_op jit(solution)/shard_map/ppermute | solution.py:410
  24.9 5.2 %collective-permute-start.8 = (bf16[128,256]{1,0:T(8,128)(2,1)S(1)}, bf16[128,256]{1,0:T(8,128)(2,1)S(1)}, u32[]{:S(2)}, u32[]{:S(2)}) collective-permute-start(bf16[128,256]{1,0:T(8,128)(2,1)S(1)} %get-tuple-element.135), channel_id=1, source_target_pairs={{0,4},{2,6},{5,9},{7,11},{8,12},{10,14},{16,20},{18,22},{21,25},{2... | collective-permute-start | bytes 196616 | tf_op jit(solution)/shard_map/ppermute | solution.py:423
  27.2 4.3 %collective-permute-start.9 = (bf16[128,256]{1,0:T(8,128)(2,1)S(1)}, bf16[128,256]{1,0:T(8,128)(2,1)S(1)}, u32[]{:S(2)}, u32[]{:S(2)}) collective-permute-start(bf16[128,256]{1,0:T(8,128)(2,1)S(1)} %get-tuple-element.139), channel_id=1, source_target_pairs={{0,2},{2,0},{1,3},{3,1},{4,6},{6,4},{5,7},{7,5},{8,10},{10,8},{9,1... | collective-permute-start | bytes 196616 | tf_op jit(solution)/shard_map/ppermute | solution.py:410
  30.2 2.3 %collective-permute-start.10 = (bf16[128,256]{1,0:T(8,128)(2,1)S(1)}, bf16[128,256]{1,0:T(8,128)(2,1)S(1)}, u32[]{:S(2)}, u32[]{:S(2)}) collective-permute-start(bf16[128,256]{1,0:T(8,128)(2,1)S(1)} %collective-permute-done.8.refs_9_), channel_id=1, source_target_pairs={{0,1},{1,0},{2,3},{3,2},{4,5},{5,4},{6,7},{7,6},{8,9},{9,8},{10,11... | collective-permute-start | bytes 196616 | tf_op jit(solution)/shard_map/ppermute | solution.py:410
  34.5 6.2 %collective-permute-start.11 = (bf16[128,256]{1,0:T(8,128)(2,1)S(1)}, bf16[128,256]{1,0:T(8,128)(2,1)S(1)}, u32[]{:S(2)}, u32[]{:S(2)}) collective-permute-start(bf16[128,256]{1,0:T(8,128)(2,1)S(1)} %get-tuple-element.153), channel_id=1, source_target_pairs={{4,0},{8,4},{12,8},{5,1},{9,5},{13,9},{6,2},{10,6},{14,10},{7,3},{... | collective-permute-start | bytes 196616 | tf_op jit(solution)/shard_map/ppermute | solution.py:446
  35.8 4.9 %collective-permute-start.12 = (bf16[128,256]{1,0:T(8,128)(2,1)S(1)}, bf16[128,256]{1,0:T(8,128)(2,1)S(1)}, u32[]{:S(2)}, u32[]{:S(2)}) collective-permute-start(bf16[128,256]{1,0:T(8,128)(2,1)S(1)} %get-tuple-element.154), channel_id=1, source_target_pairs={{0,2},{2,0},{1,3},{3,1},{4,6},{6,4},{5,7},{7,5},{8,10},{10,8},{9,1... | collective-permute-start | bytes 196616 | tf_op jit(solution)/shard_map/ppermute | solution.py:410
  40.8 12.9 %collective-permute-start.15 = (bf16[1024,128]{1,0:T(8,128)(2,1)S(1)}, bf16[1024,128]{1,0:T(8,128)(2,1)S(1)}, u32[]{:S(2)}, u32[]{:S(2)}) collective-permute-start(bf16[1024,128]{1,0:T(8,128)(2,1)S(1)} %get-tuple-element.173), channel_id=1, source_target_pairs={{0,4},{1,3},{2,6},{3,1},{4,0},{5,7},{6,2},{7,5},{8,12},{9,11},{10,... | collective-permute-start | bytes 786440 | tf_op jit(solution)/shard_map/ppermute | solution.py:423
  44.4 6.2 %collective-permute-start.13 = (bf16[128,256]{1,0:T(8,128)(2,1)S(1)}, bf16[128,256]{1,0:T(8,128)(2,1)S(1)}, u32[]{:S(2)}, u32[]{:S(2)}) collective-permute-start(bf16[128,256]{1,0:T(8,128)(2,1)S(1)} %get-tuple-element.169), channel_id=1, source_target_pairs={{4,0},{8,4},{12,8},{5,1},{9,5},{13,9},{6,2},{10,6},{14,10},{7,3},{... | collective-permute-start | bytes 196616 | tf_op jit(solution)/shard_map/ppermute | solution.py:446
  45.9 4.6 %collective-permute-start.14 = (bf16[128,256]{1,0:T(8,128)(2,1)S(1)}, bf16[128,256]{1,0:T(8,128)(2,1)S(1)}, u32[]{:S(2)}, u32[]{:S(2)}) collective-permute-start(bf16[128,256]{1,0:T(8,128)(2,1)S(1)} %get-tuple-element.170), channel_id=1, source_target_pairs={{0,2},{2,0},{1,3},{3,1},{4,6},{6,4},{5,7},{7,5},{8,10},{10,8},{9,1... | collective-permute-start | bytes 196616 | tf_op jit(solution)/shard_map/ppermute | solution.py:410
  50.6 10.4 %collective-permute-start.17 = (bf16[1024,128]{1,0:T(8,128)(2,1)S(1)}, bf16[1024,128]{1,0:T(8,128)(2,1)S(1)}, u32[]{:S(2)}, u32[]{:S(2)}) collective-permute-start(bf16[1024,128]{1,0:T(8,128)(2,1)S(1)} %get-tuple-element.190), channel_id=1, source_target_pairs={{0,4},{1,3},{2,6},{3,1},{4,0},{5,7},{6,2},{7,5},{8,12},{9,11},{10,... | collective-permute-start | bytes 786440 | tf_op jit(solution)/shard_map/ppermute | solution.py:423
  53.8 6.5 %collective-permute-start.16 = (bf16[512,128]{1,0:T(8,128)(2,1)S(1)}, bf16[512,128]{1,0:T(8,128)(2,1)S(1)}, u32[]{:S(2)}, u32[]{:S(2)}) collective-permute-start(bf16[512,128]{1,0:T(8,128)(2,1)S(1)} %get-tuple-element.186), channel_id=1, source_target_pairs={{0,2},{1,5},{2,0},{3,7},{4,6},{5,1},{6,4},{7,3},{8,10},{9,13},{10,... | collective-permute-start | bytes 393224 | tf_op jit(solution)/shard_map/ppermute | solution.py:423
  60.3 11.2 %collective-permute-start.18 = (bf16[1024,128]{1,0:T(8,128)(2,1)S(1)}, bf16[1024,128]{1,0:T(8,128)(2,1)S(1)}, u32[]{:S(2)}, u32[]{:S(2)}) collective-permute-start(bf16[1024,128]{1,0:T(8,128)(2,1)S(1)} %get-tuple-element.192), channel_id=1, source_target_pairs={{0,4},{1,3},{2,6},{3,1},{4,0},{5,7},{6,2},{7,5},{8,12},{9,11},{10,... | collective-permute-start | bytes 786440 | tf_op jit(solution)/shard_map/ppermute | solution.py:423
  60.5 13.0 %collective-permute-start.19 = (bf16[512,128]{1,0:T(8,128)(2,1)S(1)}, bf16[512,128]{1,0:T(8,128)(2,1)S(1)}, u32[]{:S(2)}, u32[]{:S(2)}) collective-permute-start(bf16[512,128]{1,0:T(8,128)(2,1)S(1)} %get-tuple-element.194), channel_id=1, source_target_pairs={{0,8},{1,9},{2,10},{3,11},{4,12},{5,13},{6,14},{7,15},{8,0},{9,1},... | collective-permute-start | bytes 393224 | tf_op jit(solution)/shard_map/ppermute | solution.py:423
  61.1 12.8 %collective-permute-start.20 = (bf16[512,128]{1,0:T(8,128)(2,1)S(1)}, bf16[512,128]{1,0:T(8,128)(2,1)S(1)}, u32[]{:S(2)}, u32[]{:S(2)}) collective-permute-start(bf16[512,128]{1,0:T(8,128)(2,1)S(1)} %get-tuple-element.196), channel_id=1, source_target_pairs={{0,2},{1,5},{2,0},{3,7},{4,6},{5,1},{6,4},{7,3},{8,10},{9,13},{10,... | collective-permute-start | bytes 393224 | tf_op jit(solution)/shard_map/ppermute | solution.py:423
  71.7 6.1 %collective-permute-start.21 = (bf16[512,128]{1,0:T(8,128)(2,1)S(1)}, bf16[512,128]{1,0:T(8,128)(2,1)S(1)}, u32[]{:S(2)}, u32[]{:S(2)}) collective-permute-start(bf16[512,128]{1,0:T(8,128)(2,1)S(1)} %get-tuple-element.198), channel_id=1, source_target_pairs={{0,2},{1,5},{2,0},{3,7},{4,6},{5,1},{6,4},{7,3},{8,10},{9,13},{10,... | collective-permute-start | bytes 393224 | tf_op jit(solution)/shard_map/ppermute | solution.py:423
  73.5 5.7 %collective-permute-start.22 = (bf16[512,128]{1,0:T(8,128)(2,1)S(1)}, bf16[512,128]{1,0:T(8,128)(2,1)S(1)}, u32[]{:S(2)}, u32[]{:S(2)}) collective-permute-start(bf16[512,128]{1,0:T(8,128)(2,1)S(1)} %get-tuple-element.200), channel_id=1, source_target_pairs={{0,2},{1,5},{2,0},{3,7},{4,6},{5,1},{6,4},{7,3},{8,10},{9,13},{10,... | collective-permute-start | bytes 393224 | tf_op jit(solution)/shard_map/ppermute | solution.py:423
  73.9 7.2 %collective-permute-start.23 = (bf16[512,128]{1,0:T(8,128)(2,1)S(1)}, bf16[512,128]{1,0:T(8,128)(2,1)S(1)}, u32[]{:S(2)}, u32[]{:S(2)}) collective-permute-start(bf16[512,128]{1,0:T(8,128)(2,1)S(1)} %get-tuple-element.202), channel_id=1, source_target_pairs={{0,8},{1,9},{2,10},{3,11},{4,12},{5,13},{6,14},{7,15},{8,0},{9,1},... | collective-permute-start | bytes 393224 | tf_op jit(solution)/shard_map/ppermute | solution.py:423
  77.9 6.7 %collective-permute-start.24 = (bf16[512,128]{1,0:T(8,128)(2,1)S(1)}, bf16[512,128]{1,0:T(8,128)(2,1)S(1)}, u32[]{:S(2)}, u32[]{:S(2)}) collective-permute-start(bf16[512,128]{1,0:T(8,128)(2,1)S(1)} %get-tuple-element.204), channel_id=1, source_target_pairs={{0,8},{1,9},{2,10},{3,11},{4,12},{5,13},{6,14},{7,15},{8,0},{9,1},... | collective-permute-start | bytes 393224 | tf_op jit(solution)/shard_map/ppermute | solution.py:423
  79.3 8.9 %collective-permute-start.26 = (bf16[1024,128]{1,0:T(8,128)(2,1)S(1)}, bf16[1024,128]{1,0:T(8,128)(2,1)S(1)}, u32[]{:S(2)}, u32[]{:S(2)}) collective-permute-start(bf16[1024,128]{1,0:T(8,128)(2,1)S(1)} %get-tuple-element.208), channel_id=1, source_target_pairs={{0,4},{1,3},{2,6},{3,1},{4,0},{5,7},{6,2},{7,5},{8,12},{9,11},{10,... | collective-permute-start | bytes 786440 | tf_op jit(solution)/shard_map/ppermute | solution.py:423
  81.2 6.3 %collective-permute-start.25 = (bf16[512,128]{1,0:T(8,128)(2,1)S(1)}, bf16[512,128]{1,0:T(8,128)(2,1)S(1)}, u32[]{:S(2)}, u32[]{:S(2)}) collective-permute-start(bf16[512,128]{1,0:T(8,128)(2,1)S(1)} %get-tuple-element.206), channel_id=1, source_target_pairs={{0,2},{1,5},{2,0},{3,7},{4,6},{5,1},{6,4},{7,3},{8,10},{9,13},{10,... | collective-permute-start | bytes 393224 | tf_op jit(solution)/shard_map/ppermute | solution.py:423
  84.7 5.0 %collective-permute-start.27 = (bf16[512,128]{1,0:T(8,128)(2,1)S(1)}, bf16[512,128]{1,0:T(8,128)(2,1)S(1)}, u32[]{:S(2)}, u32[]{:S(2)}) collective-permute-start(bf16[512,128]{1,0:T(8,128)(2,1)S(1)} %get-tuple-element.209), channel_id=1, source_target_pairs={{0,2},{1,5},{2,0},{3,7},{4,6},{5,1},{6,4},{7,3},{8,10},{9,13},{10,... | collective-permute-start | bytes 393224 | tf_op jit(solution)/shard_map/ppermute | solution.py:423
  87.5 6.4 %collective-permute-start.28 = (bf16[1024,128]{1,0:T(8,128)(2,1)S(1)}, bf16[1024,128]{1,0:T(8,128)(2,1)S(1)}, u32[]{:S(2)}, u32[]{:S(2)}) collective-permute-start(bf16[1024,128]{1,0:T(8,128)(2,1)S(1)} %get-tuple-element.214), channel_id=1, source_target_pairs={{0,4},{1,3},{2,6},{3,1},{4,0},{5,7},{6,2},{7,5},{8,12},{9,11},{10,... | collective-permute-start | bytes 786440 | tf_op jit(solution)/shard_map/ppermute | solution.py:423
  89.8 8.8 %collective-permute-start.31 = (bf16[1024,128]{1,0:T(8,128)(2,1)S(1)}, bf16[1024,128]{1,0:T(8,128)(2,1)S(1)}, u32[]{:S(2)}, u32[]{:S(2)}) collective-permute-start(bf16[1024,128]{1,0:T(8,128)(2,1)S(1)} %get-tuple-element.226), channel_id=1, source_target_pairs={{0,4},{1,3},{2,6},{3,1},{4,0},{5,7},{6,2},{7,5},{8,12},{9,11},{10,... | collective-permute-start | bytes 786440 | tf_op jit(solution)/shard_map/ppermute | solution.py:423
  89.8 7.6 %collective-permute-start.29 = (bf16[128,256]{1,0:T(8,128)(2,1)S(1)}, bf16[128,256]{1,0:T(8,128)(2,1)S(1)}, u32[]{:S(2)}, u32[]{:S(2)}) collective-permute-start(bf16[128,256]{1,0:T(8,128)(2,1)S(1)} %get-tuple-element.220), channel_id=1, source_target_pairs={{4,0},{8,4},{12,8},{5,1},{9,5},{13,9},{6,2},{10,6},{14,10},{7,3},{... | collective-permute-start | bytes 196616 | tf_op jit(solution)/shard_map/ppermute | solution.py:446
  91.1 6.3 %collective-permute-start.30 = (bf16[128,256]{1,0:T(8,128)(2,1)S(1)}, bf16[128,256]{1,0:T(8,128)(2,1)S(1)}, u32[]{:S(2)}, u32[]{:S(2)}) collective-permute-start(bf16[128,256]{1,0:T(8,128)(2,1)S(1)} %get-tuple-element.221), channel_id=1, source_target_pairs={{0,2},{2,0},{1,3},{3,1},{4,6},{6,4},{5,7},{7,5},{8,10},{10,8},{9,1... | collective-permute-start | bytes 196616 | tf_op jit(solution)/shard_map/ppermute | solution.py:410
  (6 other events, 25.7 us)

commit v13 on v11

--- a/solution.py
+++ b/solution.py
@@ -386,14 +386,15 @@
 
 
 def gathered_grad(dtotal, back, returned, spread):
-    far = jnp.concatenate([x[...] for x in returned], axis=0)
+    up = upstream_rows(*returned[:2])
+    far = jnp.concatenate([up, *(x[...] for x in returned[2:])], axis=0)
     return dtotal[...] + back[...] + mm(spread[...], far)
 
 
 def join_kernel(layer, groups, *refs):
     dtotal, back, spread, remote_t, total = refs[:5]
     weights, refs = refs[5:9], refs[9:]
-    returned, refs = refs[:groups], refs[groups:]
+    returned, refs = refs[: groups + 1], refs[groups + 1 :]
     received, outs = refs[: groups + 1], refs[groups + 1 :]
     grad = gathered_grad(dtotal, back, returned, spread)
     start_bwd(layer, norm_grad(grad, total[...]), weights, received, remote_t, outs)
@@ -437,14 +438,16 @@
     def downstream(c, b, feat):
         return (c + 1, b) if c % 2 == feat and c + 1 < chain else None
 
-    up = over_mesh(sends[0], downstream)
-    return [up] + [around(x, "basin", s + 1) for s, x in enumerate(sends[1:])]
+    others = [around(x, "basin", s + 1) for s, x in enumerate(sends[1:])]
+    return [over_mesh(sends[0], downstream), *others]
 
 
 def backward(grads):
-    chain = lax.axis_size("chain")
-    up = lax.ppermute(grads[0], "chain", [(c, c - 1) for c in range(1, chain)])
-    return [up] + [around(x, "basin", -s) for s, x in enumerate(grads) if s]
+    def upstream(c, b, feat):
+        return (c - 1, b) if c % 2 != feat and c > 0 else None
+
+    others = [around(x, "basin", -s) for s, x in enumerate(grads) if s]
+    return [over_mesh(grads[0], upstream), *others]
 
 
 def shards(features, cotangent, w_in, w_out, block_index, block_values, send_rows, send_count):
@@ -562,7 +565,7 @@
     sums = {}
 
     def back(layer, outs, after):
-        returned[layer] = backward(outs[6:])
+        up, *others = backward(outs[6:])
         grad, whole = call(
             functools.partial(back_kernel, layer, grad_scale),
             [((rows, latent), F32), ((grad_rows, LANES), F32)],
@@ -575,6 +578,10 @@
             name=f"back{layer}",
             after=after,
         )
+        if layer:
+            up, grad, others = lax.optimization_barrier((up, grad, others))
+            others = [around(up, "feat", 1), *others]
+        returned[layer] = [up, *others]
         sums[layer] = Sum(whole, stages)
         return [outs[0], grad], [grad]
 
@@ -634,7 +641,7 @@
         state, at = back(layer, outs, at)
         arrived = [sums[above].got[0] for above in range(layer + 2, layers)]
         if layer:
-            arrived += returned[layer]
+            arrived += [returned[layer][0], *returned[layer][2:]]
         at = sum_step([sums[layer]], at + arrived)
         if layer:
             for above in range(layer + 1, layers):
@@ -651,6 +658,11 @@
     for layer in reversed(range(1, layers)):
         *written, token = write(layer, written, at)
         at = [token]
+        if layer == last:
+            up, *others = returned[0]
+            up, token, others = lax.optimization_barrier((up, token, others))
+            returned[0] = [up, around(up, "feat", 1), *others]
+            at = [token]
     *written, token = write(0, written, at, (0,))
     grad, token = join(0, state, [token])
     *written, token = write(0, written, [token], (1,))

time: 99.4 us -> 102 us (1.026)
  waiting for transfers between devices: 14.4 us -> 25.5 us
  starting transfers between devices: 51 us -> 42.1 us
    ppermute x18 -> x21, waiting for transfers between devices: 6.57 us -> 22 us  [over_mesh(): return lax.ppermute(x, ('chain', 'basin', 'feat'), perm)]
    ppermute x18 -> x21, starting transfers between devices: 40.2 us -> 34.2 us  [over_mesh(): return lax.ppermute(x, ('chain', 'basin', 'feat'), perm)]
    ppermute x3 -> x0, waiting for transfers between devices: 4.27 us -> none  [backward(): up = lax.ppermute(grads[0], 'chain', [(c, c - 1) for c in range(1, chain)])]
    ppermute x3 -> x0, starting transfers between devices: 4.08 us -> none  [backward(): up = lax.ppermute(grads[0], 'chain', [(c, c - 1) for c in range(1, chain)])]
    ppermute x11 -> x14, starting transfers between devices: 6.63 us -> 7.92 us  [around(): return lax.ppermute(x, axis, [(i, (i + distance) % n) for i in range(n)])]
    ppermute x11 -> x14, waiting for transfers between devices: 3.53 us -> 3.55 us  [around(): return lax.ppermute(x, axis, [(i, (i + distance) % n) for i in range(n)])]
  transfers between devices with their start and end apart: 32 -> 35, of which waited for: 12 -> 15; matrix products, arithmetic and copies ran while one was open for 1% -> 1% of each run, Pallas kernels for 25% -> 25%
where the time goes in v13:
time: 102 us; the launch traced here: 101 us
  starting transfers between devices  42.1 us (41%)
  Pallas kernels  30.6 us (30%)
  waiting for transfers between devices  25.5 us (25%)
  between operations  1.25 us (1%)
  local copies, waits for them, and re-layouts  1.2 us (1%)
    ppermute x21, starting transfers between devices, over_mesh(): return lax.ppermute(x, ('chain', 'basin', 'feat'), perm)  34.2 us
    pallas_call x33, Pallas kernels, call(): pl.pallas_call(lambda *refs: body(*refs[skipped:]), out_shape=[jax.ShapeD...  26.2 us
    ppermute x21, waiting for transfers between devices, over_mesh(): return lax.ppermute(x, ('chain', 'basin', 'feat'), perm)  22 us
    ppermute x14, starting transfers between devices, around(): return lax.ppermute(x, axis, [(i, (i + distance) % n) for i in range(n)])  7.92 us
    pallas_call x4, Pallas kernels, write(): pl.pallas_call(functools.partial(write_kernel, layer, stages[0], len(kept...  4.44 us
    ppermute x14, waiting for transfers between devices, around(): return lax.ppermute(x, axis, [(i, (i + distance) % n) for i in range(n)])  3.55 us
  transfers between devices with their start and end apart: 35, of which 15 were waited for; matrix products, arithmetic and copies ran while one was open for 1% of the time, Pallas kernels for 25%

profile of v13, /device:TPU:0, one launch (start us, length us, event | category | flops | bytes accessed | tf_op | source)
XLA Modules:
  0.0 101.4 jit_solution(17155657421956737500)
XLA Ops:
  3.3 4.9 %collective-permute-start = (bf16[128,256]{1,0:T(8,128)(2,1)S(1)}, bf16[128,256]{1,0:T(8,128)(2,1)S(1)}, u32[]{:S(2)}, u32[]{:S(2)}) collective-permute-start(bf16[128,256]{1,0:T(8,128)(2,1)S(1)} %get-tuple-element.126), channel_id=1, source_target_pairs={{0,4},{2,6},{5,9},{7,11},{8,12},{10,14},{16,20},{18,22},{21,25},{2... | collective-permute-start | bytes 196616 | tf_op jit(solution)/shard_map/ppermute | solution.py:424
  8.2 1.6 %collective-permute-start.3 = (bf16[128,256]{1,0:T(8,128)(2,1)S(1)}, bf16[128,256]{1,0:T(8,128)(2,1)S(1)}, u32[]{:S(2)}, u32[]{:S(2)}) collective-permute-start(bf16[128,256]{1,0:T(8,128)(2,1)S(1)} %get-tuple-element.133), channel_id=1, source_target_pairs={{0,2},{2,0},{1,3},{3,1},{4,6},{6,4},{5,7},{7,5},{8,10},{10,8},{9,1... | collective-permute-start | bytes 196616 | tf_op jit(solution)/shard_map/ppermute | solution.py:411
  11.8 1.6 %adjacency.1 = (bf16[768,768]{1,0:T(8,128)(2,1)S(1)}, bf16[768,768]{1,0:T(8,128)(2,1)S(1)}, bf16[768,256]{1,0:T(8,128)(2,1)S(1)}, bf16[256,768]{1,0:T(8,128)(2,1)S(1)}) custom-call(s32[4,6]{1,0:T(4,128)S(1)} %bitcast.4, bf16[6,4,128,128]{3,2,1,0:T(8,128)(2,1)S(1)} %copy-done.3, bf16[128,768]{1,0:T(8,128)(2,1)S(1)} %get-tuple-element.127.refs_2_, ...), custom_call_target="tpu_custom_call" | custom-call | flops 150994944 | bytes 4000000 | tf_op jit(solution)/shard_map/adjacency/pallas_call | solution.py:32
  15.8 2.8 %collective-permute-start.5 = (bf16[128,256]{1,0:T(8,128)(2,1)S(1)}, bf16[128,256]{1,0:T(8,128)(2,1)S(1)}, u32[]{:S(2)}, u32[]{:S(2)}) collective-permute-start(bf16[128,256]{1,0:T(8,128)(2,1)S(1)} %get-tuple-element.137), channel_id=1, source_target_pairs={{0,4},{2,6},{5,9},{7,11},{8,12},{10,14},{16,20},{18,22},{21,25},{2... | collective-permute-start | bytes 196616 | tf_op jit(solution)/shard_map/ppermute | solution.py:424
  19.1 1.6 %local1.1 = (bf16[768,256]{1,0:T(8,128)(2,1)S(1)}, bf16[768,512]{1,0:T(8,128)(2,1)S(1)}, bf16[768,512]{1,0:T(8,128)(2,1)S(1)}, bf16[512,768]{1,0:T(8,128)(2,1)S(1)}, bf16[256,768]{1,0:T(8,128)(2,1)S(1)}) custom-call(bf16[768,256]{1,0:T(8,128)(2,1)S(1)} %get-tuple-element.138.refs_0_, bf16[3,256,512]{2,1,0:T(8,128)(2,1)S(1)} %copy-done, ...), custom_call_target="tpu_custom_call" | custom-call | flops 805306368 | bytes 4000000 | tf_op jit(solution)/shard_map/local1/pallas_call | solution.py:32
  20.8 2.0 %collective-permute-done.6.refs_7_.refs_15_ = bf16[128,256]{1,0:T(8,128)(2,1)S(1)} collective-permute-done((bf16[128,256]{1,0:T(8,128)(2,1)S(1)}, bf16[128,256]{1,0:T(8,128)(2,1)S(1)}, u32[]{:S(2)}, u32[]{:S(2)}) %collective-permute-start.6) | collective-permute-done | bytes 65568 | tf_op jit(solution)/shard_map/ppermute | solution.py:411
  24.9 2.3 %collective-permute-start.8 = (bf16[128,256]{1,0:T(8,128)(2,1)S(1)}, bf16[128,256]{1,0:T(8,128)(2,1)S(1)}, u32[]{:S(2)}, u32[]{:S(2)}) collective-permute-start(bf16[128,256]{1,0:T(8,128)(2,1)S(1)} %get-tuple-element.144), channel_id=1, source_target_pairs={{0,4},{2,6},{5,9},{7,11},{8,12},{10,14},{16,20},{18,22},{21,25},{2... | collective-permute-start | bytes 196616 | tf_op jit(solution)/shard_map/ppermute | solution.py:424
  27.2 1.4 %collective-permute-start.9 = (bf16[128,256]{1,0:T(8,128)(2,1)S(1)}, bf16[128,256]{1,0:T(8,128)(2,1)S(1)}, u32[]{:S(2)}, u32[]{:S(2)}) collective-permute-start(bf16[128,256]{1,0:T(8,128)(2,1)S(1)} %get-tuple-element.148), channel_id=1, source_target_pairs={{0,2},{2,0},{1,3},{3,1},{4,6},{6,4},{5,7},{7,5},{8,10},{10,8},{9,1... | collective-permute-start | bytes 196616 | tf_op jit(solution)/shard_map/ppermute | solution.py:411
  28.6 1.6 %local2.1 = (bf16[768,256]{1,0:T(8,128)(2,1)S(1)}, bf16[768,512]{1,0:T(8,128)(2,1)S(1)}, bf16[768,512]{1,0:T(8,128)(2,1)S(1)}, bf16[512,768]{1,0:T(8,128)(2,1)S(1)}, bf16[256,768]{1,0:T(8,128)(2,1)S(1)}) custom-call(bf16[768,256]{1,0:T(8,128)(2,1)S(1)} %get-tuple-element.145.refs_0_, bf16[3,256,512]{2,1,0:T(8,128)(2,1)S(1)} %copy-done, ...), custom_call_target="tpu_custom_call" | custom-call | flops 805306368 | bytes 4000000 | tf_op jit(solution)/shard_map/local2/pallas_call | solution.py:32
  32.5 2.0 %turn.1 = (f32[768,256]{1,0:T(8,128)S(1)}, bf16[768,256]{1,0:T(8,128)(2,1)S(1)}, bf16[256,256]{1,0:T(8,128)(2,1)S(1)}, bf16[256,256]{1,0:T(8,128)(2,1)S(1)}, bf1...) custom-call(f32[768,256]{1,0:T(8,128)S(1)} %get-tuple-element.143.re, ...), custom_call_target="tpu_custom_call" | custom-call | flops 536870912 | bytes 4000000 | tf_op jit(solution)/shard_map/turn/pallas_call | solution.py:32
  34.5 1.3 %collective-permute-start.11 = (bf16[128,256]{1,0:T(8,128)(2,1)S(1)}, bf16[128,256]{1,0:T(8,128)(2,1)S(1)}, u32[]{:S(2)}, u32[]{:S(2)}) collective-permute-start(bf16[128,256]{1,0:T(8,128)(2,1)S(1)} %get-tuple-element.151), channel_id=1, source_target_pairs={{4,0},{6,2},{9,5},{11,7},{12,8},{14,10},{20,16},{22,18},{25,21},{2... | collective-permute-start | bytes 196616 | tf_op jit(solution)/shard_map/ppermute | solution.py:424
  35.8 1.4 %collective-permute-start.12 = (bf16[128,256]{1,0:T(8,128)(2,1)S(1)}, bf16[128,256]{1,0:T(8,128)(2,1)S(1)}, u32[]{:S(2)}, u32[]{:S(2)}) collective-permute-start(bf16[128,256]{1,0:T(8,128)(2,1)S(1)} %get-tuple-element.163), channel_id=1, source_target_pairs={{0,2},{2,0},{1,3},{3,1},{4,6},{6,4},{5,7},{7,5},{8,10},{10,8},{9,1... | collective-permute-start | bytes 196616 | tf_op jit(solution)/shard_map/ppermute | solution.py:411
  37.2 2.4 %back2.1 = (f32[768,256]{1,0:T(8,128)S(1)}, f32[2048,128]{1,0:T(8,128)S(1)}) custom-call(bf16[768,256]{1,0:T(8,128)(2,1)S(1)} %get-tuple-element.152.refs_0_, bf16[768,768]{1,0:T(8,128)(2,1)S(1)} %get-tuple-element.153.refs_1_.refs_2_, bf16[768,512]{1,0:T(8,128)(2,1)S(1)} %get-tuple-element.154.refs_2_, bf16[768,512]{1,0:T(8,128)(2,1)S(1)} %get-tuple-element.155.refs_3_, ...), custom_call_target="tpu_custom_call" | custom-call | flops 2717908992 | bytes 4000000 | tf_op jit(solution)/shard_map/back2/pallas_call | solution.py:32
  40.8 1.4 %collective-permute-start.16 = (bf16[1024,128]{1,0:T(8,128)(2,1)S(1)}, bf16[1024,128]{1,0:T(8,128)(2,1)S(1)}, u32[]{:S(2)}, u32[]{:S(2)}) collective-permute-start(bf16[1024,128]{1,0:T(8,128)(2,1)S(1)} %get-tuple-element.188), channel_id=1, source_target_pairs={{0,2},{1,5},{2,0},{3,7},{4,6},{5,1},{6,4},{7,3},{8,10},{9,13},{10,... | collective-permute-start | bytes 786440 | tf_op jit(solution)/shard_map/ppermute | solution.py:424
  42.1 1.5 %join2.1 = (f32[768,256]{1,0:T(8,128)S(1)}, bf16[768,256]{1,0:T(8,128)(2,1)S(1)}, bf16[256,256]{1,0:T(8,128)(2,1)S(1)}, bf16[256,256]{1,0:T(8,128)(2,1)S(1)}, bf...) custom-call(f32[1024,128]{1,0:T(8,128)S(1)} %get-tuple-element.168.r, ...), custom_call_target="tpu_custom_call" | custom-call | flops 536870912 | bytes 4000000 | tf_op jit(solution)/shard_map/join2/pallas_call | solution.py:32
  43.6 1.5 %collective-permute-start.14 = (bf16[128,256]{1,0:T(8,128)(2,1)S(1)}, bf16[128,256]{1,0:T(8,128)(2,1)S(1)}, u32[]{:S(2)}, u32[]{:S(2)}) collective-permute-start(bf16[128,256]{1,0:T(8,128)(2,1)S(1)} %get-tuple-element.171), channel_id=1, source_target_pairs={{4,0},{6,2},{9,5},{11,7},{12,8},{14,10},{20,16},{22,18},{25,21},{2... | collective-permute-start | bytes 196616 | tf_op jit(solution)/shard_map/ppermute | solution.py:424
  46.3 2.4 %back1.1 = (f32[768,256]{1,0:T(8,128)S(1)}, f32[2048,128]{1,0:T(8,128)S(1)}) custom-call(bf16[768,256]{1,0:T(8,128)(2,1)S(1)} %get-tuple-element.172.refs_0_.refs_1_, bf16[768,256]{1,0:T(8,128)(2,1)S(1)} %get-tuple-element.172.refs_0_.refs_1_, bf16[768,768]{1,0:T(8,128)(2,1)S(1)} %get-tuple-element.153.refs_1_.refs_2_, ...), custom_call_target="tpu_custom_call" | custom-call | flops 2717908992 | bytes 4000000 | tf_op jit(solution)/shard_map/back1/pallas_call | solution.py:32
  51.1 2.4 %collective-permute-start.18 = (bf16[512,128]{1,0:T(8,128)(2,1)S(1)}, bf16[512,128]{1,0:T(8,128)(2,1)S(1)}, u32[]{:S(2)}, u32[]{:S(2)}) collective-permute-start(bf16[512,128]{1,0:T(8,128)(2,1)S(1)} %get-tuple-element.201), channel_id=1, source_target_pairs={{0,4},{1,3},{2,6},{3,1},{4,0},{5,7},{6,2},{7,5},{8,12},{9,11},{10,... | collective-permute-start | bytes 393224 | tf_op jit(solution)/shard_map/ppermute | solution.py:424
  53.5 1.5 %join1.1 = (f32[768,256]{1,0:T(8,128)S(1)}, bf16[768,256]{1,0:T(8,128)(2,1)S(1)}, bf16[256,256]{1,0:T(8,128)(2,1)S(1)}, bf16[256,256]{1,0:T(8,128)(2,1)S(1)}, bf...) custom-call(f32[512,128]{1,0:T(8,128)S(1)} %get-tuple-element.189.re, ...), custom_call_target="tpu_custom_call" | custom-call | flops 536870912 | bytes 4000000 | tf_op jit(solution)/shard_map/join1/pallas_call | solution.py:32
  55.0 2.4 %back0.1 = (f32[768,256]{1,0:T(8,128)S(1)}, f32[2048,128]{1,0:T(8,128)S(1)}) custom-call(bf16[768,256]{1,0:T(8,128)(2,1)S(1)} %get-tuple-element.191.refs_0_.refs_1_, bf16[768,256]{1,0:T(8,128)(2,1)S(1)} %get-tuple-element.191.refs_0_.refs_1_, bf16[768,768]{1,0:T(8,128)(2,1)S(1)} %get-tuple-element.153.refs_1_.refs_2_, ...), custom_call_target="tpu_custom_call" | custom-call | flops 2717908992 | bytes 4000000 | tf_op jit(solution)/shard_map/back0/pallas_call | solution.py:32
  59.0 1.7 %collective-permute-start.21 = (bf16[512,128]{1,0:T(8,128)(2,1)S(1)}, bf16[512,128]{1,0:T(8,128)(2,1)S(1)}, u32[]{:S(2)}, u32[]{:S(2)}) collective-permute-start(bf16[512,128]{1,0:T(8,128)(2,1)S(1)} %get-tuple-element.209), channel_id=1, source_target_pairs={{0,8},{1,9},{2,10},{3,11},{4,12},{5,13},{6,14},{7,15},{8,0},{9,1},... | collective-permute-start | bytes 393224 | tf_op jit(solution)/shard_map/ppermute | solution.py:424
  60.8 1.3 %collective-permute-start.22 = (bf16[512,128]{1,0:T(8,128)(2,1)S(1)}, bf16[512,128]{1,0:T(8,128)(2,1)S(1)}, u32[]{:S(2)}, u32[]{:S(2)}) collective-permute-start(bf16[512,128]{1,0:T(8,128)(2,1)S(1)} %get-tuple-element.211), channel_id=1, source_target_pairs={{0,4},{1,3},{2,6},{3,1},{4,0},{5,7},{6,2},{7,5},{8,12},{9,11},{10,... | collective-permute-start | bytes 393224 | tf_op jit(solution)/shard_map/ppermute | solution.py:424
  62.1 3.6 %collective-permute-done.20.refs_2_ = bf16[1024,128]{1,0:T(8,128)(2,1)S(1)} collective-permute-done((bf16[1024,128]{1,0:T(8,128)(2,1)S(1)}, bf16[1024,128]{1,0:T(8,128)(2,1)S(1)}, u32[]{:S(2)}, u32[]{:S(2)}) %collective-permute-start.20) | collective-permute-done | bytes 262176 | tf_op jit(solution)/shard_map/ppermute | solution.py:424
  65.8 1.8 %collective-permute-start.23 = (bf16[512,128]{1,0:T(8,128)(2,1)S(1)}, bf16[512,128]{1,0:T(8,128)(2,1)S(1)}, u32[]{:S(2)}, u32[]{:S(2)}) collective-permute-start(bf16[512,128]{1,0:T(8,128)(2,1)S(1)} %get-tuple-element.213), channel_id=1, source_target_pairs={{0,4},{1,3},{2,6},{3,1},{4,0},{5,7},{6,2},{7,5},{8,12},{9,11},{10,... | collective-permute-start | bytes 393224 | tf_op jit(solution)/shard_map/ppermute | solution.py:424
  68.1 2.6 %collective-permute-start.25 = (bf16[512,128]{1,0:T(8,128)(2,1)S(1)}, bf16[512,128]{1,0:T(8,128)(2,1)S(1)}, u32[]{:S(2)}, u32[]{:S(2)}) collective-permute-start(bf16[512,128]{1,0:T(8,128)(2,1)S(1)} %get-tuple-element.217), channel_id=1, source_target_pairs={{0,8},{1,9},{2,10},{3,11},{4,12},{5,13},{6,14},{7,15},{8,0},{9,1},... | collective-permute-start | bytes 393224 | tf_op jit(solution)/shard_map/ppermute | solution.py:424
  71.3 2.5 %collective-permute-start.26 = (bf16[512,128]{1,0:T(8,128)(2,1)S(1)}, bf16[512,128]{1,0:T(8,128)(2,1)S(1)}, u32[]{:S(2)}, u32[]{:S(2)}) collective-permute-start(bf16[512,128]{1,0:T(8,128)(2,1)S(1)} %get-tuple-element.219), channel_id=1, source_target_pairs={{0,8},{1,9},{2,10},{3,11},{4,12},{5,13},{6,14},{7,15},{8,0},{9,1},... | collective-permute-start | bytes 393224 | tf_op jit(solution)/shard_map/ppermute | solution.py:424
  75.3 3.7 %collective-permute-done.25.refs_2_ = bf16[512,128]{1,0:T(8,128)(2,1)S(1)} collective-permute-done((bf16[512,128]{1,0:T(8,128)(2,1)S(1)}, bf16[512,128]{1,0:T(8,128)(2,1)S(1)}, u32[]{:S(2)}, u32[]{:S(2)}) %collective-permute-start.25) | collective-permute-done | bytes 131104 | tf_op jit(solution)/shard_map/ppermute | solution.py:424
  79.4 3.5 %collective-permute-done.26.refs_2_ = bf16[512,128]{1,0:T(8,128)(2,1)S(1)} collective-permute-done((bf16[512,128]{1,0:T(8,128)(2,1)S(1)}, bf16[512,128]{1,0:T(8,128)(2,1)S(1)}, u32[]{:S(2)}, u32[]{:S(2)}) %collective-permute-start.26) | collective-permute-done | bytes 131104 | tf_op jit(solution)/shard_map/ppermute | solution.py:424
  84.3 1.3 %collective-permute-start.32 = (bf16[1024,128]{1,0:T(8,128)(2,1)S(1)}, bf16[1024,128]{1,0:T(8,128)(2,1)S(1)}, u32[]{:S(2)}, u32[]{:S(2)}) collective-permute-start(bf16[1024,128]{1,0:T(8,128)(2,1)S(1)} %get-tuple-element.232), channel_id=1, source_target_pairs={{0,2},{1,5},{2,0},{3,7},{4,6},{5,1},{6,4},{7,3},{8,10},{9,13},{10,... | collective-permute-start | bytes 786440 | tf_op jit(solution)/shard_map/ppermute | solution.py:424
  85.6 3.7 %collective-permute-done.29.refs_3_ = bf16[512,128]{1,0:T(8,128)(2,1)S(1)} collective-permute-done((bf16[512,128]{1,0:T(8,128)(2,1)S(1)}, bf16[512,128]{1,0:T(8,128)(2,1)S(1)}, u32[]{:S(2)}, u32[]{:S(2)}) %collective-permute-start.29) | collective-permute-done | bytes 131104 | tf_op jit(solution)/shard_map/ppermute | solution.py:424
  93.9 2.8 %collective-permute-done.30.refs_4_ = bf16[128,256]{1,0:T(8,128)(2,1)S(1)} collective-permute-done((bf16[128,256]{1,0:T(8,128)(2,1)S(1)}, bf16[128,256]{1,0:T(8,128)(2,1)S(1)}, u32[]{:S(2)}, u32[]{:S(2)}) %collective-permute-start.30) | collective-permute-done | bytes 65568 | tf_op jit(solution)/shard_map/ppermute | solution.py:424
  99.8 1.4 %write0.3 = (f32[3,256,512]{2,1,0:T(8,128)}, f32[3,512,256]{2,1,0:T(8,128)}, f32[8,128]{1,0:T(8,128)}) custom-call(f32[3,256,512]{2,1,0:T(8,128)} %get-tuple-element.241.refs_0_, f32[3,512,256]{2,1,0:T(8,128)} %get-tuple-element.242.refs_1_, f32[8,128]{1,0:T(8,128)S(1)} %get-tuple-element.243.refs_2_, ...), custom_call_target="tpu_custom_call", output_to_operand_aliasing={{0}: (0, {}), {1}: (1, {})} | custom-call | flops 1 | bytes 1 | tf_op jit(solution)/shard_map/write0/pallas_call | solution.py:612
  (88 shorter events, 30.6 us)
Async XLA Ops:
  0.7 9.1 %collective-permute-start.1 = (bf16[3,256,512]{2,1,0:T(8,128)(2,1)}, bf16[3,256,512]{2,1,0:T(8,128)(2,1)S(1)}, u32[]{:S(2)}, u32[]{:S(2)}) collective-permute-start(bf16[3,256,512]{2,1,0:T(8,128)(2,1)} %refs_7_.5), channel_id=1, source_target_pairs={{0,1},{1,0},{2,3},{3,2},{4,5},{5,4},{6,7},{7,6},{8,9},{9,8},{10,11... | collective-permute-start | bytes 2359304 | tf_op jit(solution)/shard_map/ppermute | solution.py:411
  1.2 8.6 %collective-permute-start.2 = (bf16[3,512,256]{2,1,0:T(8,128)(2,1)}, bf16[3,512,256]{2,1,0:T(8,128)(2,1)S(1)}, u32[]{:S(2)}, u32[]{:S(2)}) collective-permute-start(bf16[3,512,256]{2,1,0:T(8,128)(2,1)} %refs_9_.3), channel_id=1, source_target_pairs={{0,1},{1,0},{2,3},{3,2},{4,5},{5,4},{6,7},{7,6},{8,9},{9,8},{10,11... | collective-permute-start | bytes 2359304 | tf_op jit(solution)/shard_map/ppermute | solution.py:411
  3.3 10.1 %collective-permute-start = (bf16[128,256]{1,0:T(8,128)(2,1)S(1)}, bf16[128,256]{1,0:T(8,128)(2,1)S(1)}, u32[]{:S(2)}, u32[]{:S(2)}) collective-permute-start(bf16[128,256]{1,0:T(8,128)(2,1)S(1)} %get-tuple-element.126), channel_id=1, source_target_pairs={{0,4},{2,6},{5,9},{7,11},{8,12},{10,14},{16,20},{18,22},{21,25},{2... | collective-permute-start | bytes 196616 | tf_op jit(solution)/shard_map/ppermute | solution.py:424
  8.2 5.2 %collective-permute-start.3 = (bf16[128,256]{1,0:T(8,128)(2,1)S(1)}, bf16[128,256]{1,0:T(8,128)(2,1)S(1)}, u32[]{:S(2)}, u32[]{:S(2)}) collective-permute-start(bf16[128,256]{1,0:T(8,128)(2,1)S(1)} %get-tuple-element.133), channel_id=1, source_target_pairs={{0,2},{2,0},{1,3},{3,1},{4,6},{6,4},{5,7},{7,5},{8,10},{10,8},{9,1... | collective-permute-start | bytes 196616 | tf_op jit(solution)/shard_map/ppermute | solution.py:411
  15.8 5.0 %collective-permute-start.5 = (bf16[128,256]{1,0:T(8,128)(2,1)S(1)}, bf16[128,256]{1,0:T(8,128)(2,1)S(1)}, u32[]{:S(2)}, u32[]{:S(2)}) collective-permute-start(bf16[128,256]{1,0:T(8,128)(2,1)S(1)} %get-tuple-element.137), channel_id=1, source_target_pairs={{0,4},{2,6},{5,9},{7,11},{8,12},{10,14},{16,20},{18,22},{21,25},{2... | collective-permute-start | bytes 196616 | tf_op jit(solution)/shard_map/ppermute | solution.py:424
  18.5 4.3 %collective-permute-start.6 = (bf16[128,256]{1,0:T(8,128)(2,1)S(1)}, bf16[128,256]{1,0:T(8,128)(2,1)S(1)}, u32[]{:S(2)}, u32[]{:S(2)}) collective-permute-start(bf16[128,256]{1,0:T(8,128)(2,1)S(1)} %get-tuple-element.141), channel_id=1, source_target_pairs={{0,2},{2,0},{1,3},{3,1},{4,6},{6,4},{5,7},{7,5},{8,10},{10,8},{9,1... | collective-permute-start | bytes 196616 | tf_op jit(solution)/shard_map/ppermute | solution.py:411
  20.8 3.1 %collective-permute-start.7 = (bf16[128,256]{1,0:T(8,128)(2,1)S(1)}, bf16[128,256]{1,0:T(8,128)(2,1)S(1)}, u32[]{:S(2)}, u32[]{:S(2)}) collective-permute-start(bf16[128,256]{1,0:T(8,128)(2,1)S(1)} %collective-permute-done.5.refs_8_.refs_13_), channel_id=1, source_target_pairs={{0,1},{1,0},{2,3},{3,2},{4,5},{5,4},{6,7},{7,6},{8,9},{9,8},{10,11... | collective-permute-start | bytes 196616 | tf_op jit(solution)/shard_map/ppermute | solution.py:411
  24.9 5.2 %collective-permute-start.8 = (bf16[128,256]{1,0:T(8,128)(2,1)S(1)}, bf16[128,256]{1,0:T(8,128)(2,1)S(1)}, u32[]{:S(2)}, u32[]{:S(2)}) collective-permute-start(bf16[128,256]{1,0:T(8,128)(2,1)S(1)} %get-tuple-element.144), channel_id=1, source_target_pairs={{0,4},{2,6},{5,9},{7,11},{8,12},{10,14},{16,20},{18,22},{21,25},{2... | collective-permute-start | bytes 196616 | tf_op jit(solution)/shard_map/ppermute | solution.py:424
  27.2 4.3 %collective-permute-start.9 = (bf16[128,256]{1,0:T(8,128)(2,1)S(1)}, bf16[128,256]{1,0:T(8,128)(2,1)S(1)}, u32[]{:S(2)}, u32[]{:S(2)}) collective-permute-start(bf16[128,256]{1,0:T(8,128)(2,1)S(1)} %get-tuple-element.148), channel_id=1, source_target_pairs={{0,2},{2,0},{1,3},{3,1},{4,6},{6,4},{5,7},{7,5},{8,10},{10,8},{9,1... | collective-permute-start | bytes 196616 | tf_op jit(solution)/shard_map/ppermute | solution.py:411
  30.2 2.3 %collective-permute-start.10 = (bf16[128,256]{1,0:T(8,128)(2,1)S(1)}, bf16[128,256]{1,0:T(8,128)(2,1)S(1)}, u32[]{:S(2)}, u32[]{:S(2)}) collective-permute-start(bf16[128,256]{1,0:T(8,128)(2,1)S(1)} %collective-permute-done.8.refs_9_), channel_id=1, source_target_pairs={{0,1},{1,0},{2,3},{3,2},{4,5},{5,4},{6,7},{7,6},{8,9},{9,8},{10,11... | collective-permute-start | bytes 196616 | tf_op jit(solution)/shard_map/ppermute | solution.py:411
  34.5 6.2 %collective-permute-start.11 = (bf16[128,256]{1,0:T(8,128)(2,1)S(1)}, bf16[128,256]{1,0:T(8,128)(2,1)S(1)}, u32[]{:S(2)}, u32[]{:S(2)}) collective-permute-start(bf16[128,256]{1,0:T(8,128)(2,1)S(1)} %get-tuple-element.151), channel_id=1, source_target_pairs={{4,0},{6,2},{9,5},{11,7},{12,8},{14,10},{20,16},{22,18},{25,21},{2... | collective-permute-start | bytes 196616 | tf_op jit(solution)/shard_map/ppermute | solution.py:424
  35.8 4.9 %collective-permute-start.12 = (bf16[128,256]{1,0:T(8,128)(2,1)S(1)}, bf16[128,256]{1,0:T(8,128)(2,1)S(1)}, u32[]{:S(2)}, u32[]{:S(2)}) collective-permute-start(bf16[128,256]{1,0:T(8,128)(2,1)S(1)} %get-tuple-element.163), channel_id=1, source_target_pairs={{0,2},{2,0},{1,3},{3,1},{4,6},{6,4},{5,7},{7,5},{8,10},{10,8},{9,1... | collective-permute-start | bytes 196616 | tf_op jit(solution)/shard_map/ppermute | solution.py:411
  40.8 10.3 %collective-permute-start.16 = (bf16[1024,128]{1,0:T(8,128)(2,1)S(1)}, bf16[1024,128]{1,0:T(8,128)(2,1)S(1)}, u32[]{:S(2)}, u32[]{:S(2)}) collective-permute-start(bf16[1024,128]{1,0:T(8,128)(2,1)S(1)} %get-tuple-element.188), channel_id=1, source_target_pairs={{0,2},{1,5},{2,0},{3,7},{4,6},{5,1},{6,4},{7,3},{8,10},{9,13},{10,... | collective-permute-start | bytes 786440 | tf_op jit(solution)/shard_map/ppermute | solution.py:424
  43.6 6.2 %collective-permute-start.14 = (bf16[128,256]{1,0:T(8,128)(2,1)S(1)}, bf16[128,256]{1,0:T(8,128)(2,1)S(1)}, u32[]{:S(2)}, u32[]{:S(2)}) collective-permute-start(bf16[128,256]{1,0:T(8,128)(2,1)S(1)} %get-tuple-element.171), channel_id=1, source_target_pairs={{4,0},{6,2},{9,5},{11,7},{12,8},{14,10},{20,16},{22,18},{25,21},{2... | collective-permute-start | bytes 196616 | tf_op jit(solution)/shard_map/ppermute | solution.py:424
  45.1 4.6 %collective-permute-start.15 = (bf16[128,256]{1,0:T(8,128)(2,1)S(1)}, bf16[128,256]{1,0:T(8,128)(2,1)S(1)}, u32[]{:S(2)}, u32[]{:S(2)}) collective-permute-start(bf16[128,256]{1,0:T(8,128)(2,1)S(1)} %get-tuple-element.182), channel_id=1, source_target_pairs={{0,2},{2,0},{1,3},{3,1},{4,6},{6,4},{5,7},{7,5},{8,10},{10,8},{9,1... | collective-permute-start | bytes 196616 | tf_op jit(solution)/shard_map/ppermute | solution.py:411
  49.8 3.8 %collective-permute-start.17 = (bf16[128,256]{1,0:T(8,128)(2,1)S(1)}, bf16[128,256]{1,0:T(8,128)(2,1)S(1)}, u32[]{:S(2)}, u32[]{:S(2)}) collective-permute-start(bf16[128,256]{1,0:T(8,128)(2,1)S(1)} %collective-permute-done.14.refs_1_.refs_10_), channel_id=1, source_target_pairs={{0,1},{1,0},{2,3},{3,2},{4,5},{5,4},{6,7},{7,6},{8,9},{9,8},{10,11... | collective-permute-start | bytes 196616 | tf_op jit(solution)/shard_map/ppermute | solution.py:411
  49.8 10.8 %collective-permute-start.19 = (bf16[1024,128]{1,0:T(8,128)(2,1)S(1)}, bf16[1024,128]{1,0:T(8,128)(2,1)S(1)}, u32[]{:S(2)}, u32[]{:S(2)}) collective-permute-start(bf16[1024,128]{1,0:T(8,128)(2,1)S(1)} %get-tuple-element.205), channel_id=1, source_target_pairs={{0,2},{1,5},{2,0},{3,7},{4,6},{5,1},{6,4},{7,3},{8,10},{9,13},{10,... | collective-permute-start | bytes 786440 | tf_op jit(solution)/shard_map/ppermute | solution.py:424
  51.1 6.7 %collective-permute-start.18 = (bf16[512,128]{1,0:T(8,128)(2,1)S(1)}, bf16[512,128]{1,0:T(8,128)(2,1)S(1)}, u32[]{:S(2)}, u32[]{:S(2)}) collective-permute-start(bf16[512,128]{1,0:T(8,128)(2,1)S(1)} %get-tuple-element.201), channel_id=1, source_target_pairs={{0,4},{1,3},{2,6},{3,1},{4,0},{5,7},{6,2},{7,5},{8,12},{9,11},{10,... | collective-permute-start | bytes 393224 | tf_op jit(solution)/shard_map/ppermute | solution.py:424
  57.9 7.8 %collective-permute-start.20 = (bf16[1024,128]{1,0:T(8,128)(2,1)S(1)}, bf16[1024,128]{1,0:T(8,128)(2,1)S(1)}, u32[]{:S(2)}, u32[]{:S(2)}) collective-permute-start(bf16[1024,128]{1,0:T(8,128)(2,1)S(1)} %get-tuple-element.207), channel_id=1, source_target_pairs={{0,2},{1,5},{2,0},{3,7},{4,6},{5,1},{6,4},{7,3},{8,10},{9,13},{10,... | collective-permute-start | bytes 786440 | tf_op jit(solution)/shard_map/ppermute | solution.py:424
  59.0 8.7 %collective-permute-start.21 = (bf16[512,128]{1,0:T(8,128)(2,1)S(1)}, bf16[512,128]{1,0:T(8,128)(2,1)S(1)}, u32[]{:S(2)}, u32[]{:S(2)}) collective-permute-start(bf16[512,128]{1,0:T(8,128)(2,1)S(1)} %get-tuple-element.209), channel_id=1, source_target_pairs={{0,8},{1,9},{2,10},{3,11},{4,12},{5,13},{6,14},{7,15},{8,0},{9,1},... | collective-permute-start | bytes 393224 | tf_op jit(solution)/shard_map/ppermute | solution.py:424
  60.8 7.3 %collective-permute-start.22 = (bf16[512,128]{1,0:T(8,128)(2,1)S(1)}, bf16[512,128]{1,0:T(8,128)(2,1)S(1)}, u32[]{:S(2)}, u32[]{:S(2)}) collective-permute-start(bf16[512,128]{1,0:T(8,128)(2,1)S(1)} %get-tuple-element.211), channel_id=1, source_target_pairs={{0,4},{1,3},{2,6},{3,1},{4,0},{5,7},{6,2},{7,5},{8,12},{9,11},{10,... | collective-permute-start | bytes 393224 | tf_op jit(solution)/shard_map/ppermute | solution.py:424
  65.8 5.4 %collective-permute-start.23 = (bf16[512,128]{1,0:T(8,128)(2,1)S(1)}, bf16[512,128]{1,0:T(8,128)(2,1)S(1)}, u32[]{:S(2)}, u32[]{:S(2)}) collective-permute-start(bf16[512,128]{1,0:T(8,128)(2,1)S(1)} %get-tuple-element.213), channel_id=1, source_target_pairs={{0,4},{1,3},{2,6},{3,1},{4,0},{5,7},{6,2},{7,5},{8,12},{9,11},{10,... | collective-permute-start | bytes 393224 | tf_op jit(solution)/shard_map/ppermute | solution.py:424
  67.8 6.2 %collective-permute-start.24 = (bf16[512,128]{1,0:T(8,128)(2,1)S(1)}, bf16[512,128]{1,0:T(8,128)(2,1)S(1)}, u32[]{:S(2)}, u32[]{:S(2)}) collective-permute-start(bf16[512,128]{1,0:T(8,128)(2,1)S(1)} %get-tuple-element.215), channel_id=1, source_target_pairs={{0,4},{1,3},{2,6},{3,1},{4,0},{5,7},{6,2},{7,5},{8,12},{9,11},{10,... | collective-permute-start | bytes 393224 | tf_op jit(solution)/shard_map/ppermute | solution.py:424
  68.1 10.9 %collective-permute-start.25 = (bf16[512,128]{1,0:T(8,128)(2,1)S(1)}, bf16[512,128]{1,0:T(8,128)(2,1)S(1)}, u32[]{:S(2)}, u32[]{:S(2)}) collective-permute-start(bf16[512,128]{1,0:T(8,128)(2,1)S(1)} %get-tuple-element.217), channel_id=1, source_target_pairs={{0,8},{1,9},{2,10},{3,11},{4,12},{5,13},{6,14},{7,15},{8,0},{9,1},... | collective-permute-start | bytes 393224 | tf_op jit(solution)/shard_map/ppermute | solution.py:424
  71.3 11.6 %collective-permute-start.26 = (bf16[512,128]{1,0:T(8,128)(2,1)S(1)}, bf16[512,128]{1,0:T(8,128)(2,1)S(1)}, u32[]{:S(2)}, u32[]{:S(2)}) collective-permute-start(bf16[512,128]{1,0:T(8,128)(2,1)S(1)} %get-tuple-element.219), channel_id=1, source_target_pairs={{0,8},{1,9},{2,10},{3,11},{4,12},{5,13},{6,14},{7,15},{8,0},{9,1},... | collective-permute-start | bytes 393224 | tf_op jit(solution)/shard_map/ppermute | solution.py:424
  74.1 11.5 %collective-permute-start.28 = (bf16[1024,128]{1,0:T(8,128)(2,1)S(1)}, bf16[1024,128]{1,0:T(8,128)(2,1)S(1)}, u32[]{:S(2)}, u32[]{:S(2)}) collective-permute-start(bf16[1024,128]{1,0:T(8,128)(2,1)S(1)} %get-tuple-element.223), channel_id=1, source_target_pairs={{0,2},{1,5},{2,0},{3,7},{4,6},{5,1},{6,4},{7,3},{8,10},{9,13},{10,... | collective-permute-start | bytes 786440 | tf_op jit(solution)/shard_map/ppermute | solution.py:424
  79.1 5.2 %collective-permute-start.27 = (bf16[512,128]{1,0:T(8,128)(2,1)S(1)}, bf16[512,128]{1,0:T(8,128)(2,1)S(1)}, u32[]{:S(2)}, u32[]{:S(2)}) collective-permute-start(bf16[512,128]{1,0:T(8,128)(2,1)S(1)} %get-tuple-element.221), channel_id=1, source_target_pairs={{0,4},{1,3},{2,6},{3,1},{4,0},{5,7},{6,2},{7,5},{8,12},{9,11},{10,... | collective-permute-start | bytes 393224 | tf_op jit(solution)/shard_map/ppermute | solution.py:424
  82.9 6.4 %collective-permute-start.29 = (bf16[512,128]{1,0:T(8,128)(2,1)S(1)}, bf16[512,128]{1,0:T(8,128)(2,1)S(1)}, u32[]{:S(2)}, u32[]{:S(2)}) collective-permute-start(bf16[512,128]{1,0:T(8,128)(2,1)S(1)} %get-tuple-element.224), channel_id=1, source_target_pairs={{0,4},{1,3},{2,6},{3,1},{4,0},{5,7},{6,2},{7,5},{8,12},{9,11},{10,... | collective-permute-start | bytes 393224 | tf_op jit(solution)/shard_map/ppermute | solution.py:424
  84.3 12.4 %collective-permute-start.32 = (bf16[1024,128]{1,0:T(8,128)(2,1)S(1)}, bf16[1024,128]{1,0:T(8,128)(2,1)S(1)}, u32[]{:S(2)}, u32[]{:S(2)}) collective-permute-start(bf16[1024,128]{1,0:T(8,128)(2,1)S(1)} %get-tuple-element.232), channel_id=1, source_target_pairs={{0,2},{1,5},{2,0},{3,7},{4,6},{5,1},{6,4},{7,3},{8,10},{9,13},{10,... | collective-permute-start | bytes 786440 | tf_op jit(solution)/shard_map/ppermute | solution.py:424
  89.4 10.4 %collective-permute-start.34 = (bf16[1024,128]{1,0:T(8,128)(2,1)S(1)}, bf16[1024,128]{1,0:T(8,128)(2,1)S(1)}, u32[]{:S(2)}, u32[]{:S(2)}) collective-permute-start(bf16[1024,128]{1,0:T(8,128)(2,1)S(1)} %get-tuple-element.244), channel_id=1, source_target_pairs={{0,2},{1,5},{2,0},{3,7},{4,6},{5,1},{6,4},{7,3},{8,10},{9,13},{10,... | collective-permute-start | bytes 786440 | tf_op jit(solution)/shard_map/ppermute | solution.py:424
  90.5 6.1 %collective-permute-start.30 = (bf16[128,256]{1,0:T(8,128)(2,1)S(1)}, bf16[128,256]{1,0:T(8,128)(2,1)S(1)}, u32[]{:S(2)}, u32[]{:S(2)}) collective-permute-start(bf16[128,256]{1,0:T(8,128)(2,1)S(1)} %get-tuple-element.228), channel_id=1, source_target_pairs={{4,0},{6,2},{9,5},{11,7},{12,8},{14,10},{20,16},{22,18},{25,21},{2... | collective-permute-start | bytes 196616 | tf_op jit(solution)/shard_map/ppermute | solution.py:424
  91.8 4.9 %collective-permute-start.31 = (bf16[128,256]{1,0:T(8,128)(2,1)S(1)}, bf16[128,256]{1,0:T(8,128)(2,1)S(1)}, u32[]{:S(2)}, u32[]{:S(2)}) collective-permute-start(bf16[128,256]{1,0:T(8,128)(2,1)S(1)} %get-tuple-element.230), channel_id=1, source_target_pairs={{0,2},{2,0},{1,3},{3,1},{4,6},{6,4},{5,7},{7,5},{8,10},{10,8},{9,1... | collective-permute-start | bytes 196616 | tf_op jit(solution)/shard_map/ppermute | solution.py:411
  (9 other events, 30.5 us)

commit v14 on v12

--- a/solution.py
+++ b/solution.py
@@ -557,7 +557,7 @@
     over_basin, over_chain = distances("basin"), distances("chain")
     n = len(over_basin)
     orders = over_basin + over_chain, over_chain[:n] + over_basin + over_chain[n:]
-    stages = list(zip(*orders[::-1], strict=True))
+    stages = list(zip(*orders, strict=True)), list(zip(*orders[::-1], strict=True))
     returned = {}
     sums = {}
 
@@ -575,7 +575,7 @@
             name=f"back{layer}",
             after=after,
         )
-        sums[layer] = Sum(whole, stages)
+        sums[layer] = Sum(whole, stages[layer % 2])
         return [outs[0], grad], [grad]
 
     def join(layer, state, after):
@@ -606,7 +606,7 @@
             functools.partial(
                 write_kernel,
                 layer,
-                stages[0],
+                stages[layer % 2][0],
                 len(kept),
                 [(at, i) for (_, at), i in zip(ready, which)],
             ),
@@ -628,19 +628,16 @@
             name=f"write{layer}",
         )(*written, *after, *[x for x, _ in ready])
 
-    count = 2 * len(stages) - 1
+    count = 2 * len(stages[0]) - 1
     at = []
     for layer in reversed(range(layers)):
         state, at = back(layer, outs, at)
-        arrived = [sums[above].got[0] for above in range(layer + 2, layers)]
         if layer:
-            arrived += returned[layer]
-        at = sum_step([sums[layer]], at + arrived)
-        if layer:
-            for above in range(layer + 1, layers):
-                at = sum_step([sums[above]], at)
+            at = sum_step([sums[i] for i in range(layer, layers)], at + returned[layer])
             outs = join(layer, state, at)
             at = outs[1:2]
+        else:
+            at = sum_step([sums[0]], at)
     while sums[0].done < count:
         for layer in reversed(range(layers)):
             if sums[layer].done < count:

time: 100 us -> 105 us (1.050)
  waiting for transfers between devices: 28.7 us -> 31.9 us
  starting transfers between devices: 37.7 us -> 38.8 us
    ppermute x18 -> x17, waiting for transfers between devices: 21.8 us -> 25.7 us  [over_mesh(): return lax.ppermute(x, ('chain', 'basin', 'feat'), perm)]
    ppermute x18 -> x17, starting transfers between devices: 25.3 us -> 27.4 us  [over_mesh(): return lax.ppermute(x, ('chain', 'basin', 'feat'), perm)]
    pallas_call x33 -> x32, Pallas kernels: 26.1 us -> 26.2 us  [call(): pl.pallas_call(lambda *refs: body(*refs[skipped:]), out_shape=[jax.ShapeD...]
  transfers between devices with their start and end apart: 32 -> 31, of which waited for: 15 -> 12; matrix products, arithmetic and copies ran while one was open for 1% -> 1% of each run, Pallas kernels for 25% -> 24%
where the time goes in v14:
time: 105 us
  starting transfers between devices  38.8 us (37%)
  waiting for transfers between devices  31.9 us (30%)
  Pallas kernels  30.6 us (29%)
  between operations  1.27 us (1%)
  local copies, waits for them, and re-layouts  1.2 us (1%)
    ppermute x17, starting transfers between devices, over_mesh(): return lax.ppermute(x, ('chain', 'basin', 'feat'), perm)  27.4 us
    pallas_call x32, Pallas kernels, call(): pl.pallas_call(lambda *refs: body(*refs[skipped:]), out_shape=[jax.ShapeD...  26.2 us
    ppermute x17, waiting for transfers between devices, over_mesh(): return lax.ppermute(x, ('chain', 'basin', 'feat'), perm)  25.7 us
    ppermute x11, starting transfers between devices, around(): return lax.ppermute(x, axis, [(i, (i + distance) % n) for i in range(n)])  7.33 us
    pallas_call x4, Pallas kernels, write(): pl.pallas_call(functools.partial(write_kernel, layer, stages[layer % 2][0...  4.42 us
    ppermute x3, starting transfers between devices, backward(): up = lax.ppermute(grads[0], 'chain', [(c, c - 1) for c in range(1, chain)])  4.08 us
    ppermute x11, waiting for transfers between devices, around(): return lax.ppermute(x, axis, [(i, (i + distance) % n) for i in range(n)])  3.54 us
    ppermute x3, waiting for transfers between devices, backward(): up = lax.ppermute(grads[0], 'chain', [(c, c - 1) for c in range(1, chain)])  2.59 us
  transfers between devices with their start and end apart: 31, of which 12 were waited for; matrix products, arithmetic and copies ran while one was open for 1% of the time, Pallas kernels for 24%

profile of v14, /device:TPU:0, one launch (start us, length us, event | category | flops | bytes accessed | tf_op | source)
XLA Modules:
  0.0 104.5 jit_solution(14814946439119243702)
XLA Ops:
  3.3 4.9 %collective-permute-start = (bf16[128,256]{1,0:T(8,128)(2,1)S(1)}, bf16[128,256]{1,0:T(8,128)(2,1)S(1)}, u32[]{:S(2)}, u32[]{:S(2)}) collective-permute-start(bf16[128,256]{1,0:T(8,128)(2,1)S(1)} %get-tuple-element.116), channel_id=1, source_target_pairs={{0,4},{2,6},{5,9},{7,11},{8,12},{10,14},{16,20},{18,22},{21,25},{2... | collective-permute-start | bytes 196616 | tf_op jit(solution)/shard_map/ppermute | solution.py:423
  8.2 1.6 %collective-permute-start.3 = (bf16[128,256]{1,0:T(8,128)(2,1)S(1)}, bf16[128,256]{1,0:T(8,128)(2,1)S(1)}, u32[]{:S(2)}, u32[]{:S(2)}) collective-permute-start(bf16[128,256]{1,0:T(8,128)(2,1)S(1)} %get-tuple-element.123), channel_id=1, source_target_pairs={{0,2},{2,0},{1,3},{3,1},{4,6},{6,4},{5,7},{7,5},{8,10},{10,8},{9,1... | collective-permute-start | bytes 196616 | tf_op jit(solution)/shard_map/ppermute | solution.py:410
  11.8 1.6 %adjacency.1 = (bf16[768,768]{1,0:T(8,128)(2,1)S(1)}, bf16[768,768]{1,0:T(8,128)(2,1)S(1)}, bf16[768,256]{1,0:T(8,128)(2,1)S(1)}, bf16[256,768]{1,0:T(8,128)(2,1)S(1)}) custom-call(s32[4,6]{1,0:T(4,128)S(1)} %bitcast.4, bf16[6,4,128,128]{3,2,1,0:T(8,128)(2,1)S(1)} %copy-done.3, bf16[128,768]{1,0:T(8,128)(2,1)S(1)} %get-tuple-element.117.refs_2_, ...), custom_call_target="tpu_custom_call" | custom-call | flops 150994944 | bytes 4000000 | tf_op jit(solution)/shard_map/adjacency/pallas_call | solution.py:32
  15.8 2.8 %collective-permute-start.5 = (bf16[128,256]{1,0:T(8,128)(2,1)S(1)}, bf16[128,256]{1,0:T(8,128)(2,1)S(1)}, u32[]{:S(2)}, u32[]{:S(2)}) collective-permute-start(bf16[128,256]{1,0:T(8,128)(2,1)S(1)} %get-tuple-element.127), channel_id=1, source_target_pairs={{0,4},{2,6},{5,9},{7,11},{8,12},{10,14},{16,20},{18,22},{21,25},{2... | collective-permute-start | bytes 196616 | tf_op jit(solution)/shard_map/ppermute | solution.py:423
  19.1 1.6 %local1.1 = (bf16[768,256]{1,0:T(8,128)(2,1)S(1)}, bf16[768,512]{1,0:T(8,128)(2,1)S(1)}, bf16[768,512]{1,0:T(8,128)(2,1)S(1)}, bf16[512,768]{1,0:T(8,128)(2,1)S(1)}, bf16[256,768]{1,0:T(8,128)(2,1)S(1)}) custom-call(bf16[768,256]{1,0:T(8,128)(2,1)S(1)} %get-tuple-element.128.refs_0_, bf16[3,256,512]{2,1,0:T(8,128)(2,1)S(1)} %copy-done, ...), custom_call_target="tpu_custom_call" | custom-call | flops 805306368 | bytes 4000000 | tf_op jit(solution)/shard_map/local1/pallas_call | solution.py:32
  20.8 2.0 %collective-permute-done.6.refs_7_.refs_14_ = bf16[128,256]{1,0:T(8,128)(2,1)S(1)} collective-permute-done((bf16[128,256]{1,0:T(8,128)(2,1)S(1)}, bf16[128,256]{1,0:T(8,128)(2,1)S(1)}, u32[]{:S(2)}, u32[]{:S(2)}) %collective-permute-start.6) | collective-permute-done | bytes 65568 | tf_op jit(solution)/shard_map/ppermute | solution.py:410
  24.9 2.3 %collective-permute-start.8 = (bf16[128,256]{1,0:T(8,128)(2,1)S(1)}, bf16[128,256]{1,0:T(8,128)(2,1)S(1)}, u32[]{:S(2)}, u32[]{:S(2)}) collective-permute-start(bf16[128,256]{1,0:T(8,128)(2,1)S(1)} %get-tuple-element.134), channel_id=1, source_target_pairs={{0,4},{2,6},{5,9},{7,11},{8,12},{10,14},{16,20},{18,22},{21,25},{2... | collective-permute-start | bytes 196616 | tf_op jit(solution)/shard_map/ppermute | solution.py:423
  27.2 1.4 %collective-permute-start.9 = (bf16[128,256]{1,0:T(8,128)(2,1)S(1)}, bf16[128,256]{1,0:T(8,128)(2,1)S(1)}, u32[]{:S(2)}, u32[]{:S(2)}) collective-permute-start(bf16[128,256]{1,0:T(8,128)(2,1)S(1)} %get-tuple-element.138), channel_id=1, source_target_pairs={{0,2},{2,0},{1,3},{3,1},{4,6},{6,4},{5,7},{7,5},{8,10},{10,8},{9,1... | collective-permute-start | bytes 196616 | tf_op jit(solution)/shard_map/ppermute | solution.py:410
  28.6 1.6 %local2.1 = (bf16[768,256]{1,0:T(8,128)(2,1)S(1)}, bf16[768,512]{1,0:T(8,128)(2,1)S(1)}, bf16[768,512]{1,0:T(8,128)(2,1)S(1)}, bf16[512,768]{1,0:T(8,128)(2,1)S(1)}, bf16[256,768]{1,0:T(8,128)(2,1)S(1)}) custom-call(bf16[768,256]{1,0:T(8,128)(2,1)S(1)} %get-tuple-element.135.refs_0_, bf16[3,256,512]{2,1,0:T(8,128)(2,1)S(1)} %copy-done, ...), custom_call_target="tpu_custom_call" | custom-call | flops 805306368 | bytes 4000000 | tf_op jit(solution)/shard_map/local2/pallas_call | solution.py:32
  32.5 2.0 %turn.1 = (f32[768,256]{1,0:T(8,128)S(1)}, bf16[768,256]{1,0:T(8,128)(2,1)S(1)}, bf16[256,256]{1,0:T(8,128)(2,1)S(1)}, bf16[256,256]{1,0:T(8,128)(2,1)S(1)}, bf1...) custom-call(f32[768,256]{1,0:T(8,128)S(1)} %get-tuple-element.133.re, ...), custom_call_target="tpu_custom_call" | custom-call | flops 536870912 | bytes 4000000 | tf_op jit(solution)/shard_map/turn/pallas_call | solution.py:32
  34.5 1.3 %collective-permute-start.11 = (bf16[128,256]{1,0:T(8,128)(2,1)S(1)}, bf16[128,256]{1,0:T(8,128)(2,1)S(1)}, u32[]{:S(2)}, u32[]{:S(2)}) collective-permute-start(bf16[128,256]{1,0:T(8,128)(2,1)S(1)} %get-tuple-element.152), channel_id=1, source_target_pairs={{4,0},{8,4},{12,8},{5,1},{9,5},{13,9},{6,2},{10,6},{14,10},{7,3},{... | collective-permute-start | bytes 196616 | tf_op jit(solution)/shard_map/ppermute | solution.py:446
  35.8 1.4 %collective-permute-start.12 = (bf16[128,256]{1,0:T(8,128)(2,1)S(1)}, bf16[128,256]{1,0:T(8,128)(2,1)S(1)}, u32[]{:S(2)}, u32[]{:S(2)}) collective-permute-start(bf16[128,256]{1,0:T(8,128)(2,1)S(1)} %get-tuple-element.153), channel_id=1, source_target_pairs={{0,2},{2,0},{1,3},{3,1},{4,6},{6,4},{5,7},{7,5},{8,10},{10,8},{9,1... | collective-permute-start | bytes 196616 | tf_op jit(solution)/shard_map/ppermute | solution.py:410
  37.2 2.4 %back2.1 = (f32[768,256]{1,0:T(8,128)S(1)}, f32[2048,128]{1,0:T(8,128)S(1)}) custom-call(bf16[768,256]{1,0:T(8,128)(2,1)S(1)} %get-tuple-element.141.refs_0_, bf16[768,768]{1,0:T(8,128)(2,1)S(1)} %get-tuple-element.142.refs_1_.refs_2_, bf16[768,512]{1,0:T(8,128)(2,1)S(1)} %get-tuple-element.143.refs_2_, bf16[768,512]{1,0:T(8,128)(2,1)S(1)} %get-tuple-element.144.refs_3_, ...), custom_call_target="tpu_custom_call" | custom-call | flops 2717908992 | bytes 4000000 | tf_op jit(solution)/shard_map/back2/pallas_call | solution.py:32
  40.8 1.4 %collective-permute-start.15 = (bf16[1024,128]{1,0:T(8,128)(2,1)S(1)}, bf16[1024,128]{1,0:T(8,128)(2,1)S(1)}, u32[]{:S(2)}, u32[]{:S(2)}) collective-permute-start(bf16[1024,128]{1,0:T(8,128)(2,1)S(1)} %get-tuple-element.171), channel_id=1, source_target_pairs={{0,2},{1,5},{2,0},{3,7},{4,6},{5,1},{6,4},{7,3},{8,10},{9,13},{10,... | collective-permute-start | bytes 786440 | tf_op jit(solution)/shard_map/ppermute | solution.py:423
  42.1 1.5 %join2.1 = (f32[768,256]{1,0:T(8,128)S(1)}, bf16[768,256]{1,0:T(8,128)(2,1)S(1)}, bf16[256,256]{1,0:T(8,128)(2,1)S(1)}, bf16[256,256]{1,0:T(8,128)(2,1)S(1)}, bf...) custom-call(f32[1024,128]{1,0:T(8,128)S(1)} %get-tuple-element.155.r, ...), custom_call_target="tpu_custom_call" | custom-call | flops 536870912 | bytes 4000000 | tf_op jit(solution)/shard_map/join2/pallas_call | solution.py:32
  43.6 1.5 %collective-permute-start.13 = (bf16[128,256]{1,0:T(8,128)(2,1)S(1)}, bf16[128,256]{1,0:T(8,128)(2,1)S(1)}, u32[]{:S(2)}, u32[]{:S(2)}) collective-permute-start(bf16[128,256]{1,0:T(8,128)(2,1)S(1)} %get-tuple-element.168), channel_id=1, source_target_pairs={{4,0},{8,4},{12,8},{5,1},{9,5},{13,9},{6,2},{10,6},{14,10},{7,3},{... | collective-permute-start | bytes 196616 | tf_op jit(solution)/shard_map/ppermute | solution.py:446
  45.9 2.4 %back1.1 = (f32[768,256]{1,0:T(8,128)S(1)}, f32[2048,128]{1,0:T(8,128)S(1)}) custom-call(bf16[768,256]{1,0:T(8,128)(2,1)S(1)} %get-tuple-element.158.refs_0_.refs_1_, bf16[768,256]{1,0:T(8,128)(2,1)S(1)} %get-tuple-element.158.refs_0_.refs_1_, bf16[768,768]{1,0:T(8,128)(2,1)S(1)} %get-tuple-element.142.refs_1_.refs_2_, ...), custom_call_target="tpu_custom_call" | custom-call | flops 2717908992 | bytes 4000000 | tf_op jit(solution)/shard_map/back1/pallas_call | solution.py:32
  48.3 1.5 %collective-permute-done.13.refs_1_.refs_10_ = bf16[128,256]{1,0:T(8,128)(2,1)S(1)} collective-permute-done((bf16[128,256]{1,0:T(8,128)(2,1)S(1)}, bf16[128,256]{1,0:T(8,128)(2,1)S(1)}, u32[]{:S(2)}, u32[]{:S(2)}) %collective-permute-start.13) | collective-permute-done | bytes 65568 | tf_op jit(solution)/shard_map/ppermute | solution.py:446
  50.0 2.4 %collective-permute-start.16 = (bf16[1536,128]{1,0:T(8,128)(2,1)S(1)}, bf16[1536,128]{1,0:T(8,128)(2,1)S(1)}, u32[]{:S(2)}, u32[]{:S(2)}) collective-permute-start(bf16[1536,128]{1,0:T(8,128)(2,1)S(1)} %get-tuple-element.187), channel_id=1, source_target_pairs={{0,4},{1,3},{2,6},{3,1},{4,0},{5,7},{6,2},{7,5},{8,12},{9,11},{10,... | collective-permute-start | bytes 1179656 | tf_op jit(solution)/shard_map/ppermute | solution.py:423
  52.4 1.5 %join1.1 = (f32[768,256]{1,0:T(8,128)S(1)}, bf16[768,256]{1,0:T(8,128)(2,1)S(1)}, bf16[256,256]{1,0:T(8,128)(2,1)S(1)}, bf16[256,256]{1,0:T(8,128)(2,1)S(1)}, bf...) custom-call(f32[1024,128]{1,0:T(8,128)S(1)} %get-tuple-element.172.r, ...), custom_call_target="tpu_custom_call" | custom-call | flops 536870912 | bytes 4000000 | tf_op jit(solution)/shard_map/join1/pallas_call | solution.py:32
  53.9 2.4 %back0.1 = (f32[768,256]{1,0:T(8,128)S(1)}, f32[2048,128]{1,0:T(8,128)S(1)}) custom-call(bf16[768,256]{1,0:T(8,128)(2,1)S(1)} %get-tuple-element.174.refs_0_.refs_1_, bf16[768,256]{1,0:T(8,128)(2,1)S(1)} %get-tuple-element.174.refs_0_.refs_1_, bf16[768,768]{1,0:T(8,128)(2,1)S(1)} %get-tuple-element.142.refs_1_.refs_2_, ...), custom_call_target="tpu_custom_call" | custom-call | flops 2717908992 | bytes 4000000 | tf_op jit(solution)/shard_map/back0/pallas_call | solution.py:32
  57.2 4.5 %collective-permute-done.16.refs_2_ = bf16[1536,128]{1,0:T(8,128)(2,1)S(1)} collective-permute-done((bf16[1536,128]{1,0:T(8,128)(2,1)S(1)}, bf16[1536,128]{1,0:T(8,128)(2,1)S(1)}, u32[]{:S(2)}, u32[]{:S(2)}) %collective-permute-start.16) | collective-permute-done | bytes 393248 | tf_op jit(solution)/shard_map/ppermute | solution.py:423
  61.7 4.9 %collective-permute-start.18 = (bf16[512,128]{1,0:T(8,128)(2,1)S(1)}, bf16[512,128]{1,0:T(8,128)(2,1)S(1)}, u32[]{:S(2)}, u32[]{:S(2)}) collective-permute-start(bf16[512,128]{1,0:T(8,128)(2,1)S(1)} %get-tuple-element.192), channel_id=1, source_target_pairs={{0,8},{1,9},{2,10},{3,11},{4,12},{5,13},{6,14},{7,15},{8,0},{9,1},... | collective-permute-start | bytes 393224 | tf_op jit(solution)/shard_map/ppermute | solution.py:423
  68.2 7.0 %collective-permute-done.18.refs_2_ = bf16[512,128]{1,0:T(8,128)(2,1)S(1)} collective-permute-done((bf16[512,128]{1,0:T(8,128)(2,1)S(1)}, bf16[512,128]{1,0:T(8,128)(2,1)S(1)}, u32[]{:S(2)}, u32[]{:S(2)}) %collective-permute-start.18) | collective-permute-done | bytes 131104 | tf_op jit(solution)/shard_map/ppermute | solution.py:423
  75.6 3.5 %collective-permute-start.22 = (bf16[512,128]{1,0:T(8,128)(2,1)S(1)}, bf16[512,128]{1,0:T(8,128)(2,1)S(1)}, u32[]{:S(2)}, u32[]{:S(2)}) collective-permute-start(bf16[512,128]{1,0:T(8,128)(2,1)S(1)} %get-tuple-element.200), channel_id=1, source_target_pairs={{0,8},{1,9},{2,10},{3,11},{4,12},{5,13},{6,14},{7,15},{8,0},{9,1},... | collective-permute-start | bytes 393224 | tf_op jit(solution)/shard_map/ppermute | solution.py:423
  79.2 3.5 %collective-permute-done.21.refs_2_ = bf16[512,128]{1,0:T(8,128)(2,1)S(1)} collective-permute-done((bf16[512,128]{1,0:T(8,128)(2,1)S(1)}, bf16[512,128]{1,0:T(8,128)(2,1)S(1)}, u32[]{:S(2)}, u32[]{:S(2)}) %collective-permute-start.21) | collective-permute-done | bytes 131104 | tf_op jit(solution)/shard_map/ppermute | solution.py:423
  82.8 1.3 %collective-permute-start.25 = (bf16[1024,128]{1,0:T(8,128)(2,1)S(1)}, bf16[1024,128]{1,0:T(8,128)(2,1)S(1)}, u32[]{:S(2)}, u32[]{:S(2)}) collective-permute-start(bf16[1024,128]{1,0:T(8,128)(2,1)S(1)} %get-tuple-element.206), channel_id=1, source_target_pairs={{0,2},{1,5},{2,0},{3,7},{4,6},{5,1},{6,4},{7,3},{8,10},{9,13},{10,... | collective-permute-start | bytes 786440 | tf_op jit(solution)/shard_map/ppermute | solution.py:423
  86.4 6.9 %collective-permute-done.24.refs_2_ = bf16[512,128]{1,0:T(8,128)(2,1)S(1)} collective-permute-done((bf16[512,128]{1,0:T(8,128)(2,1)S(1)}, bf16[512,128]{1,0:T(8,128)(2,1)S(1)}, u32[]{:S(2)}, u32[]{:S(2)}) %collective-permute-start.24) | collective-permute-done | bytes 131104 | tf_op jit(solution)/shard_map/ppermute | solution.py:423
  93.5 1.3 %collective-permute-start.30 = (bf16[1024,128]{1,0:T(8,128)(2,1)S(1)}, bf16[1024,128]{1,0:T(8,128)(2,1)S(1)}, u32[]{:S(2)}, u32[]{:S(2)}) collective-permute-start(bf16[1024,128]{1,0:T(8,128)(2,1)S(1)} %get-tuple-element.224), channel_id=1, source_target_pairs={{0,2},{1,5},{2,0},{3,7},{4,6},{5,1},{6,4},{7,3},{8,10},{9,13},{10,... | collective-permute-start | bytes 786440 | tf_op jit(solution)/shard_map/ppermute | solution.py:423
  94.8 1.3 %collective-permute-start.28 = (bf16[128,256]{1,0:T(8,128)(2,1)S(1)}, bf16[128,256]{1,0:T(8,128)(2,1)S(1)}, u32[]{:S(2)}, u32[]{:S(2)}) collective-permute-start(bf16[128,256]{1,0:T(8,128)(2,1)S(1)} %get-tuple-element.218), channel_id=1, source_target_pairs={{4,0},{8,4},{12,8},{5,1},{9,5},{13,9},{6,2},{10,6},{14,10},{7,3},{... | collective-permute-start | bytes 196616 | tf_op jit(solution)/shard_map/ppermute | solution.py:446
  98.0 1.8 %collective-permute-done.27.refs_4_ = bf16[1024,128]{1,0:T(8,128)(2,1)S(1)} collective-permute-done((bf16[1024,128]{1,0:T(8,128)(2,1)S(1)}, bf16[1024,128]{1,0:T(8,128)(2,1)S(1)}, u32[]{:S(2)}, u32[]{:S(2)}) %collective-permute-start.27) | collective-permute-done | bytes 262176 | tf_op jit(solution)/shard_map/ppermute | solution.py:423
  102.9 1.4 %write0.3 = (f32[3,256,512]{2,1,0:T(8,128)}, f32[3,512,256]{2,1,0:T(8,128)}, f32[8,128]{1,0:T(8,128)}) custom-call(f32[3,256,512]{2,1,0:T(8,128)} %get-tuple-element.221.refs_0_, f32[3,512,256]{2,1,0:T(8,128)} %get-tuple-element.222.refs_1_, f32[8,128]{1,0:T(8,128)S(1)} %get-tuple-element.223.refs_2_, ...), custom_call_target="tpu_custom_call", output_to_operand_aliasing={{0}: (0, {}), {1}: (1, {})} | custom-call | flops 1 | bytes 1 | tf_op jit(solution)/shard_map/write0/pallas_call | solution.py:605
  (79 shorter events, 24.5 us)
Async XLA Ops:
  0.6 10.1 %copy-start = (bf16[3,256,512]{2,1,0:T(8,128)(2,1)S(1)}, bf16[3,256,512]{2,1,0:T(8,128)(2,1)}, u32[]{:S(2)}) copy-start(bf16[3,256,512]{2,1,0:T(8,128)(2,1)} %refs_7_.5) | copy-start | bytes 2359300
  0.7 9.1 %collective-permute-start.1 = (bf16[3,256,512]{2,1,0:T(8,128)(2,1)}, bf16[3,256,512]{2,1,0:T(8,128)(2,1)S(1)}, u32[]{:S(2)}, u32[]{:S(2)}) collective-permute-start(bf16[3,256,512]{2,1,0:T(8,128)(2,1)} %refs_7_.5), channel_id=1, source_target_pairs={{0,1},{1,0},{2,3},{3,2},{4,5},{5,4},{6,7},{7,6},{8,9},{9,8},{10,11... | collective-permute-start | bytes 2359304 | tf_op jit(solution)/shard_map/ppermute | solution.py:410
  1.2 8.6 %collective-permute-start.2 = (bf16[3,512,256]{2,1,0:T(8,128)(2,1)}, bf16[3,512,256]{2,1,0:T(8,128)(2,1)S(1)}, u32[]{:S(2)}, u32[]{:S(2)}) collective-permute-start(bf16[3,512,256]{2,1,0:T(8,128)(2,1)} %refs_9_.3), channel_id=1, source_target_pairs={{0,1},{1,0},{2,3},{3,2},{4,5},{5,4},{6,7},{7,6},{8,9},{9,8},{10,11... | collective-permute-start | bytes 2359304 | tf_op jit(solution)/shard_map/ppermute | solution.py:410
  3.3 10.1 %collective-permute-start = (bf16[128,256]{1,0:T(8,128)(2,1)S(1)}, bf16[128,256]{1,0:T(8,128)(2,1)S(1)}, u32[]{:S(2)}, u32[]{:S(2)}) collective-permute-start(bf16[128,256]{1,0:T(8,128)(2,1)S(1)} %get-tuple-element.116), channel_id=1, source_target_pairs={{0,4},{2,6},{5,9},{7,11},{8,12},{10,14},{16,20},{18,22},{21,25},{2... | collective-permute-start | bytes 196616 | tf_op jit(solution)/shard_map/ppermute | solution.py:423
  8.2 5.2 %collective-permute-start.3 = (bf16[128,256]{1,0:T(8,128)(2,1)S(1)}, bf16[128,256]{1,0:T(8,128)(2,1)S(1)}, u32[]{:S(2)}, u32[]{:S(2)}) collective-permute-start(bf16[128,256]{1,0:T(8,128)(2,1)S(1)} %get-tuple-element.123), channel_id=1, source_target_pairs={{0,2},{2,0},{1,3},{3,1},{4,6},{6,4},{5,7},{7,5},{8,10},{10,8},{9,1... | collective-permute-start | bytes 196616 | tf_op jit(solution)/shard_map/ppermute | solution.py:410
  13.4 1.3 %collective-permute-start.4 = (bf16[128,256]{1,0:T(8,128)(2,1)S(1)}, bf16[128,256]{1,0:T(8,128)(2,1)S(1)}, u32[]{:S(2)}, u32[]{:S(2)}) collective-permute-start(bf16[128,256]{1,0:T(8,128)(2,1)S(1)} %collective-permute-done.refs_8_.refs_12_), channel_id=1, source_target_pairs={{0,1},{1,0},{2,3},{3,2},{4,5},{5,4},{6,7},{7,6},{8,9},{9,8},{10,11... | collective-permute-start | bytes 196616 | tf_op jit(solution)/shard_map/ppermute | solution.py:410
  15.8 5.0 %collective-permute-start.5 = (bf16[128,256]{1,0:T(8,128)(2,1)S(1)}, bf16[128,256]{1,0:T(8,128)(2,1)S(1)}, u32[]{:S(2)}, u32[]{:S(2)}) collective-permute-start(bf16[128,256]{1,0:T(8,128)(2,1)S(1)} %get-tuple-element.127), channel_id=1, source_target_pairs={{0,4},{2,6},{5,9},{7,11},{8,12},{10,14},{16,20},{18,22},{21,25},{2... | collective-permute-start | bytes 196616 | tf_op jit(solution)/shard_map/ppermute | solution.py:423
  18.5 4.3 %collective-permute-start.6 = (bf16[128,256]{1,0:T(8,128)(2,1)S(1)}, bf16[128,256]{1,0:T(8,128)(2,1)S(1)}, u32[]{:S(2)}, u32[]{:S(2)}) collective-permute-start(bf16[128,256]{1,0:T(8,128)(2,1)S(1)} %get-tuple-element.131), channel_id=1, source_target_pairs={{0,2},{2,0},{1,3},{3,1},{4,6},{6,4},{5,7},{7,5},{8,10},{10,8},{9,1... | collective-permute-start | bytes 196616 | tf_op jit(solution)/shard_map/ppermute | solution.py:410
  20.8 3.1 %collective-permute-start.7 = (bf16[128,256]{1,0:T(8,128)(2,1)S(1)}, bf16[128,256]{1,0:T(8,128)(2,1)S(1)}, u32[]{:S(2)}, u32[]{:S(2)}) collective-permute-start(bf16[128,256]{1,0:T(8,128)(2,1)S(1)} %collective-permute-done.5.refs_8_.refs_12_), channel_id=1, source_target_pairs={{0,1},{1,0},{2,3},{3,2},{4,5},{5,4},{6,7},{7,6},{8,9},{9,8},{10,11... | collective-permute-start | bytes 196616 | tf_op jit(solution)/shard_map/ppermute | solution.py:410
  24.9 5.2 %collective-permute-start.8 = (bf16[128,256]{1,0:T(8,128)(2,1)S(1)}, bf16[128,256]{1,0:T(8,128)(2,1)S(1)}, u32[]{:S(2)}, u32[]{:S(2)}) collective-permute-start(bf16[128,256]{1,0:T(8,128)(2,1)S(1)} %get-tuple-element.134), channel_id=1, source_target_pairs={{0,4},{2,6},{5,9},{7,11},{8,12},{10,14},{16,20},{18,22},{21,25},{2... | collective-permute-start | bytes 196616 | tf_op jit(solution)/shard_map/ppermute | solution.py:423
  27.2 4.3 %collective-permute-start.9 = (bf16[128,256]{1,0:T(8,128)(2,1)S(1)}, bf16[128,256]{1,0:T(8,128)(2,1)S(1)}, u32[]{:S(2)}, u32[]{:S(2)}) collective-permute-start(bf16[128,256]{1,0:T(8,128)(2,1)S(1)} %get-tuple-element.138), channel_id=1, source_target_pairs={{0,2},{2,0},{1,3},{3,1},{4,6},{6,4},{5,7},{7,5},{8,10},{10,8},{9,1... | collective-permute-start | bytes 196616 | tf_op jit(solution)/shard_map/ppermute | solution.py:410
  30.2 2.3 %collective-permute-start.10 = (bf16[128,256]{1,0:T(8,128)(2,1)S(1)}, bf16[128,256]{1,0:T(8,128)(2,1)S(1)}, u32[]{:S(2)}, u32[]{:S(2)}) collective-permute-start(bf16[128,256]{1,0:T(8,128)(2,1)S(1)} %collective-permute-done.8.refs_9_), channel_id=1, source_target_pairs={{0,1},{1,0},{2,3},{3,2},{4,5},{5,4},{6,7},{7,6},{8,9},{9,8},{10,11... | collective-permute-start | bytes 196616 | tf_op jit(solution)/shard_map/ppermute | solution.py:410
  34.5 6.2 %collective-permute-start.11 = (bf16[128,256]{1,0:T(8,128)(2,1)S(1)}, bf16[128,256]{1,0:T(8,128)(2,1)S(1)}, u32[]{:S(2)}, u32[]{:S(2)}) collective-permute-start(bf16[128,256]{1,0:T(8,128)(2,1)S(1)} %get-tuple-element.152), channel_id=1, source_target_pairs={{4,0},{8,4},{12,8},{5,1},{9,5},{13,9},{6,2},{10,6},{14,10},{7,3},{... | collective-permute-start | bytes 196616 | tf_op jit(solution)/shard_map/ppermute | solution.py:446
  35.8 4.9 %collective-permute-start.12 = (bf16[128,256]{1,0:T(8,128)(2,1)S(1)}, bf16[128,256]{1,0:T(8,128)(2,1)S(1)}, u32[]{:S(2)}, u32[]{:S(2)}) collective-permute-start(bf16[128,256]{1,0:T(8,128)(2,1)S(1)} %get-tuple-element.153), channel_id=1, source_target_pairs={{0,2},{2,0},{1,3},{3,1},{4,6},{6,4},{5,7},{7,5},{8,10},{10,8},{9,1... | collective-permute-start | bytes 196616 | tf_op jit(solution)/shard_map/ppermute | solution.py:410
  40.8 9.1 %collective-permute-start.15 = (bf16[1024,128]{1,0:T(8,128)(2,1)S(1)}, bf16[1024,128]{1,0:T(8,128)(2,1)S(1)}, u32[]{:S(2)}, u32[]{:S(2)}) collective-permute-start(bf16[1024,128]{1,0:T(8,128)(2,1)S(1)} %get-tuple-element.171), channel_id=1, source_target_pairs={{0,2},{1,5},{2,0},{3,7},{4,6},{5,1},{6,4},{7,3},{8,10},{9,13},{10,... | collective-permute-start | bytes 786440 | tf_op jit(solution)/shard_map/ppermute | solution.py:423
  43.6 6.3 %collective-permute-start.13 = (bf16[128,256]{1,0:T(8,128)(2,1)S(1)}, bf16[128,256]{1,0:T(8,128)(2,1)S(1)}, u32[]{:S(2)}, u32[]{:S(2)}) collective-permute-start(bf16[128,256]{1,0:T(8,128)(2,1)S(1)} %get-tuple-element.168), channel_id=1, source_target_pairs={{4,0},{8,4},{12,8},{5,1},{9,5},{13,9},{6,2},{10,6},{14,10},{7,3},{... | collective-permute-start | bytes 196616 | tf_op jit(solution)/shard_map/ppermute | solution.py:446
  45.1 4.7 %collective-permute-start.14 = (bf16[128,256]{1,0:T(8,128)(2,1)S(1)}, bf16[128,256]{1,0:T(8,128)(2,1)S(1)}, u32[]{:S(2)}, u32[]{:S(2)}) collective-permute-start(bf16[128,256]{1,0:T(8,128)(2,1)S(1)} %get-tuple-element.169), channel_id=1, source_target_pairs={{0,2},{2,0},{1,3},{3,1},{4,6},{6,4},{5,7},{7,5},{8,10},{10,8},{9,1... | collective-permute-start | bytes 196616 | tf_op jit(solution)/shard_map/ppermute | solution.py:410
  50.0 11.7 %collective-permute-start.16 = (bf16[1536,128]{1,0:T(8,128)(2,1)S(1)}, bf16[1536,128]{1,0:T(8,128)(2,1)S(1)}, u32[]{:S(2)}, u32[]{:S(2)}) collective-permute-start(bf16[1536,128]{1,0:T(8,128)(2,1)S(1)} %get-tuple-element.187), channel_id=1, source_target_pairs={{0,4},{1,3},{2,6},{3,1},{4,0},{5,7},{6,2},{7,5},{8,12},{9,11},{10,... | collective-permute-start | bytes 1179656 | tf_op jit(solution)/shard_map/ppermute | solution.py:423
  56.4 11.1 %collective-permute-start.17 = (bf16[1024,128]{1,0:T(8,128)(2,1)S(1)}, bf16[1024,128]{1,0:T(8,128)(2,1)S(1)}, u32[]{:S(2)}, u32[]{:S(2)}) collective-permute-start(bf16[1024,128]{1,0:T(8,128)(2,1)S(1)} %get-tuple-element.190), channel_id=1, source_target_pairs={{0,2},{1,5},{2,0},{3,7},{4,6},{5,1},{6,4},{7,3},{8,10},{9,13},{10,... | collective-permute-start | bytes 786440 | tf_op jit(solution)/shard_map/ppermute | solution.py:423
  61.7 13.5 %collective-permute-start.18 = (bf16[512,128]{1,0:T(8,128)(2,1)S(1)}, bf16[512,128]{1,0:T(8,128)(2,1)S(1)}, u32[]{:S(2)}, u32[]{:S(2)}) collective-permute-start(bf16[512,128]{1,0:T(8,128)(2,1)S(1)} %get-tuple-element.192), channel_id=1, source_target_pairs={{0,8},{1,9},{2,10},{3,11},{4,12},{5,13},{6,14},{7,15},{8,0},{9,1},... | collective-permute-start | bytes 393224 | tf_op jit(solution)/shard_map/ppermute | solution.py:423
  66.7 8.8 %collective-permute-start.19 = (bf16[512,128]{1,0:T(8,128)(2,1)S(1)}, bf16[512,128]{1,0:T(8,128)(2,1)S(1)}, u32[]{:S(2)}, u32[]{:S(2)}) collective-permute-start(bf16[512,128]{1,0:T(8,128)(2,1)S(1)} %get-tuple-element.194), channel_id=1, source_target_pairs={{0,2},{1,5},{2,0},{3,7},{4,6},{5,1},{6,4},{7,3},{8,10},{9,13},{10,... | collective-permute-start | bytes 393224 | tf_op jit(solution)/shard_map/ppermute | solution.py:423
  67.6 11.4 %collective-permute-start.20 = (bf16[512,128]{1,0:T(8,128)(2,1)S(1)}, bf16[512,128]{1,0:T(8,128)(2,1)S(1)}, u32[]{:S(2)}, u32[]{:S(2)}) collective-permute-start(bf16[512,128]{1,0:T(8,128)(2,1)S(1)} %get-tuple-element.196), channel_id=1, source_target_pairs={{0,4},{1,3},{2,6},{3,1},{4,0},{5,7},{6,2},{7,5},{8,12},{9,11},{10,... | collective-permute-start | bytes 393224 | tf_op jit(solution)/shard_map/ppermute | solution.py:423
  75.3 7.4 %collective-permute-start.21 = (bf16[512,128]{1,0:T(8,128)(2,1)S(1)}, bf16[512,128]{1,0:T(8,128)(2,1)S(1)}, u32[]{:S(2)}, u32[]{:S(2)}) collective-permute-start(bf16[512,128]{1,0:T(8,128)(2,1)S(1)} %get-tuple-element.198), channel_id=1, source_target_pairs={{0,4},{1,3},{2,6},{3,1},{4,0},{5,7},{6,2},{7,5},{8,12},{9,11},{10,... | collective-permute-start | bytes 393224 | tf_op jit(solution)/shard_map/ppermute | solution.py:423
  75.6 9.3 %collective-permute-start.22 = (bf16[512,128]{1,0:T(8,128)(2,1)S(1)}, bf16[512,128]{1,0:T(8,128)(2,1)S(1)}, u32[]{:S(2)}, u32[]{:S(2)}) collective-permute-start(bf16[512,128]{1,0:T(8,128)(2,1)S(1)} %get-tuple-element.200), channel_id=1, source_target_pairs={{0,8},{1,9},{2,10},{3,11},{4,12},{5,13},{6,14},{7,15},{8,0},{9,1},... | collective-permute-start | bytes 393224 | tf_op jit(solution)/shard_map/ppermute | solution.py:423
  79.1 7.1 %collective-permute-start.23 = (bf16[512,128]{1,0:T(8,128)(2,1)S(1)}, bf16[512,128]{1,0:T(8,128)(2,1)S(1)}, u32[]{:S(2)}, u32[]{:S(2)}) collective-permute-start(bf16[512,128]{1,0:T(8,128)(2,1)S(1)} %get-tuple-element.202), channel_id=1, source_target_pairs={{0,8},{1,9},{2,10},{3,11},{4,12},{5,13},{6,14},{7,15},{8,0},{9,1},... | collective-permute-start | bytes 393224 | tf_op jit(solution)/shard_map/ppermute | solution.py:423
  82.8 10.6 %collective-permute-start.25 = (bf16[1024,128]{1,0:T(8,128)(2,1)S(1)}, bf16[1024,128]{1,0:T(8,128)(2,1)S(1)}, u32[]{:S(2)}, u32[]{:S(2)}) collective-permute-start(bf16[1024,128]{1,0:T(8,128)(2,1)S(1)} %get-tuple-element.206), channel_id=1, source_target_pairs={{0,2},{1,5},{2,0},{3,7},{4,6},{5,1},{6,4},{7,3},{8,10},{9,13},{10,... | collective-permute-start | bytes 786440 | tf_op jit(solution)/shard_map/ppermute | solution.py:423
  84.9 8.4 %collective-permute-start.24 = (bf16[512,128]{1,0:T(8,128)(2,1)S(1)}, bf16[512,128]{1,0:T(8,128)(2,1)S(1)}, u32[]{:S(2)}, u32[]{:S(2)}) collective-permute-start(bf16[512,128]{1,0:T(8,128)(2,1)S(1)} %get-tuple-element.204), channel_id=1, source_target_pairs={{0,2},{1,5},{2,0},{3,7},{4,6},{5,1},{6,4},{7,3},{8,10},{9,13},{10,... | collective-permute-start | bytes 393224 | tf_op jit(solution)/shard_map/ppermute | solution.py:423
  86.3 7.1 %collective-permute-start.26 = (bf16[512,128]{1,0:T(8,128)(2,1)S(1)}, bf16[512,128]{1,0:T(8,128)(2,1)S(1)}, u32[]{:S(2)}, u32[]{:S(2)}) collective-permute-start(bf16[512,128]{1,0:T(8,128)(2,1)S(1)} %get-tuple-element.207), channel_id=1, source_target_pairs={{0,4},{1,3},{2,6},{3,1},{4,0},{5,7},{6,2},{7,5},{8,12},{9,11},{10,... | collective-permute-start | bytes 393224 | tf_op jit(solution)/shard_map/ppermute | solution.py:423
  93.3 6.4 %collective-permute-start.27 = (bf16[1024,128]{1,0:T(8,128)(2,1)S(1)}, bf16[1024,128]{1,0:T(8,128)(2,1)S(1)}, u32[]{:S(2)}, u32[]{:S(2)}) collective-permute-start(bf16[1024,128]{1,0:T(8,128)(2,1)S(1)} %get-tuple-element.212), channel_id=1, source_target_pairs={{0,4},{1,3},{2,6},{3,1},{4,0},{5,7},{6,2},{7,5},{8,12},{9,11},{10,... | collective-permute-start | bytes 786440 | tf_op jit(solution)/shard_map/ppermute | solution.py:423
  93.5 9.4 %collective-permute-start.30 = (bf16[1024,128]{1,0:T(8,128)(2,1)S(1)}, bf16[1024,128]{1,0:T(8,128)(2,1)S(1)}, u32[]{:S(2)}, u32[]{:S(2)}) collective-permute-start(bf16[1024,128]{1,0:T(8,128)(2,1)S(1)} %get-tuple-element.224), channel_id=1, source_target_pairs={{0,2},{1,5},{2,0},{3,7},{4,6},{5,1},{6,4},{7,3},{8,10},{9,13},{10,... | collective-permute-start | bytes 786440 | tf_op jit(solution)/shard_map/ppermute | solution.py:423
  94.8 6.9 %collective-permute-start.28 = (bf16[128,256]{1,0:T(8,128)(2,1)S(1)}, bf16[128,256]{1,0:T(8,128)(2,1)S(1)}, u32[]{:S(2)}, u32[]{:S(2)}) collective-permute-start(bf16[128,256]{1,0:T(8,128)(2,1)S(1)} %get-tuple-element.218), channel_id=1, source_target_pairs={{4,0},{8,4},{12,8},{5,1},{9,5},{13,9},{6,2},{10,6},{14,10},{7,3},{... | collective-permute-start | bytes 196616 | tf_op jit(solution)/shard_map/ppermute | solution.py:446
  96.1 5.6 %collective-permute-start.29 = (bf16[128,256]{1,0:T(8,128)(2,1)S(1)}, bf16[128,256]{1,0:T(8,128)(2,1)S(1)}, u32[]{:S(2)}, u32[]{:S(2)}) collective-permute-start(bf16[128,256]{1,0:T(8,128)(2,1)S(1)} %get-tuple-element.219), channel_id=1, source_target_pairs={{0,2},{2,0},{1,3},{3,1},{4,6},{6,4},{5,7},{7,5},{8,10},{10,8},{9,1... | collective-permute-start | bytes 196616 | tf_op jit(solution)/shard_map/ppermute | solution.py:410
  (5 other events, 15.7 us)

commit v15 on v11

--- a/solution.py
+++ b/solution.py
@@ -558,6 +558,7 @@
     n = len(over_basin)
     orders = over_basin + over_chain, over_chain[:n] + over_basin + over_chain[n:]
     stages = list(zip(*orders, strict=True))
+    basin_first = list(zip(orders[0], orders[0], strict=True))
     returned = {}
     sums = {}
 
@@ -575,7 +576,7 @@
             name=f"back{layer}",
             after=after,
         )
-        sums[layer] = Sum(whole, stages)
+        sums[layer] = Sum(whole, basin_first if layer else stages)
         return [outs[0], grad], [grad]
 
     def join(layer, state, after):
@@ -606,7 +607,7 @@
             functools.partial(
                 write_kernel,
                 layer,
-                stages[0],
+                sums[layer].stages[0],
                 len(kept),
                 [(at, i) for (_, at), i in zip(ready, which)],
             ),

time: 99.4 us -> 97.9 us (0.985)
  starting transfers between devices: 51 us -> 41.7 us
  waiting for transfers between devices: 14.4 us -> 22.1 us
    ppermute x18, starting transfers between devices: 40.2 us -> 29.4 us  [over_mesh(): return lax.ppermute(x, ('chain', 'basin', 'feat'), perm)]
    ppermute x18, waiting for transfers between devices: 6.57 us -> 15.4 us  [over_mesh(): return lax.ppermute(x, ('chain', 'basin', 'feat'), perm)]
    ppermute x11, starting transfers between devices: 6.63 us -> 8.27 us  [around(): return lax.ppermute(x, axis, [(i, (i + distance) % n) for i in range(n)])]
    ppermute x3, waiting for transfers between devices: 4.27 us -> 2.63 us  [backward(): up = lax.ppermute(grads[0], 'chain', [(c, c - 1) for c in range(1, chain)])]
  transfers between devices with their start and end apart: 32 -> 32, of which waited for: 12 -> 14; matrix products, arithmetic and copies ran while one was open for 1% -> 1% of each run, Pallas kernels for 25% -> 26%
where the time goes in v15:
time: 97.9 us; the launch traced here: 97.7 us
  starting transfers between devices  41.7 us (43%)
  Pallas kernels  30.6 us (31%)
  waiting for transfers between devices  22.1 us (23%)
  between operations  1.25 us (1%)
  local copies, waits for them, and re-layouts  1.2 us (1%)
    ppermute x18, starting transfers between devices, over_mesh(): return lax.ppermute(x, ('chain', 'basin', 'feat'), perm)  29.4 us
    pallas_call x33, Pallas kernels, call(): pl.pallas_call(lambda *refs: body(*refs[skipped:]), out_shape=[jax.ShapeD...  26.2 us
    ppermute x18, waiting for transfers between devices, over_mesh(): return lax.ppermute(x, ('chain', 'basin', 'feat'), perm)  15.4 us
    ppermute x11, starting transfers between devices, around(): return lax.ppermute(x, axis, [(i, (i + distance) % n) for i in range(n)])  8.27 us
    pallas_call x4, Pallas kernels, write(): pl.pallas_call(functools.partial(write_kernel, layer, sums[layer].stages[...  4.44 us
    ppermute x11, waiting for transfers between devices, around(): return lax.ppermute(x, axis, [(i, (i + distance) % n) for i in range(n)])  4.15 us
    ppermute x3, starting transfers between devices, backward(): up = lax.ppermute(grads[0], 'chain', [(c, c - 1) for c in range(1, chain)])  4.08 us
    ppermute x3, waiting for transfers between devices, backward(): up = lax.ppermute(grads[0], 'chain', [(c, c - 1) for c in range(1, chain)])  2.63 us
  transfers between devices with their start and end apart: 32, of which 14 were waited for; matrix products, arithmetic and copies ran while one was open for 1% of the time, Pallas kernels for 26%

profile of v15, /device:TPU:0, one launch (start us, length us, event | category | flops | bytes accessed | tf_op | source)
XLA Modules:
  0.0 97.7 jit_solution(6279022308680737781)
XLA Ops:
  3.3 4.9 %collective-permute-start = (bf16[128,256]{1,0:T(8,128)(2,1)S(1)}, bf16[128,256]{1,0:T(8,128)(2,1)S(1)}, u32[]{:S(2)}, u32[]{:S(2)}) collective-permute-start(bf16[128,256]{1,0:T(8,128)(2,1)S(1)} %get-tuple-element.117), channel_id=1, source_target_pairs={{0,4},{2,6},{5,9},{7,11},{8,12},{10,14},{16,20},{18,22},{21,25},{2... | collective-permute-start | bytes 196616 | tf_op jit(solution)/shard_map/ppermute | solution.py:423
  8.2 1.6 %collective-permute-start.3 = (bf16[128,256]{1,0:T(8,128)(2,1)S(1)}, bf16[128,256]{1,0:T(8,128)(2,1)S(1)}, u32[]{:S(2)}, u32[]{:S(2)}) collective-permute-start(bf16[128,256]{1,0:T(8,128)(2,1)S(1)} %get-tuple-element.124), channel_id=1, source_target_pairs={{0,2},{2,0},{1,3},{3,1},{4,6},{6,4},{5,7},{7,5},{8,10},{10,8},{9,1... | collective-permute-start | bytes 196616 | tf_op jit(solution)/shard_map/ppermute | solution.py:410
  11.8 1.6 %adjacency.1 = (bf16[768,768]{1,0:T(8,128)(2,1)S(1)}, bf16[768,768]{1,0:T(8,128)(2,1)S(1)}, bf16[768,256]{1,0:T(8,128)(2,1)S(1)}, bf16[256,768]{1,0:T(8,128)(2,1)S(1)}) custom-call(s32[4,6]{1,0:T(4,128)S(1)} %bitcast.4, bf16[6,4,128,128]{3,2,1,0:T(8,128)(2,1)S(1)} %copy-done.3, bf16[128,768]{1,0:T(8,128)(2,1)S(1)} %get-tuple-element.118.refs_2_, ...), custom_call_target="tpu_custom_call" | custom-call | flops 150994944 | bytes 4000000 | tf_op jit(solution)/shard_map/adjacency/pallas_call | solution.py:32
  15.8 2.8 %collective-permute-start.5 = (bf16[128,256]{1,0:T(8,128)(2,1)S(1)}, bf16[128,256]{1,0:T(8,128)(2,1)S(1)}, u32[]{:S(2)}, u32[]{:S(2)}) collective-permute-start(bf16[128,256]{1,0:T(8,128)(2,1)S(1)} %get-tuple-element.128), channel_id=1, source_target_pairs={{0,4},{2,6},{5,9},{7,11},{8,12},{10,14},{16,20},{18,22},{21,25},{2... | collective-permute-start | bytes 196616 | tf_op jit(solution)/shard_map/ppermute | solution.py:423
  19.1 1.6 %local1.1 = (bf16[768,256]{1,0:T(8,128)(2,1)S(1)}, bf16[768,512]{1,0:T(8,128)(2,1)S(1)}, bf16[768,512]{1,0:T(8,128)(2,1)S(1)}, bf16[512,768]{1,0:T(8,128)(2,1)S(1)}, bf16[256,768]{1,0:T(8,128)(2,1)S(1)}) custom-call(bf16[768,256]{1,0:T(8,128)(2,1)S(1)} %get-tuple-element.129.refs_0_, bf16[3,256,512]{2,1,0:T(8,128)(2,1)S(1)} %copy-done, ...), custom_call_target="tpu_custom_call" | custom-call | flops 805306368 | bytes 4000000 | tf_op jit(solution)/shard_map/local1/pallas_call | solution.py:32
  20.8 2.0 %collective-permute-done.6.refs_7_.refs_14_ = bf16[128,256]{1,0:T(8,128)(2,1)S(1)} collective-permute-done((bf16[128,256]{1,0:T(8,128)(2,1)S(1)}, bf16[128,256]{1,0:T(8,128)(2,1)S(1)}, u32[]{:S(2)}, u32[]{:S(2)}) %collective-permute-start.6) | collective-permute-done | bytes 65568 | tf_op jit(solution)/shard_map/ppermute | solution.py:410
  24.9 2.3 %collective-permute-start.8 = (bf16[128,256]{1,0:T(8,128)(2,1)S(1)}, bf16[128,256]{1,0:T(8,128)(2,1)S(1)}, u32[]{:S(2)}, u32[]{:S(2)}) collective-permute-start(bf16[128,256]{1,0:T(8,128)(2,1)S(1)} %get-tuple-element.135), channel_id=1, source_target_pairs={{0,4},{2,6},{5,9},{7,11},{8,12},{10,14},{16,20},{18,22},{21,25},{2... | collective-permute-start | bytes 196616 | tf_op jit(solution)/shard_map/ppermute | solution.py:423
  28.6 1.6 %local2.1 = (bf16[768,256]{1,0:T(8,128)(2,1)S(1)}, bf16[768,512]{1,0:T(8,128)(2,1)S(1)}, bf16[768,512]{1,0:T(8,128)(2,1)S(1)}, bf16[512,768]{1,0:T(8,128)(2,1)S(1)}, bf16[256,768]{1,0:T(8,128)(2,1)S(1)}) custom-call(bf16[768,256]{1,0:T(8,128)(2,1)S(1)} %get-tuple-element.136.refs_0_, bf16[3,256,512]{2,1,0:T(8,128)(2,1)S(1)} %copy-done, ...), custom_call_target="tpu_custom_call" | custom-call | flops 805306368 | bytes 4000000 | tf_op jit(solution)/shard_map/local2/pallas_call | solution.py:32
  32.5 2.0 %turn.1 = (f32[768,256]{1,0:T(8,128)S(1)}, bf16[768,256]{1,0:T(8,128)(2,1)S(1)}, bf16[256,256]{1,0:T(8,128)(2,1)S(1)}, bf16[256,256]{1,0:T(8,128)(2,1)S(1)}, bf1...) custom-call(f32[768,256]{1,0:T(8,128)S(1)} %get-tuple-element.134.re, ...), custom_call_target="tpu_custom_call" | custom-call | flops 536870912 | bytes 4000000 | tf_op jit(solution)/shard_map/turn/pallas_call | solution.py:32
  35.8 1.4 %collective-permute-start.12 = (bf16[128,256]{1,0:T(8,128)(2,1)S(1)}, bf16[128,256]{1,0:T(8,128)(2,1)S(1)}, u32[]{:S(2)}, u32[]{:S(2)}) collective-permute-start(bf16[128,256]{1,0:T(8,128)(2,1)S(1)} %get-tuple-element.154), channel_id=1, source_target_pairs={{0,2},{2,0},{1,3},{3,1},{4,6},{6,4},{5,7},{7,5},{8,10},{10,8},{9,1... | collective-permute-start | bytes 196616 | tf_op jit(solution)/shard_map/ppermute | solution.py:410
  37.2 2.4 %back2.1 = (f32[768,256]{1,0:T(8,128)S(1)}, f32[2048,128]{1,0:T(8,128)S(1)}) custom-call(bf16[768,256]{1,0:T(8,128)(2,1)S(1)} %get-tuple-element.142.refs_0_, bf16[768,768]{1,0:T(8,128)(2,1)S(1)} %get-tuple-element.143.refs_1_.refs_2_, bf16[768,512]{1,0:T(8,128)(2,1)S(1)} %get-tuple-element.144.refs_2_, bf16[768,512]{1,0:T(8,128)(2,1)S(1)} %get-tuple-element.145.refs_3_, ...), custom_call_target="tpu_custom_call" | custom-call | flops 2717908992 | bytes 4000000 | tf_op jit(solution)/shard_map/back2/pallas_call | solution.py:32
  40.8 1.4 %collective-permute-start.15 = (bf16[1024,128]{1,0:T(8,128)(2,1)S(1)}, bf16[1024,128]{1,0:T(8,128)(2,1)S(1)}, u32[]{:S(2)}, u32[]{:S(2)}) collective-permute-start(bf16[1024,128]{1,0:T(8,128)(2,1)S(1)} %get-tuple-element.173), channel_id=1, source_target_pairs={{0,2},{1,3},{2,0},{3,1},{4,6},{5,7},{6,4},{7,5},{8,10},{9,11},{10,... | collective-permute-start | bytes 786440 | tf_op jit(solution)/shard_map/ppermute | solution.py:423
  42.1 1.5 %join2.1 = (f32[768,256]{1,0:T(8,128)S(1)}, bf16[768,256]{1,0:T(8,128)(2,1)S(1)}, bf16[256,256]{1,0:T(8,128)(2,1)S(1)}, bf16[256,256]{1,0:T(8,128)(2,1)S(1)}, bf...) custom-call(f32[1024,128]{1,0:T(8,128)S(1)} %get-tuple-element.156.r, ...), custom_call_target="tpu_custom_call" | custom-call | flops 536870912 | bytes 4000000 | tf_op jit(solution)/shard_map/join2/pallas_call | solution.py:32
  43.6 1.5 %collective-permute-start.13 = (bf16[128,256]{1,0:T(8,128)(2,1)S(1)}, bf16[128,256]{1,0:T(8,128)(2,1)S(1)}, u32[]{:S(2)}, u32[]{:S(2)}) collective-permute-start(bf16[128,256]{1,0:T(8,128)(2,1)S(1)} %get-tuple-element.169), channel_id=1, source_target_pairs={{4,0},{8,4},{12,8},{5,1},{9,5},{13,9},{6,2},{10,6},{14,10},{7,3},{... | collective-permute-start | bytes 196616 | tf_op jit(solution)/shard_map/ppermute | solution.py:446
  45.9 2.4 %back1.1 = (f32[768,256]{1,0:T(8,128)S(1)}, f32[2048,128]{1,0:T(8,128)S(1)}) custom-call(bf16[768,256]{1,0:T(8,128)(2,1)S(1)} %get-tuple-element.159.refs_0_.refs_1_, bf16[768,256]{1,0:T(8,128)(2,1)S(1)} %get-tuple-element.159.refs_0_.refs_1_, bf16[768,768]{1,0:T(8,128)(2,1)S(1)} %get-tuple-element.143.refs_1_.refs_2_, ...), custom_call_target="tpu_custom_call" | custom-call | flops 2717908992 | bytes 4000000 | tf_op jit(solution)/shard_map/back1/pallas_call | solution.py:32
  48.3 1.5 %collective-permute-done.13.refs_1_.refs_10_ = bf16[128,256]{1,0:T(8,128)(2,1)S(1)} collective-permute-done((bf16[128,256]{1,0:T(8,128)(2,1)S(1)}, bf16[128,256]{1,0:T(8,128)(2,1)S(1)}, u32[]{:S(2)}, u32[]{:S(2)}) %collective-permute-start.13) | collective-permute-done | bytes 65568 | tf_op jit(solution)/shard_map/ppermute | solution.py:446
  50.8 2.4 %collective-permute-start.16 = (bf16[512,128]{1,0:T(8,128)(2,1)S(1)}, bf16[512,128]{1,0:T(8,128)(2,1)S(1)}, u32[]{:S(2)}, u32[]{:S(2)}) collective-permute-start(bf16[512,128]{1,0:T(8,128)(2,1)S(1)} %get-tuple-element.186), channel_id=1, source_target_pairs={{0,4},{1,5},{2,6},{3,7},{4,0},{5,1},{6,2},{7,3},{8,12},{9,13},{10,... | collective-permute-start | bytes 393224 | tf_op jit(solution)/shard_map/ppermute | solution.py:423
  53.2 1.5 %join1.1 = (f32[768,256]{1,0:T(8,128)S(1)}, bf16[768,256]{1,0:T(8,128)(2,1)S(1)}, bf16[256,256]{1,0:T(8,128)(2,1)S(1)}, bf16[256,256]{1,0:T(8,128)(2,1)S(1)}, bf...) custom-call(f32[512,128]{1,0:T(8,128)S(1)} %get-tuple-element.174.re, ...), custom_call_target="tpu_custom_call" | custom-call | flops 536870912 | bytes 4000000 | tf_op jit(solution)/shard_map/join1/pallas_call | solution.py:32
  54.7 2.4 %back0.1 = (f32[768,256]{1,0:T(8,128)S(1)}, f32[2048,128]{1,0:T(8,128)S(1)}) custom-call(bf16[768,256]{1,0:T(8,128)(2,1)S(1)} %get-tuple-element.176.refs_0_.refs_1_, bf16[768,256]{1,0:T(8,128)(2,1)S(1)} %get-tuple-element.176.refs_0_.refs_1_, bf16[768,768]{1,0:T(8,128)(2,1)S(1)} %get-tuple-element.143.refs_1_.refs_2_, ...), custom_call_target="tpu_custom_call" | custom-call | flops 2717908992 | bytes 4000000 | tf_op jit(solution)/shard_map/back0/pallas_call | solution.py:32
  57.2 1.5 %collective-permute-start.18 = (bf16[1024,128]{1,0:T(8,128)(2,1)S(1)}, bf16[1024,128]{1,0:T(8,128)(2,1)S(1)}, u32[]{:S(2)}, u32[]{:S(2)}) collective-permute-start(bf16[1024,128]{1,0:T(8,128)(2,1)S(1)} %get-tuple-element.192), channel_id=1, source_target_pairs={{0,2},{1,5},{2,0},{3,7},{4,6},{5,1},{6,4},{7,3},{8,10},{9,13},{10,... | collective-permute-start | bytes 786440 | tf_op jit(solution)/shard_map/ppermute | solution.py:423
  58.7 4.2 %collective-permute-start.19 = (bf16[512,128]{1,0:T(8,128)(2,1)S(1)}, bf16[512,128]{1,0:T(8,128)(2,1)S(1)}, u32[]{:S(2)}, u32[]{:S(2)}) collective-permute-start(bf16[512,128]{1,0:T(8,128)(2,1)S(1)} %get-tuple-element.194), channel_id=1, source_target_pairs={{0,8},{1,9},{2,10},{3,11},{4,12},{5,13},{6,14},{7,15},{8,0},{9,1},... | collective-permute-start | bytes 393224 | tf_op jit(solution)/shard_map/ppermute | solution.py:423
  63.8 3.6 %collective-permute-start.21 = (bf16[512,128]{1,0:T(8,128)(2,1)S(1)}, bf16[512,128]{1,0:T(8,128)(2,1)S(1)}, u32[]{:S(2)}, u32[]{:S(2)}) collective-permute-start(bf16[512,128]{1,0:T(8,128)(2,1)S(1)} %get-tuple-element.198), channel_id=1, source_target_pairs={{0,4},{1,3},{2,6},{3,1},{4,0},{5,7},{6,2},{7,5},{8,12},{9,11},{10,... | collective-permute-start | bytes 393224 | tf_op jit(solution)/shard_map/ppermute | solution.py:423
  68.1 2.7 %collective-permute-done.20.refs_2_ = bf16[512,128]{1,0:T(8,128)(2,1)S(1)} collective-permute-done((bf16[512,128]{1,0:T(8,128)(2,1)S(1)}, bf16[512,128]{1,0:T(8,128)(2,1)S(1)}, u32[]{:S(2)}, u32[]{:S(2)}) %collective-permute-start.20) | collective-permute-done | bytes 131104 | tf_op jit(solution)/shard_map/ppermute | solution.py:423
  71.1 1.4 %collective-permute-done.21.refs_2_ = bf16[512,128]{1,0:T(8,128)(2,1)S(1)} collective-permute-done((bf16[512,128]{1,0:T(8,128)(2,1)S(1)}, bf16[512,128]{1,0:T(8,128)(2,1)S(1)}, u32[]{:S(2)}, u32[]{:S(2)}) %collective-permute-start.21) | collective-permute-done | bytes 131104 | tf_op jit(solution)/shard_map/ppermute | solution.py:423
  72.5 1.8 %collective-permute-start.24 = (bf16[512,128]{1,0:T(8,128)(2,1)S(1)}, bf16[512,128]{1,0:T(8,128)(2,1)S(1)}, u32[]{:S(2)}, u32[]{:S(2)}) collective-permute-start(bf16[512,128]{1,0:T(8,128)(2,1)S(1)} %get-tuple-element.204), channel_id=1, source_target_pairs={{0,8},{1,9},{2,10},{3,11},{4,12},{5,13},{6,14},{7,15},{8,0},{9,1},... | collective-permute-start | bytes 393224 | tf_op jit(solution)/shard_map/ppermute | solution.py:423
  74.3 2.6 %collective-permute-done.22.refs_2_ = bf16[512,128]{1,0:T(8,128)(2,1)S(1)} collective-permute-done((bf16[512,128]{1,0:T(8,128)(2,1)S(1)}, bf16[512,128]{1,0:T(8,128)(2,1)S(1)}, u32[]{:S(2)}, u32[]{:S(2)}) %collective-permute-start.22) | collective-permute-done | bytes 131104 | tf_op jit(solution)/shard_map/ppermute | solution.py:423
  77.0 1.5 %collective-permute-start.26 = (bf16[1024,128]{1,0:T(8,128)(2,1)S(1)}, bf16[1024,128]{1,0:T(8,128)(2,1)S(1)}, u32[]{:S(2)}, u32[]{:S(2)}) collective-permute-start(bf16[1024,128]{1,0:T(8,128)(2,1)S(1)} %get-tuple-element.208), channel_id=1, source_target_pairs={{0,2},{1,3},{2,0},{3,1},{4,6},{5,7},{6,4},{7,5},{8,10},{9,11},{10,... | collective-permute-start | bytes 786440 | tf_op jit(solution)/shard_map/ppermute | solution.py:423
  78.6 2.4 %collective-permute-done.24.refs_2_ = bf16[512,128]{1,0:T(8,128)(2,1)S(1)} collective-permute-done((bf16[512,128]{1,0:T(8,128)(2,1)S(1)}, bf16[512,128]{1,0:T(8,128)(2,1)S(1)}, u32[]{:S(2)}, u32[]{:S(2)}) %collective-permute-start.24) | collective-permute-done | bytes 131104 | tf_op jit(solution)/shard_map/ppermute | solution.py:423
  81.1 3.8 %collective-permute-done.25.refs_2_ = bf16[512,128]{1,0:T(8,128)(2,1)S(1)} collective-permute-done((bf16[512,128]{1,0:T(8,128)(2,1)S(1)}, bf16[512,128]{1,0:T(8,128)(2,1)S(1)}, u32[]{:S(2)}, u32[]{:S(2)}) %collective-permute-start.25) | collective-permute-done | bytes 131104 | tf_op jit(solution)/shard_map/ppermute | solution.py:423
  86.1 1.6 %collective-permute-done.27.refs_3_ = bf16[512,128]{1,0:T(8,128)(2,1)S(1)} collective-permute-done((bf16[512,128]{1,0:T(8,128)(2,1)S(1)}, bf16[512,128]{1,0:T(8,128)(2,1)S(1)}, u32[]{:S(2)}, u32[]{:S(2)}) %collective-permute-start.27) | collective-permute-done | bytes 131104 | tf_op jit(solution)/shard_map/ppermute | solution.py:423
  89.4 1.8 %collective-permute-start.30 = (bf16[128,256]{1,0:T(8,128)(2,1)S(1)}, bf16[128,256]{1,0:T(8,128)(2,1)S(1)}, u32[]{:S(2)}, u32[]{:S(2)}) collective-permute-start(bf16[128,256]{1,0:T(8,128)(2,1)S(1)} %get-tuple-element.221), channel_id=1, source_target_pairs={{0,2},{2,0},{1,3},{3,1},{4,6},{6,4},{5,7},{7,5},{8,10},{10,8},{9,1... | collective-permute-start | bytes 196616 | tf_op jit(solution)/shard_map/ppermute | solution.py:410
  96.0 1.4 %write0.3 = (f32[3,256,512]{2,1,0:T(8,128)}, f32[3,512,256]{2,1,0:T(8,128)}, f32[8,128]{1,0:T(8,128)}) custom-call(f32[3,256,512]{2,1,0:T(8,128)} %get-tuple-element.223.refs_0_, f32[3,512,256]{2,1,0:T(8,128)} %get-tuple-element.224.refs_1_, f32[8,128]{1,0:T(8,128)S(1)} %get-tuple-element.225.refs_2_, ...), custom_call_target="tpu_custom_call", output_to_operand_aliasing={{0}: (0, {}), {1}: (1, {})} | custom-call | flops 1 | bytes 1 | tf_op jit(solution)/shard_map/write0/pallas_call | solution.py:606
  (82 shorter events, 27.7 us)
Async XLA Ops:
  0.7 9.1 %collective-permute-start.1 = (bf16[3,256,512]{2,1,0:T(8,128)(2,1)}, bf16[3,256,512]{2,1,0:T(8,128)(2,1)S(1)}, u32[]{:S(2)}, u32[]{:S(2)}) collective-permute-start(bf16[3,256,512]{2,1,0:T(8,128)(2,1)} %refs_7_.5), channel_id=1, source_target_pairs={{0,1},{1,0},{2,3},{3,2},{4,5},{5,4},{6,7},{7,6},{8,9},{9,8},{10,11... | collective-permute-start | bytes 2359304 | tf_op jit(solution)/shard_map/ppermute | solution.py:410
  1.2 8.6 %collective-permute-start.2 = (bf16[3,512,256]{2,1,0:T(8,128)(2,1)}, bf16[3,512,256]{2,1,0:T(8,128)(2,1)S(1)}, u32[]{:S(2)}, u32[]{:S(2)}) collective-permute-start(bf16[3,512,256]{2,1,0:T(8,128)(2,1)} %refs_9_.3), channel_id=1, source_target_pairs={{0,1},{1,0},{2,3},{3,2},{4,5},{5,4},{6,7},{7,6},{8,9},{9,8},{10,11... | collective-permute-start | bytes 2359304 | tf_op jit(solution)/shard_map/ppermute | solution.py:410
  3.3 10.1 %collective-permute-start = (bf16[128,256]{1,0:T(8,128)(2,1)S(1)}, bf16[128,256]{1,0:T(8,128)(2,1)S(1)}, u32[]{:S(2)}, u32[]{:S(2)}) collective-permute-start(bf16[128,256]{1,0:T(8,128)(2,1)S(1)} %get-tuple-element.117), channel_id=1, source_target_pairs={{0,4},{2,6},{5,9},{7,11},{8,12},{10,14},{16,20},{18,22},{21,25},{2... | collective-permute-start | bytes 196616 | tf_op jit(solution)/shard_map/ppermute | solution.py:423
  8.2 5.2 %collective-permute-start.3 = (bf16[128,256]{1,0:T(8,128)(2,1)S(1)}, bf16[128,256]{1,0:T(8,128)(2,1)S(1)}, u32[]{:S(2)}, u32[]{:S(2)}) collective-permute-start(bf16[128,256]{1,0:T(8,128)(2,1)S(1)} %get-tuple-element.124), channel_id=1, source_target_pairs={{0,2},{2,0},{1,3},{3,1},{4,6},{6,4},{5,7},{7,5},{8,10},{10,8},{9,1... | collective-permute-start | bytes 196616 | tf_op jit(solution)/shard_map/ppermute | solution.py:410
  13.4 1.3 %collective-permute-start.4 = (bf16[128,256]{1,0:T(8,128)(2,1)S(1)}, bf16[128,256]{1,0:T(8,128)(2,1)S(1)}, u32[]{:S(2)}, u32[]{:S(2)}) collective-permute-start(bf16[128,256]{1,0:T(8,128)(2,1)S(1)} %collective-permute-done.refs_8_.refs_12_), channel_id=1, source_target_pairs={{0,1},{1,0},{2,3},{3,2},{4,5},{5,4},{6,7},{7,6},{8,9},{9,8},{10,11... | collective-permute-start | bytes 196616 | tf_op jit(solution)/shard_map/ppermute | solution.py:410
  15.8 5.0 %collective-permute-start.5 = (bf16[128,256]{1,0:T(8,128)(2,1)S(1)}, bf16[128,256]{1,0:T(8,128)(2,1)S(1)}, u32[]{:S(2)}, u32[]{:S(2)}) collective-permute-start(bf16[128,256]{1,0:T(8,128)(2,1)S(1)} %get-tuple-element.128), channel_id=1, source_target_pairs={{0,4},{2,6},{5,9},{7,11},{8,12},{10,14},{16,20},{18,22},{21,25},{2... | collective-permute-start | bytes 196616 | tf_op jit(solution)/shard_map/ppermute | solution.py:423
  18.5 4.3 %collective-permute-start.6 = (bf16[128,256]{1,0:T(8,128)(2,1)S(1)}, bf16[128,256]{1,0:T(8,128)(2,1)S(1)}, u32[]{:S(2)}, u32[]{:S(2)}) collective-permute-start(bf16[128,256]{1,0:T(8,128)(2,1)S(1)} %get-tuple-element.132), channel_id=1, source_target_pairs={{0,2},{2,0},{1,3},{3,1},{4,6},{6,4},{5,7},{7,5},{8,10},{10,8},{9,1... | collective-permute-start | bytes 196616 | tf_op jit(solution)/shard_map/ppermute | solution.py:410
  20.8 3.1 %collective-permute-start.7 = (bf16[128,256]{1,0:T(8,128)(2,1)S(1)}, bf16[128,256]{1,0:T(8,128)(2,1)S(1)}, u32[]{:S(2)}, u32[]{:S(2)}) collective-permute-start(bf16[128,256]{1,0:T(8,128)(2,1)S(1)} %collective-permute-done.5.refs_8_.refs_12_), channel_id=1, source_target_pairs={{0,1},{1,0},{2,3},{3,2},{4,5},{5,4},{6,7},{7,6},{8,9},{9,8},{10,11... | collective-permute-start | bytes 196616 | tf_op jit(solution)/shard_map/ppermute | solution.py:410
  24.9 5.2 %collective-permute-start.8 = (bf16[128,256]{1,0:T(8,128)(2,1)S(1)}, bf16[128,256]{1,0:T(8,128)(2,1)S(1)}, u32[]{:S(2)}, u32[]{:S(2)}) collective-permute-start(bf16[128,256]{1,0:T(8,128)(2,1)S(1)} %get-tuple-element.135), channel_id=1, source_target_pairs={{0,4},{2,6},{5,9},{7,11},{8,12},{10,14},{16,20},{18,22},{21,25},{2... | collective-permute-start | bytes 196616 | tf_op jit(solution)/shard_map/ppermute | solution.py:423
  27.2 4.3 %collective-permute-start.9 = (bf16[128,256]{1,0:T(8,128)(2,1)S(1)}, bf16[128,256]{1,0:T(8,128)(2,1)S(1)}, u32[]{:S(2)}, u32[]{:S(2)}) collective-permute-start(bf16[128,256]{1,0:T(8,128)(2,1)S(1)} %get-tuple-element.139), channel_id=1, source_target_pairs={{0,2},{2,0},{1,3},{3,1},{4,6},{6,4},{5,7},{7,5},{8,10},{10,8},{9,1... | collective-permute-start | bytes 196616 | tf_op jit(solution)/shard_map/ppermute | solution.py:410
  30.2 2.3 %collective-permute-start.10 = (bf16[128,256]{1,0:T(8,128)(2,1)S(1)}, bf16[128,256]{1,0:T(8,128)(2,1)S(1)}, u32[]{:S(2)}, u32[]{:S(2)}) collective-permute-start(bf16[128,256]{1,0:T(8,128)(2,1)S(1)} %collective-permute-done.8.refs_9_), channel_id=1, source_target_pairs={{0,1},{1,0},{2,3},{3,2},{4,5},{5,4},{6,7},{7,6},{8,9},{9,8},{10,11... | collective-permute-start | bytes 196616 | tf_op jit(solution)/shard_map/ppermute | solution.py:410
  34.5 6.2 %collective-permute-start.11 = (bf16[128,256]{1,0:T(8,128)(2,1)S(1)}, bf16[128,256]{1,0:T(8,128)(2,1)S(1)}, u32[]{:S(2)}, u32[]{:S(2)}) collective-permute-start(bf16[128,256]{1,0:T(8,128)(2,1)S(1)} %get-tuple-element.153), channel_id=1, source_target_pairs={{4,0},{8,4},{12,8},{5,1},{9,5},{13,9},{6,2},{10,6},{14,10},{7,3},{... | collective-permute-start | bytes 196616 | tf_op jit(solution)/shard_map/ppermute | solution.py:446
  35.8 4.9 %collective-permute-start.12 = (bf16[128,256]{1,0:T(8,128)(2,1)S(1)}, bf16[128,256]{1,0:T(8,128)(2,1)S(1)}, u32[]{:S(2)}, u32[]{:S(2)}) collective-permute-start(bf16[128,256]{1,0:T(8,128)(2,1)S(1)} %get-tuple-element.154), channel_id=1, source_target_pairs={{0,2},{2,0},{1,3},{3,1},{4,6},{6,4},{5,7},{7,5},{8,10},{10,8},{9,1... | collective-permute-start | bytes 196616 | tf_op jit(solution)/shard_map/ppermute | solution.py:410
  40.8 10.0 %collective-permute-start.15 = (bf16[1024,128]{1,0:T(8,128)(2,1)S(1)}, bf16[1024,128]{1,0:T(8,128)(2,1)S(1)}, u32[]{:S(2)}, u32[]{:S(2)}) collective-permute-start(bf16[1024,128]{1,0:T(8,128)(2,1)S(1)} %get-tuple-element.173), channel_id=1, source_target_pairs={{0,2},{1,3},{2,0},{3,1},{4,6},{5,7},{6,4},{7,5},{8,10},{9,11},{10,... | collective-permute-start | bytes 786440 | tf_op jit(solution)/shard_map/ppermute | solution.py:423
  43.6 6.3 %collective-permute-start.13 = (bf16[128,256]{1,0:T(8,128)(2,1)S(1)}, bf16[128,256]{1,0:T(8,128)(2,1)S(1)}, u32[]{:S(2)}, u32[]{:S(2)}) collective-permute-start(bf16[128,256]{1,0:T(8,128)(2,1)S(1)} %get-tuple-element.169), channel_id=1, source_target_pairs={{4,0},{8,4},{12,8},{5,1},{9,5},{13,9},{6,2},{10,6},{14,10},{7,3},{... | collective-permute-start | bytes 196616 | tf_op jit(solution)/shard_map/ppermute | solution.py:446
  45.1 4.7 %collective-permute-start.14 = (bf16[128,256]{1,0:T(8,128)(2,1)S(1)}, bf16[128,256]{1,0:T(8,128)(2,1)S(1)}, u32[]{:S(2)}, u32[]{:S(2)}) collective-permute-start(bf16[128,256]{1,0:T(8,128)(2,1)S(1)} %get-tuple-element.170), channel_id=1, source_target_pairs={{0,2},{2,0},{1,3},{3,1},{4,6},{6,4},{5,7},{7,5},{8,10},{10,8},{9,1... | collective-permute-start | bytes 196616 | tf_op jit(solution)/shard_map/ppermute | solution.py:410
  49.9 13.0 %collective-permute-start.17 = (bf16[1024,128]{1,0:T(8,128)(2,1)S(1)}, bf16[1024,128]{1,0:T(8,128)(2,1)S(1)}, u32[]{:S(2)}, u32[]{:S(2)}) collective-permute-start(bf16[1024,128]{1,0:T(8,128)(2,1)S(1)} %get-tuple-element.190), channel_id=1, source_target_pairs={{0,2},{1,3},{2,0},{3,1},{4,6},{5,7},{6,4},{7,5},{8,10},{9,11},{10,... | collective-permute-start | bytes 786440 | tf_op jit(solution)/shard_map/ppermute | solution.py:423
  50.8 6.3 %collective-permute-start.16 = (bf16[512,128]{1,0:T(8,128)(2,1)S(1)}, bf16[512,128]{1,0:T(8,128)(2,1)S(1)}, u32[]{:S(2)}, u32[]{:S(2)}) collective-permute-start(bf16[512,128]{1,0:T(8,128)(2,1)S(1)} %get-tuple-element.186), channel_id=1, source_target_pairs={{0,4},{1,5},{2,6},{3,7},{4,0},{5,1},{6,2},{7,3},{8,12},{9,13},{10,... | collective-permute-start | bytes 393224 | tf_op jit(solution)/shard_map/ppermute | solution.py:423
  57.2 6.4 %collective-permute-start.18 = (bf16[1024,128]{1,0:T(8,128)(2,1)S(1)}, bf16[1024,128]{1,0:T(8,128)(2,1)S(1)}, u32[]{:S(2)}, u32[]{:S(2)}) collective-permute-start(bf16[1024,128]{1,0:T(8,128)(2,1)S(1)} %get-tuple-element.192), channel_id=1, source_target_pairs={{0,2},{1,5},{2,0},{3,7},{4,6},{5,1},{6,4},{7,3},{8,10},{9,13},{10,... | collective-permute-start | bytes 786440 | tf_op jit(solution)/shard_map/ppermute | solution.py:423
  58.7 8.6 %collective-permute-start.19 = (bf16[512,128]{1,0:T(8,128)(2,1)S(1)}, bf16[512,128]{1,0:T(8,128)(2,1)S(1)}, u32[]{:S(2)}, u32[]{:S(2)}) collective-permute-start(bf16[512,128]{1,0:T(8,128)(2,1)S(1)} %get-tuple-element.194), channel_id=1, source_target_pairs={{0,8},{1,9},{2,10},{3,11},{4,12},{5,13},{6,14},{7,15},{8,0},{9,1},... | collective-permute-start | bytes 393224 | tf_op jit(solution)/shard_map/ppermute | solution.py:423
  63.1 7.7 %collective-permute-start.20 = (bf16[512,128]{1,0:T(8,128)(2,1)S(1)}, bf16[512,128]{1,0:T(8,128)(2,1)S(1)}, u32[]{:S(2)}, u32[]{:S(2)}) collective-permute-start(bf16[512,128]{1,0:T(8,128)(2,1)S(1)} %get-tuple-element.196), channel_id=1, source_target_pairs={{0,4},{1,5},{2,6},{3,7},{4,0},{5,1},{6,2},{7,3},{8,12},{9,13},{10,... | collective-permute-start | bytes 393224 | tf_op jit(solution)/shard_map/ppermute | solution.py:423
  63.8 8.7 %collective-permute-start.21 = (bf16[512,128]{1,0:T(8,128)(2,1)S(1)}, bf16[512,128]{1,0:T(8,128)(2,1)S(1)}, u32[]{:S(2)}, u32[]{:S(2)}) collective-permute-start(bf16[512,128]{1,0:T(8,128)(2,1)S(1)} %get-tuple-element.198), channel_id=1, source_target_pairs={{0,4},{1,3},{2,6},{3,1},{4,0},{5,7},{6,2},{7,5},{8,12},{9,11},{10,... | collective-permute-start | bytes 393224 | tf_op jit(solution)/shard_map/ppermute | solution.py:423
  67.4 9.5 %collective-permute-start.22 = (bf16[512,128]{1,0:T(8,128)(2,1)S(1)}, bf16[512,128]{1,0:T(8,128)(2,1)S(1)}, u32[]{:S(2)}, u32[]{:S(2)}) collective-permute-start(bf16[512,128]{1,0:T(8,128)(2,1)S(1)} %get-tuple-element.200), channel_id=1, source_target_pairs={{0,4},{1,5},{2,6},{3,7},{4,0},{5,1},{6,2},{7,3},{8,12},{9,13},{10,... | collective-permute-start | bytes 393224 | tf_op jit(solution)/shard_map/ppermute | solution.py:423
  70.8 7.6 %collective-permute-start.23 = (bf16[512,128]{1,0:T(8,128)(2,1)S(1)}, bf16[512,128]{1,0:T(8,128)(2,1)S(1)}, u32[]{:S(2)}, u32[]{:S(2)}) collective-permute-start(bf16[512,128]{1,0:T(8,128)(2,1)S(1)} %get-tuple-element.202), channel_id=1, source_target_pairs={{0,8},{1,9},{2,10},{3,11},{4,12},{5,13},{6,14},{7,15},{8,0},{9,1},... | collective-permute-start | bytes 393224 | tf_op jit(solution)/shard_map/ppermute | solution.py:423
  72.5 8.4 %collective-permute-start.24 = (bf16[512,128]{1,0:T(8,128)(2,1)S(1)}, bf16[512,128]{1,0:T(8,128)(2,1)S(1)}, u32[]{:S(2)}, u32[]{:S(2)}) collective-permute-start(bf16[512,128]{1,0:T(8,128)(2,1)S(1)} %get-tuple-element.204), channel_id=1, source_target_pairs={{0,8},{1,9},{2,10},{3,11},{4,12},{5,13},{6,14},{7,15},{8,0},{9,1},... | collective-permute-start | bytes 393224 | tf_op jit(solution)/shard_map/ppermute | solution.py:423
  77.0 9.2 %collective-permute-start.26 = (bf16[1024,128]{1,0:T(8,128)(2,1)S(1)}, bf16[1024,128]{1,0:T(8,128)(2,1)S(1)}, u32[]{:S(2)}, u32[]{:S(2)}) collective-permute-start(bf16[1024,128]{1,0:T(8,128)(2,1)S(1)} %get-tuple-element.208), channel_id=1, source_target_pairs={{0,2},{1,3},{2,0},{3,1},{4,6},{5,7},{6,4},{7,5},{8,10},{9,11},{10,... | collective-permute-start | bytes 786440 | tf_op jit(solution)/shard_map/ppermute | solution.py:423
  78.5 6.4 %collective-permute-start.25 = (bf16[512,128]{1,0:T(8,128)(2,1)S(1)}, bf16[512,128]{1,0:T(8,128)(2,1)S(1)}, u32[]{:S(2)}, u32[]{:S(2)}) collective-permute-start(bf16[512,128]{1,0:T(8,128)(2,1)S(1)} %get-tuple-element.206), channel_id=1, source_target_pairs={{0,4},{1,5},{2,6},{3,7},{4,0},{5,1},{6,2},{7,3},{8,12},{9,13},{10,... | collective-permute-start | bytes 393224 | tf_op jit(solution)/shard_map/ppermute | solution.py:423
  81.0 6.7 %collective-permute-start.27 = (bf16[512,128]{1,0:T(8,128)(2,1)S(1)}, bf16[512,128]{1,0:T(8,128)(2,1)S(1)}, u32[]{:S(2)}, u32[]{:S(2)}) collective-permute-start(bf16[512,128]{1,0:T(8,128)(2,1)S(1)} %get-tuple-element.209), channel_id=1, source_target_pairs={{0,4},{1,3},{2,6},{3,1},{4,0},{5,7},{6,2},{7,5},{8,12},{9,11},{10,... | collective-permute-start | bytes 393224 | tf_op jit(solution)/shard_map/ppermute | solution.py:423
  84.9 7.3 %collective-permute-start.28 = (bf16[1024,128]{1,0:T(8,128)(2,1)S(1)}, bf16[1024,128]{1,0:T(8,128)(2,1)S(1)}, u32[]{:S(2)}, u32[]{:S(2)}) collective-permute-start(bf16[1024,128]{1,0:T(8,128)(2,1)S(1)} %get-tuple-element.214), channel_id=1, source_target_pairs={{0,2},{1,3},{2,0},{3,1},{4,6},{5,7},{6,4},{7,5},{8,10},{9,11},{10,... | collective-permute-start | bytes 786440 | tf_op jit(solution)/shard_map/ppermute | solution.py:423
  87.7 8.3 %collective-permute-start.31 = (bf16[1024,128]{1,0:T(8,128)(2,1)S(1)}, bf16[1024,128]{1,0:T(8,128)(2,1)S(1)}, u32[]{:S(2)}, u32[]{:S(2)}) collective-permute-start(bf16[1024,128]{1,0:T(8,128)(2,1)S(1)} %get-tuple-element.226), channel_id=1, source_target_pairs={{0,2},{1,5},{2,0},{3,7},{4,6},{5,1},{6,4},{7,3},{8,10},{9,13},{10,... | collective-permute-start | bytes 786440 | tf_op jit(solution)/shard_map/ppermute | solution.py:423
  88.1 6.1 %collective-permute-start.29 = (bf16[128,256]{1,0:T(8,128)(2,1)S(1)}, bf16[128,256]{1,0:T(8,128)(2,1)S(1)}, u32[]{:S(2)}, u32[]{:S(2)}) collective-permute-start(bf16[128,256]{1,0:T(8,128)(2,1)S(1)} %get-tuple-element.220), channel_id=1, source_target_pairs={{4,0},{8,4},{12,8},{5,1},{9,5},{13,9},{6,2},{10,6},{14,10},{7,3},{... | collective-permute-start | bytes 196616 | tf_op jit(solution)/shard_map/ppermute | solution.py:446
  89.4 5.5 %collective-permute-start.30 = (bf16[128,256]{1,0:T(8,128)(2,1)S(1)}, bf16[128,256]{1,0:T(8,128)(2,1)S(1)}, u32[]{:S(2)}, u32[]{:S(2)}) collective-permute-start(bf16[128,256]{1,0:T(8,128)(2,1)S(1)} %get-tuple-element.221), channel_id=1, source_target_pairs={{0,2},{2,0},{1,3},{3,1},{4,6},{6,4},{5,7},{7,5},{8,10},{10,8},{9,1... | collective-permute-start | bytes 196616 | tf_op jit(solution)/shard_map/ppermute | solution.py:410
  (6 other events, 25.7 us)

commit v16 on v15

--- a/solution.py
+++ b/solution.py
@@ -646,14 +646,15 @@
         for layer in reversed(range(layers)):
             if sums[layer].done < count:
                 if layer == 0 and sums[0].done == count - 1:
-                    at = at + [sums[above].got[0] for above in range(2, layers)]
+                    at = at + returned[0] + [sums[above].got[0] for above in range(2, layers)]
                 at = sum_step([sums[layer]], at)
+    grad, token = join(0, state, at)
+    at = [token]
     written = []
     for layer in reversed(range(1, layers)):
         *written, token = write(layer, written, at)
         at = [token]
     *written, token = write(0, written, at, (0,))
-    grad, token = join(0, state, [token])
     *written, token = write(0, written, [token], (1,))
     return (grad, *written)
 

time: 97.9 us -> 96.8 us (0.989)
    ppermute x18, waiting for transfers between devices: 15.4 us -> 12.2 us  [over_mesh(): return lax.ppermute(x, ('chain', 'basin', 'feat'), perm)]
    ppermute x3, waiting for transfers between devices: 2.63 us -> 5.73 us  [backward(): up = lax.ppermute(grads[0], 'chain', [(c, c - 1) for c in range(1, chain)])]
  transfers between devices with their start and end apart: 32 -> 32, of which waited for: 14 -> 13; matrix products, arithmetic and copies ran while one was open for 1% -> 1% of each run, Pallas kernels for 26% -> 26%
where the time goes in v16:
time: 96.8 us; the launch traced here: 96.6 us
  starting transfers between devices  41.3 us (43%)
  Pallas kernels  30.6 us (32%)
  waiting for transfers between devices  21.4 us (22%)
  between operations  1.26 us (1%)
  local copies, waits for them, and re-layouts  1.2 us (1%)
    ppermute x18, starting transfers between devices, over_mesh(): return lax.ppermute(x, ('chain', 'basin', 'feat'), perm)  29.9 us
    pallas_call x33, Pallas kernels, call(): pl.pallas_call(lambda *refs: body(*refs[skipped:]), out_shape=[jax.ShapeD...  26.2 us
    ppermute x18, waiting for transfers between devices, over_mesh(): return lax.ppermute(x, ('chain', 'basin', 'feat'), perm)  12.2 us
    ppermute x11, starting transfers between devices, around(): return lax.ppermute(x, axis, [(i, (i + distance) % n) for i in range(n)])  7.32 us
    ppermute x3, waiting for transfers between devices, backward(): up = lax.ppermute(grads[0], 'chain', [(c, c - 1) for c in range(1, chain)])  5.73 us
    pallas_call x4, Pallas kernels, write(): pl.pallas_call(functools.partial(write_kernel, layer, sums[layer].stages[...  4.44 us
    ppermute x3, starting transfers between devices, backward(): up = lax.ppermute(grads[0], 'chain', [(c, c - 1) for c in range(1, chain)])  4.1 us
    ppermute x11, waiting for transfers between devices, around(): return lax.ppermute(x, axis, [(i, (i + distance) % n) for i in range(n)])  3.53 us
  transfers between devices with their start and end apart: 32, of which 13 were waited for; matrix products, arithmetic and copies ran while one was open for 1% of the time, Pallas kernels for 26%

profile of v16, /device:TPU:0, one launch (start us, length us, event | category | flops | bytes accessed | tf_op | source)
XLA Modules:
  0.0 96.6 jit_solution(15414541088704724017)
XLA Ops:
  3.3 4.9 %collective-permute-start = (bf16[128,256]{1,0:T(8,128)(2,1)S(1)}, bf16[128,256]{1,0:T(8,128)(2,1)S(1)}, u32[]{:S(2)}, u32[]{:S(2)}) collective-permute-start(bf16[128,256]{1,0:T(8,128)(2,1)S(1)} %get-tuple-element.117), channel_id=1, source_target_pairs={{0,4},{2,6},{5,9},{7,11},{8,12},{10,14},{16,20},{18,22},{21,25},{2... | collective-permute-start | bytes 196616 | tf_op jit(solution)/shard_map/ppermute | solution.py:423
  8.2 1.6 %collective-permute-start.3 = (bf16[128,256]{1,0:T(8,128)(2,1)S(1)}, bf16[128,256]{1,0:T(8,128)(2,1)S(1)}, u32[]{:S(2)}, u32[]{:S(2)}) collective-permute-start(bf16[128,256]{1,0:T(8,128)(2,1)S(1)} %get-tuple-element.124), channel_id=1, source_target_pairs={{0,2},{2,0},{1,3},{3,1},{4,6},{6,4},{5,7},{7,5},{8,10},{10,8},{9,1... | collective-permute-start | bytes 196616 | tf_op jit(solution)/shard_map/ppermute | solution.py:410
  11.8 1.6 %adjacency.1 = (bf16[768,768]{1,0:T(8,128)(2,1)S(1)}, bf16[768,768]{1,0:T(8,128)(2,1)S(1)}, bf16[768,256]{1,0:T(8,128)(2,1)S(1)}, bf16[256,768]{1,0:T(8,128)(2,1)S(1)}) custom-call(s32[4,6]{1,0:T(4,128)S(1)} %bitcast.4, bf16[6,4,128,128]{3,2,1,0:T(8,128)(2,1)S(1)} %copy-done.3, bf16[128,768]{1,0:T(8,128)(2,1)S(1)} %get-tuple-element.118.refs_2_, ...), custom_call_target="tpu_custom_call" | custom-call | flops 150994944 | bytes 4000000 | tf_op jit(solution)/shard_map/adjacency/pallas_call | solution.py:32
  15.8 2.8 %collective-permute-start.5 = (bf16[128,256]{1,0:T(8,128)(2,1)S(1)}, bf16[128,256]{1,0:T(8,128)(2,1)S(1)}, u32[]{:S(2)}, u32[]{:S(2)}) collective-permute-start(bf16[128,256]{1,0:T(8,128)(2,1)S(1)} %get-tuple-element.128), channel_id=1, source_target_pairs={{0,4},{2,6},{5,9},{7,11},{8,12},{10,14},{16,20},{18,22},{21,25},{2... | collective-permute-start | bytes 196616 | tf_op jit(solution)/shard_map/ppermute | solution.py:423
  19.1 1.6 %local1.1 = (bf16[768,256]{1,0:T(8,128)(2,1)S(1)}, bf16[768,512]{1,0:T(8,128)(2,1)S(1)}, bf16[768,512]{1,0:T(8,128)(2,1)S(1)}, bf16[512,768]{1,0:T(8,128)(2,1)S(1)}, bf16[256,768]{1,0:T(8,128)(2,1)S(1)}) custom-call(bf16[768,256]{1,0:T(8,128)(2,1)S(1)} %get-tuple-element.129.refs_0_, bf16[3,256,512]{2,1,0:T(8,128)(2,1)S(1)} %copy-done, ...), custom_call_target="tpu_custom_call" | custom-call | flops 805306368 | bytes 4000000 | tf_op jit(solution)/shard_map/local1/pallas_call | solution.py:32
  20.8 2.0 %collective-permute-done.6.refs_7_.refs_14_ = bf16[128,256]{1,0:T(8,128)(2,1)S(1)} collective-permute-done((bf16[128,256]{1,0:T(8,128)(2,1)S(1)}, bf16[128,256]{1,0:T(8,128)(2,1)S(1)}, u32[]{:S(2)}, u32[]{:S(2)}) %collective-permute-start.6) | collective-permute-done | bytes 65568 | tf_op jit(solution)/shard_map/ppermute | solution.py:410
  24.9 2.3 %collective-permute-start.8 = (bf16[128,256]{1,0:T(8,128)(2,1)S(1)}, bf16[128,256]{1,0:T(8,128)(2,1)S(1)}, u32[]{:S(2)}, u32[]{:S(2)}) collective-permute-start(bf16[128,256]{1,0:T(8,128)(2,1)S(1)} %get-tuple-element.135), channel_id=1, source_target_pairs={{0,4},{2,6},{5,9},{7,11},{8,12},{10,14},{16,20},{18,22},{21,25},{2... | collective-permute-start | bytes 196616 | tf_op jit(solution)/shard_map/ppermute | solution.py:423
  27.2 1.4 %collective-permute-start.9 = (bf16[128,256]{1,0:T(8,128)(2,1)S(1)}, bf16[128,256]{1,0:T(8,128)(2,1)S(1)}, u32[]{:S(2)}, u32[]{:S(2)}) collective-permute-start(bf16[128,256]{1,0:T(8,128)(2,1)S(1)} %get-tuple-element.139), channel_id=1, source_target_pairs={{0,2},{2,0},{1,3},{3,1},{4,6},{6,4},{5,7},{7,5},{8,10},{10,8},{9,1... | collective-permute-start | bytes 196616 | tf_op jit(solution)/shard_map/ppermute | solution.py:410
  28.6 1.6 %local2.1 = (bf16[768,256]{1,0:T(8,128)(2,1)S(1)}, bf16[768,512]{1,0:T(8,128)(2,1)S(1)}, bf16[768,512]{1,0:T(8,128)(2,1)S(1)}, bf16[512,768]{1,0:T(8,128)(2,1)S(1)}, bf16[256,768]{1,0:T(8,128)(2,1)S(1)}) custom-call(bf16[768,256]{1,0:T(8,128)(2,1)S(1)} %get-tuple-element.136.refs_0_, bf16[3,256,512]{2,1,0:T(8,128)(2,1)S(1)} %copy-done, ...), custom_call_target="tpu_custom_call" | custom-call | flops 805306368 | bytes 4000000 | tf_op jit(solution)/shard_map/local2/pallas_call | solution.py:32
  32.5 2.0 %turn.1 = (f32[768,256]{1,0:T(8,128)S(1)}, bf16[768,256]{1,0:T(8,128)(2,1)S(1)}, bf16[256,256]{1,0:T(8,128)(2,1)S(1)}, bf16[256,256]{1,0:T(8,128)(2,1)S(1)}, bf1...) custom-call(f32[768,256]{1,0:T(8,128)S(1)} %get-tuple-element.134.re, ...), custom_call_target="tpu_custom_call" | custom-call | flops 536870912 | bytes 4000000 | tf_op jit(solution)/shard_map/turn/pallas_call | solution.py:32
  35.8 1.4 %collective-permute-start.12 = (bf16[128,256]{1,0:T(8,128)(2,1)S(1)}, bf16[128,256]{1,0:T(8,128)(2,1)S(1)}, u32[]{:S(2)}, u32[]{:S(2)}) collective-permute-start(bf16[128,256]{1,0:T(8,128)(2,1)S(1)} %get-tuple-element.154), channel_id=1, source_target_pairs={{0,2},{2,0},{1,3},{3,1},{4,6},{6,4},{5,7},{7,5},{8,10},{10,8},{9,1... | collective-permute-start | bytes 196616 | tf_op jit(solution)/shard_map/ppermute | solution.py:410
  37.2 2.4 %back2.1 = (f32[768,256]{1,0:T(8,128)S(1)}, f32[2048,128]{1,0:T(8,128)S(1)}) custom-call(bf16[768,256]{1,0:T(8,128)(2,1)S(1)} %get-tuple-element.142.refs_0_, bf16[768,768]{1,0:T(8,128)(2,1)S(1)} %get-tuple-element.143.refs_1_.refs_2_, bf16[768,512]{1,0:T(8,128)(2,1)S(1)} %get-tuple-element.144.refs_2_, bf16[768,512]{1,0:T(8,128)(2,1)S(1)} %get-tuple-element.145.refs_3_, ...), custom_call_target="tpu_custom_call" | custom-call | flops 2717908992 | bytes 4000000 | tf_op jit(solution)/shard_map/back2/pallas_call | solution.py:32
  40.8 1.4 %collective-permute-start.15 = (bf16[1024,128]{1,0:T(8,128)(2,1)S(1)}, bf16[1024,128]{1,0:T(8,128)(2,1)S(1)}, u32[]{:S(2)}, u32[]{:S(2)}) collective-permute-start(bf16[1024,128]{1,0:T(8,128)(2,1)S(1)} %get-tuple-element.173), channel_id=1, source_target_pairs={{0,2},{1,3},{2,0},{3,1},{4,6},{5,7},{6,4},{7,5},{8,10},{9,11},{10,... | collective-permute-start | bytes 786440 | tf_op jit(solution)/shard_map/ppermute | solution.py:423
  42.1 1.5 %join2.1 = (f32[768,256]{1,0:T(8,128)S(1)}, bf16[768,256]{1,0:T(8,128)(2,1)S(1)}, bf16[256,256]{1,0:T(8,128)(2,1)S(1)}, bf16[256,256]{1,0:T(8,128)(2,1)S(1)}, bf...) custom-call(f32[1024,128]{1,0:T(8,128)S(1)} %get-tuple-element.156.r, ...), custom_call_target="tpu_custom_call" | custom-call | flops 536870912 | bytes 4000000 | tf_op jit(solution)/shard_map/join2/pallas_call | solution.py:32
  43.6 1.5 %collective-permute-start.13 = (bf16[128,256]{1,0:T(8,128)(2,1)S(1)}, bf16[128,256]{1,0:T(8,128)(2,1)S(1)}, u32[]{:S(2)}, u32[]{:S(2)}) collective-permute-start(bf16[128,256]{1,0:T(8,128)(2,1)S(1)} %get-tuple-element.169), channel_id=1, source_target_pairs={{4,0},{8,4},{12,8},{5,1},{9,5},{13,9},{6,2},{10,6},{14,10},{7,3},{... | collective-permute-start | bytes 196616 | tf_op jit(solution)/shard_map/ppermute | solution.py:446
  45.9 2.4 %back1.1 = (f32[768,256]{1,0:T(8,128)S(1)}, f32[2048,128]{1,0:T(8,128)S(1)}) custom-call(bf16[768,256]{1,0:T(8,128)(2,1)S(1)} %get-tuple-element.159.refs_0_.refs_1_, bf16[768,256]{1,0:T(8,128)(2,1)S(1)} %get-tuple-element.159.refs_0_.refs_1_, bf16[768,768]{1,0:T(8,128)(2,1)S(1)} %get-tuple-element.143.refs_1_.refs_2_, ...), custom_call_target="tpu_custom_call" | custom-call | flops 2717908992 | bytes 4000000 | tf_op jit(solution)/shard_map/back1/pallas_call | solution.py:32
  48.3 1.5 %collective-permute-done.13.refs_1_.refs_10_ = bf16[128,256]{1,0:T(8,128)(2,1)S(1)} collective-permute-done((bf16[128,256]{1,0:T(8,128)(2,1)S(1)}, bf16[128,256]{1,0:T(8,128)(2,1)S(1)}, u32[]{:S(2)}, u32[]{:S(2)}) %collective-permute-start.13) | collective-permute-done | bytes 65568 | tf_op jit(solution)/shard_map/ppermute | solution.py:446
  50.8 2.4 %collective-permute-start.16 = (bf16[512,128]{1,0:T(8,128)(2,1)S(1)}, bf16[512,128]{1,0:T(8,128)(2,1)S(1)}, u32[]{:S(2)}, u32[]{:S(2)}) collective-permute-start(bf16[512,128]{1,0:T(8,128)(2,1)S(1)} %get-tuple-element.186), channel_id=1, source_target_pairs={{0,4},{1,5},{2,6},{3,7},{4,0},{5,1},{6,2},{7,3},{8,12},{9,13},{10,... | collective-permute-start | bytes 393224 | tf_op jit(solution)/shard_map/ppermute | solution.py:423
  53.2 1.5 %join1.1 = (f32[768,256]{1,0:T(8,128)S(1)}, bf16[768,256]{1,0:T(8,128)(2,1)S(1)}, bf16[256,256]{1,0:T(8,128)(2,1)S(1)}, bf16[256,256]{1,0:T(8,128)(2,1)S(1)}, bf...) custom-call(f32[512,128]{1,0:T(8,128)S(1)} %get-tuple-element.174.re, ...), custom_call_target="tpu_custom_call" | custom-call | flops 536870912 | bytes 4000000 | tf_op jit(solution)/shard_map/join1/pallas_call | solution.py:32
  54.7 2.4 %back0.1 = (f32[768,256]{1,0:T(8,128)S(1)}, f32[2048,128]{1,0:T(8,128)S(1)}) custom-call(bf16[768,256]{1,0:T(8,128)(2,1)S(1)} %get-tuple-element.176.refs_0_.refs_1_, bf16[768,256]{1,0:T(8,128)(2,1)S(1)} %get-tuple-element.176.refs_0_.refs_1_, bf16[768,768]{1,0:T(8,128)(2,1)S(1)} %get-tuple-element.143.refs_1_.refs_2_, ...), custom_call_target="tpu_custom_call" | custom-call | flops 2717908992 | bytes 4000000 | tf_op jit(solution)/shard_map/back0/pallas_call | solution.py:32
  57.2 1.5 %collective-permute-start.18 = (bf16[1024,128]{1,0:T(8,128)(2,1)S(1)}, bf16[1024,128]{1,0:T(8,128)(2,1)S(1)}, u32[]{:S(2)}, u32[]{:S(2)}) collective-permute-start(bf16[1024,128]{1,0:T(8,128)(2,1)S(1)} %get-tuple-element.192), channel_id=1, source_target_pairs={{0,2},{1,5},{2,0},{3,7},{4,6},{5,1},{6,4},{7,3},{8,10},{9,13},{10,... | collective-permute-start | bytes 786440 | tf_op jit(solution)/shard_map/ppermute | solution.py:423
  58.7 4.2 %collective-permute-start.19 = (bf16[512,128]{1,0:T(8,128)(2,1)S(1)}, bf16[512,128]{1,0:T(8,128)(2,1)S(1)}, u32[]{:S(2)}, u32[]{:S(2)}) collective-permute-start(bf16[512,128]{1,0:T(8,128)(2,1)S(1)} %get-tuple-element.194), channel_id=1, source_target_pairs={{0,8},{1,9},{2,10},{3,11},{4,12},{5,13},{6,14},{7,15},{8,0},{9,1},... | collective-permute-start | bytes 393224 | tf_op jit(solution)/shard_map/ppermute | solution.py:423
  63.8 3.6 %collective-permute-start.21 = (bf16[512,128]{1,0:T(8,128)(2,1)S(1)}, bf16[512,128]{1,0:T(8,128)(2,1)S(1)}, u32[]{:S(2)}, u32[]{:S(2)}) collective-permute-start(bf16[512,128]{1,0:T(8,128)(2,1)S(1)} %get-tuple-element.198), channel_id=1, source_target_pairs={{0,4},{1,3},{2,6},{3,1},{4,0},{5,7},{6,2},{7,5},{8,12},{9,11},{10,... | collective-permute-start | bytes 393224 | tf_op jit(solution)/shard_map/ppermute | solution.py:423
  68.1 2.7 %collective-permute-done.20.refs_2_ = bf16[512,128]{1,0:T(8,128)(2,1)S(1)} collective-permute-done((bf16[512,128]{1,0:T(8,128)(2,1)S(1)}, bf16[512,128]{1,0:T(8,128)(2,1)S(1)}, u32[]{:S(2)}, u32[]{:S(2)}) %collective-permute-start.20) | collective-permute-done | bytes 131104 | tf_op jit(solution)/shard_map/ppermute | solution.py:423
  71.1 1.4 %collective-permute-done.21.refs_2_ = bf16[512,128]{1,0:T(8,128)(2,1)S(1)} collective-permute-done((bf16[512,128]{1,0:T(8,128)(2,1)S(1)}, bf16[512,128]{1,0:T(8,128)(2,1)S(1)}, u32[]{:S(2)}, u32[]{:S(2)}) %collective-permute-start.21) | collective-permute-done | bytes 131104 | tf_op jit(solution)/shard_map/ppermute | solution.py:423
  72.5 1.8 %collective-permute-start.24 = (bf16[512,128]{1,0:T(8,128)(2,1)S(1)}, bf16[512,128]{1,0:T(8,128)(2,1)S(1)}, u32[]{:S(2)}, u32[]{:S(2)}) collective-permute-start(bf16[512,128]{1,0:T(8,128)(2,1)S(1)} %get-tuple-element.204), channel_id=1, source_target_pairs={{0,8},{1,9},{2,10},{3,11},{4,12},{5,13},{6,14},{7,15},{8,0},{9,1},... | collective-permute-start | bytes 393224 | tf_op jit(solution)/shard_map/ppermute | solution.py:423
  74.3 2.6 %collective-permute-done.22.refs_2_ = bf16[512,128]{1,0:T(8,128)(2,1)S(1)} collective-permute-done((bf16[512,128]{1,0:T(8,128)(2,1)S(1)}, bf16[512,128]{1,0:T(8,128)(2,1)S(1)}, u32[]{:S(2)}, u32[]{:S(2)}) %collective-permute-start.22) | collective-permute-done | bytes 131104 | tf_op jit(solution)/shard_map/ppermute | solution.py:423
  76.9 1.5 %collective-permute-start.28 = (bf16[1024,128]{1,0:T(8,128)(2,1)S(1)}, bf16[1024,128]{1,0:T(8,128)(2,1)S(1)}, u32[]{:S(2)}, u32[]{:S(2)}) collective-permute-start(bf16[1024,128]{1,0:T(8,128)(2,1)S(1)} %get-tuple-element.210), channel_id=1, source_target_pairs={{0,2},{1,3},{2,0},{3,1},{4,6},{5,7},{6,4},{7,5},{8,10},{9,11},{10,... | collective-permute-start | bytes 786440 | tf_op jit(solution)/shard_map/ppermute | solution.py:423
  78.6 3.0 %collective-permute-done.24.refs_2_ = bf16[512,128]{1,0:T(8,128)(2,1)S(1)} collective-permute-done((bf16[512,128]{1,0:T(8,128)(2,1)S(1)}, bf16[512,128]{1,0:T(8,128)(2,1)S(1)}, u32[]{:S(2)}, u32[]{:S(2)}) %collective-permute-start.24) | collective-permute-done | bytes 131104 | tf_op jit(solution)/shard_map/ppermute | solution.py:423
  85.3 3.1 %collective-permute-done.26.refs_1_.refs_4_ = bf16[128,256]{1,0:T(8,128)(2,1)S(1)} collective-permute-done((bf16[128,256]{1,0:T(8,128)(2,1)S(1)}, bf16[128,256]{1,0:T(8,128)(2,1)S(1)}, u32[]{:S(2)}, u32[]{:S(2)}) %collective-permute-start.26) | collective-permute-done | bytes 65568 | tf_op jit(solution)/shard_map/ppermute | solution.py:446
  93.3 1.6 %collective-permute-done.31.refs_3_ = bf16[1024,128]{1,0:T(8,128)(2,1)S(1)} collective-permute-done((bf16[1024,128]{1,0:T(8,128)(2,1)S(1)}, bf16[1024,128]{1,0:T(8,128)(2,1)S(1)}, u32[]{:S(2)}, u32[]{:S(2)}) %collective-permute-start.31) | collective-permute-done | bytes 262176 | tf_op jit(solution)/shard_map/ppermute | solution.py:423
  94.9 1.4 %write0.3 = (f32[3,256,512]{2,1,0:T(8,128)}, f32[3,512,256]{2,1,0:T(8,128)}, f32[8,128]{1,0:T(8,128)}) custom-call(f32[3,256,512]{2,1,0:T(8,128)} %get-tuple-element.223.refs_0_, f32[3,512,256]{2,1,0:T(8,128)} %get-tuple-element.224.refs_1_, f32[8,128]{1,0:T(8,128)S(1)} %get-tuple-element.225.refs_2_, ...), custom_call_target="tpu_custom_call", output_to_operand_aliasing={{0}: (0, {}), {1}: (1, {})} | custom-call | flops 1 | bytes 1 | tf_op jit(solution)/shard_map/write0/pallas_call | solution.py:606
  (82 shorter events, 27.0 us)
Async XLA Ops:
  0.7 9.1 %collective-permute-start.1 = (bf16[3,256,512]{2,1,0:T(8,128)(2,1)}, bf16[3,256,512]{2,1,0:T(8,128)(2,1)S(1)}, u32[]{:S(2)}, u32[]{:S(2)}) collective-permute-start(bf16[3,256,512]{2,1,0:T(8,128)(2,1)} %refs_7_.5), channel_id=1, source_target_pairs={{0,1},{1,0},{2,3},{3,2},{4,5},{5,4},{6,7},{7,6},{8,9},{9,8},{10,11... | collective-permute-start | bytes 2359304 | tf_op jit(solution)/shard_map/ppermute | solution.py:410
  1.2 8.6 %collective-permute-start.2 = (bf16[3,512,256]{2,1,0:T(8,128)(2,1)}, bf16[3,512,256]{2,1,0:T(8,128)(2,1)S(1)}, u32[]{:S(2)}, u32[]{:S(2)}) collective-permute-start(bf16[3,512,256]{2,1,0:T(8,128)(2,1)} %refs_9_.3), channel_id=1, source_target_pairs={{0,1},{1,0},{2,3},{3,2},{4,5},{5,4},{6,7},{7,6},{8,9},{9,8},{10,11... | collective-permute-start | bytes 2359304 | tf_op jit(solution)/shard_map/ppermute | solution.py:410
  3.3 10.1 %collective-permute-start = (bf16[128,256]{1,0:T(8,128)(2,1)S(1)}, bf16[128,256]{1,0:T(8,128)(2,1)S(1)}, u32[]{:S(2)}, u32[]{:S(2)}) collective-permute-start(bf16[128,256]{1,0:T(8,128)(2,1)S(1)} %get-tuple-element.117), channel_id=1, source_target_pairs={{0,4},{2,6},{5,9},{7,11},{8,12},{10,14},{16,20},{18,22},{21,25},{2... | collective-permute-start | bytes 196616 | tf_op jit(solution)/shard_map/ppermute | solution.py:423
  8.2 5.2 %collective-permute-start.3 = (bf16[128,256]{1,0:T(8,128)(2,1)S(1)}, bf16[128,256]{1,0:T(8,128)(2,1)S(1)}, u32[]{:S(2)}, u32[]{:S(2)}) collective-permute-start(bf16[128,256]{1,0:T(8,128)(2,1)S(1)} %get-tuple-element.124), channel_id=1, source_target_pairs={{0,2},{2,0},{1,3},{3,1},{4,6},{6,4},{5,7},{7,5},{8,10},{10,8},{9,1... | collective-permute-start | bytes 196616 | tf_op jit(solution)/shard_map/ppermute | solution.py:410
  13.4 1.3 %collective-permute-start.4 = (bf16[128,256]{1,0:T(8,128)(2,1)S(1)}, bf16[128,256]{1,0:T(8,128)(2,1)S(1)}, u32[]{:S(2)}, u32[]{:S(2)}) collective-permute-start(bf16[128,256]{1,0:T(8,128)(2,1)S(1)} %collective-permute-done.refs_8_.refs_12_), channel_id=1, source_target_pairs={{0,1},{1,0},{2,3},{3,2},{4,5},{5,4},{6,7},{7,6},{8,9},{9,8},{10,11... | collective-permute-start | bytes 196616 | tf_op jit(solution)/shard_map/ppermute | solution.py:410
  15.8 5.0 %collective-permute-start.5 = (bf16[128,256]{1,0:T(8,128)(2,1)S(1)}, bf16[128,256]{1,0:T(8,128)(2,1)S(1)}, u32[]{:S(2)}, u32[]{:S(2)}) collective-permute-start(bf16[128,256]{1,0:T(8,128)(2,1)S(1)} %get-tuple-element.128), channel_id=1, source_target_pairs={{0,4},{2,6},{5,9},{7,11},{8,12},{10,14},{16,20},{18,22},{21,25},{2... | collective-permute-start | bytes 196616 | tf_op jit(solution)/shard_map/ppermute | solution.py:423
  18.5 4.3 %collective-permute-start.6 = (bf16[128,256]{1,0:T(8,128)(2,1)S(1)}, bf16[128,256]{1,0:T(8,128)(2,1)S(1)}, u32[]{:S(2)}, u32[]{:S(2)}) collective-permute-start(bf16[128,256]{1,0:T(8,128)(2,1)S(1)} %get-tuple-element.132), channel_id=1, source_target_pairs={{0,2},{2,0},{1,3},{3,1},{4,6},{6,4},{5,7},{7,5},{8,10},{10,8},{9,1... | collective-permute-start | bytes 196616 | tf_op jit(solution)/shard_map/ppermute | solution.py:410
  20.8 3.1 %collective-permute-start.7 = (bf16[128,256]{1,0:T(8,128)(2,1)S(1)}, bf16[128,256]{1,0:T(8,128)(2,1)S(1)}, u32[]{:S(2)}, u32[]{:S(2)}) collective-permute-start(bf16[128,256]{1,0:T(8,128)(2,1)S(1)} %collective-permute-done.5.refs_8_.refs_12_), channel_id=1, source_target_pairs={{0,1},{1,0},{2,3},{3,2},{4,5},{5,4},{6,7},{7,6},{8,9},{9,8},{10,11... | collective-permute-start | bytes 196616 | tf_op jit(solution)/shard_map/ppermute | solution.py:410
  24.9 5.2 %collective-permute-start.8 = (bf16[128,256]{1,0:T(8,128)(2,1)S(1)}, bf16[128,256]{1,0:T(8,128)(2,1)S(1)}, u32[]{:S(2)}, u32[]{:S(2)}) collective-permute-start(bf16[128,256]{1,0:T(8,128)(2,1)S(1)} %get-tuple-element.135), channel_id=1, source_target_pairs={{0,4},{2,6},{5,9},{7,11},{8,12},{10,14},{16,20},{18,22},{21,25},{2... | collective-permute-start | bytes 196616 | tf_op jit(solution)/shard_map/ppermute | solution.py:423
  27.2 4.3 %collective-permute-start.9 = (bf16[128,256]{1,0:T(8,128)(2,1)S(1)}, bf16[128,256]{1,0:T(8,128)(2,1)S(1)}, u32[]{:S(2)}, u32[]{:S(2)}) collective-permute-start(bf16[128,256]{1,0:T(8,128)(2,1)S(1)} %get-tuple-element.139), channel_id=1, source_target_pairs={{0,2},{2,0},{1,3},{3,1},{4,6},{6,4},{5,7},{7,5},{8,10},{10,8},{9,1... | collective-permute-start | bytes 196616 | tf_op jit(solution)/shard_map/ppermute | solution.py:410
  30.2 2.3 %collective-permute-start.10 = (bf16[128,256]{1,0:T(8,128)(2,1)S(1)}, bf16[128,256]{1,0:T(8,128)(2,1)S(1)}, u32[]{:S(2)}, u32[]{:S(2)}) collective-permute-start(bf16[128,256]{1,0:T(8,128)(2,1)S(1)} %collective-permute-done.8.refs_9_), channel_id=1, source_target_pairs={{0,1},{1,0},{2,3},{3,2},{4,5},{5,4},{6,7},{7,6},{8,9},{9,8},{10,11... | collective-permute-start | bytes 196616 | tf_op jit(solution)/shard_map/ppermute | solution.py:410
  34.5 6.2 %collective-permute-start.11 = (bf16[128,256]{1,0:T(8,128)(2,1)S(1)}, bf16[128,256]{1,0:T(8,128)(2,1)S(1)}, u32[]{:S(2)}, u32[]{:S(2)}) collective-permute-start(bf16[128,256]{1,0:T(8,128)(2,1)S(1)} %get-tuple-element.153), channel_id=1, source_target_pairs={{4,0},{8,4},{12,8},{5,1},{9,5},{13,9},{6,2},{10,6},{14,10},{7,3},{... | collective-permute-start | bytes 196616 | tf_op jit(solution)/shard_map/ppermute | solution.py:446
  35.8 4.9 %collective-permute-start.12 = (bf16[128,256]{1,0:T(8,128)(2,1)S(1)}, bf16[128,256]{1,0:T(8,128)(2,1)S(1)}, u32[]{:S(2)}, u32[]{:S(2)}) collective-permute-start(bf16[128,256]{1,0:T(8,128)(2,1)S(1)} %get-tuple-element.154), channel_id=1, source_target_pairs={{0,2},{2,0},{1,3},{3,1},{4,6},{6,4},{5,7},{7,5},{8,10},{10,8},{9,1... | collective-permute-start | bytes 196616 | tf_op jit(solution)/shard_map/ppermute | solution.py:410
  40.8 10.0 %collective-permute-start.15 = (bf16[1024,128]{1,0:T(8,128)(2,1)S(1)}, bf16[1024,128]{1,0:T(8,128)(2,1)S(1)}, u32[]{:S(2)}, u32[]{:S(2)}) collective-permute-start(bf16[1024,128]{1,0:T(8,128)(2,1)S(1)} %get-tuple-element.173), channel_id=1, source_target_pairs={{0,2},{1,3},{2,0},{3,1},{4,6},{5,7},{6,4},{7,5},{8,10},{9,11},{10,... | collective-permute-start | bytes 786440 | tf_op jit(solution)/shard_map/ppermute | solution.py:423
  43.6 6.3 %collective-permute-start.13 = (bf16[128,256]{1,0:T(8,128)(2,1)S(1)}, bf16[128,256]{1,0:T(8,128)(2,1)S(1)}, u32[]{:S(2)}, u32[]{:S(2)}) collective-permute-start(bf16[128,256]{1,0:T(8,128)(2,1)S(1)} %get-tuple-element.169), channel_id=1, source_target_pairs={{4,0},{8,4},{12,8},{5,1},{9,5},{13,9},{6,2},{10,6},{14,10},{7,3},{... | collective-permute-start | bytes 196616 | tf_op jit(solution)/shard_map/ppermute | solution.py:446
  45.1 4.7 %collective-permute-start.14 = (bf16[128,256]{1,0:T(8,128)(2,1)S(1)}, bf16[128,256]{1,0:T(8,128)(2,1)S(1)}, u32[]{:S(2)}, u32[]{:S(2)}) collective-permute-start(bf16[128,256]{1,0:T(8,128)(2,1)S(1)} %get-tuple-element.170), channel_id=1, source_target_pairs={{0,2},{2,0},{1,3},{3,1},{4,6},{6,4},{5,7},{7,5},{8,10},{10,8},{9,1... | collective-permute-start | bytes 196616 | tf_op jit(solution)/shard_map/ppermute | solution.py:410
  49.9 13.0 %collective-permute-start.17 = (bf16[1024,128]{1,0:T(8,128)(2,1)S(1)}, bf16[1024,128]{1,0:T(8,128)(2,1)S(1)}, u32[]{:S(2)}, u32[]{:S(2)}) collective-permute-start(bf16[1024,128]{1,0:T(8,128)(2,1)S(1)} %get-tuple-element.190), channel_id=1, source_target_pairs={{0,2},{1,3},{2,0},{3,1},{4,6},{5,7},{6,4},{7,5},{8,10},{9,11},{10,... | collective-permute-start | bytes 786440 | tf_op jit(solution)/shard_map/ppermute | solution.py:423
  50.8 6.3 %collective-permute-start.16 = (bf16[512,128]{1,0:T(8,128)(2,1)S(1)}, bf16[512,128]{1,0:T(8,128)(2,1)S(1)}, u32[]{:S(2)}, u32[]{:S(2)}) collective-permute-start(bf16[512,128]{1,0:T(8,128)(2,1)S(1)} %get-tuple-element.186), channel_id=1, source_target_pairs={{0,4},{1,5},{2,6},{3,7},{4,0},{5,1},{6,2},{7,3},{8,12},{9,13},{10,... | collective-permute-start | bytes 393224 | tf_op jit(solution)/shard_map/ppermute | solution.py:423
  57.2 6.4 %collective-permute-start.18 = (bf16[1024,128]{1,0:T(8,128)(2,1)S(1)}, bf16[1024,128]{1,0:T(8,128)(2,1)S(1)}, u32[]{:S(2)}, u32[]{:S(2)}) collective-permute-start(bf16[1024,128]{1,0:T(8,128)(2,1)S(1)} %get-tuple-element.192), channel_id=1, source_target_pairs={{0,2},{1,5},{2,0},{3,7},{4,6},{5,1},{6,4},{7,3},{8,10},{9,13},{10,... | collective-permute-start | bytes 786440 | tf_op jit(solution)/shard_map/ppermute | solution.py:423
  58.7 8.6 %collective-permute-start.19 = (bf16[512,128]{1,0:T(8,128)(2,1)S(1)}, bf16[512,128]{1,0:T(8,128)(2,1)S(1)}, u32[]{:S(2)}, u32[]{:S(2)}) collective-permute-start(bf16[512,128]{1,0:T(8,128)(2,1)S(1)} %get-tuple-element.194), channel_id=1, source_target_pairs={{0,8},{1,9},{2,10},{3,11},{4,12},{5,13},{6,14},{7,15},{8,0},{9,1},... | collective-permute-start | bytes 393224 | tf_op jit(solution)/shard_map/ppermute | solution.py:423
  63.0 7.7 %collective-permute-start.20 = (bf16[512,128]{1,0:T(8,128)(2,1)S(1)}, bf16[512,128]{1,0:T(8,128)(2,1)S(1)}, u32[]{:S(2)}, u32[]{:S(2)}) collective-permute-start(bf16[512,128]{1,0:T(8,128)(2,1)S(1)} %get-tuple-element.196), channel_id=1, source_target_pairs={{0,4},{1,5},{2,6},{3,7},{4,0},{5,1},{6,2},{7,3},{8,12},{9,13},{10,... | collective-permute-start | bytes 393224 | tf_op jit(solution)/shard_map/ppermute | solution.py:423
  63.8 8.7 %collective-permute-start.21 = (bf16[512,128]{1,0:T(8,128)(2,1)S(1)}, bf16[512,128]{1,0:T(8,128)(2,1)S(1)}, u32[]{:S(2)}, u32[]{:S(2)}) collective-permute-start(bf16[512,128]{1,0:T(8,128)(2,1)S(1)} %get-tuple-element.198), channel_id=1, source_target_pairs={{0,4},{1,3},{2,6},{3,1},{4,0},{5,7},{6,2},{7,5},{8,12},{9,11},{10,... | collective-permute-start | bytes 393224 | tf_op jit(solution)/shard_map/ppermute | solution.py:423
  67.4 9.5 %collective-permute-start.22 = (bf16[512,128]{1,0:T(8,128)(2,1)S(1)}, bf16[512,128]{1,0:T(8,128)(2,1)S(1)}, u32[]{:S(2)}, u32[]{:S(2)}) collective-permute-start(bf16[512,128]{1,0:T(8,128)(2,1)S(1)} %get-tuple-element.200), channel_id=1, source_target_pairs={{0,4},{1,5},{2,6},{3,7},{4,0},{5,1},{6,2},{7,3},{8,12},{9,13},{10,... | collective-permute-start | bytes 393224 | tf_op jit(solution)/shard_map/ppermute | solution.py:423
  70.8 7.6 %collective-permute-start.23 = (bf16[512,128]{1,0:T(8,128)(2,1)S(1)}, bf16[512,128]{1,0:T(8,128)(2,1)S(1)}, u32[]{:S(2)}, u32[]{:S(2)}) collective-permute-start(bf16[512,128]{1,0:T(8,128)(2,1)S(1)} %get-tuple-element.202), channel_id=1, source_target_pairs={{0,8},{1,9},{2,10},{3,11},{4,12},{5,13},{6,14},{7,15},{8,0},{9,1},... | collective-permute-start | bytes 393224 | tf_op jit(solution)/shard_map/ppermute | solution.py:423
  72.5 9.1 %collective-permute-start.24 = (bf16[512,128]{1,0:T(8,128)(2,1)S(1)}, bf16[512,128]{1,0:T(8,128)(2,1)S(1)}, u32[]{:S(2)}, u32[]{:S(2)}) collective-permute-start(bf16[512,128]{1,0:T(8,128)(2,1)S(1)} %get-tuple-element.204), channel_id=1, source_target_pairs={{0,8},{1,9},{2,10},{3,11},{4,12},{5,13},{6,14},{7,15},{8,0},{9,1},... | collective-permute-start | bytes 393224 | tf_op jit(solution)/shard_map/ppermute | solution.py:423
  76.9 11.5 %collective-permute-start.28 = (bf16[1024,128]{1,0:T(8,128)(2,1)S(1)}, bf16[1024,128]{1,0:T(8,128)(2,1)S(1)}, u32[]{:S(2)}, u32[]{:S(2)}) collective-permute-start(bf16[1024,128]{1,0:T(8,128)(2,1)S(1)} %get-tuple-element.210), channel_id=1, source_target_pairs={{0,2},{1,3},{2,0},{3,1},{4,6},{5,7},{6,4},{7,5},{8,10},{9,11},{10,... | collective-permute-start | bytes 786440 | tf_op jit(solution)/shard_map/ppermute | solution.py:423
  78.5 5.7 %collective-permute-start.25 = (bf16[512,128]{1,0:T(8,128)(2,1)S(1)}, bf16[512,128]{1,0:T(8,128)(2,1)S(1)}, u32[]{:S(2)}, u32[]{:S(2)}) collective-permute-start(bf16[512,128]{1,0:T(8,128)(2,1)S(1)} %get-tuple-element.206), channel_id=1, source_target_pairs={{0,4},{1,5},{2,6},{3,7},{4,0},{5,1},{6,2},{7,3},{8,12},{9,13},{10,... | collective-permute-start | bytes 393224 | tf_op jit(solution)/shard_map/ppermute | solution.py:423
  81.7 6.8 %collective-permute-start.29 = (bf16[512,128]{1,0:T(8,128)(2,1)S(1)}, bf16[512,128]{1,0:T(8,128)(2,1)S(1)}, u32[]{:S(2)}, u32[]{:S(2)}) collective-permute-start(bf16[512,128]{1,0:T(8,128)(2,1)S(1)} %get-tuple-element.211), channel_id=1, source_target_pairs={{0,4},{1,3},{2,6},{3,1},{4,0},{5,7},{6,2},{7,5},{8,12},{9,11},{10,... | collective-permute-start | bytes 393224 | tf_op jit(solution)/shard_map/ppermute | solution.py:423
  81.8 6.7 %collective-permute-start.26 = (bf16[128,256]{1,0:T(8,128)(2,1)S(1)}, bf16[128,256]{1,0:T(8,128)(2,1)S(1)}, u32[]{:S(2)}, u32[]{:S(2)}) collective-permute-start(bf16[128,256]{1,0:T(8,128)(2,1)S(1)} %get-tuple-element.208), channel_id=1, source_target_pairs={{4,0},{8,4},{12,8},{5,1},{9,5},{13,9},{6,2},{10,6},{14,10},{7,3},{... | collective-permute-start | bytes 196616 | tf_op jit(solution)/shard_map/ppermute | solution.py:446
  83.1 5.4 %collective-permute-start.27 = (bf16[128,256]{1,0:T(8,128)(2,1)S(1)}, bf16[128,256]{1,0:T(8,128)(2,1)S(1)}, u32[]{:S(2)}, u32[]{:S(2)}) collective-permute-start(bf16[128,256]{1,0:T(8,128)(2,1)S(1)} %get-tuple-element.209), channel_id=1, source_target_pairs={{0,2},{2,0},{1,3},{3,1},{4,6},{6,4},{5,7},{7,5},{8,10},{10,8},{9,1... | collective-permute-start | bytes 196616 | tf_op jit(solution)/shard_map/ppermute | solution.py:410
  84.3 7.1 %collective-permute-start.30 = (bf16[1024,128]{1,0:T(8,128)(2,1)S(1)}, bf16[1024,128]{1,0:T(8,128)(2,1)S(1)}, u32[]{:S(2)}, u32[]{:S(2)}) collective-permute-start(bf16[1024,128]{1,0:T(8,128)(2,1)S(1)} %get-tuple-element.219), channel_id=1, source_target_pairs={{0,2},{1,3},{2,0},{3,1},{4,6},{5,7},{6,4},{7,5},{8,10},{9,11},{10,... | collective-permute-start | bytes 786440 | tf_op jit(solution)/shard_map/ppermute | solution.py:423
  88.5 6.4 %collective-permute-start.31 = (bf16[1024,128]{1,0:T(8,128)(2,1)S(1)}, bf16[1024,128]{1,0:T(8,128)(2,1)S(1)}, u32[]{:S(2)}, u32[]{:S(2)}) collective-permute-start(bf16[1024,128]{1,0:T(8,128)(2,1)S(1)} %get-tuple-element.226), channel_id=1, source_target_pairs={{0,2},{1,5},{2,0},{3,7},{4,6},{5,1},{6,4},{7,3},{8,10},{9,13},{10,... | collective-permute-start | bytes 786440 | tf_op jit(solution)/shard_map/ppermute | solution.py:423
  (6 other events, 25.7 us)

commit v17 on v16

--- a/solution.py
+++ b/solution.py
@@ -399,10 +399,37 @@
     start_bwd(layer, norm_grad(grad, total[...]), weights, received, remote_t, outs)
 
 
-def last_kernel(*refs):
+def last_kernel(parts, *refs):
     dtotal, back, spread = refs[:3]
-    refs[-2][...] = gathered_grad(dtotal, back, refs[3:-2], spread)
-    refs[-1][...] = jnp.zeros_like(refs[-1])
+    returned, outs, token = refs[3 : -1 - parts], refs[-1 - parts : -1], refs[-1]
+    token[...] = jnp.zeros_like(token)
+
+    @pl.when(lax.axis_index("feat") > 0)
+    def _():
+        grad = gathered_grad(dtotal, back, returned, spread)
+        m = grad.shape[0] // parts
+        for i, out in enumerate(outs):
+            out[...] = grad[i * m : (i + 1) * m, :]
+
+
+def choose_kernel(parts, *refs):
+    out, sems = refs[-2:]
+    feat = lax.axis_index("feat")
+    m = out.shape[0] // parts
+    for i in range(parts):
+        own, got, to = refs[i], refs[parts + i], out.at[i * m : (i + 1) * m]
+
+        @pl.when(feat > 0)
+        def _():
+            pltpu.make_async_copy(own, to, sems.at[i]).start()
+
+        @pl.when(feat == 0)
+        def _():
+            pltpu.make_async_copy(got, to, sems.at[i]).start()
+
+    for i in range(parts):
+        to = out.at[i * m : (i + 1) * m]
+        pltpu.make_async_copy(refs[i], to, sems.at[i]).wait()
 
 
 def around(x, axis, distance):
@@ -445,6 +472,17 @@
     chain = lax.axis_size("chain")
     up = lax.ppermute(grads[0], "chain", [(c, c - 1) for c in range(1, chain)])
     return [up] + [around(x, "basin", -s) for s, x in enumerate(grads) if s]
+
+
+def backward_on_one(grads):
+    groups = lax.axis_size("basin")
+
+    def target(s, c, b, feat):
+        if feat == 0 or (s == 0 and c == 0):
+            return None
+        return (c, (b - s) % groups) if s else (c - 1, b)
+
+    return [over_mesh(x, functools.partial(target, s)) for s, x in enumerate(grads)]
 
 
 def shards(features, cotangent, w_in, w_out, block_index, block_values, send_rows, send_count):
@@ -561,9 +599,10 @@
     basin_first = list(zip(orders[0], orders[0], strict=True))
     returned = {}
     sums = {}
+    parts = rows // 256
 
     def back(layer, outs, after):
-        returned[layer] = backward(outs[6:])
+        returned[layer] = backward(outs[6:]) if layer else backward_on_one(outs[6:])
         grad, whole = call(
             functools.partial(back_kernel, layer, grad_scale),
             [((rows, latent), F32), ((grad_rows, LANES), F32)],
@@ -591,8 +630,8 @@
                 after=after,
             )
         return call(
-            last_kernel,
-            [((rows, latent), F32), ((8, LANES), F32)],
+            functools.partial(last_kernel, parts),
+            [((rows // parts, latent), F32)] * parts + [((8, LANES), F32)],
             [*state, spread, *returned[layer]],
             2 * rows * far_rows * latent,
             name="join0",
@@ -648,13 +687,24 @@
                 if layer == 0 and sums[0].done == count - 1:
                     at = at + returned[0] + [sums[above].got[0] for above in range(2, layers)]
                 at = sum_step([sums[layer]], at)
-    grad, token = join(0, state, at)
+    *mine, token = join(0, state, at)
+    got = [lax.ppermute(x, "feat", [(1, 0)]) for x in mine]
     at = [token]
     written = []
     for layer in reversed(range(1, layers)):
         *written, token = write(layer, written, at)
         at = [token]
     *written, token = write(0, written, at, (0,))
+    grad = pl.pallas_call(
+        functools.partial(choose_kernel, parts),
+        out_shape=jax.ShapeDtypeStruct((rows, latent), F32),
+        in_specs=[ANY] * (2 * parts),
+        out_specs=ANY,
+        scratch_shapes=[pltpu.SemaphoreType.DMA((parts,))],
+        cost_estimate=pl.CostEstimate(flops=1, bytes_accessed=1, transcendentals=0),
+        name="choose",
+    )(*mine, *got)
+    grad, token = lax.optimization_barrier((grad, token))
     *written, token = write(0, written, [token], (1,))
     return (grad, *written)
 

time: 96.8 us -> 123 us (1.27)
  Pallas kernels: 30.6 us -> 54.4 us
  starting transfers between devices: 41.3 us -> 44.2 us
  waiting for transfers between devices: 21.4 us -> 19.3 us
  local copies, waits for them, and re-layouts: 1.2 us -> 2.69 us
    pallas_call x0 -> x1, Pallas kernels: none -> 24.9 us  [shards(): pl.pallas_call(functools.partial(choose_kernel, parts), out_shape=jax.Sha...]
    ppermute x0 -> x3, starting transfers between devices: none -> 3.88 us  [shards(): got = [lax.ppermute(x, 'feat', [(1, 0)]) for x in mine]]
    ppermute x3 -> x2, waiting for transfers between devices: 5.73 us -> 2.59 us  [backward(): up = lax.ppermute(grads[0], 'chain', [(c, c - 1) for c in range(1, chain)])]
    unnamed x12 -> x24, local copies, waits for them, and re-layouts: 1.2 us -> 2.69 us
    ppermute x3 -> x2, starting transfers between devices: 4.1 us -> 2.8 us  [backward(): up = lax.ppermute(grads[0], 'chain', [(c, c - 1) for c in range(1, chain)])]
    ppermute x18 -> x20, starting transfers between devices: 29.9 us -> 31 us  [over_mesh(): return lax.ppermute(x, ('chain', 'basin', 'feat'), perm)]
    ppermute x18 -> x20, waiting for transfers between devices: 12.2 us -> 13.2 us  [over_mesh(): return lax.ppermute(x, ('chain', 'basin', 'feat'), perm)]
    ppermute x11 -> x10, starting transfers between devices: 7.32 us -> 6.49 us  [around(): return lax.ppermute(x, axis, [(i, (i + distance) % n) for i in range(n)])]
  transfers between devices with their start and end apart: 32 -> 35, of which waited for: 13 -> 13; matrix products, arithmetic and copies ran while one was open for 1% -> 1% of each run, Pallas kernels for 26% -> 40%
where the time goes in v17:
time: 123 us
  Pallas kernels  54.4 us (44%)
  starting transfers between devices  44.2 us (36%)
  waiting for transfers between devices  19.3 us (16%)
  local copies, waits for them, and re-layouts  2.69 us (2%)
  between operations  1.4 us (1%)
    ppermute x20, starting transfers between devices, over_mesh(): return lax.ppermute(x, ('chain', 'basin', 'feat'), perm)  31 us
    pallas_call x33, Pallas kernels, call(): pl.pallas_call(lambda *refs: body(*refs[skipped:]), out_shape=[jax.ShapeD...  25 us
    pallas_call x1, Pallas kernels, shards(): pl.pallas_call(functools.partial(choose_kernel, parts), out_shape=jax.Sha...  24.9 us
    ppermute x20, waiting for transfers between devices, over_mesh(): return lax.ppermute(x, ('chain', 'basin', 'feat'), perm)  13.2 us
    ppermute x10, starting transfers between devices, around(): return lax.ppermute(x, axis, [(i, (i + distance) % n) for i in range(n)])  6.49 us
    pallas_call x4, Pallas kernels, write(): pl.pallas_call(functools.partial(write_kernel, layer, sums[layer].stages[...  4.46 us
    ppermute x3, starting transfers between devices, shards(): got = [lax.ppermute(x, 'feat', [(1, 0)]) for x in mine]  3.88 us
    ppermute x10, waiting for transfers between devices, around(): return lax.ppermute(x, axis, [(i, (i + distance) % n) for i in range(n)])  3.54 us
  transfers between devices with their start and end apart: 35, of which 13 were waited for; matrix products, arithmetic and copies ran while one was open for 1% of the time, Pallas kernels for 40%

profile of v17, /device:TPU:0, one launch (start us, length us, event | category | flops | bytes accessed | tf_op | source)
XLA Modules:
  0.0 122.7 jit_solution(12321356059615636703)
XLA Ops:
  3.3 4.9 %collective-permute-start = (bf16[128,256]{1,0:T(8,128)(2,1)S(1)}, bf16[128,256]{1,0:T(8,128)(2,1)S(1)}, u32[]{:S(2)}, u32[]{:S(2)}) collective-permute-start(bf16[128,256]{1,0:T(8,128)(2,1)S(1)} %get-tuple-element.121), channel_id=1, source_target_pairs={{0,4},{2,6},{5,9},{7,11},{8,12},{10,14},{16,20},{18,22},{21,25},{2... | collective-permute-start | bytes 196616 | tf_op jit(solution)/shard_map/ppermute | solution.py:450
  8.2 1.6 %collective-permute-start.3 = (bf16[128,256]{1,0:T(8,128)(2,1)S(1)}, bf16[128,256]{1,0:T(8,128)(2,1)S(1)}, u32[]{:S(2)}, u32[]{:S(2)}) collective-permute-start(bf16[128,256]{1,0:T(8,128)(2,1)S(1)} %get-tuple-element.128), channel_id=1, source_target_pairs={{0,2},{2,0},{1,3},{3,1},{4,6},{6,4},{5,7},{7,5},{8,10},{10,8},{9,1... | collective-permute-start | bytes 196616 | tf_op jit(solution)/shard_map/ppermute | solution.py:437
  11.8 1.6 %adjacency.1 = (bf16[768,768]{1,0:T(8,128)(2,1)S(1)}, bf16[768,768]{1,0:T(8,128)(2,1)S(1)}, bf16[768,256]{1,0:T(8,128)(2,1)S(1)}, bf16[256,768]{1,0:T(8,128)(2,1)S(1)}) custom-call(s32[4,6]{1,0:T(4,128)S(1)} %bitcast.4, bf16[6,4,128,128]{3,2,1,0:T(8,128)(2,1)S(1)} %copy-done.3, bf16[128,768]{1,0:T(8,128)(2,1)S(1)} %get-tuple-element.122.refs_2_, ...), custom_call_target="tpu_custom_call" | custom-call | flops 150994944 | bytes 4000000 | tf_op jit(solution)/shard_map/adjacency/pallas_call | solution.py:32
  15.8 2.8 %collective-permute-start.5 = (bf16[128,256]{1,0:T(8,128)(2,1)S(1)}, bf16[128,256]{1,0:T(8,128)(2,1)S(1)}, u32[]{:S(2)}, u32[]{:S(2)}) collective-permute-start(bf16[128,256]{1,0:T(8,128)(2,1)S(1)} %get-tuple-element.132), channel_id=1, source_target_pairs={{0,4},{2,6},{5,9},{7,11},{8,12},{10,14},{16,20},{18,22},{21,25},{2... | collective-permute-start | bytes 196616 | tf_op jit(solution)/shard_map/ppermute | solution.py:450
  19.1 1.6 %local1.1 = (bf16[768,256]{1,0:T(8,128)(2,1)S(1)}, bf16[768,512]{1,0:T(8,128)(2,1)S(1)}, bf16[768,512]{1,0:T(8,128)(2,1)S(1)}, bf16[512,768]{1,0:T(8,128)(2,1)S(1)}, bf16[256,768]{1,0:T(8,128)(2,1)S(1)}) custom-call(bf16[768,256]{1,0:T(8,128)(2,1)S(1)} %get-tuple-element.133.refs_0_, bf16[3,256,512]{2,1,0:T(8,128)(2,1)S(1)} %copy-done, ...), custom_call_target="tpu_custom_call" | custom-call | flops 805306368 | bytes 4000000 | tf_op jit(solution)/shard_map/local1/pallas_call | solution.py:32
  20.8 2.0 %collective-permute-done.6.refs_7_.refs_14_ = bf16[128,256]{1,0:T(8,128)(2,1)S(1)} collective-permute-done((bf16[128,256]{1,0:T(8,128)(2,1)S(1)}, bf16[128,256]{1,0:T(8,128)(2,1)S(1)}, u32[]{:S(2)}, u32[]{:S(2)}) %collective-permute-start.6) | collective-permute-done | bytes 65568 | tf_op jit(solution)/shard_map/ppermute | solution.py:437
  24.9 2.3 %collective-permute-start.8 = (bf16[128,256]{1,0:T(8,128)(2,1)S(1)}, bf16[128,256]{1,0:T(8,128)(2,1)S(1)}, u32[]{:S(2)}, u32[]{:S(2)}) collective-permute-start(bf16[128,256]{1,0:T(8,128)(2,1)S(1)} %get-tuple-element.139), channel_id=1, source_target_pairs={{0,4},{2,6},{5,9},{7,11},{8,12},{10,14},{16,20},{18,22},{21,25},{2... | collective-permute-start | bytes 196616 | tf_op jit(solution)/shard_map/ppermute | solution.py:450
  27.2 1.4 %collective-permute-start.9 = (bf16[128,256]{1,0:T(8,128)(2,1)S(1)}, bf16[128,256]{1,0:T(8,128)(2,1)S(1)}, u32[]{:S(2)}, u32[]{:S(2)}) collective-permute-start(bf16[128,256]{1,0:T(8,128)(2,1)S(1)} %get-tuple-element.143), channel_id=1, source_target_pairs={{0,2},{2,0},{1,3},{3,1},{4,6},{6,4},{5,7},{7,5},{8,10},{10,8},{9,1... | collective-permute-start | bytes 196616 | tf_op jit(solution)/shard_map/ppermute | solution.py:437
  28.6 1.6 %local2.1 = (bf16[768,256]{1,0:T(8,128)(2,1)S(1)}, bf16[768,512]{1,0:T(8,128)(2,1)S(1)}, bf16[768,512]{1,0:T(8,128)(2,1)S(1)}, bf16[512,768]{1,0:T(8,128)(2,1)S(1)}, bf16[256,768]{1,0:T(8,128)(2,1)S(1)}) custom-call(bf16[768,256]{1,0:T(8,128)(2,1)S(1)} %get-tuple-element.140.refs_0_, bf16[3,256,512]{2,1,0:T(8,128)(2,1)S(1)} %copy-done, ...), custom_call_target="tpu_custom_call" | custom-call | flops 805306368 | bytes 4000000 | tf_op jit(solution)/shard_map/local2/pallas_call | solution.py:32
  32.5 2.0 %turn.1 = (f32[768,256]{1,0:T(8,128)S(1)}, bf16[768,256]{1,0:T(8,128)(2,1)S(1)}, bf16[256,256]{1,0:T(8,128)(2,1)S(1)}, bf16[256,256]{1,0:T(8,128)(2,1)S(1)}, bf1...) custom-call(f32[768,256]{1,0:T(8,128)S(1)} %get-tuple-element.138.re, ...), custom_call_target="tpu_custom_call" | custom-call | flops 536870912 | bytes 4000000 | tf_op jit(solution)/shard_map/turn/pallas_call | solution.py:32
  35.8 1.4 %collective-permute-start.12 = (bf16[128,256]{1,0:T(8,128)(2,1)S(1)}, bf16[128,256]{1,0:T(8,128)(2,1)S(1)}, u32[]{:S(2)}, u32[]{:S(2)}) collective-permute-start(bf16[128,256]{1,0:T(8,128)(2,1)S(1)} %get-tuple-element.158), channel_id=1, source_target_pairs={{0,2},{2,0},{1,3},{3,1},{4,6},{6,4},{5,7},{7,5},{8,10},{10,8},{9,1... | collective-permute-start | bytes 196616 | tf_op jit(solution)/shard_map/ppermute | solution.py:437
  37.2 2.4 %back2.1 = (f32[768,256]{1,0:T(8,128)S(1)}, f32[2048,128]{1,0:T(8,128)S(1)}) custom-call(bf16[768,256]{1,0:T(8,128)(2,1)S(1)} %get-tuple-element.146.refs_0_, bf16[768,768]{1,0:T(8,128)(2,1)S(1)} %get-tuple-element.147.refs_1_.refs_2_, bf16[768,512]{1,0:T(8,128)(2,1)S(1)} %get-tuple-element.148.refs_2_, bf16[768,512]{1,0:T(8,128)(2,1)S(1)} %get-tuple-element.149.refs_3_, ...), custom_call_target="tpu_custom_call" | custom-call | flops 2717908992 | bytes 4000000 | tf_op jit(solution)/shard_map/back2/pallas_call | solution.py:32
  40.8 1.4 %collective-permute-start.15 = (bf16[1024,128]{1,0:T(8,128)(2,1)S(1)}, bf16[1024,128]{1,0:T(8,128)(2,1)S(1)}, u32[]{:S(2)}, u32[]{:S(2)}) collective-permute-start(bf16[1024,128]{1,0:T(8,128)(2,1)S(1)} %get-tuple-element.177), channel_id=1, source_target_pairs={{0,2},{1,3},{2,0},{3,1},{4,6},{5,7},{6,4},{7,5},{8,10},{9,11},{10,... | collective-permute-start | bytes 786440 | tf_op jit(solution)/shard_map/ppermute | solution.py:450
  42.1 1.5 %join2.1 = (f32[768,256]{1,0:T(8,128)S(1)}, bf16[768,256]{1,0:T(8,128)(2,1)S(1)}, bf16[256,256]{1,0:T(8,128)(2,1)S(1)}, bf16[256,256]{1,0:T(8,128)(2,1)S(1)}, bf...) custom-call(f32[1024,128]{1,0:T(8,128)S(1)} %get-tuple-element.160.r, ...), custom_call_target="tpu_custom_call" | custom-call | flops 536870912 | bytes 4000000 | tf_op jit(solution)/shard_map/join2/pallas_call | solution.py:32
  43.6 1.5 %collective-permute-start.13 = (bf16[128,256]{1,0:T(8,128)(2,1)S(1)}, bf16[128,256]{1,0:T(8,128)(2,1)S(1)}, u32[]{:S(2)}, u32[]{:S(2)}) collective-permute-start(bf16[128,256]{1,0:T(8,128)(2,1)S(1)} %get-tuple-element.173), channel_id=1, source_target_pairs={{4,0},{8,4},{12,8},{5,1},{9,5},{13,9},{6,2},{10,6},{14,10},{7,3},{... | collective-permute-start | bytes 196616 | tf_op jit(solution)/shard_map/ppermute | solution.py:473
  45.9 2.4 %back1.1 = (f32[768,256]{1,0:T(8,128)S(1)}, f32[2048,128]{1,0:T(8,128)S(1)}) custom-call(bf16[768,256]{1,0:T(8,128)(2,1)S(1)} %get-tuple-element.163.refs_0_.refs_1_, bf16[768,256]{1,0:T(8,128)(2,1)S(1)} %get-tuple-element.163.refs_0_.refs_1_, bf16[768,768]{1,0:T(8,128)(2,1)S(1)} %get-tuple-element.147.refs_1_.refs_2_, ...), custom_call_target="tpu_custom_call" | custom-call | flops 2717908992 | bytes 4000000 | tf_op jit(solution)/shard_map/back1/pallas_call | solution.py:32
  48.3 1.5 %collective-permute-done.13.refs_1_.refs_10_ = bf16[128,256]{1,0:T(8,128)(2,1)S(1)} collective-permute-done((bf16[128,256]{1,0:T(8,128)(2,1)S(1)}, bf16[128,256]{1,0:T(8,128)(2,1)S(1)}, u32[]{:S(2)}, u32[]{:S(2)}) %collective-permute-start.13) | collective-permute-done | bytes 65568 | tf_op jit(solution)/shard_map/ppermute | solution.py:473
  50.8 2.4 %collective-permute-start.16 = (bf16[512,128]{1,0:T(8,128)(2,1)S(1)}, bf16[512,128]{1,0:T(8,128)(2,1)S(1)}, u32[]{:S(2)}, u32[]{:S(2)}) collective-permute-start(bf16[512,128]{1,0:T(8,128)(2,1)S(1)} %get-tuple-element.190), channel_id=1, source_target_pairs={{0,4},{1,5},{2,6},{3,7},{4,0},{5,1},{6,2},{7,3},{8,12},{9,13},{10,... | collective-permute-start | bytes 393224 | tf_op jit(solution)/shard_map/ppermute | solution.py:450
  53.2 1.5 %join1.1 = (f32[768,256]{1,0:T(8,128)S(1)}, bf16[768,256]{1,0:T(8,128)(2,1)S(1)}, bf16[256,256]{1,0:T(8,128)(2,1)S(1)}, bf16[256,256]{1,0:T(8,128)(2,1)S(1)}, bf...) custom-call(f32[512,128]{1,0:T(8,128)S(1)} %get-tuple-element.178.re, ...), custom_call_target="tpu_custom_call" | custom-call | flops 536870912 | bytes 4000000 | tf_op jit(solution)/shard_map/join1/pallas_call | solution.py:32
  54.7 2.4 %back0.1 = (f32[768,256]{1,0:T(8,128)S(1)}, f32[2048,128]{1,0:T(8,128)S(1)}) custom-call(bf16[768,256]{1,0:T(8,128)(2,1)S(1)} %get-tuple-element.180.refs_0_.refs_1_, bf16[768,256]{1,0:T(8,128)(2,1)S(1)} %get-tuple-element.180.refs_0_.refs_1_, bf16[768,768]{1,0:T(8,128)(2,1)S(1)} %get-tuple-element.147.refs_1_.refs_2_, ...), custom_call_target="tpu_custom_call" | custom-call | flops 2717908992 | bytes 4000000 | tf_op jit(solution)/shard_map/back0/pallas_call | solution.py:32
  57.2 1.5 %collective-permute-start.18 = (bf16[1024,128]{1,0:T(8,128)(2,1)S(1)}, bf16[1024,128]{1,0:T(8,128)(2,1)S(1)}, u32[]{:S(2)}, u32[]{:S(2)}) collective-permute-start(bf16[1024,128]{1,0:T(8,128)(2,1)S(1)} %get-tuple-element.196), channel_id=1, source_target_pairs={{0,2},{1,5},{2,0},{3,7},{4,6},{5,1},{6,4},{7,3},{8,10},{9,13},{10,... | collective-permute-start | bytes 786440 | tf_op jit(solution)/shard_map/ppermute | solution.py:450
  58.7 4.2 %collective-permute-start.19 = (bf16[512,128]{1,0:T(8,128)(2,1)S(1)}, bf16[512,128]{1,0:T(8,128)(2,1)S(1)}, u32[]{:S(2)}, u32[]{:S(2)}) collective-permute-start(bf16[512,128]{1,0:T(8,128)(2,1)S(1)} %get-tuple-element.198), channel_id=1, source_target_pairs={{0,8},{1,9},{2,10},{3,11},{4,12},{5,13},{6,14},{7,15},{8,0},{9,1},... | collective-permute-start | bytes 393224 | tf_op jit(solution)/shard_map/ppermute | solution.py:450
  63.8 3.6 %collective-permute-start.21 = (bf16[512,128]{1,0:T(8,128)(2,1)S(1)}, bf16[512,128]{1,0:T(8,128)(2,1)S(1)}, u32[]{:S(2)}, u32[]{:S(2)}) collective-permute-start(bf16[512,128]{1,0:T(8,128)(2,1)S(1)} %get-tuple-element.202), channel_id=1, source_target_pairs={{0,4},{1,3},{2,6},{3,1},{4,0},{5,7},{6,2},{7,5},{8,12},{9,11},{10,... | collective-permute-start | bytes 393224 | tf_op jit(solution)/shard_map/ppermute | solution.py:450
  68.1 2.7 %collective-permute-done.20.refs_2_ = bf16[512,128]{1,0:T(8,128)(2,1)S(1)} collective-permute-done((bf16[512,128]{1,0:T(8,128)(2,1)S(1)}, bf16[512,128]{1,0:T(8,128)(2,1)S(1)}, u32[]{:S(2)}, u32[]{:S(2)}) %collective-permute-start.20) | collective-permute-done | bytes 131104 | tf_op jit(solution)/shard_map/ppermute | solution.py:450
  71.1 1.4 %collective-permute-done.21.refs_2_ = bf16[512,128]{1,0:T(8,128)(2,1)S(1)} collective-permute-done((bf16[512,128]{1,0:T(8,128)(2,1)S(1)}, bf16[512,128]{1,0:T(8,128)(2,1)S(1)}, u32[]{:S(2)}, u32[]{:S(2)}) %collective-permute-start.21) | collective-permute-done | bytes 131104 | tf_op jit(solution)/shard_map/ppermute | solution.py:450
  72.5 1.8 %collective-permute-start.24 = (bf16[512,128]{1,0:T(8,128)(2,1)S(1)}, bf16[512,128]{1,0:T(8,128)(2,1)S(1)}, u32[]{:S(2)}, u32[]{:S(2)}) collective-permute-start(bf16[512,128]{1,0:T(8,128)(2,1)S(1)} %get-tuple-element.208), channel_id=1, source_target_pairs={{0,8},{1,9},{2,10},{3,11},{4,12},{5,13},{6,14},{7,15},{8,0},{9,1},... | collective-permute-start | bytes 393224 | tf_op jit(solution)/shard_map/ppermute | solution.py:450
  74.3 2.6 %collective-permute-done.22.refs_2_ = bf16[512,128]{1,0:T(8,128)(2,1)S(1)} collective-permute-done((bf16[512,128]{1,0:T(8,128)(2,1)S(1)}, bf16[512,128]{1,0:T(8,128)(2,1)S(1)}, u32[]{:S(2)}, u32[]{:S(2)}) %collective-permute-start.22) | collective-permute-done | bytes 131104 | tf_op jit(solution)/shard_map/ppermute | solution.py:450
  77.0 1.5 %collective-permute-start.28 = (bf16[1024,128]{1,0:T(8,128)(2,1)S(1)}, bf16[1024,128]{1,0:T(8,128)(2,1)S(1)}, u32[]{:S(2)}, u32[]{:S(2)}) collective-permute-start(bf16[1024,128]{1,0:T(8,128)(2,1)S(1)} %get-tuple-element.214), channel_id=1, source_target_pairs={{0,2},{1,3},{2,0},{3,1},{4,6},{5,7},{6,4},{7,5},{8,10},{9,11},{10,... | collective-permute-start | bytes 786440 | tf_op jit(solution)/shard_map/ppermute | solution.py:450
  78.6 3.1 %collective-permute-done.24.refs_2_ = bf16[512,128]{1,0:T(8,128)(2,1)S(1)} collective-permute-done((bf16[512,128]{1,0:T(8,128)(2,1)S(1)}, bf16[512,128]{1,0:T(8,128)(2,1)S(1)}, u32[]{:S(2)}, u32[]{:S(2)}) %collective-permute-start.24) | collective-permute-done | bytes 131104 | tf_op jit(solution)/shard_map/ppermute | solution.py:450
  84.3 1.9 %collective-permute-done.28.refs_3_.refs_2_ = bf16[1024,128]{1,0:T(8,128)(2,1)S(1)} collective-permute-done((bf16[1024,128]{1,0:T(8,128)(2,1)S(1)}, bf16[1024,128]{1,0:T(8,128)(2,1)S(1)}, u32[]{:S(2)}, u32[]{:S(2)}) %collective-permute-start.28) | collective-permute-done | bytes 262176 | tf_op jit(solution)/shard_map/ppermute | solution.py:450
  96.1 24.9 %choose.1 = f32[768,256]{1,0:T(8,128)} custom-call(f32[256,256]{1,0:T(8,128)} %copy-done.5, f32[256,256]{1,0:T(8,128)} %copy-done.6, f32[256,256]{1,0:T(8,128)} %copy-done.7, f32[256,256]{1,0:T(8,128)} %copy-done.9, f32[256,256]{1,0:T(8,128)} %copy-done.10, f32[256,256]{1,0:T(8,128)} %copy-done.11), custom_call_target="tpu_custom_call" | custom-call | flops 1 | bytes 1 | tf_op jit(solution)/shard_map/choose/pallas_call | solution.py:698
  121.1 1.5 %write0.3 = (f32[3,256,512]{2,1,0:T(8,128)}, f32[3,512,256]{2,1,0:T(8,128)}, f32[8,128]{1,0:T(8,128)}) custom-call(f32[3,256,512]{2,1,0:T(8,128)} %get-tuple-element.231.refs_0_, f32[3,512,256]{2,1,0:T(8,128)} %get-tuple-element.232.refs_1_, f32[8,128]{1,0:T(8,128)S(1)} %get-tuple-element.233.refs_2_, ...), custom_call_target="tpu_custom_call", output_to_operand_aliasing={{0}: (0, {}), {1}: (1, {})} | custom-call | flops 1 | bytes 1 | tf_op jit(solution)/shard_map/write0/pallas_call | solution.py:645
  (101 shorter events, 30.8 us)
Async XLA Ops:
  0.7 9.1 %collective-permute-start.1 = (bf16[3,256,512]{2,1,0:T(8,128)(2,1)}, bf16[3,256,512]{2,1,0:T(8,128)(2,1)S(1)}, u32[]{:S(2)}, u32[]{:S(2)}) collective-permute-start(bf16[3,256,512]{2,1,0:T(8,128)(2,1)} %refs_7_.5), channel_id=1, source_target_pairs={{0,1},{1,0},{2,3},{3,2},{4,5},{5,4},{6,7},{7,6},{8,9},{9,8},{10,11... | collective-permute-start | bytes 2359304 | tf_op jit(solution)/shard_map/ppermute | solution.py:437
  1.2 8.6 %collective-permute-start.2 = (bf16[3,512,256]{2,1,0:T(8,128)(2,1)}, bf16[3,512,256]{2,1,0:T(8,128)(2,1)S(1)}, u32[]{:S(2)}, u32[]{:S(2)}) collective-permute-start(bf16[3,512,256]{2,1,0:T(8,128)(2,1)} %refs_9_.3), channel_id=1, source_target_pairs={{0,1},{1,0},{2,3},{3,2},{4,5},{5,4},{6,7},{7,6},{8,9},{9,8},{10,11... | collective-permute-start | bytes 2359304 | tf_op jit(solution)/shard_map/ppermute | solution.py:437
  3.3 10.1 %collective-permute-start = (bf16[128,256]{1,0:T(8,128)(2,1)S(1)}, bf16[128,256]{1,0:T(8,128)(2,1)S(1)}, u32[]{:S(2)}, u32[]{:S(2)}) collective-permute-start(bf16[128,256]{1,0:T(8,128)(2,1)S(1)} %get-tuple-element.121), channel_id=1, source_target_pairs={{0,4},{2,6},{5,9},{7,11},{8,12},{10,14},{16,20},{18,22},{21,25},{2... | collective-permute-start | bytes 196616 | tf_op jit(solution)/shard_map/ppermute | solution.py:450
  8.2 5.2 %collective-permute-start.3 = (bf16[128,256]{1,0:T(8,128)(2,1)S(1)}, bf16[128,256]{1,0:T(8,128)(2,1)S(1)}, u32[]{:S(2)}, u32[]{:S(2)}) collective-permute-start(bf16[128,256]{1,0:T(8,128)(2,1)S(1)} %get-tuple-element.128), channel_id=1, source_target_pairs={{0,2},{2,0},{1,3},{3,1},{4,6},{6,4},{5,7},{7,5},{8,10},{10,8},{9,1... | collective-permute-start | bytes 196616 | tf_op jit(solution)/shard_map/ppermute | solution.py:437
  15.8 5.0 %collective-permute-start.5 = (bf16[128,256]{1,0:T(8,128)(2,1)S(1)}, bf16[128,256]{1,0:T(8,128)(2,1)S(1)}, u32[]{:S(2)}, u32[]{:S(2)}) collective-permute-start(bf16[128,256]{1,0:T(8,128)(2,1)S(1)} %get-tuple-element.132), channel_id=1, source_target_pairs={{0,4},{2,6},{5,9},{7,11},{8,12},{10,14},{16,20},{18,22},{21,25},{2... | collective-permute-start | bytes 196616 | tf_op jit(solution)/shard_map/ppermute | solution.py:450
  18.5 4.3 %collective-permute-start.6 = (bf16[128,256]{1,0:T(8,128)(2,1)S(1)}, bf16[128,256]{1,0:T(8,128)(2,1)S(1)}, u32[]{:S(2)}, u32[]{:S(2)}) collective-permute-start(bf16[128,256]{1,0:T(8,128)(2,1)S(1)} %get-tuple-element.136), channel_id=1, source_target_pairs={{0,2},{2,0},{1,3},{3,1},{4,6},{6,4},{5,7},{7,5},{8,10},{10,8},{9,1... | collective-permute-start | bytes 196616 | tf_op jit(solution)/shard_map/ppermute | solution.py:437
  20.8 3.1 %collective-permute-start.7 = (bf16[128,256]{1,0:T(8,128)(2,1)S(1)}, bf16[128,256]{1,0:T(8,128)(2,1)S(1)}, u32[]{:S(2)}, u32[]{:S(2)}) collective-permute-start(bf16[128,256]{1,0:T(8,128)(2,1)S(1)} %collective-permute-done.5.refs_8_.refs_12_), channel_id=1, source_target_pairs={{0,1},{1,0},{2,3},{3,2},{4,5},{5,4},{6,7},{7,6},{8,9},{9,8},{10,11... | collective-permute-start | bytes 196616 | tf_op jit(solution)/shard_map/ppermute | solution.py:437
  24.9 5.2 %collective-permute-start.8 = (bf16[128,256]{1,0:T(8,128)(2,1)S(1)}, bf16[128,256]{1,0:T(8,128)(2,1)S(1)}, u32[]{:S(2)}, u32[]{:S(2)}) collective-permute-start(bf16[128,256]{1,0:T(8,128)(2,1)S(1)} %get-tuple-element.139), channel_id=1, source_target_pairs={{0,4},{2,6},{5,9},{7,11},{8,12},{10,14},{16,20},{18,22},{21,25},{2... | collective-permute-start | bytes 196616 | tf_op jit(solution)/shard_map/ppermute | solution.py:450
  27.2 4.3 %collective-permute-start.9 = (bf16[128,256]{1,0:T(8,128)(2,1)S(1)}, bf16[128,256]{1,0:T(8,128)(2,1)S(1)}, u32[]{:S(2)}, u32[]{:S(2)}) collective-permute-start(bf16[128,256]{1,0:T(8,128)(2,1)S(1)} %get-tuple-element.143), channel_id=1, source_target_pairs={{0,2},{2,0},{1,3},{3,1},{4,6},{6,4},{5,7},{7,5},{8,10},{10,8},{9,1... | collective-permute-start | bytes 196616 | tf_op jit(solution)/shard_map/ppermute | solution.py:437
  34.5 6.2 %collective-permute-start.11 = (bf16[128,256]{1,0:T(8,128)(2,1)S(1)}, bf16[128,256]{1,0:T(8,128)(2,1)S(1)}, u32[]{:S(2)}, u32[]{:S(2)}) collective-permute-start(bf16[128,256]{1,0:T(8,128)(2,1)S(1)} %get-tuple-element.157), channel_id=1, source_target_pairs={{4,0},{8,4},{12,8},{5,1},{9,5},{13,9},{6,2},{10,6},{14,10},{7,3},{... | collective-permute-start | bytes 196616 | tf_op jit(solution)/shard_map/ppermute | solution.py:473
  35.8 4.9 %collective-permute-start.12 = (bf16[128,256]{1,0:T(8,128)(2,1)S(1)}, bf16[128,256]{1,0:T(8,128)(2,1)S(1)}, u32[]{:S(2)}, u32[]{:S(2)}) collective-permute-start(bf16[128,256]{1,0:T(8,128)(2,1)S(1)} %get-tuple-element.158), channel_id=1, source_target_pairs={{0,2},{2,0},{1,3},{3,1},{4,6},{6,4},{5,7},{7,5},{8,10},{10,8},{9,1... | collective-permute-start | bytes 196616 | tf_op jit(solution)/shard_map/ppermute | solution.py:437
  40.8 10.0 %collective-permute-start.15 = (bf16[1024,128]{1,0:T(8,128)(2,1)S(1)}, bf16[1024,128]{1,0:T(8,128)(2,1)S(1)}, u32[]{:S(2)}, u32[]{:S(2)}) collective-permute-start(bf16[1024,128]{1,0:T(8,128)(2,1)S(1)} %get-tuple-element.177), channel_id=1, source_target_pairs={{0,2},{1,3},{2,0},{3,1},{4,6},{5,7},{6,4},{7,5},{8,10},{9,11},{10,... | collective-permute-start | bytes 786440 | tf_op jit(solution)/shard_map/ppermute | solution.py:450
  43.6 6.3 %collective-permute-start.13 = (bf16[128,256]{1,0:T(8,128)(2,1)S(1)}, bf16[128,256]{1,0:T(8,128)(2,1)S(1)}, u32[]{:S(2)}, u32[]{:S(2)}) collective-permute-start(bf16[128,256]{1,0:T(8,128)(2,1)S(1)} %get-tuple-element.173), channel_id=1, source_target_pairs={{4,0},{8,4},{12,8},{5,1},{9,5},{13,9},{6,2},{10,6},{14,10},{7,3},{... | collective-permute-start | bytes 196616 | tf_op jit(solution)/shard_map/ppermute | solution.py:473
  45.1 4.7 %collective-permute-start.14 = (bf16[128,256]{1,0:T(8,128)(2,1)S(1)}, bf16[128,256]{1,0:T(8,128)(2,1)S(1)}, u32[]{:S(2)}, u32[]{:S(2)}) collective-permute-start(bf16[128,256]{1,0:T(8,128)(2,1)S(1)} %get-tuple-element.174), channel_id=1, source_target_pairs={{0,2},{2,0},{1,3},{3,1},{4,6},{6,4},{5,7},{7,5},{8,10},{10,8},{9,1... | collective-permute-start | bytes 196616 | tf_op jit(solution)/shard_map/ppermute | solution.py:437
  49.9 13.0 %collective-permute-start.17 = (bf16[1024,128]{1,0:T(8,128)(2,1)S(1)}, bf16[1024,128]{1,0:T(8,128)(2,1)S(1)}, u32[]{:S(2)}, u32[]{:S(2)}) collective-permute-start(bf16[1024,128]{1,0:T(8,128)(2,1)S(1)} %get-tuple-element.194), channel_id=1, source_target_pairs={{0,2},{1,3},{2,0},{3,1},{4,6},{5,7},{6,4},{7,5},{8,10},{9,11},{10,... | collective-permute-start | bytes 786440 | tf_op jit(solution)/shard_map/ppermute | solution.py:450
  50.8 6.3 %collective-permute-start.16 = (bf16[512,128]{1,0:T(8,128)(2,1)S(1)}, bf16[512,128]{1,0:T(8,128)(2,1)S(1)}, u32[]{:S(2)}, u32[]{:S(2)}) collective-permute-start(bf16[512,128]{1,0:T(8,128)(2,1)S(1)} %get-tuple-element.190), channel_id=1, source_target_pairs={{0,4},{1,5},{2,6},{3,7},{4,0},{5,1},{6,2},{7,3},{8,12},{9,13},{10,... | collective-permute-start | bytes 393224 | tf_op jit(solution)/shard_map/ppermute | solution.py:450
  57.2 6.4 %collective-permute-start.18 = (bf16[1024,128]{1,0:T(8,128)(2,1)S(1)}, bf16[1024,128]{1,0:T(8,128)(2,1)S(1)}, u32[]{:S(2)}, u32[]{:S(2)}) collective-permute-start(bf16[1024,128]{1,0:T(8,128)(2,1)S(1)} %get-tuple-element.196), channel_id=1, source_target_pairs={{0,2},{1,5},{2,0},{3,7},{4,6},{5,1},{6,4},{7,3},{8,10},{9,13},{10,... | collective-permute-start | bytes 786440 | tf_op jit(solution)/shard_map/ppermute | solution.py:450
  58.7 8.6 %collective-permute-start.19 = (bf16[512,128]{1,0:T(8,128)(2,1)S(1)}, bf16[512,128]{1,0:T(8,128)(2,1)S(1)}, u32[]{:S(2)}, u32[]{:S(2)}) collective-permute-start(bf16[512,128]{1,0:T(8,128)(2,1)S(1)} %get-tuple-element.198), channel_id=1, source_target_pairs={{0,8},{1,9},{2,10},{3,11},{4,12},{5,13},{6,14},{7,15},{8,0},{9,1},... | collective-permute-start | bytes 393224 | tf_op jit(solution)/shard_map/ppermute | solution.py:450
  63.1 7.7 %collective-permute-start.20 = (bf16[512,128]{1,0:T(8,128)(2,1)S(1)}, bf16[512,128]{1,0:T(8,128)(2,1)S(1)}, u32[]{:S(2)}, u32[]{:S(2)}) collective-permute-start(bf16[512,128]{1,0:T(8,128)(2,1)S(1)} %get-tuple-element.200), channel_id=1, source_target_pairs={{0,4},{1,5},{2,6},{3,7},{4,0},{5,1},{6,2},{7,3},{8,12},{9,13},{10,... | collective-permute-start | bytes 393224 | tf_op jit(solution)/shard_map/ppermute | solution.py:450
  63.8 8.7 %collective-permute-start.21 = (bf16[512,128]{1,0:T(8,128)(2,1)S(1)}, bf16[512,128]{1,0:T(8,128)(2,1)S(1)}, u32[]{:S(2)}, u32[]{:S(2)}) collective-permute-start(bf16[512,128]{1,0:T(8,128)(2,1)S(1)} %get-tuple-element.202), channel_id=1, source_target_pairs={{0,4},{1,3},{2,6},{3,1},{4,0},{5,7},{6,2},{7,5},{8,12},{9,11},{10,... | collective-permute-start | bytes 393224 | tf_op jit(solution)/shard_map/ppermute | solution.py:450
  67.4 9.5 %collective-permute-start.22 = (bf16[512,128]{1,0:T(8,128)(2,1)S(1)}, bf16[512,128]{1,0:T(8,128)(2,1)S(1)}, u32[]{:S(2)}, u32[]{:S(2)}) collective-permute-start(bf16[512,128]{1,0:T(8,128)(2,1)S(1)} %get-tuple-element.204), channel_id=1, source_target_pairs={{0,4},{1,5},{2,6},{3,7},{4,0},{5,1},{6,2},{7,3},{8,12},{9,13},{10,... | collective-permute-start | bytes 393224 | tf_op jit(solution)/shard_map/ppermute | solution.py:450
  70.8 7.6 %collective-permute-start.23 = (bf16[512,128]{1,0:T(8,128)(2,1)S(1)}, bf16[512,128]{1,0:T(8,128)(2,1)S(1)}, u32[]{:S(2)}, u32[]{:S(2)}) collective-permute-start(bf16[512,128]{1,0:T(8,128)(2,1)S(1)} %get-tuple-element.206), channel_id=1, source_target_pairs={{0,8},{1,9},{2,10},{3,11},{4,12},{5,13},{6,14},{7,15},{8,0},{9,1},... | collective-permute-start | bytes 393224 | tf_op jit(solution)/shard_map/ppermute | solution.py:450
  72.5 9.2 %collective-permute-start.24 = (bf16[512,128]{1,0:T(8,128)(2,1)S(1)}, bf16[512,128]{1,0:T(8,128)(2,1)S(1)}, u32[]{:S(2)}, u32[]{:S(2)}) collective-permute-start(bf16[512,128]{1,0:T(8,128)(2,1)S(1)} %get-tuple-element.208), channel_id=1, source_target_pairs={{0,8},{1,9},{2,10},{3,11},{4,12},{5,13},{6,14},{7,15},{8,0},{9,1},... | collective-permute-start | bytes 393224 | tf_op jit(solution)/shard_map/ppermute | solution.py:450
  77.0 9.2 %collective-permute-start.28 = (bf16[1024,128]{1,0:T(8,128)(2,1)S(1)}, bf16[1024,128]{1,0:T(8,128)(2,1)S(1)}, u32[]{:S(2)}, u32[]{:S(2)}) collective-permute-start(bf16[1024,128]{1,0:T(8,128)(2,1)S(1)} %get-tuple-element.214), channel_id=1, source_target_pairs={{0,2},{1,3},{2,0},{3,1},{4,6},{5,7},{6,4},{7,5},{8,10},{9,11},{10,... | collective-permute-start | bytes 786440 | tf_op jit(solution)/shard_map/ppermute | solution.py:450
  78.5 5.0 %collective-permute-start.25 = (bf16[512,128]{1,0:T(8,128)(2,1)S(1)}, bf16[512,128]{1,0:T(8,128)(2,1)S(1)}, u32[]{:S(2)}, u32[]{:S(2)}) collective-permute-start(bf16[512,128]{1,0:T(8,128)(2,1)S(1)} %get-tuple-element.210), channel_id=1, source_target_pairs={{0,4},{1,5},{2,6},{3,7},{4,0},{5,1},{6,2},{7,3},{8,12},{9,13},{10,... | collective-permute-start | bytes 393224 | tf_op jit(solution)/shard_map/ppermute | solution.py:450
  81.7 5.0 %collective-permute-start.29 = (bf16[512,128]{1,0:T(8,128)(2,1)S(1)}, bf16[512,128]{1,0:T(8,128)(2,1)S(1)}, u32[]{:S(2)}, u32[]{:S(2)}) collective-permute-start(bf16[512,128]{1,0:T(8,128)(2,1)S(1)} %get-tuple-element.215), channel_id=1, source_target_pairs={{0,4},{1,3},{2,6},{3,1},{4,0},{5,7},{6,2},{7,5},{8,12},{9,11},{10,... | collective-permute-start | bytes 393224 | tf_op jit(solution)/shard_map/ppermute | solution.py:450
  81.8 2.5 %collective-permute-start.26 = (bf16[128,256]{1,0:T(8,128)(2,1)S(1)}, bf16[128,256]{1,0:T(8,128)(2,1)S(1)}, u32[]{:S(2)}, u32[]{:S(2)}) collective-permute-start(bf16[128,256]{1,0:T(8,128)(2,1)S(1)} %get-tuple-element.212), channel_id=1, source_target_pairs={{5,1},{7,3},{9,5},{11,7},{13,9},{15,11},{21,17},{23,19},{25,21},{2... | collective-permute-start | bytes 196616 | tf_op jit(solution)/shard_map/ppermute | solution.py:450
  83.6 9.0 %collective-permute-start.33 = (bf16[1024,128]{1,0:T(8,128)(2,1)S(1)}, bf16[1024,128]{1,0:T(8,128)(2,1)S(1)}, u32[]{:S(2)}, u32[]{:S(2)}) collective-permute-start(bf16[1024,128]{1,0:T(8,128)(2,1)S(1)} %get-tuple-element.225), channel_id=1, source_target_pairs={{0,2},{1,3},{2,0},{3,1},{4,6},{5,7},{6,4},{7,5},{8,10},{9,11},{10,... | collective-permute-start | bytes 786440 | tf_op jit(solution)/shard_map/ppermute | solution.py:450
  86.8 7.8 %collective-permute-start.30 = (f32[256,256]{1,0:T(8,128)S(1)}, f32[256,256]{1,0:T(8,128)S(1)}, u32[]{:S(2)}, u32[]{:S(2)}) collective-permute-start(f32[256,256]{1,0:T(8,128)S(1)} %get-tuple-element.218.refs_0_), channel_id=1, source_target_pairs={{1,0},{3,2},{5,4},{7,6},{9,8},{11,10},{13,12},{15,14},{17,16},{19,... | collective-permute-start | bytes 786440 | tf_op jit(solution)/shard_map/ppermute | solution.py:691
  88.1 6.5 %collective-permute-start.31 = (f32[256,256]{1,0:T(8,128)S(1)}, f32[256,256]{1,0:T(8,128)S(1)}, u32[]{:S(2)}, u32[]{:S(2)}) collective-permute-start(f32[256,256]{1,0:T(8,128)S(1)} %get-tuple-element.219.refs_1_), channel_id=1, source_target_pairs={{1,0},{3,2},{5,4},{7,6},{9,8},{11,10},{13,12},{15,14},{17,16},{19,... | collective-permute-start | bytes 786440 | tf_op jit(solution)/shard_map/ppermute | solution.py:691
  89.4 5.2 %collective-permute-start.32 = (f32[256,256]{1,0:T(8,128)S(1)}, f32[256,256]{1,0:T(8,128)S(1)}, u32[]{:S(2)}, u32[]{:S(2)}) collective-permute-start(f32[256,256]{1,0:T(8,128)S(1)} %get-tuple-element.220.refs_2_), channel_id=1, source_target_pairs={{1,0},{3,2},{5,4},{7,6},{9,8},{11,10},{13,12},{15,14},{17,16},{19,... | collective-permute-start | bytes 786440 | tf_op jit(solution)/shard_map/ppermute | solution.py:691
  90.7 30.3 %collective-permute-start.34 = (bf16[1024,128]{1,0:T(8,128)(2,1)S(1)}, bf16[1024,128]{1,0:T(8,128)(2,1)S(1)}, u32[]{:S(2)}, u32[]{:S(2)}) collective-permute-start(bf16[1024,128]{1,0:T(8,128)(2,1)S(1)} %get-tuple-element.234), channel_id=1, source_target_pairs={{0,2},{1,5},{2,0},{3,7},{4,6},{5,1},{6,4},{7,3},{8,10},{9,13},{10,... | collective-permute-start | bytes 786440 | tf_op jit(solution)/shard_map/ppermute | solution.py:450
  (15 other events, 54.0 us)

commit v18 on v16

--- a/solution.py
+++ b/solution.py
@@ -634,9 +634,7 @@
     for layer in reversed(range(layers)):
         state, at = back(layer, outs, at)
         arrived = [sums[above].got[0] for above in range(layer + 2, layers)]
-        if layer:
-            arrived += returned[layer]
-        at = sum_step([sums[layer]], at + arrived)
+        at = sum_step([sums[layer]], at + arrived + returned[layer])
         if layer:
             for above in range(layer + 1, layers):
                 at = sum_step([sums[above]], at)
@@ -646,7 +644,7 @@
         for layer in reversed(range(layers)):
             if sums[layer].done < count:
                 if layer == 0 and sums[0].done == count - 1:
-                    at = at + returned[0] + [sums[above].got[0] for above in range(2, layers)]
+                    at = at + [sums[above].got[0] for above in range(2, layers)]
                 at = sum_step([sums[layer]], at)
     grad, token = join(0, state, at)
     at = [token]

time: 96.8 us -> 103 us (1.064)
  starting transfers between devices: 41.3 us -> 51.6 us
  waiting for transfers between devices: 21.4 us -> 17.6 us
    ppermute x18, starting transfers between devices: 29.9 us -> 39.6 us  [over_mesh(): return lax.ppermute(x, ('chain', 'basin', 'feat'), perm)]
    ppermute x3, waiting for transfers between devices: 5.73 us -> 2.81 us  [backward(): up = lax.ppermute(grads[0], 'chain', [(c, c - 1) for c in range(1, chain)])]
  transfers between devices with their start and end apart: 32 -> 32, of which waited for: 13 -> 12; matrix products, arithmetic and copies ran while one was open for 1% -> 1% of each run, Pallas kernels for 26% -> 24%
where the time goes in v18:
time: 103 us
  starting transfers between devices  51.6 us (50%)
  Pallas kernels  30.6 us (30%)
  waiting for transfers between devices  17.6 us (17%)
  between operations  1.26 us (1%)
  local copies, waits for them, and re-layouts  1.2 us (1%)
    ppermute x18, starting transfers between devices, over_mesh(): return lax.ppermute(x, ('chain', 'basin', 'feat'), perm)  39.6 us
    pallas_call x33, Pallas kernels, call(): pl.pallas_call(lambda *refs: body(*refs[skipped:]), out_shape=[jax.ShapeD...  26.1 us
    ppermute x18, waiting for transfers between devices, over_mesh(): return lax.ppermute(x, ('chain', 'basin', 'feat'), perm)  11.2 us
    ppermute x11, starting transfers between devices, around(): return lax.ppermute(x, axis, [(i, (i + distance) % n) for i in range(n)])  7.86 us
    pallas_call x4, Pallas kernels, write(): pl.pallas_call(functools.partial(write_kernel, layer, sums[layer].stages[...  4.42 us
    ppermute x3, starting transfers between devices, backward(): up = lax.ppermute(grads[0], 'chain', [(c, c - 1) for c in range(1, chain)])  4.1 us
    ppermute x11, waiting for transfers between devices, around(): return lax.ppermute(x, axis, [(i, (i + distance) % n) for i in range(n)])  3.54 us
    ppermute x3, waiting for transfers between devices, backward(): up = lax.ppermute(grads[0], 'chain', [(c, c - 1) for c in range(1, chain)])  2.81 us
  transfers between devices with their start and end apart: 32, of which 12 were waited for; matrix products, arithmetic and copies ran while one was open for 1% of the time, Pallas kernels for 24%

profile of v18, /device:TPU:0, one launch (start us, length us, event | category | flops | bytes accessed | tf_op | source)
XLA Modules:
  0.0 102.9 jit_solution(416997179222500783)
XLA Ops:
  3.3 4.9 %collective-permute-start = (bf16[128,256]{1,0:T(8,128)(2,1)S(1)}, bf16[128,256]{1,0:T(8,128)(2,1)S(1)}, u32[]{:S(2)}, u32[]{:S(2)}) collective-permute-start(bf16[128,256]{1,0:T(8,128)(2,1)S(1)} %get-tuple-element.117), channel_id=1, source_target_pairs={{0,4},{2,6},{5,9},{7,11},{8,12},{10,14},{16,20},{18,22},{21,25},{2... | collective-permute-start | bytes 196616 | tf_op jit(solution)/shard_map/ppermute | solution.py:423
  8.2 1.6 %collective-permute-start.3 = (bf16[128,256]{1,0:T(8,128)(2,1)S(1)}, bf16[128,256]{1,0:T(8,128)(2,1)S(1)}, u32[]{:S(2)}, u32[]{:S(2)}) collective-permute-start(bf16[128,256]{1,0:T(8,128)(2,1)S(1)} %get-tuple-element.124), channel_id=1, source_target_pairs={{0,2},{2,0},{1,3},{3,1},{4,6},{6,4},{5,7},{7,5},{8,10},{10,8},{9,1... | collective-permute-start | bytes 196616 | tf_op jit(solution)/shard_map/ppermute | solution.py:410
  11.8 1.6 %adjacency.1 = (bf16[768,768]{1,0:T(8,128)(2,1)S(1)}, bf16[768,768]{1,0:T(8,128)(2,1)S(1)}, bf16[768,256]{1,0:T(8,128)(2,1)S(1)}, bf16[256,768]{1,0:T(8,128)(2,1)S(1)}) custom-call(s32[4,6]{1,0:T(4,128)S(1)} %bitcast.4, bf16[6,4,128,128]{3,2,1,0:T(8,128)(2,1)S(1)} %copy-done.3, bf16[128,768]{1,0:T(8,128)(2,1)S(1)} %get-tuple-element.118.refs_2_, ...), custom_call_target="tpu_custom_call" | custom-call | flops 150994944 | bytes 4000000 | tf_op jit(solution)/shard_map/adjacency/pallas_call | solution.py:32
  15.8 2.8 %collective-permute-start.5 = (bf16[128,256]{1,0:T(8,128)(2,1)S(1)}, bf16[128,256]{1,0:T(8,128)(2,1)S(1)}, u32[]{:S(2)}, u32[]{:S(2)}) collective-permute-start(bf16[128,256]{1,0:T(8,128)(2,1)S(1)} %get-tuple-element.128), channel_id=1, source_target_pairs={{0,4},{2,6},{5,9},{7,11},{8,12},{10,14},{16,20},{18,22},{21,25},{2... | collective-permute-start | bytes 196616 | tf_op jit(solution)/shard_map/ppermute | solution.py:423
  19.1 1.6 %local1.1 = (bf16[768,256]{1,0:T(8,128)(2,1)S(1)}, bf16[768,512]{1,0:T(8,128)(2,1)S(1)}, bf16[768,512]{1,0:T(8,128)(2,1)S(1)}, bf16[512,768]{1,0:T(8,128)(2,1)S(1)}, bf16[256,768]{1,0:T(8,128)(2,1)S(1)}) custom-call(bf16[768,256]{1,0:T(8,128)(2,1)S(1)} %get-tuple-element.129.refs_0_, bf16[3,256,512]{2,1,0:T(8,128)(2,1)S(1)} %copy-done, ...), custom_call_target="tpu_custom_call" | custom-call | flops 805306368 | bytes 4000000 | tf_op jit(solution)/shard_map/local1/pallas_call | solution.py:32
  20.8 2.0 %collective-permute-done.6.refs_7_.refs_14_ = bf16[128,256]{1,0:T(8,128)(2,1)S(1)} collective-permute-done((bf16[128,256]{1,0:T(8,128)(2,1)S(1)}, bf16[128,256]{1,0:T(8,128)(2,1)S(1)}, u32[]{:S(2)}, u32[]{:S(2)}) %collective-permute-start.6) | collective-permute-done | bytes 65568 | tf_op jit(solution)/shard_map/ppermute | solution.py:410
  24.9 2.3 %collective-permute-start.8 = (bf16[128,256]{1,0:T(8,128)(2,1)S(1)}, bf16[128,256]{1,0:T(8,128)(2,1)S(1)}, u32[]{:S(2)}, u32[]{:S(2)}) collective-permute-start(bf16[128,256]{1,0:T(8,128)(2,1)S(1)} %get-tuple-element.135), channel_id=1, source_target_pairs={{0,4},{2,6},{5,9},{7,11},{8,12},{10,14},{16,20},{18,22},{21,25},{2... | collective-permute-start | bytes 196616 | tf_op jit(solution)/shard_map/ppermute | solution.py:423
  28.6 1.6 %local2.1 = (bf16[768,256]{1,0:T(8,128)(2,1)S(1)}, bf16[768,512]{1,0:T(8,128)(2,1)S(1)}, bf16[768,512]{1,0:T(8,128)(2,1)S(1)}, bf16[512,768]{1,0:T(8,128)(2,1)S(1)}, bf16[256,768]{1,0:T(8,128)(2,1)S(1)}) custom-call(bf16[768,256]{1,0:T(8,128)(2,1)S(1)} %get-tuple-element.136.refs_0_, bf16[3,256,512]{2,1,0:T(8,128)(2,1)S(1)} %copy-done, ...), custom_call_target="tpu_custom_call" | custom-call | flops 805306368 | bytes 4000000 | tf_op jit(solution)/shard_map/local2/pallas_call | solution.py:32
  32.5 2.0 %turn.1 = (f32[768,256]{1,0:T(8,128)S(1)}, bf16[768,256]{1,0:T(8,128)(2,1)S(1)}, bf16[256,256]{1,0:T(8,128)(2,1)S(1)}, bf16[256,256]{1,0:T(8,128)(2,1)S(1)}, bf1...) custom-call(f32[768,256]{1,0:T(8,128)S(1)} %get-tuple-element.134.re, ...), custom_call_target="tpu_custom_call" | custom-call | flops 536870912 | bytes 4000000 | tf_op jit(solution)/shard_map/turn/pallas_call | solution.py:32
  35.8 1.4 %collective-permute-start.12 = (bf16[128,256]{1,0:T(8,128)(2,1)S(1)}, bf16[128,256]{1,0:T(8,128)(2,1)S(1)}, u32[]{:S(2)}, u32[]{:S(2)}) collective-permute-start(bf16[128,256]{1,0:T(8,128)(2,1)S(1)} %get-tuple-element.154), channel_id=1, source_target_pairs={{0,2},{2,0},{1,3},{3,1},{4,6},{6,4},{5,7},{7,5},{8,10},{10,8},{9,1... | collective-permute-start | bytes 196616 | tf_op jit(solution)/shard_map/ppermute | solution.py:410
  37.2 2.4 %back2.1 = (f32[768,256]{1,0:T(8,128)S(1)}, f32[2048,128]{1,0:T(8,128)S(1)}) custom-call(bf16[768,256]{1,0:T(8,128)(2,1)S(1)} %get-tuple-element.142.refs_0_, bf16[768,768]{1,0:T(8,128)(2,1)S(1)} %get-tuple-element.143.refs_1_.refs_2_, bf16[768,512]{1,0:T(8,128)(2,1)S(1)} %get-tuple-element.144.refs_2_, bf16[768,512]{1,0:T(8,128)(2,1)S(1)} %get-tuple-element.145.refs_3_, ...), custom_call_target="tpu_custom_call" | custom-call | flops 2717908992 | bytes 4000000 | tf_op jit(solution)/shard_map/back2/pallas_call | solution.py:32
  40.8 1.4 %collective-permute-start.15 = (bf16[1024,128]{1,0:T(8,128)(2,1)S(1)}, bf16[1024,128]{1,0:T(8,128)(2,1)S(1)}, u32[]{:S(2)}, u32[]{:S(2)}) collective-permute-start(bf16[1024,128]{1,0:T(8,128)(2,1)S(1)} %get-tuple-element.173), channel_id=1, source_target_pairs={{0,2},{1,3},{2,0},{3,1},{4,6},{5,7},{6,4},{7,5},{8,10},{9,11},{10,... | collective-permute-start | bytes 786440 | tf_op jit(solution)/shard_map/ppermute | solution.py:423
  42.1 1.5 %join2.1 = (f32[768,256]{1,0:T(8,128)S(1)}, bf16[768,256]{1,0:T(8,128)(2,1)S(1)}, bf16[256,256]{1,0:T(8,128)(2,1)S(1)}, bf16[256,256]{1,0:T(8,128)(2,1)S(1)}, bf...) custom-call(f32[1024,128]{1,0:T(8,128)S(1)} %get-tuple-element.156.r, ...), custom_call_target="tpu_custom_call" | custom-call | flops 536870912 | bytes 4000000 | tf_op jit(solution)/shard_map/join2/pallas_call | solution.py:32
  45.7 2.4 %back1.1 = (f32[768,256]{1,0:T(8,128)S(1)}, f32[2048,128]{1,0:T(8,128)S(1)}) custom-call(bf16[768,256]{1,0:T(8,128)(2,1)S(1)} %get-tuple-element.159.refs_0_.refs_1_, bf16[768,256]{1,0:T(8,128)(2,1)S(1)} %get-tuple-element.159.refs_0_.refs_1_, bf16[768,768]{1,0:T(8,128)(2,1)S(1)} %get-tuple-element.143.refs_1_.refs_2_, ...), custom_call_target="tpu_custom_call" | custom-call | flops 2717908992 | bytes 4000000 | tf_op jit(solution)/shard_map/back1/pallas_call | solution.py:32
  48.1 1.7 %collective-permute-done.13.refs_1_.refs_10_ = bf16[128,256]{1,0:T(8,128)(2,1)S(1)} collective-permute-done((bf16[128,256]{1,0:T(8,128)(2,1)S(1)}, bf16[128,256]{1,0:T(8,128)(2,1)S(1)}, u32[]{:S(2)}, u32[]{:S(2)}) %collective-permute-start.13) | collective-permute-done | bytes 65568 | tf_op jit(solution)/shard_map/ppermute | solution.py:446
  50.8 1.5 %join1.1 = (f32[768,256]{1,0:T(8,128)S(1)}, bf16[768,256]{1,0:T(8,128)(2,1)S(1)}, bf16[256,256]{1,0:T(8,128)(2,1)S(1)}, bf16[256,256]{1,0:T(8,128)(2,1)S(1)}, bf...) custom-call(f32[512,128]{1,0:T(8,128)S(1)} %get-tuple-element.174.re, ...), custom_call_target="tpu_custom_call" | custom-call | flops 536870912 | bytes 4000000 | tf_op jit(solution)/shard_map/join1/pallas_call | solution.py:32
  52.3 1.5 %collective-permute-start.17 = (bf16[128,256]{1,0:T(8,128)(2,1)S(1)}, bf16[128,256]{1,0:T(8,128)(2,1)S(1)}, u32[]{:S(2)}, u32[]{:S(2)}) collective-permute-start(bf16[128,256]{1,0:T(8,128)(2,1)S(1)} %get-tuple-element.187), channel_id=1, source_target_pairs={{4,0},{8,4},{12,8},{5,1},{9,5},{13,9},{6,2},{10,6},{14,10},{7,3},{... | collective-permute-start | bytes 196616 | tf_op jit(solution)/shard_map/ppermute | solution.py:446
  53.8 1.4 %collective-permute-start.18 = (bf16[128,256]{1,0:T(8,128)(2,1)S(1)}, bf16[128,256]{1,0:T(8,128)(2,1)S(1)}, u32[]{:S(2)}, u32[]{:S(2)}) collective-permute-start(bf16[128,256]{1,0:T(8,128)(2,1)S(1)} %get-tuple-element.188), channel_id=1, source_target_pairs={{0,2},{2,0},{1,3},{3,1},{4,6},{6,4},{5,7},{7,5},{8,10},{10,8},{9,1... | collective-permute-start | bytes 196616 | tf_op jit(solution)/shard_map/ppermute | solution.py:410
  55.2 2.9 %collective-permute-start.16 = (bf16[512,128]{1,0:T(8,128)(2,1)S(1)}, bf16[512,128]{1,0:T(8,128)(2,1)S(1)}, u32[]{:S(2)}, u32[]{:S(2)}) collective-permute-start(bf16[512,128]{1,0:T(8,128)(2,1)S(1)} %get-tuple-element.186), channel_id=1, source_target_pairs={{0,4},{1,5},{2,6},{3,7},{4,0},{5,1},{6,2},{7,3},{8,12},{9,13},{10,... | collective-permute-start | bytes 393224 | tf_op jit(solution)/shard_map/ppermute | solution.py:423
  58.1 2.4 %back0.1 = (f32[768,256]{1,0:T(8,128)S(1)}, f32[2048,128]{1,0:T(8,128)S(1)}) custom-call(bf16[768,256]{1,0:T(8,128)(2,1)S(1)} %get-tuple-element.176.refs_0_.refs_1_, bf16[768,256]{1,0:T(8,128)(2,1)S(1)} %get-tuple-element.176.refs_0_.refs_1_, bf16[768,768]{1,0:T(8,128)(2,1)S(1)} %get-tuple-element.143.refs_1_.refs_2_, ...), custom_call_target="tpu_custom_call" | custom-call | flops 2717908992 | bytes 4000000 | tf_op jit(solution)/shard_map/back0/pallas_call | solution.py:32
  60.5 3.3 %collective-permute-done.16.refs_1_.refs_2_ = bf16[512,128]{1,0:T(8,128)(2,1)S(1)} collective-permute-done((bf16[512,128]{1,0:T(8,128)(2,1)S(1)}, bf16[512,128]{1,0:T(8,128)(2,1)S(1)}, u32[]{:S(2)}, u32[]{:S(2)}) %collective-permute-start.16) | collective-permute-done | bytes 131104 | tf_op jit(solution)/shard_map/ppermute | solution.py:423
  64.0 3.6 %collective-permute-start.21 = (bf16[512,128]{1,0:T(8,128)(2,1)S(1)}, bf16[512,128]{1,0:T(8,128)(2,1)S(1)}, u32[]{:S(2)}, u32[]{:S(2)}) collective-permute-start(bf16[512,128]{1,0:T(8,128)(2,1)S(1)} %get-tuple-element.196), channel_id=1, source_target_pairs={{0,8},{1,9},{2,10},{3,11},{4,12},{5,13},{6,14},{7,15},{8,0},{9,1},... | collective-permute-start | bytes 393224 | tf_op jit(solution)/shard_map/ppermute | solution.py:423
  67.7 2.5 %collective-permute-start.22 = (bf16[512,128]{1,0:T(8,128)(2,1)S(1)}, bf16[512,128]{1,0:T(8,128)(2,1)S(1)}, u32[]{:S(2)}, u32[]{:S(2)}) collective-permute-start(bf16[512,128]{1,0:T(8,128)(2,1)S(1)} %get-tuple-element.198), channel_id=1, source_target_pairs={{0,4},{1,5},{2,6},{3,7},{4,0},{5,1},{6,2},{7,3},{8,12},{9,13},{10,... | collective-permute-start | bytes 393224 | tf_op jit(solution)/shard_map/ppermute | solution.py:423
  70.2 1.5 %collective-permute-done.20.refs_2_ = bf16[1024,128]{1,0:T(8,128)(2,1)S(1)} collective-permute-done((bf16[1024,128]{1,0:T(8,128)(2,1)S(1)}, bf16[1024,128]{1,0:T(8,128)(2,1)S(1)}, u32[]{:S(2)}, u32[]{:S(2)}) %collective-permute-start.20) | collective-permute-done | bytes 262176 | tf_op jit(solution)/shard_map/ppermute | solution.py:423
  72.6 4.7 %collective-permute-start.24 = (bf16[512,128]{1,0:T(8,128)(2,1)S(1)}, bf16[512,128]{1,0:T(8,128)(2,1)S(1)}, u32[]{:S(2)}, u32[]{:S(2)}) collective-permute-start(bf16[512,128]{1,0:T(8,128)(2,1)S(1)} %get-tuple-element.202), channel_id=1, source_target_pairs={{0,4},{1,5},{2,6},{3,7},{4,0},{5,1},{6,2},{7,3},{8,12},{9,13},{10,... | collective-permute-start | bytes 393224 | tf_op jit(solution)/shard_map/ppermute | solution.py:423
  77.3 3.6 %collective-permute-start.25 = (bf16[512,128]{1,0:T(8,128)(2,1)S(1)}, bf16[512,128]{1,0:T(8,128)(2,1)S(1)}, u32[]{:S(2)}, u32[]{:S(2)}) collective-permute-start(bf16[512,128]{1,0:T(8,128)(2,1)S(1)} %get-tuple-element.204), channel_id=1, source_target_pairs={{0,8},{1,9},{2,10},{3,11},{4,12},{5,13},{6,14},{7,15},{8,0},{9,1},... | collective-permute-start | bytes 393224 | tf_op jit(solution)/shard_map/ppermute | solution.py:423
  81.1 2.2 %collective-permute-start.28 = (bf16[1024,128]{1,0:T(8,128)(2,1)S(1)}, bf16[1024,128]{1,0:T(8,128)(2,1)S(1)}, u32[]{:S(2)}, u32[]{:S(2)}) collective-permute-start(bf16[1024,128]{1,0:T(8,128)(2,1)S(1)} %get-tuple-element.210), channel_id=1, source_target_pairs={{0,2},{1,3},{2,0},{3,1},{4,6},{5,7},{6,4},{7,5},{8,10},{9,11},{10,... | collective-permute-start | bytes 786440 | tf_op jit(solution)/shard_map/ppermute | solution.py:423
  83.9 2.1 %collective-permute-start.27 = (bf16[512,128]{1,0:T(8,128)(2,1)S(1)}, bf16[512,128]{1,0:T(8,128)(2,1)S(1)}, u32[]{:S(2)}, u32[]{:S(2)}) collective-permute-start(bf16[512,128]{1,0:T(8,128)(2,1)S(1)} %get-tuple-element.208), channel_id=1, source_target_pairs={{0,4},{1,5},{2,6},{3,7},{4,0},{5,1},{6,2},{7,3},{8,12},{9,13},{10,... | collective-permute-start | bytes 393224 | tf_op jit(solution)/shard_map/ppermute | solution.py:423
  86.1 2.2 %collective-permute-done.26.refs_2_ = bf16[512,128]{1,0:T(8,128)(2,1)S(1)} collective-permute-done((bf16[512,128]{1,0:T(8,128)(2,1)S(1)}, bf16[512,128]{1,0:T(8,128)(2,1)S(1)}, u32[]{:S(2)}, u32[]{:S(2)}) %collective-permute-start.26) | collective-permute-done | bytes 131104 | tf_op jit(solution)/shard_map/ppermute | solution.py:423
  88.4 2.0 %collective-permute-done.27.refs_2_ = bf16[512,128]{1,0:T(8,128)(2,1)S(1)} collective-permute-done((bf16[512,128]{1,0:T(8,128)(2,1)S(1)}, bf16[512,128]{1,0:T(8,128)(2,1)S(1)}, u32[]{:S(2)}, u32[]{:S(2)}) %collective-permute-start.27) | collective-permute-done | bytes 131104 | tf_op jit(solution)/shard_map/ppermute | solution.py:423
  90.5 3.6 %collective-permute-start.30 = (bf16[1024,128]{1,0:T(8,128)(2,1)S(1)}, bf16[1024,128]{1,0:T(8,128)(2,1)S(1)}, u32[]{:S(2)}, u32[]{:S(2)}) collective-permute-start(bf16[1024,128]{1,0:T(8,128)(2,1)S(1)} %get-tuple-element.219), channel_id=1, source_target_pairs={{0,2},{1,3},{2,0},{3,1},{4,6},{5,7},{6,4},{7,5},{8,10},{9,11},{10,... | collective-permute-start | bytes 786440 | tf_op jit(solution)/shard_map/ppermute | solution.py:423
  101.3 1.4 %write0.3 = (f32[3,256,512]{2,1,0:T(8,128)}, f32[3,512,256]{2,1,0:T(8,128)}, f32[8,128]{1,0:T(8,128)}) custom-call(f32[3,256,512]{2,1,0:T(8,128)} %get-tuple-element.223.refs_0_, f32[3,512,256]{2,1,0:T(8,128)} %get-tuple-element.224.refs_1_, f32[8,128]{1,0:T(8,128)S(1)} %get-tuple-element.225.refs_2_, ...), custom_call_target="tpu_custom_call", output_to_operand_aliasing={{0}: (0, {}), {1}: (1, {})} | custom-call | flops 1 | bytes 1 | tf_op jit(solution)/shard_map/write0/pallas_call | solution.py:606
  (82 shorter events, 28.1 us)
Async XLA Ops:
  0.7 9.1 %collective-permute-start.1 = (bf16[3,256,512]{2,1,0:T(8,128)(2,1)}, bf16[3,256,512]{2,1,0:T(8,128)(2,1)S(1)}, u32[]{:S(2)}, u32[]{:S(2)}) collective-permute-start(bf16[3,256,512]{2,1,0:T(8,128)(2,1)} %refs_7_.5), channel_id=1, source_target_pairs={{0,1},{1,0},{2,3},{3,2},{4,5},{5,4},{6,7},{7,6},{8,9},{9,8},{10,11... | collective-permute-start | bytes 2359304 | tf_op jit(solution)/shard_map/ppermute | solution.py:410
  1.2 8.6 %collective-permute-start.2 = (bf16[3,512,256]{2,1,0:T(8,128)(2,1)}, bf16[3,512,256]{2,1,0:T(8,128)(2,1)S(1)}, u32[]{:S(2)}, u32[]{:S(2)}) collective-permute-start(bf16[3,512,256]{2,1,0:T(8,128)(2,1)} %refs_9_.3), channel_id=1, source_target_pairs={{0,1},{1,0},{2,3},{3,2},{4,5},{5,4},{6,7},{7,6},{8,9},{9,8},{10,11... | collective-permute-start | bytes 2359304 | tf_op jit(solution)/shard_map/ppermute | solution.py:410
  3.3 10.1 %collective-permute-start = (bf16[128,256]{1,0:T(8,128)(2,1)S(1)}, bf16[128,256]{1,0:T(8,128)(2,1)S(1)}, u32[]{:S(2)}, u32[]{:S(2)}) collective-permute-start(bf16[128,256]{1,0:T(8,128)(2,1)S(1)} %get-tuple-element.117), channel_id=1, source_target_pairs={{0,4},{2,6},{5,9},{7,11},{8,12},{10,14},{16,20},{18,22},{21,25},{2... | collective-permute-start | bytes 196616 | tf_op jit(solution)/shard_map/ppermute | solution.py:423
  8.2 5.2 %collective-permute-start.3 = (bf16[128,256]{1,0:T(8,128)(2,1)S(1)}, bf16[128,256]{1,0:T(8,128)(2,1)S(1)}, u32[]{:S(2)}, u32[]{:S(2)}) collective-permute-start(bf16[128,256]{1,0:T(8,128)(2,1)S(1)} %get-tuple-element.124), channel_id=1, source_target_pairs={{0,2},{2,0},{1,3},{3,1},{4,6},{6,4},{5,7},{7,5},{8,10},{10,8},{9,1... | collective-permute-start | bytes 196616 | tf_op jit(solution)/shard_map/ppermute | solution.py:410
  13.4 1.3 %collective-permute-start.4 = (bf16[128,256]{1,0:T(8,128)(2,1)S(1)}, bf16[128,256]{1,0:T(8,128)(2,1)S(1)}, u32[]{:S(2)}, u32[]{:S(2)}) collective-permute-start(bf16[128,256]{1,0:T(8,128)(2,1)S(1)} %collective-permute-done.refs_8_.refs_12_), channel_id=1, source_target_pairs={{0,1},{1,0},{2,3},{3,2},{4,5},{5,4},{6,7},{7,6},{8,9},{9,8},{10,11... | collective-permute-start | bytes 196616 | tf_op jit(solution)/shard_map/ppermute | solution.py:410
  15.8 5.0 %collective-permute-start.5 = (bf16[128,256]{1,0:T(8,128)(2,1)S(1)}, bf16[128,256]{1,0:T(8,128)(2,1)S(1)}, u32[]{:S(2)}, u32[]{:S(2)}) collective-permute-start(bf16[128,256]{1,0:T(8,128)(2,1)S(1)} %get-tuple-element.128), channel_id=1, source_target_pairs={{0,4},{2,6},{5,9},{7,11},{8,12},{10,14},{16,20},{18,22},{21,25},{2... | collective-permute-start | bytes 196616 | tf_op jit(solution)/shard_map/ppermute | solution.py:423
  18.5 4.3 %collective-permute-start.6 = (bf16[128,256]{1,0:T(8,128)(2,1)S(1)}, bf16[128,256]{1,0:T(8,128)(2,1)S(1)}, u32[]{:S(2)}, u32[]{:S(2)}) collective-permute-start(bf16[128,256]{1,0:T(8,128)(2,1)S(1)} %get-tuple-element.132), channel_id=1, source_target_pairs={{0,2},{2,0},{1,3},{3,1},{4,6},{6,4},{5,7},{7,5},{8,10},{10,8},{9,1... | collective-permute-start | bytes 196616 | tf_op jit(solution)/shard_map/ppermute | solution.py:410
  20.8 3.1 %collective-permute-start.7 = (bf16[128,256]{1,0:T(8,128)(2,1)S(1)}, bf16[128,256]{1,0:T(8,128)(2,1)S(1)}, u32[]{:S(2)}, u32[]{:S(2)}) collective-permute-start(bf16[128,256]{1,0:T(8,128)(2,1)S(1)} %collective-permute-done.5.refs_8_.refs_12_), channel_id=1, source_target_pairs={{0,1},{1,0},{2,3},{3,2},{4,5},{5,4},{6,7},{7,6},{8,9},{9,8},{10,11... | collective-permute-start | bytes 196616 | tf_op jit(solution)/shard_map/ppermute | solution.py:410
  24.9 5.2 %collective-permute-start.8 = (bf16[128,256]{1,0:T(8,128)(2,1)S(1)}, bf16[128,256]{1,0:T(8,128)(2,1)S(1)}, u32[]{:S(2)}, u32[]{:S(2)}) collective-permute-start(bf16[128,256]{1,0:T(8,128)(2,1)S(1)} %get-tuple-element.135), channel_id=1, source_target_pairs={{0,4},{2,6},{5,9},{7,11},{8,12},{10,14},{16,20},{18,22},{21,25},{2... | collective-permute-start | bytes 196616 | tf_op jit(solution)/shard_map/ppermute | solution.py:423
  27.2 4.3 %collective-permute-start.9 = (bf16[128,256]{1,0:T(8,128)(2,1)S(1)}, bf16[128,256]{1,0:T(8,128)(2,1)S(1)}, u32[]{:S(2)}, u32[]{:S(2)}) collective-permute-start(bf16[128,256]{1,0:T(8,128)(2,1)S(1)} %get-tuple-element.139), channel_id=1, source_target_pairs={{0,2},{2,0},{1,3},{3,1},{4,6},{6,4},{5,7},{7,5},{8,10},{10,8},{9,1... | collective-permute-start | bytes 196616 | tf_op jit(solution)/shard_map/ppermute | solution.py:410
  30.2 2.3 %collective-permute-start.10 = (bf16[128,256]{1,0:T(8,128)(2,1)S(1)}, bf16[128,256]{1,0:T(8,128)(2,1)S(1)}, u32[]{:S(2)}, u32[]{:S(2)}) collective-permute-start(bf16[128,256]{1,0:T(8,128)(2,1)S(1)} %collective-permute-done.8.refs_9_), channel_id=1, source_target_pairs={{0,1},{1,0},{2,3},{3,2},{4,5},{5,4},{6,7},{7,6},{8,9},{9,8},{10,11... | collective-permute-start | bytes 196616 | tf_op jit(solution)/shard_map/ppermute | solution.py:410
  34.5 6.2 %collective-permute-start.11 = (bf16[128,256]{1,0:T(8,128)(2,1)S(1)}, bf16[128,256]{1,0:T(8,128)(2,1)S(1)}, u32[]{:S(2)}, u32[]{:S(2)}) collective-permute-start(bf16[128,256]{1,0:T(8,128)(2,1)S(1)} %get-tuple-element.153), channel_id=1, source_target_pairs={{4,0},{8,4},{12,8},{5,1},{9,5},{13,9},{6,2},{10,6},{14,10},{7,3},{... | collective-permute-start | bytes 196616 | tf_op jit(solution)/shard_map/ppermute | solution.py:446
  35.8 4.9 %collective-permute-start.12 = (bf16[128,256]{1,0:T(8,128)(2,1)S(1)}, bf16[128,256]{1,0:T(8,128)(2,1)S(1)}, u32[]{:S(2)}, u32[]{:S(2)}) collective-permute-start(bf16[128,256]{1,0:T(8,128)(2,1)S(1)} %get-tuple-element.154), channel_id=1, source_target_pairs={{0,2},{2,0},{1,3},{3,1},{4,6},{6,4},{5,7},{7,5},{8,10},{10,8},{9,1... | collective-permute-start | bytes 196616 | tf_op jit(solution)/shard_map/ppermute | solution.py:410
  40.8 10.0 %collective-permute-start.15 = (bf16[1024,128]{1,0:T(8,128)(2,1)S(1)}, bf16[1024,128]{1,0:T(8,128)(2,1)S(1)}, u32[]{:S(2)}, u32[]{:S(2)}) collective-permute-start(bf16[1024,128]{1,0:T(8,128)(2,1)S(1)} %get-tuple-element.173), channel_id=1, source_target_pairs={{0,2},{1,3},{2,0},{3,1},{4,6},{5,7},{6,4},{7,5},{8,10},{9,11},{10,... | collective-permute-start | bytes 786440 | tf_op jit(solution)/shard_map/ppermute | solution.py:423
  43.6 6.3 %collective-permute-start.13 = (bf16[128,256]{1,0:T(8,128)(2,1)S(1)}, bf16[128,256]{1,0:T(8,128)(2,1)S(1)}, u32[]{:S(2)}, u32[]{:S(2)}) collective-permute-start(bf16[128,256]{1,0:T(8,128)(2,1)S(1)} %get-tuple-element.169), channel_id=1, source_target_pairs={{4,0},{8,4},{12,8},{5,1},{9,5},{13,9},{6,2},{10,6},{14,10},{7,3},{... | collective-permute-start | bytes 196616 | tf_op jit(solution)/shard_map/ppermute | solution.py:446
  44.9 5.0 %collective-permute-start.14 = (bf16[128,256]{1,0:T(8,128)(2,1)S(1)}, bf16[128,256]{1,0:T(8,128)(2,1)S(1)}, u32[]{:S(2)}, u32[]{:S(2)}) collective-permute-start(bf16[128,256]{1,0:T(8,128)(2,1)S(1)} %get-tuple-element.170), channel_id=1, source_target_pairs={{0,2},{2,0},{1,3},{3,1},{4,6},{6,4},{5,7},{7,5},{8,10},{10,8},{9,1... | collective-permute-start | bytes 196616 | tf_op jit(solution)/shard_map/ppermute | solution.py:410
  49.9 17.7 %collective-permute-start.19 = (bf16[1024,128]{1,0:T(8,128)(2,1)S(1)}, bf16[1024,128]{1,0:T(8,128)(2,1)S(1)}, u32[]{:S(2)}, u32[]{:S(2)}) collective-permute-start(bf16[1024,128]{1,0:T(8,128)(2,1)S(1)} %get-tuple-element.192), channel_id=1, source_target_pairs={{0,2},{1,3},{2,0},{3,1},{4,6},{5,7},{6,4},{7,5},{8,10},{9,11},{10,... | collective-permute-start | bytes 786440 | tf_op jit(solution)/shard_map/ppermute | solution.py:423
  52.3 8.2 %collective-permute-start.17 = (bf16[128,256]{1,0:T(8,128)(2,1)S(1)}, bf16[128,256]{1,0:T(8,128)(2,1)S(1)}, u32[]{:S(2)}, u32[]{:S(2)}) collective-permute-start(bf16[128,256]{1,0:T(8,128)(2,1)S(1)} %get-tuple-element.187), channel_id=1, source_target_pairs={{4,0},{8,4},{12,8},{5,1},{9,5},{13,9},{6,2},{10,6},{14,10},{7,3},{... | collective-permute-start | bytes 196616 | tf_op jit(solution)/shard_map/ppermute | solution.py:446
  53.8 6.7 %collective-permute-start.18 = (bf16[128,256]{1,0:T(8,128)(2,1)S(1)}, bf16[128,256]{1,0:T(8,128)(2,1)S(1)}, u32[]{:S(2)}, u32[]{:S(2)}) collective-permute-start(bf16[128,256]{1,0:T(8,128)(2,1)S(1)} %get-tuple-element.188), channel_id=1, source_target_pairs={{0,2},{2,0},{1,3},{3,1},{4,6},{6,4},{5,7},{7,5},{8,10},{10,8},{9,1... | collective-permute-start | bytes 196616 | tf_op jit(solution)/shard_map/ppermute | solution.py:410
  55.2 8.6 %collective-permute-start.16 = (bf16[512,128]{1,0:T(8,128)(2,1)S(1)}, bf16[512,128]{1,0:T(8,128)(2,1)S(1)}, u32[]{:S(2)}, u32[]{:S(2)}) collective-permute-start(bf16[512,128]{1,0:T(8,128)(2,1)S(1)} %get-tuple-element.186), channel_id=1, source_target_pairs={{0,4},{1,5},{2,6},{3,7},{4,0},{5,1},{6,2},{7,3},{8,12},{9,13},{10,... | collective-permute-start | bytes 393224 | tf_op jit(solution)/shard_map/ppermute | solution.py:423
  63.9 7.8 %collective-permute-start.20 = (bf16[1024,128]{1,0:T(8,128)(2,1)S(1)}, bf16[1024,128]{1,0:T(8,128)(2,1)S(1)}, u32[]{:S(2)}, u32[]{:S(2)}) collective-permute-start(bf16[1024,128]{1,0:T(8,128)(2,1)S(1)} %get-tuple-element.194), channel_id=1, source_target_pairs={{0,2},{1,5},{2,0},{3,7},{4,6},{5,1},{6,4},{7,3},{8,10},{9,13},{10,... | collective-permute-start | bytes 786440 | tf_op jit(solution)/shard_map/ppermute | solution.py:423
  64.0 8.5 %collective-permute-start.21 = (bf16[512,128]{1,0:T(8,128)(2,1)S(1)}, bf16[512,128]{1,0:T(8,128)(2,1)S(1)}, u32[]{:S(2)}, u32[]{:S(2)}) collective-permute-start(bf16[512,128]{1,0:T(8,128)(2,1)S(1)} %get-tuple-element.196), channel_id=1, source_target_pairs={{0,8},{1,9},{2,10},{3,11},{4,12},{5,13},{6,14},{7,15},{8,0},{9,1},... | collective-permute-start | bytes 393224 | tf_op jit(solution)/shard_map/ppermute | solution.py:423
  67.7 9.6 %collective-permute-start.22 = (bf16[512,128]{1,0:T(8,128)(2,1)S(1)}, bf16[512,128]{1,0:T(8,128)(2,1)S(1)}, u32[]{:S(2)}, u32[]{:S(2)}) collective-permute-start(bf16[512,128]{1,0:T(8,128)(2,1)S(1)} %get-tuple-element.198), channel_id=1, source_target_pairs={{0,4},{1,5},{2,6},{3,7},{4,0},{5,1},{6,2},{7,3},{8,12},{9,13},{10,... | collective-permute-start | bytes 393224 | tf_op jit(solution)/shard_map/ppermute | solution.py:423
  71.8 9.1 %collective-permute-start.23 = (bf16[512,128]{1,0:T(8,128)(2,1)S(1)}, bf16[512,128]{1,0:T(8,128)(2,1)S(1)}, u32[]{:S(2)}, u32[]{:S(2)}) collective-permute-start(bf16[512,128]{1,0:T(8,128)(2,1)S(1)} %get-tuple-element.200), channel_id=1, source_target_pairs={{0,4},{1,3},{2,6},{3,1},{4,0},{5,7},{6,2},{7,5},{8,12},{9,11},{10,... | collective-permute-start | bytes 393224 | tf_op jit(solution)/shard_map/ppermute | solution.py:423
  72.6 8.5 %collective-permute-start.24 = (bf16[512,128]{1,0:T(8,128)(2,1)S(1)}, bf16[512,128]{1,0:T(8,128)(2,1)S(1)}, u32[]{:S(2)}, u32[]{:S(2)}) collective-permute-start(bf16[512,128]{1,0:T(8,128)(2,1)S(1)} %get-tuple-element.202), channel_id=1, source_target_pairs={{0,4},{1,5},{2,6},{3,7},{4,0},{5,1},{6,2},{7,3},{8,12},{9,13},{10,... | collective-permute-start | bytes 393224 | tf_op jit(solution)/shard_map/ppermute | solution.py:423
  77.3 6.6 %collective-permute-start.25 = (bf16[512,128]{1,0:T(8,128)(2,1)S(1)}, bf16[512,128]{1,0:T(8,128)(2,1)S(1)}, u32[]{:S(2)}, u32[]{:S(2)}) collective-permute-start(bf16[512,128]{1,0:T(8,128)(2,1)S(1)} %get-tuple-element.204), channel_id=1, source_target_pairs={{0,8},{1,9},{2,10},{3,11},{4,12},{5,13},{6,14},{7,15},{8,0},{9,1},... | collective-permute-start | bytes 393224 | tf_op jit(solution)/shard_map/ppermute | solution.py:423
  81.0 7.3 %collective-permute-start.26 = (bf16[512,128]{1,0:T(8,128)(2,1)S(1)}, bf16[512,128]{1,0:T(8,128)(2,1)S(1)}, u32[]{:S(2)}, u32[]{:S(2)}) collective-permute-start(bf16[512,128]{1,0:T(8,128)(2,1)S(1)} %get-tuple-element.206), channel_id=1, source_target_pairs={{0,8},{1,9},{2,10},{3,11},{4,12},{5,13},{6,14},{7,15},{8,0},{9,1},... | collective-permute-start | bytes 393224 | tf_op jit(solution)/shard_map/ppermute | solution.py:423
  81.1 13.0 %collective-permute-start.28 = (bf16[1024,128]{1,0:T(8,128)(2,1)S(1)}, bf16[1024,128]{1,0:T(8,128)(2,1)S(1)}, u32[]{:S(2)}, u32[]{:S(2)}) collective-permute-start(bf16[1024,128]{1,0:T(8,128)(2,1)S(1)} %get-tuple-element.210), channel_id=1, source_target_pairs={{0,2},{1,3},{2,0},{3,1},{4,6},{5,7},{6,4},{7,5},{8,10},{9,11},{10,... | collective-permute-start | bytes 786440 | tf_op jit(solution)/shard_map/ppermute | solution.py:423
  83.9 6.5 %collective-permute-start.27 = (bf16[512,128]{1,0:T(8,128)(2,1)S(1)}, bf16[512,128]{1,0:T(8,128)(2,1)S(1)}, u32[]{:S(2)}, u32[]{:S(2)}) collective-permute-start(bf16[512,128]{1,0:T(8,128)(2,1)S(1)} %get-tuple-element.208), channel_id=1, source_target_pairs={{0,4},{1,5},{2,6},{3,7},{4,0},{5,1},{6,2},{7,3},{8,12},{9,13},{10,... | collective-permute-start | bytes 393224 | tf_op jit(solution)/shard_map/ppermute | solution.py:423
  88.4 5.8 %collective-permute-start.29 = (bf16[512,128]{1,0:T(8,128)(2,1)S(1)}, bf16[512,128]{1,0:T(8,128)(2,1)S(1)}, u32[]{:S(2)}, u32[]{:S(2)}) collective-permute-start(bf16[512,128]{1,0:T(8,128)(2,1)S(1)} %get-tuple-element.211), channel_id=1, source_target_pairs={{0,4},{1,3},{2,6},{3,1},{4,0},{5,7},{6,2},{7,5},{8,12},{9,11},{10,... | collective-permute-start | bytes 393224 | tf_op jit(solution)/shard_map/ppermute | solution.py:423
  90.5 8.0 %collective-permute-start.30 = (bf16[1024,128]{1,0:T(8,128)(2,1)S(1)}, bf16[1024,128]{1,0:T(8,128)(2,1)S(1)}, u32[]{:S(2)}, u32[]{:S(2)}) collective-permute-start(bf16[1024,128]{1,0:T(8,128)(2,1)S(1)} %get-tuple-element.219), channel_id=1, source_target_pairs={{0,2},{1,3},{2,0},{3,1},{4,6},{5,7},{6,4},{7,5},{8,10},{9,11},{10,... | collective-permute-start | bytes 786440 | tf_op jit(solution)/shard_map/ppermute | solution.py:423
  94.2 7.1 %collective-permute-start.31 = (bf16[1024,128]{1,0:T(8,128)(2,1)S(1)}, bf16[1024,128]{1,0:T(8,128)(2,1)S(1)}, u32[]{:S(2)}, u32[]{:S(2)}) collective-permute-start(bf16[1024,128]{1,0:T(8,128)(2,1)S(1)} %get-tuple-element.226), channel_id=1, source_target_pairs={{0,2},{1,5},{2,0},{3,7},{4,6},{5,1},{6,4},{7,3},{8,10},{9,13},{10,... | collective-permute-start | bytes 786440 | tf_op jit(solution)/shard_map/ppermute | solution.py:423
  (6 other events, 25.7 us)

commit v19 on v16

--- a/solution.py
+++ b/solution.py
@@ -85,15 +85,17 @@
     return scale * (grad - normed * jnp.mean(grad * normed, axis=-1, keepdims=True))
 
 
-def setup_kernel(groups, features, sent, *refs):
+def setup_kernel(groups, pairs, features, sent, *refs):
     pick, spread, pick_self, held = refs[:4]
     sends = refs[4:]
     rows = features.shape[0]
     held[...] = features[...]
-    b = lax.axis_index("basin")
-    for route in range(-1, groups):
+    b, feat = lax.axis_index("basin"), lax.axis_index("feat")
+    for route in range(-1, 2 * pairs):
         if route == 0:
             chosen = lax.broadcasted_iota(jnp.int32, (1, BLOCK), 1) + (rows - BLOCK)
+        elif route >= groups:
+            chosen = jnp.full((1, BLOCK), -1, jnp.int32)
         else:
             chosen = sent[pl.ds(lax.rem(b + max(route, 0), groups), 1), :]
         across = jnp.broadcast_to(chosen, (BLOCK, BLOCK))
@@ -104,19 +106,18 @@
             if route < 0:
                 pick_self[:, r : r + BLOCK] = hot
                 continue
-            if route > 0:
-                pick[(route - 1) * BLOCK : route * BLOCK, r : r + BLOCK] = hot
+
+            @pl.when(route % 2 == feat)
+            def _():
+                pick[route // 2 * BLOCK : (route // 2 + 1) * BLOCK, r : r + BLOCK] = hot
+
             at = lax.broadcasted_iota(jnp.int32, (BLOCK, BLOCK), 0) + r
-            spread[r : r + BLOCK, route * BLOCK : (route + 1) * BLOCK] = (
-                (across == at).astype(F32).astype(BF16)
-            )
-    pick_sends(features[...], pick, sends)
-
-
-def pick_sends(rows, pick, sends):
-    sends[0][...] = rows[rows.shape[0] - BLOCK :, :]
-    for s, send in enumerate(sends[1:]):
-        send[...] = mm(pick[s * BLOCK : (s + 1) * BLOCK, :], rows).astype(BF16)
+            if route < groups:
+                spread[r : r + BLOCK, route * BLOCK : (route + 1) * BLOCK] = (
+                    (across == at).astype(F32).astype(BF16)
+                )
+    for i, send in enumerate(sends):
+        send[...] = mm(pick[i * BLOCK : (i + 1) * BLOCK, :], features[...]).astype(BF16)
 
 
 def adjacency_kernel(groups, sources, values, pick_self, _, *refs):
@@ -177,51 +178,61 @@
         msg[here, :] = (part[here, :] + own).astype(BF16)
 
 
-def remote_mixed(layer, received, columns, weights):
+def remote_mixed(layer, received, remote, feat, weights):
     wi0, wi1, wo0, wo1 = weights
     halves = [(wi0[layer], wo0[layer]), (wi1[layer], wo1[layer])]
-    far = jnp.concatenate([x[...] for x in received], axis=0)
-    return mm(columns, message_of(far, halves))
-
-
-def part_kernel(layer, *refs):
+    total = None
+    for i, block in enumerate(received):
+        route = jnp.minimum(2 * i + feat, remote.shape[1] // BLOCK - 1)
+        columns = remote[:, pl.ds(pl.multiple_of(route * BLOCK, BLOCK), BLOCK)]
+        part = mm(columns, message_of(block[...], halves))
+        total = part if total is None else total + part
+    return total
+
+
+def part_kernel(layer, pairs, *refs):
     local, msg, remote = refs[:3]
-    weights, received, mixed = refs[3:7], refs[7:-1], refs[-1]
-    total = mm(local[...], msg[...])
-    if received:
-        total = total + remote_mixed(layer, received, remote[:, BLOCK:], weights)
-    mixed[...] = total
-
-
-def upstream_rows(got, swapped_got):
-    return got[...] + swapped_got[...]
-
-
-def mixed_total(layer, state, mixed, up, remote, weights):
-    return state + mixed[...] + remote_mixed(layer, [up], remote[:, :BLOCK], weights)
-
-
-def mix_kernel(layer, *refs):
+    weights, received, mixed = refs[3:7], refs[7 : 7 + pairs], refs[-1]
+    mixed[...] = mm(local[...], msg[...]) + remote_mixed(
+        layer, received, remote, lax.axis_index("feat"), weights
+    )
+
+
+def mixed_total(layer, state, mixed, received, remote, weights):
+    return state + mixed[...] + remote_mixed(
+        layer, received, remote, 1 - lax.axis_index("feat"), weights
+    )
+
+
+def mix_kernel(layer, pairs, *refs):
     prev, mixed, remote, pick = refs[:4]
-    weights, up = refs[4:8], upstream_rows(*refs[8:10])
-    total, inputs = refs[10:12]
+    weights = refs[4:8]
+    received = refs[8 : 8 + pairs]
+    total, inputs = refs[8 + pairs : 10 + pairs]
+    sends = refs[10 + pairs :]
     state = prev[...].astype(F32) if layer == 0 else normed_of(prev[...])[1]
-    total[...] = mixed_total(layer, state, mixed, up, remote, weights)
+    total[...] = mixed_total(layer, state, mixed, received, remote, weights)
     new = normed_of(total[...])[1].astype(BF16)
     inputs[...] = new
-    pick_sends(new, pick, refs[12:])
-
-
-def start_bwd(layer, dtotal_now, weights, received, remote_t, outs):
+    for i, send in enumerate(sends):
+        send[...] = mm(pick[i * BLOCK : (i + 1) * BLOCK, :], new).astype(BF16)
+
+
+def start_bwd(layer, groups, dtotal_now, weights, mine, others, remote_t, outs):
     dtotal, dround, far_x, far_dmsg, far_act, far_dpre = outs[:6]
     backs = outs[6:]
     wi0, wi1, wo0, wo1 = weights
     halves = [(wi0[layer], wo0[layer]), (wi1[layer], wo1[layer])]
     dtotal[...] = dtotal_now
     dround[...] = dtotal_now.astype(BF16)
-    far_x[:BLOCK, :] = upstream_rows(*received[:2])
-    for i, block in enumerate(received[2:]):
-        far_x[(i + 1) * BLOCK : (i + 2) * BLOCK, :] = block[...]
+    for first in range(2):
+
+        @pl.when(lax.axis_index("feat") == first)
+        def _():
+            for route in range(groups):
+                block = (mine, others)[(route + first) % 2][route // 2]
+                far_x[route * BLOCK : (route + 1) * BLOCK, :] = block[...]
+
     dmsg = mm(remote_t[...], dround[...]).astype(BF16)
     back, (act, dpre) = message_grad(far_x[...], dmsg, halves)
     far_dmsg[...] = dmsg
@@ -231,12 +242,15 @@
         out[...] = back[i * BLOCK : (i + 1) * BLOCK, :].astype(BF16)
 
 
-def turn_kernel(layer, groups, *refs):
+def turn_kernel(layer, groups, pairs, *refs):
     prev, mixed, remote, remote_t, cot = refs[:5]
-    weights, received, outs = refs[5:9], refs[9 : 10 + groups], refs[10 + groups :]
+    weights = refs[5:9]
+    mine, others = refs[9 : 9 + pairs], refs[9 + pairs : 9 + 2 * pairs]
+    outs = refs[9 + 2 * pairs :]
     state = normed_of(prev[...])[1]
-    total = mixed_total(layer, state, mixed, upstream_rows(*received[:2]), remote, weights)
-    start_bwd(layer, norm_grad(cot[...], total), weights, received, remote_t, outs)
+    total = mixed_total(layer, state, mixed, others, remote, weights)
+    dtotal = norm_grad(cot[...], total)
+    start_bwd(layer, groups, dtotal, weights, mine, others, remote_t, outs)
 
 
 def back_kernel(layer, grad_scale, *refs):
@@ -390,13 +404,14 @@
     return dtotal[...] + back[...] + mm(spread[...], far)
 
 
-def join_kernel(layer, groups, *refs):
+def join_kernel(layer, groups, pairs, *refs):
     dtotal, back, spread, remote_t, total = refs[:5]
     weights, refs = refs[5:9], refs[9:]
     returned, refs = refs[:groups], refs[groups:]
-    received, outs = refs[: groups + 1], refs[groups + 1 :]
+    mine, others, outs = refs[:pairs], refs[pairs : 2 * pairs], refs[2 * pairs :]
     grad = gathered_grad(dtotal, back, returned, spread)
-    start_bwd(layer, norm_grad(grad, total[...]), weights, received, remote_t, outs)
+    dtotal = norm_grad(grad, total[...])
+    start_bwd(layer, groups, dtotal, weights, mine, others, remote_t, outs)
 
 
 def last_kernel(*refs):
@@ -432,13 +447,18 @@
 
 
 def forward(sends):
-    chain = lax.axis_size("chain")
-
-    def downstream(c, b, feat):
-        return (c + 1, b) if c % 2 == feat and c + 1 < chain else None
-
-    up = over_mesh(sends[0], downstream)
-    return [up] + [around(x, "basin", s + 1) for s, x in enumerate(sends[1:])]
+    def target(i, c, b, feat):
+        route = 2 * i + feat
+        if route == 0:
+            return (c + 1, b) if c + 1 < lax.axis_size("chain") else None
+        groups = lax.axis_size("basin")
+        return (c, (b + route) % groups) if route < groups else None
+
+    return [over_mesh(x, functools.partial(target, i)) for i, x in enumerate(sends)]
+
+
+def other_core(got):
+    return [around(x, "feat", 1) for x in got]
 
 
 def backward(grads):
@@ -450,6 +470,7 @@
 def shards(features, cotangent, w_in, w_out, block_index, block_values, send_rows, send_count):
     rows, latent = features.shape
     groups = lax.axis_size("basin")
+    pairs = (groups + 1) // 2
     layers, _, half = w_in.shape
     far_rows = groups * BLOCK
     own = rows // BLOCK
@@ -467,10 +488,9 @@
     sent = jnp.where(live, send_rows[0], -1)
     sources = block_index.T
     pick, spread, pick_self, features, *sends = call(
-        functools.partial(setup_kernel, groups),
-        [act16(max(groups - 1, 1) * BLOCK, rows), act16(rows, far_rows), act16(BLOCK, rows)]
-        + [act16(rows)]
-        + [act16(BLOCK)] * groups,
+        functools.partial(setup_kernel, groups, pairs),
+        [act16(pairs * BLOCK, rows), act16(rows, far_rows), act16(BLOCK, rows), act16(rows)]
+        + [act16(BLOCK)] * pairs,
         [features, sent],
         2 * rows * far_rows * latent,
         name="setup",
@@ -479,9 +499,10 @@
     inputs = [features]
     saved = []
     totals = []
-    received = []
+    mine = []
+    others = []
     for layer in range(layers):
-        up, *others = forward(sends)
+        mine.append(forward(sends))
         if layer == 0:
             part, slope1 = call(
                 half_kernel,
@@ -506,7 +527,7 @@
                 name="adjacency",
                 scalars=sources,
             )
-            up, local = lax.optimization_barrier((up, local))
+            mine[0], local = lax.optimization_barrier((mine[0], local))
         else:
             msg, slope0, slope1, act_t, x_t = call(
                 functools.partial(local_kernel, layer),
@@ -516,22 +537,22 @@
                 rows * ffn,
                 name=f"local{layer}",
             )
-            up, msg = lax.optimization_barrier((up, msg))
+            mine[layer], msg = lax.optimization_barrier((mine[layer], msg))
         saved.append([slope0, slope1, act_t, x_t])
-        received.append([up, around(up, "feat", 1), *others])
+        others.append(other_core(mine[layer]))
         (mixed,) = call(
-            functools.partial(part_kernel, layer),
+            functools.partial(part_kernel, layer, pairs),
             [((rows, latent), F32)],
-            [local, msg, remote, *weights, *others],
+            [local, msg, remote, *weights, *mine[layer]],
             2 * rows * rows * latent,
             name=f"part{layer}",
         )
         prev = totals[-1] if layer else features
         if layer < last:
             total, new, *sends = call(
-                functools.partial(mix_kernel, layer),
-                [((rows, latent), F32), act16(rows)] + [act16(BLOCK)] * groups,
-                [prev, mixed, remote, pick, *weights, *received[layer][:2]],
+                functools.partial(mix_kernel, layer, pairs),
+                [((rows, latent), F32), act16(rows)] + [act16(BLOCK)] * pairs,
+                [prev, mixed, remote, pick, *weights, *others[layer]],
                 far_rows * ffn + 2 * rows * far_rows * latent,
                 name=f"mix{layer}",
             )
@@ -543,9 +564,9 @@
         + [act16(BLOCK)] * groups
     )
     outs = call(
-        functools.partial(turn_kernel, last, groups),
+        functools.partial(turn_kernel, last, groups, pairs),
         bwd_outs,
-        [totals[-1], mixed, remote, remote_t, cotangent, *weights, *received[last]],
+        [totals[-1], mixed, remote, remote_t, cotangent, *weights, *mine[last], *others[last]],
         2 * far_rows * ffn,
         name="turn",
     )
@@ -582,10 +603,10 @@
     def join(layer, state, after):
         if layer:
             return call(
-                functools.partial(join_kernel, layer - 1, groups),
+                functools.partial(join_kernel, layer - 1, groups, pairs),
                 bwd_outs,
                 [*state, spread, remote_t, totals[layer - 1]]
-                + [*weights, *returned[layer], *received[layer - 1]],
+                + [*weights, *returned[layer], *mine[layer - 1], *others[layer - 1]],
                 2 * far_rows * ffn,
                 name=f"join{layer}",
                 after=after,

time: 96.8 us -> 95.9 us (level)
  starting transfers between devices: 41.3 us -> 35.8 us
  waiting for transfers between devices: 21.4 us -> 25.4 us
    ppermute x18, waiting for transfers between devices: 12.2 us -> 18.2 us  [over_mesh(): return lax.ppermute(x, ('chain', 'basin', 'feat'), perm)]
    ppermute x11 -> x8, starting transfers between devices: 7.32 us -> 3.59 us  [around(): return lax.ppermute(x, axis, [(i, (i + distance) % n) for i in range(n)])]
    ppermute x11 -> x8, waiting for transfers between devices: 3.53 us -> 1.16 us  [around(): return lax.ppermute(x, axis, [(i, (i + distance) % n) for i in range(n)])]
    ppermute x18, starting transfers between devices: 29.9 us -> 28.4 us  [over_mesh(): return lax.ppermute(x, ('chain', 'basin', 'feat'), perm)]
  transfers between devices with their start and end apart: 32 -> 29, of which waited for: 13 -> 20; matrix products, arithmetic and copies ran while one was open for 1% -> 1% of each run, Pallas kernels for 26% -> 27%
where the time goes in v19:
time: 95.9 us; the launch traced here: 95.6 us
  starting transfers between devices  35.8 us (37%)
  Pallas kernels  31.3 us (33%)
  waiting for transfers between devices  25.4 us (26%)
  local copies, waits for them, and re-layouts  1.2 us (1%)
  between operations  1.18 us (1%)
    ppermute x18, starting transfers between devices, over_mesh(): return lax.ppermute(x, ('chain', 'basin', 'feat'), perm)  28.4 us
    pallas_call x33, Pallas kernels, call(): pl.pallas_call(lambda *refs: body(*refs[skipped:]), out_shape=[jax.ShapeD...  26.9 us
    ppermute x18, waiting for transfers between devices, over_mesh(): return lax.ppermute(x, ('chain', 'basin', 'feat'), perm)  18.2 us
    ppermute x3, waiting for transfers between devices, backward(): up = lax.ppermute(grads[0], 'chain', [(c, c - 1) for c in range(1, chain)])  6.01 us
    pallas_call x4, Pallas kernels, write(): pl.pallas_call(functools.partial(write_kernel, layer, sums[layer].stages[...  4.43 us
    ppermute x3, starting transfers between devices, backward(): up = lax.ppermute(grads[0], 'chain', [(c, c - 1) for c in range(1, chain)])  3.86 us
    ppermute x8, starting transfers between devices, around(): return lax.ppermute(x, axis, [(i, (i + distance) % n) for i in range(n)])  3.59 us
  transfers between devices with their start and end apart: 29, of which 20 were waited for; matrix products, arithmetic and copies ran while one was open for 1% of the time, Pallas kernels for 27%

profile of v19, /device:TPU:0, one launch (start us, length us, event | category | flops | bytes accessed | tf_op | source)
XLA Modules:
  0.0 95.6 jit_solution(10284521253074681578)
XLA Ops:
  3.6 4.9 %collective-permute-start = (bf16[128,256]{1,0:T(8,128)(2,1)S(1)}, bf16[128,256]{1,0:T(8,128)(2,1)S(1)}, u32[]{:S(2)}, u32[]{:S(2)}) collective-permute-start(bf16[128,256]{1,0:T(8,128)(2,1)S(1)} %get-tuple-element.114), channel_id=1, source_target_pairs={{0,4},{1,3},{2,6},{3,1},{4,8},{5,7},{6,10},{7,5},{8,12},{9,11},{10... | collective-permute-start | bytes 196616 | tf_op jit(solution)/shard_map/ppermute | solution.py:438
  10.5 1.6 %adjacency.1 = (bf16[768,768]{1,0:T(8,128)(2,1)S(1)}, bf16[768,768]{1,0:T(8,128)(2,1)S(1)}, bf16[768,256]{1,0:T(8,128)(2,1)S(1)}, bf16[256,768]{1,0:T(8,128)(2,1)S(1)}) custom-call(s32[4,6]{1,0:T(4,128)S(1)} %bitcast.4, bf16[6,4,128,128]{3,2,1,0:T(8,128)(2,1)S(1)} %copy-done.3, bf16[128,768]{1,0:T(8,128)(2,1)S(1)} %get-tuple-element.115.refs_2_, ...), custom_call_target="tpu_custom_call" | custom-call | flops 150994944 | bytes 4000000 | tf_op jit(solution)/shard_map/adjacency/pallas_call | solution.py:32
  14.5 3.5 %collective-permute-start.4 = (bf16[128,256]{1,0:T(8,128)(2,1)S(1)}, bf16[128,256]{1,0:T(8,128)(2,1)S(1)}, u32[]{:S(2)}, u32[]{:S(2)}) collective-permute-start(bf16[128,256]{1,0:T(8,128)(2,1)S(1)} %get-tuple-element.124), channel_id=1, source_target_pairs={{0,4},{1,3},{2,6},{3,1},{4,8},{5,7},{6,10},{7,5},{8,12},{9,11},{10... | collective-permute-start | bytes 196616 | tf_op jit(solution)/shard_map/ppermute | solution.py:438
  18.0 1.6 %local1.1 = (bf16[768,256]{1,0:T(8,128)(2,1)S(1)}, bf16[768,512]{1,0:T(8,128)(2,1)S(1)}, bf16[768,512]{1,0:T(8,128)(2,1)S(1)}, bf16[512,768]{1,0:T(8,128)(2,1)S(1)}, bf16[256,768]{1,0:T(8,128)(2,1)S(1)}) custom-call(bf16[768,256]{1,0:T(8,128)(2,1)S(1)} %get-tuple-element.125.refs_0_, bf16[3,256,512]{2,1,0:T(8,128)(2,1)S(1)} %copy-done, ...), custom_call_target="tpu_custom_call" | custom-call | flops 805306368 | bytes 4000000 | tf_op jit(solution)/shard_map/local1/pallas_call | solution.py:32
  22.2 4.3 %collective-permute-start.6 = (bf16[128,256]{1,0:T(8,128)(2,1)S(1)}, bf16[128,256]{1,0:T(8,128)(2,1)S(1)}, u32[]{:S(2)}, u32[]{:S(2)}) collective-permute-start(bf16[128,256]{1,0:T(8,128)(2,1)S(1)} %get-tuple-element.130), channel_id=1, source_target_pairs={{0,4},{1,3},{2,6},{3,1},{4,8},{5,7},{6,10},{7,5},{8,12},{9,11},{10... | collective-permute-start | bytes 196616 | tf_op jit(solution)/shard_map/ppermute | solution.py:438
  26.5 1.6 %local2.1 = (bf16[768,256]{1,0:T(8,128)(2,1)S(1)}, bf16[768,512]{1,0:T(8,128)(2,1)S(1)}, bf16[768,512]{1,0:T(8,128)(2,1)S(1)}, bf16[512,768]{1,0:T(8,128)(2,1)S(1)}, bf16[256,768]{1,0:T(8,128)(2,1)S(1)}) custom-call(bf16[768,256]{1,0:T(8,128)(2,1)S(1)} %get-tuple-element.131.refs_0_, bf16[3,256,512]{2,1,0:T(8,128)(2,1)S(1)} %copy-done, ...), custom_call_target="tpu_custom_call" | custom-call | flops 805306368 | bytes 4000000 | tf_op jit(solution)/shard_map/local2/pallas_call | solution.py:32
  29.6 2.2 %turn.1 = (f32[768,256]{1,0:T(8,128)S(1)}, bf16[768,256]{1,0:T(8,128)(2,1)S(1)}, bf16[256,256]{1,0:T(8,128)(2,1)S(1)}, bf16[256,256]{1,0:T(8,128)(2,1)S(1)}, bf1...) custom-call(f32[768,256]{1,0:T(8,128)S(1)} %get-tuple-element.129.re, ...), custom_call_target="tpu_custom_call" | custom-call | flops 536870912 | bytes 4000000 | tf_op jit(solution)/shard_map/turn/pallas_call | solution.py:32
  31.9 1.3 %collective-permute-start.8 = (bf16[128,256]{1,0:T(8,128)(2,1)S(1)}, bf16[128,256]{1,0:T(8,128)(2,1)S(1)}, u32[]{:S(2)}, u32[]{:S(2)}) collective-permute-start(bf16[128,256]{1,0:T(8,128)(2,1)S(1)} %get-tuple-element.147), channel_id=1, source_target_pairs={{4,0},{8,4},{12,8},{5,1},{9,5},{13,9},{6,2},{10,6},{14,10},{7,3},{... | collective-permute-start | bytes 196616 | tf_op jit(solution)/shard_map/ppermute | solution.py:466
  33.2 1.6 %collective-permute-start.9 = (bf16[128,256]{1,0:T(8,128)(2,1)S(1)}, bf16[128,256]{1,0:T(8,128)(2,1)S(1)}, u32[]{:S(2)}, u32[]{:S(2)}) collective-permute-start(bf16[128,256]{1,0:T(8,128)(2,1)S(1)} %get-tuple-element.148), channel_id=1, source_target_pairs={{0,2},{2,0},{1,3},{3,1},{4,6},{6,4},{5,7},{7,5},{8,10},{10,8},{9,1... | collective-permute-start | bytes 196616 | tf_op jit(solution)/shard_map/ppermute | solution.py:425
  34.8 2.4 %back2.1 = (f32[768,256]{1,0:T(8,128)S(1)}, f32[2048,128]{1,0:T(8,128)S(1)}) custom-call(bf16[768,256]{1,0:T(8,128)(2,1)S(1)} %get-tuple-element.136.refs_0_, bf16[768,768]{1,0:T(8,128)(2,1)S(1)} %get-tuple-element.137.refs_1_.refs_2_, bf16[768,512]{1,0:T(8,128)(2,1)S(1)} %get-tuple-element.138.refs_2_, bf16[768,512]{1,0:T(8,128)(2,1)S(1)} %get-tuple-element.139.refs_3_, ...), custom_call_target="tpu_custom_call" | custom-call | flops 2717908992 | bytes 4000000 | tf_op jit(solution)/shard_map/back2/pallas_call | solution.py:32
  37.2 1.5 %collective-permute-done.8.refs_1_.refs_10_ = bf16[128,256]{1,0:T(8,128)(2,1)S(1)} collective-permute-done((bf16[128,256]{1,0:T(8,128)(2,1)S(1)}, bf16[128,256]{1,0:T(8,128)(2,1)S(1)}, u32[]{:S(2)}, u32[]{:S(2)}) %collective-permute-start.8) | collective-permute-done | bytes 65568 | tf_op jit(solution)/shard_map/ppermute | solution.py:466
  38.8 1.6 %collective-permute-start.12 = (bf16[1024,128]{1,0:T(8,128)(2,1)S(1)}, bf16[1024,128]{1,0:T(8,128)(2,1)S(1)}, u32[]{:S(2)}, u32[]{:S(2)}) collective-permute-start(bf16[1024,128]{1,0:T(8,128)(2,1)S(1)} %get-tuple-element.167), channel_id=1, source_target_pairs={{0,2},{1,3},{2,0},{3,1},{4,6},{5,7},{6,4},{7,5},{8,10},{9,11},{10,... | collective-permute-start | bytes 786440 | tf_op jit(solution)/shard_map/ppermute | solution.py:438
  40.3 1.6 %join2.1 = (f32[768,256]{1,0:T(8,128)S(1)}, bf16[768,256]{1,0:T(8,128)(2,1)S(1)}, bf16[256,256]{1,0:T(8,128)(2,1)S(1)}, bf16[256,256]{1,0:T(8,128)(2,1)S(1)}, bf...) custom-call(f32[1024,128]{1,0:T(8,128)S(1)} %get-tuple-element.150.r, ...), custom_call_target="tpu_custom_call" | custom-call | flops 536870912 | bytes 4000000 | tf_op jit(solution)/shard_map/join2/pallas_call | solution.py:32
  41.9 1.3 %collective-permute-start.10 = (bf16[128,256]{1,0:T(8,128)(2,1)S(1)}, bf16[128,256]{1,0:T(8,128)(2,1)S(1)}, u32[]{:S(2)}, u32[]{:S(2)}) collective-permute-start(bf16[128,256]{1,0:T(8,128)(2,1)S(1)} %get-tuple-element.163), channel_id=1, source_target_pairs={{4,0},{8,4},{12,8},{5,1},{9,5},{13,9},{6,2},{10,6},{14,10},{7,3},{... | collective-permute-start | bytes 196616 | tf_op jit(solution)/shard_map/ppermute | solution.py:466
  43.8 2.4 %back1.1 = (f32[768,256]{1,0:T(8,128)S(1)}, f32[2048,128]{1,0:T(8,128)S(1)}) custom-call(bf16[768,256]{1,0:T(8,128)(2,1)S(1)} %get-tuple-element.153.refs_0_.refs_1_, bf16[768,256]{1,0:T(8,128)(2,1)S(1)} %get-tuple-element.153.refs_0_.refs_1_, bf16[768,768]{1,0:T(8,128)(2,1)S(1)} %get-tuple-element.137.refs_1_.refs_2_, ...), custom_call_target="tpu_custom_call" | custom-call | flops 2717908992 | bytes 4000000 | tf_op jit(solution)/shard_map/back1/pallas_call | solution.py:32
  46.2 1.9 %collective-permute-done.10.refs_1_.refs_10_ = bf16[128,256]{1,0:T(8,128)(2,1)S(1)} collective-permute-done((bf16[128,256]{1,0:T(8,128)(2,1)S(1)}, bf16[128,256]{1,0:T(8,128)(2,1)S(1)}, u32[]{:S(2)}, u32[]{:S(2)}) %collective-permute-start.10) | collective-permute-done | bytes 65568 | tf_op jit(solution)/shard_map/ppermute | solution.py:466
  48.3 1.6 %collective-permute-start.14 = (bf16[1024,128]{1,0:T(8,128)(2,1)S(1)}, bf16[1024,128]{1,0:T(8,128)(2,1)S(1)}, u32[]{:S(2)}, u32[]{:S(2)}) collective-permute-start(bf16[1024,128]{1,0:T(8,128)(2,1)S(1)} %get-tuple-element.184), channel_id=1, source_target_pairs={{0,2},{1,3},{2,0},{3,1},{4,6},{5,7},{6,4},{7,5},{8,10},{9,11},{10,... | collective-permute-start | bytes 786440 | tf_op jit(solution)/shard_map/ppermute | solution.py:438
  50.0 1.6 %collective-permute-start.13 = (bf16[512,128]{1,0:T(8,128)(2,1)S(1)}, bf16[512,128]{1,0:T(8,128)(2,1)S(1)}, u32[]{:S(2)}, u32[]{:S(2)}) collective-permute-start(bf16[512,128]{1,0:T(8,128)(2,1)S(1)} %get-tuple-element.180), channel_id=1, source_target_pairs={{0,4},{1,5},{2,6},{3,7},{4,0},{5,1},{6,2},{7,3},{8,12},{9,13},{10,... | collective-permute-start | bytes 393224 | tf_op jit(solution)/shard_map/ppermute | solution.py:438
  51.5 1.6 %join1.1 = (f32[768,256]{1,0:T(8,128)S(1)}, bf16[768,256]{1,0:T(8,128)(2,1)S(1)}, bf16[256,256]{1,0:T(8,128)(2,1)S(1)}, bf16[256,256]{1,0:T(8,128)(2,1)S(1)}, bf...) custom-call(f32[512,128]{1,0:T(8,128)S(1)} %get-tuple-element.168.re, ...), custom_call_target="tpu_custom_call" | custom-call | flops 536870912 | bytes 4000000 | tf_op jit(solution)/shard_map/join1/pallas_call | solution.py:32
  53.1 2.4 %back0.1 = (f32[768,256]{1,0:T(8,128)S(1)}, f32[2048,128]{1,0:T(8,128)S(1)}) custom-call(bf16[768,256]{1,0:T(8,128)(2,1)S(1)} %get-tuple-element.170.refs_0_.refs_1_, bf16[768,256]{1,0:T(8,128)(2,1)S(1)} %get-tuple-element.170.refs_0_.refs_1_, bf16[768,768]{1,0:T(8,128)(2,1)S(1)} %get-tuple-element.137.refs_1_.refs_2_, ...), custom_call_target="tpu_custom_call" | custom-call | flops 2717908992 | bytes 4000000 | tf_op jit(solution)/shard_map/back0/pallas_call | solution.py:32
  56.7 3.3 %collective-permute-start.16 = (bf16[512,128]{1,0:T(8,128)(2,1)S(1)}, bf16[512,128]{1,0:T(8,128)(2,1)S(1)}, u32[]{:S(2)}, u32[]{:S(2)}) collective-permute-start(bf16[512,128]{1,0:T(8,128)(2,1)S(1)} %get-tuple-element.188), channel_id=1, source_target_pairs={{0,8},{1,9},{2,10},{3,11},{4,12},{5,13},{6,14},{7,15},{8,0},{9,1},... | collective-permute-start | bytes 393224 | tf_op jit(solution)/shard_map/ppermute | solution.py:438
  63.2 2.5 %collective-permute-done.16.refs_2_ = bf16[512,128]{1,0:T(8,128)(2,1)S(1)} collective-permute-done((bf16[512,128]{1,0:T(8,128)(2,1)S(1)}, bf16[512,128]{1,0:T(8,128)(2,1)S(1)}, u32[]{:S(2)}, u32[]{:S(2)}) %collective-permute-start.16) | collective-permute-done | bytes 131104 | tf_op jit(solution)/shard_map/ppermute | solution.py:438
  65.9 1.2 %collective-permute-done.17.refs_2_ = bf16[512,128]{1,0:T(8,128)(2,1)S(1)} collective-permute-done((bf16[512,128]{1,0:T(8,128)(2,1)S(1)}, bf16[512,128]{1,0:T(8,128)(2,1)S(1)}, u32[]{:S(2)}, u32[]{:S(2)}) %collective-permute-start.17) | collective-permute-done | bytes 131104 | tf_op jit(solution)/shard_map/ppermute | solution.py:438
  67.1 1.4 %collective-permute-start.20 = (bf16[512,128]{1,0:T(8,128)(2,1)S(1)}, bf16[512,128]{1,0:T(8,128)(2,1)S(1)}, u32[]{:S(2)}, u32[]{:S(2)}) collective-permute-start(bf16[512,128]{1,0:T(8,128)(2,1)S(1)} %get-tuple-element.196), channel_id=1, source_target_pairs={{0,8},{1,9},{2,10},{3,11},{4,12},{5,13},{6,14},{7,15},{8,0},{9,1},... | collective-permute-start | bytes 393224 | tf_op jit(solution)/shard_map/ppermute | solution.py:438
  68.6 2.2 %collective-permute-done.18.refs_2_ = bf16[512,128]{1,0:T(8,128)(2,1)S(1)} collective-permute-done((bf16[512,128]{1,0:T(8,128)(2,1)S(1)}, bf16[512,128]{1,0:T(8,128)(2,1)S(1)}, u32[]{:S(2)}, u32[]{:S(2)}) %collective-permute-start.18) | collective-permute-done | bytes 131104 | tf_op jit(solution)/shard_map/ppermute | solution.py:438
  71.5 2.2 %collective-permute-done.19.refs_2_ = bf16[512,128]{1,0:T(8,128)(2,1)S(1)} collective-permute-done((bf16[512,128]{1,0:T(8,128)(2,1)S(1)}, bf16[512,128]{1,0:T(8,128)(2,1)S(1)}, u32[]{:S(2)}, u32[]{:S(2)}) %collective-permute-start.19) | collective-permute-done | bytes 131104 | tf_op jit(solution)/shard_map/ppermute | solution.py:438
  73.9 4.4 %collective-permute-done.20.refs_2_ = bf16[512,128]{1,0:T(8,128)(2,1)S(1)} collective-permute-done((bf16[512,128]{1,0:T(8,128)(2,1)S(1)}, bf16[512,128]{1,0:T(8,128)(2,1)S(1)}, u32[]{:S(2)}, u32[]{:S(2)}) %collective-permute-start.20) | collective-permute-done | bytes 131104 | tf_op jit(solution)/shard_map/ppermute | solution.py:438
  78.4 1.3 %collective-permute-done.21.refs_2_ = bf16[512,128]{1,0:T(8,128)(2,1)S(1)} collective-permute-done((bf16[512,128]{1,0:T(8,128)(2,1)S(1)}, bf16[512,128]{1,0:T(8,128)(2,1)S(1)}, u32[]{:S(2)}, u32[]{:S(2)}) %collective-permute-start.21) | collective-permute-done | bytes 131104 | tf_op jit(solution)/shard_map/ppermute | solution.py:438
  80.5 1.3 %collective-permute-start.23 = (bf16[128,256]{1,0:T(8,128)(2,1)S(1)}, bf16[128,256]{1,0:T(8,128)(2,1)S(1)}, u32[]{:S(2)}, u32[]{:S(2)}) collective-permute-start(bf16[128,256]{1,0:T(8,128)(2,1)S(1)} %get-tuple-element.202), channel_id=1, source_target_pairs={{4,0},{8,4},{12,8},{5,1},{9,5},{13,9},{6,2},{10,6},{14,10},{7,3},{... | collective-permute-start | bytes 196616 | tf_op jit(solution)/shard_map/ppermute | solution.py:466
  84.0 2.6 %collective-permute-done.23.refs_1_.refs_4_ = bf16[128,256]{1,0:T(8,128)(2,1)S(1)} collective-permute-done((bf16[128,256]{1,0:T(8,128)(2,1)S(1)}, bf16[128,256]{1,0:T(8,128)(2,1)S(1)}, u32[]{:S(2)}, u32[]{:S(2)}) %collective-permute-start.23) | collective-permute-done | bytes 65568 | tf_op jit(solution)/shard_map/ppermute | solution.py:466
  89.9 1.3 %collective-permute-done.27.refs_4_ = bf16[1024,128]{1,0:T(8,128)(2,1)S(1)} collective-permute-done((bf16[1024,128]{1,0:T(8,128)(2,1)S(1)}, bf16[1024,128]{1,0:T(8,128)(2,1)S(1)}, u32[]{:S(2)}, u32[]{:S(2)}) %collective-permute-start.27) | collective-permute-done | bytes 262176 | tf_op jit(solution)/shard_map/ppermute | solution.py:438
  94.0 1.4 %write0.3 = (f32[3,256,512]{2,1,0:T(8,128)}, f32[3,512,256]{2,1,0:T(8,128)}, f32[8,128]{1,0:T(8,128)}) custom-call(f32[3,256,512]{2,1,0:T(8,128)} %get-tuple-element.217.refs_0_, f32[3,512,256]{2,1,0:T(8,128)} %get-tuple-element.218.refs_1_, f32[8,128]{1,0:T(8,128)S(1)} %get-tuple-element.219.refs_2_, ...), custom_call_target="tpu_custom_call", output_to_operand_aliasing={{0}: (0, {}), {1}: (1, {})} | custom-call | flops 1 | bytes 1 | tf_op jit(solution)/shard_map/write0/pallas_call | solution.py:627
  (76 shorter events, 26.9 us)
Async XLA Ops:
  0.6 8.8 %copy-start = (bf16[3,256,512]{2,1,0:T(8,128)(2,1)S(1)}, bf16[3,256,512]{2,1,0:T(8,128)(2,1)}, u32[]{:S(2)}) copy-start(bf16[3,256,512]{2,1,0:T(8,128)(2,1)} %refs_7_.5) | copy-start | bytes 2359300
  0.6 8.8 %copy-start.1 = (bf16[3,512,256]{2,1,0:T(8,128)(2,1)S(1)}, bf16[3,512,256]{2,1,0:T(8,128)(2,1)}, u32[]{:S(2)}) copy-start(bf16[3,512,256]{2,1,0:T(8,128)(2,1)} %refs_9_.3) | copy-start | bytes 2359300
  0.7 7.9 %collective-permute-start.1 = (bf16[3,256,512]{2,1,0:T(8,128)(2,1)}, bf16[3,256,512]{2,1,0:T(8,128)(2,1)S(1)}, u32[]{:S(2)}, u32[]{:S(2)}) collective-permute-start(bf16[3,256,512]{2,1,0:T(8,128)(2,1)} %refs_7_.5), channel_id=1, source_target_pairs={{0,1},{1,0},{2,3},{3,2},{4,5},{5,4},{6,7},{7,6},{8,9},{9,8},{10,11... | collective-permute-start | bytes 2359304 | tf_op jit(solution)/shard_map/ppermute | solution.py:425
  1.2 7.4 %collective-permute-start.2 = (bf16[3,512,256]{2,1,0:T(8,128)(2,1)}, bf16[3,512,256]{2,1,0:T(8,128)(2,1)S(1)}, u32[]{:S(2)}, u32[]{:S(2)}) collective-permute-start(bf16[3,512,256]{2,1,0:T(8,128)(2,1)} %refs_9_.3), channel_id=1, source_target_pairs={{0,1},{1,0},{2,3},{3,2},{4,5},{5,4},{6,7},{7,6},{8,9},{9,8},{10,11... | collective-permute-start | bytes 2359304 | tf_op jit(solution)/shard_map/ppermute | solution.py:425
  3.6 8.5 %collective-permute-start = (bf16[128,256]{1,0:T(8,128)(2,1)S(1)}, bf16[128,256]{1,0:T(8,128)(2,1)S(1)}, u32[]{:S(2)}, u32[]{:S(2)}) collective-permute-start(bf16[128,256]{1,0:T(8,128)(2,1)S(1)} %get-tuple-element.114), channel_id=1, source_target_pairs={{0,4},{1,3},{2,6},{3,1},{4,8},{5,7},{6,10},{7,5},{8,12},{9,11},{10... | collective-permute-start | bytes 196616 | tf_op jit(solution)/shard_map/ppermute | solution.py:438
  12.1 1.3 %collective-permute-start.3 = (bf16[128,256]{1,0:T(8,128)(2,1)S(1)}, bf16[128,256]{1,0:T(8,128)(2,1)S(1)}, u32[]{:S(2)}, u32[]{:S(2)}) collective-permute-start(bf16[128,256]{1,0:T(8,128)(2,1)S(1)} %collective-permute-done.refs_7_.refs_12_), channel_id=1, source_target_pairs={{0,1},{1,0},{2,3},{3,2},{4,5},{5,4},{6,7},{7,6},{8,9},{9,8},{10,11... | collective-permute-start | bytes 196616 | tf_op jit(solution)/shard_map/ppermute | solution.py:425
  14.5 5.4 %collective-permute-start.4 = (bf16[128,256]{1,0:T(8,128)(2,1)S(1)}, bf16[128,256]{1,0:T(8,128)(2,1)S(1)}, u32[]{:S(2)}, u32[]{:S(2)}) collective-permute-start(bf16[128,256]{1,0:T(8,128)(2,1)S(1)} %get-tuple-element.124), channel_id=1, source_target_pairs={{0,4},{1,3},{2,6},{3,1},{4,8},{5,7},{6,10},{7,5},{8,12},{9,11},{10... | collective-permute-start | bytes 196616 | tf_op jit(solution)/shard_map/ppermute | solution.py:438
  19.9 1.3 %collective-permute-start.5 = (bf16[128,256]{1,0:T(8,128)(2,1)S(1)}, bf16[128,256]{1,0:T(8,128)(2,1)S(1)}, u32[]{:S(2)}, u32[]{:S(2)}) collective-permute-start(bf16[128,256]{1,0:T(8,128)(2,1)S(1)} %collective-permute-done.4.refs_7_.refs_12_), channel_id=1, source_target_pairs={{0,1},{1,0},{2,3},{3,2},{4,5},{5,4},{6,7},{7,6},{8,9},{9,8},{10,11... | collective-permute-start | bytes 196616 | tf_op jit(solution)/shard_map/ppermute | solution.py:425
  22.2 6.2 %collective-permute-start.6 = (bf16[128,256]{1,0:T(8,128)(2,1)S(1)}, bf16[128,256]{1,0:T(8,128)(2,1)S(1)}, u32[]{:S(2)}, u32[]{:S(2)}) collective-permute-start(bf16[128,256]{1,0:T(8,128)(2,1)S(1)} %get-tuple-element.130), channel_id=1, source_target_pairs={{0,4},{1,3},{2,6},{3,1},{4,8},{5,7},{6,10},{7,5},{8,12},{9,11},{10... | collective-permute-start | bytes 196616 | tf_op jit(solution)/shard_map/ppermute | solution.py:438
  28.4 1.3 %copy-start.2 = (f32[768,256]{1,0:T(8,128)S(1)}, f32[768,256]{1,0:T(8,128)}, u32[]{:S(2)}) copy-start(f32[768,256]{1,0:T(8,128)} %refs_4_.5) | copy-start | bytes 2359300
  28.4 1.3 %collective-permute-start.7 = (bf16[128,256]{1,0:T(8,128)(2,1)S(1)}, bf16[128,256]{1,0:T(8,128)(2,1)S(1)}, u32[]{:S(2)}, u32[]{:S(2)}) collective-permute-start(bf16[128,256]{1,0:T(8,128)(2,1)S(1)} %collective-permute-done.6.refs_7_.refs_9_), channel_id=1, source_target_pairs={{0,1},{1,0},{2,3},{3,2},{4,5},{5,4},{6,7},{7,6},{8,9},{9,8},{10,11... | collective-permute-start | bytes 196616 | tf_op jit(solution)/shard_map/ppermute | solution.py:425
  31.9 6.8 %collective-permute-start.8 = (bf16[128,256]{1,0:T(8,128)(2,1)S(1)}, bf16[128,256]{1,0:T(8,128)(2,1)S(1)}, u32[]{:S(2)}, u32[]{:S(2)}) collective-permute-start(bf16[128,256]{1,0:T(8,128)(2,1)S(1)} %get-tuple-element.147), channel_id=1, source_target_pairs={{4,0},{8,4},{12,8},{5,1},{9,5},{13,9},{6,2},{10,6},{14,10},{7,3},{... | collective-permute-start | bytes 196616 | tf_op jit(solution)/shard_map/ppermute | solution.py:466
  33.2 5.5 %collective-permute-start.9 = (bf16[128,256]{1,0:T(8,128)(2,1)S(1)}, bf16[128,256]{1,0:T(8,128)(2,1)S(1)}, u32[]{:S(2)}, u32[]{:S(2)}) collective-permute-start(bf16[128,256]{1,0:T(8,128)(2,1)S(1)} %get-tuple-element.148), channel_id=1, source_target_pairs={{0,2},{2,0},{1,3},{3,1},{4,6},{6,4},{5,7},{7,5},{8,10},{10,8},{9,1... | collective-permute-start | bytes 196616 | tf_op jit(solution)/shard_map/ppermute | solution.py:425
  38.8 11.1 %collective-permute-start.12 = (bf16[1024,128]{1,0:T(8,128)(2,1)S(1)}, bf16[1024,128]{1,0:T(8,128)(2,1)S(1)}, u32[]{:S(2)}, u32[]{:S(2)}) collective-permute-start(bf16[1024,128]{1,0:T(8,128)(2,1)S(1)} %get-tuple-element.167), channel_id=1, source_target_pairs={{0,2},{1,3},{2,0},{3,1},{4,6},{5,7},{6,4},{7,5},{8,10},{9,11},{10,... | collective-permute-start | bytes 786440 | tf_op jit(solution)/shard_map/ppermute | solution.py:438
  41.9 6.2 %collective-permute-start.10 = (bf16[128,256]{1,0:T(8,128)(2,1)S(1)}, bf16[128,256]{1,0:T(8,128)(2,1)S(1)}, u32[]{:S(2)}, u32[]{:S(2)}) collective-permute-start(bf16[128,256]{1,0:T(8,128)(2,1)S(1)} %get-tuple-element.163), channel_id=1, source_target_pairs={{4,0},{8,4},{12,8},{5,1},{9,5},{13,9},{6,2},{10,6},{14,10},{7,3},{... | collective-permute-start | bytes 196616 | tf_op jit(solution)/shard_map/ppermute | solution.py:466
  43.2 5.0 %collective-permute-start.11 = (bf16[128,256]{1,0:T(8,128)(2,1)S(1)}, bf16[128,256]{1,0:T(8,128)(2,1)S(1)}, u32[]{:S(2)}, u32[]{:S(2)}) collective-permute-start(bf16[128,256]{1,0:T(8,128)(2,1)S(1)} %get-tuple-element.164), channel_id=1, source_target_pairs={{0,2},{2,0},{1,3},{3,1},{4,6},{6,4},{5,7},{7,5},{8,10},{10,8},{9,1... | collective-permute-start | bytes 196616 | tf_op jit(solution)/shard_map/ppermute | solution.py:425
  48.3 11.7 %collective-permute-start.14 = (bf16[1024,128]{1,0:T(8,128)(2,1)S(1)}, bf16[1024,128]{1,0:T(8,128)(2,1)S(1)}, u32[]{:S(2)}, u32[]{:S(2)}) collective-permute-start(bf16[1024,128]{1,0:T(8,128)(2,1)S(1)} %get-tuple-element.184), channel_id=1, source_target_pairs={{0,2},{1,3},{2,0},{3,1},{4,6},{5,7},{6,4},{7,5},{8,10},{9,11},{10,... | collective-permute-start | bytes 786440 | tf_op jit(solution)/shard_map/ppermute | solution.py:438
  50.0 5.6 %collective-permute-start.13 = (bf16[512,128]{1,0:T(8,128)(2,1)S(1)}, bf16[512,128]{1,0:T(8,128)(2,1)S(1)}, u32[]{:S(2)}, u32[]{:S(2)}) collective-permute-start(bf16[512,128]{1,0:T(8,128)(2,1)S(1)} %get-tuple-element.180), channel_id=1, source_target_pairs={{0,4},{1,5},{2,6},{3,7},{4,0},{5,1},{6,2},{7,3},{8,12},{9,13},{10,... | collective-permute-start | bytes 393224 | tf_op jit(solution)/shard_map/ppermute | solution.py:438
  55.6 6.4 %collective-permute-start.15 = (bf16[1024,128]{1,0:T(8,128)(2,1)S(1)}, bf16[1024,128]{1,0:T(8,128)(2,1)S(1)}, u32[]{:S(2)}, u32[]{:S(2)}) collective-permute-start(bf16[1024,128]{1,0:T(8,128)(2,1)S(1)} %get-tuple-element.186), channel_id=1, source_target_pairs={{0,2},{1,5},{2,0},{3,7},{4,6},{5,1},{6,4},{7,3},{8,10},{9,13},{10,... | collective-permute-start | bytes 786440 | tf_op jit(solution)/shard_map/ppermute | solution.py:438
  56.7 9.1 %collective-permute-start.16 = (bf16[512,128]{1,0:T(8,128)(2,1)S(1)}, bf16[512,128]{1,0:T(8,128)(2,1)S(1)}, u32[]{:S(2)}, u32[]{:S(2)}) collective-permute-start(bf16[512,128]{1,0:T(8,128)(2,1)S(1)} %get-tuple-element.188), channel_id=1, source_target_pairs={{0,8},{1,9},{2,10},{3,11},{4,12},{5,13},{6,14},{7,15},{8,0},{9,1},... | collective-permute-start | bytes 393224 | tf_op jit(solution)/shard_map/ppermute | solution.py:438
  60.1 7.0 %collective-permute-start.17 = (bf16[512,128]{1,0:T(8,128)(2,1)S(1)}, bf16[512,128]{1,0:T(8,128)(2,1)S(1)}, u32[]{:S(2)}, u32[]{:S(2)}) collective-permute-start(bf16[512,128]{1,0:T(8,128)(2,1)S(1)} %get-tuple-element.190), channel_id=1, source_target_pairs={{0,4},{1,5},{2,6},{3,7},{4,0},{5,1},{6,2},{7,3},{8,12},{9,13},{10,... | collective-permute-start | bytes 393224 | tf_op jit(solution)/shard_map/ppermute | solution.py:438
  62.1 8.6 %collective-permute-start.18 = (bf16[512,128]{1,0:T(8,128)(2,1)S(1)}, bf16[512,128]{1,0:T(8,128)(2,1)S(1)}, u32[]{:S(2)}, u32[]{:S(2)}) collective-permute-start(bf16[512,128]{1,0:T(8,128)(2,1)S(1)} %get-tuple-element.192), channel_id=1, source_target_pairs={{0,4},{1,3},{2,6},{3,1},{4,0},{5,7},{6,2},{7,5},{8,12},{9,11},{10,... | collective-permute-start | bytes 393224 | tf_op jit(solution)/shard_map/ppermute | solution.py:438
  65.8 7.9 %collective-permute-start.19 = (bf16[512,128]{1,0:T(8,128)(2,1)S(1)}, bf16[512,128]{1,0:T(8,128)(2,1)S(1)}, u32[]{:S(2)}, u32[]{:S(2)}) collective-permute-start(bf16[512,128]{1,0:T(8,128)(2,1)S(1)} %get-tuple-element.194), channel_id=1, source_target_pairs={{0,4},{1,5},{2,6},{3,7},{4,0},{5,1},{6,2},{7,3},{8,12},{9,13},{10,... | collective-permute-start | bytes 393224 | tf_op jit(solution)/shard_map/ppermute | solution.py:438
  67.1 11.1 %collective-permute-start.20 = (bf16[512,128]{1,0:T(8,128)(2,1)S(1)}, bf16[512,128]{1,0:T(8,128)(2,1)S(1)}, u32[]{:S(2)}, u32[]{:S(2)}) collective-permute-start(bf16[512,128]{1,0:T(8,128)(2,1)S(1)} %get-tuple-element.196), channel_id=1, source_target_pairs={{0,8},{1,9},{2,10},{3,11},{4,12},{5,13},{6,14},{7,15},{8,0},{9,1},... | collective-permute-start | bytes 393224 | tf_op jit(solution)/shard_map/ppermute | solution.py:438
  70.8 8.9 %collective-permute-start.21 = (bf16[512,128]{1,0:T(8,128)(2,1)S(1)}, bf16[512,128]{1,0:T(8,128)(2,1)S(1)}, u32[]{:S(2)}, u32[]{:S(2)}) collective-permute-start(bf16[512,128]{1,0:T(8,128)(2,1)S(1)} %get-tuple-element.198), channel_id=1, source_target_pairs={{0,8},{1,9},{2,10},{3,11},{4,12},{5,13},{6,14},{7,15},{8,0},{9,1},... | collective-permute-start | bytes 393224 | tf_op jit(solution)/shard_map/ppermute | solution.py:438
  73.8 13.1 %collective-permute-start.25 = (bf16[1024,128]{1,0:T(8,128)(2,1)S(1)}, bf16[1024,128]{1,0:T(8,128)(2,1)S(1)}, u32[]{:S(2)}, u32[]{:S(2)}) collective-permute-start(bf16[1024,128]{1,0:T(8,128)(2,1)S(1)} %get-tuple-element.204), channel_id=1, source_target_pairs={{0,2},{1,3},{2,0},{3,1},{4,6},{5,7},{6,4},{7,5},{8,10},{9,11},{10,... | collective-permute-start | bytes 786440 | tf_op jit(solution)/shard_map/ppermute | solution.py:438
  78.3 5.0 %collective-permute-start.22 = (bf16[512,128]{1,0:T(8,128)(2,1)S(1)}, bf16[512,128]{1,0:T(8,128)(2,1)S(1)}, u32[]{:S(2)}, u32[]{:S(2)}) collective-permute-start(bf16[512,128]{1,0:T(8,128)(2,1)S(1)} %get-tuple-element.200), channel_id=1, source_target_pairs={{0,4},{1,5},{2,6},{3,7},{4,0},{5,1},{6,2},{7,3},{8,12},{9,13},{10,... | collective-permute-start | bytes 393224 | tf_op jit(solution)/shard_map/ppermute | solution.py:438
  79.7 7.2 %collective-permute-start.26 = (bf16[512,128]{1,0:T(8,128)(2,1)S(1)}, bf16[512,128]{1,0:T(8,128)(2,1)S(1)}, u32[]{:S(2)}, u32[]{:S(2)}) collective-permute-start(bf16[512,128]{1,0:T(8,128)(2,1)S(1)} %get-tuple-element.205), channel_id=1, source_target_pairs={{0,4},{1,3},{2,6},{3,1},{4,0},{5,7},{6,2},{7,5},{8,12},{9,11},{10,... | collective-permute-start | bytes 393224 | tf_op jit(solution)/shard_map/ppermute | solution.py:438
  80.5 6.1 %collective-permute-start.23 = (bf16[128,256]{1,0:T(8,128)(2,1)S(1)}, bf16[128,256]{1,0:T(8,128)(2,1)S(1)}, u32[]{:S(2)}, u32[]{:S(2)}) collective-permute-start(bf16[128,256]{1,0:T(8,128)(2,1)S(1)} %get-tuple-element.202), channel_id=1, source_target_pairs={{4,0},{8,4},{12,8},{5,1},{9,5},{13,9},{6,2},{10,6},{14,10},{7,3},{... | collective-permute-start | bytes 196616 | tf_op jit(solution)/shard_map/ppermute | solution.py:466
  81.8 5.1 %collective-permute-start.24 = (bf16[128,256]{1,0:T(8,128)(2,1)S(1)}, bf16[128,256]{1,0:T(8,128)(2,1)S(1)}, u32[]{:S(2)}, u32[]{:S(2)}) collective-permute-start(bf16[128,256]{1,0:T(8,128)(2,1)S(1)} %get-tuple-element.203), channel_id=1, source_target_pairs={{0,2},{2,0},{1,3},{3,1},{4,6},{6,4},{5,7},{7,5},{8,10},{10,8},{9,1... | collective-permute-start | bytes 196616 | tf_op jit(solution)/shard_map/ppermute | solution.py:425
  83.4 7.8 %collective-permute-start.27 = (bf16[1024,128]{1,0:T(8,128)(2,1)S(1)}, bf16[1024,128]{1,0:T(8,128)(2,1)S(1)}, u32[]{:S(2)}, u32[]{:S(2)}) collective-permute-start(bf16[1024,128]{1,0:T(8,128)(2,1)S(1)} %get-tuple-element.213), channel_id=1, source_target_pairs={{0,2},{1,3},{2,0},{3,1},{4,6},{5,7},{6,4},{7,5},{8,10},{9,11},{10,... | collective-permute-start | bytes 786440 | tf_op jit(solution)/shard_map/ppermute | solution.py:438
  86.9 7.1 %collective-permute-start.28 = (bf16[1024,128]{1,0:T(8,128)(2,1)S(1)}, bf16[1024,128]{1,0:T(8,128)(2,1)S(1)}, u32[]{:S(2)}, u32[]{:S(2)}) collective-permute-start(bf16[1024,128]{1,0:T(8,128)(2,1)S(1)} %get-tuple-element.220), channel_id=1, source_target_pairs={{0,2},{1,5},{2,0},{3,7},{4,6},{5,1},{6,4},{7,3},{8,10},{9,13},{10,... | collective-permute-start | bytes 786440 | tf_op jit(solution)/shard_map/ppermute | solution.py:438
  (3 other events, 3.3 us)

commit v20 on v19

--- a/solution.py
+++ b/solution.py
@@ -597,7 +597,7 @@
             name=f"back{layer}",
             after=after,
         )
-        sums[layer] = Sum(whole, basin_first if layer else stages)
+        sums[layer] = Sum(whole, basin_first if layer > 1 else stages)
         return [outs[0], grad], [grad]
 
     def join(layer, state, after):

time: 95.9 us -> 97.5 us (1.017)
  starting transfers between devices: 35.8 us -> 46.8 us
  waiting for transfers between devices: 25.4 us -> 15.9 us
    ppermute x18, starting transfers between devices: 28.4 us -> 38.8 us  [over_mesh(): return lax.ppermute(x, ('chain', 'basin', 'feat'), perm)]
    ppermute x18, waiting for transfers between devices: 18.2 us -> 8.28 us  [over_mesh(): return lax.ppermute(x, ('chain', 'basin', 'feat'), perm)]
  transfers between devices with their start and end apart: 29 -> 29, of which waited for: 20 -> 15; matrix products, arithmetic and copies ran while one was open for 1% -> 1% of each run, Pallas kernels for 27% -> 26%
where the time goes in v20:
time: 97.5 us; the launch traced here: 97.2 us
  starting transfers between devices  46.8 us (48%)
  Pallas kernels  31.3 us (32%)
  waiting for transfers between devices  15.9 us (16%)
  local copies, waits for them, and re-layouts  1.2 us (1%)
  between operations  1.18 us (1%)
    ppermute x18, starting transfers between devices, over_mesh(): return lax.ppermute(x, ('chain', 'basin', 'feat'), perm)  38.8 us
    pallas_call x33, Pallas kernels, call(): pl.pallas_call(lambda *refs: body(*refs[skipped:]), out_shape=[jax.ShapeD...  26.9 us
    ppermute x18, waiting for transfers between devices, over_mesh(): return lax.ppermute(x, ('chain', 'basin', 'feat'), perm)  8.28 us
    ppermute x3, waiting for transfers between devices, backward(): up = lax.ppermute(grads[0], 'chain', [(c, c - 1) for c in range(1, chain)])  6.71 us
    pallas_call x4, Pallas kernels, write(): pl.pallas_call(functools.partial(write_kernel, layer, sums[layer].stages[...  4.45 us
    ppermute x8, starting transfers between devices, around(): return lax.ppermute(x, axis, [(i, (i + distance) % n) for i in range(n)])  4.09 us
    ppermute x3, starting transfers between devices, backward(): up = lax.ppermute(grads[0], 'chain', [(c, c - 1) for c in range(1, chain)])  3.88 us
  transfers between devices with their start and end apart: 29, of which 15 were waited for; matrix products, arithmetic and copies ran while one was open for 1% of the time, Pallas kernels for 26%

profile of v20, /device:TPU:0, one launch (start us, length us, event | category | flops | bytes accessed | tf_op | source)
XLA Modules:
  0.0 97.2 jit_solution(15806762961070176237)
XLA Ops:
  3.6 4.9 %collective-permute-start = (bf16[128,256]{1,0:T(8,128)(2,1)S(1)}, bf16[128,256]{1,0:T(8,128)(2,1)S(1)}, u32[]{:S(2)}, u32[]{:S(2)}) collective-permute-start(bf16[128,256]{1,0:T(8,128)(2,1)S(1)} %get-tuple-element.114), channel_id=1, source_target_pairs={{0,4},{1,3},{2,6},{3,1},{4,8},{5,7},{6,10},{7,5},{8,12},{9,11},{10... | collective-permute-start | bytes 196616 | tf_op jit(solution)/shard_map/ppermute | solution.py:438
  10.5 1.6 %adjacency.1 = (bf16[768,768]{1,0:T(8,128)(2,1)S(1)}, bf16[768,768]{1,0:T(8,128)(2,1)S(1)}, bf16[768,256]{1,0:T(8,128)(2,1)S(1)}, bf16[256,768]{1,0:T(8,128)(2,1)S(1)}) custom-call(s32[4,6]{1,0:T(4,128)S(1)} %bitcast.4, bf16[6,4,128,128]{3,2,1,0:T(8,128)(2,1)S(1)} %copy-done.3, bf16[128,768]{1,0:T(8,128)(2,1)S(1)} %get-tuple-element.115.refs_2_, ...), custom_call_target="tpu_custom_call" | custom-call | flops 150994944 | bytes 4000000 | tf_op jit(solution)/shard_map/adjacency/pallas_call | solution.py:32
  14.5 3.5 %collective-permute-start.4 = (bf16[128,256]{1,0:T(8,128)(2,1)S(1)}, bf16[128,256]{1,0:T(8,128)(2,1)S(1)}, u32[]{:S(2)}, u32[]{:S(2)}) collective-permute-start(bf16[128,256]{1,0:T(8,128)(2,1)S(1)} %get-tuple-element.124), channel_id=1, source_target_pairs={{0,4},{1,3},{2,6},{3,1},{4,8},{5,7},{6,10},{7,5},{8,12},{9,11},{10... | collective-permute-start | bytes 196616 | tf_op jit(solution)/shard_map/ppermute | solution.py:438
  18.0 1.6 %local1.1 = (bf16[768,256]{1,0:T(8,128)(2,1)S(1)}, bf16[768,512]{1,0:T(8,128)(2,1)S(1)}, bf16[768,512]{1,0:T(8,128)(2,1)S(1)}, bf16[512,768]{1,0:T(8,128)(2,1)S(1)}, bf16[256,768]{1,0:T(8,128)(2,1)S(1)}) custom-call(bf16[768,256]{1,0:T(8,128)(2,1)S(1)} %get-tuple-element.125.refs_0_, bf16[3,256,512]{2,1,0:T(8,128)(2,1)S(1)} %copy-done, ...), custom_call_target="tpu_custom_call" | custom-call | flops 805306368 | bytes 4000000 | tf_op jit(solution)/shard_map/local1/pallas_call | solution.py:32
  22.2 4.3 %collective-permute-start.6 = (bf16[128,256]{1,0:T(8,128)(2,1)S(1)}, bf16[128,256]{1,0:T(8,128)(2,1)S(1)}, u32[]{:S(2)}, u32[]{:S(2)}) collective-permute-start(bf16[128,256]{1,0:T(8,128)(2,1)S(1)} %get-tuple-element.130), channel_id=1, source_target_pairs={{0,4},{1,3},{2,6},{3,1},{4,8},{5,7},{6,10},{7,5},{8,12},{9,11},{10... | collective-permute-start | bytes 196616 | tf_op jit(solution)/shard_map/ppermute | solution.py:438
  26.5 1.6 %local2.1 = (bf16[768,256]{1,0:T(8,128)(2,1)S(1)}, bf16[768,512]{1,0:T(8,128)(2,1)S(1)}, bf16[768,512]{1,0:T(8,128)(2,1)S(1)}, bf16[512,768]{1,0:T(8,128)(2,1)S(1)}, bf16[256,768]{1,0:T(8,128)(2,1)S(1)}) custom-call(bf16[768,256]{1,0:T(8,128)(2,1)S(1)} %get-tuple-element.131.refs_0_, bf16[3,256,512]{2,1,0:T(8,128)(2,1)S(1)} %copy-done, ...), custom_call_target="tpu_custom_call" | custom-call | flops 805306368 | bytes 4000000 | tf_op jit(solution)/shard_map/local2/pallas_call | solution.py:32
  29.6 2.2 %turn.1 = (f32[768,256]{1,0:T(8,128)S(1)}, bf16[768,256]{1,0:T(8,128)(2,1)S(1)}, bf16[256,256]{1,0:T(8,128)(2,1)S(1)}, bf16[256,256]{1,0:T(8,128)(2,1)S(1)}, bf1...) custom-call(f32[768,256]{1,0:T(8,128)S(1)} %get-tuple-element.129.re, ...), custom_call_target="tpu_custom_call" | custom-call | flops 536870912 | bytes 4000000 | tf_op jit(solution)/shard_map/turn/pallas_call | solution.py:32
  31.9 1.3 %collective-permute-start.8 = (bf16[128,256]{1,0:T(8,128)(2,1)S(1)}, bf16[128,256]{1,0:T(8,128)(2,1)S(1)}, u32[]{:S(2)}, u32[]{:S(2)}) collective-permute-start(bf16[128,256]{1,0:T(8,128)(2,1)S(1)} %get-tuple-element.147), channel_id=1, source_target_pairs={{4,0},{8,4},{12,8},{5,1},{9,5},{13,9},{6,2},{10,6},{14,10},{7,3},{... | collective-permute-start | bytes 196616 | tf_op jit(solution)/shard_map/ppermute | solution.py:466
  33.2 1.6 %collective-permute-start.9 = (bf16[128,256]{1,0:T(8,128)(2,1)S(1)}, bf16[128,256]{1,0:T(8,128)(2,1)S(1)}, u32[]{:S(2)}, u32[]{:S(2)}) collective-permute-start(bf16[128,256]{1,0:T(8,128)(2,1)S(1)} %get-tuple-element.148), channel_id=1, source_target_pairs={{0,2},{2,0},{1,3},{3,1},{4,6},{6,4},{5,7},{7,5},{8,10},{10,8},{9,1... | collective-permute-start | bytes 196616 | tf_op jit(solution)/shard_map/ppermute | solution.py:425
  34.8 2.4 %back2.1 = (f32[768,256]{1,0:T(8,128)S(1)}, f32[2048,128]{1,0:T(8,128)S(1)}) custom-call(bf16[768,256]{1,0:T(8,128)(2,1)S(1)} %get-tuple-element.136.refs_0_, bf16[768,768]{1,0:T(8,128)(2,1)S(1)} %get-tuple-element.137.refs_1_.refs_2_, bf16[768,512]{1,0:T(8,128)(2,1)S(1)} %get-tuple-element.138.refs_2_, bf16[768,512]{1,0:T(8,128)(2,1)S(1)} %get-tuple-element.139.refs_3_, ...), custom_call_target="tpu_custom_call" | custom-call | flops 2717908992 | bytes 4000000 | tf_op jit(solution)/shard_map/back2/pallas_call | solution.py:32
  37.2 1.5 %collective-permute-done.8.refs_1_.refs_10_ = bf16[128,256]{1,0:T(8,128)(2,1)S(1)} collective-permute-done((bf16[128,256]{1,0:T(8,128)(2,1)S(1)}, bf16[128,256]{1,0:T(8,128)(2,1)S(1)}, u32[]{:S(2)}, u32[]{:S(2)}) %collective-permute-start.8) | collective-permute-done | bytes 65568 | tf_op jit(solution)/shard_map/ppermute | solution.py:466
  38.8 1.6 %collective-permute-start.12 = (bf16[1024,128]{1,0:T(8,128)(2,1)S(1)}, bf16[1024,128]{1,0:T(8,128)(2,1)S(1)}, u32[]{:S(2)}, u32[]{:S(2)}) collective-permute-start(bf16[1024,128]{1,0:T(8,128)(2,1)S(1)} %get-tuple-element.167), channel_id=1, source_target_pairs={{0,2},{1,3},{2,0},{3,1},{4,6},{5,7},{6,4},{7,5},{8,10},{9,11},{10,... | collective-permute-start | bytes 786440 | tf_op jit(solution)/shard_map/ppermute | solution.py:438
  40.3 1.6 %join2.1 = (f32[768,256]{1,0:T(8,128)S(1)}, bf16[768,256]{1,0:T(8,128)(2,1)S(1)}, bf16[256,256]{1,0:T(8,128)(2,1)S(1)}, bf16[256,256]{1,0:T(8,128)(2,1)S(1)}, bf...) custom-call(f32[1024,128]{1,0:T(8,128)S(1)} %get-tuple-element.150.r, ...), custom_call_target="tpu_custom_call" | custom-call | flops 536870912 | bytes 4000000 | tf_op jit(solution)/shard_map/join2/pallas_call | solution.py:32
  41.9 1.3 %collective-permute-start.10 = (bf16[128,256]{1,0:T(8,128)(2,1)S(1)}, bf16[128,256]{1,0:T(8,128)(2,1)S(1)}, u32[]{:S(2)}, u32[]{:S(2)}) collective-permute-start(bf16[128,256]{1,0:T(8,128)(2,1)S(1)} %get-tuple-element.163), channel_id=1, source_target_pairs={{4,0},{8,4},{12,8},{5,1},{9,5},{13,9},{6,2},{10,6},{14,10},{7,3},{... | collective-permute-start | bytes 196616 | tf_op jit(solution)/shard_map/ppermute | solution.py:466
  43.8 2.4 %back1.1 = (f32[768,256]{1,0:T(8,128)S(1)}, f32[2048,128]{1,0:T(8,128)S(1)}) custom-call(bf16[768,256]{1,0:T(8,128)(2,1)S(1)} %get-tuple-element.153.refs_0_.refs_1_, bf16[768,256]{1,0:T(8,128)(2,1)S(1)} %get-tuple-element.153.refs_0_.refs_1_, bf16[768,768]{1,0:T(8,128)(2,1)S(1)} %get-tuple-element.137.refs_1_.refs_2_, ...), custom_call_target="tpu_custom_call" | custom-call | flops 2717908992 | bytes 4000000 | tf_op jit(solution)/shard_map/back1/pallas_call | solution.py:32
  46.2 1.9 %collective-permute-done.10.refs_1_.refs_10_ = bf16[128,256]{1,0:T(8,128)(2,1)S(1)} collective-permute-done((bf16[128,256]{1,0:T(8,128)(2,1)S(1)}, bf16[128,256]{1,0:T(8,128)(2,1)S(1)}, u32[]{:S(2)}, u32[]{:S(2)}) %collective-permute-start.10) | collective-permute-done | bytes 65568 | tf_op jit(solution)/shard_map/ppermute | solution.py:466
  48.3 1.6 %collective-permute-start.14 = (bf16[1024,128]{1,0:T(8,128)(2,1)S(1)}, bf16[1024,128]{1,0:T(8,128)(2,1)S(1)}, u32[]{:S(2)}, u32[]{:S(2)}) collective-permute-start(bf16[1024,128]{1,0:T(8,128)(2,1)S(1)} %get-tuple-element.184), channel_id=1, source_target_pairs={{0,2},{1,5},{2,0},{3,7},{4,6},{5,1},{6,4},{7,3},{8,10},{9,13},{10,... | collective-permute-start | bytes 786440 | tf_op jit(solution)/shard_map/ppermute | solution.py:438
  50.0 1.6 %collective-permute-start.13 = (bf16[512,128]{1,0:T(8,128)(2,1)S(1)}, bf16[512,128]{1,0:T(8,128)(2,1)S(1)}, u32[]{:S(2)}, u32[]{:S(2)}) collective-permute-start(bf16[512,128]{1,0:T(8,128)(2,1)S(1)} %get-tuple-element.180), channel_id=1, source_target_pairs={{0,4},{1,5},{2,6},{3,7},{4,0},{5,1},{6,2},{7,3},{8,12},{9,13},{10,... | collective-permute-start | bytes 393224 | tf_op jit(solution)/shard_map/ppermute | solution.py:438
  51.5 1.6 %join1.1 = (f32[768,256]{1,0:T(8,128)S(1)}, bf16[768,256]{1,0:T(8,128)(2,1)S(1)}, bf16[256,256]{1,0:T(8,128)(2,1)S(1)}, bf16[256,256]{1,0:T(8,128)(2,1)S(1)}, bf...) custom-call(f32[512,128]{1,0:T(8,128)S(1)} %get-tuple-element.168.re, ...), custom_call_target="tpu_custom_call" | custom-call | flops 536870912 | bytes 4000000 | tf_op jit(solution)/shard_map/join1/pallas_call | solution.py:32
  53.1 2.4 %back0.1 = (f32[768,256]{1,0:T(8,128)S(1)}, f32[2048,128]{1,0:T(8,128)S(1)}) custom-call(bf16[768,256]{1,0:T(8,128)(2,1)S(1)} %get-tuple-element.170.refs_0_.refs_1_, bf16[768,256]{1,0:T(8,128)(2,1)S(1)} %get-tuple-element.170.refs_0_.refs_1_, bf16[768,768]{1,0:T(8,128)(2,1)S(1)} %get-tuple-element.137.refs_1_.refs_2_, ...), custom_call_target="tpu_custom_call" | custom-call | flops 2717908992 | bytes 4000000 | tf_op jit(solution)/shard_map/back0/pallas_call | solution.py:32
  57.1 2.9 %collective-permute-start.16 = (bf16[512,128]{1,0:T(8,128)(2,1)S(1)}, bf16[512,128]{1,0:T(8,128)(2,1)S(1)}, u32[]{:S(2)}, u32[]{:S(2)}) collective-permute-start(bf16[512,128]{1,0:T(8,128)(2,1)S(1)} %get-tuple-element.188), channel_id=1, source_target_pairs={{0,8},{1,9},{2,10},{3,11},{4,12},{5,13},{6,14},{7,15},{8,0},{9,1},... | collective-permute-start | bytes 393224 | tf_op jit(solution)/shard_map/ppermute | solution.py:438
  60.1 1.3 %collective-permute-start.17 = (bf16[512,128]{1,0:T(8,128)(2,1)S(1)}, bf16[512,128]{1,0:T(8,128)(2,1)S(1)}, u32[]{:S(2)}, u32[]{:S(2)}) collective-permute-start(bf16[512,128]{1,0:T(8,128)(2,1)S(1)} %get-tuple-element.190), channel_id=1, source_target_pairs={{0,4},{1,3},{2,6},{3,1},{4,0},{5,7},{6,2},{7,5},{8,12},{9,11},{10,... | collective-permute-start | bytes 393224 | tf_op jit(solution)/shard_map/ppermute | solution.py:438
  62.5 3.2 %collective-permute-start.18 = (bf16[512,128]{1,0:T(8,128)(2,1)S(1)}, bf16[512,128]{1,0:T(8,128)(2,1)S(1)}, u32[]{:S(2)}, u32[]{:S(2)}) collective-permute-start(bf16[512,128]{1,0:T(8,128)(2,1)S(1)} %get-tuple-element.192), channel_id=1, source_target_pairs={{0,4},{1,3},{2,6},{3,1},{4,0},{5,7},{6,2},{7,5},{8,12},{9,11},{10,... | collective-permute-start | bytes 393224 | tf_op jit(solution)/shard_map/ppermute | solution.py:438
  66.4 3.5 %collective-permute-start.20 = (bf16[512,128]{1,0:T(8,128)(2,1)S(1)}, bf16[512,128]{1,0:T(8,128)(2,1)S(1)}, u32[]{:S(2)}, u32[]{:S(2)}) collective-permute-start(bf16[512,128]{1,0:T(8,128)(2,1)S(1)} %get-tuple-element.196), channel_id=1, source_target_pairs={{0,8},{1,9},{2,10},{3,11},{4,12},{5,13},{6,14},{7,15},{8,0},{9,1},... | collective-permute-start | bytes 393224 | tf_op jit(solution)/shard_map/ppermute | solution.py:438
  69.9 2.7 %collective-permute-start.21 = (bf16[512,128]{1,0:T(8,128)(2,1)S(1)}, bf16[512,128]{1,0:T(8,128)(2,1)S(1)}, u32[]{:S(2)}, u32[]{:S(2)}) collective-permute-start(bf16[512,128]{1,0:T(8,128)(2,1)S(1)} %get-tuple-element.198), channel_id=1, source_target_pairs={{0,8},{1,9},{2,10},{3,11},{4,12},{5,13},{6,14},{7,15},{8,0},{9,1},... | collective-permute-start | bytes 393224 | tf_op jit(solution)/shard_map/ppermute | solution.py:438
  72.6 1.9 %collective-permute-done.19.refs_2_ = bf16[512,128]{1,0:T(8,128)(2,1)S(1)} collective-permute-done((bf16[512,128]{1,0:T(8,128)(2,1)S(1)}, bf16[512,128]{1,0:T(8,128)(2,1)S(1)}, u32[]{:S(2)}, u32[]{:S(2)}) %collective-permute-start.19) | collective-permute-done | bytes 131104 | tf_op jit(solution)/shard_map/ppermute | solution.py:438
  75.1 4.2 %collective-permute-start.22 = (bf16[512,128]{1,0:T(8,128)(2,1)S(1)}, bf16[512,128]{1,0:T(8,128)(2,1)S(1)}, u32[]{:S(2)}, u32[]{:S(2)}) collective-permute-start(bf16[512,128]{1,0:T(8,128)(2,1)S(1)} %get-tuple-element.200), channel_id=1, source_target_pairs={{0,4},{1,3},{2,6},{3,1},{4,0},{5,7},{6,2},{7,5},{8,12},{9,11},{10,... | collective-permute-start | bytes 393224 | tf_op jit(solution)/shard_map/ppermute | solution.py:438
  79.3 2.8 %collective-permute-done.21.refs_2_ = bf16[512,128]{1,0:T(8,128)(2,1)S(1)} collective-permute-done((bf16[512,128]{1,0:T(8,128)(2,1)S(1)}, bf16[512,128]{1,0:T(8,128)(2,1)S(1)}, u32[]{:S(2)}, u32[]{:S(2)}) %collective-permute-start.21) | collective-permute-done | bytes 131104 | tf_op jit(solution)/shard_map/ppermute | solution.py:438
  82.2 1.3 %collective-permute-start.23 = (bf16[128,256]{1,0:T(8,128)(2,1)S(1)}, bf16[128,256]{1,0:T(8,128)(2,1)S(1)}, u32[]{:S(2)}, u32[]{:S(2)}) collective-permute-start(bf16[128,256]{1,0:T(8,128)(2,1)S(1)} %get-tuple-element.202), channel_id=1, source_target_pairs={{4,0},{8,4},{12,8},{5,1},{9,5},{13,9},{6,2},{10,6},{14,10},{7,3},{... | collective-permute-start | bytes 196616 | tf_op jit(solution)/shard_map/ppermute | solution.py:466
  83.5 1.3 %collective-permute-start.24 = (bf16[128,256]{1,0:T(8,128)(2,1)S(1)}, bf16[128,256]{1,0:T(8,128)(2,1)S(1)}, u32[]{:S(2)}, u32[]{:S(2)}) collective-permute-start(bf16[128,256]{1,0:T(8,128)(2,1)S(1)} %get-tuple-element.203), channel_id=1, source_target_pairs={{0,2},{2,0},{1,3},{3,1},{4,6},{6,4},{5,7},{7,5},{8,10},{10,8},{9,1... | collective-permute-start | bytes 196616 | tf_op jit(solution)/shard_map/ppermute | solution.py:425
  85.7 3.3 %collective-permute-done.23.refs_1_.refs_4_ = bf16[128,256]{1,0:T(8,128)(2,1)S(1)} collective-permute-done((bf16[128,256]{1,0:T(8,128)(2,1)S(1)}, bf16[128,256]{1,0:T(8,128)(2,1)S(1)}, u32[]{:S(2)}, u32[]{:S(2)}) %collective-permute-start.23) | collective-permute-done | bytes 65568 | tf_op jit(solution)/shard_map/ppermute | solution.py:466
  95.6 1.4 %write0.3 = (f32[3,256,512]{2,1,0:T(8,128)}, f32[3,512,256]{2,1,0:T(8,128)}, f32[8,128]{1,0:T(8,128)}) custom-call(f32[3,256,512]{2,1,0:T(8,128)} %get-tuple-element.217.refs_0_, f32[3,512,256]{2,1,0:T(8,128)} %get-tuple-element.218.refs_1_, f32[8,128]{1,0:T(8,128)S(1)} %get-tuple-element.219.refs_2_, ...), custom_call_target="tpu_custom_call", output_to_operand_aliasing={{0}: (0, {}), {1}: (1, {})} | custom-call | flops 1 | bytes 1 | tf_op jit(solution)/shard_map/write0/pallas_call | solution.py:627
  (76 shorter events, 24.0 us)
Async XLA Ops:
  0.6 8.8 %copy-start = (bf16[3,256,512]{2,1,0:T(8,128)(2,1)S(1)}, bf16[3,256,512]{2,1,0:T(8,128)(2,1)}, u32[]{:S(2)}) copy-start(bf16[3,256,512]{2,1,0:T(8,128)(2,1)} %refs_7_.5) | copy-start | bytes 2359300
  0.6 8.8 %copy-start.1 = (bf16[3,512,256]{2,1,0:T(8,128)(2,1)S(1)}, bf16[3,512,256]{2,1,0:T(8,128)(2,1)}, u32[]{:S(2)}) copy-start(bf16[3,512,256]{2,1,0:T(8,128)(2,1)} %refs_9_.3) | copy-start | bytes 2359300
  0.7 7.9 %collective-permute-start.1 = (bf16[3,256,512]{2,1,0:T(8,128)(2,1)}, bf16[3,256,512]{2,1,0:T(8,128)(2,1)S(1)}, u32[]{:S(2)}, u32[]{:S(2)}) collective-permute-start(bf16[3,256,512]{2,1,0:T(8,128)(2,1)} %refs_7_.5), channel_id=1, source_target_pairs={{0,1},{1,0},{2,3},{3,2},{4,5},{5,4},{6,7},{7,6},{8,9},{9,8},{10,11... | collective-permute-start | bytes 2359304 | tf_op jit(solution)/shard_map/ppermute | solution.py:425
  1.2 7.4 %collective-permute-start.2 = (bf16[3,512,256]{2,1,0:T(8,128)(2,1)}, bf16[3,512,256]{2,1,0:T(8,128)(2,1)S(1)}, u32[]{:S(2)}, u32[]{:S(2)}) collective-permute-start(bf16[3,512,256]{2,1,0:T(8,128)(2,1)} %refs_9_.3), channel_id=1, source_target_pairs={{0,1},{1,0},{2,3},{3,2},{4,5},{5,4},{6,7},{7,6},{8,9},{9,8},{10,11... | collective-permute-start | bytes 2359304 | tf_op jit(solution)/shard_map/ppermute | solution.py:425
  3.6 8.5 %collective-permute-start = (bf16[128,256]{1,0:T(8,128)(2,1)S(1)}, bf16[128,256]{1,0:T(8,128)(2,1)S(1)}, u32[]{:S(2)}, u32[]{:S(2)}) collective-permute-start(bf16[128,256]{1,0:T(8,128)(2,1)S(1)} %get-tuple-element.114), channel_id=1, source_target_pairs={{0,4},{1,3},{2,6},{3,1},{4,8},{5,7},{6,10},{7,5},{8,12},{9,11},{10... | collective-permute-start | bytes 196616 | tf_op jit(solution)/shard_map/ppermute | solution.py:438
  12.1 1.3 %collective-permute-start.3 = (bf16[128,256]{1,0:T(8,128)(2,1)S(1)}, bf16[128,256]{1,0:T(8,128)(2,1)S(1)}, u32[]{:S(2)}, u32[]{:S(2)}) collective-permute-start(bf16[128,256]{1,0:T(8,128)(2,1)S(1)} %collective-permute-done.refs_7_.refs_12_), channel_id=1, source_target_pairs={{0,1},{1,0},{2,3},{3,2},{4,5},{5,4},{6,7},{7,6},{8,9},{9,8},{10,11... | collective-permute-start | bytes 196616 | tf_op jit(solution)/shard_map/ppermute | solution.py:425
  14.5 5.4 %collective-permute-start.4 = (bf16[128,256]{1,0:T(8,128)(2,1)S(1)}, bf16[128,256]{1,0:T(8,128)(2,1)S(1)}, u32[]{:S(2)}, u32[]{:S(2)}) collective-permute-start(bf16[128,256]{1,0:T(8,128)(2,1)S(1)} %get-tuple-element.124), channel_id=1, source_target_pairs={{0,4},{1,3},{2,6},{3,1},{4,8},{5,7},{6,10},{7,5},{8,12},{9,11},{10... | collective-permute-start | bytes 196616 | tf_op jit(solution)/shard_map/ppermute | solution.py:438
  19.9 1.3 %collective-permute-start.5 = (bf16[128,256]{1,0:T(8,128)(2,1)S(1)}, bf16[128,256]{1,0:T(8,128)(2,1)S(1)}, u32[]{:S(2)}, u32[]{:S(2)}) collective-permute-start(bf16[128,256]{1,0:T(8,128)(2,1)S(1)} %collective-permute-done.4.refs_7_.refs_12_), channel_id=1, source_target_pairs={{0,1},{1,0},{2,3},{3,2},{4,5},{5,4},{6,7},{7,6},{8,9},{9,8},{10,11... | collective-permute-start | bytes 196616 | tf_op jit(solution)/shard_map/ppermute | solution.py:425
  22.2 6.2 %collective-permute-start.6 = (bf16[128,256]{1,0:T(8,128)(2,1)S(1)}, bf16[128,256]{1,0:T(8,128)(2,1)S(1)}, u32[]{:S(2)}, u32[]{:S(2)}) collective-permute-start(bf16[128,256]{1,0:T(8,128)(2,1)S(1)} %get-tuple-element.130), channel_id=1, source_target_pairs={{0,4},{1,3},{2,6},{3,1},{4,8},{5,7},{6,10},{7,5},{8,12},{9,11},{10... | collective-permute-start | bytes 196616 | tf_op jit(solution)/shard_map/ppermute | solution.py:438
  28.4 1.3 %copy-start.2 = (f32[768,256]{1,0:T(8,128)S(1)}, f32[768,256]{1,0:T(8,128)}, u32[]{:S(2)}) copy-start(f32[768,256]{1,0:T(8,128)} %refs_4_.5) | copy-start | bytes 2359300
  28.4 1.3 %collective-permute-start.7 = (bf16[128,256]{1,0:T(8,128)(2,1)S(1)}, bf16[128,256]{1,0:T(8,128)(2,1)S(1)}, u32[]{:S(2)}, u32[]{:S(2)}) collective-permute-start(bf16[128,256]{1,0:T(8,128)(2,1)S(1)} %collective-permute-done.6.refs_7_.refs_9_), channel_id=1, source_target_pairs={{0,1},{1,0},{2,3},{3,2},{4,5},{5,4},{6,7},{7,6},{8,9},{9,8},{10,11... | collective-permute-start | bytes 196616 | tf_op jit(solution)/shard_map/ppermute | solution.py:425
  31.9 6.8 %collective-permute-start.8 = (bf16[128,256]{1,0:T(8,128)(2,1)S(1)}, bf16[128,256]{1,0:T(8,128)(2,1)S(1)}, u32[]{:S(2)}, u32[]{:S(2)}) collective-permute-start(bf16[128,256]{1,0:T(8,128)(2,1)S(1)} %get-tuple-element.147), channel_id=1, source_target_pairs={{4,0},{8,4},{12,8},{5,1},{9,5},{13,9},{6,2},{10,6},{14,10},{7,3},{... | collective-permute-start | bytes 196616 | tf_op jit(solution)/shard_map/ppermute | solution.py:466
  33.2 5.5 %collective-permute-start.9 = (bf16[128,256]{1,0:T(8,128)(2,1)S(1)}, bf16[128,256]{1,0:T(8,128)(2,1)S(1)}, u32[]{:S(2)}, u32[]{:S(2)}) collective-permute-start(bf16[128,256]{1,0:T(8,128)(2,1)S(1)} %get-tuple-element.148), channel_id=1, source_target_pairs={{0,2},{2,0},{1,3},{3,1},{4,6},{6,4},{5,7},{7,5},{8,10},{10,8},{9,1... | collective-permute-start | bytes 196616 | tf_op jit(solution)/shard_map/ppermute | solution.py:425
  38.8 11.1 %collective-permute-start.12 = (bf16[1024,128]{1,0:T(8,128)(2,1)S(1)}, bf16[1024,128]{1,0:T(8,128)(2,1)S(1)}, u32[]{:S(2)}, u32[]{:S(2)}) collective-permute-start(bf16[1024,128]{1,0:T(8,128)(2,1)S(1)} %get-tuple-element.167), channel_id=1, source_target_pairs={{0,2},{1,3},{2,0},{3,1},{4,6},{5,7},{6,4},{7,5},{8,10},{9,11},{10,... | collective-permute-start | bytes 786440 | tf_op jit(solution)/shard_map/ppermute | solution.py:438
  41.9 6.2 %collective-permute-start.10 = (bf16[128,256]{1,0:T(8,128)(2,1)S(1)}, bf16[128,256]{1,0:T(8,128)(2,1)S(1)}, u32[]{:S(2)}, u32[]{:S(2)}) collective-permute-start(bf16[128,256]{1,0:T(8,128)(2,1)S(1)} %get-tuple-element.163), channel_id=1, source_target_pairs={{4,0},{8,4},{12,8},{5,1},{9,5},{13,9},{6,2},{10,6},{14,10},{7,3},{... | collective-permute-start | bytes 196616 | tf_op jit(solution)/shard_map/ppermute | solution.py:466
  43.2 5.0 %collective-permute-start.11 = (bf16[128,256]{1,0:T(8,128)(2,1)S(1)}, bf16[128,256]{1,0:T(8,128)(2,1)S(1)}, u32[]{:S(2)}, u32[]{:S(2)}) collective-permute-start(bf16[128,256]{1,0:T(8,128)(2,1)S(1)} %get-tuple-element.164), channel_id=1, source_target_pairs={{0,2},{2,0},{1,3},{3,1},{4,6},{6,4},{5,7},{7,5},{8,10},{10,8},{9,1... | collective-permute-start | bytes 196616 | tf_op jit(solution)/shard_map/ppermute | solution.py:425
  48.3 11.7 %collective-permute-start.14 = (bf16[1024,128]{1,0:T(8,128)(2,1)S(1)}, bf16[1024,128]{1,0:T(8,128)(2,1)S(1)}, u32[]{:S(2)}, u32[]{:S(2)}) collective-permute-start(bf16[1024,128]{1,0:T(8,128)(2,1)S(1)} %get-tuple-element.184), channel_id=1, source_target_pairs={{0,2},{1,5},{2,0},{3,7},{4,6},{5,1},{6,4},{7,3},{8,10},{9,13},{10,... | collective-permute-start | bytes 786440 | tf_op jit(solution)/shard_map/ppermute | solution.py:438
  50.0 5.9 %collective-permute-start.13 = (bf16[512,128]{1,0:T(8,128)(2,1)S(1)}, bf16[512,128]{1,0:T(8,128)(2,1)S(1)}, u32[]{:S(2)}, u32[]{:S(2)}) collective-permute-start(bf16[512,128]{1,0:T(8,128)(2,1)S(1)} %get-tuple-element.180), channel_id=1, source_target_pairs={{0,4},{1,5},{2,6},{3,7},{4,0},{5,1},{6,2},{7,3},{8,12},{9,13},{10,... | collective-permute-start | bytes 393224 | tf_op jit(solution)/shard_map/ppermute | solution.py:438
  56.0 6.4 %collective-permute-start.15 = (bf16[1024,128]{1,0:T(8,128)(2,1)S(1)}, bf16[1024,128]{1,0:T(8,128)(2,1)S(1)}, u32[]{:S(2)}, u32[]{:S(2)}) collective-permute-start(bf16[1024,128]{1,0:T(8,128)(2,1)S(1)} %get-tuple-element.186), channel_id=1, source_target_pairs={{0,2},{1,5},{2,0},{3,7},{4,6},{5,1},{6,4},{7,3},{8,10},{9,13},{10,... | collective-permute-start | bytes 786440 | tf_op jit(solution)/shard_map/ppermute | solution.py:438
  57.1 9.0 %collective-permute-start.16 = (bf16[512,128]{1,0:T(8,128)(2,1)S(1)}, bf16[512,128]{1,0:T(8,128)(2,1)S(1)}, u32[]{:S(2)}, u32[]{:S(2)}) collective-permute-start(bf16[512,128]{1,0:T(8,128)(2,1)S(1)} %get-tuple-element.188), channel_id=1, source_target_pairs={{0,8},{1,9},{2,10},{3,11},{4,12},{5,13},{6,14},{7,15},{8,0},{9,1},... | collective-permute-start | bytes 393224 | tf_op jit(solution)/shard_map/ppermute | solution.py:438
  60.1 6.2 %collective-permute-start.17 = (bf16[512,128]{1,0:T(8,128)(2,1)S(1)}, bf16[512,128]{1,0:T(8,128)(2,1)S(1)}, u32[]{:S(2)}, u32[]{:S(2)}) collective-permute-start(bf16[512,128]{1,0:T(8,128)(2,1)S(1)} %get-tuple-element.190), channel_id=1, source_target_pairs={{0,4},{1,3},{2,6},{3,1},{4,0},{5,7},{6,2},{7,5},{8,12},{9,11},{10,... | collective-permute-start | bytes 393224 | tf_op jit(solution)/shard_map/ppermute | solution.py:438
  62.5 7.3 %collective-permute-start.18 = (bf16[512,128]{1,0:T(8,128)(2,1)S(1)}, bf16[512,128]{1,0:T(8,128)(2,1)S(1)}, u32[]{:S(2)}, u32[]{:S(2)}) collective-permute-start(bf16[512,128]{1,0:T(8,128)(2,1)S(1)} %get-tuple-element.192), channel_id=1, source_target_pairs={{0,4},{1,3},{2,6},{3,1},{4,0},{5,7},{6,2},{7,5},{8,12},{9,11},{10,... | collective-permute-start | bytes 393224 | tf_op jit(solution)/shard_map/ppermute | solution.py:438
  66.2 8.3 %collective-permute-start.19 = (bf16[512,128]{1,0:T(8,128)(2,1)S(1)}, bf16[512,128]{1,0:T(8,128)(2,1)S(1)}, u32[]{:S(2)}, u32[]{:S(2)}) collective-permute-start(bf16[512,128]{1,0:T(8,128)(2,1)S(1)} %get-tuple-element.194), channel_id=1, source_target_pairs={{0,4},{1,5},{2,6},{3,7},{4,0},{5,1},{6,2},{7,3},{8,12},{9,13},{10,... | collective-permute-start | bytes 393224 | tf_op jit(solution)/shard_map/ppermute | solution.py:438
  66.4 8.7 %collective-permute-start.20 = (bf16[512,128]{1,0:T(8,128)(2,1)S(1)}, bf16[512,128]{1,0:T(8,128)(2,1)S(1)}, u32[]{:S(2)}, u32[]{:S(2)}) collective-permute-start(bf16[512,128]{1,0:T(8,128)(2,1)S(1)} %get-tuple-element.196), channel_id=1, source_target_pairs={{0,8},{1,9},{2,10},{3,11},{4,12},{5,13},{6,14},{7,15},{8,0},{9,1},... | collective-permute-start | bytes 393224 | tf_op jit(solution)/shard_map/ppermute | solution.py:438
  69.9 12.2 %collective-permute-start.21 = (bf16[512,128]{1,0:T(8,128)(2,1)S(1)}, bf16[512,128]{1,0:T(8,128)(2,1)S(1)}, u32[]{:S(2)}, u32[]{:S(2)}) collective-permute-start(bf16[512,128]{1,0:T(8,128)(2,1)S(1)} %get-tuple-element.198), channel_id=1, source_target_pairs={{0,8},{1,9},{2,10},{3,11},{4,12},{5,13},{6,14},{7,15},{8,0},{9,1},... | collective-permute-start | bytes 393224 | tf_op jit(solution)/shard_map/ppermute | solution.py:438
  74.5 14.5 %collective-permute-start.25 = (bf16[1024,128]{1,0:T(8,128)(2,1)S(1)}, bf16[1024,128]{1,0:T(8,128)(2,1)S(1)}, u32[]{:S(2)}, u32[]{:S(2)}) collective-permute-start(bf16[1024,128]{1,0:T(8,128)(2,1)S(1)} %get-tuple-element.204), channel_id=1, source_target_pairs={{0,2},{1,3},{2,0},{3,1},{4,6},{5,7},{6,4},{7,5},{8,10},{9,11},{10,... | collective-permute-start | bytes 786440 | tf_op jit(solution)/shard_map/ppermute | solution.py:438
  75.1 9.7 %collective-permute-start.22 = (bf16[512,128]{1,0:T(8,128)(2,1)S(1)}, bf16[512,128]{1,0:T(8,128)(2,1)S(1)}, u32[]{:S(2)}, u32[]{:S(2)}) collective-permute-start(bf16[512,128]{1,0:T(8,128)(2,1)S(1)} %get-tuple-element.200), channel_id=1, source_target_pairs={{0,4},{1,3},{2,6},{3,1},{4,0},{5,7},{6,2},{7,5},{8,12},{9,11},{10,... | collective-permute-start | bytes 393224 | tf_op jit(solution)/shard_map/ppermute | solution.py:438
  82.1 6.9 %collective-permute-start.26 = (bf16[512,128]{1,0:T(8,128)(2,1)S(1)}, bf16[512,128]{1,0:T(8,128)(2,1)S(1)}, u32[]{:S(2)}, u32[]{:S(2)}) collective-permute-start(bf16[512,128]{1,0:T(8,128)(2,1)S(1)} %get-tuple-element.205), channel_id=1, source_target_pairs={{0,4},{1,3},{2,6},{3,1},{4,0},{5,7},{6,2},{7,5},{8,12},{9,11},{10,... | collective-permute-start | bytes 393224 | tf_op jit(solution)/shard_map/ppermute | solution.py:438
  82.2 6.9 %collective-permute-start.23 = (bf16[128,256]{1,0:T(8,128)(2,1)S(1)}, bf16[128,256]{1,0:T(8,128)(2,1)S(1)}, u32[]{:S(2)}, u32[]{:S(2)}) collective-permute-start(bf16[128,256]{1,0:T(8,128)(2,1)S(1)} %get-tuple-element.202), channel_id=1, source_target_pairs={{4,0},{8,4},{12,8},{5,1},{9,5},{13,9},{6,2},{10,6},{14,10},{7,3},{... | collective-permute-start | bytes 196616 | tf_op jit(solution)/shard_map/ppermute | solution.py:466
  83.5 5.6 %collective-permute-start.24 = (bf16[128,256]{1,0:T(8,128)(2,1)S(1)}, bf16[128,256]{1,0:T(8,128)(2,1)S(1)}, u32[]{:S(2)}, u32[]{:S(2)}) collective-permute-start(bf16[128,256]{1,0:T(8,128)(2,1)S(1)} %get-tuple-element.203), channel_id=1, source_target_pairs={{0,2},{2,0},{1,3},{3,1},{4,6},{6,4},{5,7},{7,5},{8,10},{10,8},{9,1... | collective-permute-start | bytes 196616 | tf_op jit(solution)/shard_map/ppermute | solution.py:425
  84.8 7.5 %collective-permute-start.27 = (bf16[1024,128]{1,0:T(8,128)(2,1)S(1)}, bf16[1024,128]{1,0:T(8,128)(2,1)S(1)}, u32[]{:S(2)}, u32[]{:S(2)}) collective-permute-start(bf16[1024,128]{1,0:T(8,128)(2,1)S(1)} %get-tuple-element.213), channel_id=1, source_target_pairs={{0,2},{1,5},{2,0},{3,7},{4,6},{5,1},{6,4},{7,3},{8,10},{9,13},{10,... | collective-permute-start | bytes 786440 | tf_op jit(solution)/shard_map/ppermute | solution.py:438
  89.1 6.4 %collective-permute-start.28 = (bf16[1024,128]{1,0:T(8,128)(2,1)S(1)}, bf16[1024,128]{1,0:T(8,128)(2,1)S(1)}, u32[]{:S(2)}, u32[]{:S(2)}) collective-permute-start(bf16[1024,128]{1,0:T(8,128)(2,1)S(1)} %get-tuple-element.220), channel_id=1, source_target_pairs={{0,2},{1,5},{2,0},{3,7},{4,6},{5,1},{6,4},{7,3},{8,10},{9,13},{10,... | collective-permute-start | bytes 786440 | tf_op jit(solution)/shard_map/ppermute | solution.py:438
  (3 other events, 3.3 us)

commit v21 on v20

--- a/solution.py
+++ b/solution.py
@@ -597,7 +597,7 @@
             name=f"back{layer}",
             after=after,
         )
-        sums[layer] = Sum(whole, basin_first if layer > 1 else stages)
+        sums[layer] = Sum(whole, basin_first)
         return [outs[0], grad], [grad]
 
     def join(layer, state, after):

time: 97.5 us -> 95.9 us (0.984)
  starting transfers between devices: 46.8 us -> 35.6 us
  waiting for transfers between devices: 15.9 us -> 25.1 us
    ppermute x18, starting transfers between devices: 38.8 us -> 28 us  [over_mesh(): return lax.ppermute(x, ('chain', 'basin', 'feat'), perm)]
    ppermute x18, waiting for transfers between devices: 8.28 us -> 18.5 us  [over_mesh(): return lax.ppermute(x, ('chain', 'basin', 'feat'), perm)]
    ppermute x3, waiting for transfers between devices: 6.71 us -> 5.66 us  [backward(): up = lax.ppermute(grads[0], 'chain', [(c, c - 1) for c in range(1, chain)])]
  transfers between devices with their start and end apart: 29 -> 29, of which waited for: 15 -> 19; matrix products, arithmetic and copies ran while one was open for 1% -> 1% of each run, Pallas kernels for 26% -> 27%
where the time goes in v21:
time: 95.9 us; the launch traced here: 95.1 us
  starting transfers between devices  35.6 us (37%)
  Pallas kernels  31.3 us (33%)
  waiting for transfers between devices  25.1 us (26%)
  local copies, waits for them, and re-layouts  1.2 us (1%)
  between operations  1.18 us (1%)
    ppermute x18, starting transfers between devices, over_mesh(): return lax.ppermute(x, ('chain', 'basin', 'feat'), perm)  28 us
    pallas_call x33, Pallas kernels, call(): pl.pallas_call(lambda *refs: body(*refs[skipped:]), out_shape=[jax.ShapeD...  26.9 us
    ppermute x18, waiting for transfers between devices, over_mesh(): return lax.ppermute(x, ('chain', 'basin', 'feat'), perm)  18.5 us
    ppermute x3, waiting for transfers between devices, backward(): up = lax.ppermute(grads[0], 'chain', [(c, c - 1) for c in range(1, chain)])  5.66 us
    pallas_call x4, Pallas kernels, write(): pl.pallas_call(functools.partial(write_kernel, layer, sums[layer].stages[...  4.42 us
    ppermute x3, starting transfers between devices, backward(): up = lax.ppermute(grads[0], 'chain', [(c, c - 1) for c in range(1, chain)])  3.86 us
    ppermute x8, starting transfers between devices, around(): return lax.ppermute(x, axis, [(i, (i + distance) % n) for i in range(n)])  3.71 us
  transfers between devices with their start and end apart: 29, of which 19 were waited for; matrix products, arithmetic and copies ran while one was open for 1% of the time, Pallas kernels for 27%

profile of v21, /device:TPU:0, one launch (start us, length us, event | category | flops | bytes accessed | tf_op | source)
XLA Modules:
  0.0 95.1 jit_solution(5558812750869330718)
XLA Ops:
  3.6 4.9 %collective-permute-start = (bf16[128,256]{1,0:T(8,128)(2,1)S(1)}, bf16[128,256]{1,0:T(8,128)(2,1)S(1)}, u32[]{:S(2)}, u32[]{:S(2)}) collective-permute-start(bf16[128,256]{1,0:T(8,128)(2,1)S(1)} %get-tuple-element.114), channel_id=1, source_target_pairs={{0,4},{1,3},{2,6},{3,1},{4,8},{5,7},{6,10},{7,5},{8,12},{9,11},{10... | collective-permute-start | bytes 196616 | tf_op jit(solution)/shard_map/ppermute | solution.py:438
  10.5 1.6 %adjacency.1 = (bf16[768,768]{1,0:T(8,128)(2,1)S(1)}, bf16[768,768]{1,0:T(8,128)(2,1)S(1)}, bf16[768,256]{1,0:T(8,128)(2,1)S(1)}, bf16[256,768]{1,0:T(8,128)(2,1)S(1)}) custom-call(s32[4,6]{1,0:T(4,128)S(1)} %bitcast.4, bf16[6,4,128,128]{3,2,1,0:T(8,128)(2,1)S(1)} %copy-done.3, bf16[128,768]{1,0:T(8,128)(2,1)S(1)} %get-tuple-element.115.refs_2_, ...), custom_call_target="tpu_custom_call" | custom-call | flops 150994944 | bytes 4000000 | tf_op jit(solution)/shard_map/adjacency/pallas_call | solution.py:32
  14.5 3.5 %collective-permute-start.4 = (bf16[128,256]{1,0:T(8,128)(2,1)S(1)}, bf16[128,256]{1,0:T(8,128)(2,1)S(1)}, u32[]{:S(2)}, u32[]{:S(2)}) collective-permute-start(bf16[128,256]{1,0:T(8,128)(2,1)S(1)} %get-tuple-element.124), channel_id=1, source_target_pairs={{0,4},{1,3},{2,6},{3,1},{4,8},{5,7},{6,10},{7,5},{8,12},{9,11},{10... | collective-permute-start | bytes 196616 | tf_op jit(solution)/shard_map/ppermute | solution.py:438
  18.0 1.6 %local1.1 = (bf16[768,256]{1,0:T(8,128)(2,1)S(1)}, bf16[768,512]{1,0:T(8,128)(2,1)S(1)}, bf16[768,512]{1,0:T(8,128)(2,1)S(1)}, bf16[512,768]{1,0:T(8,128)(2,1)S(1)}, bf16[256,768]{1,0:T(8,128)(2,1)S(1)}) custom-call(bf16[768,256]{1,0:T(8,128)(2,1)S(1)} %get-tuple-element.125.refs_0_, bf16[3,256,512]{2,1,0:T(8,128)(2,1)S(1)} %copy-done, ...), custom_call_target="tpu_custom_call" | custom-call | flops 805306368 | bytes 4000000 | tf_op jit(solution)/shard_map/local1/pallas_call | solution.py:32
  22.2 4.3 %collective-permute-start.6 = (bf16[128,256]{1,0:T(8,128)(2,1)S(1)}, bf16[128,256]{1,0:T(8,128)(2,1)S(1)}, u32[]{:S(2)}, u32[]{:S(2)}) collective-permute-start(bf16[128,256]{1,0:T(8,128)(2,1)S(1)} %get-tuple-element.130), channel_id=1, source_target_pairs={{0,4},{1,3},{2,6},{3,1},{4,8},{5,7},{6,10},{7,5},{8,12},{9,11},{10... | collective-permute-start | bytes 196616 | tf_op jit(solution)/shard_map/ppermute | solution.py:438
  26.5 1.6 %local2.1 = (bf16[768,256]{1,0:T(8,128)(2,1)S(1)}, bf16[768,512]{1,0:T(8,128)(2,1)S(1)}, bf16[768,512]{1,0:T(8,128)(2,1)S(1)}, bf16[512,768]{1,0:T(8,128)(2,1)S(1)}, bf16[256,768]{1,0:T(8,128)(2,1)S(1)}) custom-call(bf16[768,256]{1,0:T(8,128)(2,1)S(1)} %get-tuple-element.131.refs_0_, bf16[3,256,512]{2,1,0:T(8,128)(2,1)S(1)} %copy-done, ...), custom_call_target="tpu_custom_call" | custom-call | flops 805306368 | bytes 4000000 | tf_op jit(solution)/shard_map/local2/pallas_call | solution.py:32
  29.6 2.2 %turn.1 = (f32[768,256]{1,0:T(8,128)S(1)}, bf16[768,256]{1,0:T(8,128)(2,1)S(1)}, bf16[256,256]{1,0:T(8,128)(2,1)S(1)}, bf16[256,256]{1,0:T(8,128)(2,1)S(1)}, bf1...) custom-call(f32[768,256]{1,0:T(8,128)S(1)} %get-tuple-element.129.re, ...), custom_call_target="tpu_custom_call" | custom-call | flops 536870912 | bytes 4000000 | tf_op jit(solution)/shard_map/turn/pallas_call | solution.py:32
  31.9 1.3 %collective-permute-start.8 = (bf16[128,256]{1,0:T(8,128)(2,1)S(1)}, bf16[128,256]{1,0:T(8,128)(2,1)S(1)}, u32[]{:S(2)}, u32[]{:S(2)}) collective-permute-start(bf16[128,256]{1,0:T(8,128)(2,1)S(1)} %get-tuple-element.147), channel_id=1, source_target_pairs={{4,0},{8,4},{12,8},{5,1},{9,5},{13,9},{6,2},{10,6},{14,10},{7,3},{... | collective-permute-start | bytes 196616 | tf_op jit(solution)/shard_map/ppermute | solution.py:466
  33.2 1.6 %collective-permute-start.9 = (bf16[128,256]{1,0:T(8,128)(2,1)S(1)}, bf16[128,256]{1,0:T(8,128)(2,1)S(1)}, u32[]{:S(2)}, u32[]{:S(2)}) collective-permute-start(bf16[128,256]{1,0:T(8,128)(2,1)S(1)} %get-tuple-element.148), channel_id=1, source_target_pairs={{0,2},{2,0},{1,3},{3,1},{4,6},{6,4},{5,7},{7,5},{8,10},{10,8},{9,1... | collective-permute-start | bytes 196616 | tf_op jit(solution)/shard_map/ppermute | solution.py:425
  34.8 2.4 %back2.1 = (f32[768,256]{1,0:T(8,128)S(1)}, f32[2048,128]{1,0:T(8,128)S(1)}) custom-call(bf16[768,256]{1,0:T(8,128)(2,1)S(1)} %get-tuple-element.136.refs_0_, bf16[768,768]{1,0:T(8,128)(2,1)S(1)} %get-tuple-element.137.refs_1_.refs_2_, bf16[768,512]{1,0:T(8,128)(2,1)S(1)} %get-tuple-element.138.refs_2_, bf16[768,512]{1,0:T(8,128)(2,1)S(1)} %get-tuple-element.139.refs_3_, ...), custom_call_target="tpu_custom_call" | custom-call | flops 2717908992 | bytes 4000000 | tf_op jit(solution)/shard_map/back2/pallas_call | solution.py:32
  37.2 1.5 %collective-permute-done.8.refs_1_.refs_10_ = bf16[128,256]{1,0:T(8,128)(2,1)S(1)} collective-permute-done((bf16[128,256]{1,0:T(8,128)(2,1)S(1)}, bf16[128,256]{1,0:T(8,128)(2,1)S(1)}, u32[]{:S(2)}, u32[]{:S(2)}) %collective-permute-start.8) | collective-permute-done | bytes 65568 | tf_op jit(solution)/shard_map/ppermute | solution.py:466
  38.8 1.6 %collective-permute-start.12 = (bf16[1024,128]{1,0:T(8,128)(2,1)S(1)}, bf16[1024,128]{1,0:T(8,128)(2,1)S(1)}, u32[]{:S(2)}, u32[]{:S(2)}) collective-permute-start(bf16[1024,128]{1,0:T(8,128)(2,1)S(1)} %get-tuple-element.167), channel_id=1, source_target_pairs={{0,2},{1,3},{2,0},{3,1},{4,6},{5,7},{6,4},{7,5},{8,10},{9,11},{10,... | collective-permute-start | bytes 786440 | tf_op jit(solution)/shard_map/ppermute | solution.py:438
  40.3 1.6 %join2.1 = (f32[768,256]{1,0:T(8,128)S(1)}, bf16[768,256]{1,0:T(8,128)(2,1)S(1)}, bf16[256,256]{1,0:T(8,128)(2,1)S(1)}, bf16[256,256]{1,0:T(8,128)(2,1)S(1)}, bf...) custom-call(f32[1024,128]{1,0:T(8,128)S(1)} %get-tuple-element.150.r, ...), custom_call_target="tpu_custom_call" | custom-call | flops 536870912 | bytes 4000000 | tf_op jit(solution)/shard_map/join2/pallas_call | solution.py:32
  41.9 1.3 %collective-permute-start.10 = (bf16[128,256]{1,0:T(8,128)(2,1)S(1)}, bf16[128,256]{1,0:T(8,128)(2,1)S(1)}, u32[]{:S(2)}, u32[]{:S(2)}) collective-permute-start(bf16[128,256]{1,0:T(8,128)(2,1)S(1)} %get-tuple-element.163), channel_id=1, source_target_pairs={{4,0},{8,4},{12,8},{5,1},{9,5},{13,9},{6,2},{10,6},{14,10},{7,3},{... | collective-permute-start | bytes 196616 | tf_op jit(solution)/shard_map/ppermute | solution.py:466
  43.8 2.4 %back1.1 = (f32[768,256]{1,0:T(8,128)S(1)}, f32[2048,128]{1,0:T(8,128)S(1)}) custom-call(bf16[768,256]{1,0:T(8,128)(2,1)S(1)} %get-tuple-element.153.refs_0_.refs_1_, bf16[768,256]{1,0:T(8,128)(2,1)S(1)} %get-tuple-element.153.refs_0_.refs_1_, bf16[768,768]{1,0:T(8,128)(2,1)S(1)} %get-tuple-element.137.refs_1_.refs_2_, ...), custom_call_target="tpu_custom_call" | custom-call | flops 2717908992 | bytes 4000000 | tf_op jit(solution)/shard_map/back1/pallas_call | solution.py:32
  46.2 1.9 %collective-permute-done.10.refs_1_.refs_10_ = bf16[128,256]{1,0:T(8,128)(2,1)S(1)} collective-permute-done((bf16[128,256]{1,0:T(8,128)(2,1)S(1)}, bf16[128,256]{1,0:T(8,128)(2,1)S(1)}, u32[]{:S(2)}, u32[]{:S(2)}) %collective-permute-start.10) | collective-permute-done | bytes 65568 | tf_op jit(solution)/shard_map/ppermute | solution.py:466
  48.3 1.6 %collective-permute-start.14 = (bf16[1024,128]{1,0:T(8,128)(2,1)S(1)}, bf16[1024,128]{1,0:T(8,128)(2,1)S(1)}, u32[]{:S(2)}, u32[]{:S(2)}) collective-permute-start(bf16[1024,128]{1,0:T(8,128)(2,1)S(1)} %get-tuple-element.184), channel_id=1, source_target_pairs={{0,2},{1,3},{2,0},{3,1},{4,6},{5,7},{6,4},{7,5},{8,10},{9,11},{10,... | collective-permute-start | bytes 786440 | tf_op jit(solution)/shard_map/ppermute | solution.py:438
  50.0 1.6 %collective-permute-start.13 = (bf16[512,128]{1,0:T(8,128)(2,1)S(1)}, bf16[512,128]{1,0:T(8,128)(2,1)S(1)}, u32[]{:S(2)}, u32[]{:S(2)}) collective-permute-start(bf16[512,128]{1,0:T(8,128)(2,1)S(1)} %get-tuple-element.180), channel_id=1, source_target_pairs={{0,4},{1,5},{2,6},{3,7},{4,0},{5,1},{6,2},{7,3},{8,12},{9,13},{10,... | collective-permute-start | bytes 393224 | tf_op jit(solution)/shard_map/ppermute | solution.py:438
  51.5 1.6 %join1.1 = (f32[768,256]{1,0:T(8,128)S(1)}, bf16[768,256]{1,0:T(8,128)(2,1)S(1)}, bf16[256,256]{1,0:T(8,128)(2,1)S(1)}, bf16[256,256]{1,0:T(8,128)(2,1)S(1)}, bf...) custom-call(f32[512,128]{1,0:T(8,128)S(1)} %get-tuple-element.168.re, ...), custom_call_target="tpu_custom_call" | custom-call | flops 536870912 | bytes 4000000 | tf_op jit(solution)/shard_map/join1/pallas_call | solution.py:32
  53.1 2.4 %back0.1 = (f32[768,256]{1,0:T(8,128)S(1)}, f32[2048,128]{1,0:T(8,128)S(1)}) custom-call(bf16[768,256]{1,0:T(8,128)(2,1)S(1)} %get-tuple-element.170.refs_0_.refs_1_, bf16[768,256]{1,0:T(8,128)(2,1)S(1)} %get-tuple-element.170.refs_0_.refs_1_, bf16[768,768]{1,0:T(8,128)(2,1)S(1)} %get-tuple-element.137.refs_1_.refs_2_, ...), custom_call_target="tpu_custom_call" | custom-call | flops 2717908992 | bytes 4000000 | tf_op jit(solution)/shard_map/back0/pallas_call | solution.py:32
  56.7 3.3 %collective-permute-start.16 = (bf16[512,128]{1,0:T(8,128)(2,1)S(1)}, bf16[512,128]{1,0:T(8,128)(2,1)S(1)}, u32[]{:S(2)}, u32[]{:S(2)}) collective-permute-start(bf16[512,128]{1,0:T(8,128)(2,1)S(1)} %get-tuple-element.188), channel_id=1, source_target_pairs={{0,8},{1,9},{2,10},{3,11},{4,12},{5,13},{6,14},{7,15},{8,0},{9,1},... | collective-permute-start | bytes 393224 | tf_op jit(solution)/shard_map/ppermute | solution.py:438
  62.1 1.3 %collective-permute-start.18 = (bf16[512,128]{1,0:T(8,128)(2,1)S(1)}, bf16[512,128]{1,0:T(8,128)(2,1)S(1)}, u32[]{:S(2)}, u32[]{:S(2)}) collective-permute-start(bf16[512,128]{1,0:T(8,128)(2,1)S(1)} %get-tuple-element.192), channel_id=1, source_target_pairs={{0,4},{1,5},{2,6},{3,7},{4,0},{5,1},{6,2},{7,3},{8,12},{9,13},{10,... | collective-permute-start | bytes 393224 | tf_op jit(solution)/shard_map/ppermute | solution.py:438
  64.6 3.7 %collective-permute-done.17.refs_2_ = bf16[512,128]{1,0:T(8,128)(2,1)S(1)} collective-permute-done((bf16[512,128]{1,0:T(8,128)(2,1)S(1)}, bf16[512,128]{1,0:T(8,128)(2,1)S(1)}, u32[]{:S(2)}, u32[]{:S(2)}) %collective-permute-start.17) | collective-permute-done | bytes 131104 | tf_op jit(solution)/shard_map/ppermute | solution.py:438
  68.4 3.9 %collective-permute-done.18.refs_2_ = bf16[512,128]{1,0:T(8,128)(2,1)S(1)} collective-permute-done((bf16[512,128]{1,0:T(8,128)(2,1)S(1)}, bf16[512,128]{1,0:T(8,128)(2,1)S(1)}, u32[]{:S(2)}, u32[]{:S(2)}) %collective-permute-start.18) | collective-permute-done | bytes 131104 | tf_op jit(solution)/shard_map/ppermute | solution.py:438
  72.5 1.4 %collective-permute-done.19.refs_2_ = bf16[512,128]{1,0:T(8,128)(2,1)S(1)} collective-permute-done((bf16[512,128]{1,0:T(8,128)(2,1)S(1)}, bf16[512,128]{1,0:T(8,128)(2,1)S(1)}, u32[]{:S(2)}, u32[]{:S(2)}) %collective-permute-start.19) | collective-permute-done | bytes 131104 | tf_op jit(solution)/shard_map/ppermute | solution.py:438
  76.5 2.5 %collective-permute-done.21.refs_2_ = bf16[512,128]{1,0:T(8,128)(2,1)S(1)} collective-permute-done((bf16[512,128]{1,0:T(8,128)(2,1)S(1)}, bf16[512,128]{1,0:T(8,128)(2,1)S(1)}, u32[]{:S(2)}, u32[]{:S(2)}) %collective-permute-start.21) | collective-permute-done | bytes 131104 | tf_op jit(solution)/shard_map/ppermute | solution.py:438
  79.3 1.3 %collective-permute-start.23 = (bf16[128,256]{1,0:T(8,128)(2,1)S(1)}, bf16[128,256]{1,0:T(8,128)(2,1)S(1)}, u32[]{:S(2)}, u32[]{:S(2)}) collective-permute-start(bf16[128,256]{1,0:T(8,128)(2,1)S(1)} %get-tuple-element.202), channel_id=1, source_target_pairs={{4,0},{8,4},{12,8},{5,1},{9,5},{13,9},{6,2},{10,6},{14,10},{7,3},{... | collective-permute-start | bytes 196616 | tf_op jit(solution)/shard_map/ppermute | solution.py:466
  83.1 2.3 %collective-permute-done.23.refs_1_.refs_4_ = bf16[128,256]{1,0:T(8,128)(2,1)S(1)} collective-permute-done((bf16[128,256]{1,0:T(8,128)(2,1)S(1)}, bf16[128,256]{1,0:T(8,128)(2,1)S(1)}, u32[]{:S(2)}, u32[]{:S(2)}) %collective-permute-start.23) | collective-permute-done | bytes 65568 | tf_op jit(solution)/shard_map/ppermute | solution.py:466
  85.5 1.1 %collective-permute-start.28 = (bf16[1024,128]{1,0:T(8,128)(2,1)S(1)}, bf16[1024,128]{1,0:T(8,128)(2,1)S(1)}, u32[]{:S(2)}, u32[]{:S(2)}) collective-permute-start(bf16[1024,128]{1,0:T(8,128)(2,1)S(1)} %get-tuple-element.220), channel_id=1, source_target_pairs={{0,2},{1,3},{2,0},{3,1},{4,6},{5,7},{6,4},{7,5},{8,10},{9,11},{10,... | collective-permute-start | bytes 786440 | tf_op jit(solution)/shard_map/ppermute | solution.py:438
  86.6 1.1 %join0.1 = (f32[768,256]{1,0:T(8,128)}, f32[8,128]{1,0:T(8,128)S(1)}) custom-call(bf16[1024,128]{1,0:T(8,128)(2,1)S(1)} %get-tuple-element.206.refs_0_.refs_3_, f32[768,256]{1,0:T(8,128)S(1)} %get-tuple-element.207.refs_1_, f32[768,256]{1,0:T(8,128)S(1)} %get-tuple-element.179.refs_0_.refs_2_, bf16[768,256]{1,0:T(8,128)(2,1)S(1)} %get-tuple-element.152.refs_3_, ...), custom_call_target="tpu_custom_call" | custom-call | flops 100663296 | bytes 4000000 | tf_op jit(solution)/shard_map/join0/pallas_call | solution.py:32
  88.8 1.9 %collective-permute-done.27.refs_4_ = bf16[1024,128]{1,0:T(8,128)(2,1)S(1)} collective-permute-done((bf16[1024,128]{1,0:T(8,128)(2,1)S(1)}, bf16[1024,128]{1,0:T(8,128)(2,1)S(1)}, u32[]{:S(2)}, u32[]{:S(2)}) %collective-permute-start.27) | collective-permute-done | bytes 262176 | tf_op jit(solution)/shard_map/ppermute | solution.py:438
  93.5 1.4 %write0.3 = (f32[3,256,512]{2,1,0:T(8,128)}, f32[3,512,256]{2,1,0:T(8,128)}, f32[8,128]{1,0:T(8,128)}) custom-call(f32[3,256,512]{2,1,0:T(8,128)} %get-tuple-element.217.refs_0_, f32[3,512,256]{2,1,0:T(8,128)} %get-tuple-element.218.refs_1_, f32[8,128]{1,0:T(8,128)S(1)} %get-tuple-element.219.refs_2_, ...), custom_call_target="tpu_custom_call", output_to_operand_aliasing={{0}: (0, {}), {1}: (1, {})} | custom-call | flops 1 | bytes 1 | tf_op jit(solution)/shard_map/write0/pallas_call | solution.py:627
  (76 shorter events, 26.3 us)
Async XLA Ops:
  0.6 8.8 %copy-start = (bf16[3,256,512]{2,1,0:T(8,128)(2,1)S(1)}, bf16[3,256,512]{2,1,0:T(8,128)(2,1)}, u32[]{:S(2)}) copy-start(bf16[3,256,512]{2,1,0:T(8,128)(2,1)} %refs_7_.5) | copy-start | bytes 2359300
  0.6 8.8 %copy-start.1 = (bf16[3,512,256]{2,1,0:T(8,128)(2,1)S(1)}, bf16[3,512,256]{2,1,0:T(8,128)(2,1)}, u32[]{:S(2)}) copy-start(bf16[3,512,256]{2,1,0:T(8,128)(2,1)} %refs_9_.3) | copy-start | bytes 2359300
  0.7 7.9 %collective-permute-start.1 = (bf16[3,256,512]{2,1,0:T(8,128)(2,1)}, bf16[3,256,512]{2,1,0:T(8,128)(2,1)S(1)}, u32[]{:S(2)}, u32[]{:S(2)}) collective-permute-start(bf16[3,256,512]{2,1,0:T(8,128)(2,1)} %refs_7_.5), channel_id=1, source_target_pairs={{0,1},{1,0},{2,3},{3,2},{4,5},{5,4},{6,7},{7,6},{8,9},{9,8},{10,11... | collective-permute-start | bytes 2359304 | tf_op jit(solution)/shard_map/ppermute | solution.py:425
  1.2 7.4 %collective-permute-start.2 = (bf16[3,512,256]{2,1,0:T(8,128)(2,1)}, bf16[3,512,256]{2,1,0:T(8,128)(2,1)S(1)}, u32[]{:S(2)}, u32[]{:S(2)}) collective-permute-start(bf16[3,512,256]{2,1,0:T(8,128)(2,1)} %refs_9_.3), channel_id=1, source_target_pairs={{0,1},{1,0},{2,3},{3,2},{4,5},{5,4},{6,7},{7,6},{8,9},{9,8},{10,11... | collective-permute-start | bytes 2359304 | tf_op jit(solution)/shard_map/ppermute | solution.py:425
  3.6 8.5 %collective-permute-start = (bf16[128,256]{1,0:T(8,128)(2,1)S(1)}, bf16[128,256]{1,0:T(8,128)(2,1)S(1)}, u32[]{:S(2)}, u32[]{:S(2)}) collective-permute-start(bf16[128,256]{1,0:T(8,128)(2,1)S(1)} %get-tuple-element.114), channel_id=1, source_target_pairs={{0,4},{1,3},{2,6},{3,1},{4,8},{5,7},{6,10},{7,5},{8,12},{9,11},{10... | collective-permute-start | bytes 196616 | tf_op jit(solution)/shard_map/ppermute | solution.py:438
  12.1 1.3 %collective-permute-start.3 = (bf16[128,256]{1,0:T(8,128)(2,1)S(1)}, bf16[128,256]{1,0:T(8,128)(2,1)S(1)}, u32[]{:S(2)}, u32[]{:S(2)}) collective-permute-start(bf16[128,256]{1,0:T(8,128)(2,1)S(1)} %collective-permute-done.refs_7_.refs_12_), channel_id=1, source_target_pairs={{0,1},{1,0},{2,3},{3,2},{4,5},{5,4},{6,7},{7,6},{8,9},{9,8},{10,11... | collective-permute-start | bytes 196616 | tf_op jit(solution)/shard_map/ppermute | solution.py:425
  14.5 5.4 %collective-permute-start.4 = (bf16[128,256]{1,0:T(8,128)(2,1)S(1)}, bf16[128,256]{1,0:T(8,128)(2,1)S(1)}, u32[]{:S(2)}, u32[]{:S(2)}) collective-permute-start(bf16[128,256]{1,0:T(8,128)(2,1)S(1)} %get-tuple-element.124), channel_id=1, source_target_pairs={{0,4},{1,3},{2,6},{3,1},{4,8},{5,7},{6,10},{7,5},{8,12},{9,11},{10... | collective-permute-start | bytes 196616 | tf_op jit(solution)/shard_map/ppermute | solution.py:438
  19.9 1.3 %collective-permute-start.5 = (bf16[128,256]{1,0:T(8,128)(2,1)S(1)}, bf16[128,256]{1,0:T(8,128)(2,1)S(1)}, u32[]{:S(2)}, u32[]{:S(2)}) collective-permute-start(bf16[128,256]{1,0:T(8,128)(2,1)S(1)} %collective-permute-done.4.refs_7_.refs_12_), channel_id=1, source_target_pairs={{0,1},{1,0},{2,3},{3,2},{4,5},{5,4},{6,7},{7,6},{8,9},{9,8},{10,11... | collective-permute-start | bytes 196616 | tf_op jit(solution)/shard_map/ppermute | solution.py:425
  22.2 6.2 %collective-permute-start.6 = (bf16[128,256]{1,0:T(8,128)(2,1)S(1)}, bf16[128,256]{1,0:T(8,128)(2,1)S(1)}, u32[]{:S(2)}, u32[]{:S(2)}) collective-permute-start(bf16[128,256]{1,0:T(8,128)(2,1)S(1)} %get-tuple-element.130), channel_id=1, source_target_pairs={{0,4},{1,3},{2,6},{3,1},{4,8},{5,7},{6,10},{7,5},{8,12},{9,11},{10... | collective-permute-start | bytes 196616 | tf_op jit(solution)/shard_map/ppermute | solution.py:438
  28.4 1.3 %copy-start.2 = (f32[768,256]{1,0:T(8,128)S(1)}, f32[768,256]{1,0:T(8,128)}, u32[]{:S(2)}) copy-start(f32[768,256]{1,0:T(8,128)} %refs_4_.5) | copy-start | bytes 2359300
  28.4 1.3 %collective-permute-start.7 = (bf16[128,256]{1,0:T(8,128)(2,1)S(1)}, bf16[128,256]{1,0:T(8,128)(2,1)S(1)}, u32[]{:S(2)}, u32[]{:S(2)}) collective-permute-start(bf16[128,256]{1,0:T(8,128)(2,1)S(1)} %collective-permute-done.6.refs_7_.refs_9_), channel_id=1, source_target_pairs={{0,1},{1,0},{2,3},{3,2},{4,5},{5,4},{6,7},{7,6},{8,9},{9,8},{10,11... | collective-permute-start | bytes 196616 | tf_op jit(solution)/shard_map/ppermute | solution.py:425
  31.9 6.8 %collective-permute-start.8 = (bf16[128,256]{1,0:T(8,128)(2,1)S(1)}, bf16[128,256]{1,0:T(8,128)(2,1)S(1)}, u32[]{:S(2)}, u32[]{:S(2)}) collective-permute-start(bf16[128,256]{1,0:T(8,128)(2,1)S(1)} %get-tuple-element.147), channel_id=1, source_target_pairs={{4,0},{8,4},{12,8},{5,1},{9,5},{13,9},{6,2},{10,6},{14,10},{7,3},{... | collective-permute-start | bytes 196616 | tf_op jit(solution)/shard_map/ppermute | solution.py:466
  33.2 5.5 %collective-permute-start.9 = (bf16[128,256]{1,0:T(8,128)(2,1)S(1)}, bf16[128,256]{1,0:T(8,128)(2,1)S(1)}, u32[]{:S(2)}, u32[]{:S(2)}) collective-permute-start(bf16[128,256]{1,0:T(8,128)(2,1)S(1)} %get-tuple-element.148), channel_id=1, source_target_pairs={{0,2},{2,0},{1,3},{3,1},{4,6},{6,4},{5,7},{7,5},{8,10},{10,8},{9,1... | collective-permute-start | bytes 196616 | tf_op jit(solution)/shard_map/ppermute | solution.py:425
  38.8 11.1 %collective-permute-start.12 = (bf16[1024,128]{1,0:T(8,128)(2,1)S(1)}, bf16[1024,128]{1,0:T(8,128)(2,1)S(1)}, u32[]{:S(2)}, u32[]{:S(2)}) collective-permute-start(bf16[1024,128]{1,0:T(8,128)(2,1)S(1)} %get-tuple-element.167), channel_id=1, source_target_pairs={{0,2},{1,3},{2,0},{3,1},{4,6},{5,7},{6,4},{7,5},{8,10},{9,11},{10,... | collective-permute-start | bytes 786440 | tf_op jit(solution)/shard_map/ppermute | solution.py:438
  41.9 6.2 %collective-permute-start.10 = (bf16[128,256]{1,0:T(8,128)(2,1)S(1)}, bf16[128,256]{1,0:T(8,128)(2,1)S(1)}, u32[]{:S(2)}, u32[]{:S(2)}) collective-permute-start(bf16[128,256]{1,0:T(8,128)(2,1)S(1)} %get-tuple-element.163), channel_id=1, source_target_pairs={{4,0},{8,4},{12,8},{5,1},{9,5},{13,9},{6,2},{10,6},{14,10},{7,3},{... | collective-permute-start | bytes 196616 | tf_op jit(solution)/shard_map/ppermute | solution.py:466
  43.2 5.0 %collective-permute-start.11 = (bf16[128,256]{1,0:T(8,128)(2,1)S(1)}, bf16[128,256]{1,0:T(8,128)(2,1)S(1)}, u32[]{:S(2)}, u32[]{:S(2)}) collective-permute-start(bf16[128,256]{1,0:T(8,128)(2,1)S(1)} %get-tuple-element.164), channel_id=1, source_target_pairs={{0,2},{2,0},{1,3},{3,1},{4,6},{6,4},{5,7},{7,5},{8,10},{10,8},{9,1... | collective-permute-start | bytes 196616 | tf_op jit(solution)/shard_map/ppermute | solution.py:425
  48.3 11.7 %collective-permute-start.14 = (bf16[1024,128]{1,0:T(8,128)(2,1)S(1)}, bf16[1024,128]{1,0:T(8,128)(2,1)S(1)}, u32[]{:S(2)}, u32[]{:S(2)}) collective-permute-start(bf16[1024,128]{1,0:T(8,128)(2,1)S(1)} %get-tuple-element.184), channel_id=1, source_target_pairs={{0,2},{1,3},{2,0},{3,1},{4,6},{5,7},{6,4},{7,5},{8,10},{9,11},{10,... | collective-permute-start | bytes 786440 | tf_op jit(solution)/shard_map/ppermute | solution.py:438
  50.0 5.6 %collective-permute-start.13 = (bf16[512,128]{1,0:T(8,128)(2,1)S(1)}, bf16[512,128]{1,0:T(8,128)(2,1)S(1)}, u32[]{:S(2)}, u32[]{:S(2)}) collective-permute-start(bf16[512,128]{1,0:T(8,128)(2,1)S(1)} %get-tuple-element.180), channel_id=1, source_target_pairs={{0,4},{1,5},{2,6},{3,7},{4,0},{5,1},{6,2},{7,3},{8,12},{9,13},{10,... | collective-permute-start | bytes 393224 | tf_op jit(solution)/shard_map/ppermute | solution.py:438
  55.6 6.4 %collective-permute-start.15 = (bf16[1024,128]{1,0:T(8,128)(2,1)S(1)}, bf16[1024,128]{1,0:T(8,128)(2,1)S(1)}, u32[]{:S(2)}, u32[]{:S(2)}) collective-permute-start(bf16[1024,128]{1,0:T(8,128)(2,1)S(1)} %get-tuple-element.186), channel_id=1, source_target_pairs={{0,2},{1,3},{2,0},{3,1},{4,6},{5,7},{6,4},{7,5},{8,10},{9,11},{10,... | collective-permute-start | bytes 786440 | tf_op jit(solution)/shard_map/ppermute | solution.py:438
  56.7 7.8 %collective-permute-start.16 = (bf16[512,128]{1,0:T(8,128)(2,1)S(1)}, bf16[512,128]{1,0:T(8,128)(2,1)S(1)}, u32[]{:S(2)}, u32[]{:S(2)}) collective-permute-start(bf16[512,128]{1,0:T(8,128)(2,1)S(1)} %get-tuple-element.188), channel_id=1, source_target_pairs={{0,8},{1,9},{2,10},{3,11},{4,12},{5,13},{6,14},{7,15},{8,0},{9,1},... | collective-permute-start | bytes 393224 | tf_op jit(solution)/shard_map/ppermute | solution.py:438
  60.1 8.2 %collective-permute-start.17 = (bf16[512,128]{1,0:T(8,128)(2,1)S(1)}, bf16[512,128]{1,0:T(8,128)(2,1)S(1)}, u32[]{:S(2)}, u32[]{:S(2)}) collective-permute-start(bf16[512,128]{1,0:T(8,128)(2,1)S(1)} %get-tuple-element.190), channel_id=1, source_target_pairs={{0,4},{1,5},{2,6},{3,7},{4,0},{5,1},{6,2},{7,3},{8,12},{9,13},{10,... | collective-permute-start | bytes 393224 | tf_op jit(solution)/shard_map/ppermute | solution.py:438
  62.1 10.2 %collective-permute-start.18 = (bf16[512,128]{1,0:T(8,128)(2,1)S(1)}, bf16[512,128]{1,0:T(8,128)(2,1)S(1)}, u32[]{:S(2)}, u32[]{:S(2)}) collective-permute-start(bf16[512,128]{1,0:T(8,128)(2,1)S(1)} %get-tuple-element.192), channel_id=1, source_target_pairs={{0,4},{1,5},{2,6},{3,7},{4,0},{5,1},{6,2},{7,3},{8,12},{9,13},{10,... | collective-permute-start | bytes 393224 | tf_op jit(solution)/shard_map/ppermute | solution.py:438
  64.5 9.4 %collective-permute-start.19 = (bf16[512,128]{1,0:T(8,128)(2,1)S(1)}, bf16[512,128]{1,0:T(8,128)(2,1)S(1)}, u32[]{:S(2)}, u32[]{:S(2)}) collective-permute-start(bf16[512,128]{1,0:T(8,128)(2,1)S(1)} %get-tuple-element.194), channel_id=1, source_target_pairs={{0,4},{1,5},{2,6},{3,7},{4,0},{5,1},{6,2},{7,3},{8,12},{9,13},{10,... | collective-permute-start | bytes 393224 | tf_op jit(solution)/shard_map/ppermute | solution.py:438
  68.4 7.8 %collective-permute-start.20 = (bf16[512,128]{1,0:T(8,128)(2,1)S(1)}, bf16[512,128]{1,0:T(8,128)(2,1)S(1)}, u32[]{:S(2)}, u32[]{:S(2)}) collective-permute-start(bf16[512,128]{1,0:T(8,128)(2,1)S(1)} %get-tuple-element.196), channel_id=1, source_target_pairs={{0,8},{1,9},{2,10},{3,11},{4,12},{5,13},{6,14},{7,15},{8,0},{9,1},... | collective-permute-start | bytes 393224 | tf_op jit(solution)/shard_map/ppermute | solution.py:438
  72.4 6.6 %collective-permute-start.21 = (bf16[512,128]{1,0:T(8,128)(2,1)S(1)}, bf16[512,128]{1,0:T(8,128)(2,1)S(1)}, u32[]{:S(2)}, u32[]{:S(2)}) collective-permute-start(bf16[512,128]{1,0:T(8,128)(2,1)S(1)} %get-tuple-element.198), channel_id=1, source_target_pairs={{0,8},{1,9},{2,10},{3,11},{4,12},{5,13},{6,14},{7,15},{8,0},{9,1},... | collective-permute-start | bytes 393224 | tf_op jit(solution)/shard_map/ppermute | solution.py:438
  73.9 11.5 %collective-permute-start.25 = (bf16[1024,128]{1,0:T(8,128)(2,1)S(1)}, bf16[1024,128]{1,0:T(8,128)(2,1)S(1)}, u32[]{:S(2)}, u32[]{:S(2)}) collective-permute-start(bf16[1024,128]{1,0:T(8,128)(2,1)S(1)} %get-tuple-element.204), channel_id=1, source_target_pairs={{0,2},{1,3},{2,0},{3,1},{4,6},{5,7},{6,4},{7,5},{8,10},{9,11},{10,... | collective-permute-start | bytes 786440 | tf_op jit(solution)/shard_map/ppermute | solution.py:438
  76.2 5.9 %collective-permute-start.22 = (bf16[512,128]{1,0:T(8,128)(2,1)S(1)}, bf16[512,128]{1,0:T(8,128)(2,1)S(1)}, u32[]{:S(2)}, u32[]{:S(2)}) collective-permute-start(bf16[512,128]{1,0:T(8,128)(2,1)S(1)} %get-tuple-element.200), channel_id=1, source_target_pairs={{0,4},{1,5},{2,6},{3,7},{4,0},{5,1},{6,2},{7,3},{8,12},{9,13},{10,... | collective-permute-start | bytes 393224 | tf_op jit(solution)/shard_map/ppermute | solution.py:438
  79.1 6.3 %collective-permute-start.26 = (bf16[512,128]{1,0:T(8,128)(2,1)S(1)}, bf16[512,128]{1,0:T(8,128)(2,1)S(1)}, u32[]{:S(2)}, u32[]{:S(2)}) collective-permute-start(bf16[512,128]{1,0:T(8,128)(2,1)S(1)} %get-tuple-element.205), channel_id=1, source_target_pairs={{0,4},{1,5},{2,6},{3,7},{4,0},{5,1},{6,2},{7,3},{8,12},{9,13},{10,... | collective-permute-start | bytes 393224 | tf_op jit(solution)/shard_map/ppermute | solution.py:438
  79.3 6.1 %collective-permute-start.23 = (bf16[128,256]{1,0:T(8,128)(2,1)S(1)}, bf16[128,256]{1,0:T(8,128)(2,1)S(1)}, u32[]{:S(2)}, u32[]{:S(2)}) collective-permute-start(bf16[128,256]{1,0:T(8,128)(2,1)S(1)} %get-tuple-element.202), channel_id=1, source_target_pairs={{4,0},{8,4},{12,8},{5,1},{9,5},{13,9},{6,2},{10,6},{14,10},{7,3},{... | collective-permute-start | bytes 196616 | tf_op jit(solution)/shard_map/ppermute | solution.py:466
  80.5 4.9 %collective-permute-start.24 = (bf16[128,256]{1,0:T(8,128)(2,1)S(1)}, bf16[128,256]{1,0:T(8,128)(2,1)S(1)}, u32[]{:S(2)}, u32[]{:S(2)}) collective-permute-start(bf16[128,256]{1,0:T(8,128)(2,1)S(1)} %get-tuple-element.203), channel_id=1, source_target_pairs={{0,2},{2,0},{1,3},{3,1},{4,6},{6,4},{5,7},{7,5},{8,10},{10,8},{9,1... | collective-permute-start | bytes 196616 | tf_op jit(solution)/shard_map/ppermute | solution.py:425
  82.1 8.6 %collective-permute-start.27 = (bf16[1024,128]{1,0:T(8,128)(2,1)S(1)}, bf16[1024,128]{1,0:T(8,128)(2,1)S(1)}, u32[]{:S(2)}, u32[]{:S(2)}) collective-permute-start(bf16[1024,128]{1,0:T(8,128)(2,1)S(1)} %get-tuple-element.213), channel_id=1, source_target_pairs={{0,2},{1,3},{2,0},{3,1},{4,6},{5,7},{6,4},{7,5},{8,10},{9,11},{10,... | collective-permute-start | bytes 786440 | tf_op jit(solution)/shard_map/ppermute | solution.py:438
  85.5 8.0 %collective-permute-start.28 = (bf16[1024,128]{1,0:T(8,128)(2,1)S(1)}, bf16[1024,128]{1,0:T(8,128)(2,1)S(1)}, u32[]{:S(2)}, u32[]{:S(2)}) collective-permute-start(bf16[1024,128]{1,0:T(8,128)(2,1)S(1)} %get-tuple-element.220), channel_id=1, source_target_pairs={{0,2},{1,3},{2,0},{3,1},{4,6},{5,7},{6,4},{7,5},{8,10},{9,11},{10,... | collective-permute-start | bytes 786440 | tf_op jit(solution)/shard_map/ppermute | solution.py:438
  (3 other events, 3.3 us)

commit v22 on v19

--- a/solution.py
+++ b/solution.py
@@ -664,7 +664,10 @@
             outs = join(layer, state, at)
             at = outs[1:2]
     while sums[0].done < count:
-        for layer in reversed(range(layers)):
+        turn = list(reversed(range(layers)))
+        if sums[0].done == 1 and layers > 2:
+            turn = [*turn[1:-1], turn[0], 0]
+        for layer in turn:
             if sums[layer].done < count:
                 if layer == 0 and sums[0].done == count - 1:
                     at = at + returned[0] + [sums[above].got[0] for above in range(2, layers)]

time: 95.9 us -> 95.8 us (level)
  no operation moved by 1% of the time
where the time goes in v22:
time: 95.8 us; the launch traced here: 95.5 us
  starting transfers between devices  36.2 us (38%)
  Pallas kernels  31.3 us (33%)
  waiting for transfers between devices  24.9 us (26%)
  local copies, waits for them, and re-layouts  1.2 us (1%)
  between operations  1.18 us (1%)
    ppermute x18, starting transfers between devices, over_mesh(): return lax.ppermute(x, ('chain', 'basin', 'feat'), perm)  28.7 us
    pallas_call x33, Pallas kernels, call(): pl.pallas_call(lambda *refs: body(*refs[skipped:]), out_shape=[jax.ShapeD...  26.9 us
    ppermute x18, waiting for transfers between devices, over_mesh(): return lax.ppermute(x, ('chain', 'basin', 'feat'), perm)  17.7 us
    ppermute x3, waiting for transfers between devices, backward(): up = lax.ppermute(grads[0], 'chain', [(c, c - 1) for c in range(1, chain)])  6.02 us
    pallas_call x4, Pallas kernels, write(): pl.pallas_call(functools.partial(write_kernel, layer, sums[layer].stages[...  4.43 us
    ppermute x3, starting transfers between devices, backward(): up = lax.ppermute(grads[0], 'chain', [(c, c - 1) for c in range(1, chain)])  3.86 us
    ppermute x8, starting transfers between devices, around(): return lax.ppermute(x, axis, [(i, (i + distance) % n) for i in range(n)])  3.58 us
  transfers between devices with their start and end apart: 29, of which 20 were waited for; matrix products, arithmetic and copies ran while one was open for 1% of the time, Pallas kernels for 27%

profile of v22, /device:TPU:0, one launch (start us, length us, event | category | flops | bytes accessed | tf_op | source)
XLA Modules:
  0.0 95.5 jit_solution(15159231590495331380)
XLA Ops:
  3.6 4.9 %collective-permute-start = (bf16[128,256]{1,0:T(8,128)(2,1)S(1)}, bf16[128,256]{1,0:T(8,128)(2,1)S(1)}, u32[]{:S(2)}, u32[]{:S(2)}) collective-permute-start(bf16[128,256]{1,0:T(8,128)(2,1)S(1)} %get-tuple-element.114), channel_id=1, source_target_pairs={{0,4},{1,3},{2,6},{3,1},{4,8},{5,7},{6,10},{7,5},{8,12},{9,11},{10... | collective-permute-start | bytes 196616 | tf_op jit(solution)/shard_map/ppermute | solution.py:438
  10.5 1.6 %adjacency.1 = (bf16[768,768]{1,0:T(8,128)(2,1)S(1)}, bf16[768,768]{1,0:T(8,128)(2,1)S(1)}, bf16[768,256]{1,0:T(8,128)(2,1)S(1)}, bf16[256,768]{1,0:T(8,128)(2,1)S(1)}) custom-call(s32[4,6]{1,0:T(4,128)S(1)} %bitcast.4, bf16[6,4,128,128]{3,2,1,0:T(8,128)(2,1)S(1)} %copy-done.3, bf16[128,768]{1,0:T(8,128)(2,1)S(1)} %get-tuple-element.115.refs_2_, ...), custom_call_target="tpu_custom_call" | custom-call | flops 150994944 | bytes 4000000 | tf_op jit(solution)/shard_map/adjacency/pallas_call | solution.py:32
  14.5 3.5 %collective-permute-start.4 = (bf16[128,256]{1,0:T(8,128)(2,1)S(1)}, bf16[128,256]{1,0:T(8,128)(2,1)S(1)}, u32[]{:S(2)}, u32[]{:S(2)}) collective-permute-start(bf16[128,256]{1,0:T(8,128)(2,1)S(1)} %get-tuple-element.124), channel_id=1, source_target_pairs={{0,4},{1,3},{2,6},{3,1},{4,8},{5,7},{6,10},{7,5},{8,12},{9,11},{10... | collective-permute-start | bytes 196616 | tf_op jit(solution)/shard_map/ppermute | solution.py:438
  18.0 1.6 %local1.1 = (bf16[768,256]{1,0:T(8,128)(2,1)S(1)}, bf16[768,512]{1,0:T(8,128)(2,1)S(1)}, bf16[768,512]{1,0:T(8,128)(2,1)S(1)}, bf16[512,768]{1,0:T(8,128)(2,1)S(1)}, bf16[256,768]{1,0:T(8,128)(2,1)S(1)}) custom-call(bf16[768,256]{1,0:T(8,128)(2,1)S(1)} %get-tuple-element.125.refs_0_, bf16[3,256,512]{2,1,0:T(8,128)(2,1)S(1)} %copy-done, ...), custom_call_target="tpu_custom_call" | custom-call | flops 805306368 | bytes 4000000 | tf_op jit(solution)/shard_map/local1/pallas_call | solution.py:32
  22.2 4.3 %collective-permute-start.6 = (bf16[128,256]{1,0:T(8,128)(2,1)S(1)}, bf16[128,256]{1,0:T(8,128)(2,1)S(1)}, u32[]{:S(2)}, u32[]{:S(2)}) collective-permute-start(bf16[128,256]{1,0:T(8,128)(2,1)S(1)} %get-tuple-element.130), channel_id=1, source_target_pairs={{0,4},{1,3},{2,6},{3,1},{4,8},{5,7},{6,10},{7,5},{8,12},{9,11},{10... | collective-permute-start | bytes 196616 | tf_op jit(solution)/shard_map/ppermute | solution.py:438
  26.5 1.6 %local2.1 = (bf16[768,256]{1,0:T(8,128)(2,1)S(1)}, bf16[768,512]{1,0:T(8,128)(2,1)S(1)}, bf16[768,512]{1,0:T(8,128)(2,1)S(1)}, bf16[512,768]{1,0:T(8,128)(2,1)S(1)}, bf16[256,768]{1,0:T(8,128)(2,1)S(1)}) custom-call(bf16[768,256]{1,0:T(8,128)(2,1)S(1)} %get-tuple-element.131.refs_0_, bf16[3,256,512]{2,1,0:T(8,128)(2,1)S(1)} %copy-done, ...), custom_call_target="tpu_custom_call" | custom-call | flops 805306368 | bytes 4000000 | tf_op jit(solution)/shard_map/local2/pallas_call | solution.py:32
  29.6 2.2 %turn.1 = (f32[768,256]{1,0:T(8,128)S(1)}, bf16[768,256]{1,0:T(8,128)(2,1)S(1)}, bf16[256,256]{1,0:T(8,128)(2,1)S(1)}, bf16[256,256]{1,0:T(8,128)(2,1)S(1)}, bf1...) custom-call(f32[768,256]{1,0:T(8,128)S(1)} %get-tuple-element.129.re, ...), custom_call_target="tpu_custom_call" | custom-call | flops 536870912 | bytes 4000000 | tf_op jit(solution)/shard_map/turn/pallas_call | solution.py:32
  31.9 1.3 %collective-permute-start.8 = (bf16[128,256]{1,0:T(8,128)(2,1)S(1)}, bf16[128,256]{1,0:T(8,128)(2,1)S(1)}, u32[]{:S(2)}, u32[]{:S(2)}) collective-permute-start(bf16[128,256]{1,0:T(8,128)(2,1)S(1)} %get-tuple-element.147), channel_id=1, source_target_pairs={{4,0},{8,4},{12,8},{5,1},{9,5},{13,9},{6,2},{10,6},{14,10},{7,3},{... | collective-permute-start | bytes 196616 | tf_op jit(solution)/shard_map/ppermute | solution.py:466
  33.2 1.6 %collective-permute-start.9 = (bf16[128,256]{1,0:T(8,128)(2,1)S(1)}, bf16[128,256]{1,0:T(8,128)(2,1)S(1)}, u32[]{:S(2)}, u32[]{:S(2)}) collective-permute-start(bf16[128,256]{1,0:T(8,128)(2,1)S(1)} %get-tuple-element.148), channel_id=1, source_target_pairs={{0,2},{2,0},{1,3},{3,1},{4,6},{6,4},{5,7},{7,5},{8,10},{10,8},{9,1... | collective-permute-start | bytes 196616 | tf_op jit(solution)/shard_map/ppermute | solution.py:425
  34.8 2.4 %back2.1 = (f32[768,256]{1,0:T(8,128)S(1)}, f32[2048,128]{1,0:T(8,128)S(1)}) custom-call(bf16[768,256]{1,0:T(8,128)(2,1)S(1)} %get-tuple-element.136.refs_0_, bf16[768,768]{1,0:T(8,128)(2,1)S(1)} %get-tuple-element.137.refs_1_.refs_2_, bf16[768,512]{1,0:T(8,128)(2,1)S(1)} %get-tuple-element.138.refs_2_, bf16[768,512]{1,0:T(8,128)(2,1)S(1)} %get-tuple-element.139.refs_3_, ...), custom_call_target="tpu_custom_call" | custom-call | flops 2717908992 | bytes 4000000 | tf_op jit(solution)/shard_map/back2/pallas_call | solution.py:32
  37.2 1.5 %collective-permute-done.8.refs_1_.refs_10_ = bf16[128,256]{1,0:T(8,128)(2,1)S(1)} collective-permute-done((bf16[128,256]{1,0:T(8,128)(2,1)S(1)}, bf16[128,256]{1,0:T(8,128)(2,1)S(1)}, u32[]{:S(2)}, u32[]{:S(2)}) %collective-permute-start.8) | collective-permute-done | bytes 65568 | tf_op jit(solution)/shard_map/ppermute | solution.py:466
  38.8 1.6 %collective-permute-start.12 = (bf16[1024,128]{1,0:T(8,128)(2,1)S(1)}, bf16[1024,128]{1,0:T(8,128)(2,1)S(1)}, u32[]{:S(2)}, u32[]{:S(2)}) collective-permute-start(bf16[1024,128]{1,0:T(8,128)(2,1)S(1)} %get-tuple-element.167), channel_id=1, source_target_pairs={{0,2},{1,3},{2,0},{3,1},{4,6},{5,7},{6,4},{7,5},{8,10},{9,11},{10,... | collective-permute-start | bytes 786440 | tf_op jit(solution)/shard_map/ppermute | solution.py:438
  40.3 1.6 %join2.1 = (f32[768,256]{1,0:T(8,128)S(1)}, bf16[768,256]{1,0:T(8,128)(2,1)S(1)}, bf16[256,256]{1,0:T(8,128)(2,1)S(1)}, bf16[256,256]{1,0:T(8,128)(2,1)S(1)}, bf...) custom-call(f32[1024,128]{1,0:T(8,128)S(1)} %get-tuple-element.150.r, ...), custom_call_target="tpu_custom_call" | custom-call | flops 536870912 | bytes 4000000 | tf_op jit(solution)/shard_map/join2/pallas_call | solution.py:32
  41.9 1.3 %collective-permute-start.10 = (bf16[128,256]{1,0:T(8,128)(2,1)S(1)}, bf16[128,256]{1,0:T(8,128)(2,1)S(1)}, u32[]{:S(2)}, u32[]{:S(2)}) collective-permute-start(bf16[128,256]{1,0:T(8,128)(2,1)S(1)} %get-tuple-element.163), channel_id=1, source_target_pairs={{4,0},{8,4},{12,8},{5,1},{9,5},{13,9},{6,2},{10,6},{14,10},{7,3},{... | collective-permute-start | bytes 196616 | tf_op jit(solution)/shard_map/ppermute | solution.py:466
  43.8 2.4 %back1.1 = (f32[768,256]{1,0:T(8,128)S(1)}, f32[2048,128]{1,0:T(8,128)S(1)}) custom-call(bf16[768,256]{1,0:T(8,128)(2,1)S(1)} %get-tuple-element.153.refs_0_.refs_1_, bf16[768,256]{1,0:T(8,128)(2,1)S(1)} %get-tuple-element.153.refs_0_.refs_1_, bf16[768,768]{1,0:T(8,128)(2,1)S(1)} %get-tuple-element.137.refs_1_.refs_2_, ...), custom_call_target="tpu_custom_call" | custom-call | flops 2717908992 | bytes 4000000 | tf_op jit(solution)/shard_map/back1/pallas_call | solution.py:32
  46.2 1.9 %collective-permute-done.10.refs_1_.refs_10_ = bf16[128,256]{1,0:T(8,128)(2,1)S(1)} collective-permute-done((bf16[128,256]{1,0:T(8,128)(2,1)S(1)}, bf16[128,256]{1,0:T(8,128)(2,1)S(1)}, u32[]{:S(2)}, u32[]{:S(2)}) %collective-permute-start.10) | collective-permute-done | bytes 65568 | tf_op jit(solution)/shard_map/ppermute | solution.py:466
  48.3 1.6 %collective-permute-start.14 = (bf16[1024,128]{1,0:T(8,128)(2,1)S(1)}, bf16[1024,128]{1,0:T(8,128)(2,1)S(1)}, u32[]{:S(2)}, u32[]{:S(2)}) collective-permute-start(bf16[1024,128]{1,0:T(8,128)(2,1)S(1)} %get-tuple-element.183), channel_id=1, source_target_pairs={{0,2},{1,3},{2,0},{3,1},{4,6},{5,7},{6,4},{7,5},{8,10},{9,11},{10,... | collective-permute-start | bytes 786440 | tf_op jit(solution)/shard_map/ppermute | solution.py:438
  50.0 1.6 %collective-permute-start.13 = (bf16[512,128]{1,0:T(8,128)(2,1)S(1)}, bf16[512,128]{1,0:T(8,128)(2,1)S(1)}, u32[]{:S(2)}, u32[]{:S(2)}) collective-permute-start(bf16[512,128]{1,0:T(8,128)(2,1)S(1)} %get-tuple-element.180), channel_id=1, source_target_pairs={{0,4},{1,5},{2,6},{3,7},{4,0},{5,1},{6,2},{7,3},{8,12},{9,13},{10,... | collective-permute-start | bytes 393224 | tf_op jit(solution)/shard_map/ppermute | solution.py:438
  51.5 1.6 %join1.1 = (f32[768,256]{1,0:T(8,128)S(1)}, bf16[768,256]{1,0:T(8,128)(2,1)S(1)}, bf16[256,256]{1,0:T(8,128)(2,1)S(1)}, bf16[256,256]{1,0:T(8,128)(2,1)S(1)}, bf...) custom-call(f32[512,128]{1,0:T(8,128)S(1)} %get-tuple-element.168.re, ...), custom_call_target="tpu_custom_call" | custom-call | flops 536870912 | bytes 4000000 | tf_op jit(solution)/shard_map/join1/pallas_call | solution.py:32
  53.1 2.4 %back0.1 = (f32[768,256]{1,0:T(8,128)S(1)}, f32[2048,128]{1,0:T(8,128)S(1)}) custom-call(bf16[768,256]{1,0:T(8,128)(2,1)S(1)} %get-tuple-element.170.refs_0_.refs_1_, bf16[768,256]{1,0:T(8,128)(2,1)S(1)} %get-tuple-element.170.refs_0_.refs_1_, bf16[768,768]{1,0:T(8,128)(2,1)S(1)} %get-tuple-element.137.refs_1_.refs_2_, ...), custom_call_target="tpu_custom_call" | custom-call | flops 2717908992 | bytes 4000000 | tf_op jit(solution)/shard_map/back0/pallas_call | solution.py:32
  56.8 3.3 %collective-permute-start.16 = (bf16[512,128]{1,0:T(8,128)(2,1)S(1)}, bf16[512,128]{1,0:T(8,128)(2,1)S(1)}, u32[]{:S(2)}, u32[]{:S(2)}) collective-permute-start(bf16[512,128]{1,0:T(8,128)(2,1)S(1)} %get-tuple-element.188), channel_id=1, source_target_pairs={{0,8},{1,9},{2,10},{3,11},{4,12},{5,13},{6,14},{7,15},{8,0},{9,1},... | collective-permute-start | bytes 393224 | tf_op jit(solution)/shard_map/ppermute | solution.py:438
  63.2 2.5 %collective-permute-done.16.refs_2_ = bf16[512,128]{1,0:T(8,128)(2,1)S(1)} collective-permute-done((bf16[512,128]{1,0:T(8,128)(2,1)S(1)}, bf16[512,128]{1,0:T(8,128)(2,1)S(1)}, u32[]{:S(2)}, u32[]{:S(2)}) %collective-permute-start.16) | collective-permute-done | bytes 131104 | tf_op jit(solution)/shard_map/ppermute | solution.py:438
  67.0 1.6 %collective-permute-start.20 = (bf16[512,128]{1,0:T(8,128)(2,1)S(1)}, bf16[512,128]{1,0:T(8,128)(2,1)S(1)}, u32[]{:S(2)}, u32[]{:S(2)}) collective-permute-start(bf16[512,128]{1,0:T(8,128)(2,1)S(1)} %get-tuple-element.196), channel_id=1, source_target_pairs={{0,8},{1,9},{2,10},{3,11},{4,12},{5,13},{6,14},{7,15},{8,0},{9,1},... | collective-permute-start | bytes 393224 | tf_op jit(solution)/shard_map/ppermute | solution.py:438
  68.7 2.0 %collective-permute-done.18.refs_2_ = bf16[512,128]{1,0:T(8,128)(2,1)S(1)} collective-permute-done((bf16[512,128]{1,0:T(8,128)(2,1)S(1)}, bf16[512,128]{1,0:T(8,128)(2,1)S(1)}, u32[]{:S(2)}, u32[]{:S(2)}) %collective-permute-start.18) | collective-permute-done | bytes 131104 | tf_op jit(solution)/shard_map/ppermute | solution.py:438
  71.7 2.0 %collective-permute-done.19.refs_2_ = bf16[512,128]{1,0:T(8,128)(2,1)S(1)} collective-permute-done((bf16[512,128]{1,0:T(8,128)(2,1)S(1)}, bf16[512,128]{1,0:T(8,128)(2,1)S(1)}, u32[]{:S(2)}, u32[]{:S(2)}) %collective-permute-start.19) | collective-permute-done | bytes 131104 | tf_op jit(solution)/shard_map/ppermute | solution.py:438
  73.8 4.3 %collective-permute-done.20.refs_2_ = bf16[512,128]{1,0:T(8,128)(2,1)S(1)} collective-permute-done((bf16[512,128]{1,0:T(8,128)(2,1)S(1)}, bf16[512,128]{1,0:T(8,128)(2,1)S(1)}, u32[]{:S(2)}, u32[]{:S(2)}) %collective-permute-start.20) | collective-permute-done | bytes 131104 | tf_op jit(solution)/shard_map/ppermute | solution.py:438
  78.3 1.3 %collective-permute-done.21.refs_2_ = bf16[512,128]{1,0:T(8,128)(2,1)S(1)} collective-permute-done((bf16[512,128]{1,0:T(8,128)(2,1)S(1)}, bf16[512,128]{1,0:T(8,128)(2,1)S(1)}, u32[]{:S(2)}, u32[]{:S(2)}) %collective-permute-start.21) | collective-permute-done | bytes 131104 | tf_op jit(solution)/shard_map/ppermute | solution.py:438
  80.4 1.3 %collective-permute-start.23 = (bf16[128,256]{1,0:T(8,128)(2,1)S(1)}, bf16[128,256]{1,0:T(8,128)(2,1)S(1)}, u32[]{:S(2)}, u32[]{:S(2)}) collective-permute-start(bf16[128,256]{1,0:T(8,128)(2,1)S(1)} %get-tuple-element.202), channel_id=1, source_target_pairs={{4,0},{8,4},{12,8},{5,1},{9,5},{13,9},{6,2},{10,6},{14,10},{7,3},{... | collective-permute-start | bytes 196616 | tf_op jit(solution)/shard_map/ppermute | solution.py:466
  83.9 2.6 %collective-permute-done.23.refs_1_.refs_4_ = bf16[128,256]{1,0:T(8,128)(2,1)S(1)} collective-permute-done((bf16[128,256]{1,0:T(8,128)(2,1)S(1)}, bf16[128,256]{1,0:T(8,128)(2,1)S(1)}, u32[]{:S(2)}, u32[]{:S(2)}) %collective-permute-start.23) | collective-permute-done | bytes 65568 | tf_op jit(solution)/shard_map/ppermute | solution.py:466
  87.6 1.1 %join0.1 = (f32[768,256]{1,0:T(8,128)}, f32[8,128]{1,0:T(8,128)S(1)}) custom-call(bf16[1024,128]{1,0:T(8,128)(2,1)S(1)} %get-tuple-element.206.refs_0_.refs_3_, f32[768,256]{1,0:T(8,128)S(1)} %get-tuple-element.207.refs_1_, f32[768,256]{1,0:T(8,128)S(1)} %get-tuple-element.179.refs_0_.refs_2_, bf16[768,256]{1,0:T(8,128)(2,1)S(1)} %get-tuple-element.152.refs_3_, ...), custom_call_target="tpu_custom_call" | custom-call | flops 100663296 | bytes 4000000 | tf_op jit(solution)/shard_map/join0/pallas_call | solution.py:32
  89.8 1.3 %collective-permute-done.27.refs_4_ = bf16[1024,128]{1,0:T(8,128)(2,1)S(1)} collective-permute-done((bf16[1024,128]{1,0:T(8,128)(2,1)S(1)}, bf16[1024,128]{1,0:T(8,128)(2,1)S(1)}, u32[]{:S(2)}, u32[]{:S(2)}) %collective-permute-start.27) | collective-permute-done | bytes 262176 | tf_op jit(solution)/shard_map/ppermute | solution.py:438
  93.9 1.4 %write0.3 = (f32[3,256,512]{2,1,0:T(8,128)}, f32[3,512,256]{2,1,0:T(8,128)}, f32[8,128]{1,0:T(8,128)}) custom-call(f32[3,256,512]{2,1,0:T(8,128)} %get-tuple-element.217.refs_0_, f32[3,512,256]{2,1,0:T(8,128)} %get-tuple-element.218.refs_1_, f32[8,128]{1,0:T(8,128)S(1)} %get-tuple-element.219.refs_2_, ...), custom_call_target="tpu_custom_call", output_to_operand_aliasing={{0}: (0, {}), {1}: (1, {})} | custom-call | flops 1 | bytes 1 | tf_op jit(solution)/shard_map/write0/pallas_call | solution.py:627
  (76 shorter events, 27.1 us)
Async XLA Ops:
  0.6 8.8 %copy-start = (bf16[3,256,512]{2,1,0:T(8,128)(2,1)S(1)}, bf16[3,256,512]{2,1,0:T(8,128)(2,1)}, u32[]{:S(2)}) copy-start(bf16[3,256,512]{2,1,0:T(8,128)(2,1)} %refs_7_.5) | copy-start | bytes 2359300
  0.6 8.8 %copy-start.1 = (bf16[3,512,256]{2,1,0:T(8,128)(2,1)S(1)}, bf16[3,512,256]{2,1,0:T(8,128)(2,1)}, u32[]{:S(2)}) copy-start(bf16[3,512,256]{2,1,0:T(8,128)(2,1)} %refs_9_.3) | copy-start | bytes 2359300
  0.7 7.9 %collective-permute-start.1 = (bf16[3,256,512]{2,1,0:T(8,128)(2,1)}, bf16[3,256,512]{2,1,0:T(8,128)(2,1)S(1)}, u32[]{:S(2)}, u32[]{:S(2)}) collective-permute-start(bf16[3,256,512]{2,1,0:T(8,128)(2,1)} %refs_7_.5), channel_id=1, source_target_pairs={{0,1},{1,0},{2,3},{3,2},{4,5},{5,4},{6,7},{7,6},{8,9},{9,8},{10,11... | collective-permute-start | bytes 2359304 | tf_op jit(solution)/shard_map/ppermute | solution.py:425
  1.2 7.4 %collective-permute-start.2 = (bf16[3,512,256]{2,1,0:T(8,128)(2,1)}, bf16[3,512,256]{2,1,0:T(8,128)(2,1)S(1)}, u32[]{:S(2)}, u32[]{:S(2)}) collective-permute-start(bf16[3,512,256]{2,1,0:T(8,128)(2,1)} %refs_9_.3), channel_id=1, source_target_pairs={{0,1},{1,0},{2,3},{3,2},{4,5},{5,4},{6,7},{7,6},{8,9},{9,8},{10,11... | collective-permute-start | bytes 2359304 | tf_op jit(solution)/shard_map/ppermute | solution.py:425
  3.6 8.5 %collective-permute-start = (bf16[128,256]{1,0:T(8,128)(2,1)S(1)}, bf16[128,256]{1,0:T(8,128)(2,1)S(1)}, u32[]{:S(2)}, u32[]{:S(2)}) collective-permute-start(bf16[128,256]{1,0:T(8,128)(2,1)S(1)} %get-tuple-element.114), channel_id=1, source_target_pairs={{0,4},{1,3},{2,6},{3,1},{4,8},{5,7},{6,10},{7,5},{8,12},{9,11},{10... | collective-permute-start | bytes 196616 | tf_op jit(solution)/shard_map/ppermute | solution.py:438
  12.1 1.3 %collective-permute-start.3 = (bf16[128,256]{1,0:T(8,128)(2,1)S(1)}, bf16[128,256]{1,0:T(8,128)(2,1)S(1)}, u32[]{:S(2)}, u32[]{:S(2)}) collective-permute-start(bf16[128,256]{1,0:T(8,128)(2,1)S(1)} %collective-permute-done.refs_7_.refs_12_), channel_id=1, source_target_pairs={{0,1},{1,0},{2,3},{3,2},{4,5},{5,4},{6,7},{7,6},{8,9},{9,8},{10,11... | collective-permute-start | bytes 196616 | tf_op jit(solution)/shard_map/ppermute | solution.py:425
  14.5 5.4 %collective-permute-start.4 = (bf16[128,256]{1,0:T(8,128)(2,1)S(1)}, bf16[128,256]{1,0:T(8,128)(2,1)S(1)}, u32[]{:S(2)}, u32[]{:S(2)}) collective-permute-start(bf16[128,256]{1,0:T(8,128)(2,1)S(1)} %get-tuple-element.124), channel_id=1, source_target_pairs={{0,4},{1,3},{2,6},{3,1},{4,8},{5,7},{6,10},{7,5},{8,12},{9,11},{10... | collective-permute-start | bytes 196616 | tf_op jit(solution)/shard_map/ppermute | solution.py:438
  19.9 1.3 %collective-permute-start.5 = (bf16[128,256]{1,0:T(8,128)(2,1)S(1)}, bf16[128,256]{1,0:T(8,128)(2,1)S(1)}, u32[]{:S(2)}, u32[]{:S(2)}) collective-permute-start(bf16[128,256]{1,0:T(8,128)(2,1)S(1)} %collective-permute-done.4.refs_7_.refs_12_), channel_id=1, source_target_pairs={{0,1},{1,0},{2,3},{3,2},{4,5},{5,4},{6,7},{7,6},{8,9},{9,8},{10,11... | collective-permute-start | bytes 196616 | tf_op jit(solution)/shard_map/ppermute | solution.py:425
  22.2 6.2 %collective-permute-start.6 = (bf16[128,256]{1,0:T(8,128)(2,1)S(1)}, bf16[128,256]{1,0:T(8,128)(2,1)S(1)}, u32[]{:S(2)}, u32[]{:S(2)}) collective-permute-start(bf16[128,256]{1,0:T(8,128)(2,1)S(1)} %get-tuple-element.130), channel_id=1, source_target_pairs={{0,4},{1,3},{2,6},{3,1},{4,8},{5,7},{6,10},{7,5},{8,12},{9,11},{10... | collective-permute-start | bytes 196616 | tf_op jit(solution)/shard_map/ppermute | solution.py:438
  28.4 1.3 %copy-start.2 = (f32[768,256]{1,0:T(8,128)S(1)}, f32[768,256]{1,0:T(8,128)}, u32[]{:S(2)}) copy-start(f32[768,256]{1,0:T(8,128)} %refs_4_.5) | copy-start | bytes 2359300
  28.4 1.3 %collective-permute-start.7 = (bf16[128,256]{1,0:T(8,128)(2,1)S(1)}, bf16[128,256]{1,0:T(8,128)(2,1)S(1)}, u32[]{:S(2)}, u32[]{:S(2)}) collective-permute-start(bf16[128,256]{1,0:T(8,128)(2,1)S(1)} %collective-permute-done.6.refs_7_.refs_9_), channel_id=1, source_target_pairs={{0,1},{1,0},{2,3},{3,2},{4,5},{5,4},{6,7},{7,6},{8,9},{9,8},{10,11... | collective-permute-start | bytes 196616 | tf_op jit(solution)/shard_map/ppermute | solution.py:425
  31.9 6.8 %collective-permute-start.8 = (bf16[128,256]{1,0:T(8,128)(2,1)S(1)}, bf16[128,256]{1,0:T(8,128)(2,1)S(1)}, u32[]{:S(2)}, u32[]{:S(2)}) collective-permute-start(bf16[128,256]{1,0:T(8,128)(2,1)S(1)} %get-tuple-element.147), channel_id=1, source_target_pairs={{4,0},{8,4},{12,8},{5,1},{9,5},{13,9},{6,2},{10,6},{14,10},{7,3},{... | collective-permute-start | bytes 196616 | tf_op jit(solution)/shard_map/ppermute | solution.py:466
  33.2 5.5 %collective-permute-start.9 = (bf16[128,256]{1,0:T(8,128)(2,1)S(1)}, bf16[128,256]{1,0:T(8,128)(2,1)S(1)}, u32[]{:S(2)}, u32[]{:S(2)}) collective-permute-start(bf16[128,256]{1,0:T(8,128)(2,1)S(1)} %get-tuple-element.148), channel_id=1, source_target_pairs={{0,2},{2,0},{1,3},{3,1},{4,6},{6,4},{5,7},{7,5},{8,10},{10,8},{9,1... | collective-permute-start | bytes 196616 | tf_op jit(solution)/shard_map/ppermute | solution.py:425
  38.8 11.1 %collective-permute-start.12 = (bf16[1024,128]{1,0:T(8,128)(2,1)S(1)}, bf16[1024,128]{1,0:T(8,128)(2,1)S(1)}, u32[]{:S(2)}, u32[]{:S(2)}) collective-permute-start(bf16[1024,128]{1,0:T(8,128)(2,1)S(1)} %get-tuple-element.167), channel_id=1, source_target_pairs={{0,2},{1,3},{2,0},{3,1},{4,6},{5,7},{6,4},{7,5},{8,10},{9,11},{10,... | collective-permute-start | bytes 786440 | tf_op jit(solution)/shard_map/ppermute | solution.py:438
  41.9 6.2 %collective-permute-start.10 = (bf16[128,256]{1,0:T(8,128)(2,1)S(1)}, bf16[128,256]{1,0:T(8,128)(2,1)S(1)}, u32[]{:S(2)}, u32[]{:S(2)}) collective-permute-start(bf16[128,256]{1,0:T(8,128)(2,1)S(1)} %get-tuple-element.163), channel_id=1, source_target_pairs={{4,0},{8,4},{12,8},{5,1},{9,5},{13,9},{6,2},{10,6},{14,10},{7,3},{... | collective-permute-start | bytes 196616 | tf_op jit(solution)/shard_map/ppermute | solution.py:466
  43.2 5.0 %collective-permute-start.11 = (bf16[128,256]{1,0:T(8,128)(2,1)S(1)}, bf16[128,256]{1,0:T(8,128)(2,1)S(1)}, u32[]{:S(2)}, u32[]{:S(2)}) collective-permute-start(bf16[128,256]{1,0:T(8,128)(2,1)S(1)} %get-tuple-element.164), channel_id=1, source_target_pairs={{0,2},{2,0},{1,3},{3,1},{4,6},{6,4},{5,7},{7,5},{8,10},{10,8},{9,1... | collective-permute-start | bytes 196616 | tf_op jit(solution)/shard_map/ppermute | solution.py:425
  48.3 8.4 %collective-permute-start.14 = (bf16[1024,128]{1,0:T(8,128)(2,1)S(1)}, bf16[1024,128]{1,0:T(8,128)(2,1)S(1)}, u32[]{:S(2)}, u32[]{:S(2)}) collective-permute-start(bf16[1024,128]{1,0:T(8,128)(2,1)S(1)} %get-tuple-element.183), channel_id=1, source_target_pairs={{0,2},{1,3},{2,0},{3,1},{4,6},{5,7},{6,4},{7,5},{8,10},{9,11},{10,... | collective-permute-start | bytes 786440 | tf_op jit(solution)/shard_map/ppermute | solution.py:438
  50.0 5.6 %collective-permute-start.13 = (bf16[512,128]{1,0:T(8,128)(2,1)S(1)}, bf16[512,128]{1,0:T(8,128)(2,1)S(1)}, u32[]{:S(2)}, u32[]{:S(2)}) collective-permute-start(bf16[512,128]{1,0:T(8,128)(2,1)S(1)} %get-tuple-element.180), channel_id=1, source_target_pairs={{0,4},{1,5},{2,6},{3,7},{4,0},{5,1},{6,2},{7,3},{8,12},{9,13},{10,... | collective-permute-start | bytes 393224 | tf_op jit(solution)/shard_map/ppermute | solution.py:438
  55.6 6.4 %collective-permute-start.15 = (bf16[1024,128]{1,0:T(8,128)(2,1)S(1)}, bf16[1024,128]{1,0:T(8,128)(2,1)S(1)}, u32[]{:S(2)}, u32[]{:S(2)}) collective-permute-start(bf16[1024,128]{1,0:T(8,128)(2,1)S(1)} %get-tuple-element.186), channel_id=1, source_target_pairs={{0,2},{1,5},{2,0},{3,7},{4,6},{5,1},{6,4},{7,3},{8,10},{9,13},{10,... | collective-permute-start | bytes 786440 | tf_op jit(solution)/shard_map/ppermute | solution.py:438
  56.8 9.0 %collective-permute-start.16 = (bf16[512,128]{1,0:T(8,128)(2,1)S(1)}, bf16[512,128]{1,0:T(8,128)(2,1)S(1)}, u32[]{:S(2)}, u32[]{:S(2)}) collective-permute-start(bf16[512,128]{1,0:T(8,128)(2,1)S(1)} %get-tuple-element.188), channel_id=1, source_target_pairs={{0,8},{1,9},{2,10},{3,11},{4,12},{5,13},{6,14},{7,15},{8,0},{9,1},... | collective-permute-start | bytes 393224 | tf_op jit(solution)/shard_map/ppermute | solution.py:438
  60.1 6.9 %collective-permute-start.17 = (bf16[512,128]{1,0:T(8,128)(2,1)S(1)}, bf16[512,128]{1,0:T(8,128)(2,1)S(1)}, u32[]{:S(2)}, u32[]{:S(2)}) collective-permute-start(bf16[512,128]{1,0:T(8,128)(2,1)S(1)} %get-tuple-element.190), channel_id=1, source_target_pairs={{0,4},{1,5},{2,6},{3,7},{4,0},{5,1},{6,2},{7,3},{8,12},{9,13},{10,... | collective-permute-start | bytes 393224 | tf_op jit(solution)/shard_map/ppermute | solution.py:438
  62.1 8.6 %collective-permute-start.18 = (bf16[512,128]{1,0:T(8,128)(2,1)S(1)}, bf16[512,128]{1,0:T(8,128)(2,1)S(1)}, u32[]{:S(2)}, u32[]{:S(2)}) collective-permute-start(bf16[512,128]{1,0:T(8,128)(2,1)S(1)} %get-tuple-element.192), channel_id=1, source_target_pairs={{0,4},{1,3},{2,6},{3,1},{4,0},{5,7},{6,2},{7,5},{8,12},{9,11},{10,... | collective-permute-start | bytes 393224 | tf_op jit(solution)/shard_map/ppermute | solution.py:438
  65.8 7.9 %collective-permute-start.19 = (bf16[512,128]{1,0:T(8,128)(2,1)S(1)}, bf16[512,128]{1,0:T(8,128)(2,1)S(1)}, u32[]{:S(2)}, u32[]{:S(2)}) collective-permute-start(bf16[512,128]{1,0:T(8,128)(2,1)S(1)} %get-tuple-element.194), channel_id=1, source_target_pairs={{0,4},{1,5},{2,6},{3,7},{4,0},{5,1},{6,2},{7,3},{8,12},{9,13},{10,... | collective-permute-start | bytes 393224 | tf_op jit(solution)/shard_map/ppermute | solution.py:438
  67.0 11.1 %collective-permute-start.20 = (bf16[512,128]{1,0:T(8,128)(2,1)S(1)}, bf16[512,128]{1,0:T(8,128)(2,1)S(1)}, u32[]{:S(2)}, u32[]{:S(2)}) collective-permute-start(bf16[512,128]{1,0:T(8,128)(2,1)S(1)} %get-tuple-element.196), channel_id=1, source_target_pairs={{0,8},{1,9},{2,10},{3,11},{4,12},{5,13},{6,14},{7,15},{8,0},{9,1},... | collective-permute-start | bytes 393224 | tf_op jit(solution)/shard_map/ppermute | solution.py:438
  70.8 8.8 %collective-permute-start.21 = (bf16[512,128]{1,0:T(8,128)(2,1)S(1)}, bf16[512,128]{1,0:T(8,128)(2,1)S(1)}, u32[]{:S(2)}, u32[]{:S(2)}) collective-permute-start(bf16[512,128]{1,0:T(8,128)(2,1)S(1)} %get-tuple-element.198), channel_id=1, source_target_pairs={{0,8},{1,9},{2,10},{3,11},{4,12},{5,13},{6,14},{7,15},{8,0},{9,1},... | collective-permute-start | bytes 393224 | tf_op jit(solution)/shard_map/ppermute | solution.py:438
  73.8 13.0 %collective-permute-start.25 = (bf16[1024,128]{1,0:T(8,128)(2,1)S(1)}, bf16[1024,128]{1,0:T(8,128)(2,1)S(1)}, u32[]{:S(2)}, u32[]{:S(2)}) collective-permute-start(bf16[1024,128]{1,0:T(8,128)(2,1)S(1)} %get-tuple-element.204), channel_id=1, source_target_pairs={{0,2},{1,3},{2,0},{3,1},{4,6},{5,7},{6,4},{7,5},{8,10},{9,11},{10,... | collective-permute-start | bytes 786440 | tf_op jit(solution)/shard_map/ppermute | solution.py:438
  78.2 5.0 %collective-permute-start.22 = (bf16[512,128]{1,0:T(8,128)(2,1)S(1)}, bf16[512,128]{1,0:T(8,128)(2,1)S(1)}, u32[]{:S(2)}, u32[]{:S(2)}) collective-permute-start(bf16[512,128]{1,0:T(8,128)(2,1)S(1)} %get-tuple-element.200), channel_id=1, source_target_pairs={{0,4},{1,5},{2,6},{3,7},{4,0},{5,1},{6,2},{7,3},{8,12},{9,13},{10,... | collective-permute-start | bytes 393224 | tf_op jit(solution)/shard_map/ppermute | solution.py:438
  79.6 7.2 %collective-permute-start.26 = (bf16[512,128]{1,0:T(8,128)(2,1)S(1)}, bf16[512,128]{1,0:T(8,128)(2,1)S(1)}, u32[]{:S(2)}, u32[]{:S(2)}) collective-permute-start(bf16[512,128]{1,0:T(8,128)(2,1)S(1)} %get-tuple-element.205), channel_id=1, source_target_pairs={{0,4},{1,3},{2,6},{3,1},{4,0},{5,7},{6,2},{7,5},{8,12},{9,11},{10,... | collective-permute-start | bytes 393224 | tf_op jit(solution)/shard_map/ppermute | solution.py:438
  80.4 6.1 %collective-permute-start.23 = (bf16[128,256]{1,0:T(8,128)(2,1)S(1)}, bf16[128,256]{1,0:T(8,128)(2,1)S(1)}, u32[]{:S(2)}, u32[]{:S(2)}) collective-permute-start(bf16[128,256]{1,0:T(8,128)(2,1)S(1)} %get-tuple-element.202), channel_id=1, source_target_pairs={{4,0},{8,4},{12,8},{5,1},{9,5},{13,9},{6,2},{10,6},{14,10},{7,3},{... | collective-permute-start | bytes 196616 | tf_op jit(solution)/shard_map/ppermute | solution.py:466
  81.7 5.1 %collective-permute-start.24 = (bf16[128,256]{1,0:T(8,128)(2,1)S(1)}, bf16[128,256]{1,0:T(8,128)(2,1)S(1)}, u32[]{:S(2)}, u32[]{:S(2)}) collective-permute-start(bf16[128,256]{1,0:T(8,128)(2,1)S(1)} %get-tuple-element.203), channel_id=1, source_target_pairs={{0,2},{2,0},{1,3},{3,1},{4,6},{6,4},{5,7},{7,5},{8,10},{10,8},{9,1... | collective-permute-start | bytes 196616 | tf_op jit(solution)/shard_map/ppermute | solution.py:425
  83.3 7.8 %collective-permute-start.27 = (bf16[1024,128]{1,0:T(8,128)(2,1)S(1)}, bf16[1024,128]{1,0:T(8,128)(2,1)S(1)}, u32[]{:S(2)}, u32[]{:S(2)}) collective-permute-start(bf16[1024,128]{1,0:T(8,128)(2,1)S(1)} %get-tuple-element.213), channel_id=1, source_target_pairs={{0,2},{1,3},{2,0},{3,1},{4,6},{5,7},{6,4},{7,5},{8,10},{9,11},{10,... | collective-permute-start | bytes 786440 | tf_op jit(solution)/shard_map/ppermute | solution.py:438
  86.8 7.1 %collective-permute-start.28 = (bf16[1024,128]{1,0:T(8,128)(2,1)S(1)}, bf16[1024,128]{1,0:T(8,128)(2,1)S(1)}, u32[]{:S(2)}, u32[]{:S(2)}) collective-permute-start(bf16[1024,128]{1,0:T(8,128)(2,1)S(1)} %get-tuple-element.220), channel_id=1, source_target_pairs={{0,2},{1,5},{2,0},{3,7},{4,6},{5,1},{6,4},{7,3},{8,10},{9,13},{10,... | collective-permute-start | bytes 786440 | tf_op jit(solution)/shard_map/ppermute | solution.py:438
  (3 other events, 3.3 us)
